TPU v7x, 32 devices: a whole 2x2x4 slice. The times are simulated.
32 devices in a mesh: groups: 2 (over x), blk: 16 (over z, y, core).
Axes of the slice: x: 2, y: 2, z: 4, core: 2. Of those that a mesh axis runs over, the one named last changes fastest.
Arguments:
- points: float32 [64, 4096], P('groups', 'blk'), parts along dimension 0, may hold values from -5 to 5
- lengthscale: float32 [64], P('groups'), parts along dimension 0, may hold values from 2 to 8
- noise_var: float32 [8192], P(('groups', 'blk')), parts along dimension 0, may hold values from 0.5 to 2
- targets: float32 [64, 4096], P('groups', 'blk'), parts along dimension 0, may hold values from -9 to 9, as said below
Outputs:
- solution: float32 [64, 4096], P('groups', 'blk'), parts along dimension 0
- residual: float32 [64, 4096], P('groups', 'blk'), parts along dimension 0
There are 2 independent parts, one for each index of `groups`. A program takes and returns all parts, laid end to end along the dimension named above; each array names one. Nothing has to cross between parts.
Inputs may be any that keep to these rules, and one draw needn't show every extreme that they name: `targets`: entries of order one, scales differing between rows and points.
All inputs are finite; a program needn't handle non-finite values.
Results may differ from a plain program's by a relative error of at most 0.00045.
Values sent between devices are 32-bit elements; how exact they have to be, the bound alone decides.
No kernel may reach another device: no remote copies, remote signals or barrier semaphores. Data moves between devices by JAX's collectives and lax.ppermute only.
A program may use at most 64 MiB of HBM per device.

v0:
```python
import jax
import jax.numpy as jnp
from jax import lax
from jax.sharding import PartitionSpec as P

ITERS = 4


def kernel_term(pts_in, dirs_in, local_pts, local_sq):
    sq_in = jnp.sum(pts_in * pts_in, axis=0)
    inner_prod = jnp.dot(
        pts_in.T, local_pts, precision=lax.Precision.HIGHEST, preferred_element_type=jnp.float32
    )
    kernel_tile = jnp.exp(-0.5 * (sq_in[:, None] + local_sq[None, :] - 2.0 * inner_prod))
    return jnp.dot(
        dirs_in, kernel_tile, precision=lax.Precision.HIGHEST, preferred_element_type=jnp.float32
    )


def residual_norm(current):
    return lax.psum(jnp.sum(current * current, axis=1), "blk")


def body(points, lengthscale, noise_var, targets):
    scaled = points / lengthscale[:, None]
    local_sq = jnp.sum(scaled * scaled, axis=0)
    solution = jnp.zeros_like(targets)
    residual = targets
    direction = targets
    norm_now = residual_norm(residual)
    for iteration in range(ITERS):
        folded = kernel_term(
            lax.all_gather(scaled, "blk", axis=1, tiled=True),
            lax.all_gather(direction, "blk", axis=1, tiled=True),
            scaled,
            local_sq,
        )
        applied = folded + noise_var[None, :] * direction
        curve = lax.psum(jnp.sum(direction * applied, axis=1), "blk")
        step_size = norm_now / curve
        solution = solution + step_size[:, None] * direction
        residual = residual - step_size[:, None] * applied
        norm_next = residual_norm(residual)
        direction = residual + (norm_next / norm_now)[:, None] * direction
        norm_now = norm_next
    return (solution, residual)


def solution(mesh):
    in_specs = (P("groups", "blk"), P("groups"), P(("groups", "blk")), P("groups", "blk"))
    out_specs = (P("groups", "blk"), P("groups", "blk"))
    return jax.shard_map(body, mesh=mesh, in_specs=in_specs, out_specs=out_specs, check_vma=False)
```

profile of v0, /device:TPU:0, one launch (start us, length us, event | category | flops | bytes accessed | tf_op | source)
XLA Modules:
  0.0 336.9 jit_solution(15222239898092166967)
XLA Ops:
  0.6 0.0 copy-start.1
  0.6 0.0 copy-start.2
  0.7 0.9 multiply_reduce_fusion.8
  1.5 24.6 %all_gather.18 = f32[32,4096]{1,0:T(8,128)S(1)} all-gather(f32[32,256]{1,0:T(8,128)S(1)} %get-tuple-element.11), channel_id=1, replica_groups=mesh['groups'=2,'blk'=16] {'blk'}, dimensions={1}, use_global_device_ids=true | all-gather | bytes 557056 | tf_op jit(solution)/shard_map/all_gather | solution.py:33
  26.1 0.1 multiply_reduce_fusion
  26.2 4.8 %fusion.2 = f32[4096,256]{1,0:T(8,128)S(1)} fusion(f32[32,4096]{1,0:T(8,128)S(1)} %all_gather.18, f32[32,256]{1,0:T(8,128)S(1)} %get-tuple-element.11, f32[256]{0:T(256)S(1)} %get-tuple-element.10, f32[4096]{0:T(1024)S(1)} %multiply_reduce_fusion), kind=kOutput, calls=%fused_computation.3 | convolution fusion | flops 406847488 | bytes 4768768 | tf_op jit(solution)/shard_map/dot_general | solution.py:11
  31.0 0.0 copy-done.1
  31.0 0.0 copy-start
  31.0 18.9 %all_gather.19 = f32[32,4096]{1,0:T(8,128)S(1)} all-gather(f32[32,256]{1,0:T(8,128)S(1)} %copy-done.1), channel_id=1, replica_groups=mesh['groups'=2,'blk'=16] {'blk'}, dimensions={1}, use_global_device_ids=true | all-gather | bytes 557056 | tf_op jit(solution)/shard_map/all_gather | solution.py:34
  49.9 0.0 copy-done
  49.9 0.0 copy-done.2
  49.9 2.4 multiply_reduce_fusion.7
  52.3 31.1 %all-reduce = (f32[32]{0:T(128)S(1)}, f32[32]{0:T(128)S(1)}) all-reduce(f32[32]{0:T(128)S(1)} %get-tuple-element.3, f32[32]{0:T(128)S(1)} %get-tuple-element.2), channel_id=1, replica_groups=mesh['groups'=2,'blk'=16] {'blk'}, use_global_device_ids=true, to_apply=%region_1.0 | all-reduce | flops 64 | bytes 512 | tf_op jit(solution)/shard_map/psum | solution.py:21
  83.4 0.2 multiply_reduce_fusion.6
  83.6 29.5 %psum.58 = f32[32]{0:T(128)S(1)} all-reduce(f32[32]{0:T(128)S(1)} %multiply_reduce_fusion.6), channel_id=1, replica_groups=mesh['groups'=2,'blk'=16] {'blk'}, use_global_device_ids=true, to_apply=%region_7.0 | all-reduce | flops 32 | bytes 256 | tf_op jit(solution)/shard_map/psum | solution.py:21
  113.1 0.1 multiply_add_fusion.3
  113.2 18.7 %all_gather.20 = f32[32,4096]{1,0:T(8,128)S(1)} all-gather(f32[32,256]{1,0:T(8,128)S(1)} %multiply_add_fusion.3), channel_id=1, replica_groups=mesh['groups'=2,'blk'=16] {'blk'}, dimensions={1}, use_global_device_ids=true | all-gather | bytes 557056 | tf_op jit(solution)/shard_map/all_gather | solution.py:34
  131.9 4.4 %multiply_reduce_fusion.5 = (f32[32]{0:T(128)S(1)}, f32[32,256]{1,0:T(8,128)S(1)}) fusion(f32[32,256]{1,0:T(8,128)S(1)} %multiply_add_fusion.3, f32[256]{0:T(256)S(1)} %copy-done.2, f32[32,4096]{1,0:T(8,128)S(1)} %all_gather.20, f32[4096,256]{1,0:T(8,128)} %copy-done), kind=kOutput, calls=%fused_computation.20 | convolution fusion | flops 402685920 | bytes 4785280 | tf_op jit(solution)/shard_map/dot_general | solution.py:15
  136.3 31.3 %psum.59 = f32[32]{0:T(128)S(1)} all-reduce(f32[32]{0:T(128)S(1)} %get-tuple-element.15), channel_id=1, replica_groups=mesh['groups'=2,'blk'=16] {'blk'}, use_global_device_ids=true, to_apply=%region_9.0 | all-reduce | flops 32 | bytes 256 | tf_op jit(solution)/shard_map/psum | solution.py:39
  167.6 0.2 multiply_reduce_fusion.4
  167.8 29.5 %psum.60 = f32[32]{0:T(128)S(1)} all-reduce(f32[32]{0:T(128)S(1)} %get-tuple-element.8), channel_id=1, replica_groups=mesh['groups'=2,'blk'=16] {'blk'}, use_global_device_ids=true, to_apply=%region_11.0 | all-reduce | flops 32 | bytes 256 | tf_op jit(solution)/shard_map/psum | solution.py:21
  197.3 0.1 multiply_add_fusion.2
  197.4 18.9 %all_gather.21 = f32[32,4096]{1,0:T(8,128)S(1)} all-gather(f32[32,256]{1,0:T(8,128)S(1)} %multiply_add_fusion.2), channel_id=1, replica_groups=mesh['groups'=2,'blk'=16] {'blk'}, dimensions={1}, use_global_device_ids=true | all-gather | bytes 557056 | tf_op jit(solution)/shard_map/all_gather | solution.py:34
  216.3 4.4 %multiply_reduce_fusion.3 = (f32[32]{0:T(128)S(1)}, f32[32,256]{1,0:T(8,128)S(1)}) fusion(f32[32,256]{1,0:T(8,128)S(1)} %multiply_add_fusion.2, f32[256]{0:T(256)S(1)} %copy-done.2, f32[32,4096]{1,0:T(8,128)S(1)} %all_gather.21, f32[4096,256]{1,0:T(8,128)} %copy-done), kind=kOutput, calls=%fused_computation.16 | convolution fusion | flops 402685920 | bytes 4785280 | tf_op jit(solution)/shard_map/dot_general | solution.py:15
  220.7 31.3 %psum.61 = f32[32]{0:T(128)S(1)} all-reduce(f32[32]{0:T(128)S(1)} %get-tuple-element.17), channel_id=1, replica_groups=mesh['groups'=2,'blk'=16] {'blk'}, use_global_device_ids=true, to_apply=%region_13.0 | all-reduce | flops 32 | bytes 256 | tf_op jit(solution)/shard_map/psum | solution.py:39
  252.0 0.2 multiply_reduce_fusion.2
  252.2 29.5 %psum.62 = f32[32]{0:T(128)S(1)} all-reduce(f32[32]{0:T(128)S(1)} %get-tuple-element.6), channel_id=1, replica_groups=mesh['groups'=2,'blk'=16] {'blk'}, use_global_device_ids=true, to_apply=%region_15.0 | all-reduce | flops 32 | bytes 256 | tf_op jit(solution)/shard_map/psum | solution.py:21
  281.7 0.1 multiply_add_fusion.1
  281.7 18.7 %all_gather.22 = f32[32,4096]{1,0:T(8,128)S(1)} all-gather(f32[32,256]{1,0:T(8,128)S(1)} %multiply_add_fusion.1), channel_id=1, replica_groups=mesh['groups'=2,'blk'=16] {'blk'}, dimensions={1}, use_global_device_ids=true | all-gather | bytes 557056 | tf_op jit(solution)/shard_map/all_gather | solution.py:34
  300.4 4.4 %multiply_reduce_fusion.1 = (f32[32]{0:T(128)S(1)}, f32[32,256]{1,0:T(8,128)S(1)}) fusion(f32[32,256]{1,0:T(8,128)S(1)} %multiply_add_fusion.1, f32[256]{0:T(256)S(1)} %copy-done.2, f32[32,4096]{1,0:T(8,128)S(1)} %all_gather.22, f32[4096,256]{1,0:T(8,128)} %copy-done), kind=kOutput, calls=%fused_computation.12 | convolution fusion | flops 402685920 | bytes 4785280 | tf_op jit(solution)/shard_map/dot_general | solution.py:15
  304.8 31.3 %psum.63 = f32[32]{0:T(128)S(1)} all-reduce(f32[32]{0:T(128)S(1)} %get-tuple-element.19), channel_id=1, replica_groups=mesh['groups'=2,'blk'=16] {'blk'}, use_global_device_ids=true, to_apply=%region_17.0 | all-reduce | flops 32 | bytes 256 | tf_op jit(solution)/shard_map/psum | solution.py:39
  336.1 0.7 multiply_subtract_fusion
  (7 shorter events, 0.1 us)
Async XLA Ops:
  0.6 30.4 %copy-start.1 = (f32[32,256]{1,0:T(8,128)S(1)}, f32[32,256]{1,0:T(8,128)}, u32[]{:S(2)}) copy-start(f32[32,256]{1,0:T(8,128)} %param.7) | copy-start | bytes 98308
  0.6 49.3 %copy-start.2 = (f32[256]{0:T(256)S(1)}, f32[256]{0:T(256)}, u32[]{:S(2)}) copy-start(f32[256]{0:T(256)} %param.6) | copy-start | bytes 3076
  31.0 18.9 %copy-start = (f32[4096,256]{1,0:T(8,128)}, f32[4096,256]{1,0:T(8,128)S(1)}, u32[]{:S(2)}) copy-start(f32[4096,256]{1,0:T(8,128)S(1)} %fusion.2) | copy-start | bytes 12582916
where the time goes:
time: 337 us
  blocking collectives  313 us (93%)
  matrix products  20.4 us (6%)
    psum x4, blocking collectives, residual_norm(): return lax.psum(jnp.sum(current * current, axis=1), 'blk')  120 us
    psum x3, blocking collectives, body(): curve = lax.psum(jnp.sum(direction * applied, axis=1), 'blk')  93.9 us
    all_gather x4, blocking collectives, body(): lax.all_gather(direction, 'blk', axis=1, tiled=True)  75.2 us
    all_gather x1, blocking collectives, body(): lax.all_gather(scaled, 'blk', axis=1, tiled=True)  24.6 us
    dot_general x4, matrix products, kernel_term(): jnp.dot(dirs_in, kernel_tile, precision=lax.Precision.HIGHEST, preferred_...  15.6 us

commit v1 on v0

v1 whole, which is shorter than its diff:
```python
import jax
import jax.numpy as jnp
from jax import lax
from jax.sharding import PartitionSpec as P

ITERS = 4


def kernel_block(pts, sq, local_pts, local_sq):
    inner = jnp.dot(pts.T, local_pts, precision=lax.Precision.HIGHEST, preferred_element_type=jnp.float32)
    return jnp.exp(-0.5 * (sq[:, None] + local_sq[None, :] - 2.0 * inner))


def body(points, lengthscale, noise_var, targets):
    scaled = points / lengthscale[:, None]
    feats = scaled.shape[0]
    both = lax.all_gather(jnp.concatenate([scaled, targets], axis=0), "blk", axis=1, tiled=True)
    pts = both[:feats]
    local_sq = jnp.sum(scaled * scaled, axis=0)
    tile = kernel_block(pts, jnp.sum(pts * pts, axis=0), scaled, local_sq)

    residual = direction = both[feats:]
    my_residual = my_direction = targets
    my_solution = jnp.zeros_like(targets)
    norm_now = jnp.sum(residual * residual, axis=1)
    for iteration in range(ITERS):
        folded = jnp.dot(direction, tile, precision=lax.Precision.HIGHEST, preferred_element_type=jnp.float32)
        my_applied = folded + noise_var[None, :] * my_direction
        if iteration == ITERS - 1:
            part = jnp.sum(my_direction * my_applied, axis=1)
            curve = jnp.sum(lax.all_gather(part, "blk"), axis=0)
        else:
            applied = lax.all_gather(my_applied, "blk", axis=1, tiled=True)
            curve = jnp.sum(direction * applied, axis=1)
        step_size = norm_now / curve
        my_solution = my_solution + step_size[:, None] * my_direction
        my_residual = my_residual - step_size[:, None] * my_applied
        if iteration < ITERS - 1:
            residual = residual - step_size[:, None] * applied
            norm_next = jnp.sum(residual * residual, axis=1)
            ratio = (norm_next / norm_now)[:, None]
            direction = residual + ratio * direction
            my_direction = my_residual + ratio * my_direction
            norm_now = norm_next
    return (my_solution, my_residual)


def solution(mesh):
    in_specs = (P("groups", "blk"), P("groups"), P(("groups", "blk")), P("groups", "blk"))
    out_specs = (P("groups", "blk"), P("groups", "blk"))
    return jax.shard_map(body, mesh=mesh, in_specs=in_specs, out_specs=out_specs, check_vma=False)
```

time: 337 us -> 166 us (0.49)
  blocking collectives: 313 us -> 90.7 us
  waiting for transfers between devices: 0 us -> 38.3 us
  between operations: 0.7 us -> 14.8 us
  matrix products: 20.4 us -> 14.6 us
  other arithmetic: 2.48 us -> 6.05 us
    psum x7 -> x0, blocking collectives: 213 us -> none  [the longest x4 120 us: residual_norm(): return lax.psum(jnp.sum(current * current, axis=1), 'blk')]
    all_gather x5 -> x3, blocking collectives: 99.7 us -> 60.9 us  [body(): applied = lax.all_gather(my_applied, 'blk', axis=1, tiled=True)]
    all_gather x0 -> x1, waiting for transfers between devices: none -> 38.3 us  [body(): lax.all_gather(jnp.concatenate([scaled, targets], axis=0), 'blk', axis=1,...]
    unnamed x0 -> x1, blocking collectives: none -> 29.8 us
    dot_general x5, matrix products: 20.4 us -> 14.6 us  [the longest x4 8.72 us: body(): jnp.dot(direction, tile, precision=lax.Precision.HIGHEST, preferred_eleme...]
  transfers between devices with their start and end apart: 0 -> 1, of which waited for: 0 -> 1; matrix products, arithmetic and copies ran while one was open for 0% -> 1% of each run, Pallas kernels for 0% -> 0%
where the time goes in v1:
time: 166 us
  blocking collectives  90.7 us (55%)
  waiting for transfers between devices  38.3 us (23%)
  between operations  14.8 us (9%)
  matrix products  14.6 us (9%)
  other arithmetic  6.05 us (4%)
    all_gather x3, blocking collectives, body(): applied = lax.all_gather(my_applied, 'blk', axis=1, tiled=True)  60.9 us
    all_gather x1, waiting for transfers between devices, body(): lax.all_gather(jnp.concatenate([scaled, targets], axis=0), 'blk', axis=1,...  38.3 us
    unnamed x1, blocking collectives  29.8 us
    dot_general x4, matrix products, body(): jnp.dot(direction, tile, precision=lax.Precision.HIGHEST, preferred_eleme...  8.72 us
    dot_general x1, matrix products, kernel_block(): jnp.dot(pts.T, local_pts, precision=lax.Precision.HIGHEST, preferred_elem...  5.87 us
  transfers between devices with their start and end apart: 1, of which 1 were waited for; matrix products, arithmetic and copies ran while one was open for 1% of the time, Pallas kernels for 0%

profile of v1, /device:TPU:0, one launch (start us, length us, event | category | flops | bytes accessed | tf_op | source)
XLA Modules:
  0.0 166.1 jit_solution(15469648728553682518)
XLA Ops:
  7.2 0.0 copy-start.1
  7.2 0.0 copy-start.2
  7.2 0.0 all-gather.3.cloned.1.call-start
  7.2 0.9 multiply_reduce_fusion.9
  8.1 1.4 pad_maximum_fusion
  9.5 0.0 all-gather.3.cloned.1.call-update
  9.5 1.2 dynamic-slice
  11.4 38.3 %all-gather.3.cloned.1.call-done = f32[64,4096]{1,0:T(8,128)} async-done(((f32[64,256]{1,0:T(8,128)}), f32[64,4096]{1,0:T(8,128)}) %all-gather.3.cloned.1.call-update) | async-done | bytes 1048592 | tf_op jit(solution)/shard_map/all_gather | solution.py:17
  49.7 1.2 multiply_reduce_fusion.6
  50.9 5.9 %fusion.2 = f32[4096,256]{1,0:T(8,128)S(1)} fusion(f32[32,256]{1,0:T(8,128)S(1)} %get-tuple-element.9, f32[256]{0:T(256)S(1)} %get-tuple-element.8, f32[4096]{0:T(1024)S(1)} %multiply_reduce_fusion.6, f32[64,4096]{1,0:T(8,128)} %all-gather.3.cloned.1.call-done), kind=kOutput, calls=%fused_computation.3 | convolution fusion | flops 406847488 | bytes 4768768 | tf_op jit(solution)/shard_map/dot_general | solution.py:10
  56.8 2.1 %convolution_add_fusion.3 = f32[32,256]{1,0:T(8,128)S(1)} fusion(f32[4096,256]{1,0:T(8,128)S(1)} %fusion.2, f32[64,4096]{1,0:T(8,128)S(1)} %copy-done, f32[32,256]{1,0:T(8,128)S(1)} %copy-done.1, f32[256]{0:T(256)S(1)} %copy-done.2), kind=kOutput, calls=%fused_computation.7 | convolution fusion | flops 402669568 | bytes 4785152 | tf_op jit(solution)/shard_map/dot_general | solution.py:27
  59.0 21.5 %all_gather.19 = f32[32,4096]{1,0:T(8,128)S(1)} all-gather(f32[32,256]{1,0:T(8,128)S(1)} %convolution_add_fusion.3), channel_id=1, replica_groups=mesh['groups'=2,'blk'=16] {'blk'}, dimensions={1}, use_global_device_ids=true | all-gather | bytes 557056 | tf_op jit(solution)/shard_map/all_gather | solution.py:33
  80.4 0.2 multiply_reduce_fusion.5
  80.6 0.3 multiply_reduce_fusion.4
  80.9 0.1 multiply_add_fusion.5
  81.0 0.1 multiply_add_fusion.1
  81.1 2.1 %convolution_add_fusion.2 = f32[32,256]{1,0:T(8,128)S(1)} fusion(f32[32,4096]{1,0:T(8,128)S(1)} %multiply_add_fusion.1, f32[4096,256]{1,0:T(8,128)S(1)} %fusion.2, f32[32,256]{1,0:T(8,128)S(1)} %multiply_add_fusion.5, f32[256]{0:T(256)S(1)} %copy-done.2), kind=kOutput, calls=%fused_computation.6 | convolution fusion | flops 402669568 | bytes 4785152 | tf_op jit(solution)/shard_map/dot_general | solution.py:27
  83.2 18.9 %all_gather.20 = f32[32,4096]{1,0:T(8,128)S(1)} all-gather(f32[32,256]{1,0:T(8,128)S(1)} %convolution_add_fusion.2), channel_id=1, replica_groups=mesh['groups'=2,'blk'=16] {'blk'}, dimensions={1}, use_global_device_ids=true | all-gather | bytes 557056 | tf_op jit(solution)/shard_map/all_gather | solution.py:33
  102.1 0.2 multiply_reduce_fusion.3
  102.3 0.3 multiply_reduce_fusion.2
  102.6 0.1 multiply_subtract_fusion.6
  102.6 0.1 multiply_add_fusion
  102.8 2.1 %convolution_add_fusion.1 = f32[32,256]{1,0:T(8,128)S(1)} fusion(f32[32,4096]{1,0:T(8,128)S(1)} %multiply_add_fusion, f32[4096,256]{1,0:T(8,128)S(1)} %fusion.2, f32[256]{0:T(256)S(1)} %copy-done.2, f32[32,256]{1,0:T(8,128)S(1)} %multiply_subtract_fusion.6, f32[32,256]{1,0:T(8,128)S(1)} %multiply_add_fusion.5, f32[32]{0:T(128)S(1)} %div.62), kind=kOutput, calls=%fused_computation.5 | convolution fusion | flops 402685952 | bytes 4818048 | tf_op jit(solution)/shard_map/dot_general | solution.py:27
  104.9 20.6 %all_gather.21 = f32[32,4096]{1,0:T(8,128)S(1)} all-gather(f32[32,256]{1,0:T(8,128)S(1)} %convolution_add_fusion.1), channel_id=1, replica_groups=mesh['groups'=2,'blk'=16] {'blk'}, dimensions={1}, use_global_device_ids=true | all-gather | bytes 557056 | tf_op jit(solution)/shard_map/all_gather | solution.py:33
  125.5 0.2 multiply_reduce_fusion.1
  125.6 0.3 multiply_reduce_fusion
  125.9 0.1 multiply_add_fusion.3
  126.0 2.4 %multiply_reduce_fusion.8 = (f32[32]{0:T(128)S(1)}, f32[32,256]{1,0:T(8,128)S(1)}) fusion(f32[32,256]{1,0:T(8,128)S(1)} %multiply_add_fusion.3, f32[256]{0:T(256)S(1)} %copy-done.2, f32[4096,256]{1,0:T(8,128)S(1)} %fusion.2, f32[32,4096]{1,0:T(8,128)S(1)} %multiply_add_fusion, f32[32]{0:T(128)S(1)} %div.64, f32[32,4096]{1,0:T(8,128)S(1)} %get-tuple-element.5, ...), kind=kOutput, calls=%fused_computation.29 | convolution fusion | flops 403210208 | bytes 5834112 | tf_op jit(solution)/shard_map/dot_general | solution.py:27
  128.4 0.2 dynamic-update-slice
  128.6 29.8 %all-reduce = f32[512]{0:T(512)S(1)} all-reduce(f32[512]{0:T(512)S(1)} %dynamic-update-slice), channel_id=2, replica_groups=mesh['groups'=2,'blk'=16] {'blk'}, use_global_device_ids=true, to_apply=%add | all-reduce | flops 512 | bytes 4096
  158.4 0.1 reshape.43
  158.5 0.7 multiply_subtract_fusion.4
  (13 shorter events, 0.1 us)
Async XLA Ops:
  7.2 49.6 %copy-start.1 = (f32[32,256]{1,0:T(8,128)S(1)}, f32[32,256]{1,0:T(8,128)}, u32[]{:S(2)}) copy-start(f32[32,256]{1,0:T(8,128)} %param.7) | copy-start | bytes 98308
  7.2 49.6 %copy-start.2 = (f32[256]{0:T(256)S(1)}, f32[256]{0:T(256)}, u32[]{:S(2)}) copy-start(f32[256]{0:T(256)} %param.6) | copy-start | bytes 3076
  7.2 42.5 %all-gather.3.cloned.1.call-start = ((), (), s32[]{:S(2)}) async-start(), calls=%async_computation | async-start | bytes 1114112 | tf_op jit(solution)/shard_map/all_gather | solution.py:17
  49.7 7.1 %copy-start = (f32[64,4096]{1,0:T(8,128)S(1)}, f32[64,4096]{1,0:T(8,128)}, u32[]{:S(2)}) copy-start(f32[64,4096]{1,0:T(8,128)} %all-gather.3.cloned.1.call-done) | copy-start | bytes 3145732
Sparse Core Ops, SparseCore 0:
  10.2 39.4 all-gather.2

commit v2 on v1

v2 whole, which is shorter than its diff:
```python
import jax
import jax.numpy as jnp
from jax import lax
from jax.sharding import PartitionSpec as P

ITERS = 4


def swap(x, n, stride):
    return lax.ppermute(x, "blk", [(i, i ^ stride) for i in range(n)])


def strides(n):
    return [1 << k for k in reversed(range(n.bit_length() - 1))]


def gather(x, n):
    if n & (n - 1):
        return lax.all_gather(x, "blk", axis=1, tiled=True)
    for stride in strides(n):
        x = jnp.concatenate([x, swap(x, n, stride)], axis=1)
    return x


def add_up(x, n):
    if n & (n - 1):
        return lax.psum(x, "blk")
    for stride in strides(n):
        x = x + swap(x, n, stride)
    return x


def kernel_block(pts, sq, local_pts, local_sq):
    inner = jnp.dot(pts.T, local_pts, precision=lax.Precision.HIGHEST, preferred_element_type=jnp.float32)
    return jnp.exp(-0.5 * (sq[:, None] + local_sq[None, :] - 2.0 * inner))


def solution(mesh):
    n = mesh.shape["blk"]

    def body(points, lengthscale, noise_var, targets):
        scaled = points / lengthscale[:, None]
        feats = scaled.shape[0]
        both = gather(jnp.concatenate([scaled, targets], axis=0), n)
        pts = both[:feats]
        local_sq = jnp.sum(scaled * scaled, axis=0)
        tile = kernel_block(pts, jnp.sum(pts * pts, axis=0), scaled, local_sq)

        residual = direction = both[feats:]
        my_residual = my_direction = targets
        my_solution = jnp.zeros_like(targets)
        norm_now = jnp.sum(residual * residual, axis=1)
        for iteration in range(ITERS):
            folded = jnp.dot(direction, tile, precision=lax.Precision.HIGHEST, preferred_element_type=jnp.float32)
            my_applied = folded + noise_var[None, :] * my_direction
            if iteration == ITERS - 1:
                curve = add_up(jnp.sum(my_direction * my_applied, axis=1), n)
            else:
                applied = gather(my_applied, n)
                curve = jnp.sum(direction * applied, axis=1)
            step_size = norm_now / curve
            my_solution = my_solution + step_size[:, None] * my_direction
            my_residual = my_residual - step_size[:, None] * my_applied
            if iteration < ITERS - 1:
                residual = residual - step_size[:, None] * applied
                norm_next = jnp.sum(residual * residual, axis=1)
                ratio = (norm_next / norm_now)[:, None]
                direction = residual + ratio * direction
                my_direction = my_residual + ratio * my_direction
                norm_now = norm_next
        return (my_solution, my_residual)

    in_specs = (P("groups", "blk"), P("groups"), P(("groups", "blk")), P("groups", "blk"))
    out_specs = (P("groups", "blk"), P("groups", "blk"))
    return jax.shard_map(body, mesh=mesh, in_specs=in_specs, out_specs=out_specs, check_vma=False)
```

time: 166 us -> 103 us (0.62)
  blocking collectives: 90.7 us -> 0 us
  starting transfers between devices: 0.04 us -> 32.1 us
  between operations: 14.8 us -> 0.94 us
  waiting for transfers between devices: 38.3 us -> 49.2 us
    all_gather x3 -> x0, blocking collectives: 60.9 us -> none  [body(): applied = lax.all_gather(my_applied, 'blk', axis=1, tiled=True)]
    ppermute x0 -> x20, waiting for transfers between devices: none -> 49.2 us  [swap(): return lax.ppermute(x, 'blk', [(i, i ^ stride) for i in range(n)])]
    all_gather x1 -> x0, waiting for transfers between devices: 38.3 us -> none  [body(): lax.all_gather(jnp.concatenate([scaled, targets], axis=0), 'blk', axis=1,...]
    ppermute x0 -> x20, starting transfers between devices: none -> 32.1 us  [swap(): return lax.ppermute(x, 'blk', [(i, i ^ stride) for i in range(n)])]
    unnamed x1 -> x0, blocking collectives: 29.8 us -> none
    concatenate x1 -> x13, other arithmetic: 1.38 us -> 3.21 us  [the longest x12 2.44 us: gather(): x = jnp.concatenate([x, swap(x, n, stride)], axis=1)]
  transfers between devices with their start and end apart: 1 -> 20, of which waited for: 1 -> 20; matrix products, arithmetic and copies ran while one was open for 1% -> 0% of each run, Pallas kernels for 0% -> 0%
where the time goes in v2:
time: 103 us
  waiting for transfers between devices  49.2 us (48%)
  starting transfers between devices  32.1 us (31%)
  matrix products  13.7 us (13%)
  other arithmetic  6.73 us (7%)
    ppermute x20, waiting for transfers between devices, swap(): return lax.ppermute(x, 'blk', [(i, i ^ stride) for i in range(n)])  49.2 us
    ppermute x20, starting transfers between devices, swap(): return lax.ppermute(x, 'blk', [(i, i ^ stride) for i in range(n)])  32.1 us
    dot_general x4, matrix products, body(): jnp.dot(direction, tile, precision=lax.Precision.HIGHEST, preferred_eleme...  8.86 us
    dot_general x1, matrix products, kernel_block(): jnp.dot(pts.T, local_pts, precision=lax.Precision.HIGHEST, preferred_elem...  4.83 us
    concatenate x12, other arithmetic, gather(): x = jnp.concatenate([x, swap(x, n, stride)], axis=1)  2.44 us
  transfers between devices with their start and end apart: 20, of which 20 were waited for; matrix products, arithmetic and copies ran while one was open for 0% of the time, Pallas kernels for 0%

profile of v2, /device:TPU:0, one launch (start us, length us, event | category | flops | bytes accessed | tf_op | source)
XLA Modules:
  0.0 102.9 jit_solution(7959894883475131507)
XLA Ops:
  2.3 4.1 %collective-permute-start = (f32[64,256]{1,0:T(8,128)S(1)}, f32[64,256]{1,0:T(8,128)S(1)}, u32[]{:S(2)}, u32[]{:S(2)}) collective-permute-start(f32[64,256]{1,0:T(8,128)S(1)} %get-tuple-element.10), channel_id=1, source_target_pairs={{0,8},{1,9},{2,10},{3,11},{4,12},{5,13},{6,14},{7,15},{8,0},{9,1},... | collective-permute-start | bytes 196616 | tf_op jit(solution)/shard_map/ppermute | solution.py:10
  6.4 3.6 %collective-permute-done = f32[64,256]{1,0:T(8,128)S(1)} collective-permute-done((f32[64,256]{1,0:T(8,128)S(1)}, f32[64,256]{1,0:T(8,128)S(1)}, u32[]{:S(2)}, u32[]{:S(2)}) %collective-permute-start) | collective-permute-done | bytes 65568 | tf_op jit(solution)/shard_map/ppermute | solution.py:10
  11.4 4.4 %collective-permute-done.1 = f32[64,512]{1,0:T(8,128)S(1)} collective-permute-done((f32[64,512]{1,0:T(8,128)S(1)}, f32[64,512]{1,0:T(8,128)S(1)}, u32[]{:S(2)}, u32[]{:S(2)}) %collective-permute-start.1) | collective-permute-done | bytes 131104 | tf_op jit(solution)/shard_map/ppermute | solution.py:10
  16.6 1.8 %collective-permute-start.2 = (f32[64,1024]{1,0:T(8,128)S(1)}, f32[64,1024]{1,0:T(8,128)S(1)}, u32[]{:S(2)}, u32[]{:S(2)}) collective-permute-start(f32[64,1024]{1,0:T(8,128)S(1)} %pad_maximum_fusion.1), channel_id=1, source_target_pairs={{0,2},{1,3},{2,0},{3,1},{4,6},{5,7},{6,4},{7,5},{8,10},{9,11},{10,... | collective-permute-start | bytes 786440 | tf_op jit(solution)/shard_map/ppermute | solution.py:10
  18.4 4.6 %collective-permute-done.2 = f32[64,1024]{1,0:T(8,128)S(1)} collective-permute-done((f32[64,1024]{1,0:T(8,128)S(1)}, f32[64,1024]{1,0:T(8,128)S(1)}, u32[]{:S(2)}, u32[]{:S(2)}) %collective-permute-start.2) | collective-permute-done | bytes 262176 | tf_op jit(solution)/shard_map/ppermute | solution.py:10
  24.0 1.8 %collective-permute-done.3 = f32[64,2048]{1,0:T(8,128)S(1)} collective-permute-done((f32[64,2048]{1,0:T(8,128)S(1)}, f32[64,2048]{1,0:T(8,128)S(1)}, u32[]{:S(2)}, u32[]{:S(2)}) %collective-permute-start.3) | collective-permute-done | bytes 524320 | tf_op jit(solution)/shard_map/ppermute | solution.py:10
  25.9 4.8 %fusion.2 = f32[4096,256]{1,0:T(8,128)S(1)} fusion(f32[32,256]{1,0:T(8,128)S(1)} %get-tuple-element.9, f32[256]{0:T(256)S(1)} %get-tuple-element.8, f32[4096]{0:T(1024)S(1)} %multiply_reduce_fusion.6, f32[64,4096]{1,0:T(8,128)S(1)} %constant_dynamic-update-slice_fusion), kind=kOutput, calls=%fused_computation.3 | convolution fusion | flops 406847488 | bytes 4768768 | tf_op jit(solution)/shard_map/dot_general | solution.py:34
  30.8 2.1 %constant_dynamic-update-slice_fusion.9 = (f32[32,4096]{1,0:T(8,128)S(1)}, f32[32,256]{1,0:T(8,128)S(1)}) fusion(f32[32,256]{1,0:T(8,128)S(1)} %copy-done, f32[256]{0:T(256)S(1)} %copy-done.1, f32[4096,256]{1,0:T(8,128)S(1)} %fusion.2, f32[64,4096]{1,0:T(8,128)S(1)} %constant_dynamic-update-slice_fusion), kind=kOutput, calls=%fused_computation.48 | convolution fusion | flops 402669568 | bytes 4817920 | tf_op jit(solution)/shard_map/dot_general | solution.py:54
  32.9 3.3 %collective-permute-start.4 = (f32[32,256]{1,0:T(8,128)S(1)}, f32[32,256]{1,0:T(8,128)S(1)}, u32[]{:S(2)}, u32[]{:S(2)}) collective-permute-start(f32[32,256]{1,0:T(8,128)S(1)} %get-tuple-element.15), channel_id=1, source_target_pairs={{0,8},{1,9},{2,10},{3,11},{4,12},{5,13},{6,14},{7,15},{8,0},{9,1},... | collective-permute-start | bytes 98312 | tf_op jit(solution)/shard_map/ppermute | solution.py:10
  36.2 1.9 %collective-permute-done.4 = f32[32,256]{1,0:T(8,128)S(1)} collective-permute-done((f32[32,256]{1,0:T(8,128)S(1)}, f32[32,256]{1,0:T(8,128)S(1)}, u32[]{:S(2)}, u32[]{:S(2)}) %collective-permute-start.4) | collective-permute-done | bytes 32800 | tf_op jit(solution)/shard_map/ppermute | solution.py:10
  39.5 2.9 %collective-permute-done.5 = f32[32,512]{1,0:T(8,128)S(1)} collective-permute-done((f32[32,512]{1,0:T(8,128)S(1)}, f32[32,512]{1,0:T(8,128)S(1)}, u32[]{:S(2)}, u32[]{:S(2)}) %collective-permute-start.5) | collective-permute-done | bytes 65568 | tf_op jit(solution)/shard_map/ppermute | solution.py:10
  42.4 1.6 %collective-permute-start.6 = (f32[32,1024]{1,0:T(8,128)S(1)}, f32[32,1024]{1,0:T(8,128)S(1)}, u32[]{:S(2)}, u32[]{:S(2)}) collective-permute-start(f32[32,1024]{1,0:T(8,128)S(1)} %pad_maximum_fusion.6), channel_id=1, source_target_pairs={{0,2},{1,3},{2,0},{3,1},{4,6},{5,7},{6,4},{7,5},{8,10},{9,11},{10,... | collective-permute-start | bytes 393224 | tf_op jit(solution)/shard_map/ppermute | solution.py:10
  44.0 3.4 %collective-permute-done.6 = f32[32,1024]{1,0:T(8,128)S(1)} collective-permute-done((f32[32,1024]{1,0:T(8,128)S(1)}, f32[32,1024]{1,0:T(8,128)S(1)}, u32[]{:S(2)}, u32[]{:S(2)}) %collective-permute-start.6) | collective-permute-done | bytes 131104 | tf_op jit(solution)/shard_map/ppermute | solution.py:10
  49.8 2.1 %constant_dynamic-update-slice_fusion.14 = (f32[32,4096]{1,0:T(8,128)S(1)}, f32[32,256]{1,0:T(8,128)S(1)}) fusion(f32[32,256]{1,0:T(8,128)S(1)} %multiply_add_fusion.5, f32[256]{0:T(256)S(1)} %copy-done.1, f32[32,4096]{1,0:T(8,128)S(1)} %multiply_add_fusion.1, f32[4096,256]{1,0:T(8,128)S(1)} %fusion.2), kind=kOutput, calls=%fused_computation.53 | convolution fusion | flops 402669568 | bytes 4817920 | tf_op jit(solution)/shard_map/dot_general | solution.py:54
  51.9 3.0 %collective-permute-start.8 = (f32[32,256]{1,0:T(8,128)S(1)}, f32[32,256]{1,0:T(8,128)S(1)}, u32[]{:S(2)}, u32[]{:S(2)}) collective-permute-start(f32[32,256]{1,0:T(8,128)S(1)} %get-tuple-element.17), channel_id=1, source_target_pairs={{0,8},{1,9},{2,10},{3,11},{4,12},{5,13},{6,14},{7,15},{8,0},{9,1},... | collective-permute-start | bytes 98312 | tf_op jit(solution)/shard_map/ppermute | solution.py:10
  54.9 1.9 %collective-permute-done.8 = f32[32,256]{1,0:T(8,128)S(1)} collective-permute-done((f32[32,256]{1,0:T(8,128)S(1)}, f32[32,256]{1,0:T(8,128)S(1)}, u32[]{:S(2)}, u32[]{:S(2)}) %collective-permute-start.8) | collective-permute-done | bytes 32800 | tf_op jit(solution)/shard_map/ppermute | solution.py:10
  56.8 1.8 %collective-permute-start.9 = (f32[32,512]{1,0:T(8,128)S(1)}, f32[32,512]{1,0:T(8,128)S(1)}, u32[]{:S(2)}, u32[]{:S(2)}) collective-permute-start(f32[32,512]{1,0:T(8,128)S(1)} %pad_maximum_fusion.11), channel_id=1, source_target_pairs={{0,4},{1,5},{2,6},{3,7},{4,0},{5,1},{6,2},{7,3},{8,12},{9,13},{10,... | collective-permute-start | bytes 196616 | tf_op jit(solution)/shard_map/ppermute | solution.py:10
  58.5 2.5 %collective-permute-done.9 = f32[32,512]{1,0:T(8,128)S(1)} collective-permute-done((f32[32,512]{1,0:T(8,128)S(1)}, f32[32,512]{1,0:T(8,128)S(1)}, u32[]{:S(2)}, u32[]{:S(2)}) %collective-permute-start.9) | collective-permute-done | bytes 65568 | tf_op jit(solution)/shard_map/ppermute | solution.py:10
  61.1 1.6 %collective-permute-start.10 = (f32[32,1024]{1,0:T(8,128)S(1)}, f32[32,1024]{1,0:T(8,128)S(1)}, u32[]{:S(2)}, u32[]{:S(2)}) collective-permute-start(f32[32,1024]{1,0:T(8,128)S(1)} %pad_maximum_fusion.7), channel_id=1, source_target_pairs={{0,2},{1,3},{2,0},{3,1},{4,6},{5,7},{6,4},{7,5},{8,10},{9,11},{10,... | collective-permute-start | bytes 393224 | tf_op jit(solution)/shard_map/ppermute | solution.py:10
  62.6 3.4 %collective-permute-done.10 = f32[32,1024]{1,0:T(8,128)S(1)} collective-permute-done((f32[32,1024]{1,0:T(8,128)S(1)}, f32[32,1024]{1,0:T(8,128)S(1)}, u32[]{:S(2)}, u32[]{:S(2)}) %collective-permute-start.10) | collective-permute-done | bytes 131104 | tf_op jit(solution)/shard_map/ppermute | solution.py:10
  68.4 2.3 %constant_dynamic-update-slice_fusion.19 = (f32[32,4096]{1,0:T(8,128)S(1)}, f32[32,256]{1,0:T(8,128)S(1)}) fusion(f32[32,256]{1,0:T(8,128)S(1)} %multiply_subtract_fusion.6, f32[32,256]{1,0:T(8,128)S(1)} %multiply_add_fusion.5, f32[32]{0:T(128)S(1)} %div.58, f32[256]{0:T(256)S(1)} %copy-done.1, f32[32,4096]{1,0:T(8,128)S(1)} %multiply_add_fusion, ...), kind=kOutput, calls=%fused_computation.58 | convolution fusion | flops 402685952 | bytes 4850816 | tf_op jit(solution)/shard_map/dot_general | solution.py:54
  70.7 3.0 %collective-permute-start.12 = (f32[32,256]{1,0:T(8,128)S(1)}, f32[32,256]{1,0:T(8,128)S(1)}, u32[]{:S(2)}, u32[]{:S(2)}) collective-permute-start(f32[32,256]{1,0:T(8,128)S(1)} %get-tuple-element.19), channel_id=1, source_target_pairs={{0,8},{1,9},{2,10},{3,11},{4,12},{5,13},{6,14},{7,15},{8,0},{9,1},... | collective-permute-start | bytes 98312 | tf_op jit(solution)/shard_map/ppermute | solution.py:10
  73.7 1.9 %collective-permute-done.12 = f32[32,256]{1,0:T(8,128)S(1)} collective-permute-done((f32[32,256]{1,0:T(8,128)S(1)}, f32[32,256]{1,0:T(8,128)S(1)}, u32[]{:S(2)}, u32[]{:S(2)}) %collective-permute-start.12) | collective-permute-done | bytes 32800 | tf_op jit(solution)/shard_map/ppermute | solution.py:10
  75.6 1.8 %collective-permute-start.13 = (f32[32,512]{1,0:T(8,128)S(1)}, f32[32,512]{1,0:T(8,128)S(1)}, u32[]{:S(2)}, u32[]{:S(2)}) collective-permute-start(f32[32,512]{1,0:T(8,128)S(1)} %pad_maximum_fusion.12), channel_id=1, source_target_pairs={{0,4},{1,5},{2,6},{3,7},{4,0},{5,1},{6,2},{7,3},{8,12},{9,13},{10,... | collective-permute-start | bytes 196616 | tf_op jit(solution)/shard_map/ppermute | solution.py:10
  77.4 2.5 %collective-permute-done.13 = f32[32,512]{1,0:T(8,128)S(1)} collective-permute-done((f32[32,512]{1,0:T(8,128)S(1)}, f32[32,512]{1,0:T(8,128)S(1)}, u32[]{:S(2)}, u32[]{:S(2)}) %collective-permute-start.13) | collective-permute-done | bytes 65568 | tf_op jit(solution)/shard_map/ppermute | solution.py:10
  79.9 1.6 %collective-permute-start.14 = (f32[32,1024]{1,0:T(8,128)S(1)}, f32[32,1024]{1,0:T(8,128)S(1)}, u32[]{:S(2)}, u32[]{:S(2)}) collective-permute-start(f32[32,1024]{1,0:T(8,128)S(1)} %pad_maximum_fusion.8), channel_id=1, source_target_pairs={{0,2},{1,3},{2,0},{3,1},{4,6},{5,7},{6,4},{7,5},{8,10},{9,11},{10,... | collective-permute-start | bytes 393224 | tf_op jit(solution)/shard_map/ppermute | solution.py:10
  81.4 3.4 %collective-permute-done.14 = f32[32,1024]{1,0:T(8,128)S(1)} collective-permute-done((f32[32,1024]{1,0:T(8,128)S(1)}, f32[32,1024]{1,0:T(8,128)S(1)}, u32[]{:S(2)}, u32[]{:S(2)}) %collective-permute-start.14) | collective-permute-done | bytes 131104 | tf_op jit(solution)/shard_map/ppermute | solution.py:10
  87.1 2.4 %multiply_reduce_fusion.8 = (f32[32]{0:T(128)S(1)}, f32[32,256]{1,0:T(8,128)S(1)}) fusion(f32[32,256]{1,0:T(8,128)S(1)} %multiply_add_fusion.3, f32[256]{0:T(256)S(1)} %copy-done.1, f32[4096,256]{1,0:T(8,128)S(1)} %fusion.2, f32[32,4096]{1,0:T(8,128)S(1)} %multiply_add_fusion, f32[32]{0:T(128)S(1)} %div.60, f32[32,4096]{1,0:T(8,128)S(1)} %get-tuple-element.5, ...), kind=kOutput, calls=%fused_computation.61 | convolution fusion | flops 403210208 | bytes 5834112 | tf_op jit(solution)/shard_map/dot_general | solution.py:54
  89.4 3.0 %collective-permute-start.16 = (f32[32]{0:T(128)S(1)}, f32[32]{0:T(128)S(1)}, u32[]{:S(2)}, u32[]{:S(2)}) collective-permute-start(f32[32]{0:T(128)S(1)} %get-tuple-element.20), channel_id=1, source_target_pairs={{0,8},{1,9},{2,10},{3,11},{4,12},{5,13},{6,14},{7,15},{8,0},{9,1},... | collective-permute-start | bytes 392 | tf_op jit(solution)/shard_map/ppermute | solution.py:10
  94.0 1.8 %collective-permute-start.17 = (f32[32]{0:T(128)S(1)}, f32[32]{0:T(128)S(1)}, u32[]{:S(2)}, u32[]{:S(2)}) collective-permute-start(f32[32]{0:T(128)S(1)} %add.79), channel_id=1, source_target_pairs={{0,4},{1,5},{2,6},{3,7},{4,0},{5,1},{6,2},{7,3},{8,12},{9,13},{10,... | collective-permute-start | bytes 392 | tf_op jit(solution)/shard_map/ppermute | solution.py:10
  95.8 1.7 %collective-permute-done.17 = f32[32]{0:T(128)S(1)} collective-permute-done((f32[32]{0:T(128)S(1)}, f32[32]{0:T(128)S(1)}, u32[]{:S(2)}, u32[]{:S(2)}) %collective-permute-start.17) | collective-permute-done | bytes 160 | tf_op jit(solution)/shard_map/ppermute | solution.py:10
  99.0 2.0 %collective-permute-done.18 = f32[32]{0:T(128)S(1)} collective-permute-done((f32[32]{0:T(128)S(1)}, f32[32]{0:T(128)S(1)}, u32[]{:S(2)}, u32[]{:S(2)}) %collective-permute-start.18) | collective-permute-done | bytes 160 | tf_op jit(solution)/shard_map/ppermute | solution.py:10
  (70 shorter events, 17.9 us)
Async XLA Ops:
  2.3 7.8 %collective-permute-start = (f32[64,256]{1,0:T(8,128)S(1)}, f32[64,256]{1,0:T(8,128)S(1)}, u32[]{:S(2)}, u32[]{:S(2)}) collective-permute-start(f32[64,256]{1,0:T(8,128)S(1)} %get-tuple-element.10), channel_id=1, source_target_pairs={{0,8},{1,9},{2,10},{3,11},{4,12},{5,13},{6,14},{7,15},{8,0},{9,1},... | collective-permute-start | bytes 196616 | tf_op jit(solution)/shard_map/ppermute | solution.py:10
  10.8 5.0 %collective-permute-start.1 = (f32[64,512]{1,0:T(8,128)S(1)}, f32[64,512]{1,0:T(8,128)S(1)}, u32[]{:S(2)}, u32[]{:S(2)}) collective-permute-start(f32[64,512]{1,0:T(8,128)S(1)} %pad_maximum_fusion.5), channel_id=1, source_target_pairs={{0,4},{1,5},{2,6},{3,7},{4,0},{5,1},{6,2},{7,3},{8,12},{9,13},{10,... | collective-permute-start | bytes 393224 | tf_op jit(solution)/shard_map/ppermute | solution.py:10
  16.6 14.2 %copy-start = (f32[32,256]{1,0:T(8,128)S(1)}, f32[32,256]{1,0:T(8,128)}, u32[]{:S(2)}) copy-start(f32[32,256]{1,0:T(8,128)} %param.7) | copy-start | bytes 98308
  16.6 14.2 %copy-start.1 = (f32[256]{0:T(256)S(1)}, f32[256]{0:T(256)}, u32[]{:S(2)}) copy-start(f32[256]{0:T(256)} %param.6) | copy-start | bytes 3076
  16.6 6.4 %collective-permute-start.2 = (f32[64,1024]{1,0:T(8,128)S(1)}, f32[64,1024]{1,0:T(8,128)S(1)}, u32[]{:S(2)}, u32[]{:S(2)}) collective-permute-start(f32[64,1024]{1,0:T(8,128)S(1)} %pad_maximum_fusion.1), channel_id=1, source_target_pairs={{0,2},{1,3},{2,0},{3,1},{4,6},{5,7},{6,4},{7,5},{8,10},{9,11},{10,... | collective-permute-start | bytes 786440 | tf_op jit(solution)/shard_map/ppermute | solution.py:10
  23.8 2.0 %collective-permute-start.3 = (f32[64,2048]{1,0:T(8,128)S(1)}, f32[64,2048]{1,0:T(8,128)S(1)}, u32[]{:S(2)}, u32[]{:S(2)}) collective-permute-start(f32[64,2048]{1,0:T(8,128)S(1)} %pad_maximum_fusion), channel_id=1, source_target_pairs={{0,1},{1,0},{2,3},{3,2},{4,5},{5,4},{6,7},{7,6},{8,9},{9,8},{10,11... | collective-permute-start | bytes 1572872 | tf_op jit(solution)/shard_map/ppermute | solution.py:10
  32.9 5.2 %collective-permute-start.4 = (f32[32,256]{1,0:T(8,128)S(1)}, f32[32,256]{1,0:T(8,128)S(1)}, u32[]{:S(2)}, u32[]{:S(2)}) collective-permute-start(f32[32,256]{1,0:T(8,128)S(1)} %get-tuple-element.15), channel_id=1, source_target_pairs={{0,8},{1,9},{2,10},{3,11},{4,12},{5,13},{6,14},{7,15},{8,0},{9,1},... | collective-permute-start | bytes 98312 | tf_op jit(solution)/shard_map/ppermute | solution.py:10
  38.1 4.3 %collective-permute-start.5 = (f32[32,512]{1,0:T(8,128)S(1)}, f32[32,512]{1,0:T(8,128)S(1)}, u32[]{:S(2)}, u32[]{:S(2)}) collective-permute-start(f32[32,512]{1,0:T(8,128)S(1)} %pad_maximum_fusion.10), channel_id=1, source_target_pairs={{0,4},{1,5},{2,6},{3,7},{4,0},{5,1},{6,2},{7,3},{8,12},{9,13},{10,... | collective-permute-start | bytes 196616 | tf_op jit(solution)/shard_map/ppermute | solution.py:10
  42.4 5.0 %collective-permute-start.6 = (f32[32,1024]{1,0:T(8,128)S(1)}, f32[32,1024]{1,0:T(8,128)S(1)}, u32[]{:S(2)}, u32[]{:S(2)}) collective-permute-start(f32[32,1024]{1,0:T(8,128)S(1)} %pad_maximum_fusion.6), channel_id=1, source_target_pairs={{0,2},{1,3},{2,0},{3,1},{4,6},{5,7},{6,4},{7,5},{8,10},{9,11},{10,... | collective-permute-start | bytes 393224 | tf_op jit(solution)/shard_map/ppermute | solution.py:10
  47.5 1.6 %collective-permute-start.7 = (f32[32,2048]{1,0:T(8,128)S(1)}, f32[32,2048]{1,0:T(8,128)S(1)}, u32[]{:S(2)}, u32[]{:S(2)}) collective-permute-start(f32[32,2048]{1,0:T(8,128)S(1)} %pad_maximum_fusion.2), channel_id=1, source_target_pairs={{0,1},{1,0},{2,3},{3,2},{4,5},{5,4},{6,7},{7,6},{8,9},{9,8},{10,11... | collective-permute-start | bytes 786440 | tf_op jit(solution)/shard_map/ppermute | solution.py:10
  51.9 4.9 %collective-permute-start.8 = (f32[32,256]{1,0:T(8,128)S(1)}, f32[32,256]{1,0:T(8,128)S(1)}, u32[]{:S(2)}, u32[]{:S(2)}) collective-permute-start(f32[32,256]{1,0:T(8,128)S(1)} %get-tuple-element.17), channel_id=1, source_target_pairs={{0,8},{1,9},{2,10},{3,11},{4,12},{5,13},{6,14},{7,15},{8,0},{9,1},... | collective-permute-start | bytes 98312 | tf_op jit(solution)/shard_map/ppermute | solution.py:10
  56.8 4.3 %collective-permute-start.9 = (f32[32,512]{1,0:T(8,128)S(1)}, f32[32,512]{1,0:T(8,128)S(1)}, u32[]{:S(2)}, u32[]{:S(2)}) collective-permute-start(f32[32,512]{1,0:T(8,128)S(1)} %pad_maximum_fusion.11), channel_id=1, source_target_pairs={{0,4},{1,5},{2,6},{3,7},{4,0},{5,1},{6,2},{7,3},{8,12},{9,13},{10,... | collective-permute-start | bytes 196616 | tf_op jit(solution)/shard_map/ppermute | solution.py:10
  61.1 5.0 %collective-permute-start.10 = (f32[32,1024]{1,0:T(8,128)S(1)}, f32[32,1024]{1,0:T(8,128)S(1)}, u32[]{:S(2)}, u32[]{:S(2)}) collective-permute-start(f32[32,1024]{1,0:T(8,128)S(1)} %pad_maximum_fusion.7), channel_id=1, source_target_pairs={{0,2},{1,3},{2,0},{3,1},{4,6},{5,7},{6,4},{7,5},{8,10},{9,11},{10,... | collective-permute-start | bytes 393224 | tf_op jit(solution)/shard_map/ppermute | solution.py:10
  66.1 1.6 %collective-permute-start.11 = (f32[32,2048]{1,0:T(8,128)S(1)}, f32[32,2048]{1,0:T(8,128)S(1)}, u32[]{:S(2)}, u32[]{:S(2)}) collective-permute-start(f32[32,2048]{1,0:T(8,128)S(1)} %pad_maximum_fusion.3), channel_id=1, source_target_pairs={{0,1},{1,0},{2,3},{3,2},{4,5},{5,4},{6,7},{7,6},{8,9},{9,8},{10,11... | collective-permute-start | bytes 786440 | tf_op jit(solution)/shard_map/ppermute | solution.py:10
  70.7 4.9 %collective-permute-start.12 = (f32[32,256]{1,0:T(8,128)S(1)}, f32[32,256]{1,0:T(8,128)S(1)}, u32[]{:S(2)}, u32[]{:S(2)}) collective-permute-start(f32[32,256]{1,0:T(8,128)S(1)} %get-tuple-element.19), channel_id=1, source_target_pairs={{0,8},{1,9},{2,10},{3,11},{4,12},{5,13},{6,14},{7,15},{8,0},{9,1},... | collective-permute-start | bytes 98312 | tf_op jit(solution)/shard_map/ppermute | solution.py:10
  75.6 4.3 %collective-permute-start.13 = (f32[32,512]{1,0:T(8,128)S(1)}, f32[32,512]{1,0:T(8,128)S(1)}, u32[]{:S(2)}, u32[]{:S(2)}) collective-permute-start(f32[32,512]{1,0:T(8,128)S(1)} %pad_maximum_fusion.12), channel_id=1, source_target_pairs={{0,4},{1,5},{2,6},{3,7},{4,0},{5,1},{6,2},{7,3},{8,12},{9,13},{10,... | collective-permute-start | bytes 196616 | tf_op jit(solution)/shard_map/ppermute | solution.py:10
  79.9 5.0 %collective-permute-start.14 = (f32[32,1024]{1,0:T(8,128)S(1)}, f32[32,1024]{1,0:T(8,128)S(1)}, u32[]{:S(2)}, u32[]{:S(2)}) collective-permute-start(f32[32,1024]{1,0:T(8,128)S(1)} %pad_maximum_fusion.8), channel_id=1, source_target_pairs={{0,2},{1,3},{2,0},{3,1},{4,6},{5,7},{6,4},{7,5},{8,10},{9,11},{10,... | collective-permute-start | bytes 393224 | tf_op jit(solution)/shard_map/ppermute | solution.py:10
  84.9 1.6 %collective-permute-start.15 = (f32[32,2048]{1,0:T(8,128)S(1)}, f32[32,2048]{1,0:T(8,128)S(1)}, u32[]{:S(2)}, u32[]{:S(2)}) collective-permute-start(f32[32,2048]{1,0:T(8,128)S(1)} %pad_maximum_fusion.4), channel_id=1, source_target_pairs={{0,1},{1,0},{2,3},{3,2},{4,5},{5,4},{6,7},{7,6},{8,9},{9,8},{10,11... | collective-permute-start | bytes 786440 | tf_op jit(solution)/shard_map/ppermute | solution.py:10
  89.4 4.5 %collective-permute-start.16 = (f32[32]{0:T(128)S(1)}, f32[32]{0:T(128)S(1)}, u32[]{:S(2)}, u32[]{:S(2)}) collective-permute-start(f32[32]{0:T(128)S(1)} %get-tuple-element.20), channel_id=1, source_target_pairs={{0,8},{1,9},{2,10},{3,11},{4,12},{5,13},{6,14},{7,15},{8,0},{9,1},... | collective-permute-start | bytes 392 | tf_op jit(solution)/shard_map/ppermute | solution.py:10
  94.0 3.5 %collective-permute-start.17 = (f32[32]{0:T(128)S(1)}, f32[32]{0:T(128)S(1)}, u32[]{:S(2)}, u32[]{:S(2)}) collective-permute-start(f32[32]{0:T(128)S(1)} %add.79), channel_id=1, source_target_pairs={{0,4},{1,5},{2,6},{3,7},{4,0},{5,1},{6,2},{7,3},{8,12},{9,13},{10,... | collective-permute-start | bytes 392 | tf_op jit(solution)/shard_map/ppermute | solution.py:10
  97.5 3.5 %collective-permute-start.18 = (f32[32]{0:T(128)S(1)}, f32[32]{0:T(128)S(1)}, u32[]{:S(2)}, u32[]{:S(2)}) collective-permute-start(f32[32]{0:T(128)S(1)} %add.80), channel_id=1, source_target_pairs={{0,2},{1,3},{2,0},{3,1},{4,6},{5,7},{6,4},{7,5},{8,10},{9,11},{10,... | collective-permute-start | bytes 392 | tf_op jit(solution)/shard_map/ppermute | solution.py:10
  101.0 1.1 %collective-permute-start.19 = (f32[32]{0:T(128)S(1)}, f32[32]{0:T(128)S(1)}, u32[]{:S(2)}, u32[]{:S(2)}) collective-permute-start(f32[32]{0:T(128)S(1)} %add.81), channel_id=1, source_target_pairs={{0,1},{1,0},{2,3},{3,2},{4,5},{5,4},{6,7},{7,6},{8,9},{9,8},{10,11... | collective-permute-start | bytes 392 | tf_op jit(solution)/shard_map/ppermute | solution.py:10

commit v3 on v2

v3 whole, which is shorter than its diff:
```python
import jax
import jax.numpy as jnp
from jax import lax
from jax.sharding import PartitionSpec as P

ITERS = 4
TILE_BYTES = 16 << 20


def swap(x, n, stride):
    return lax.ppermute(x, "blk", [(i, i ^ stride) for i in range(n)])


def gather(x, n, strides):
    for stride in strides:
        x = jnp.concatenate([x, swap(x, n, stride)], axis=1)
    return x


def add_up(x, n, strides):
    for stride in strides:
        x = x + swap(x, n, stride)
    return x


def split(x, parts):
    out = []
    for _ in range(parts):
        high = lax.reduce_precision(x, 8, 7)
        out.append(high.astype(jnp.bfloat16))
        x = x - high
    return out


def kernel_block(pts, cols):
    high, mid, low = split(pts, 3)
    norms = split(-0.5 * jnp.sum(pts * pts, axis=0, keepdims=True), 3)
    ones = [jnp.ones_like(norms[0])] * 3
    left = jnp.concatenate([high, high, mid, high, low, mid] + norms + ones, axis=0)
    right = jnp.concatenate([high, mid, high, low, high, mid] + ones + norms, axis=0)[:, :cols]
    tile = jnp.exp(lax.dot_general(left, right, (((0,), (0,)), ((), ())), preferred_element_type=jnp.float32))
    return split(tile, 2)


def apply_block(direction, tile):
    rows = direction.shape[0]
    parts = split(direction, 3)
    high = jnp.dot(jnp.concatenate(parts, axis=0), tile[0], preferred_element_type=jnp.float32)
    low = jnp.dot(jnp.concatenate(parts[:2], axis=0), tile[1], preferred_element_type=jnp.float32)
    return high[:rows] + ((high[rows : 2 * rows] + low[:rows]) + (high[2 * rows :] + low[rows:]))


def solution(mesh):
    n = mesh.shape["blk"]
    strides = [1 << k for k in reversed(range(n.bit_length() - 1))]

    def body(points, lengthscale, noise_var, targets):
        feats, width = points.shape
        team = min(n, 4)
        while team < n and (n * width) * (n * width) // team * 4 > TILE_BYTES:
            team *= 2
        outer, inner = [s for s in strides if s >= team], [s for s in strides if s < team]
        cols = n // team * width

        scaled = points / lengthscale[:, None]
        mine = gather(jnp.concatenate([scaled, targets, noise_var[None, :]], axis=0), n, outer)
        noise = mine[-1:]
        both = gather(mine[:-1], n, inner)
        tile = kernel_block(both[:feats], cols)

        residual = direction = both[feats:]
        my_solution = jnp.zeros_like(targets)
        norm_now = jnp.sum(residual * residual, axis=1)
        for iteration in range(ITERS):
            my_applied = apply_block(direction, tile) + noise * direction[:, :cols]
            if iteration == ITERS - 1:
                curve = add_up(jnp.sum(direction[:, :cols] * my_applied, axis=1), n, inner)
                step_size = (norm_now / curve)[:, None]
                my_solution = my_solution + step_size * direction[:, :width]
                return my_solution, residual[:, :width] - step_size * my_applied[:, :width]
            applied = gather(my_applied, n, inner)
            curve = jnp.sum(direction * applied, axis=1)
            step_size = (norm_now / curve)[:, None]
            my_solution = my_solution + step_size * direction[:, :width]
            residual = residual - step_size * applied
            norm_next = jnp.sum(residual * residual, axis=1)
            direction = residual + (norm_next / norm_now)[:, None] * direction
            norm_now = norm_next

    in_specs = (P("groups", "blk"), P("groups"), P(("groups", "blk")), P("groups", "blk"))
    out_specs = (P("groups", "blk"), P("groups", "blk"))
    return jax.shard_map(body, mesh=mesh, in_specs=in_specs, out_specs=out_specs, check_vma=False)
```

time: 103 us -> 86.3 us (0.84)
  starting transfers between devices: 32.1 us -> 14 us
  waiting for transfers between devices: 49.2 us -> 33.1 us
  local copies, waits for them, and re-layouts: 0.21 us -> 10.1 us
  matrix products: 13.7 us -> 18.3 us
  other arithmetic: 6.73 us -> 9.17 us
    ppermute x20 -> x12, starting transfers between devices: 32.1 us -> 14 us  [swap(): return lax.ppermute(x, 'blk', [(i, i ^ stride) for i in range(n)])]
    ppermute x20 -> x12, waiting for transfers between devices: 49.2 us -> 33.1 us  [swap(): return lax.ppermute(x, 'blk', [(i, i ^ stride) for i in range(n)])]
    concatenate x4 -> x2, local copies, waits for them, and re-layouts: 0.09 us -> 7.48 us  [the longest x1 6.07 us: kernel_block(): jnp.concatenate([high, high, mid, high, low, mid] + norms + ones, axis=0)]
    dot_general x5 -> x9, matrix products: 13.7 us -> 18.3 us  [the longest x4 6.32 us: apply_block(): jnp.dot(jnp.concatenate(parts[:2], axis=0), tile[1], preferred_element_ty...]
    convert_element_type x0 -> x8, other arithmetic: none -> 2.59 us  [split(): out.append(high.astype(jnp.bfloat16))]
    unnamed x16 -> x24, local copies, waits for them, and re-layouts: 0.12 us -> 1.96 us
    concatenate x12 -> x7, other arithmetic: 2.44 us -> 1.79 us  [gather(): x = jnp.concatenate([x, swap(x, n, stride)], axis=1)]
  transfers between devices with their start and end apart: 20 -> 12, of which waited for: 20 -> 12; matrix products, arithmetic and copies ran while one was open for 0% -> 1% of each run, Pallas kernels for 0% -> 0%
where the time goes in v3:
time: 86.3 us; the launch traced here: 85.6 us
  waiting for transfers between devices  33.1 us (38%)
  matrix products  18.3 us (21%)
  starting transfers between devices  14 us (16%)
  local copies, waits for them, and re-layouts  10.1 us (12%)
  other arithmetic  9.17 us (11%)
  between operations  0.95 us (1%)
    ppermute x12, waiting for transfers between devices, swap(): return lax.ppermute(x, 'blk', [(i, i ^ stride) for i in range(n)])  33.1 us
    ppermute x12, starting transfers between devices, swap(): return lax.ppermute(x, 'blk', [(i, i ^ stride) for i in range(n)])  14 us
    dot_general x4, matrix products, apply_block(): jnp.dot(jnp.concatenate(parts[:2], axis=0), tile[1], preferred_element_ty...  6.32 us
    concatenate x1, local copies, waits for them, and re-layouts, kernel_block(): jnp.concatenate([high, high, mid, high, low, mid] + norms + ones, axis=0)  6.07 us
    dot_general x4, matrix products, apply_block(): jnp.dot(jnp.concatenate(parts, axis=0), tile[0], preferred_element_type=j...  6.02 us
    dot_general x1, matrix products, kernel_block(): lax.dot_general(left, right, (((0,), (0,)), ((), ())), preferred_element_...  5.92 us
    convert_element_type x8, other arithmetic, split(): out.append(high.astype(jnp.bfloat16))  2.59 us
    unnamed x24, local copies, waits for them, and re-layouts  1.96 us
  transfers between devices with their start and end apart: 12, of which 12 were waited for; matrix products, arithmetic and copies ran while one was open for 1% of the time, Pallas kernels for 0%

profile of v3, /device:TPU:0, one launch (start us, length us, event | category | flops | bytes accessed | tf_op | source)
XLA Modules:
  0.0 85.6 jit_solution(9540594440478943015)
XLA Ops:
  2.3 4.0 %collective-permute-start = (f32[65,256]{1,0:T(8,128)S(1)}, f32[65,256]{1,0:T(8,128)S(1)}, u32[]{:S(2)}, u32[]{:S(2)}) collective-permute-start(f32[65,256]{1,0:T(8,128)S(1)} %pad_maximum_fusion.10), channel_id=1, source_target_pairs={{0,8},{1,9},{2,10},{3,11},{4,12},{5,13},{6,14},{7,15},{8,0},{9,1},... | collective-permute-start | bytes 199688 | tf_op jit(solution)/shard_map/ppermute | solution.py:11
  6.3 3.9 %collective-permute-done = f32[65,256]{1,0:T(8,128)S(1)} collective-permute-done((f32[65,256]{1,0:T(8,128)S(1)}, f32[65,256]{1,0:T(8,128)S(1)}, u32[]{:S(2)}, u32[]{:S(2)}) %collective-permute-start) | collective-permute-done | bytes 66592 | tf_op jit(solution)/shard_map/ppermute | solution.py:11
  11.7 4.5 %collective-permute-done.1 = f32[65,512]{1,0:T(8,128)S(1)} collective-permute-done((f32[65,512]{1,0:T(8,128)S(1)}, f32[65,512]{1,0:T(8,128)S(1)}, u32[]{:S(2)}, u32[]{:S(2)}) %collective-permute-start.1) | collective-permute-done | bytes 133152 | tf_op jit(solution)/shard_map/ppermute | solution.py:11
  16.2 0.8 pad_maximum_fusion.5
  17.1 1.8 %collective-permute-start.2 = (f32[64,1024]{1,0:T(8,128)S(1)}, f32[64,1024]{1,0:T(8,128)S(1)}, u32[]{:S(2)}, u32[]{:S(2)}) collective-permute-start(f32[64,1024]{1,0:T(8,128)S(1)} %slice.145), channel_id=1, source_target_pairs={{0,2},{1,3},{2,0},{3,1},{4,6},{5,7},{6,4},{7,5},{8,10},{9,11},{10,... | collective-permute-start | bytes 786440 | tf_op jit(solution)/shard_map/ppermute | solution.py:11
  18.9 4.6 %collective-permute-done.2 = f32[64,1024]{1,0:T(8,128)S(1)} collective-permute-done((f32[64,1024]{1,0:T(8,128)S(1)}, f32[64,1024]{1,0:T(8,128)S(1)}, u32[]{:S(2)}, u32[]{:S(2)}) %collective-permute-start.2) | collective-permute-done | bytes 262176 | tf_op jit(solution)/shard_map/ppermute | solution.py:11
  24.4 1.2 %collective-permute-done.3 = f32[64,2048]{1,0:T(8,128)S(1)} collective-permute-done((f32[64,2048]{1,0:T(8,128)S(1)}, f32[64,2048]{1,0:T(8,128)S(1)}, u32[]{:S(2)}, u32[]{:S(2)}) %collective-permute-start.3) | collective-permute-done | bytes 524320 | tf_op jit(solution)/shard_map/ppermute | solution.py:11
  25.6 1.1 %fusion.27 = (bf16[32,4096]{1,0:T(8,128)(2,1)}, bf16[32,4096]{1,0:T(8,128)(2,1)}, bf16[32,4096]{1,0:T(8,128)(2,1)S(1)}, f32[4096]{0:T(1024)S(1)}, bf16[32,4096]{...) fusion(f32[64,4096]{1,0:T(8,128)S(1)} %pad_maximum_fusion), kind=kLoop, calls=%fused_computation.50 | loop fusion | flops 2355200 | bytes 2637824 | tf_op jit(solution)/shard_map/convert_element_type | solution.py:30
  28.1 1.4 %concatenate.75 = bf16[198,4096]{1,0:T(8,128)(2,1)S(1)} concatenate(bf16[32,4096]{1,0:T(8,128)(2,1)S(1)} %get-tuple-element.25, bf16[32,4096]{1,0:T(8,128)(2,1)S(1)} %get-tuple-element.22, bf16[32,4096]{1,0:T(8,128)(2,1)S(1)} %get-tuple-element.25, bf16[32,4096]{1,0:T(8,128)(2,1)S(1)} %get-tuple-element.24, bf16[32,4096]{1,0:T(8,128)(2,1)S(1)} %get-tuple-element.25, ...), dimensions={0} | concatenate | bytes 3244032 | tf_op jit(solution)/shard_map/concatenate | solution.py:40
  29.5 6.1 %concatenate.74 = bf16[198,4096]{1,0:T(8,128)(2,1)} concatenate(bf16[32,4096]{1,0:T(8,128)(2,1)S(1)} %get-tuple-element.25, bf16[32,4096]{1,0:T(8,128)(2,1)S(1)} %get-tuple-element.25, bf16[32,4096]{1,0:T(8,128)(2,1)S(1)} %get-tuple-element.22, bf16[32,4096]{1,0:T(8,128)(2,1)S(1)} %get-tuple-element.25, bf16[32,4096]{1,0:T(8,128)(2,1)S(1)} %get-tuple-element.24, ...), dimensions={0} | concatenate | bytes 3244032 | tf_op jit(solution)/shard_map/concatenate | solution.py:39
  35.5 5.9 %reduce-precision_convert_fusion = (bf16[4096,1024]{1,0:T(8,128)(2,1)S(1)}, bf16[4096,1024]{1,0:T(8,128)(2,1)S(1)}) fusion(bf16[198,4096]{1,0:T(8,128)(2,1)} %concatenate.74, bf16[198,4096]{1,0:T(8,128)(2,1)S(1)} %concatenate.75), kind=kOutput, calls=%fused_computation.1 | convolution fusion | flops 1681915904 | bytes 18808832 | tf_op jit(solution)/shard_map/dot_general | solution.py:41
  41.5 1.6 %fusion.36 = f32[64,1024]{1,0:T(8,128)S(1)} fusion(bf16[4096,1024]{1,0:T(8,128)(2,1)S(1)} %get-tuple-element.19, bf16[32,4096]{1,0:T(8,128)(2,1)S(1)} %copy-done.5, bf16[32,4096]{1,0:T(8,128)(2,1)S(1)} %copy-done.6), kind=kOutput, calls=%fused_computation.60 | convolution fusion | flops 537919488 | bytes 9175040 | tf_op jit(solution)/shard_map/dot_general | solution.py:49
  43.2 1.5 %fusion.2 = f32[96,1024]{1,0:T(8,128)S(1)} fusion(bf16[4096,1024]{1,0:T(8,128)(2,1)S(1)} %get-tuple-element.18, bf16[32,4096]{1,0:T(8,128)(2,1)S(1)} %copy-done.7, bf16[32,4096]{1,0:T(8,128)(2,1)S(1)} %copy-done.5, bf16[32,4096]{1,0:T(8,128)(2,1)S(1)} %copy-done.6), kind=kOutput, calls=%fused_computation.5 | convolution fusion | flops 807665664 | bytes 9568256 | tf_op jit(solution)/shard_map/dot_general | solution.py:48
  44.8 1.8 %collective-permute-start.4 = (f32[32,1024]{1,0:T(8,128)S(1)}, f32[32,1024]{1,0:T(8,128)S(1)}, u32[]{:S(2)}, u32[]{:S(2)}) collective-permute-start(f32[32,1024]{1,0:T(8,128)S(1)} %fusion.63), channel_id=1, source_target_pairs={{0,2},{1,3},{2,0},{3,1},{4,6},{5,7},{6,4},{7,5},{8,10},{9,11},{10,... | collective-permute-start | bytes 393224 | tf_op jit(solution)/shard_map/ppermute | solution.py:11
  46.6 3.8 %collective-permute-done.4 = f32[32,1024]{1,0:T(8,128)S(1)} collective-permute-done((f32[32,1024]{1,0:T(8,128)S(1)}, f32[32,1024]{1,0:T(8,128)S(1)}, u32[]{:S(2)}, u32[]{:S(2)}) %collective-permute-start.4) | collective-permute-done | bytes 131104 | tf_op jit(solution)/shard_map/ppermute | solution.py:11
  50.5 1.5 %collective-permute-done.5 = f32[32,2048]{1,0:T(8,128)S(1)} collective-permute-done((f32[32,2048]{1,0:T(8,128)S(1)}, f32[32,2048]{1,0:T(8,128)S(1)}, u32[]{:S(2)}, u32[]{:S(2)}) %collective-permute-start.5) | collective-permute-done | bytes 262176 | tf_op jit(solution)/shard_map/ppermute | solution.py:11
  52.8 1.6 %fusion.40 = f32[64,1024]{1,0:T(8,128)S(1)} fusion(bf16[4096,1024]{1,0:T(8,128)(2,1)S(1)} %get-tuple-element.19, bf16[32,4096]{1,0:T(8,128)(2,1)S(1)} %get-tuple-element.32, bf16[32,4096]{1,0:T(8,128)(2,1)S(1)} %get-tuple-element.31), kind=kOutput, calls=%fused_computation.65 | convolution fusion | flops 537919488 | bytes 9175040 | tf_op jit(solution)/shard_map/dot_general | solution.py:49
  55.0 1.3 %slice-done.1 = s8[4194304]{0:T(1024)(128)(4,1)S(1)} async-done(((s8[8388608]{0:T(1024)(128)(4,1)}), s8[4194304]{0:T(1024)(128)(4,1)S(1)}, s32[]{:S(2)}) %slice-start.1) | async-done | bytes 4194328
  56.2 1.5 %fusion.8 = f32[96,1024]{1,0:T(8,128)S(1)} fusion(bf16[4096,1024]{1,0:T(8,128)(2,1)S(1)} %bitcast.23, bf16[32,4096]{1,0:T(8,128)(2,1)S(1)} %get-tuple-element.14, bf16[32,4096]{1,0:T(8,128)(2,1)S(1)} %get-tuple-element.32, bf16[32,4096]{1,0:T(8,128)(2,1)S(1)} %get-tuple-element.31), kind=kOutput, calls=%fused_computation.11 | convolution fusion | flops 807665664 | bytes 9568256 | tf_op jit(solution)/shard_map/dot_general | solution.py:48
  57.8 1.8 %collective-permute-start.6 = (f32[32,1024]{1,0:T(8,128)S(1)}, f32[32,1024]{1,0:T(8,128)S(1)}, u32[]{:S(2)}, u32[]{:S(2)}) collective-permute-start(f32[32,1024]{1,0:T(8,128)S(1)} %fusion.60), channel_id=1, source_target_pairs={{0,2},{1,3},{2,0},{3,1},{4,6},{5,7},{6,4},{7,5},{8,10},{9,11},{10,... | collective-permute-start | bytes 393224 | tf_op jit(solution)/shard_map/ppermute | solution.py:11
  59.6 3.8 %collective-permute-done.6 = f32[32,1024]{1,0:T(8,128)S(1)} collective-permute-done((f32[32,1024]{1,0:T(8,128)S(1)}, f32[32,1024]{1,0:T(8,128)S(1)}, u32[]{:S(2)}, u32[]{:S(2)}) %collective-permute-start.6) | collective-permute-done | bytes 131104 | tf_op jit(solution)/shard_map/ppermute | solution.py:11
  63.5 1.5 %collective-permute-done.7 = f32[32,2048]{1,0:T(8,128)S(1)} collective-permute-done((f32[32,2048]{1,0:T(8,128)S(1)}, f32[32,2048]{1,0:T(8,128)S(1)}, u32[]{:S(2)}, u32[]{:S(2)}) %collective-permute-start.7) | collective-permute-done | bytes 262176 | tf_op jit(solution)/shard_map/ppermute | solution.py:11
  65.8 1.6 %fusion.44 = f32[64,1024]{1,0:T(8,128)S(1)} fusion(bf16[4096,1024]{1,0:T(8,128)(2,1)S(1)} %get-tuple-element.19, bf16[32,4096]{1,0:T(8,128)(2,1)S(1)} %get-tuple-element.30, bf16[32,4096]{1,0:T(8,128)(2,1)S(1)} %get-tuple-element.29), kind=kOutput, calls=%fused_computation.70 | convolution fusion | flops 537919488 | bytes 9175040 | tf_op jit(solution)/shard_map/dot_general | solution.py:49
  67.4 1.5 %fusion.14 = f32[96,1024]{1,0:T(8,128)S(1)} fusion(bf16[4096,1024]{1,0:T(8,128)(2,1)S(1)} %bitcast.23, bf16[32,4096]{1,0:T(8,128)(2,1)S(1)} %get-tuple-element.10, bf16[32,4096]{1,0:T(8,128)(2,1)S(1)} %get-tuple-element.30, bf16[32,4096]{1,0:T(8,128)(2,1)S(1)} %get-tuple-element.29), kind=kOutput, calls=%fused_computation.17 | convolution fusion | flops 807665664 | bytes 9568256 | tf_op jit(solution)/shard_map/dot_general | solution.py:48
  68.9 1.8 %collective-permute-start.8 = (f32[32,1024]{1,0:T(8,128)S(1)}, f32[32,1024]{1,0:T(8,128)S(1)}, u32[]{:S(2)}, u32[]{:S(2)}) collective-permute-start(f32[32,1024]{1,0:T(8,128)S(1)} %fusion.57), channel_id=1, source_target_pairs={{0,2},{1,3},{2,0},{3,1},{4,6},{5,7},{6,4},{7,5},{8,10},{9,11},{10,... | collective-permute-start | bytes 393224 | tf_op jit(solution)/shard_map/ppermute | solution.py:11
  70.7 3.8 %collective-permute-done.8 = f32[32,1024]{1,0:T(8,128)S(1)} collective-permute-done((f32[32,1024]{1,0:T(8,128)S(1)}, f32[32,1024]{1,0:T(8,128)S(1)}, u32[]{:S(2)}, u32[]{:S(2)}) %collective-permute-start.8) | collective-permute-done | bytes 131104 | tf_op jit(solution)/shard_map/ppermute | solution.py:11
  74.6 1.5 %collective-permute-done.9 = f32[32,2048]{1,0:T(8,128)S(1)} collective-permute-done((f32[32,2048]{1,0:T(8,128)S(1)}, f32[32,2048]{1,0:T(8,128)S(1)}, u32[]{:S(2)}, u32[]{:S(2)}) %collective-permute-start.9) | collective-permute-done | bytes 262176 | tf_op jit(solution)/shard_map/ppermute | solution.py:11
  76.9 1.6 %fusion.48 = f32[64,1024]{1,0:T(8,128)S(1)} fusion(bf16[4096,1024]{1,0:T(8,128)(2,1)S(1)} %get-tuple-element.19, bf16[32,4096]{1,0:T(8,128)(2,1)S(1)} %get-tuple-element.28, bf16[32,4096]{1,0:T(8,128)(2,1)S(1)} %get-tuple-element.27), kind=kOutput, calls=%fused_computation.75 | convolution fusion | flops 537919488 | bytes 9175040 | tf_op jit(solution)/shard_map/dot_general | solution.py:49
  78.5 1.5 %fusion.20 = f32[96,1024]{1,0:T(8,128)S(1)} fusion(bf16[4096,1024]{1,0:T(8,128)(2,1)S(1)} %bitcast.23, bf16[32,4096]{1,0:T(8,128)(2,1)S(1)} %get-tuple-element.6, bf16[32,4096]{1,0:T(8,128)(2,1)S(1)} %get-tuple-element.28, bf16[32,4096]{1,0:T(8,128)(2,1)S(1)} %get-tuple-element.27), kind=kOutput, calls=%fused_computation.23 | convolution fusion | flops 807665664 | bytes 9568256 | tf_op jit(solution)/shard_map/dot_general | solution.py:48
  80.2 1.8 %collective-permute-start.10 = (f32[32]{0:T(128)S(1)}, f32[32]{0:T(128)S(1)}, u32[]{:S(2)}, u32[]{:S(2)}) collective-permute-start(f32[32]{0:T(128)S(1)} %get-tuple-element.4), channel_id=1, source_target_pairs={{0,2},{1,3},{2,0},{3,1},{4,6},{5,7},{6,4},{7,5},{8,10},{9,11},{10,... | collective-permute-start | bytes 392 | tf_op jit(solution)/shard_map/ppermute | solution.py:11
  82.0 1.8 %collective-permute-done.10 = f32[32]{0:T(128)S(1)} collective-permute-done((f32[32]{0:T(128)S(1)}, f32[32]{0:T(128)S(1)}, u32[]{:S(2)}, u32[]{:S(2)}) %collective-permute-start.10) | collective-permute-done | bytes 160 | tf_op jit(solution)/shard_map/ppermute | solution.py:11
  83.8 1.1 %collective-permute-done.11 = f32[32]{0:T(128)S(1)} collective-permute-done((f32[32]{0:T(128)S(1)}, f32[32]{0:T(128)S(1)}, u32[]{:S(2)}, u32[]{:S(2)}) %collective-permute-start.11) | collective-permute-done | bytes 160 | tf_op jit(solution)/shard_map/ppermute | solution.py:11
  (68 shorter events, 9.5 us)
Async XLA Ops:
  1.5 22.9 %copy-start.2 = (f32[32,256]{1,0:T(8,128)}, f32[32,256]{1,0:T(8,128)S(1)}, u32[]{:S(2)}) copy-start(f32[32,256]{1,0:T(8,128)S(1)} %broadcast_divide_fusion) | copy-start | bytes 98308
  2.3 7.9 %collective-permute-start = (f32[65,256]{1,0:T(8,128)S(1)}, f32[65,256]{1,0:T(8,128)S(1)}, u32[]{:S(2)}, u32[]{:S(2)}) collective-permute-start(f32[65,256]{1,0:T(8,128)S(1)} %pad_maximum_fusion.10), channel_id=1, source_target_pairs={{0,8},{1,9},{2,10},{3,11},{4,12},{5,13},{6,14},{7,15},{8,0},{9,1},... | collective-permute-start | bytes 199688 | tf_op jit(solution)/shard_map/ppermute | solution.py:11
  11.0 5.2 %collective-permute-start.1 = (f32[65,512]{1,0:T(8,128)S(1)}, f32[65,512]{1,0:T(8,128)S(1)}, u32[]{:S(2)}, u32[]{:S(2)}) collective-permute-start(f32[65,512]{1,0:T(8,128)S(1)} %pad_maximum_fusion.9), channel_id=1, source_target_pairs={{0,4},{1,5},{2,6},{3,7},{4,0},{5,1},{6,2},{7,3},{8,12},{9,13},{10,... | collective-permute-start | bytes 399368 | tf_op jit(solution)/shard_map/ppermute | solution.py:11
  16.2 8.1 %copy-start = (f32[65,512]{1,0:T(8,128)}, f32[65,512]{1,0:T(8,128)S(1)}, u32[]{:S(2)}) copy-start(f32[65,512]{1,0:T(8,128)S(1)} %collective-permute-done.1) | copy-start | bytes 399364
  17.1 6.4 %collective-permute-start.2 = (f32[64,1024]{1,0:T(8,128)S(1)}, f32[64,1024]{1,0:T(8,128)S(1)}, u32[]{:S(2)}, u32[]{:S(2)}) collective-permute-start(f32[64,1024]{1,0:T(8,128)S(1)} %slice.145), channel_id=1, source_target_pairs={{0,2},{1,3},{2,0},{3,1},{4,6},{5,7},{6,4},{7,5},{8,10},{9,11},{10,... | collective-permute-start | bytes 786440 | tf_op jit(solution)/shard_map/ppermute | solution.py:11
  23.6 2.0 %collective-permute-start.3 = (f32[64,2048]{1,0:T(8,128)S(1)}, f32[64,2048]{1,0:T(8,128)S(1)}, u32[]{:S(2)}, u32[]{:S(2)}) collective-permute-start(f32[64,2048]{1,0:T(8,128)S(1)} %pad_maximum_fusion.1), channel_id=1, source_target_pairs={{0,1},{1,0},{2,3},{3,2},{4,5},{5,4},{6,7},{7,6},{8,9},{9,8},{10,11... | collective-permute-start | bytes 1572872 | tf_op jit(solution)/shard_map/ppermute | solution.py:11
  35.5 6.0 %copy-start.5 = (bf16[32,4096]{1,0:T(8,128)(2,1)S(1)}, bf16[32,4096]{1,0:T(8,128)(2,1)}, u32[]{:S(2)}) copy-start(bf16[32,4096]{1,0:T(8,128)(2,1)} %get-tuple-element.21) | copy-start | bytes 786436
  35.5 6.0 %copy-start.6 = (bf16[32,4096]{1,0:T(8,128)(2,1)S(1)}, bf16[32,4096]{1,0:T(8,128)(2,1)}, u32[]{:S(2)}) copy-start(bf16[32,4096]{1,0:T(8,128)(2,1)} %get-tuple-element.26) | copy-start | bytes 786436
  41.5 3.2 %copy-start.9 = (bf16[4096,1024]{1,0:T(8,128)(2,1)}, bf16[4096,1024]{1,0:T(8,128)(2,1)S(1)}, u32[]{:S(2)}) copy-start(bf16[4096,1024]{1,0:T(8,128)(2,1)S(1)} %get-tuple-element.18) | copy-start | bytes 25165828
  41.5 1.6 %copy-start.7 = (bf16[32,4096]{1,0:T(8,128)(2,1)S(1)}, bf16[32,4096]{1,0:T(8,128)(2,1)}, u32[]{:S(2)}) copy-start(bf16[32,4096]{1,0:T(8,128)(2,1)} %get-tuple-element.20) | copy-start | bytes 786436
  43.1 1.6 %copy-start.1 = (f32[65,512]{1,0:T(8,128)S(1)}, f32[65,512]{1,0:T(8,128)}, u32[]{:S(2)}) copy-start(f32[65,512]{1,0:T(8,128)} %copy-done) | copy-start | bytes 399364
  43.1 1.6 %copy-start.3 = (f32[32,256]{1,0:T(8,128)S(1)}, f32[32,256]{1,0:T(8,128)}, u32[]{:S(2)}) copy-start(f32[32,256]{1,0:T(8,128)} %copy-done.2) | copy-start | bytes 98308
  43.1 1.6 %copy-start.4 = (f32[32,256]{1,0:T(8,128)S(1)}, f32[32,256]{1,0:T(8,128)}, u32[]{:S(2)}) copy-start(f32[32,256]{1,0:T(8,128)} %param.7) | copy-start | bytes 98308
  43.2 1.6 %copy-start.8 = (f32[256]{0:T(256)S(1)}, f32[256]{0:T(256)}, u32[]{:S(2)}) copy-start(f32[256]{0:T(256)} %param.6) | copy-start | bytes 3076
  44.8 5.6 %collective-permute-start.4 = (f32[32,1024]{1,0:T(8,128)S(1)}, f32[32,1024]{1,0:T(8,128)S(1)}, u32[]{:S(2)}, u32[]{:S(2)}) collective-permute-start(f32[32,1024]{1,0:T(8,128)S(1)} %fusion.63), channel_id=1, source_target_pairs={{0,2},{1,3},{2,0},{3,1},{4,6},{5,7},{6,4},{7,5},{8,10},{9,11},{10,... | collective-permute-start | bytes 393224 | tf_op jit(solution)/shard_map/ppermute | solution.py:11
  50.4 1.6 %collective-permute-start.5 = (f32[32,2048]{1,0:T(8,128)S(1)}, f32[32,2048]{1,0:T(8,128)S(1)}, u32[]{:S(2)}, u32[]{:S(2)}) collective-permute-start(f32[32,2048]{1,0:T(8,128)S(1)} %pad_maximum_fusion.6), channel_id=1, source_target_pairs={{0,1},{1,0},{2,3},{3,2},{4,5},{5,4},{6,7},{7,6},{8,9},{9,8},{10,11... | collective-permute-start | bytes 786440 | tf_op jit(solution)/shard_map/ppermute | solution.py:11
  52.8 2.2 %slice-start = ((s8[8388608]{0:T(1024)(128)(4,1)}), s8[4194304]{0:T(1024)(128)(4,1)S(1)}, s32[]{:S(2)}) async-start(s8[8388608]{0:T(1024)(128)(4,1)} %bitcast.22), calls=%async_computation | async-start | bytes 8388608
  52.8 3.5 %slice-start.1 = ((s8[8388608]{0:T(1024)(128)(4,1)}), s8[4194304]{0:T(1024)(128)(4,1)S(1)}, s32[]{:S(2)}) async-start(s8[8388608]{0:T(1024)(128)(4,1)} %bitcast.22), calls=%async_computation.1 | async-start | bytes 8388608
  57.8 5.6 %collective-permute-start.6 = (f32[32,1024]{1,0:T(8,128)S(1)}, f32[32,1024]{1,0:T(8,128)S(1)}, u32[]{:S(2)}, u32[]{:S(2)}) collective-permute-start(f32[32,1024]{1,0:T(8,128)S(1)} %fusion.60), channel_id=1, source_target_pairs={{0,2},{1,3},{2,0},{3,1},{4,6},{5,7},{6,4},{7,5},{8,10},{9,11},{10,... | collective-permute-start | bytes 393224 | tf_op jit(solution)/shard_map/ppermute | solution.py:11
  63.4 1.6 %collective-permute-start.7 = (f32[32,2048]{1,0:T(8,128)S(1)}, f32[32,2048]{1,0:T(8,128)S(1)}, u32[]{:S(2)}, u32[]{:S(2)}) collective-permute-start(f32[32,2048]{1,0:T(8,128)S(1)} %pad_maximum_fusion.7), channel_id=1, source_target_pairs={{0,1},{1,0},{2,3},{3,2},{4,5},{5,4},{6,7},{7,6},{8,9},{9,8},{10,11... | collective-permute-start | bytes 786440 | tf_op jit(solution)/shard_map/ppermute | solution.py:11
  68.9 5.6 %collective-permute-start.8 = (f32[32,1024]{1,0:T(8,128)S(1)}, f32[32,1024]{1,0:T(8,128)S(1)}, u32[]{:S(2)}, u32[]{:S(2)}) collective-permute-start(f32[32,1024]{1,0:T(8,128)S(1)} %fusion.57), channel_id=1, source_target_pairs={{0,2},{1,3},{2,0},{3,1},{4,6},{5,7},{6,4},{7,5},{8,10},{9,11},{10,... | collective-permute-start | bytes 393224 | tf_op jit(solution)/shard_map/ppermute | solution.py:11
  74.6 1.6 %collective-permute-start.9 = (f32[32,2048]{1,0:T(8,128)S(1)}, f32[32,2048]{1,0:T(8,128)S(1)}, u32[]{:S(2)}, u32[]{:S(2)}) collective-permute-start(f32[32,2048]{1,0:T(8,128)S(1)} %pad_maximum_fusion.8), channel_id=1, source_target_pairs={{0,1},{1,0},{2,3},{3,2},{4,5},{5,4},{6,7},{7,6},{8,9},{9,8},{10,11... | collective-permute-start | bytes 786440 | tf_op jit(solution)/shard_map/ppermute | solution.py:11
  80.2 3.6 %collective-permute-start.10 = (f32[32]{0:T(128)S(1)}, f32[32]{0:T(128)S(1)}, u32[]{:S(2)}, u32[]{:S(2)}) collective-permute-start(f32[32]{0:T(128)S(1)} %get-tuple-element.4), channel_id=1, source_target_pairs={{0,2},{1,3},{2,0},{3,1},{4,6},{5,7},{6,4},{7,5},{8,10},{9,11},{10,... | collective-permute-start | bytes 392 | tf_op jit(solution)/shard_map/ppermute | solution.py:11
  83.8 1.1 %collective-permute-start.11 = (f32[32]{0:T(128)S(1)}, f32[32]{0:T(128)S(1)}, u32[]{:S(2)}, u32[]{:S(2)}) collective-permute-start(f32[32]{0:T(128)S(1)} %add.109), channel_id=1, source_target_pairs={{0,1},{1,0},{2,3},{3,2},{4,5},{5,4},{6,7},{7,6},{8,9},{9,8},{10,11... | collective-permute-start | bytes 392 | tf_op jit(solution)/shard_map/ppermute | solution.py:11

commit v4 on v3

--- a/solution.py
+++ b/solution.py
@@ -1,10 +1,17 @@
+import math
+
 import jax
 import jax.numpy as jnp
 from jax import lax
+from jax.experimental import pallas as pl
+from jax.experimental.pallas import tpu as pltpu
 from jax.sharding import PartitionSpec as P
 
 ITERS = 4
 TILE_BYTES = 16 << 20
+VMEM_BYTES = 16 << 20
+NORM_ROWS = 16
+POINT_SCALE = math.sqrt(math.log2(math.e))
 
 
 def swap(x, n, stride):
@@ -32,14 +39,68 @@
     return out
 
 
-def kernel_block(pts, cols):
-    high, mid, low = split(pts, 3)
-    norms = split(-0.5 * jnp.sum(pts * pts, axis=0, keepdims=True), 3)
-    ones = [jnp.ones_like(norms[0])] * 3
-    left = jnp.concatenate([high, high, mid, high, low, mid] + norms + ones, axis=0)
-    right = jnp.concatenate([high, mid, high, low, high, mid] + ones + norms, axis=0)[:, :cols]
-    tile = jnp.exp(lax.dot_general(left, right, (((0,), (0,)), ((), ())), preferred_element_type=jnp.float32))
-    return split(tile, 2)
+def halve(x):
+    high = x.astype(jnp.bfloat16)
+    return high, x - high.astype(jnp.float32)
+
+
+def operands(pts):
+    high, rest = halve(pts)
+    mid, rest = halve(rest)
+    low = rest.astype(jnp.bfloat16)
+    norms = -0.5 * jnp.sum(pts * pts, axis=0, keepdims=True)
+    row = lax.broadcasted_iota(jnp.int32, (NORM_ROWS, pts.shape[1]), 0)
+    left = jnp.where((row >= 3) & (row < 6), 1.0, 0.0)
+    right = jnp.where(row < 3, 1.0, 0.0)
+    for k in range(3):
+        part, norms = halve(norms)
+        part = part.astype(jnp.float32)
+        left = jnp.where(row == k, part, left)
+        right = jnp.where(row == 3 + k, part, right)
+    left = jnp.concatenate([high, high, mid, high, low, mid, left.astype(jnp.bfloat16)], axis=0)
+    right = jnp.concatenate([high, mid, high, low, high, mid, right.astype(jnp.bfloat16)], axis=0)
+    return left, right
+
+
+def build_kernel(all_ref, mine_ref, scale_ref, high_ref, low_ref, right_ref):
+    @pl.when(pl.program_id(0) == 0)
+    def _():
+        right_ref[...] = operands(mine_ref[...] * scale_ref[...])[1]
+
+    left = operands(all_ref[...] * scale_ref[...])[0]
+    cols = right_ref.shape[1]
+    step = min(cols, 256)
+    for at in range(0, cols, step):
+        here = pl.ds(at, step)
+        power = lax.dot_general(
+            left, right_ref[:, here], (((0,), (0,)), ((), ())), preferred_element_type=jnp.float32
+        )
+        high, rest = halve(jnp.exp2(power))
+        high_ref[:, here] = high
+        low_ref[:, here] = rest.astype(jnp.bfloat16)
+
+
+def kernel_block(pts, scale, cols):
+    feats, total = pts.shape
+    block = min(total, 512)
+    out = jax.ShapeDtypeStruct((total, cols), jnp.bfloat16)
+    spec = pl.BlockSpec((block, cols), lambda i: (i, 0))
+    return pl.pallas_call(
+        build_kernel,
+        grid=(total // block,),
+        out_shape=(out, out),
+        in_specs=[
+            pl.BlockSpec((feats, block), lambda i: (0, i)),
+            pl.BlockSpec((feats, cols), lambda i: (0, 0)),
+            pl.BlockSpec((feats, 1), lambda i: (0, 0)),
+        ],
+        out_specs=(spec, spec),
+        scratch_shapes=[pltpu.VMEM((6 * feats + NORM_ROWS, cols), jnp.bfloat16)],
+        compiler_params=pltpu.CompilerParams(vmem_limit_bytes=VMEM_BYTES),
+        cost_estimate=pl.CostEstimate(
+            flops=2 * total * cols * 256, bytes_accessed=4 * total * (cols + feats), transcendentals=total * cols
+        ),
+    )(pts, pts[:, :cols], scale)
 
 
 def apply_block(direction, tile):
@@ -62,14 +123,14 @@
         outer, inner = [s for s in strides if s >= team], [s for s in strides if s < team]
         cols = n // team * width
 
-        scaled = points / lengthscale[:, None]
-        mine = gather(jnp.concatenate([scaled, targets, noise_var[None, :]], axis=0), n, outer)
+        block = lax.optimization_barrier(jnp.concatenate([points, targets, noise_var[None, :]], axis=0))
+        mine = gather(block, n, outer)
         noise = mine[-1:]
         both = gather(mine[:-1], n, inner)
-        tile = kernel_block(both[:feats], cols)
+        tile = kernel_block(both[:feats], (POINT_SCALE / lengthscale)[:, None], cols)
 
         residual = direction = both[feats:]
-        my_solution = jnp.zeros_like(targets)
+        my_solution = jnp.zeros_like(block[feats:-1])
         norm_now = jnp.sum(residual * residual, axis=1)
         for iteration in range(ITERS):
             my_applied = apply_block(direction, tile) + noise * direction[:, :cols]

time: 86.3 us -> 71.2 us (0.83)
  local copies, waits for them, and re-layouts: 10.1 us -> 0.12 us
  matrix products: 18.3 us -> 12.2 us
  Pallas kernels: 0 us -> 5.74 us
  other arithmetic: 9.17 us -> 5 us
    concatenate x2 -> x0, local copies, waits for them, and re-layouts: 7.48 us -> none  [the longest x1 6.07 us: kernel_block(): jnp.concatenate([high, high, mid, high, low, mid] + norms + ones, axis=0)]
    dot_general x1 -> x0, matrix products: 5.92 us -> none  [kernel_block(): lax.dot_general(left, right, (((0,), (0,)), ((), ())), preferred_element_...]
    pallas_call x0 -> x1, Pallas kernels: none -> 5.74 us  [kernel_block(): pl.pallas_call(build_kernel, grid=(total // block,), out_shape=(out, out)...]
    unnamed x24 -> x0, local copies, waits for them, and re-layouts: 1.96 us -> none
    convert_element_type x8 -> x7, other arithmetic: 2.59 us -> 0.9 us  [split(): out.append(high.astype(jnp.bfloat16))]
    concatenate x7, other arithmetic: 1.79 us -> 0.19 us  [gather(): x = jnp.concatenate([x, swap(x, n, stride)], axis=1)]
where the time goes in v4:
time: 71.2 us; the launch traced here: 71 us
  waiting for transfers between devices  33 us (46%)
  starting transfers between devices  14 us (20%)
  matrix products  12.2 us (17%)
  Pallas kernels  5.74 us (8%)
  other arithmetic  5 us (7%)
  between operations  0.86 us (1%)
    ppermute x12, waiting for transfers between devices, swap(): return lax.ppermute(x, 'blk', [(i, i ^ stride) for i in range(n)])  33 us
    ppermute x12, starting transfers between devices, swap(): return lax.ppermute(x, 'blk', [(i, i ^ stride) for i in range(n)])  14 us
    dot_general x4, matrix products, apply_block(): jnp.dot(jnp.concatenate(parts[:2], axis=0), tile[1], preferred_element_ty...  6.3 us
    dot_general x4, matrix products, apply_block(): jnp.dot(jnp.concatenate(parts, axis=0), tile[0], preferred_element_type=j...  5.86 us
    pallas_call x1, Pallas kernels, kernel_block(): pl.pallas_call(build_kernel, grid=(total // block,), out_shape=(out, out)...  5.74 us
  transfers between devices with their start and end apart: 12, of which 12 were waited for; matrix products, arithmetic and copies ran while one was open for 1% of the time, Pallas kernels for 0%

profile of v4, /device:TPU:0, one launch (start us, length us, event | category | flops | bytes accessed | tf_op | source)
XLA Modules:
  0.0 71.0 jit_solution(939308667881521098)
XLA Ops:
  0.6 0.8 %pad_maximum_fusion.10 = f32[65,256]{1,0:T(8,128)S(1)} fusion(f32[1,256]{1,0:T(1,128)} %bitcast.16, f32[32,256]{1,0:T(8,128)} %param.7, f32[32,256]{1,0:T(8,128)} %param.4), kind=kLoop, calls=%fused_computation.111 | loop fusion | flops 33280 | bytes 133120 | tf_op jit(solution)/shard_map/concatenate | solution.py:126
  1.4 4.0 %collective-permute-start = (f32[65,256]{1,0:T(8,128)S(1)}, f32[65,256]{1,0:T(8,128)S(1)}, u32[]{:S(2)}, u32[]{:S(2)}) collective-permute-start(f32[65,256]{1,0:T(8,128)S(1)} %pad_maximum_fusion.10), channel_id=1, source_target_pairs={{0,8},{1,9},{2,10},{3,11},{4,12},{5,13},{6,14},{7,15},{8,0},{9,1},... | collective-permute-start | bytes 199688 | tf_op jit(solution)/shard_map/ppermute | solution.py:18
  5.5 3.9 %collective-permute-done = f32[65,256]{1,0:T(8,128)S(1)} collective-permute-done((f32[65,256]{1,0:T(8,128)S(1)}, f32[65,256]{1,0:T(8,128)S(1)}, u32[]{:S(2)}, u32[]{:S(2)}) %collective-permute-start) | collective-permute-done | bytes 66592 | tf_op jit(solution)/shard_map/ppermute | solution.py:18
  9.4 0.7 %collective-permute-start.1 = (f32[65,512]{1,0:T(8,128)S(1)}, f32[65,512]{1,0:T(8,128)S(1)}, u32[]{:S(2)}, u32[]{:S(2)}) collective-permute-start(f32[65,512]{1,0:T(8,128)S(1)} %pad_maximum_fusion.9), channel_id=1, source_target_pairs={{0,4},{1,5},{2,6},{3,7},{4,0},{5,1},{6,2},{7,3},{8,12},{9,13},{10,... | collective-permute-start | bytes 399368 | tf_op jit(solution)/shard_map/ppermute | solution.py:18
  10.1 4.5 %collective-permute-done.1 = f32[65,512]{1,0:T(8,128)S(1)} collective-permute-done((f32[65,512]{1,0:T(8,128)S(1)}, f32[65,512]{1,0:T(8,128)S(1)}, u32[]{:S(2)}, u32[]{:S(2)}) %collective-permute-start.1) | collective-permute-done | bytes 133152 | tf_op jit(solution)/shard_map/ppermute | solution.py:18
  14.7 1.8 %collective-permute-start.2 = (f32[64,1024]{1,0:T(8,128)S(1)}, f32[64,1024]{1,0:T(8,128)S(1)}, u32[]{:S(2)}, u32[]{:S(2)}) collective-permute-start(f32[64,1024]{1,0:T(8,128)S(1)} %slice.151), channel_id=1, source_target_pairs={{0,2},{1,3},{2,0},{3,1},{4,6},{5,7},{6,4},{7,5},{8,10},{9,11},{10,... | collective-permute-start | bytes 786440 | tf_op jit(solution)/shard_map/ppermute | solution.py:18
  16.4 4.6 %collective-permute-done.2 = f32[64,1024]{1,0:T(8,128)S(1)} collective-permute-done((f32[64,1024]{1,0:T(8,128)S(1)}, f32[64,1024]{1,0:T(8,128)S(1)}, u32[]{:S(2)}, u32[]{:S(2)}) %collective-permute-start.2) | collective-permute-done | bytes 262176 | tf_op jit(solution)/shard_map/ppermute | solution.py:18
  21.2 0.7 divide_bitcast_fusion
  22.0 1.1 %collective-permute-done.3 = f32[64,2048]{1,0:T(8,128)S(1)} collective-permute-done((f32[64,2048]{1,0:T(8,128)S(1)}, f32[64,2048]{1,0:T(8,128)S(1)}, u32[]{:S(2)}, u32[]{:S(2)}) %collective-permute-start.3) | collective-permute-done | bytes 524320 | tf_op jit(solution)/shard_map/ppermute | solution.py:18
  23.3 5.7 %shard_map.59 = (bf16[4096,1024]{1,0:T(8,128)(2,1)S(1)}, bf16[4096,1024]{1,0:T(8,128)(2,1)S(1)}) custom-call(f32[32,4096]{1,0:T(8,128)S(1)} %get-tuple-element.24.all_ref, f32[32,1024]{1,0:T(8,128)S(1)} %slice.154.mine_ref, f32[32,1]{1,0:T(8,128)S(1)} %copy.6.scale_ref), custom_call_target="tpu_custom_call" | custom-call | flops 2147483648 | bytes 17301504 | tf_op jit(solution)/shard_map/pallas_call | solution.py:88
  29.1 1.6 %fusion.32 = f32[64,1024]{1,0:T(8,128)S(1)} fusion(bf16[4096,1024]{1,0:T(8,128)(2,1)S(1)} %get-tuple-element.5, bf16[32,4096]{1,0:T(8,128)(2,1)S(1)} %get-tuple-element.23, bf16[32,4096]{1,0:T(8,128)(2,1)S(1)} %get-tuple-element.25), kind=kOutput, calls=%fused_computation.50 | convolution fusion | flops 537919488 | bytes 9175040 | tf_op jit(solution)/shard_map/dot_general | solution.py:110
  30.6 1.5 %fusion = f32[96,1024]{1,0:T(8,128)S(1)} fusion(bf16[4096,1024]{1,0:T(8,128)(2,1)S(1)} %get-tuple-element.4, bf16[32,4096]{1,0:T(8,128)(2,1)S(1)} %get-tuple-element.22, bf16[32,4096]{1,0:T(8,128)(2,1)S(1)} %get-tuple-element.23, bf16[32,4096]{1,0:T(8,128)(2,1)S(1)} %get-tuple-element.25), kind=kOutput, calls=%fused_computation.1 | convolution fusion | flops 807665664 | bytes 9568256 | tf_op jit(solution)/shard_map/dot_general | solution.py:109
  32.2 1.8 %collective-permute-start.4 = (f32[32,1024]{1,0:T(8,128)S(1)}, f32[32,1024]{1,0:T(8,128)S(1)}, u32[]{:S(2)}, u32[]{:S(2)}) collective-permute-start(f32[32,1024]{1,0:T(8,128)S(1)} %fusion.57), channel_id=1, source_target_pairs={{0,2},{1,3},{2,0},{3,1},{4,6},{5,7},{6,4},{7,5},{8,10},{9,11},{10,... | collective-permute-start | bytes 393224 | tf_op jit(solution)/shard_map/ppermute | solution.py:18
  34.0 3.8 %collective-permute-done.4 = f32[32,1024]{1,0:T(8,128)S(1)} collective-permute-done((f32[32,1024]{1,0:T(8,128)S(1)}, f32[32,1024]{1,0:T(8,128)S(1)}, u32[]{:S(2)}, u32[]{:S(2)}) %collective-permute-start.4) | collective-permute-done | bytes 131104 | tf_op jit(solution)/shard_map/ppermute | solution.py:18
  37.9 1.5 %collective-permute-done.5 = f32[32,2048]{1,0:T(8,128)S(1)} collective-permute-done((f32[32,2048]{1,0:T(8,128)S(1)}, f32[32,2048]{1,0:T(8,128)S(1)}, u32[]{:S(2)}, u32[]{:S(2)}) %collective-permute-start.5) | collective-permute-done | bytes 262176 | tf_op jit(solution)/shard_map/ppermute | solution.py:18
  40.2 1.6 %fusion.36 = f32[64,1024]{1,0:T(8,128)S(1)} fusion(bf16[4096,1024]{1,0:T(8,128)(2,1)S(1)} %get-tuple-element.5, bf16[32,4096]{1,0:T(8,128)(2,1)S(1)} %get-tuple-element.31, bf16[32,4096]{1,0:T(8,128)(2,1)S(1)} %get-tuple-element.30), kind=kOutput, calls=%fused_computation.55 | convolution fusion | flops 537919488 | bytes 9175040 | tf_op jit(solution)/shard_map/dot_general | solution.py:110
  41.8 1.5 %fusion.6 = f32[96,1024]{1,0:T(8,128)S(1)} fusion(bf16[4096,1024]{1,0:T(8,128)(2,1)S(1)} %get-tuple-element.4, bf16[32,4096]{1,0:T(8,128)(2,1)S(1)} %get-tuple-element.18, bf16[32,4096]{1,0:T(8,128)(2,1)S(1)} %get-tuple-element.31, bf16[32,4096]{1,0:T(8,128)(2,1)S(1)} %get-tuple-element.30), kind=kOutput, calls=%fused_computation.7 | convolution fusion | flops 807665664 | bytes 9568256 | tf_op jit(solution)/shard_map/dot_general | solution.py:109
  43.3 1.8 %collective-permute-start.6 = (f32[32,1024]{1,0:T(8,128)S(1)}, f32[32,1024]{1,0:T(8,128)S(1)}, u32[]{:S(2)}, u32[]{:S(2)}) collective-permute-start(f32[32,1024]{1,0:T(8,128)S(1)} %fusion.54), channel_id=1, source_target_pairs={{0,2},{1,3},{2,0},{3,1},{4,6},{5,7},{6,4},{7,5},{8,10},{9,11},{10,... | collective-permute-start | bytes 393224 | tf_op jit(solution)/shard_map/ppermute | solution.py:18
  45.1 3.8 %collective-permute-done.6 = f32[32,1024]{1,0:T(8,128)S(1)} collective-permute-done((f32[32,1024]{1,0:T(8,128)S(1)}, f32[32,1024]{1,0:T(8,128)S(1)}, u32[]{:S(2)}, u32[]{:S(2)}) %collective-permute-start.6) | collective-permute-done | bytes 131104 | tf_op jit(solution)/shard_map/ppermute | solution.py:18
  49.0 1.5 %collective-permute-done.7 = f32[32,2048]{1,0:T(8,128)S(1)} collective-permute-done((f32[32,2048]{1,0:T(8,128)S(1)}, f32[32,2048]{1,0:T(8,128)S(1)}, u32[]{:S(2)}, u32[]{:S(2)}) %collective-permute-start.7) | collective-permute-done | bytes 262176 | tf_op jit(solution)/shard_map/ppermute | solution.py:18
  50.7 0.3 multiply_reduce_fusion.2
  51.3 1.6 %fusion.40 = f32[64,1024]{1,0:T(8,128)S(1)} fusion(bf16[4096,1024]{1,0:T(8,128)(2,1)S(1)} %get-tuple-element.5, bf16[32,4096]{1,0:T(8,128)(2,1)S(1)} %get-tuple-element.29, bf16[32,4096]{1,0:T(8,128)(2,1)S(1)} %get-tuple-element.28), kind=kOutput, calls=%fused_computation.60 | convolution fusion | flops 537919488 | bytes 9175040 | tf_op jit(solution)/shard_map/dot_general | solution.py:110
  52.8 1.5 %fusion.12 = f32[96,1024]{1,0:T(8,128)S(1)} fusion(bf16[4096,1024]{1,0:T(8,128)(2,1)S(1)} %get-tuple-element.4, bf16[32,4096]{1,0:T(8,128)(2,1)S(1)} %get-tuple-element.14, bf16[32,4096]{1,0:T(8,128)(2,1)S(1)} %get-tuple-element.29, bf16[32,4096]{1,0:T(8,128)(2,1)S(1)} %get-tuple-element.28), kind=kOutput, calls=%fused_computation.13 | convolution fusion | flops 807665664 | bytes 9568256 | tf_op jit(solution)/shard_map/dot_general | solution.py:109
  54.3 1.8 %collective-permute-start.8 = (f32[32,1024]{1,0:T(8,128)S(1)}, f32[32,1024]{1,0:T(8,128)S(1)}, u32[]{:S(2)}, u32[]{:S(2)}) collective-permute-start(f32[32,1024]{1,0:T(8,128)S(1)} %fusion.51), channel_id=1, source_target_pairs={{0,2},{1,3},{2,0},{3,1},{4,6},{5,7},{6,4},{7,5},{8,10},{9,11},{10,... | collective-permute-start | bytes 393224 | tf_op jit(solution)/shard_map/ppermute | solution.py:18
  56.2 3.8 %collective-permute-done.8 = f32[32,1024]{1,0:T(8,128)S(1)} collective-permute-done((f32[32,1024]{1,0:T(8,128)S(1)}, f32[32,1024]{1,0:T(8,128)S(1)}, u32[]{:S(2)}, u32[]{:S(2)}) %collective-permute-start.8) | collective-permute-done | bytes 131104 | tf_op jit(solution)/shard_map/ppermute | solution.py:18
  60.1 1.5 %collective-permute-done.9 = f32[32,2048]{1,0:T(8,128)S(1)} collective-permute-done((f32[32,2048]{1,0:T(8,128)S(1)}, f32[32,2048]{1,0:T(8,128)S(1)}, u32[]{:S(2)}, u32[]{:S(2)}) %collective-permute-start.9) | collective-permute-done | bytes 262176 | tf_op jit(solution)/shard_map/ppermute | solution.py:18
  62.3 1.6 %fusion.44 = f32[64,1024]{1,0:T(8,128)S(1)} fusion(bf16[4096,1024]{1,0:T(8,128)(2,1)S(1)} %get-tuple-element.5, bf16[32,4096]{1,0:T(8,128)(2,1)S(1)} %get-tuple-element.27, bf16[32,4096]{1,0:T(8,128)(2,1)S(1)} %get-tuple-element.26), kind=kOutput, calls=%fused_computation.65 | convolution fusion | flops 537919488 | bytes 9175040 | tf_op jit(solution)/shard_map/dot_general | solution.py:110
  63.9 1.5 %fusion.18 = f32[96,1024]{1,0:T(8,128)S(1)} fusion(bf16[4096,1024]{1,0:T(8,128)(2,1)S(1)} %get-tuple-element.4, bf16[32,4096]{1,0:T(8,128)(2,1)S(1)} %get-tuple-element.10, bf16[32,4096]{1,0:T(8,128)(2,1)S(1)} %get-tuple-element.27, bf16[32,4096]{1,0:T(8,128)(2,1)S(1)} %get-tuple-element.26), kind=kOutput, calls=%fused_computation.19 | convolution fusion | flops 807665664 | bytes 9568256 | tf_op jit(solution)/shard_map/dot_general | solution.py:109
  65.5 1.8 %collective-permute-start.10 = (f32[32]{0:T(128)S(1)}, f32[32]{0:T(128)S(1)}, u32[]{:S(2)}, u32[]{:S(2)}) collective-permute-start(f32[32]{0:T(128)S(1)} %get-tuple-element.8), channel_id=1, source_target_pairs={{0,2},{1,3},{2,0},{3,1},{4,6},{5,7},{6,4},{7,5},{8,10},{9,11},{10,... | collective-permute-start | bytes 392 | tf_op jit(solution)/shard_map/ppermute | solution.py:18
  67.3 1.8 %collective-permute-done.10 = f32[32]{0:T(128)S(1)} collective-permute-done((f32[32]{0:T(128)S(1)}, f32[32]{0:T(128)S(1)}, u32[]{:S(2)}, u32[]{:S(2)}) %collective-permute-start.10) | collective-permute-done | bytes 160 | tf_op jit(solution)/shard_map/ppermute | solution.py:18
  69.1 1.1 %collective-permute-done.11 = f32[32]{0:T(128)S(1)} collective-permute-done((f32[32]{0:T(128)S(1)}, f32[32]{0:T(128)S(1)}, u32[]{:S(2)}, u32[]{:S(2)}) %collective-permute-start.11) | collective-permute-done | bytes 160 | tf_op jit(solution)/shard_map/ppermute | solution.py:18
  70.2 0.7 %fusion.60 = (f32[32,256]{1,0:T(8,128)}, f32[32,256]{1,0:T(8,128)}) fusion(f32[32,1024]{1,0:T(8,128)S(1)} %get-tuple-element.9, f32[32,4096]{1,0:T(8,128)S(1)} %get-tuple-element.13, f32[32]{0:T(128)S(1)} %add_divide_fusion, f32[32,4096]{1,0:T(8,128)S(1)} %get-tuple-element.11, f32[32,4096]{1,0:T(8,128)S(1)} %get-tuple-element.15, f32[32]{0:T(128)S(1)} %div.57, ...), kind=kLoop, calls=%fused_computation.113 | loop fusion | flops 73728 | bytes 262656 | tf_op jit(solution)/shard_map/sub | solution.py:141
  (40 shorter events, 3.0 us)
Async XLA Ops:
  1.4 7.9 %collective-permute-start = (f32[65,256]{1,0:T(8,128)S(1)}, f32[65,256]{1,0:T(8,128)S(1)}, u32[]{:S(2)}, u32[]{:S(2)}) collective-permute-start(f32[65,256]{1,0:T(8,128)S(1)} %pad_maximum_fusion.10), channel_id=1, source_target_pairs={{0,8},{1,9},{2,10},{3,11},{4,12},{5,13},{6,14},{7,15},{8,0},{9,1},... | collective-permute-start | bytes 199688 | tf_op jit(solution)/shard_map/ppermute | solution.py:18
  9.4 5.2 %collective-permute-start.1 = (f32[65,512]{1,0:T(8,128)S(1)}, f32[65,512]{1,0:T(8,128)S(1)}, u32[]{:S(2)}, u32[]{:S(2)}) collective-permute-start(f32[65,512]{1,0:T(8,128)S(1)} %pad_maximum_fusion.9), channel_id=1, source_target_pairs={{0,4},{1,5},{2,6},{3,7},{4,0},{5,1},{6,2},{7,3},{8,12},{9,13},{10,... | collective-permute-start | bytes 399368 | tf_op jit(solution)/shard_map/ppermute | solution.py:18
  14.7 6.4 %collective-permute-start.2 = (f32[64,1024]{1,0:T(8,128)S(1)}, f32[64,1024]{1,0:T(8,128)S(1)}, u32[]{:S(2)}, u32[]{:S(2)}) collective-permute-start(f32[64,1024]{1,0:T(8,128)S(1)} %slice.151), channel_id=1, source_target_pairs={{0,2},{1,3},{2,0},{3,1},{4,6},{5,7},{6,4},{7,5},{8,10},{9,11},{10,... | collective-permute-start | bytes 786440 | tf_op jit(solution)/shard_map/ppermute | solution.py:18
  21.1 2.0 %collective-permute-start.3 = (f32[64,2048]{1,0:T(8,128)S(1)}, f32[64,2048]{1,0:T(8,128)S(1)}, u32[]{:S(2)}, u32[]{:S(2)}) collective-permute-start(f32[64,2048]{1,0:T(8,128)S(1)} %pad_maximum_fusion.1), channel_id=1, source_target_pairs={{0,1},{1,0},{2,3},{3,2},{4,5},{5,4},{6,7},{7,6},{8,9},{9,8},{10,11... | collective-permute-start | bytes 1572872 | tf_op jit(solution)/shard_map/ppermute | solution.py:18
  32.2 5.6 %collective-permute-start.4 = (f32[32,1024]{1,0:T(8,128)S(1)}, f32[32,1024]{1,0:T(8,128)S(1)}, u32[]{:S(2)}, u32[]{:S(2)}) collective-permute-start(f32[32,1024]{1,0:T(8,128)S(1)} %fusion.57), channel_id=1, source_target_pairs={{0,2},{1,3},{2,0},{3,1},{4,6},{5,7},{6,4},{7,5},{8,10},{9,11},{10,... | collective-permute-start | bytes 393224 | tf_op jit(solution)/shard_map/ppermute | solution.py:18
  37.8 1.6 %collective-permute-start.5 = (f32[32,2048]{1,0:T(8,128)S(1)}, f32[32,2048]{1,0:T(8,128)S(1)}, u32[]{:S(2)}, u32[]{:S(2)}) collective-permute-start(f32[32,2048]{1,0:T(8,128)S(1)} %pad_maximum_fusion.6), channel_id=1, source_target_pairs={{0,1},{1,0},{2,3},{3,2},{4,5},{5,4},{6,7},{7,6},{8,9},{9,8},{10,11... | collective-permute-start | bytes 786440 | tf_op jit(solution)/shard_map/ppermute | solution.py:18
  43.3 5.6 %collective-permute-start.6 = (f32[32,1024]{1,0:T(8,128)S(1)}, f32[32,1024]{1,0:T(8,128)S(1)}, u32[]{:S(2)}, u32[]{:S(2)}) collective-permute-start(f32[32,1024]{1,0:T(8,128)S(1)} %fusion.54), channel_id=1, source_target_pairs={{0,2},{1,3},{2,0},{3,1},{4,6},{5,7},{6,4},{7,5},{8,10},{9,11},{10,... | collective-permute-start | bytes 393224 | tf_op jit(solution)/shard_map/ppermute | solution.py:18
  48.9 1.6 %collective-permute-start.7 = (f32[32,2048]{1,0:T(8,128)S(1)}, f32[32,2048]{1,0:T(8,128)S(1)}, u32[]{:S(2)}, u32[]{:S(2)}) collective-permute-start(f32[32,2048]{1,0:T(8,128)S(1)} %pad_maximum_fusion.7), channel_id=1, source_target_pairs={{0,1},{1,0},{2,3},{3,2},{4,5},{5,4},{6,7},{7,6},{8,9},{9,8},{10,11... | collective-permute-start | bytes 786440 | tf_op jit(solution)/shard_map/ppermute | solution.py:18
  54.3 5.6 %collective-permute-start.8 = (f32[32,1024]{1,0:T(8,128)S(1)}, f32[32,1024]{1,0:T(8,128)S(1)}, u32[]{:S(2)}, u32[]{:S(2)}) collective-permute-start(f32[32,1024]{1,0:T(8,128)S(1)} %fusion.51), channel_id=1, source_target_pairs={{0,2},{1,3},{2,0},{3,1},{4,6},{5,7},{6,4},{7,5},{8,10},{9,11},{10,... | collective-permute-start | bytes 393224 | tf_op jit(solution)/shard_map/ppermute | solution.py:18
  60.0 1.6 %collective-permute-start.9 = (f32[32,2048]{1,0:T(8,128)S(1)}, f32[32,2048]{1,0:T(8,128)S(1)}, u32[]{:S(2)}, u32[]{:S(2)}) collective-permute-start(f32[32,2048]{1,0:T(8,128)S(1)} %pad_maximum_fusion.8), channel_id=1, source_target_pairs={{0,1},{1,0},{2,3},{3,2},{4,5},{5,4},{6,7},{7,6},{8,9},{9,8},{10,11... | collective-permute-start | bytes 786440 | tf_op jit(solution)/shard_map/ppermute | solution.py:18
  65.5 3.6 %collective-permute-start.10 = (f32[32]{0:T(128)S(1)}, f32[32]{0:T(128)S(1)}, u32[]{:S(2)}, u32[]{:S(2)}) collective-permute-start(f32[32]{0:T(128)S(1)} %get-tuple-element.8), channel_id=1, source_target_pairs={{0,2},{1,3},{2,0},{3,1},{4,6},{5,7},{6,4},{7,5},{8,10},{9,11},{10,... | collective-permute-start | bytes 392 | tf_op jit(solution)/shard_map/ppermute | solution.py:18
  69.1 1.1 %collective-permute-start.11 = (f32[32]{0:T(128)S(1)}, f32[32]{0:T(128)S(1)}, u32[]{:S(2)}, u32[]{:S(2)}) collective-permute-start(f32[32]{0:T(128)S(1)} %add.109), channel_id=1, source_target_pairs={{0,1},{1,0},{2,3},{3,2},{4,5},{5,4},{6,7},{7,6},{8,9},{9,8},{10,11... | collective-permute-start | bytes 392 | tf_op jit(solution)/shard_map/ppermute | solution.py:18

commit v5 on v4

--- a/solution.py
+++ b/solution.py
@@ -22,6 +22,11 @@
     for stride in strides:
         x = jnp.concatenate([x, swap(x, n, stride)], axis=1)
     return x
+
+
+def line(x, n, low, high):
+    groups = [[base + low * k for k in range(high // low)] for base in range(n) if base % high < low]
+    return lax.all_gather(x, "blk", axis_index_groups=groups, axis=1, tiled=True)
 
 
 def add_up(x, n, strides):
@@ -80,8 +85,9 @@
         low_ref[:, here] = rest.astype(jnp.bfloat16)
 
 
-def kernel_block(pts, scale, cols):
+def kernel_block(pts, mine, scale):
     feats, total = pts.shape
+    cols = mine.shape[1]
     block = min(total, 512)
     out = jax.ShapeDtypeStruct((total, cols), jnp.bfloat16)
     spec = pl.BlockSpec((block, cols), lambda i: (i, 0))
@@ -100,7 +106,7 @@
         cost_estimate=pl.CostEstimate(
             flops=2 * total * cols * 256, bytes_accessed=4 * total * (cols + feats), transcendentals=total * cols
         ),
-    )(pts, pts[:, :cols], scale)
+    )(pts, mine, scale)
 
 
 def apply_block(direction, tile):
@@ -120,29 +126,39 @@
         team = min(n, 4)
         while team < n and (n * width) * (n * width) // team * 4 > TILE_BYTES:
             team *= 2
-        outer, inner = [s for s in strides if s >= team], [s for s in strides if s < team]
+        inner = [s for s in strides if s < team // 2]
+        index = lax.axis_index("blk")
         cols = n // team * width
+        cols_at = index // (team // 2) % 2 * cols
+        block_at = cols_at + index // team * width
+
+        def gather_team(x):
+            return gather(line(x, n, team // 2, team), n, inner)
 
         block = lax.optimization_barrier(jnp.concatenate([points, targets, noise_var[None, :]], axis=0))
-        mine = gather(block, n, outer)
+        mine = line(block, n, team, n) if team < n else block
         noise = mine[-1:]
-        both = gather(mine[:-1], n, inner)
-        tile = kernel_block(both[:feats], (POINT_SCALE / lengthscale)[:, None], cols)
+        both = gather_team(mine[:-1])
+        tile = kernel_block(both[:feats], mine[:feats], (POINT_SCALE / lengthscale)[:, None])
+
+        def own(x, at, size):
+            return lax.dynamic_slice_in_dim(x, at, size, 1)
 
         residual = direction = both[feats:]
         my_solution = jnp.zeros_like(block[feats:-1])
         norm_now = jnp.sum(residual * residual, axis=1)
         for iteration in range(ITERS):
-            my_applied = apply_block(direction, tile) + noise * direction[:, :cols]
+            my_direction = own(direction, cols_at, cols)
+            my_applied = apply_block(direction, tile) + noise * my_direction
             if iteration == ITERS - 1:
-                curve = add_up(jnp.sum(direction[:, :cols] * my_applied, axis=1), n, inner)
+                curve = add_up(jnp.sum(my_direction * my_applied, axis=1), n, [team // 2] + inner)
                 step_size = (norm_now / curve)[:, None]
-                my_solution = my_solution + step_size * direction[:, :width]
-                return my_solution, residual[:, :width] - step_size * my_applied[:, :width]
-            applied = gather(my_applied, n, inner)
+                my_solution = my_solution + step_size * own(direction, block_at, width)
+                return my_solution, own(residual, block_at, width) - step_size * own(my_applied, index // team * width, width)
+            applied = gather_team(my_applied)
             curve = jnp.sum(direction * applied, axis=1)
             step_size = (norm_now / curve)[:, None]
-            my_solution = my_solution + step_size * direction[:, :width]
+            my_solution = my_solution + step_size * own(direction, block_at, width)
             residual = residual - step_size * applied
             norm_next = jnp.sum(residual * residual, axis=1)
             direction = residual + (norm_next / norm_now)[:, None] * direction

time: 71.2 us -> 80.4 us (1.13)
  blocking collectives: 0 us -> 41.5 us
  waiting for transfers between devices: 33 us -> 8.76 us
  starting transfers between devices: 14 us -> 1.59 us
  matrix products: 12.2 us -> 15.7 us
  local copies, waits for them, and re-layouts: 0.12 us -> 1.02 us
    all_gather x0 -> x5, blocking collectives: none -> 41.5 us  [line(): lax.all_gather(x, 'blk', axis_index_groups=groups, axis=1, tiled=True)]
    ppermute x12 -> x6, waiting for transfers between devices: 33 us -> 8.76 us  [swap(): return lax.ppermute(x, 'blk', [(i, i ^ stride) for i in range(n)])]
    ppermute x12 -> x6, starting transfers between devices: 14 us -> 1.59 us  [swap(): return lax.ppermute(x, 'blk', [(i, i ^ stride) for i in range(n)])]
    dot_general x4, matrix products: 6.3 us -> 9.82 us  [apply_block(): jnp.dot(jnp.concatenate(parts[:2], axis=0), tile[1], preferred_element_ty...]
    unnamed x0 -> x12, local copies, waits for them, and re-layouts: none -> 0.81 us
  transfers between devices with their start and end apart: 12 -> 6, of which waited for: 12 -> 6; matrix products, arithmetic and copies ran while one was open for 1% -> 1% of each run, Pallas kernels for 0% -> 0%
where the time goes in v5:
time: 80.4 us; the launch traced here: 80.2 us
  blocking collectives  41.5 us (52%)
  matrix products  15.7 us (20%)
  waiting for transfers between devices  8.76 us (11%)
  Pallas kernels  5.73 us (7%)
  other arithmetic  5 us (6%)
  starting transfers between devices  1.59 us (2%)
  local copies, waits for them, and re-layouts  1.02 us (1%)
  between operations  0.89 us (1%)
    all_gather x5, blocking collectives, line(): lax.all_gather(x, 'blk', axis_index_groups=groups, axis=1, tiled=True)  41.5 us
    dot_general x4, matrix products, apply_block(): jnp.dot(jnp.concatenate(parts[:2], axis=0), tile[1], preferred_element_ty...  9.82 us
    ppermute x6, waiting for transfers between devices, swap(): return lax.ppermute(x, 'blk', [(i, i ^ stride) for i in range(n)])  8.76 us
    dot_general x4, matrix products, apply_block(): jnp.dot(jnp.concatenate(parts, axis=0), tile[0], preferred_element_type=j...  5.85 us
    pallas_call x1, Pallas kernels, kernel_block(): pl.pallas_call(build_kernel, grid=(total // block,), out_shape=(out, out)...  5.73 us
  transfers between devices with their start and end apart: 6, of which 6 were waited for; matrix products, arithmetic and copies ran while one was open for 1% of the time, Pallas kernels for 0%

profile of v5, /device:TPU:0, one launch (start us, length us, event | category | flops | bytes accessed | tf_op | source)
XLA Modules:
  0.0 80.2 jit_solution(14404614272446684680)
XLA Ops:
  0.6 0.8 pad_maximum_fusion
  1.4 15.6 %all_gather.15 = f32[65,1024]{1,0:T(8,128)S(1)} all-gather(f32[65,256]{1,0:T(8,128)S(1)} %pad_maximum_fusion), channel_id=1, replica_groups={{0,4,8,12},{1,5,9,13},{2,6,10,14},{3,7,11,15},{16,20,24,28},{17,21,25,2..., dimensions={1}, use_global_device_ids=true | all-gather | bytes 332800 | tf_op jit(solution)/shard_map/all_gather | solution.py:29
  17.1 7.0 %all_gather.16 = f32[64,2048]{1,0:T(8,128)S(1)} all-gather(f32[64,1024]{1,0:T(8,128)S(1)} %slice.100), channel_id=1, replica_groups={{0,2},{1,3},{4,6},{5,7},{8,10},{9,11},{12,14},{13,15},{16,18},{17,19},{..., dimensions={1}, use_global_device_ids=true | all-gather | bytes 786432 | tf_op jit(solution)/shard_map/all_gather | solution.py:29
  24.2 0.7 divide_bitcast_fusion
  25.0 1.1 %collective-permute-done = f32[64,2048]{1,0:T(8,128)S(1)} collective-permute-done((f32[64,2048]{1,0:T(8,128)S(1)}, f32[64,2048]{1,0:T(8,128)S(1)}, u32[]{:S(2)}, u32[]{:S(2)}) %collective-permute-start) | collective-permute-done | bytes 524320 | tf_op jit(solution)/shard_map/ppermute | solution.py:18
  26.3 5.7 %shard_map.59 = (bf16[4096,1024]{1,0:T(8,128)(2,1)S(1)}, bf16[4096,1024]{1,0:T(8,128)(2,1)S(1)}) custom-call(f32[32,4096]{1,0:T(8,128)S(1)} %get-tuple-element.24.all_ref, f32[32,1024]{1,0:T(8,128)S(1)} %slice.103.mine_ref, f32[32,1]{1,0:T(8,128)S(1)} %copy.6.scale_ref), custom_call_target="tpu_custom_call" | custom-call | flops 2147483648 | bytes 17301504 | tf_op jit(solution)/shard_map/pallas_call | solution.py:94
  32.0 1.6 %fusion.32 = f32[64,1024]{1,0:T(8,128)S(1)} fusion(bf16[4096,1024]{1,0:T(8,128)(2,1)S(1)} %get-tuple-element.5, bf16[32,4096]{1,0:T(8,128)(2,1)S(1)} %get-tuple-element.22, bf16[32,4096]{1,0:T(8,128)(2,1)S(1)} %get-tuple-element.21), kind=kOutput, calls=%fused_computation.48 | convolution fusion | flops 537919488 | bytes 9175040 | tf_op jit(solution)/shard_map/dot_general | solution.py:116
  33.6 1.5 %fusion = f32[96,1024]{1,0:T(8,128)S(1)} fusion(bf16[4096,1024]{1,0:T(8,128)(2,1)S(1)} %get-tuple-element.4, bf16[32,4096]{1,0:T(8,128)(2,1)S(1)} %get-tuple-element.23, bf16[32,4096]{1,0:T(8,128)(2,1)S(1)} %get-tuple-element.22, bf16[32,4096]{1,0:T(8,128)(2,1)S(1)} %get-tuple-element.21), kind=kOutput, calls=%fused_computation | convolution fusion | flops 807665664 | bytes 9568256 | tf_op jit(solution)/shard_map/dot_general | solution.py:115
  35.1 6.2 %all_gather.17 = f32[32,2048]{1,0:T(8,128)S(1)} all-gather(f32[32,1024]{1,0:T(8,128)S(1)} %fusion.59), channel_id=1, replica_groups={{0,2},{1,3},{4,6},{5,7},{8,10},{9,11},{12,14},{13,15},{16,18},{17,19},{..., dimensions={1}, use_global_device_ids=true | all-gather | bytes 393216 | tf_op jit(solution)/shard_map/all_gather | solution.py:29
  41.4 1.5 %collective-permute-done.1 = f32[32,2048]{1,0:T(8,128)S(1)} collective-permute-done((f32[32,2048]{1,0:T(8,128)S(1)}, f32[32,2048]{1,0:T(8,128)S(1)}, u32[]{:S(2)}, u32[]{:S(2)}) %collective-permute-start.1) | collective-permute-done | bytes 262176 | tf_op jit(solution)/shard_map/ppermute | solution.py:18
  42.9 0.2 multiply_reduce_fusion.5
  43.1 0.3 multiply_reduce_fusion.4
  43.4 0.2 fusion.27
  43.7 1.6 %fusion.36 = f32[64,1024]{1,0:T(8,128)S(1)} fusion(bf16[4096,1024]{1,0:T(8,128)(2,1)S(1)} %get-tuple-element.5, bf16[32,4096]{1,0:T(8,128)(2,1)S(1)} %get-tuple-element.30, bf16[32,4096]{1,0:T(8,128)(2,1)S(1)} %get-tuple-element.29), kind=kOutput, calls=%fused_computation.52 | convolution fusion | flops 537919488 | bytes 9175040 | tf_op jit(solution)/shard_map/dot_general | solution.py:116
  45.3 1.5 %fusion.6 = f32[96,1024]{1,0:T(8,128)S(1)} fusion(bf16[4096,1024]{1,0:T(8,128)(2,1)S(1)} %get-tuple-element.4, bf16[32,4096]{1,0:T(8,128)(2,1)S(1)} %get-tuple-element.18, bf16[32,4096]{1,0:T(8,128)(2,1)S(1)} %get-tuple-element.30, bf16[32,4096]{1,0:T(8,128)(2,1)S(1)} %get-tuple-element.29), kind=kOutput, calls=%fused_computation.6 | convolution fusion | flops 807665664 | bytes 9568256 | tf_op jit(solution)/shard_map/dot_general | solution.py:115
  46.8 6.2 %all_gather.18 = f32[32,2048]{1,0:T(8,128)S(1)} all-gather(f32[32,1024]{1,0:T(8,128)S(1)} %fusion.56), channel_id=1, replica_groups={{0,2},{1,3},{4,6},{5,7},{8,10},{9,11},{12,14},{13,15},{16,18},{17,19},{..., dimensions={1}, use_global_device_ids=true | all-gather | bytes 393216 | tf_op jit(solution)/shard_map/all_gather | solution.py:29
  53.0 1.5 %collective-permute-done.2 = f32[32,2048]{1,0:T(8,128)S(1)} collective-permute-done((f32[32,2048]{1,0:T(8,128)S(1)}, f32[32,2048]{1,0:T(8,128)S(1)}, u32[]{:S(2)}, u32[]{:S(2)}) %collective-permute-start.2) | collective-permute-done | bytes 262176 | tf_op jit(solution)/shard_map/ppermute | solution.py:18
  54.8 0.3 multiply_reduce_fusion.2
  55.1 0.2 fusion.29
  55.4 1.6 %fusion.40 = f32[64,1024]{1,0:T(8,128)S(1)} fusion(bf16[4096,1024]{1,0:T(8,128)(2,1)S(1)} %get-tuple-element.5, bf16[32,4096]{1,0:T(8,128)(2,1)S(1)} %get-tuple-element.28, bf16[32,4096]{1,0:T(8,128)(2,1)S(1)} %get-tuple-element.27), kind=kOutput, calls=%fused_computation.56 | convolution fusion | flops 537919488 | bytes 9175040 | tf_op jit(solution)/shard_map/dot_general | solution.py:116
  57.0 1.5 %fusion.12 = f32[96,1024]{1,0:T(8,128)S(1)} fusion(bf16[4096,1024]{1,0:T(8,128)(2,1)S(1)} %get-tuple-element.4, bf16[32,4096]{1,0:T(8,128)(2,1)S(1)} %get-tuple-element.14, bf16[32,4096]{1,0:T(8,128)(2,1)S(1)} %get-tuple-element.28, bf16[32,4096]{1,0:T(8,128)(2,1)S(1)} %get-tuple-element.27), kind=kOutput, calls=%fused_computation.12 | convolution fusion | flops 807665664 | bytes 9568256 | tf_op jit(solution)/shard_map/dot_general | solution.py:115
  58.5 6.4 %all_gather.19 = f32[32,2048]{1,0:T(8,128)S(1)} all-gather(f32[32,1024]{1,0:T(8,128)S(1)} %fusion.53), channel_id=1, replica_groups={{0,2},{1,3},{4,6},{5,7},{8,10},{9,11},{12,14},{13,15},{16,18},{17,19},{..., dimensions={1}, use_global_device_ids=true | all-gather | bytes 393216 | tf_op jit(solution)/shard_map/all_gather | solution.py:29
  64.9 1.5 %collective-permute-done.3 = f32[32,2048]{1,0:T(8,128)S(1)} collective-permute-done((f32[32,2048]{1,0:T(8,128)S(1)}, f32[32,2048]{1,0:T(8,128)S(1)}, u32[]{:S(2)}, u32[]{:S(2)}) %collective-permute-start.3) | collective-permute-done | bytes 262176 | tf_op jit(solution)/shard_map/ppermute | solution.py:18
  66.7 0.3 multiply_reduce_fusion
  66.9 0.2 fusion.31
  67.2 5.1 %fusion.44 = f32[64,1024]{1,0:T(8,128)S(1)} fusion(bf16[4096,1024]{1,0:T(8,128)(2,1)} %copy-done, bf16[32,4096]{1,0:T(8,128)(2,1)S(1)} %get-tuple-element.26, bf16[32,4096]{1,0:T(8,128)(2,1)S(1)} %get-tuple-element.25), kind=kOutput, calls=%fused_computation.60 | convolution fusion | flops 537919488 | bytes 9175040 | tf_op jit(solution)/shard_map/dot_general | solution.py:116
  72.4 0.7 slice-done.1
  73.1 1.5 %fusion.18 = f32[96,1024]{1,0:T(8,128)S(1)} fusion(bf16[4096,1024]{1,0:T(8,128)(2,1)S(1)} %bitcast.13, bf16[32,4096]{1,0:T(8,128)(2,1)S(1)} %get-tuple-element.10, bf16[32,4096]{1,0:T(8,128)(2,1)S(1)} %get-tuple-element.26, bf16[32,4096]{1,0:T(8,128)(2,1)S(1)} %get-tuple-element.25), kind=kOutput, calls=%fused_computation.18 | convolution fusion | flops 807665664 | bytes 9568256 | tf_op jit(solution)/shard_map/dot_general | solution.py:115
  74.7 1.6 %collective-permute-start.4 = (f32[32]{0:T(128)S(1)}, f32[32]{0:T(128)S(1)}, u32[]{:S(2)}, u32[]{:S(2)}) collective-permute-start(f32[32]{0:T(128)S(1)} %get-tuple-element.8), channel_id=1, source_target_pairs={{0,2},{1,3},{2,0},{3,1},{4,6},{5,7},{6,4},{7,5},{8,10},{9,11},{10,... | collective-permute-start | bytes 392 | tf_op jit(solution)/shard_map/ppermute | solution.py:18
  76.3 2.0 %collective-permute-done.4 = f32[32]{0:T(128)S(1)} collective-permute-done((f32[32]{0:T(128)S(1)}, f32[32]{0:T(128)S(1)}, u32[]{:S(2)}, u32[]{:S(2)}) %collective-permute-start.4) | collective-permute-done | bytes 160 | tf_op jit(solution)/shard_map/ppermute | solution.py:18
  78.3 1.1 %collective-permute-done.5 = f32[32]{0:T(128)S(1)} collective-permute-done((f32[32]{0:T(128)S(1)}, f32[32]{0:T(128)S(1)}, u32[]{:S(2)}, u32[]{:S(2)}) %collective-permute-start.5) | collective-permute-done | bytes 160 | tf_op jit(solution)/shard_map/ppermute | solution.py:18
  79.4 0.7 multiply_subtract_fusion.3
  (43 shorter events, 1.4 us)
Async XLA Ops:
  24.1 1.9 %collective-permute-start = (f32[64,2048]{1,0:T(8,128)S(1)}, f32[64,2048]{1,0:T(8,128)S(1)}, u32[]{:S(2)}, u32[]{:S(2)}) collective-permute-start(f32[64,2048]{1,0:T(8,128)S(1)} %all_gather.16), channel_id=1, source_target_pairs={{0,1},{1,0},{2,3},{3,2},{4,5},{5,4},{6,7},{7,6},{8,9},{9,8},{10,11... | collective-permute-start | bytes 1572872 | tf_op jit(solution)/shard_map/ppermute | solution.py:18
  32.0 23.4 %copy-start = (bf16[4096,1024]{1,0:T(8,128)(2,1)}, bf16[4096,1024]{1,0:T(8,128)(2,1)S(1)}, u32[]{:S(2)}) copy-start(bf16[4096,1024]{1,0:T(8,128)(2,1)S(1)} %get-tuple-element.5) | copy-start | bytes 25165828
  32.0 25.0 %copy-start.1 = (bf16[4096,1024]{1,0:T(8,128)(2,1)}, bf16[4096,1024]{1,0:T(8,128)(2,1)S(1)}, u32[]{:S(2)}) copy-start(bf16[4096,1024]{1,0:T(8,128)(2,1)S(1)} %get-tuple-element.4) | copy-start | bytes 25165828
  41.3 1.5 %collective-permute-start.1 = (f32[32,2048]{1,0:T(8,128)S(1)}, f32[32,2048]{1,0:T(8,128)S(1)}, u32[]{:S(2)}, u32[]{:S(2)}) collective-permute-start(f32[32,2048]{1,0:T(8,128)S(1)} %all_gather.17), channel_id=1, source_target_pairs={{0,1},{1,0},{2,3},{3,2},{4,5},{5,4},{6,7},{7,6},{8,9},{9,8},{10,11... | collective-permute-start | bytes 786440 | tf_op jit(solution)/shard_map/ppermute | solution.py:18
  53.0 1.5 %collective-permute-start.2 = (f32[32,2048]{1,0:T(8,128)S(1)}, f32[32,2048]{1,0:T(8,128)S(1)}, u32[]{:S(2)}, u32[]{:S(2)}) collective-permute-start(f32[32,2048]{1,0:T(8,128)S(1)} %all_gather.18), channel_id=1, source_target_pairs={{0,1},{1,0},{2,3},{3,2},{4,5},{5,4},{6,7},{7,6},{8,9},{9,8},{10,11... | collective-permute-start | bytes 786440 | tf_op jit(solution)/shard_map/ppermute | solution.py:18
  64.9 1.5 %collective-permute-start.3 = (f32[32,2048]{1,0:T(8,128)S(1)}, f32[32,2048]{1,0:T(8,128)S(1)}, u32[]{:S(2)}, u32[]{:S(2)}) collective-permute-start(f32[32,2048]{1,0:T(8,128)S(1)} %all_gather.19), channel_id=1, source_target_pairs={{0,1},{1,0},{2,3},{3,2},{4,5},{5,4},{6,7},{7,6},{8,9},{9,8},{10,11... | collective-permute-start | bytes 786440 | tf_op jit(solution)/shard_map/ppermute | solution.py:18
  67.2 5.1 %slice-start = ((s8[8388608]{0:T(1024)(128)(4,1)}), s8[4194304]{0:T(1024)(128)(4,1)S(1)}, s32[]{:S(2)}) async-start(s8[8388608]{0:T(1024)(128)(4,1)} %bitcast.12), calls=%async_computation | async-start | bytes 8388608
  67.2 5.8 %slice-start.1 = ((s8[8388608]{0:T(1024)(128)(4,1)}), s8[4194304]{0:T(1024)(128)(4,1)S(1)}, s32[]{:S(2)}) async-start(s8[8388608]{0:T(1024)(128)(4,1)} %bitcast.12), calls=%async_computation.1 | async-start | bytes 8388608
  74.7 3.6 %collective-permute-start.4 = (f32[32]{0:T(128)S(1)}, f32[32]{0:T(128)S(1)}, u32[]{:S(2)}, u32[]{:S(2)}) collective-permute-start(f32[32]{0:T(128)S(1)} %get-tuple-element.8), channel_id=1, source_target_pairs={{0,2},{1,3},{2,0},{3,1},{4,6},{5,7},{6,4},{7,5},{8,10},{9,11},{10,... | collective-permute-start | bytes 392 | tf_op jit(solution)/shard_map/ppermute | solution.py:18
  78.3 1.1 %collective-permute-start.5 = (f32[32]{0:T(128)S(1)}, f32[32]{0:T(128)S(1)}, u32[]{:S(2)}, u32[]{:S(2)}) collective-permute-start(f32[32]{0:T(128)S(1)} %add.138), channel_id=1, source_target_pairs={{0,1},{1,0},{2,3},{3,2},{4,5},{5,4},{6,7},{7,6},{8,9},{9,8},{10,11... | collective-permute-start | bytes 392 | tf_op jit(solution)/shard_map/ppermute | solution.py:18

commit v6 on v4

--- a/solution.py
+++ b/solution.py
@@ -122,12 +122,32 @@
             team *= 2
         outer, inner = [s for s in strides if s >= team], [s for s in strides if s < team]
         cols = n // team * width
+        at = 0
 
         block = lax.optimization_barrier(jnp.concatenate([points, targets, noise_var[None, :]], axis=0))
-        mine = gather(block, n, outer)
+        rows = block.shape[0]
+        if team == 4 and n == 16:
+            sides = n // 2
+            groups = [list(range(base, n, 2)) for base in range(2)]
+            copies = jnp.broadcast_to(block[None], (sides, *block.shape))
+            got = lax.all_to_all(copies, "blk", 0, 0, axis_index_groups=groups).reshape(sides // 2, 2, rows, width)
+            index = lax.axis_index("blk")
+            side, at = index // 2 % 2, index // team * width
+
+            def lay(which):
+                part = lax.dynamic_index_in_dim(got, which, 1, keepdims=False)
+                return jnp.transpose(part, (1, 0, 2)).reshape(rows, cols)
+
+            mine = lay(side)
+            both = gather(jnp.concatenate([mine, lay(1 - side)], axis=1)[:-1], n, [1])
+        else:
+            mine = gather(block, n, outer)
+            both = gather(mine[:-1], n, inner)
         noise = mine[-1:]
-        both = gather(mine[:-1], n, inner)
         tile = kernel_block(both[:feats], (POINT_SCALE / lengthscale)[:, None], cols)
+
+        def own(x):
+            return lax.dynamic_slice_in_dim(x, at, width, 1)
 
         residual = direction = both[feats:]
         my_solution = jnp.zeros_like(block[feats:-1])
@@ -137,12 +157,12 @@
             if iteration == ITERS - 1:
                 curve = add_up(jnp.sum(direction[:, :cols] * my_applied, axis=1), n, inner)
                 step_size = (norm_now / curve)[:, None]
-                my_solution = my_solution + step_size * direction[:, :width]
-                return my_solution, residual[:, :width] - step_size * my_applied[:, :width]
+                my_solution = my_solution + step_size * own(direction)
+                return my_solution, own(residual) - step_size * own(my_applied)
             applied = gather(my_applied, n, inner)
             curve = jnp.sum(direction * applied, axis=1)
             step_size = (norm_now / curve)[:, None]
-            my_solution = my_solution + step_size * direction[:, :width]
+            my_solution = my_solution + step_size * own(direction)
             residual = residual - step_size * applied
             norm_next = jnp.sum(residual * residual, axis=1)
             direction = residual + (norm_next / norm_now)[:, None] * direction

time: 71.2 us -> 80.5 us (1.13)
  waiting for transfers between devices: 33 us -> 36.9 us
  matrix products: 12.2 us -> 15.8 us
  local copies, waits for them, and re-layouts: 0.12 us -> 2.21 us
    all_to_all x0 -> x1, waiting for transfers between devices: none -> 15.9 us  [body(): lax.all_to_all(copies, 'blk', 0, 0, axis_index_groups=groups)]
    ppermute x12 -> x9, waiting for transfers between devices: 33 us -> 21 us  [swap(): return lax.ppermute(x, 'blk', [(i, i ^ stride) for i in range(n)])]
    ppermute x12 -> x9, starting transfers between devices: 14 us -> 6.41 us  [swap(): return lax.ppermute(x, 'blk', [(i, i ^ stride) for i in range(n)])]
    all_to_all x0 -> x1, starting transfers between devices: none -> 7.28 us  [body(): lax.all_to_all(copies, 'blk', 0, 0, axis_index_groups=groups)]
    dot_general x4, matrix products: 6.3 us -> 9.86 us  [apply_block(): jnp.dot(jnp.concatenate(parts[:2], axis=0), tile[1], preferred_element_ty...]
    unnamed x0 -> x16, local copies, waits for them, and re-layouts: none -> 0.99 us
    broadcast_in_dim x0 -> x1, local copies, waits for them, and re-layouts: none -> 0.85 us  [body(): copies = jnp.broadcast_to(block[None], (sides, *block.shape))]
  transfers between devices with their start and end apart: 12 -> 10, of which waited for: 12 -> 10; matrix products, arithmetic and copies ran while one was open for 1% -> 1% of each run, Pallas kernels for 0% -> 0%
where the time goes in v6:
time: 80.5 us; the launch traced here: 80.3 us
  waiting for transfers between devices  36.9 us (46%)
  matrix products  15.8 us (20%)
  starting transfers between devices  13.7 us (17%)
  Pallas kernels  5.73 us (7%)
  other arithmetic  5.01 us (6%)
  local copies, waits for them, and re-layouts  2.21 us (3%)
  between operations  0.98 us (1%)
    ppermute x9, waiting for transfers between devices, swap(): return lax.ppermute(x, 'blk', [(i, i ^ stride) for i in range(n)])  21 us
    all_to_all x1, waiting for transfers between devices, body(): lax.all_to_all(copies, 'blk', 0, 0, axis_index_groups=groups)  15.9 us
    dot_general x4, matrix products, apply_block(): jnp.dot(jnp.concatenate(parts[:2], axis=0), tile[1], preferred_element_ty...  9.86 us
    all_to_all x1, starting transfers between devices, body(): lax.all_to_all(copies, 'blk', 0, 0, axis_index_groups=groups)  7.28 us
    ppermute x9, starting transfers between devices, swap(): return lax.ppermute(x, 'blk', [(i, i ^ stride) for i in range(n)])  6.41 us
    dot_general x4, matrix products, apply_block(): jnp.dot(jnp.concatenate(parts, axis=0), tile[0], preferred_element_type=j...  5.9 us
    pallas_call x1, Pallas kernels, kernel_block(): pl.pallas_call(build_kernel, grid=(total // block,), out_shape=(out, out)...  5.73 us
  transfers between devices with their start and end apart: 10, of which 10 were waited for; matrix products, arithmetic and copies ran while one was open for 1% of the time, Pallas kernels for 0%

profile of v6, /device:TPU:0, one launch (start us, length us, event | category | flops | bytes accessed | tf_op | source)
XLA Modules:
  0.0 80.3 jit_solution(13953622966743978286)
XLA Ops:
  0.6 0.8 pad_maximum_fusion.8
  1.4 0.8 %broadcast_in_dim.7 = f32[8,65,256]{2,1,0:T(8,128)} broadcast(f32[65,256]{1,0:T(8,128)S(1)} %pad_maximum_fusion.8), dimensions={1,2} | broadcast | bytes 599040 | tf_op jit(solution)/shard_map/broadcast_in_dim | solution.py:132
  2.3 7.3 %all-to-all-start = ((f32[8,65,256]{2,1,0:T(8,128)}), f32[8,65,256]{2,1,0:T(8,128)S(1)}, u32[]{:S(2)}, u32[]{:S(2)}) async-start(f32[8,65,256]{2,1,0:T(8,128)} %broadcast_in_dim.7), calls=%async_computation | async-start | bytes 1179648 | tf_op jit(solution)/shard_map/all_to_all | solution.py:133
  9.6 15.9 %all-to-all-done = f32[8,65,256]{2,1,0:T(8,128)S(1)} async-done(((f32[8,65,256]{2,1,0:T(8,128)}), f32[8,65,256]{2,1,0:T(8,128)S(1)}, u32[]{:S(2)}, u32[]{:S(2)}) %all-to-all-start) | async-done | bytes 532512 | tf_op jit(solution)/shard_map/all_to_all | solution.py:133
  26.1 0.7 divide_bitcast_fusion
  27.0 1.0 %collective-permute-done = f32[64,2048]{1,0:T(8,128)S(1)} collective-permute-done((f32[64,2048]{1,0:T(8,128)S(1)}, f32[64,2048]{1,0:T(8,128)S(1)}, u32[]{:S(2)}, u32[]{:S(2)}) %collective-permute-start) | collective-permute-done | bytes 524320 | tf_op jit(solution)/shard_map/ppermute | solution.py:18
  28.2 5.7 %shard_map.59 = (bf16[4096,1024]{1,0:T(8,128)(2,1)S(1)}, bf16[4096,1024]{1,0:T(8,128)(2,1)S(1)}) custom-call(f32[32,4096]{1,0:T(8,128)S(1)} %get-tuple-element.22.all_ref, f32[32,1024]{1,0:T(8,128)S(1)} %bitcast.35, f32[32,1]{1,0:T(8,128)S(1)} %copy.9.scale_ref), custom_call_target="tpu_custom_call" | custom-call | flops 2147483648 | bytes 17301504 | tf_op jit(solution)/shard_map/pallas_call | solution.py:88
  33.9 1.6 %fusion.33 = f32[64,1024]{1,0:T(8,128)S(1)} fusion(bf16[4096,1024]{1,0:T(8,128)(2,1)S(1)} %get-tuple-element.5, bf16[32,4096]{1,0:T(8,128)(2,1)S(1)} %get-tuple-element.32, bf16[32,4096]{1,0:T(8,128)(2,1)S(1)} %get-tuple-element.31), kind=kOutput, calls=%fused_computation.53 | convolution fusion | flops 537919488 | bytes 9175040 | tf_op jit(solution)/shard_map/dot_general | solution.py:110
  35.5 1.5 %fusion = f32[96,1024]{1,0:T(8,128)S(1)} fusion(bf16[4096,1024]{1,0:T(8,128)(2,1)S(1)} %get-tuple-element.4, bf16[32,4096]{1,0:T(8,128)(2,1)S(1)} %get-tuple-element.20, bf16[32,4096]{1,0:T(8,128)(2,1)S(1)} %get-tuple-element.32, bf16[32,4096]{1,0:T(8,128)(2,1)S(1)} %get-tuple-element.31), kind=kOutput, calls=%fused_computation.2 | convolution fusion | flops 807665664 | bytes 9568256 | tf_op jit(solution)/shard_map/dot_general | solution.py:109
  37.1 1.5 %collective-permute-start.1 = (f32[32,1024]{1,0:T(8,128)S(1)}, f32[32,1024]{1,0:T(8,128)S(1)}, u32[]{:S(2)}, u32[]{:S(2)}) collective-permute-start(f32[32,1024]{1,0:T(8,128)S(1)} %fusion.60), channel_id=1, source_target_pairs={{0,2},{1,3},{2,0},{3,1},{4,6},{5,7},{6,4},{7,5},{8,10},{9,11},{10,... | collective-permute-start | bytes 393224 | tf_op jit(solution)/shard_map/ppermute | solution.py:18
  38.6 4.1 %collective-permute-done.1 = f32[32,1024]{1,0:T(8,128)S(1)} collective-permute-done((f32[32,1024]{1,0:T(8,128)S(1)}, f32[32,1024]{1,0:T(8,128)S(1)}, u32[]{:S(2)}, u32[]{:S(2)}) %collective-permute-start.1) | collective-permute-done | bytes 131104 | tf_op jit(solution)/shard_map/ppermute | solution.py:18
  42.8 1.5 %collective-permute-done.2 = f32[32,2048]{1,0:T(8,128)S(1)} collective-permute-done((f32[32,2048]{1,0:T(8,128)S(1)}, f32[32,2048]{1,0:T(8,128)S(1)}, u32[]{:S(2)}, u32[]{:S(2)}) %collective-permute-start.2) | collective-permute-done | bytes 262176 | tf_op jit(solution)/shard_map/ppermute | solution.py:18
  44.5 0.3 multiply_reduce_fusion.4
  45.1 1.6 %fusion.37 = f32[64,1024]{1,0:T(8,128)S(1)} fusion(bf16[4096,1024]{1,0:T(8,128)(2,1)S(1)} %get-tuple-element.5, bf16[32,4096]{1,0:T(8,128)(2,1)S(1)} %get-tuple-element.30, bf16[32,4096]{1,0:T(8,128)(2,1)S(1)} %get-tuple-element.29), kind=kOutput, calls=%fused_computation.58 | convolution fusion | flops 537919488 | bytes 9175040 | tf_op jit(solution)/shard_map/dot_general | solution.py:110
  46.7 1.5 %fusion.6 = f32[96,1024]{1,0:T(8,128)S(1)} fusion(bf16[4096,1024]{1,0:T(8,128)(2,1)S(1)} %get-tuple-element.4, bf16[32,4096]{1,0:T(8,128)(2,1)S(1)} %get-tuple-element.18, bf16[32,4096]{1,0:T(8,128)(2,1)S(1)} %get-tuple-element.30, bf16[32,4096]{1,0:T(8,128)(2,1)S(1)} %get-tuple-element.29), kind=kOutput, calls=%fused_computation.8 | convolution fusion | flops 807665664 | bytes 9568256 | tf_op jit(solution)/shard_map/dot_general | solution.py:109
  48.2 1.5 %collective-permute-start.3 = (f32[32,1024]{1,0:T(8,128)S(1)}, f32[32,1024]{1,0:T(8,128)S(1)}, u32[]{:S(2)}, u32[]{:S(2)}) collective-permute-start(f32[32,1024]{1,0:T(8,128)S(1)} %fusion.55), channel_id=1, source_target_pairs={{0,2},{1,3},{2,0},{3,1},{4,6},{5,7},{6,4},{7,5},{8,10},{9,11},{10,... | collective-permute-start | bytes 393224 | tf_op jit(solution)/shard_map/ppermute | solution.py:18
  49.8 4.1 %collective-permute-done.3 = f32[32,1024]{1,0:T(8,128)S(1)} collective-permute-done((f32[32,1024]{1,0:T(8,128)S(1)}, f32[32,1024]{1,0:T(8,128)S(1)}, u32[]{:S(2)}, u32[]{:S(2)}) %collective-permute-start.3) | collective-permute-done | bytes 131104 | tf_op jit(solution)/shard_map/ppermute | solution.py:18
  54.0 1.5 %collective-permute-done.4 = f32[32,2048]{1,0:T(8,128)S(1)} collective-permute-done((f32[32,2048]{1,0:T(8,128)S(1)}, f32[32,2048]{1,0:T(8,128)S(1)}, u32[]{:S(2)}, u32[]{:S(2)}) %collective-permute-start.4) | collective-permute-done | bytes 262176 | tf_op jit(solution)/shard_map/ppermute | solution.py:18
  55.7 0.3 multiply_reduce_fusion.2
  56.2 1.6 %fusion.41 = f32[64,1024]{1,0:T(8,128)S(1)} fusion(bf16[4096,1024]{1,0:T(8,128)(2,1)S(1)} %get-tuple-element.5, bf16[32,4096]{1,0:T(8,128)(2,1)S(1)} %get-tuple-element.28, bf16[32,4096]{1,0:T(8,128)(2,1)S(1)} %get-tuple-element.27), kind=kOutput, calls=%fused_computation.63 | convolution fusion | flops 537919488 | bytes 9175040 | tf_op jit(solution)/shard_map/dot_general | solution.py:110
  57.8 1.5 %fusion.12 = f32[96,1024]{1,0:T(8,128)S(1)} fusion(bf16[4096,1024]{1,0:T(8,128)(2,1)S(1)} %get-tuple-element.4, bf16[32,4096]{1,0:T(8,128)(2,1)S(1)} %get-tuple-element.14, bf16[32,4096]{1,0:T(8,128)(2,1)S(1)} %get-tuple-element.28, bf16[32,4096]{1,0:T(8,128)(2,1)S(1)} %get-tuple-element.27), kind=kOutput, calls=%fused_computation.14 | convolution fusion | flops 807665664 | bytes 9568256 | tf_op jit(solution)/shard_map/dot_general | solution.py:109
  59.4 1.5 %collective-permute-start.5 = (f32[32,1024]{1,0:T(8,128)S(1)}, f32[32,1024]{1,0:T(8,128)S(1)}, u32[]{:S(2)}, u32[]{:S(2)}) collective-permute-start(f32[32,1024]{1,0:T(8,128)S(1)} %fusion.52), channel_id=1, source_target_pairs={{0,2},{1,3},{2,0},{3,1},{4,6},{5,7},{6,4},{7,5},{8,10},{9,11},{10,... | collective-permute-start | bytes 393224 | tf_op jit(solution)/shard_map/ppermute | solution.py:18
  60.9 4.1 %collective-permute-done.5 = f32[32,1024]{1,0:T(8,128)S(1)} collective-permute-done((f32[32,1024]{1,0:T(8,128)S(1)}, f32[32,1024]{1,0:T(8,128)S(1)}, u32[]{:S(2)}, u32[]{:S(2)}) %collective-permute-start.5) | collective-permute-done | bytes 131104 | tf_op jit(solution)/shard_map/ppermute | solution.py:18
  65.1 1.5 %collective-permute-done.6 = f32[32,2048]{1,0:T(8,128)S(1)} collective-permute-done((f32[32,2048]{1,0:T(8,128)S(1)}, f32[32,2048]{1,0:T(8,128)S(1)}, u32[]{:S(2)}, u32[]{:S(2)}) %collective-permute-start.6) | collective-permute-done | bytes 262176 | tf_op jit(solution)/shard_map/ppermute | solution.py:18
  66.8 0.3 multiply_reduce_fusion
  67.3 5.1 %fusion.45 = f32[64,1024]{1,0:T(8,128)S(1)} fusion(bf16[4096,1024]{1,0:T(8,128)(2,1)} %copy-done, bf16[32,4096]{1,0:T(8,128)(2,1)S(1)} %get-tuple-element.26, bf16[32,4096]{1,0:T(8,128)(2,1)S(1)} %get-tuple-element.25), kind=kOutput, calls=%fused_computation.68 | convolution fusion | flops 537919488 | bytes 9175040 | tf_op jit(solution)/shard_map/dot_general | solution.py:110
  72.5 0.7 slice-done.1
  73.2 1.5 %fusion.18 = f32[96,1024]{1,0:T(8,128)S(1)} fusion(bf16[4096,1024]{1,0:T(8,128)(2,1)S(1)} %bitcast.37, bf16[32,4096]{1,0:T(8,128)(2,1)S(1)} %get-tuple-element.10, bf16[32,4096]{1,0:T(8,128)(2,1)S(1)} %get-tuple-element.26, bf16[32,4096]{1,0:T(8,128)(2,1)S(1)} %get-tuple-element.25), kind=kOutput, calls=%fused_computation.20 | convolution fusion | flops 807665664 | bytes 9568256 | tf_op jit(solution)/shard_map/dot_general | solution.py:109
  74.8 1.5 %collective-permute-start.7 = (f32[32]{0:T(128)S(1)}, f32[32]{0:T(128)S(1)}, u32[]{:S(2)}, u32[]{:S(2)}) collective-permute-start(f32[32]{0:T(128)S(1)} %get-tuple-element.8), channel_id=1, source_target_pairs={{0,2},{1,3},{2,0},{3,1},{4,6},{5,7},{6,4},{7,5},{8,10},{9,11},{10,... | collective-permute-start | bytes 392 | tf_op jit(solution)/shard_map/ppermute | solution.py:18
  76.3 2.1 %collective-permute-done.7 = f32[32]{0:T(128)S(1)} collective-permute-done((f32[32]{0:T(128)S(1)}, f32[32]{0:T(128)S(1)}, u32[]{:S(2)}, u32[]{:S(2)}) %collective-permute-start.7) | collective-permute-done | bytes 160 | tf_op jit(solution)/shard_map/ppermute | solution.py:18
  78.4 1.1 %collective-permute-done.8 = f32[32]{0:T(128)S(1)} collective-permute-done((f32[32]{0:T(128)S(1)}, f32[32]{0:T(128)S(1)}, u32[]{:S(2)}, u32[]{:S(2)}) %collective-permute-start.8) | collective-permute-done | bytes 160 | tf_op jit(solution)/shard_map/ppermute | solution.py:18
  79.5 0.7 multiply_subtract_fusion.3
  (52 shorter events, 3.0 us)
Async XLA Ops:
  2.3 23.2 %all-to-all-start = ((f32[8,65,256]{2,1,0:T(8,128)}), f32[8,65,256]{2,1,0:T(8,128)S(1)}, u32[]{:S(2)}, u32[]{:S(2)}) async-start(f32[8,65,256]{2,1,0:T(8,128)} %broadcast_in_dim.7), calls=%async_computation | async-start | bytes 1179648 | tf_op jit(solution)/shard_map/all_to_all | solution.py:133
  26.0 2.0 %collective-permute-start = (f32[64,2048]{1,0:T(8,128)S(1)}, f32[64,2048]{1,0:T(8,128)S(1)}, u32[]{:S(2)}, u32[]{:S(2)}) collective-permute-start(f32[64,2048]{1,0:T(8,128)S(1)} %pad_maximum_fusion.1), channel_id=1, source_target_pairs={{0,1},{1,0},{2,3},{3,2},{4,5},{5,4},{6,7},{7,6},{8,9},{9,8},{10,11... | collective-permute-start | bytes 1572872 | tf_op jit(solution)/shard_map/ppermute | solution.py:18
  33.9 22.3 %copy-start = (bf16[4096,1024]{1,0:T(8,128)(2,1)}, bf16[4096,1024]{1,0:T(8,128)(2,1)S(1)}, u32[]{:S(2)}) copy-start(bf16[4096,1024]{1,0:T(8,128)(2,1)S(1)} %get-tuple-element.5) | copy-start | bytes 25165828
  33.9 23.9 %copy-start.1 = (bf16[4096,1024]{1,0:T(8,128)(2,1)}, bf16[4096,1024]{1,0:T(8,128)(2,1)S(1)}, u32[]{:S(2)}) copy-start(bf16[4096,1024]{1,0:T(8,128)(2,1)S(1)} %get-tuple-element.4) | copy-start | bytes 25165828
  37.1 5.6 %collective-permute-start.1 = (f32[32,1024]{1,0:T(8,128)S(1)}, f32[32,1024]{1,0:T(8,128)S(1)}, u32[]{:S(2)}, u32[]{:S(2)}) collective-permute-start(f32[32,1024]{1,0:T(8,128)S(1)} %fusion.60), channel_id=1, source_target_pairs={{0,2},{1,3},{2,0},{3,1},{4,6},{5,7},{6,4},{7,5},{8,10},{9,11},{10,... | collective-permute-start | bytes 393224 | tf_op jit(solution)/shard_map/ppermute | solution.py:18
  42.7 1.6 %collective-permute-start.2 = (f32[32,2048]{1,0:T(8,128)S(1)}, f32[32,2048]{1,0:T(8,128)S(1)}, u32[]{:S(2)}, u32[]{:S(2)}) collective-permute-start(f32[32,2048]{1,0:T(8,128)S(1)} %pad_maximum_fusion.5), channel_id=1, source_target_pairs={{0,1},{1,0},{2,3},{3,2},{4,5},{5,4},{6,7},{7,6},{8,9},{9,8},{10,11... | collective-permute-start | bytes 786440 | tf_op jit(solution)/shard_map/ppermute | solution.py:18
  48.2 5.6 %collective-permute-start.3 = (f32[32,1024]{1,0:T(8,128)S(1)}, f32[32,1024]{1,0:T(8,128)S(1)}, u32[]{:S(2)}, u32[]{:S(2)}) collective-permute-start(f32[32,1024]{1,0:T(8,128)S(1)} %fusion.55), channel_id=1, source_target_pairs={{0,2},{1,3},{2,0},{3,1},{4,6},{5,7},{6,4},{7,5},{8,10},{9,11},{10,... | collective-permute-start | bytes 393224 | tf_op jit(solution)/shard_map/ppermute | solution.py:18
  53.9 1.6 %collective-permute-start.4 = (f32[32,2048]{1,0:T(8,128)S(1)}, f32[32,2048]{1,0:T(8,128)S(1)}, u32[]{:S(2)}, u32[]{:S(2)}) collective-permute-start(f32[32,2048]{1,0:T(8,128)S(1)} %pad_maximum_fusion.6), channel_id=1, source_target_pairs={{0,1},{1,0},{2,3},{3,2},{4,5},{5,4},{6,7},{7,6},{8,9},{9,8},{10,11... | collective-permute-start | bytes 786440 | tf_op jit(solution)/shard_map/ppermute | solution.py:18
  59.4 5.6 %collective-permute-start.5 = (f32[32,1024]{1,0:T(8,128)S(1)}, f32[32,1024]{1,0:T(8,128)S(1)}, u32[]{:S(2)}, u32[]{:S(2)}) collective-permute-start(f32[32,1024]{1,0:T(8,128)S(1)} %fusion.52), channel_id=1, source_target_pairs={{0,2},{1,3},{2,0},{3,1},{4,6},{5,7},{6,4},{7,5},{8,10},{9,11},{10,... | collective-permute-start | bytes 393224 | tf_op jit(solution)/shard_map/ppermute | solution.py:18
  65.0 1.6 %collective-permute-start.6 = (f32[32,2048]{1,0:T(8,128)S(1)}, f32[32,2048]{1,0:T(8,128)S(1)}, u32[]{:S(2)}, u32[]{:S(2)}) collective-permute-start(f32[32,2048]{1,0:T(8,128)S(1)} %pad_maximum_fusion.7), channel_id=1, source_target_pairs={{0,1},{1,0},{2,3},{3,2},{4,5},{5,4},{6,7},{7,6},{8,9},{9,8},{10,11... | collective-permute-start | bytes 786440 | tf_op jit(solution)/shard_map/ppermute | solution.py:18
  67.3 5.1 %slice-start = ((s8[8388608]{0:T(1024)(128)(4,1)}), s8[4194304]{0:T(1024)(128)(4,1)S(1)}, s32[]{:S(2)}) async-start(s8[8388608]{0:T(1024)(128)(4,1)} %bitcast.36), calls=%async_computation.1 | async-start | bytes 8388608
  67.3 5.8 %slice-start.1 = ((s8[8388608]{0:T(1024)(128)(4,1)}), s8[4194304]{0:T(1024)(128)(4,1)S(1)}, s32[]{:S(2)}) async-start(s8[8388608]{0:T(1024)(128)(4,1)} %bitcast.36), calls=%async_computation.2 | async-start | bytes 8388608
  74.8 3.6 %collective-permute-start.7 = (f32[32]{0:T(128)S(1)}, f32[32]{0:T(128)S(1)}, u32[]{:S(2)}, u32[]{:S(2)}) collective-permute-start(f32[32]{0:T(128)S(1)} %get-tuple-element.8), channel_id=1, source_target_pairs={{0,2},{1,3},{2,0},{3,1},{4,6},{5,7},{6,4},{7,5},{8,10},{9,11},{10,... | collective-permute-start | bytes 392 | tf_op jit(solution)/shard_map/ppermute | solution.py:18
  78.4 1.1 %collective-permute-start.8 = (f32[32]{0:T(128)S(1)}, f32[32]{0:T(128)S(1)}, u32[]{:S(2)}, u32[]{:S(2)}) collective-permute-start(f32[32]{0:T(128)S(1)} %add.137), channel_id=1, source_target_pairs={{0,1},{1,0},{2,3},{3,2},{4,5},{5,4},{6,7},{7,6},{8,9},{9,8},{10,11... | collective-permute-start | bytes 392 | tf_op jit(solution)/shard_map/ppermute | solution.py:18

commit v7 on v4

v7 whole, which is shorter than its diff:
```python
import math

import jax
import jax.numpy as jnp
from jax import lax
from jax.experimental import pallas as pl
from jax.experimental.pallas import tpu as pltpu
from jax.sharding import PartitionSpec as P

ITERS = 4
TILE_BYTES = 16 << 20
VMEM_BYTES = 16 << 20
NORM_ROWS = 64
POINT_SCALE = math.sqrt(math.log2(math.e))


def swap(x, n, stride):
    return lax.ppermute(x, "blk", [(i, i ^ stride) for i in range(n)])


def add_up(x, n, strides):
    for stride in strides:
        x = x + swap(x, n, stride)
    return x


def split(x, parts):
    out = []
    for _ in range(parts):
        high = lax.reduce_precision(x, 8, 7)
        out.append(high.astype(jnp.bfloat16))
        x = x - high
    return out


def halve(x):
    high = x.astype(jnp.bfloat16)
    return high, x - high.astype(jnp.float32)


def operands(pts):
    high, rest = halve(pts)
    mid, rest = halve(rest)
    low = rest.astype(jnp.bfloat16)
    norms = -0.5 * jnp.sum(pts * pts, axis=0, keepdims=True)
    row = lax.broadcasted_iota(jnp.int32, (NORM_ROWS, pts.shape[1]), 0)
    left = jnp.where((row >= 3) & (row < 6), 1.0, 0.0)
    right = jnp.where(row < 3, 1.0, 0.0)
    for k in range(3):
        part, norms = halve(norms)
        part = part.astype(jnp.float32)
        left = jnp.where(row == k, part, left)
        right = jnp.where(row == 3 + k, part, right)
    left = jnp.concatenate([high, high, mid, high, low, mid, left.astype(jnp.bfloat16)], axis=0)
    right = jnp.concatenate([high, mid, high, low, high, mid, right.astype(jnp.bfloat16)], axis=0)
    return left, right


def build_kernel(rows_ref, mine_ref, scale_ref, high_ref, low_ref, right_ref):
    @pl.when(pl.program_id(0) == 0)
    def _():
        right_ref[...] = operands(mine_ref[...] * scale_ref[...])[1]

    left = jnp.transpose(operands(rows_ref[...] * scale_ref[...])[0])
    cols = right_ref.shape[1]
    step = min(cols, 256)
    for at in range(0, cols, step):
        here = pl.ds(at, step)
        power = jnp.dot(left, right_ref[:, here], preferred_element_type=jnp.float32)
        high, rest = halve(jnp.exp2(power))
        high_ref[:, here] = high
        low_ref[:, here] = rest.astype(jnp.bfloat16)


def build_piece(rows, mine, scale):
    feats, total = rows.shape
    cols = mine.shape[1]
    block = min(total, 512)
    out = jax.ShapeDtypeStruct((total, cols), jnp.bfloat16)
    spec = pl.BlockSpec((block, cols), lambda i: (i, 0))
    return pl.pallas_call(
        build_kernel,
        grid=(total // block,),
        out_shape=(out, out),
        in_specs=[
            pl.BlockSpec((feats, block), lambda i: (0, i)),
            pl.BlockSpec((feats, cols), lambda i: (0, 0)),
            pl.BlockSpec((feats, 1), lambda i: (0, 0)),
        ],
        out_specs=(spec, spec),
        scratch_shapes=[pltpu.VMEM((6 * feats + NORM_ROWS, cols), jnp.bfloat16)],
        compiler_params=pltpu.CompilerParams(vmem_limit_bytes=VMEM_BYTES),
        cost_estimate=pl.CostEstimate(
            flops=2 * total * cols * 256, bytes_accessed=4 * total * (cols + feats), transcendentals=total * cols
        ),
    )(rows, mine, scale)


def apply_piece(vectors, piece):
    parts = split(vectors, 3)
    high = jnp.dot(jnp.concatenate(parts, axis=0), piece[0], preferred_element_type=jnp.float32)
    low = jnp.dot(jnp.concatenate(parts[:2], axis=0), piece[1], preferred_element_type=jnp.float32)
    return high, low


def solution(mesh):
    n = mesh.shape["blk"]
    strides = [1 << k for k in reversed(range(n.bit_length() - 1))]

    def body(points, lengthscale, noise_var, targets):
        feats, width = points.shape
        probes = targets.shape[0]
        team = min(n, 4)
        while team < n and (n * width) * (n * width) // team * 4 > TILE_BYTES:
            team *= 2
        outer, inner = [s for s in strides if s >= team], [s for s in strides if s < team]

        def arrivals(x):
            pieces = [x]
            for stride in inner:
                pieces.append(swap(jnp.concatenate(pieces, axis=1), n, stride))
            return pieces

        mine = lax.optimization_barrier(jnp.concatenate([points, targets, noise_var[None, :]], axis=0))
        for stride in outer:
            mine = jnp.concatenate([mine, swap(mine, n, stride)], axis=1)
        noise = mine[-1:]
        scale = (POINT_SCALE / lengthscale)[:, None]
        first = arrivals(mine[:-1])
        tile = [build_piece(x[:feats], mine[:feats], scale) for x in first]

        def operator(pieces):
            terms = [apply_piece(x, piece) for x, piece in zip(pieces, tile)]
            high, low = (sum(t[1:], t[0]) for t in zip(*terms))
            corrections = (high[probes : 2 * probes] + low[:probes]) + (high[2 * probes :] + low[probes:])
            return high[:probes] + corrections + noise * pieces[0]

        starts = [x[feats:] for x in first]
        residual = direction = jnp.concatenate(starts, axis=1)
        cols = noise.shape[1]
        my_solution = jnp.zeros_like(direction[:, :width])
        norm_now = jnp.sum(residual * residual, axis=1)
        my_applied = my_image = operator(starts)
        for iteration in range(ITERS - 1):
            pieces = arrivals(my_applied)
            my_next = operator(pieces)
            applied = jnp.concatenate(pieces, axis=1)
            curve = jnp.sum(direction * applied, axis=1)
            step_size = (norm_now / curve)[:, None]
            my_solution = my_solution + step_size * direction[:, :width]
            residual = residual - step_size * applied
            norm_next = jnp.sum(residual * residual, axis=1)
            ratio = (norm_next / norm_now)[:, None]
            my_image = my_image - step_size * my_next
            my_applied = my_image + ratio * my_applied
            direction = residual + ratio * direction
            norm_now = norm_next
        curve = add_up(jnp.sum(direction[:, :cols] * my_applied, axis=1), n, inner)
        step_size = (norm_now / curve)[:, None]
        my_solution = my_solution + step_size * direction[:, :width]
        return my_solution, residual[:, :width] - step_size * my_applied[:, :width]

    in_specs = (P("groups", "blk"), P("groups"), P(("groups", "blk")), P("groups", "blk"))
    out_specs = (P("groups", "blk"), P("groups", "blk"))
    return jax.shard_map(body, mesh=mesh, in_specs=in_specs, out_specs=out_specs, check_vma=False)
```

time: 71.2 us -> 65.6 us (0.921)
  waiting for transfers between devices: 33 us -> 24.5 us
  matrix products: 12.2 us -> 14.5 us
    ppermute x12, waiting for transfers between devices: 33 us -> 24.5 us  [swap(): return lax.ppermute(x, 'blk', [(i, i ^ stride) for i in range(n)])]
    dot_general x8 -> x24, matrix products: 12.2 us -> 14.5 us  [the longest x12 7.31 us: apply_piece(): jnp.dot(jnp.concatenate(parts[:2], axis=0), piece[1], preferred_element_t...]
    pallas_call x1 -> x3, Pallas kernels: 5.74 us -> 6.24 us  [build_piece(): pl.pallas_call(build_kernel, grid=(total // block,), out_shape=(out, out)...]
  transfers between devices with their start and end apart: 12 -> 12, of which waited for: 12 -> 11; matrix products, arithmetic and copies ran while one was open for 1% -> 10% of each run, Pallas kernels for 0% -> 5%
where the time goes in v7:
time: 65.6 us; the launch traced here: 65.4 us
  waiting for transfers between devices  24.5 us (37%)
  matrix products  14.5 us (22%)
  starting transfers between devices  14 us (21%)
  Pallas kernels  6.24 us (10%)
  other arithmetic  5.06 us (8%)
  between operations  0.97 us (1%)
    ppermute x12, waiting for transfers between devices, swap(): return lax.ppermute(x, 'blk', [(i, i ^ stride) for i in range(n)])  24.5 us
    ppermute x12, starting transfers between devices, swap(): return lax.ppermute(x, 'blk', [(i, i ^ stride) for i in range(n)])  14 us
    dot_general x12, matrix products, apply_piece(): jnp.dot(jnp.concatenate(parts[:2], axis=0), piece[1], preferred_element_t...  7.31 us
    dot_general x12, matrix products, apply_piece(): jnp.dot(jnp.concatenate(parts, axis=0), piece[0], preferred_element_type=...  7.21 us
    pallas_call x3, Pallas kernels, build_piece(): pl.pallas_call(build_kernel, grid=(total // block,), out_shape=(out, out)...  6.24 us
  transfers between devices with their start and end apart: 12, of which 11 were waited for; matrix products, arithmetic and copies ran while one was open for 10% of the time, Pallas kernels for 5%

profile of v7, /device:TPU:0, one launch (start us, length us, event | category | flops | bytes accessed | tf_op | source)
XLA Modules:
  0.0 65.4 jit_solution(15742292076547081681)
XLA Ops:
  0.6 0.8 %pad_maximum_fusion.10 = f32[65,256]{1,0:T(8,128)S(1)} fusion(f32[1,256]{1,0:T(1,128)} %bitcast.32, f32[32,256]{1,0:T(8,128)} %param.7, f32[32,256]{1,0:T(8,128)} %param.4), kind=kLoop, calls=%fused_computation.250 | loop fusion | flops 33280 | bytes 133120 | tf_op jit(solution)/shard_map/concatenate | solution.py:124
  1.4 4.0 %collective-permute-start = (f32[65,256]{1,0:T(8,128)S(1)}, f32[65,256]{1,0:T(8,128)S(1)}, u32[]{:S(2)}, u32[]{:S(2)}) collective-permute-start(f32[65,256]{1,0:T(8,128)S(1)} %pad_maximum_fusion.10), channel_id=1, source_target_pairs={{0,8},{1,9},{2,10},{3,11},{4,12},{5,13},{6,14},{7,15},{8,0},{9,1},... | collective-permute-start | bytes 199688 | tf_op jit(solution)/shard_map/ppermute | solution.py:18
  5.5 3.9 %collective-permute-done = f32[65,256]{1,0:T(8,128)S(1)} collective-permute-done((f32[65,256]{1,0:T(8,128)S(1)}, f32[65,256]{1,0:T(8,128)S(1)}, u32[]{:S(2)}, u32[]{:S(2)}) %collective-permute-start) | collective-permute-done | bytes 66592 | tf_op jit(solution)/shard_map/ppermute | solution.py:18
  9.4 0.7 %collective-permute-start.1 = (f32[65,512]{1,0:T(8,128)S(1)}, f32[65,512]{1,0:T(8,128)S(1)}, u32[]{:S(2)}, u32[]{:S(2)}) collective-permute-start(f32[65,512]{1,0:T(8,128)S(1)} %pad_maximum_fusion.9), channel_id=1, source_target_pairs={{0,4},{1,5},{2,6},{3,7},{4,0},{5,1},{6,2},{7,3},{8,12},{9,13},{10,... | collective-permute-start | bytes 399368 | tf_op jit(solution)/shard_map/ppermute | solution.py:18
  10.1 0.7 %divide_bitcast_fusion = f32[32,1]{0,1:T(1,128)S(1)} fusion(f32[32]{0:T(128)} %param.5), kind=kLoop, calls=%fused_computation.262 | loop fusion | flops 32 | bytes 256 | tf_op jit(solution)/shard_map/broadcast_in_dim | solution.py:128
  10.9 3.7 %collective-permute-done.1 = f32[65,512]{1,0:T(8,128)S(1)} collective-permute-done((f32[65,512]{1,0:T(8,128)S(1)}, f32[65,512]{1,0:T(8,128)S(1)}, u32[]{:S(2)}, u32[]{:S(2)}) %collective-permute-start.1) | collective-permute-done | bytes 133152 | tf_op jit(solution)/shard_map/ppermute | solution.py:18
  14.7 1.8 %collective-permute-start.2 = (f32[64,1024]{1,0:T(8,128)S(1)}, f32[64,1024]{1,0:T(8,128)S(1)}, u32[]{:S(2)}, u32[]{:S(2)}) collective-permute-start(f32[64,1024]{1,0:T(8,128)S(1)} %slice.148), channel_id=1, source_target_pairs={{0,2},{1,3},{2,0},{3,1},{4,6},{5,7},{6,4},{7,5},{8,10},{9,11},{10,... | collective-permute-start | bytes 786440 | tf_op jit(solution)/shard_map/ppermute | solution.py:18
  16.5 1.5 %shard_map.59 = (bf16[1024,1024]{1,0:T(8,128)(2,1)S(1)}, bf16[1024,1024]{1,0:T(8,128)(2,1)S(1)}) custom-call(f32[32,1024]{1,0:T(8,128)S(1)} %get-tuple-element.43.rows_ref.mine_ref, f32[32,1024]{1,0:T(8,128)S(1)} %get-tuple-element.43.rows_ref.mine_ref, f32[32,1]{1,0:T(8,128)S(1)} %copy.6.scale_ref), custom_call_target="tpu_custom_call" | custom-call | flops 536870912 | bytes 4325376 | tf_op jit(solution)/shard_map/pallas_call | solution.py:81
  19.0 2.1 %collective-permute-done.2 = f32[64,1024]{1,0:T(8,128)S(1)} collective-permute-done((f32[64,1024]{1,0:T(8,128)S(1)}, f32[64,1024]{1,0:T(8,128)S(1)}, u32[]{:S(2)}, u32[]{:S(2)}) %collective-permute-start.2) | collective-permute-done | bytes 262176 | tf_op jit(solution)/shard_map/ppermute | solution.py:18
  21.3 1.6 %shard_map.60 = (bf16[1024,1024]{1,0:T(8,128)(2,1)S(1)}, bf16[1024,1024]{1,0:T(8,128)(2,1)S(1)}) custom-call(f32[32,1024]{1,0:T(8,128)S(1)} %get-tuple-element.57.rows_ref, f32[32,1024]{1,0:T(8,128)S(1)} %get-tuple-element.43.rows_ref.mine_ref, f32[32,1]{1,0:T(8,128)S(1)} %copy.6.scale_ref), custom_call_target="tpu_custom_call" | custom-call | flops 536870912 | bytes 4325376 | tf_op jit(solution)/shard_map/pallas_call | solution.py:81
  23.5 3.1 %shard_map.61 = (bf16[2048,1024]{1,0:T(8,128)(2,1)S(1)}, bf16[2048,1024]{1,0:T(8,128)(2,1)S(1)}) custom-call(f32[32,2048]{1,0:T(8,128)S(1)} %get-tuple-element.38.rows_ref, f32[32,1024]{1,0:T(8,128)S(1)} %get-tuple-element.43.rows_ref.mine_ref, f32[32,1]{1,0:T(8,128)S(1)} %copy.6.scale_ref), custom_call_target="tpu_custom_call" | custom-call | flops 1073741824 | bytes 8650752 | tf_op jit(solution)/shard_map/pallas_call | solution.py:81
  26.6 0.9 %convolution_add_fusion.10 = f32[64,1024]{1,0:T(8,128)S(1)} fusion(f32[64,1024]{1,0:T(8,128)S(1)} %convolution_add_fusion.11, bf16[2048,1024]{1,0:T(8,128)(2,1)S(1)} %get-tuple-element.13, bf16[32,2048]{1,0:T(8,128)(2,1)S(1)} %get-tuple-element.36, bf16[32,2048]{1,0:T(8,128)(2,1)S(1)} %get-tuple-element.35), kind=kOutput, calls=%fused_computation.14 | convolution fusion | flops 269025280 | bytes 4980736 | tf_op jit(solution)/shard_map/dot_general | solution.py:102
  27.5 0.8 %fusion.4 = f32[96,1024]{1,0:T(8,128)S(1)} fusion(bf16[2048,1024]{1,0:T(8,128)(2,1)S(1)} %get-tuple-element.10, bf16[32,2048]{1,0:T(8,128)(2,1)S(1)} %get-tuple-element.37, bf16[32,2048]{1,0:T(8,128)(2,1)S(1)} %get-tuple-element.36, bf16[32,2048]{1,0:T(8,128)(2,1)S(1)} %get-tuple-element.35), kind=kOutput, calls=%fused_computation.34 | convolution fusion | flops 403832832 | bytes 4980736 | tf_op jit(solution)/shard_map/dot_general | solution.py:101
  28.9 1.8 %collective-permute-start.4 = (f32[32,1024]{1,0:T(8,128)S(1)}, f32[32,1024]{1,0:T(8,128)S(1)}, u32[]{:S(2)}, u32[]{:S(2)}) collective-permute-start(f32[32,1024]{1,0:T(8,128)S(1)} %get-tuple-element.33), channel_id=1, source_target_pairs={{0,2},{1,3},{2,0},{3,1},{4,6},{5,7},{6,4},{7,5},{8,10},{9,11},{10,... | collective-permute-start | bytes 393224 | tf_op jit(solution)/shard_map/ppermute | solution.py:18
  31.7 3.2 %collective-permute-done.4 = f32[32,1024]{1,0:T(8,128)S(1)} collective-permute-done((f32[32,1024]{1,0:T(8,128)S(1)}, f32[32,1024]{1,0:T(8,128)S(1)}, u32[]{:S(2)}, u32[]{:S(2)}) %collective-permute-start.4) | collective-permute-done | bytes 131104 | tf_op jit(solution)/shard_map/ppermute | solution.py:18
  35.5 1.0 %collective-permute-done.5 = f32[32,2048]{1,0:T(8,128)S(1)} collective-permute-done((f32[32,2048]{1,0:T(8,128)S(1)}, f32[32,2048]{1,0:T(8,128)S(1)}, u32[]{:S(2)}, u32[]{:S(2)}) %collective-permute-start.5) | collective-permute-done | bytes 262176 | tf_op jit(solution)/shard_map/ppermute | solution.py:18
  37.0 0.8 %convolution_add_fusion.8 = f32[64,1024]{1,0:T(8,128)S(1)} fusion(f32[64,1024]{1,0:T(8,128)S(1)} %convolution_add_fusion.9, bf16[2048,1024]{1,0:T(8,128)(2,1)S(1)} %get-tuple-element.13, bf16[32,2048]{1,0:T(8,128)(2,1)S(1)} %get-tuple-element.51, bf16[32,2048]{1,0:T(8,128)(2,1)S(1)} %get-tuple-element.52), kind=kOutput, calls=%fused_computation.12 | convolution fusion | flops 269025280 | bytes 4980736 | tf_op jit(solution)/shard_map/dot_general | solution.py:102
  37.9 0.8 %fusion.10 = f32[96,1024]{1,0:T(8,128)S(1)} fusion(bf16[2048,1024]{1,0:T(8,128)(2,1)S(1)} %get-tuple-element.10, bf16[32,2048]{1,0:T(8,128)(2,1)S(1)} %get-tuple-element.50, bf16[32,2048]{1,0:T(8,128)(2,1)S(1)} %get-tuple-element.51, bf16[32,2048]{1,0:T(8,128)(2,1)S(1)} %get-tuple-element.52), kind=kOutput, calls=%fused_computation.40 | convolution fusion | flops 403832832 | bytes 4980736 | tf_op jit(solution)/shard_map/dot_general | solution.py:101
  39.3 1.8 %collective-permute-start.6 = (f32[32,1024]{1,0:T(8,128)S(1)}, f32[32,1024]{1,0:T(8,128)S(1)}, u32[]{:S(2)}, u32[]{:S(2)}) collective-permute-start(f32[32,1024]{1,0:T(8,128)S(1)} %get-tuple-element.28), channel_id=1, source_target_pairs={{0,2},{1,3},{2,0},{3,1},{4,6},{5,7},{6,4},{7,5},{8,10},{9,11},{10,... | collective-permute-start | bytes 393224 | tf_op jit(solution)/shard_map/ppermute | solution.py:18
  42.1 2.8 %collective-permute-done.6 = f32[32,1024]{1,0:T(8,128)S(1)} collective-permute-done((f32[32,1024]{1,0:T(8,128)S(1)}, f32[32,1024]{1,0:T(8,128)S(1)}, u32[]{:S(2)}, u32[]{:S(2)}) %collective-permute-start.6) | collective-permute-done | bytes 131104 | tf_op jit(solution)/shard_map/ppermute | solution.py:18
  45.6 1.0 %collective-permute-done.7 = f32[32,2048]{1,0:T(8,128)S(1)} collective-permute-done((f32[32,2048]{1,0:T(8,128)S(1)}, f32[32,2048]{1,0:T(8,128)S(1)}, u32[]{:S(2)}, u32[]{:S(2)}) %collective-permute-start.7) | collective-permute-done | bytes 262176 | tf_op jit(solution)/shard_map/ppermute | solution.py:18
  47.2 0.9 %convolution_add_fusion.6 = f32[64,1024]{1,0:T(8,128)S(1)} fusion(f32[64,1024]{1,0:T(8,128)S(1)} %convolution_add_fusion.7, bf16[2048,1024]{1,0:T(8,128)(2,1)S(1)} %get-tuple-element.13, bf16[32,2048]{1,0:T(8,128)(2,1)S(1)} %get-tuple-element.48, bf16[32,2048]{1,0:T(8,128)(2,1)S(1)} %get-tuple-element.49), kind=kOutput, calls=%fused_computation.10 | convolution fusion | flops 269025280 | bytes 4980736 | tf_op jit(solution)/shard_map/dot_general | solution.py:102
  48.1 0.8 %fusion.16 = f32[96,1024]{1,0:T(8,128)S(1)} fusion(bf16[2048,1024]{1,0:T(8,128)(2,1)S(1)} %get-tuple-element.10, bf16[32,2048]{1,0:T(8,128)(2,1)S(1)} %get-tuple-element.47, bf16[32,2048]{1,0:T(8,128)(2,1)S(1)} %get-tuple-element.48, bf16[32,2048]{1,0:T(8,128)(2,1)S(1)} %get-tuple-element.49), kind=kOutput, calls=%fused_computation.46 | convolution fusion | flops 403832832 | bytes 4980736 | tf_op jit(solution)/shard_map/dot_general | solution.py:101
  49.5 1.8 %collective-permute-start.8 = (f32[32,1024]{1,0:T(8,128)S(1)}, f32[32,1024]{1,0:T(8,128)S(1)}, u32[]{:S(2)}, u32[]{:S(2)}) collective-permute-start(f32[32,1024]{1,0:T(8,128)S(1)} %get-tuple-element.19), channel_id=1, source_target_pairs={{0,2},{1,3},{2,0},{3,1},{4,6},{5,7},{6,4},{7,5},{8,10},{9,11},{10,... | collective-permute-start | bytes 393224 | tf_op jit(solution)/shard_map/ppermute | solution.py:18
  52.3 2.8 %collective-permute-done.8 = f32[32,1024]{1,0:T(8,128)S(1)} collective-permute-done((f32[32,1024]{1,0:T(8,128)S(1)}, f32[32,1024]{1,0:T(8,128)S(1)}, u32[]{:S(2)}, u32[]{:S(2)}) %collective-permute-start.8) | collective-permute-done | bytes 131104 | tf_op jit(solution)/shard_map/ppermute | solution.py:18
  55.8 1.0 %collective-permute-done.9 = f32[32,2048]{1,0:T(8,128)S(1)} collective-permute-done((f32[32,2048]{1,0:T(8,128)S(1)}, f32[32,2048]{1,0:T(8,128)S(1)}, u32[]{:S(2)}, u32[]{:S(2)}) %collective-permute-start.9) | collective-permute-done | bytes 262176 | tf_op jit(solution)/shard_map/ppermute | solution.py:18
  57.4 0.8 %convolution_add_fusion.4 = f32[64,1024]{1,0:T(8,128)S(1)} fusion(f32[64,1024]{1,0:T(8,128)S(1)} %convolution_add_fusion.5, bf16[2048,1024]{1,0:T(8,128)(2,1)S(1)} %get-tuple-element.13, bf16[32,2048]{1,0:T(8,128)(2,1)S(1)} %get-tuple-element.45, bf16[32,2048]{1,0:T(8,128)(2,1)S(1)} %get-tuple-element.46), kind=kOutput, calls=%fused_computation.8 | convolution fusion | flops 269025280 | bytes 4980736 | tf_op jit(solution)/shard_map/dot_general | solution.py:102
  58.2 0.8 %fusion.22 = f32[96,1024]{1,0:T(8,128)S(1)} fusion(bf16[2048,1024]{1,0:T(8,128)(2,1)S(1)} %get-tuple-element.10, bf16[32,2048]{1,0:T(8,128)(2,1)S(1)} %get-tuple-element.44, bf16[32,2048]{1,0:T(8,128)(2,1)S(1)} %get-tuple-element.45, bf16[32,2048]{1,0:T(8,128)(2,1)S(1)} %get-tuple-element.46), kind=kOutput, calls=%fused_computation.52 | convolution fusion | flops 403832832 | bytes 4980736 | tf_op jit(solution)/shard_map/dot_general | solution.py:101
  59.9 1.8 %collective-permute-start.10 = (f32[32]{0:T(128)S(1)}, f32[32]{0:T(128)S(1)}, u32[]{:S(2)}, u32[]{:S(2)}) collective-permute-start(f32[32]{0:T(128)S(1)} %get-tuple-element.16), channel_id=1, source_target_pairs={{0,2},{1,3},{2,0},{3,1},{4,6},{5,7},{6,4},{7,5},{8,10},{9,11},{10,... | collective-permute-start | bytes 392 | tf_op jit(solution)/shard_map/ppermute | solution.py:18
  61.7 1.8 %collective-permute-done.10 = f32[32]{0:T(128)S(1)} collective-permute-done((f32[32]{0:T(128)S(1)}, f32[32]{0:T(128)S(1)}, u32[]{:S(2)}, u32[]{:S(2)}) %collective-permute-start.10) | collective-permute-done | bytes 160 | tf_op jit(solution)/shard_map/ppermute | solution.py:18
  63.5 1.1 %collective-permute-done.11 = f32[32]{0:T(128)S(1)} collective-permute-done((f32[32]{0:T(128)S(1)}, f32[32]{0:T(128)S(1)}, u32[]{:S(2)}, u32[]{:S(2)}) %collective-permute-start.11) | collective-permute-done | bytes 160 | tf_op jit(solution)/shard_map/ppermute | solution.py:18
  64.6 0.7 %fusion.156 = (f32[32,256]{1,0:T(8,128)}, f32[32,256]{1,0:T(8,128)}) fusion(f32[32,1024]{1,0:T(8,128)S(1)} %get-tuple-element.17, f32[32,4096]{1,0:T(8,128)S(1)} %get-tuple-element.22, f32[32]{0:T(128)S(1)} %add_divide_fusion, f32[32,4096]{1,0:T(8,128)S(1)} %multiply_add_fusion, f32[32,4096]{1,0:T(8,128)S(1)} %get-tuple-element.24, f32[32]{0:T(128)S(1)} %div.57, ...), kind=kLoop, calls=%fused_computation.252 | loop fusion | flops 73728 | bytes 262656 | tf_op jit(solution)/shard_map/sub | solution.py:161
  (62 shorter events, 11.1 us)
Async XLA Ops:
  1.4 7.9 %collective-permute-start = (f32[65,256]{1,0:T(8,128)S(1)}, f32[65,256]{1,0:T(8,128)S(1)}, u32[]{:S(2)}, u32[]{:S(2)}) collective-permute-start(f32[65,256]{1,0:T(8,128)S(1)} %pad_maximum_fusion.10), channel_id=1, source_target_pairs={{0,8},{1,9},{2,10},{3,11},{4,12},{5,13},{6,14},{7,15},{8,0},{9,1},... | collective-permute-start | bytes 199688 | tf_op jit(solution)/shard_map/ppermute | solution.py:18
  9.4 5.2 %collective-permute-start.1 = (f32[65,512]{1,0:T(8,128)S(1)}, f32[65,512]{1,0:T(8,128)S(1)}, u32[]{:S(2)}, u32[]{:S(2)}) collective-permute-start(f32[65,512]{1,0:T(8,128)S(1)} %pad_maximum_fusion.9), channel_id=1, source_target_pairs={{0,4},{1,5},{2,6},{3,7},{4,0},{5,1},{6,2},{7,3},{8,12},{9,13},{10,... | collective-permute-start | bytes 399368 | tf_op jit(solution)/shard_map/ppermute | solution.py:18
  14.7 6.4 %collective-permute-start.2 = (f32[64,1024]{1,0:T(8,128)S(1)}, f32[64,1024]{1,0:T(8,128)S(1)}, u32[]{:S(2)}, u32[]{:S(2)}) collective-permute-start(f32[64,1024]{1,0:T(8,128)S(1)} %slice.148), channel_id=1, source_target_pairs={{0,2},{1,3},{2,0},{3,1},{4,6},{5,7},{6,4},{7,5},{8,10},{9,11},{10,... | collective-permute-start | bytes 786440 | tf_op jit(solution)/shard_map/ppermute | solution.py:18
  21.2 2.2 %collective-permute-start.3 = (f32[64,2048]{1,0:T(8,128)S(1)}, f32[64,2048]{1,0:T(8,128)S(1)}, u32[]{:S(2)}, u32[]{:S(2)}) collective-permute-start(f32[64,2048]{1,0:T(8,128)S(1)} %pad_maximum_fusion), channel_id=1, source_target_pairs={{0,1},{1,0},{2,3},{3,2},{4,5},{5,4},{6,7},{7,6},{8,9},{9,8},{10,11... | collective-permute-start | bytes 1572872 | tf_op jit(solution)/shard_map/ppermute | solution.py:18
  28.9 6.0 %collective-permute-start.4 = (f32[32,1024]{1,0:T(8,128)S(1)}, f32[32,1024]{1,0:T(8,128)S(1)}, u32[]{:S(2)}, u32[]{:S(2)}) collective-permute-start(f32[32,1024]{1,0:T(8,128)S(1)} %get-tuple-element.33), channel_id=1, source_target_pairs={{0,2},{1,3},{2,0},{3,1},{4,6},{5,7},{6,4},{7,5},{8,10},{9,11},{10,... | collective-permute-start | bytes 393224 | tf_op jit(solution)/shard_map/ppermute | solution.py:18
  34.9 1.6 %collective-permute-start.5 = (f32[32,2048]{1,0:T(8,128)S(1)}, f32[32,2048]{1,0:T(8,128)S(1)}, u32[]{:S(2)}, u32[]{:S(2)}) collective-permute-start(f32[32,2048]{1,0:T(8,128)S(1)} %pad_maximum_fusion.6), channel_id=1, source_target_pairs={{0,1},{1,0},{2,3},{3,2},{4,5},{5,4},{6,7},{7,6},{8,9},{9,8},{10,11... | collective-permute-start | bytes 786440 | tf_op jit(solution)/shard_map/ppermute | solution.py:18
  39.3 5.6 %collective-permute-start.6 = (f32[32,1024]{1,0:T(8,128)S(1)}, f32[32,1024]{1,0:T(8,128)S(1)}, u32[]{:S(2)}, u32[]{:S(2)}) collective-permute-start(f32[32,1024]{1,0:T(8,128)S(1)} %get-tuple-element.28), channel_id=1, source_target_pairs={{0,2},{1,3},{2,0},{3,1},{4,6},{5,7},{6,4},{7,5},{8,10},{9,11},{10,... | collective-permute-start | bytes 393224 | tf_op jit(solution)/shard_map/ppermute | solution.py:18
  44.9 1.6 %collective-permute-start.7 = (f32[32,2048]{1,0:T(8,128)S(1)}, f32[32,2048]{1,0:T(8,128)S(1)}, u32[]{:S(2)}, u32[]{:S(2)}) collective-permute-start(f32[32,2048]{1,0:T(8,128)S(1)} %pad_maximum_fusion.7), channel_id=1, source_target_pairs={{0,1},{1,0},{2,3},{3,2},{4,5},{5,4},{6,7},{7,6},{8,9},{9,8},{10,11... | collective-permute-start | bytes 786440 | tf_op jit(solution)/shard_map/ppermute | solution.py:18
  49.5 5.6 %collective-permute-start.8 = (f32[32,1024]{1,0:T(8,128)S(1)}, f32[32,1024]{1,0:T(8,128)S(1)}, u32[]{:S(2)}, u32[]{:S(2)}) collective-permute-start(f32[32,1024]{1,0:T(8,128)S(1)} %get-tuple-element.19), channel_id=1, source_target_pairs={{0,2},{1,3},{2,0},{3,1},{4,6},{5,7},{6,4},{7,5},{8,10},{9,11},{10,... | collective-permute-start | bytes 393224 | tf_op jit(solution)/shard_map/ppermute | solution.py:18
  55.2 1.6 %collective-permute-start.9 = (f32[32,2048]{1,0:T(8,128)S(1)}, f32[32,2048]{1,0:T(8,128)S(1)}, u32[]{:S(2)}, u32[]{:S(2)}) collective-permute-start(f32[32,2048]{1,0:T(8,128)S(1)} %pad_maximum_fusion.8), channel_id=1, source_target_pairs={{0,1},{1,0},{2,3},{3,2},{4,5},{5,4},{6,7},{7,6},{8,9},{9,8},{10,11... | collective-permute-start | bytes 786440 | tf_op jit(solution)/shard_map/ppermute | solution.py:18
  59.9 3.6 %collective-permute-start.10 = (f32[32]{0:T(128)S(1)}, f32[32]{0:T(128)S(1)}, u32[]{:S(2)}, u32[]{:S(2)}) collective-permute-start(f32[32]{0:T(128)S(1)} %get-tuple-element.16), channel_id=1, source_target_pairs={{0,2},{1,3},{2,0},{3,1},{4,6},{5,7},{6,4},{7,5},{8,10},{9,11},{10,... | collective-permute-start | bytes 392 | tf_op jit(solution)/shard_map/ppermute | solution.py:18
  63.5 1.1 %collective-permute-start.11 = (f32[32]{0:T(128)S(1)}, f32[32]{0:T(128)S(1)}, u32[]{:S(2)}, u32[]{:S(2)}) collective-permute-start(f32[32]{0:T(128)S(1)} %add.185), channel_id=1, source_target_pairs={{0,1},{1,0},{2,3},{3,2},{4,5},{5,4},{6,7},{7,6},{8,9},{9,8},{10,11... | collective-permute-start | bytes 392 | tf_op jit(solution)/shard_map/ppermute | solution.py:18

commit v8 on v7

--- a/solution.py
+++ b/solution.py
@@ -11,6 +11,7 @@
 TILE_BYTES = 16 << 20
 VMEM_BYTES = 16 << 20
 NORM_ROWS = 64
+BUILD_ROWS = 256
 POINT_SCALE = math.sqrt(math.log2(math.e))
 
 
@@ -57,37 +58,32 @@
 
 
 def build_kernel(rows_ref, mine_ref, scale_ref, high_ref, low_ref, right_ref):
-    @pl.when(pl.program_id(0) == 0)
-    def _():
-        right_ref[...] = operands(mine_ref[...] * scale_ref[...])[1]
+    right_ref[...] = operands(mine_ref[...] * scale_ref[...])[1]
+    total, cols = high_ref.shape
+    block, step = min(total, BUILD_ROWS), min(cols, 256)
 
-    left = jnp.transpose(operands(rows_ref[...] * scale_ref[...])[0])
-    cols = right_ref.shape[1]
-    step = min(cols, 256)
-    for at in range(0, cols, step):
-        here = pl.ds(at, step)
-        power = jnp.dot(left, right_ref[:, here], preferred_element_type=jnp.float32)
-        high, rest = halve(jnp.exp2(power))
-        high_ref[:, here] = high
-        low_ref[:, here] = rest.astype(jnp.bfloat16)
+    @pl.loop(0, total // block)
+    def _(i):
+        down = pl.ds(pl.multiple_of(i * block, block), block)
+        left = jnp.transpose(operands(rows_ref[:, down] * scale_ref[...])[0])
+        for at in range(0, cols, step):
+            here = pl.ds(at, step)
+            power = jnp.dot(left, right_ref[:, here], preferred_element_type=jnp.float32)
+            high, rest = halve(jnp.exp2(power))
+            high_ref[down, here] = high
+            low_ref[down, here] = rest.astype(jnp.bfloat16)
 
 
 def build_piece(rows, mine, scale):
     feats, total = rows.shape
     cols = mine.shape[1]
-    block = min(total, 512)
     out = jax.ShapeDtypeStruct((total, cols), jnp.bfloat16)
-    spec = pl.BlockSpec((block, cols), lambda i: (i, 0))
+    whole = pl.BlockSpec(memory_space=pltpu.VMEM)
     return pl.pallas_call(
         build_kernel,
-        grid=(total // block,),
         out_shape=(out, out),
-        in_specs=[
-            pl.BlockSpec((feats, block), lambda i: (0, i)),
-            pl.BlockSpec((feats, cols), lambda i: (0, 0)),
-            pl.BlockSpec((feats, 1), lambda i: (0, 0)),
-        ],
-        out_specs=(spec, spec),
+        in_specs=[whole] * 3,
+        out_specs=(whole, whole),
         scratch_shapes=[pltpu.VMEM((6 * feats + NORM_ROWS, cols), jnp.bfloat16)],
         compiler_params=pltpu.CompilerParams(vmem_limit_bytes=VMEM_BYTES),
         cost_estimate=pl.CostEstimate(
@@ -130,8 +126,10 @@
         tile = [build_piece(x[:feats], mine[:feats], scale) for x in first]
 
         def operator(pieces):
-            terms = [apply_piece(x, piece) for x, piece in zip(pieces, tile)]
-            high, low = (sum(t[1:], t[0]) for t in zip(*terms))
+            high, low = apply_piece(pieces[0], tile[0])
+            for x, piece in zip(pieces[1:], tile[1:]):
+                terms = apply_piece(x, piece)
+                high, low = lax.optimization_barrier((high + terms[0], low + terms[1]))
             corrections = (high[probes : 2 * probes] + low[:probes]) + (high[2 * probes :] + low[probes:])
             return high[:probes] + corrections + noise * pieces[0]
 

time: 65.6 us -> 66 us (level)
  Pallas kernels: 6.24 us -> 8.1 us
  waiting for transfers between devices: 24.5 us -> 23 us
    pallas_call x3, Pallas kernels: 6.24 us -> 8.1 us  [build_piece(): pl.pallas_call(build_kernel, out_shape=(out, out), in_specs=[whole] * 3,...]
    ppermute x12, waiting for transfers between devices: 24.5 us -> 23 us  [swap(): return lax.ppermute(x, 'blk', [(i, i ^ stride) for i in range(n)])]
  transfers between devices with their start and end apart: 12 -> 12, of which waited for: 11 -> 12; matrix products, arithmetic and copies ran while one was open for 10% -> 13% of each run, Pallas kernels for 5% -> 3%
where the time goes in v8:
time: 66 us; the launch traced here: 65.7 us
  waiting for transfers between devices  23 us (35%)
  matrix products  14.5 us (22%)
  starting transfers between devices  14 us (21%)
  Pallas kernels  8.1 us (12%)
  other arithmetic  5.03 us (8%)
  between operations  0.96 us (1%)
    ppermute x12, waiting for transfers between devices, swap(): return lax.ppermute(x, 'blk', [(i, i ^ stride) for i in range(n)])  23 us
    ppermute x12, starting transfers between devices, swap(): return lax.ppermute(x, 'blk', [(i, i ^ stride) for i in range(n)])  14 us
    pallas_call x3, Pallas kernels, build_piece(): pl.pallas_call(build_kernel, out_shape=(out, out), in_specs=[whole] * 3,...  8.1 us
    dot_general x12, matrix products, apply_piece(): jnp.dot(jnp.concatenate(parts[:2], axis=0), piece[1], preferred_element_t...  7.32 us
    dot_general x12, matrix products, apply_piece(): jnp.dot(jnp.concatenate(parts, axis=0), piece[0], preferred_element_type=...  7.2 us
  transfers between devices with their start and end apart: 12, of which 12 were waited for; matrix products, arithmetic and copies ran while one was open for 13% of the time, Pallas kernels for 3%

profile of v8, /device:TPU:0, one launch (start us, length us, event | category | flops | bytes accessed | tf_op | source)
XLA Modules:
  0.0 65.7 jit_solution(2233293767713465413)
XLA Ops:
  0.6 0.8 %pad_maximum_fusion.10 = f32[65,256]{1,0:T(8,128)S(1)} fusion(f32[1,256]{1,0:T(1,128)} %bitcast.32, f32[32,256]{1,0:T(8,128)} %param.7, f32[32,256]{1,0:T(8,128)} %param.4), kind=kLoop, calls=%fused_computation.223 | loop fusion | flops 33280 | bytes 133120 | tf_op jit(solution)/shard_map/concatenate | solution.py:120
  1.4 4.0 %collective-permute-start = (f32[65,256]{1,0:T(8,128)S(1)}, f32[65,256]{1,0:T(8,128)S(1)}, u32[]{:S(2)}, u32[]{:S(2)}) collective-permute-start(f32[65,256]{1,0:T(8,128)S(1)} %pad_maximum_fusion.10), channel_id=1, source_target_pairs={{0,8},{1,9},{2,10},{3,11},{4,12},{5,13},{6,14},{7,15},{8,0},{9,1},... | collective-permute-start | bytes 199688 | tf_op jit(solution)/shard_map/ppermute | solution.py:19
  5.5 3.9 %collective-permute-done = f32[65,256]{1,0:T(8,128)S(1)} collective-permute-done((f32[65,256]{1,0:T(8,128)S(1)}, f32[65,256]{1,0:T(8,128)S(1)}, u32[]{:S(2)}, u32[]{:S(2)}) %collective-permute-start) | collective-permute-done | bytes 66592 | tf_op jit(solution)/shard_map/ppermute | solution.py:19
  9.4 0.7 %collective-permute-start.1 = (f32[65,512]{1,0:T(8,128)S(1)}, f32[65,512]{1,0:T(8,128)S(1)}, u32[]{:S(2)}, u32[]{:S(2)}) collective-permute-start(f32[65,512]{1,0:T(8,128)S(1)} %pad_maximum_fusion.9), channel_id=1, source_target_pairs={{0,4},{1,5},{2,6},{3,7},{4,0},{5,1},{6,2},{7,3},{8,12},{9,13},{10,... | collective-permute-start | bytes 399368 | tf_op jit(solution)/shard_map/ppermute | solution.py:19
  10.1 0.7 %divide_bitcast_fusion = f32[32,1]{0,1:T(1,128)S(1)} fusion(f32[32]{0:T(128)} %param.5), kind=kLoop, calls=%fused_computation.235 | loop fusion | flops 32 | bytes 256 | tf_op jit(solution)/shard_map/broadcast_in_dim | solution.py:124
  10.9 3.7 %collective-permute-done.1 = f32[65,512]{1,0:T(8,128)S(1)} collective-permute-done((f32[65,512]{1,0:T(8,128)S(1)}, f32[65,512]{1,0:T(8,128)S(1)}, u32[]{:S(2)}, u32[]{:S(2)}) %collective-permute-start.1) | collective-permute-done | bytes 133152 | tf_op jit(solution)/shard_map/ppermute | solution.py:19
  14.7 1.8 %collective-permute-start.2 = (f32[64,1024]{1,0:T(8,128)S(1)}, f32[64,1024]{1,0:T(8,128)S(1)}, u32[]{:S(2)}, u32[]{:S(2)}) collective-permute-start(f32[64,1024]{1,0:T(8,128)S(1)} %slice.148), channel_id=1, source_target_pairs={{0,2},{1,3},{2,0},{3,1},{4,6},{5,7},{6,4},{7,5},{8,10},{9,11},{10,... | collective-permute-start | bytes 786440 | tf_op jit(solution)/shard_map/ppermute | solution.py:19
  16.5 2.0 %shard_map.59 = (bf16[1024,1024]{1,0:T(8,128)(2,1)S(1)}, bf16[1024,1024]{1,0:T(8,128)(2,1)S(1)}) custom-call(f32[32,1024]{1,0:T(8,128)S(1)} %get-tuple-element.75.rows_ref.mine_ref, f32[32,1024]{1,0:T(8,128)S(1)} %get-tuple-element.75.rows_ref.mine_ref, f32[32,1]{1,0:T(8,128)S(1)} %copy.6.scale_ref), custom_call_target="tpu_custom_call" | custom-call | flops 536870912 | bytes 4325376 | tf_op jit(solution)/shard_map/pallas_call | solution.py:82
  19.5 1.6 %collective-permute-done.2 = f32[64,1024]{1,0:T(8,128)S(1)} collective-permute-done((f32[64,1024]{1,0:T(8,128)S(1)}, f32[64,1024]{1,0:T(8,128)S(1)}, u32[]{:S(2)}, u32[]{:S(2)}) %collective-permute-start.2) | collective-permute-done | bytes 262176 | tf_op jit(solution)/shard_map/ppermute | solution.py:19
  21.2 2.0 %shard_map.60 = (bf16[1024,1024]{1,0:T(8,128)(2,1)S(1)}, bf16[1024,1024]{1,0:T(8,128)(2,1)S(1)}) custom-call(f32[32,1024]{1,0:T(8,128)S(1)} %get-tuple-element.89.rows_ref, f32[32,1024]{1,0:T(8,128)S(1)} %get-tuple-element.75.rows_ref.mine_ref, f32[32,1]{1,0:T(8,128)S(1)} %copy.6.scale_ref), custom_call_target="tpu_custom_call" | custom-call | flops 536870912 | bytes 4325376 | tf_op jit(solution)/shard_map/pallas_call | solution.py:82
  24.3 0.9 %collective-permute-done.3 = f32[64,2048]{1,0:T(8,128)S(1)} collective-permute-done((f32[64,2048]{1,0:T(8,128)S(1)}, f32[64,2048]{1,0:T(8,128)S(1)}, u32[]{:S(2)}, u32[]{:S(2)}) %collective-permute-start.3) | collective-permute-done | bytes 524320 | tf_op jit(solution)/shard_map/ppermute | solution.py:19
  25.3 4.1 %shard_map.61 = (bf16[2048,1024]{1,0:T(8,128)(2,1)S(1)}, bf16[2048,1024]{1,0:T(8,128)(2,1)S(1)}) custom-call(f32[32,2048]{1,0:T(8,128)S(1)} %get-tuple-element.70.rows_ref, f32[32,1024]{1,0:T(8,128)S(1)} %get-tuple-element.75.rows_ref.mine_ref, f32[32,1]{1,0:T(8,128)S(1)} %copy.6.scale_ref), custom_call_target="tpu_custom_call" | custom-call | flops 1073741824 | bytes 8650752 | tf_op jit(solution)/shard_map/pallas_call | solution.py:82
  29.4 0.8 %convolution_add_fusion.14 = f32[64,1024]{1,0:T(8,128)S(1)} fusion(f32[64,1024]{1,0:T(8,128)S(1)} %convolution_add_fusion.15, bf16[2048,1024]{1,0:T(8,128)(2,1)S(1)} %get-tuple-element.31, bf16[32,2048]{1,0:T(8,128)(2,1)S(1)} %get-tuple-element.68, bf16[32,2048]{1,0:T(8,128)(2,1)S(1)} %get-tuple-element.67), kind=kOutput, calls=%fused_computation.14 | convolution fusion | flops 269025280 | bytes 4980736 | tf_op jit(solution)/shard_map/dot_general | solution.py:98
  30.2 0.8 %convolution_add_fusion.7 = f32[96,1024]{1,0:T(8,128)S(1)} fusion(f32[96,1024]{1,0:T(8,128)S(1)} %convolution_add_fusion.3, bf16[2048,1024]{1,0:T(8,128)(2,1)S(1)} %get-tuple-element.29, bf16[32,2048]{1,0:T(8,128)(2,1)S(1)} %get-tuple-element.69, bf16[32,2048]{1,0:T(8,128)(2,1)S(1)} %get-tuple-element.68, bf16[32,2048]{1,0:T(8,128)(2,1)S(1)} %get-tuple-element.67), kind=kOutput, calls=%fused_computation.7 | convolution fusion | flops 403931136 | bytes 5373952 | tf_op jit(solution)/shard_map/dot_general | solution.py:97
  31.1 1.8 %collective-permute-start.4 = (f32[32,1024]{1,0:T(8,128)S(1)}, f32[32,1024]{1,0:T(8,128)S(1)}, u32[]{:S(2)}, u32[]{:S(2)}) collective-permute-start(f32[32,1024]{1,0:T(8,128)S(1)} %get-tuple-element.65), channel_id=1, source_target_pairs={{0,2},{1,3},{2,0},{3,1},{4,6},{5,7},{6,4},{7,5},{8,10},{9,11},{10,... | collective-permute-start | bytes 393224 | tf_op jit(solution)/shard_map/ppermute | solution.py:19
  33.9 2.8 %collective-permute-done.4 = f32[32,1024]{1,0:T(8,128)S(1)} collective-permute-done((f32[32,1024]{1,0:T(8,128)S(1)}, f32[32,1024]{1,0:T(8,128)S(1)}, u32[]{:S(2)}, u32[]{:S(2)}) %collective-permute-start.4) | collective-permute-done | bytes 131104 | tf_op jit(solution)/shard_map/ppermute | solution.py:19
  37.9 0.5 collective-permute-done.5
  38.9 0.9 %convolution_add_fusion.12 = f32[64,1024]{1,0:T(8,128)S(1)} fusion(f32[64,1024]{1,0:T(8,128)S(1)} %convolution_add_fusion.13, bf16[2048,1024]{1,0:T(8,128)(2,1)S(1)} %get-tuple-element.31, bf16[32,2048]{1,0:T(8,128)(2,1)S(1)} %get-tuple-element.84, bf16[32,2048]{1,0:T(8,128)(2,1)S(1)} %get-tuple-element.82), kind=kOutput, calls=%fused_computation.12 | convolution fusion | flops 269025280 | bytes 4980736 | tf_op jit(solution)/shard_map/dot_general | solution.py:98
  39.8 0.8 %convolution_add_fusion.6 = f32[96,1024]{1,0:T(8,128)S(1)} fusion(f32[96,1024]{1,0:T(8,128)S(1)} %convolution_add_fusion.2, bf16[2048,1024]{1,0:T(8,128)(2,1)S(1)} %get-tuple-element.29, bf16[32,2048]{1,0:T(8,128)(2,1)S(1)} %get-tuple-element.83, bf16[32,2048]{1,0:T(8,128)(2,1)S(1)} %get-tuple-element.84, bf16[32,2048]{1,0:T(8,128)(2,1)S(1)} %get-tuple-element.82), kind=kOutput, calls=%fused_computation.6 | convolution fusion | flops 403931136 | bytes 5373952 | tf_op jit(solution)/shard_map/dot_general | solution.py:97
  40.7 1.8 %collective-permute-start.6 = (f32[32,1024]{1,0:T(8,128)S(1)}, f32[32,1024]{1,0:T(8,128)S(1)}, u32[]{:S(2)}, u32[]{:S(2)}) collective-permute-start(f32[32,1024]{1,0:T(8,128)S(1)} %get-tuple-element.60), channel_id=1, source_target_pairs={{0,2},{1,3},{2,0},{3,1},{4,6},{5,7},{6,4},{7,5},{8,10},{9,11},{10,... | collective-permute-start | bytes 393224 | tf_op jit(solution)/shard_map/ppermute | solution.py:19
  43.5 2.8 %collective-permute-done.6 = f32[32,1024]{1,0:T(8,128)S(1)} collective-permute-done((f32[32,1024]{1,0:T(8,128)S(1)}, f32[32,1024]{1,0:T(8,128)S(1)}, u32[]{:S(2)}, u32[]{:S(2)}) %collective-permute-start.6) | collective-permute-done | bytes 131104 | tf_op jit(solution)/shard_map/ppermute | solution.py:19
  48.6 0.8 %convolution_add_fusion.10 = f32[64,1024]{1,0:T(8,128)S(1)} fusion(f32[64,1024]{1,0:T(8,128)S(1)} %convolution_add_fusion.11, bf16[2048,1024]{1,0:T(8,128)(2,1)S(1)} %get-tuple-element.31, bf16[32,2048]{1,0:T(8,128)(2,1)S(1)} %get-tuple-element.81, bf16[32,2048]{1,0:T(8,128)(2,1)S(1)} %get-tuple-element.79), kind=kOutput, calls=%fused_computation.10 | convolution fusion | flops 269025280 | bytes 4980736 | tf_op jit(solution)/shard_map/dot_general | solution.py:98
  49.5 0.8 %convolution_add_fusion.5 = f32[96,1024]{1,0:T(8,128)S(1)} fusion(f32[96,1024]{1,0:T(8,128)S(1)} %convolution_add_fusion.1, bf16[2048,1024]{1,0:T(8,128)(2,1)S(1)} %get-tuple-element.29, bf16[32,2048]{1,0:T(8,128)(2,1)S(1)} %get-tuple-element.80, bf16[32,2048]{1,0:T(8,128)(2,1)S(1)} %get-tuple-element.81, bf16[32,2048]{1,0:T(8,128)(2,1)S(1)} %get-tuple-element.79), kind=kOutput, calls=%fused_computation.5 | convolution fusion | flops 403931136 | bytes 5373952 | tf_op jit(solution)/shard_map/dot_general | solution.py:97
  50.4 1.8 %collective-permute-start.8 = (f32[32,1024]{1,0:T(8,128)S(1)}, f32[32,1024]{1,0:T(8,128)S(1)}, u32[]{:S(2)}, u32[]{:S(2)}) collective-permute-start(f32[32,1024]{1,0:T(8,128)S(1)} %get-tuple-element.51), channel_id=1, source_target_pairs={{0,2},{1,3},{2,0},{3,1},{4,6},{5,7},{6,4},{7,5},{8,10},{9,11},{10,... | collective-permute-start | bytes 393224 | tf_op jit(solution)/shard_map/ppermute | solution.py:19
  53.2 2.8 %collective-permute-done.8 = f32[32,1024]{1,0:T(8,128)S(1)} collective-permute-done((f32[32,1024]{1,0:T(8,128)S(1)}, f32[32,1024]{1,0:T(8,128)S(1)}, u32[]{:S(2)}, u32[]{:S(2)}) %collective-permute-start.8) | collective-permute-done | bytes 131104 | tf_op jit(solution)/shard_map/ppermute | solution.py:19
  56.1 0.5 convolution_add_fusion
  58.2 0.9 %convolution_add_fusion.8 = f32[64,1024]{1,0:T(8,128)S(1)} fusion(f32[64,1024]{1,0:T(8,128)S(1)} %convolution_add_fusion.9, bf16[2048,1024]{1,0:T(8,128)(2,1)S(1)} %get-tuple-element.31, bf16[32,2048]{1,0:T(8,128)(2,1)S(1)} %get-tuple-element.78, bf16[32,2048]{1,0:T(8,128)(2,1)S(1)} %get-tuple-element.76), kind=kOutput, calls=%fused_computation.8 | convolution fusion | flops 269025280 | bytes 4980736 | tf_op jit(solution)/shard_map/dot_general | solution.py:98
  59.1 0.8 %convolution_add_fusion.4 = f32[96,1024]{1,0:T(8,128)S(1)} fusion(f32[96,1024]{1,0:T(8,128)S(1)} %convolution_add_fusion, bf16[2048,1024]{1,0:T(8,128)(2,1)S(1)} %get-tuple-element.29, bf16[32,2048]{1,0:T(8,128)(2,1)S(1)} %get-tuple-element.77, bf16[32,2048]{1,0:T(8,128)(2,1)S(1)} %get-tuple-element.78, bf16[32,2048]{1,0:T(8,128)(2,1)S(1)} %get-tuple-element.76), kind=kOutput, calls=%fused_computation.4 | convolution fusion | flops 403931136 | bytes 5373952 | tf_op jit(solution)/shard_map/dot_general | solution.py:97
  60.3 1.8 %collective-permute-start.10 = (f32[32]{0:T(128)S(1)}, f32[32]{0:T(128)S(1)}, u32[]{:S(2)}, u32[]{:S(2)}) collective-permute-start(f32[32]{0:T(128)S(1)} %get-tuple-element.48), channel_id=1, source_target_pairs={{0,2},{1,3},{2,0},{3,1},{4,6},{5,7},{6,4},{7,5},{8,10},{9,11},{10,... | collective-permute-start | bytes 392 | tf_op jit(solution)/shard_map/ppermute | solution.py:19
  62.0 1.8 %collective-permute-done.10 = f32[32]{0:T(128)S(1)} collective-permute-done((f32[32]{0:T(128)S(1)}, f32[32]{0:T(128)S(1)}, u32[]{:S(2)}, u32[]{:S(2)}) %collective-permute-start.10) | collective-permute-done | bytes 160 | tf_op jit(solution)/shard_map/ppermute | solution.py:19
  63.9 1.1 %collective-permute-done.11 = f32[32]{0:T(128)S(1)} collective-permute-done((f32[32]{0:T(128)S(1)}, f32[32]{0:T(128)S(1)}, u32[]{:S(2)}, u32[]{:S(2)}) %collective-permute-start.11) | collective-permute-done | bytes 160 | tf_op jit(solution)/shard_map/ppermute | solution.py:19
  65.0 0.7 %fusion.129 = (f32[32,256]{1,0:T(8,128)}, f32[32,256]{1,0:T(8,128)}) fusion(f32[32,1024]{1,0:T(8,128)S(1)} %get-tuple-element.49, f32[32,4096]{1,0:T(8,128)S(1)} %get-tuple-element.54, f32[32]{0:T(128)S(1)} %add_divide_fusion, f32[32,4096]{1,0:T(8,128)S(1)} %multiply_add_fusion, f32[32,4096]{1,0:T(8,128)S(1)} %get-tuple-element.56, f32[32]{0:T(128)S(1)} %div.57, ...), kind=kLoop, calls=%fused_computation.225 | loop fusion | flops 73728 | bytes 262656 | tf_op jit(solution)/shard_map/sub | solution.py:159
  (62 shorter events, 11.5 us)
Async XLA Ops:
  1.4 7.9 %collective-permute-start = (f32[65,256]{1,0:T(8,128)S(1)}, f32[65,256]{1,0:T(8,128)S(1)}, u32[]{:S(2)}, u32[]{:S(2)}) collective-permute-start(f32[65,256]{1,0:T(8,128)S(1)} %pad_maximum_fusion.10), channel_id=1, source_target_pairs={{0,8},{1,9},{2,10},{3,11},{4,12},{5,13},{6,14},{7,15},{8,0},{9,1},... | collective-permute-start | bytes 199688 | tf_op jit(solution)/shard_map/ppermute | solution.py:19
  9.4 5.2 %collective-permute-start.1 = (f32[65,512]{1,0:T(8,128)S(1)}, f32[65,512]{1,0:T(8,128)S(1)}, u32[]{:S(2)}, u32[]{:S(2)}) collective-permute-start(f32[65,512]{1,0:T(8,128)S(1)} %pad_maximum_fusion.9), channel_id=1, source_target_pairs={{0,4},{1,5},{2,6},{3,7},{4,0},{5,1},{6,2},{7,3},{8,12},{9,13},{10,... | collective-permute-start | bytes 399368 | tf_op jit(solution)/shard_map/ppermute | solution.py:19
  14.7 6.4 %collective-permute-start.2 = (f32[64,1024]{1,0:T(8,128)S(1)}, f32[64,1024]{1,0:T(8,128)S(1)}, u32[]{:S(2)}, u32[]{:S(2)}) collective-permute-start(f32[64,1024]{1,0:T(8,128)S(1)} %slice.148), channel_id=1, source_target_pairs={{0,2},{1,3},{2,0},{3,1},{4,6},{5,7},{6,4},{7,5},{8,10},{9,11},{10,... | collective-permute-start | bytes 786440 | tf_op jit(solution)/shard_map/ppermute | solution.py:19
  23.2 2.0 %collective-permute-start.3 = (f32[64,2048]{1,0:T(8,128)S(1)}, f32[64,2048]{1,0:T(8,128)S(1)}, u32[]{:S(2)}, u32[]{:S(2)}) collective-permute-start(f32[64,2048]{1,0:T(8,128)S(1)} %pad_maximum_fusion), channel_id=1, source_target_pairs={{0,1},{1,0},{2,3},{3,2},{4,5},{5,4},{6,7},{7,6},{8,9},{9,8},{10,11... | collective-permute-start | bytes 1572872 | tf_op jit(solution)/shard_map/ppermute | solution.py:19
  31.1 5.6 %collective-permute-start.4 = (f32[32,1024]{1,0:T(8,128)S(1)}, f32[32,1024]{1,0:T(8,128)S(1)}, u32[]{:S(2)}, u32[]{:S(2)}) collective-permute-start(f32[32,1024]{1,0:T(8,128)S(1)} %get-tuple-element.65), channel_id=1, source_target_pairs={{0,2},{1,3},{2,0},{3,1},{4,6},{5,7},{6,4},{7,5},{8,10},{9,11},{10,... | collective-permute-start | bytes 393224 | tf_op jit(solution)/shard_map/ppermute | solution.py:19
  36.8 1.6 %collective-permute-start.5 = (f32[32,2048]{1,0:T(8,128)S(1)}, f32[32,2048]{1,0:T(8,128)S(1)}, u32[]{:S(2)}, u32[]{:S(2)}) collective-permute-start(f32[32,2048]{1,0:T(8,128)S(1)} %pad_maximum_fusion.6), channel_id=1, source_target_pairs={{0,1},{1,0},{2,3},{3,2},{4,5},{5,4},{6,7},{7,6},{8,9},{9,8},{10,11... | collective-permute-start | bytes 786440 | tf_op jit(solution)/shard_map/ppermute | solution.py:19
  40.7 5.6 %collective-permute-start.6 = (f32[32,1024]{1,0:T(8,128)S(1)}, f32[32,1024]{1,0:T(8,128)S(1)}, u32[]{:S(2)}, u32[]{:S(2)}) collective-permute-start(f32[32,1024]{1,0:T(8,128)S(1)} %get-tuple-element.60), channel_id=1, source_target_pairs={{0,2},{1,3},{2,0},{3,1},{4,6},{5,7},{6,4},{7,5},{8,10},{9,11},{10,... | collective-permute-start | bytes 393224 | tf_op jit(solution)/shard_map/ppermute | solution.py:19
  46.3 1.6 %collective-permute-start.7 = (f32[32,2048]{1,0:T(8,128)S(1)}, f32[32,2048]{1,0:T(8,128)S(1)}, u32[]{:S(2)}, u32[]{:S(2)}) collective-permute-start(f32[32,2048]{1,0:T(8,128)S(1)} %pad_maximum_fusion.7), channel_id=1, source_target_pairs={{0,1},{1,0},{2,3},{3,2},{4,5},{5,4},{6,7},{7,6},{8,9},{9,8},{10,11... | collective-permute-start | bytes 786440 | tf_op jit(solution)/shard_map/ppermute | solution.py:19
  50.4 5.6 %collective-permute-start.8 = (f32[32,1024]{1,0:T(8,128)S(1)}, f32[32,1024]{1,0:T(8,128)S(1)}, u32[]{:S(2)}, u32[]{:S(2)}) collective-permute-start(f32[32,1024]{1,0:T(8,128)S(1)} %get-tuple-element.51), channel_id=1, source_target_pairs={{0,2},{1,3},{2,0},{3,1},{4,6},{5,7},{6,4},{7,5},{8,10},{9,11},{10,... | collective-permute-start | bytes 393224 | tf_op jit(solution)/shard_map/ppermute | solution.py:19
  56.0 1.6 %collective-permute-start.9 = (f32[32,2048]{1,0:T(8,128)S(1)}, f32[32,2048]{1,0:T(8,128)S(1)}, u32[]{:S(2)}, u32[]{:S(2)}) collective-permute-start(f32[32,2048]{1,0:T(8,128)S(1)} %pad_maximum_fusion.8), channel_id=1, source_target_pairs={{0,1},{1,0},{2,3},{3,2},{4,5},{5,4},{6,7},{7,6},{8,9},{9,8},{10,11... | collective-permute-start | bytes 786440 | tf_op jit(solution)/shard_map/ppermute | solution.py:19
  60.3 3.6 %collective-permute-start.10 = (f32[32]{0:T(128)S(1)}, f32[32]{0:T(128)S(1)}, u32[]{:S(2)}, u32[]{:S(2)}) collective-permute-start(f32[32]{0:T(128)S(1)} %get-tuple-element.48), channel_id=1, source_target_pairs={{0,2},{1,3},{2,0},{3,1},{4,6},{5,7},{6,4},{7,5},{8,10},{9,11},{10,... | collective-permute-start | bytes 392 | tf_op jit(solution)/shard_map/ppermute | solution.py:19
  63.9 1.1 %collective-permute-start.11 = (f32[32]{0:T(128)S(1)}, f32[32]{0:T(128)S(1)}, u32[]{:S(2)}, u32[]{:S(2)}) collective-permute-start(f32[32]{0:T(128)S(1)} %add.185), channel_id=1, source_target_pairs={{0,1},{1,0},{2,3},{3,2},{4,5},{5,4},{6,7},{7,6},{8,9},{9,8},{10,11... | collective-permute-start | bytes 392 | tf_op jit(solution)/shard_map/ppermute | solution.py:19

commit v9 on v8

--- a/solution.py
+++ b/solution.py
@@ -11,7 +11,7 @@
 TILE_BYTES = 16 << 20
 VMEM_BYTES = 16 << 20
 NORM_ROWS = 64
-BUILD_ROWS = 256
+BUILD_ROWS = 1024
 POINT_SCALE = math.sqrt(math.log2(math.e))
 
 
@@ -57,46 +57,61 @@
     return left, right
 
 
-def build_kernel(rows_ref, mine_ref, scale_ref, high_ref, low_ref, right_ref):
+def scaled_operand_kernel(mine_ref, scale_ref, right_ref):
     right_ref[...] = operands(mine_ref[...] * scale_ref[...])[1]
-    total, cols = high_ref.shape
+
+
+def build_kernel(rows_ref, vectors_ref, scale_ref, right_ref, sum_ref, tile_ref, out_ref):
+    total, cols = rows_ref.shape[1], right_ref.shape[1]
+    probes = vectors_ref.shape[0]
     block, step = min(total, BUILD_ROWS), min(cols, 256)
-
-    @pl.loop(0, total // block)
-    def _(i):
-        down = pl.ds(pl.multiple_of(i * block, block), block)
+    high, rest = halve(vectors_ref[...])
+    mid, rest = halve(rest)
+    twice = jnp.concatenate([high, mid], axis=0)
+    thrice = jnp.concatenate([high, mid, rest.astype(jnp.bfloat16)], axis=0)
+    for top in range(0, total, block):
+        down = slice(top, top + block)
         left = jnp.transpose(operands(rows_ref[:, down] * scale_ref[...])[0])
         for at in range(0, cols, step):
-            here = pl.ds(at, step)
+            here = slice(at, at + step)
             power = jnp.dot(left, right_ref[:, here], preferred_element_type=jnp.float32)
             high, rest = halve(jnp.exp2(power))
-            high_ref[down, here] = high
-            low_ref[down, here] = rest.astype(jnp.bfloat16)
+            low = rest.astype(jnp.bfloat16)
+            tile_ref[down, here] = high
+            tile_ref[total + top : total + top + block, here] = low
+            large = jnp.dot(thrice[:, down], high, preferred_element_type=jnp.float32)
+            small = jnp.dot(twice[:, down], low, preferred_element_type=jnp.float32)
+            term = large[:probes] + (
+                (large[probes : 2 * probes] + small[:probes]) + (large[2 * probes :] + small[probes:])
+            )
+            before = sum_ref if top == 0 else out_ref
+            out_ref[:, here] = before[:, here] + term
 
 
-def build_piece(rows, mine, scale):
-    feats, total = rows.shape
-    cols = mine.shape[1]
-    out = jax.ShapeDtypeStruct((total, cols), jnp.bfloat16)
+def call(kernel, outs, *args, **cost):
     whole = pl.BlockSpec(memory_space=pltpu.VMEM)
     return pl.pallas_call(
-        build_kernel,
-        out_shape=(out, out),
-        in_specs=[whole] * 3,
-        out_specs=(whole, whole),
-        scratch_shapes=[pltpu.VMEM((6 * feats + NORM_ROWS, cols), jnp.bfloat16)],
+        kernel,
+        out_shape=outs,
+        in_specs=[whole] * len(args),
+        out_specs=jax.tree.map(lambda _: whole, outs),
         compiler_params=pltpu.CompilerParams(vmem_limit_bytes=VMEM_BYTES),
-        cost_estimate=pl.CostEstimate(
-            flops=2 * total * cols * 256, bytes_accessed=4 * total * (cols + feats), transcendentals=total * cols
-        ),
-    )(rows, mine, scale)
+        cost_estimate=pl.CostEstimate(**cost),
+    )(*args)
+
+
+def build_piece(rows, vectors, scale, right, total):
+    count, cols = rows.shape[1], right.shape[1]
+    outs = (jax.ShapeDtypeStruct((2 * count, cols), jnp.bfloat16), jax.ShapeDtypeStruct(total.shape, jnp.float32))
+    cost = dict(flops=2 * count * cols * 416, bytes_accessed=4 * count * cols, transcendentals=count * cols)
+    return call(build_kernel, outs, rows, vectors, scale, right, total, **cost)
 
 
 def apply_piece(vectors, piece):
-    parts = split(vectors, 3)
-    high = jnp.dot(jnp.concatenate(parts, axis=0), piece[0], preferred_element_type=jnp.float32)
-    low = jnp.dot(jnp.concatenate(parts[:2], axis=0), piece[1], preferred_element_type=jnp.float32)
-    return high, low
+    high, mid, low = split(vectors, 3)
+    left = jnp.concatenate([high, mid, low], axis=0)
+    right = jnp.concatenate([high, mid, jnp.zeros_like(low)], axis=0)
+    return jnp.dot(jnp.concatenate([left, right], axis=1), piece, preferred_element_type=jnp.float32)
 
 
 def solution(mesh):
@@ -112,9 +127,11 @@
         outer, inner = [s for s in strides if s >= team], [s for s in strides if s < team]
 
         def arrivals(x):
-            pieces = [x]
-            for stride in inner:
-                pieces.append(swap(jnp.concatenate(pieces, axis=1), n, stride))
+            pieces, sent = [x, swap(x, n, 1)], [x]
+            for stride in inner[:-1]:
+                came = swap(sent[0] if len(sent) == 1 else jnp.concatenate(sent, axis=1), n, stride)
+                sent.append(came)
+                pieces += [came, swap(came, n, 1)]
             return pieces
 
         mine = lax.optimization_barrier(jnp.concatenate([points, targets, noise_var[None, :]], axis=0))
@@ -123,22 +140,33 @@
         noise = mine[-1:]
         scale = (POINT_SCALE / lengthscale)[:, None]
         first = arrivals(mine[:-1])
-        tile = [build_piece(x[:feats], mine[:feats], scale) for x in first]
+        cols = noise.shape[1]
+        right = call(
+            scaled_operand_kernel,
+            jax.ShapeDtypeStruct((6 * feats + NORM_ROWS, cols), jnp.bfloat16),
+            mine[:feats],
+            scale,
+            flops=feats * cols,
+            bytes_accessed=feats * cols,
+            transcendentals=0,
+        )
+        starts = [x[feats:] for x in first]
+        tile = []
+        my_applied = noise * starts[0]
+        for x, start in zip(first, starts):
+            piece, my_applied = build_piece(x[:feats], start, scale, right, my_applied)
+            tile.append(piece)
 
         def operator(pieces):
-            high, low = apply_piece(pieces[0], tile[0])
+            total = apply_piece(pieces[0], tile[0])
             for x, piece in zip(pieces[1:], tile[1:]):
-                terms = apply_piece(x, piece)
-                high, low = lax.optimization_barrier((high + terms[0], low + terms[1]))
-            corrections = (high[probes : 2 * probes] + low[:probes]) + (high[2 * probes :] + low[probes:])
-            return high[:probes] + corrections + noise * pieces[0]
+                total = lax.optimization_barrier(total + apply_piece(x, piece))
+            return total[:probes] + (total[probes : 2 * probes] + total[2 * probes :]) + noise * pieces[0]
 
-        starts = [x[feats:] for x in first]
         residual = direction = jnp.concatenate(starts, axis=1)
-        cols = noise.shape[1]
         my_solution = jnp.zeros_like(direction[:, :width])
         norm_now = jnp.sum(residual * residual, axis=1)
-        my_applied = my_image = operator(starts)
+        my_image = my_applied
         for iteration in range(ITERS - 1):
             pieces = arrivals(my_applied)
             my_next = operator(pieces)

time: 66 us -> 56.5 us (0.86)
  matrix products: 14.5 us -> 9.83 us
  waiting for transfers between devices: 23 us -> 19.7 us
  Pallas kernels: 8.1 us -> 6.97 us
    dot_general x24 -> x12, matrix products: 14.5 us -> 9.83 us  [apply_piece(): jnp.dot(jnp.concatenate([left, right], axis=1), piece, preferred_element_...]
    ppermute x12 -> x16, waiting for transfers between devices: 23 us -> 19.7 us  [swap(): return lax.ppermute(x, 'blk', [(i, i ^ stride) for i in range(n)])]
    pallas_call x3 -> x5, Pallas kernels: 8.1 us -> 6.97 us  [call(): pl.pallas_call(kernel, out_shape=outs, in_specs=[whole] * len(args), out_...]
    ppermute x12 -> x16, starting transfers between devices: 14 us -> 13.9 us  [swap(): return lax.ppermute(x, 'blk', [(i, i ^ stride) for i in range(n)])]
  transfers between devices with their start and end apart: 12 -> 16, of which waited for: 12 -> 14; matrix products, arithmetic and copies ran while one was open for 13% -> 15% of each run, Pallas kernels for 3% -> 9%
where the time goes in v9:
time: 56.5 us; the launch traced here: 56.2 us
  waiting for transfers between devices  19.7 us (35%)
  starting transfers between devices  13.9 us (25%)
  matrix products  9.83 us (17%)
  Pallas kernels  6.97 us (12%)
  other arithmetic  4.77 us (8%)
  between operations  0.83 us (1%)
    ppermute x16, waiting for transfers between devices, swap(): return lax.ppermute(x, 'blk', [(i, i ^ stride) for i in range(n)])  19.7 us
    ppermute x16, starting transfers between devices, swap(): return lax.ppermute(x, 'blk', [(i, i ^ stride) for i in range(n)])  13.9 us
    dot_general x12, matrix products, apply_piece(): jnp.dot(jnp.concatenate([left, right], axis=1), piece, preferred_element_...  9.83 us
    pallas_call x5, Pallas kernels, call(): pl.pallas_call(kernel, out_shape=outs, in_specs=[whole] * len(args), out_...  6.97 us
  transfers between devices with their start and end apart: 16, of which 14 were waited for; matrix products, arithmetic and copies ran while one was open for 15% of the time, Pallas kernels for 9%

profile of v9, /device:TPU:0, one launch (start us, length us, event | category | flops | bytes accessed | tf_op | source)
XLA Modules:
  0.0 56.2 jit_solution(15573724985692603837)
XLA Ops:
  0.6 0.8 %pad_maximum_fusion.17 = f32[65,256]{1,0:T(8,128)S(1)} fusion(f32[1,256]{1,0:T(1,128)} %bitcast.20, f32[32,256]{1,0:T(8,128)} %param.7, f32[32,256]{1,0:T(8,128)} %param.4), kind=kLoop, calls=%fused_computation.242 | loop fusion | flops 33280 | bytes 133120 | tf_op jit(solution)/shard_map/concatenate | solution.py:137
  1.4 4.0 %collective-permute-start = (f32[65,256]{1,0:T(8,128)S(1)}, f32[65,256]{1,0:T(8,128)S(1)}, u32[]{:S(2)}, u32[]{:S(2)}) collective-permute-start(f32[65,256]{1,0:T(8,128)S(1)} %pad_maximum_fusion.17), channel_id=1, source_target_pairs={{0,8},{1,9},{2,10},{3,11},{4,12},{5,13},{6,14},{7,15},{8,0},{9,1},... | collective-permute-start | bytes 199688 | tf_op jit(solution)/shard_map/ppermute | solution.py:19
  5.5 3.9 %collective-permute-done = f32[65,256]{1,0:T(8,128)S(1)} collective-permute-done((f32[65,256]{1,0:T(8,128)S(1)}, f32[65,256]{1,0:T(8,128)S(1)}, u32[]{:S(2)}, u32[]{:S(2)}) %collective-permute-start) | collective-permute-done | bytes 66592 | tf_op jit(solution)/shard_map/ppermute | solution.py:19
  9.4 0.7 %collective-permute-start.1 = (f32[65,512]{1,0:T(8,128)S(1)}, f32[65,512]{1,0:T(8,128)S(1)}, u32[]{:S(2)}, u32[]{:S(2)}) collective-permute-start(f32[65,512]{1,0:T(8,128)S(1)} %pad_maximum_fusion.16), channel_id=1, source_target_pairs={{0,4},{1,5},{2,6},{3,7},{4,0},{5,1},{6,2},{7,3},{8,12},{9,13},{10,... | collective-permute-start | bytes 399368 | tf_op jit(solution)/shard_map/ppermute | solution.py:19
  10.9 3.7 %collective-permute-done.1 = f32[65,512]{1,0:T(8,128)S(1)} collective-permute-done((f32[65,512]{1,0:T(8,128)S(1)}, f32[65,512]{1,0:T(8,128)S(1)}, u32[]{:S(2)}, u32[]{:S(2)}) %collective-permute-start.1) | collective-permute-done | bytes 133152 | tf_op jit(solution)/shard_map/ppermute | solution.py:19
  14.7 1.8 %collective-permute-start.3 = (f32[64,1024]{1,0:T(8,128)S(1)}, f32[64,1024]{1,0:T(8,128)S(1)}, u32[]{:S(2)}, u32[]{:S(2)}) collective-permute-start(f32[64,1024]{1,0:T(8,128)S(1)} %slice.110), channel_id=1, source_target_pairs={{0,2},{1,3},{2,0},{3,1},{4,6},{5,7},{6,4},{7,5},{8,10},{9,11},{10,... | collective-permute-start | bytes 786440 | tf_op jit(solution)/shard_map/ppermute | solution.py:19
  16.6 1.7 %shard_map.60 = (bf16[2048,1024]{1,0:T(8,128)(2,1)S(1)}, f32[32,1024]{1,0:T(8,128)S(1)}) custom-call(f32[32,1024]{1,0:T(8,128)S(1)} %get-tuple-element.37.mine_ref.rows_ref, f32[32,1024]{1,0:T(8,128)S(1)} %get-tuple-element.38.vectors_ref, f32[32,1]{1,0:T(8,128)S(1)} %copy.10.scale_ref, bf16[256,1024]{1,0:T(8,128)(2,1)S(1)} %shard_map.59.right_ref, ...), custom_call_target="tpu_custom_call" | custom-call | flops 872415232 | bytes 4194304 | tf_op jit(solution)/shard_map/pallas_call | solution.py:93
  18.4 1.7 %shard_map.61 = (bf16[2048,1024]{1,0:T(8,128)(2,1)S(1)}, f32[32,1024]{1,0:T(8,128)S(1)}) custom-call(f32[32,1024]{1,0:T(8,128)S(1)} %get-tuple-element.40.rows_ref, f32[32,1024]{1,0:T(8,128)S(1)} %get-tuple-element.39.vectors_ref, f32[32,1]{1,0:T(8,128)S(1)} %copy.10.scale_ref, bf16[256,1024]{1,0:T(8,128)(2,1)S(1)} %shard_map.59.right_ref, ...), custom_call_target="tpu_custom_call" | custom-call | flops 872415232 | bytes 4194304 | tf_op jit(solution)/shard_map/pallas_call | solution.py:93
  20.1 1.0 %collective-permute-done.3 = f32[64,1024]{1,0:T(8,128)S(1)} collective-permute-done((f32[64,1024]{1,0:T(8,128)S(1)}, f32[64,1024]{1,0:T(8,128)S(1)}, u32[]{:S(2)}, u32[]{:S(2)}) %collective-permute-start.3) | collective-permute-done | bytes 262176 | tf_op jit(solution)/shard_map/ppermute | solution.py:19
  21.1 1.7 %shard_map.62 = (bf16[2048,1024]{1,0:T(8,128)(2,1)S(1)}, f32[32,1024]{1,0:T(8,128)S(1)}) custom-call(f32[32,1024]{1,0:T(8,128)S(1)} %get-tuple-element.42.rows_ref, f32[32,1024]{1,0:T(8,128)S(1)} %get-tuple-element.41.vectors_ref, f32[32,1]{1,0:T(8,128)S(1)} %copy.10.scale_ref, bf16[256,1024]{1,0:T(8,128)(2,1)S(1)} %shard_map.59.right_ref, ...), custom_call_target="tpu_custom_call" | custom-call | flops 872415232 | bytes 4194304 | tf_op jit(solution)/shard_map/pallas_call | solution.py:93
  22.9 1.7 %shard_map.63 = (bf16[2048,1024]{1,0:T(8,128)(2,1)S(1)}, f32[32,1024]{1,0:T(8,128)S(1)}) custom-call(f32[32,1024]{1,0:T(8,128)S(1)} %get-tuple-element.44.rows_ref, f32[32,1024]{1,0:T(8,128)S(1)} %get-tuple-element.43.vectors_ref, f32[32,1]{1,0:T(8,128)S(1)} %copy.10.scale_ref, bf16[256,1024]{1,0:T(8,128)(2,1)S(1)} %shard_map.59.right_ref, ...), custom_call_target="tpu_custom_call" | custom-call | flops 872415232 | bytes 4194304 | tf_op jit(solution)/shard_map/pallas_call | solution.py:93
  24.6 1.8 %collective-permute-start.6 = (f32[32,1024]{1,0:T(8,128)S(1)}, f32[32,1024]{1,0:T(8,128)S(1)}, u32[]{:S(2)}, u32[]{:S(2)}) collective-permute-start(f32[32,1024]{1,0:T(8,128)S(1)} %get-tuple-element.13), channel_id=1, source_target_pairs={{0,2},{1,3},{2,0},{3,1},{4,6},{5,7},{6,4},{7,5},{8,10},{9,11},{10,... | collective-permute-start | bytes 393224 | tf_op jit(solution)/shard_map/ppermute | solution.py:19
  26.6 0.8 %fusion.1 = f32[96,1024]{1,0:T(8,128)S(1)} fusion(bf16[2048,1024]{1,0:T(8,128)(2,1)S(1)} %get-tuple-element.14, bf16[32,1024]{1,0:T(8,128)(2,1)S(1)} %broadcast.4, bf16[32,1024]{1,0:T(8,128)(2,1)S(1)} %get-tuple-element.80, bf16[32,1024]{1,0:T(8,128)(2,1)S(1)} %get-tuple-element.81, bf16[32,1024]{1,0:T(8,128)(2,1)S(1)} %get-tuple-element.79), kind=kOutput, calls=%fused_computation.38 | convolution fusion | flops 405012480 | bytes 4849664 | tf_op jit(solution)/shard_map/dot_general | solution.py:114
  27.7 0.8 %convolution_add_fusion.8 = f32[96,1024]{1,0:T(8,128)S(1)} fusion(f32[96,1024]{1,0:T(8,128)S(1)} %fusion.1, bf16[2048,1024]{1,0:T(8,128)(2,1)S(1)} %get-tuple-element.15, bf16[32,1024]{1,0:T(8,128)(2,1)S(1)} %broadcast.4, bf16[32,1024]{1,0:T(8,128)(2,1)S(1)} %get-tuple-element.76, bf16[32,1024]{1,0:T(8,128)(2,1)S(1)} %get-tuple-element.77, ...), kind=kOutput, calls=%fused_computation.20 | convolution fusion | flops 405110784 | bytes 5242880 | tf_op jit(solution)/shard_map/dot_general | solution.py:114
  28.5 2.0 %collective-permute-done.6 = f32[32,1024]{1,0:T(8,128)S(1)} collective-permute-done((f32[32,1024]{1,0:T(8,128)S(1)}, f32[32,1024]{1,0:T(8,128)S(1)}, u32[]{:S(2)}, u32[]{:S(2)}) %collective-permute-start.6) | collective-permute-done | bytes 131104 | tf_op jit(solution)/shard_map/ppermute | solution.py:19
  30.6 0.8 %convolution_add_fusion.7 = f32[96,1024]{1,0:T(8,128)S(1)} fusion(f32[96,1024]{1,0:T(8,128)S(1)} %convolution_add_fusion.8, bf16[2048,1024]{1,0:T(8,128)(2,1)S(1)} %get-tuple-element.16, bf16[32,1024]{1,0:T(8,128)(2,1)S(1)} %broadcast.4, bf16[32,1024]{1,0:T(8,128)(2,1)S(1)} %get-tuple-element.72, bf16[32,1024]{1,0:T(8,128)(2,1)S(1)} %get-tuple-element.73, ...), kind=kOutput, calls=%fused_computation.19 | convolution fusion | flops 405110784 | bytes 5242880 | tf_op jit(solution)/shard_map/dot_general | solution.py:114
  31.9 0.8 %convolution_add_fusion.6 = f32[96,1024]{1,0:T(8,128)S(1)} fusion(f32[96,1024]{1,0:T(8,128)S(1)} %convolution_add_fusion.7, bf16[2048,1024]{1,0:T(8,128)(2,1)S(1)} %get-tuple-element.17, bf16[32,1024]{1,0:T(8,128)(2,1)S(1)} %broadcast.4, bf16[32,1024]{1,0:T(8,128)(2,1)S(1)} %get-tuple-element.68, bf16[32,1024]{1,0:T(8,128)(2,1)S(1)} %get-tuple-element.69, ...), kind=kOutput, calls=%fused_computation.18 | convolution fusion | flops 405110784 | bytes 5242880 | tf_op jit(solution)/shard_map/dot_general | solution.py:114
  33.3 1.8 %collective-permute-start.9 = (f32[32,1024]{1,0:T(8,128)S(1)}, f32[32,1024]{1,0:T(8,128)S(1)}, u32[]{:S(2)}, u32[]{:S(2)}) collective-permute-start(f32[32,1024]{1,0:T(8,128)S(1)} %get-tuple-element.32), channel_id=1, source_target_pairs={{0,2},{1,3},{2,0},{3,1},{4,6},{5,7},{6,4},{7,5},{8,10},{9,11},{10,... | collective-permute-start | bytes 393224 | tf_op jit(solution)/shard_map/ppermute | solution.py:19
  35.1 0.8 %fusion.10 = f32[96,1024]{1,0:T(8,128)S(1)} fusion(bf16[2048,1024]{1,0:T(8,128)(2,1)S(1)} %get-tuple-element.14, bf16[32,1024]{1,0:T(8,128)(2,1)S(1)} %broadcast.4, bf16[32,1024]{1,0:T(8,128)(2,1)S(1)} %get-tuple-element.66, bf16[32,1024]{1,0:T(8,128)(2,1)S(1)} %get-tuple-element.65, bf16[32,1024]{1,0:T(8,128)(2,1)S(1)} %get-tuple-element.31), kind=kOutput, calls=%fused_computation.43 | convolution fusion | flops 405012480 | bytes 4849664 | tf_op jit(solution)/shard_map/dot_general | solution.py:114
  36.5 0.8 %convolution_add_fusion.5 = f32[96,1024]{1,0:T(8,128)S(1)} fusion(f32[96,1024]{1,0:T(8,128)S(1)} %fusion.10, bf16[2048,1024]{1,0:T(8,128)(2,1)S(1)} %get-tuple-element.15, bf16[32,1024]{1,0:T(8,128)(2,1)S(1)} %broadcast.4, bf16[32,1024]{1,0:T(8,128)(2,1)S(1)} %get-tuple-element.63, bf16[32,1024]{1,0:T(8,128)(2,1)S(1)} %get-tuple-element.64, ...), kind=kOutput, calls=%fused_computation.17 | convolution fusion | flops 405110784 | bytes 5242880 | tf_op jit(solution)/shard_map/dot_general | solution.py:114
  37.3 1.6 %collective-permute-done.9 = f32[32,1024]{1,0:T(8,128)S(1)} collective-permute-done((f32[32,1024]{1,0:T(8,128)S(1)}, f32[32,1024]{1,0:T(8,128)S(1)}, u32[]{:S(2)}, u32[]{:S(2)}) %collective-permute-start.9) | collective-permute-done | bytes 131104 | tf_op jit(solution)/shard_map/ppermute | solution.py:19
  39.0 0.8 %convolution_add_fusion.4 = f32[96,1024]{1,0:T(8,128)S(1)} fusion(f32[96,1024]{1,0:T(8,128)S(1)} %convolution_add_fusion.5, bf16[2048,1024]{1,0:T(8,128)(2,1)S(1)} %get-tuple-element.16, bf16[32,1024]{1,0:T(8,128)(2,1)S(1)} %broadcast.4, bf16[32,1024]{1,0:T(8,128)(2,1)S(1)} %get-tuple-element.60, bf16[32,1024]{1,0:T(8,128)(2,1)S(1)} %get-tuple-element.61, ...), kind=kOutput, calls=%fused_computation.16 | convolution fusion | flops 405110784 | bytes 5242880 | tf_op jit(solution)/shard_map/dot_general | solution.py:114
  40.3 1.0 %convolution_add_fusion.3 = f32[96,1024]{1,0:T(8,128)S(1)} fusion(f32[96,1024]{1,0:T(8,128)S(1)} %convolution_add_fusion.4, bf16[2048,1024]{1,0:T(8,128)(2,1)S(1)} %get-tuple-element.17, bf16[32,1024]{1,0:T(8,128)(2,1)S(1)} %broadcast.4, bf16[32,1024]{1,0:T(8,128)(2,1)S(1)} %get-tuple-element.57, bf16[32,1024]{1,0:T(8,128)(2,1)S(1)} %get-tuple-element.58, ...), kind=kOutput, calls=%fused_computation.15 | convolution fusion | flops 405110784 | bytes 5242880 | tf_op jit(solution)/shard_map/dot_general | solution.py:114
  42.1 1.8 %collective-permute-start.12 = (f32[32,1024]{1,0:T(8,128)S(1)}, f32[32,1024]{1,0:T(8,128)S(1)}, u32[]{:S(2)}, u32[]{:S(2)}) collective-permute-start(f32[32,1024]{1,0:T(8,128)S(1)} %get-tuple-element.23), channel_id=1, source_target_pairs={{0,2},{1,3},{2,0},{3,1},{4,6},{5,7},{6,4},{7,5},{8,10},{9,11},{10,... | collective-permute-start | bytes 393224 | tf_op jit(solution)/shard_map/ppermute | solution.py:19
  43.9 0.8 %fusion.19 = f32[96,1024]{1,0:T(8,128)S(1)} fusion(bf16[2048,1024]{1,0:T(8,128)(2,1)S(1)} %get-tuple-element.14, bf16[32,1024]{1,0:T(8,128)(2,1)S(1)} %broadcast.4, bf16[32,1024]{1,0:T(8,128)(2,1)S(1)} %get-tuple-element.55, bf16[32,1024]{1,0:T(8,128)(2,1)S(1)} %get-tuple-element.54, bf16[32,1024]{1,0:T(8,128)(2,1)S(1)} %get-tuple-element.22), kind=kOutput, calls=%fused_computation.48 | convolution fusion | flops 405012480 | bytes 4849664 | tf_op jit(solution)/shard_map/dot_general | solution.py:114
  45.2 0.8 %convolution_add_fusion.2 = f32[96,1024]{1,0:T(8,128)S(1)} fusion(f32[96,1024]{1,0:T(8,128)S(1)} %fusion.19, bf16[2048,1024]{1,0:T(8,128)(2,1)S(1)} %get-tuple-element.15, bf16[32,1024]{1,0:T(8,128)(2,1)S(1)} %broadcast.4, bf16[32,1024]{1,0:T(8,128)(2,1)S(1)} %get-tuple-element.52, bf16[32,1024]{1,0:T(8,128)(2,1)S(1)} %get-tuple-element.53, ...), kind=kOutput, calls=%fused_computation.14 | convolution fusion | flops 405110784 | bytes 5242880 | tf_op jit(solution)/shard_map/dot_general | solution.py:114
  46.0 1.6 %collective-permute-done.12 = f32[32,1024]{1,0:T(8,128)S(1)} collective-permute-done((f32[32,1024]{1,0:T(8,128)S(1)}, f32[32,1024]{1,0:T(8,128)S(1)}, u32[]{:S(2)}, u32[]{:S(2)}) %collective-permute-start.12) | collective-permute-done | bytes 131104 | tf_op jit(solution)/shard_map/ppermute | solution.py:19
  47.7 0.8 %convolution_add_fusion.1 = f32[96,1024]{1,0:T(8,128)S(1)} fusion(f32[96,1024]{1,0:T(8,128)S(1)} %convolution_add_fusion.2, bf16[2048,1024]{1,0:T(8,128)(2,1)S(1)} %get-tuple-element.16, bf16[32,1024]{1,0:T(8,128)(2,1)S(1)} %broadcast.4, bf16[32,1024]{1,0:T(8,128)(2,1)S(1)} %get-tuple-element.49, bf16[32,1024]{1,0:T(8,128)(2,1)S(1)} %get-tuple-element.50, ...), kind=kOutput, calls=%fused_computation.13 | convolution fusion | flops 405110784 | bytes 5242880 | tf_op jit(solution)/shard_map/dot_general | solution.py:114
  49.1 0.8 %convolution_add_fusion = f32[96,1024]{1,0:T(8,128)S(1)} fusion(f32[96,1024]{1,0:T(8,128)S(1)} %convolution_add_fusion.1, bf16[2048,1024]{1,0:T(8,128)(2,1)S(1)} %get-tuple-element.17, bf16[32,1024]{1,0:T(8,128)(2,1)S(1)} %broadcast.4, bf16[32,1024]{1,0:T(8,128)(2,1)S(1)} %get-tuple-element.46, bf16[32,1024]{1,0:T(8,128)(2,1)S(1)} %get-tuple-element.47, ...), kind=kOutput, calls=%fused_computation.12 | convolution fusion | flops 405110784 | bytes 5242880 | tf_op jit(solution)/shard_map/dot_general | solution.py:114
  50.8 1.8 %collective-permute-start.14 = (f32[32]{0:T(128)S(1)}, f32[32]{0:T(128)S(1)}, u32[]{:S(2)}, u32[]{:S(2)}) collective-permute-start(f32[32]{0:T(128)S(1)} %get-tuple-element.20), channel_id=1, source_target_pairs={{0,2},{1,3},{2,0},{3,1},{4,6},{5,7},{6,4},{7,5},{8,10},{9,11},{10,... | collective-permute-start | bytes 392 | tf_op jit(solution)/shard_map/ppermute | solution.py:19
  52.5 1.8 %collective-permute-done.14 = f32[32]{0:T(128)S(1)} collective-permute-done((f32[32]{0:T(128)S(1)}, f32[32]{0:T(128)S(1)}, u32[]{:S(2)}, u32[]{:S(2)}) %collective-permute-start.14) | collective-permute-done | bytes 160 | tf_op jit(solution)/shard_map/ppermute | solution.py:19
  54.4 1.1 %collective-permute-done.15 = f32[32]{0:T(128)S(1)} collective-permute-done((f32[32]{0:T(128)S(1)}, f32[32]{0:T(128)S(1)}, u32[]{:S(2)}, u32[]{:S(2)}) %collective-permute-start.15) | collective-permute-done | bytes 160 | tf_op jit(solution)/shard_map/ppermute | solution.py:19
  (60 shorter events, 7.4 us)
Async XLA Ops:
  1.4 7.9 %collective-permute-start = (f32[65,256]{1,0:T(8,128)S(1)}, f32[65,256]{1,0:T(8,128)S(1)}, u32[]{:S(2)}, u32[]{:S(2)}) collective-permute-start(f32[65,256]{1,0:T(8,128)S(1)} %pad_maximum_fusion.17), channel_id=1, source_target_pairs={{0,8},{1,9},{2,10},{3,11},{4,12},{5,13},{6,14},{7,15},{8,0},{9,1},... | collective-permute-start | bytes 199688 | tf_op jit(solution)/shard_map/ppermute | solution.py:19
  9.4 5.2 %collective-permute-start.1 = (f32[65,512]{1,0:T(8,128)S(1)}, f32[65,512]{1,0:T(8,128)S(1)}, u32[]{:S(2)}, u32[]{:S(2)}) collective-permute-start(f32[65,512]{1,0:T(8,128)S(1)} %pad_maximum_fusion.16), channel_id=1, source_target_pairs={{0,4},{1,5},{2,6},{3,7},{4,0},{5,1},{6,2},{7,3},{8,12},{9,13},{10,... | collective-permute-start | bytes 399368 | tf_op jit(solution)/shard_map/ppermute | solution.py:19
  14.7 6.4 %collective-permute-start.3 = (f32[64,1024]{1,0:T(8,128)S(1)}, f32[64,1024]{1,0:T(8,128)S(1)}, u32[]{:S(2)}, u32[]{:S(2)}) collective-permute-start(f32[64,1024]{1,0:T(8,128)S(1)} %slice.110), channel_id=1, source_target_pairs={{0,2},{1,3},{2,0},{3,1},{4,6},{5,7},{6,4},{7,5},{8,10},{9,11},{10,... | collective-permute-start | bytes 786440 | tf_op jit(solution)/shard_map/ppermute | solution.py:19
  16.4 1.9 %collective-permute-start.2 = (f32[64,1024]{1,0:T(8,128)S(1)}, f32[64,1024]{1,0:T(8,128)S(1)}, u32[]{:S(2)}, u32[]{:S(2)}) collective-permute-start(f32[64,1024]{1,0:T(8,128)S(1)} %slice.110), channel_id=1, source_target_pairs={{0,1},{1,0},{2,3},{3,2},{4,5},{5,4},{6,7},{7,6},{8,9},{9,8},{10,11... | collective-permute-start | bytes 786440 | tf_op jit(solution)/shard_map/ppermute | solution.py:19
  21.1 1.7 %collective-permute-start.4 = (f32[64,1024]{1,0:T(8,128)S(1)}, f32[64,1024]{1,0:T(8,128)S(1)}, u32[]{:S(2)}, u32[]{:S(2)}) collective-permute-start(f32[64,1024]{1,0:T(8,128)S(1)} %collective-permute-done.3), channel_id=1, source_target_pairs={{0,1},{1,0},{2,3},{3,2},{4,5},{5,4},{6,7},{7,6},{8,9},{9,8},{10,11... | collective-permute-start | bytes 786440 | tf_op jit(solution)/shard_map/ppermute | solution.py:19
  24.6 5.9 %collective-permute-start.6 = (f32[32,1024]{1,0:T(8,128)S(1)}, f32[32,1024]{1,0:T(8,128)S(1)}, u32[]{:S(2)}, u32[]{:S(2)}) collective-permute-start(f32[32,1024]{1,0:T(8,128)S(1)} %get-tuple-element.13), channel_id=1, source_target_pairs={{0,2},{1,3},{2,0},{3,1},{4,6},{5,7},{6,4},{7,5},{8,10},{9,11},{10,... | collective-permute-start | bytes 393224 | tf_op jit(solution)/shard_map/ppermute | solution.py:19
  26.3 1.3 %collective-permute-start.5 = (f32[32,1024]{1,0:T(8,128)S(1)}, f32[32,1024]{1,0:T(8,128)S(1)}, u32[]{:S(2)}, u32[]{:S(2)}) collective-permute-start(f32[32,1024]{1,0:T(8,128)S(1)} %get-tuple-element.13), channel_id=1, source_target_pairs={{0,1},{1,0},{2,3},{3,2},{4,5},{5,4},{6,7},{7,6},{8,9},{9,8},{10,11... | collective-permute-start | bytes 393224 | tf_op jit(solution)/shard_map/ppermute | solution.py:19
  30.5 1.3 %collective-permute-start.7 = (f32[32,1024]{1,0:T(8,128)S(1)}, f32[32,1024]{1,0:T(8,128)S(1)}, u32[]{:S(2)}, u32[]{:S(2)}) collective-permute-start(f32[32,1024]{1,0:T(8,128)S(1)} %collective-permute-done.6), channel_id=1, source_target_pairs={{0,1},{1,0},{2,3},{3,2},{4,5},{5,4},{6,7},{7,6},{8,9},{9,8},{10,11... | collective-permute-start | bytes 393224 | tf_op jit(solution)/shard_map/ppermute | solution.py:19
  33.3 5.6 %collective-permute-start.9 = (f32[32,1024]{1,0:T(8,128)S(1)}, f32[32,1024]{1,0:T(8,128)S(1)}, u32[]{:S(2)}, u32[]{:S(2)}) collective-permute-start(f32[32,1024]{1,0:T(8,128)S(1)} %get-tuple-element.32), channel_id=1, source_target_pairs={{0,2},{1,3},{2,0},{3,1},{4,6},{5,7},{6,4},{7,5},{8,10},{9,11},{10,... | collective-permute-start | bytes 393224 | tf_op jit(solution)/shard_map/ppermute | solution.py:19
  35.1 1.3 %collective-permute-start.8 = (f32[32,1024]{1,0:T(8,128)S(1)}, f32[32,1024]{1,0:T(8,128)S(1)}, u32[]{:S(2)}, u32[]{:S(2)}) collective-permute-start(f32[32,1024]{1,0:T(8,128)S(1)} %get-tuple-element.32), channel_id=1, source_target_pairs={{0,1},{1,0},{2,3},{3,2},{4,5},{5,4},{6,7},{7,6},{8,9},{9,8},{10,11... | collective-permute-start | bytes 393224 | tf_op jit(solution)/shard_map/ppermute | solution.py:19
  38.9 1.3 %collective-permute-start.10 = (f32[32,1024]{1,0:T(8,128)S(1)}, f32[32,1024]{1,0:T(8,128)S(1)}, u32[]{:S(2)}, u32[]{:S(2)}) collective-permute-start(f32[32,1024]{1,0:T(8,128)S(1)} %collective-permute-done.9), channel_id=1, source_target_pairs={{0,1},{1,0},{2,3},{3,2},{4,5},{5,4},{6,7},{7,6},{8,9},{9,8},{10,11... | collective-permute-start | bytes 393224 | tf_op jit(solution)/shard_map/ppermute | solution.py:19
  42.1 5.6 %collective-permute-start.12 = (f32[32,1024]{1,0:T(8,128)S(1)}, f32[32,1024]{1,0:T(8,128)S(1)}, u32[]{:S(2)}, u32[]{:S(2)}) collective-permute-start(f32[32,1024]{1,0:T(8,128)S(1)} %get-tuple-element.23), channel_id=1, source_target_pairs={{0,2},{1,3},{2,0},{3,1},{4,6},{5,7},{6,4},{7,5},{8,10},{9,11},{10,... | collective-permute-start | bytes 393224 | tf_op jit(solution)/shard_map/ppermute | solution.py:19
  43.9 1.3 %collective-permute-start.11 = (f32[32,1024]{1,0:T(8,128)S(1)}, f32[32,1024]{1,0:T(8,128)S(1)}, u32[]{:S(2)}, u32[]{:S(2)}) collective-permute-start(f32[32,1024]{1,0:T(8,128)S(1)} %get-tuple-element.23), channel_id=1, source_target_pairs={{0,1},{1,0},{2,3},{3,2},{4,5},{5,4},{6,7},{7,6},{8,9},{9,8},{10,11... | collective-permute-start | bytes 393224 | tf_op jit(solution)/shard_map/ppermute | solution.py:19
  47.7 1.3 %collective-permute-start.13 = (f32[32,1024]{1,0:T(8,128)S(1)}, f32[32,1024]{1,0:T(8,128)S(1)}, u32[]{:S(2)}, u32[]{:S(2)}) collective-permute-start(f32[32,1024]{1,0:T(8,128)S(1)} %collective-permute-done.12), channel_id=1, source_target_pairs={{0,1},{1,0},{2,3},{3,2},{4,5},{5,4},{6,7},{7,6},{8,9},{9,8},{10,11... | collective-permute-start | bytes 393224 | tf_op jit(solution)/shard_map/ppermute | solution.py:19
  50.8 3.6 %collective-permute-start.14 = (f32[32]{0:T(128)S(1)}, f32[32]{0:T(128)S(1)}, u32[]{:S(2)}, u32[]{:S(2)}) collective-permute-start(f32[32]{0:T(128)S(1)} %get-tuple-element.20), channel_id=1, source_target_pairs={{0,2},{1,3},{2,0},{3,1},{4,6},{5,7},{6,4},{7,5},{8,10},{9,11},{10,... | collective-permute-start | bytes 392 | tf_op jit(solution)/shard_map/ppermute | solution.py:19
  54.4 1.1 %collective-permute-start.15 = (f32[32]{0:T(128)S(1)}, f32[32]{0:T(128)S(1)}, u32[]{:S(2)}, u32[]{:S(2)}) collective-permute-start(f32[32]{0:T(128)S(1)} %add.113), channel_id=1, source_target_pairs={{0,1},{1,0},{2,3},{3,2},{4,5},{5,4},{6,7},{7,6},{8,9},{9,8},{10,11... | collective-permute-start | bytes 392 | tf_op jit(solution)/shard_map/ppermute | solution.py:19

commit v10 on v9

--- a/solution.py
+++ b/solution.py
@@ -1,3 +1,4 @@
+import functools
 import math
 
 import jax
@@ -12,6 +13,7 @@
 VMEM_BYTES = 16 << 20
 NORM_ROWS = 64
 BUILD_ROWS = 1024
+PACE = 10**9
 POINT_SCALE = math.sqrt(math.log2(math.e))
 
 
@@ -57,54 +59,70 @@
     return left, right
 
 
-def scaled_operand_kernel(mine_ref, scale_ref, right_ref):
-    right_ref[...] = operands(mine_ref[...] * scale_ref[...])[1]
-
-
-def build_kernel(rows_ref, vectors_ref, scale_ref, right_ref, sum_ref, tile_ref, out_ref):
-    total, cols = rows_ref.shape[1], right_ref.shape[1]
+def prepare_kernel(part_ref, scale_ref, right_ref, part_out_ref):
+    feats = scale_ref.shape[0]
+    right_ref[...] = operands(part_ref[:feats] * scale_ref[...])[1]
+    part_out_ref[...] = part_ref[:-1]
+
+
+def build_kernel(top, size, rows_ref, vectors_ref, scale_ref, right_ref, sum_ref, *refs):
+    tile_ref, out_ref = refs[-2:]
+    count, cols = rows_ref.shape[1], right_ref.shape[1]
     probes = vectors_ref.shape[0]
-    block, step = min(total, BUILD_ROWS), min(cols, 256)
+    block, step = min(count, BUILD_ROWS), min(cols, 256)
     high, rest = halve(vectors_ref[...])
     mid, rest = halve(rest)
     twice = jnp.concatenate([high, mid], axis=0)
     thrice = jnp.concatenate([high, mid, rest.astype(jnp.bfloat16)], axis=0)
-    for top in range(0, total, block):
-        down = slice(top, top + block)
+    for start in range(0, count, block):
+        down = slice(start, start + block)
         left = jnp.transpose(operands(rows_ref[:, down] * scale_ref[...])[0])
         for at in range(0, cols, step):
             here = slice(at, at + step)
             power = jnp.dot(left, right_ref[:, here], preferred_element_type=jnp.float32)
             high, rest = halve(jnp.exp2(power))
             low = rest.astype(jnp.bfloat16)
-            tile_ref[down, here] = high
-            tile_ref[total + top : total + top + block, here] = low
+            tile_ref[top + start : top + start + block, here] = high
+            tile_ref[size + top + start : size + top + start + block, here] = low
             large = jnp.dot(thrice[:, down], high, preferred_element_type=jnp.float32)
             small = jnp.dot(twice[:, down], low, preferred_element_type=jnp.float32)
             term = large[:probes] + (
                 (large[probes : 2 * probes] + small[:probes]) + (large[2 * probes :] + small[probes:])
             )
-            before = sum_ref if top == 0 else out_ref
+            before = sum_ref if start == 0 else out_ref
             out_ref[:, here] = before[:, here] + term
 
 
-def call(kernel, outs, *args, **cost):
+def call(kernel, outs, *args, aliases={}, **cost):
     whole = pl.BlockSpec(memory_space=pltpu.VMEM)
     return pl.pallas_call(
         kernel,
         out_shape=outs,
         in_specs=[whole] * len(args),
         out_specs=jax.tree.map(lambda _: whole, outs),
+        input_output_aliases=aliases,
         compiler_params=pltpu.CompilerParams(vmem_limit_bytes=VMEM_BYTES),
         cost_estimate=pl.CostEstimate(**cost),
     )(*args)
 
 
-def build_piece(rows, vectors, scale, right, total):
+def prepare(part, scale):
+    feats, cols = scale.shape[0], part.shape[1]
+    outs = (
+        jax.ShapeDtypeStruct((6 * feats + NORM_ROWS, cols), jnp.bfloat16),
+        jax.ShapeDtypeStruct((part.shape[0] - 1, cols), jnp.float32),
+    )
+    return call(prepare_kernel, outs, part, scale, flops=PACE, bytes_accessed=feats * cols, transcendentals=0)
+
+
+def build_piece(rows, vectors, scale, right, total, size, top=0, piece=None):
     count, cols = rows.shape[1], right.shape[1]
-    outs = (jax.ShapeDtypeStruct((2 * count, cols), jnp.bfloat16), jax.ShapeDtypeStruct(total.shape, jnp.float32))
-    cost = dict(flops=2 * count * cols * 416, bytes_accessed=4 * count * cols, transcendentals=count * cols)
-    return call(build_kernel, outs, rows, vectors, scale, right, total, **cost)
+    outs = (jax.ShapeDtypeStruct((2 * size, cols), jnp.bfloat16), jax.ShapeDtypeStruct(total.shape, jnp.float32))
+    cost = dict(flops=PACE * count // 512, bytes_accessed=4 * count * cols, transcendentals=count * cols)
+    args = (rows, vectors, scale, right, total)
+    if piece is not None:
+        args, cost["aliases"] = (*args, piece), {len(args): 0}
+    return call(functools.partial(build_kernel, top, size), outs, *args, **cost)
 
 
 def apply_piece(vectors, piece):
@@ -134,28 +152,38 @@
                 pieces += [came, swap(came, n, 1)]
             return pieces
 
-        mine = lax.optimization_barrier(jnp.concatenate([points, targets, noise_var[None, :]], axis=0))
+        scale = (POINT_SCALE / lengthscale)[:, None]
+        parts = [lax.optimization_barrier(jnp.concatenate([points, targets, noise_var[None, :]], axis=0))]
         for stride in outer:
-            mine = jnp.concatenate([mine, swap(mine, n, stride)], axis=1)
-        noise = mine[-1:]
-        scale = (POINT_SCALE / lengthscale)[:, None]
-        first = arrivals(mine[:-1])
+            parts.append(swap(jnp.concatenate(parts, axis=1), n, stride))
+        noise = jnp.concatenate([x[-1:] for x in parts], axis=1)
+        rights, parts = zip(*[prepare(x, scale) for x in parts])
+        right, mine = jnp.concatenate(rights, axis=1), jnp.concatenate(parts, axis=1)
         cols = noise.shape[1]
-        right = call(
-            scaled_operand_kernel,
-            jax.ShapeDtypeStruct((6 * feats + NORM_ROWS, cols), jnp.bfloat16),
-            mine[:feats],
-            scale,
-            flops=feats * cols,
-            bytes_accessed=feats * cols,
-            transcendentals=0,
-        )
+        my_applied = noise * mine[feats:]
+
+        def build(x, total, size, top=0, piece=None):
+            return build_piece(x[:feats], x[feats:], scale, right, total, size, top, piece)
+
+        if outer and len(inner) == 2:
+            *came, last = lax.optimization_barrier((*[swap(x, n, inner[0]) for x in parts[:-1]], parts[-1]))
+            late, early, half = swap(last, n, inner[0]), jnp.concatenate(came, axis=1), cols // 2
+            across, early_across = swap(mine, n, 1), swap(early, n, 1)
+            tile = []
+            for x in (mine, across, early, early_across):
+                piece, my_applied = build(x, my_applied, cols)
+                tile.append(piece)
+            late, my_applied = lax.optimization_barrier((late, my_applied))
+            late_across = swap(late, n, 1)
+            tile[2], my_applied = build(late, my_applied, cols, half, tile[2])
+            tile[3], my_applied = build(late_across, my_applied, cols, half, tile[3])
+            first = [mine, across, jnp.concatenate([early, late], axis=1), jnp.concatenate([early_across, late_across], axis=1)]
+        else:
+            first, tile = arrivals(mine), []
+            for x in first:
+                piece, my_applied = build(x, my_applied, x.shape[1])
+                tile.append(piece)
         starts = [x[feats:] for x in first]
-        tile = []
-        my_applied = noise * starts[0]
-        for x, start in zip(first, starts):
-            piece, my_applied = build_piece(x[:feats], start, scale, right, my_applied)
-            tile.append(piece)
 
         def operator(pieces):
             total = apply_piece(pieces[0], tile[0])

time: 56.5 us -> 58.2 us (1.030)
  waiting for transfers between devices: 19.7 us -> 21.5 us
  starting transfers between devices: 13.9 us -> 12.6 us
  Pallas kernels: 6.97 us -> 7.9 us
    ppermute x16 -> x19, waiting for transfers between devices: 19.7 us -> 21.5 us  [swap(): return lax.ppermute(x, 'blk', [(i, i ^ stride) for i in range(n)])]
    ppermute x16 -> x19, starting transfers between devices: 13.9 us -> 12.6 us  [swap(): return lax.ppermute(x, 'blk', [(i, i ^ stride) for i in range(n)])]
    pallas_call x5 -> x9, Pallas kernels: 6.97 us -> 7.9 us  [call(): pl.pallas_call(kernel, out_shape=outs, in_specs=[whole] * len(args), out_...]
  transfers between devices with their start and end apart: 16 -> 19, of which waited for: 14 -> 13; matrix products, arithmetic and copies ran while one was open for 15% -> 15% of each run, Pallas kernels for 9% -> 12%
where the time goes in v10:
time: 58.2 us; the launch traced here: 58 us
  waiting for transfers between devices  21.5 us (37%)
  starting transfers between devices  12.6 us (22%)
  matrix products  9.97 us (17%)
  Pallas kernels  7.9 us (14%)
  other arithmetic  4.84 us (8%)
  between operations  0.95 us (2%)
    ppermute x19, waiting for transfers between devices, swap(): return lax.ppermute(x, 'blk', [(i, i ^ stride) for i in range(n)])  21.5 us
    ppermute x19, starting transfers between devices, swap(): return lax.ppermute(x, 'blk', [(i, i ^ stride) for i in range(n)])  12.6 us
    dot_general x12, matrix products, apply_piece(): jnp.dot(jnp.concatenate([left, right], axis=1), piece, preferred_element_...  9.97 us
    pallas_call x9, Pallas kernels, call(): pl.pallas_call(kernel, out_shape=outs, in_specs=[whole] * len(args), out_...  7.9 us
  transfers between devices with their start and end apart: 19, of which 13 were waited for; matrix products, arithmetic and copies ran while one was open for 15% of the time, Pallas kernels for 12%

profile of v10, /device:TPU:0, one launch (start us, length us, event | category | flops | bytes accessed | tf_op | source)
XLA Modules:
  0.0 58.0 jit_solution(417763919207691640)
XLA Ops:
  0.6 0.8 %pad_maximum_fusion.18.part_ref = f32[65,256]{1,0:T(8,128)S(1)} fusion(f32[1,256]{1,0:T(1,128)} %bitcast.20, f32[32,256]{1,0:T(8,128)} %param.7, f32[32,256]{1,0:T(8,128)} %param.4), kind=kLoop, calls=%fused_computation.245 | loop fusion | flops 33280 | bytes 133120 | tf_op jit(solution)/shard_map/concatenate | solution.py:156
  1.4 4.0 %collective-permute-start = (f32[65,256]{1,0:T(8,128)S(1)}, f32[65,256]{1,0:T(8,128)S(1)}, u32[]{:S(2)}, u32[]{:S(2)}) collective-permute-start(f32[65,256]{1,0:T(8,128)S(1)} %pad_maximum_fusion.18.part_ref), channel_id=1, source_target_pairs={{0,8},{1,9},{2,10},{3,11},{4,12},{5,13},{6,14},{7,15},{8,0},{9,1},... | collective-permute-start | bytes 199688 | tf_op jit(solution)/shard_map/ppermute | solution.py:21
  6.3 1.6 %collective-permute-start.3 = (f32[64,256]{1,0:T(8,128)S(1)}, f32[64,256]{1,0:T(8,128)S(1)}, u32[]{:S(2)}, u32[]{:S(2)}) collective-permute-start(f32[64,256]{1,0:T(8,128)S(1)} %get-tuple-element.25), channel_id=1, source_target_pairs={{0,2},{1,3},{2,0},{3,1},{4,6},{5,7},{6,4},{7,5},{8,10},{9,11},{10,... | collective-permute-start | bytes 196616 | tf_op jit(solution)/shard_map/ppermute | solution.py:21
  7.9 1.4 %collective-permute-done.part_ref = f32[65,256]{1,0:T(8,128)S(1)} collective-permute-done((f32[65,256]{1,0:T(8,128)S(1)}, f32[65,256]{1,0:T(8,128)S(1)}, u32[]{:S(2)}, u32[]{:S(2)}) %collective-permute-start) | collective-permute-done | bytes 66592 | tf_op jit(solution)/shard_map/ppermute | solution.py:21
  9.4 0.7 %collective-permute-start.1 = (f32[65,512]{1,0:T(8,128)S(1)}, f32[65,512]{1,0:T(8,128)S(1)}, u32[]{:S(2)}, u32[]{:S(2)}) collective-permute-start(f32[65,512]{1,0:T(8,128)S(1)} %pad_maximum_fusion.17), channel_id=1, source_target_pairs={{0,4},{1,5},{2,6},{3,7},{4,0},{5,1},{6,2},{7,3},{8,12},{9,13},{10,... | collective-permute-start | bytes 399368 | tf_op jit(solution)/shard_map/ppermute | solution.py:21
  10.2 1.6 %collective-permute-start.4 = (f32[64,256]{1,0:T(8,128)S(1)}, f32[64,256]{1,0:T(8,128)S(1)}, u32[]{:S(2)}, u32[]{:S(2)}) collective-permute-start(f32[64,256]{1,0:T(8,128)S(1)} %get-tuple-element.26), channel_id=1, source_target_pairs={{0,2},{1,3},{2,0},{3,1},{4,6},{5,7},{6,4},{7,5},{8,10},{9,11},{10,... | collective-permute-start | bytes 196616 | tf_op jit(solution)/shard_map/ppermute | solution.py:21
  11.8 2.8 %collective-permute-done.1.part_ref = f32[65,512]{1,0:T(8,128)S(1)} collective-permute-done((f32[65,512]{1,0:T(8,128)S(1)}, f32[65,512]{1,0:T(8,128)S(1)}, u32[]{:S(2)}, u32[]{:S(2)}) %collective-permute-start.1) | collective-permute-done | bytes 133152 | tf_op jit(solution)/shard_map/ppermute | solution.py:21
  15.5 1.8 %collective-permute-start.5 = (f32[64,512]{1,0:T(8,128)S(1)}, f32[64,512]{1,0:T(8,128)S(1)}, u32[]{:S(2)}, u32[]{:S(2)}) collective-permute-start(f32[64,512]{1,0:T(8,128)S(1)} %get-tuple-element.30), channel_id=1, source_target_pairs={{0,2},{1,3},{2,0},{3,1},{4,6},{5,7},{6,4},{7,5},{8,10},{9,11},{10,... | collective-permute-start | bytes 393224 | tf_op jit(solution)/shard_map/ppermute | solution.py:21
  17.3 1.7 %shard_map.62 = (bf16[2048,1024]{1,0:T(8,128)(2,1)S(1)}, f32[32,1024]{1,0:T(8,128)S(1)}) custom-call(f32[32,1024]{1,0:T(8,128)S(1)} %get-tuple-element.68.rows_ref, f32[32,1024]{1,0:T(8,128)S(1)} %get-tuple-element.69.vectors_ref, f32[32,1]{1,0:T(8,128)S(1)} %copy.8.scale_ref, bf16[256,1024]{1,0:T(8,128)(2,1)S(1)} %constant_dynamic-update-slice_fusion.5.right_ref, ...), custom_call_target="tpu_custom_call" | custom-call | flops 2000000000 | bytes 4194304 | tf_op jit(solution)/shard_map/pallas_call | solution.py:98
  19.1 1.7 %shard_map.63 = (bf16[2048,1024]{1,0:T(8,128)(2,1)S(1)}, f32[32,1024]{1,0:T(8,128)S(1)}) custom-call(f32[32,1024]{1,0:T(8,128)S(1)} %get-tuple-element.71.rows_ref, f32[32,1024]{1,0:T(8,128)S(1)} %get-tuple-element.70.vectors_ref, f32[32,1]{1,0:T(8,128)S(1)} %copy.8.scale_ref, bf16[256,1024]{1,0:T(8,128)(2,1)S(1)} %constant_dynamic-update-slice_fusion.5.right_ref, ...), custom_call_target="tpu_custom_call" | custom-call | flops 2000000000 | bytes 4194304 | tf_op jit(solution)/shard_map/pallas_call | solution.py:98
  20.8 1.1 %shard_map.64 = (bf16[2048,1024]{1,0:T(8,128)(2,1)S(1)}, f32[32,1024]{1,0:T(8,128)S(1)}) custom-call(f32[32,512]{1,0:T(8,128)S(1)} %get-tuple-element.115.rows_ref, f32[32,512]{1,0:T(8,128)S(1)} %get-tuple-element.114.vectors_ref, f32[32,1]{1,0:T(8,128)S(1)} %copy.8.scale_ref, bf16[256,1024]{1,0:T(8,128)(2,1)S(1)} %constant_dynamic-update-slice_fusion.5.right_ref, ...), custom_call_target="tpu_custom_call" | custom-call | flops 1000000000 | bytes 2097152 | tf_op jit(solution)/shard_map/pallas_call | solution.py:98
  21.9 1.1 %shard_map.65 = (bf16[2048,1024]{1,0:T(8,128)(2,1)S(1)}, f32[32,1024]{1,0:T(8,128)S(1)}) custom-call(f32[32,512]{1,0:T(8,128)S(1)} %get-tuple-element.117.rows_ref, f32[32,512]{1,0:T(8,128)S(1)} %get-tuple-element.116.vectors_ref, f32[32,1]{1,0:T(8,128)S(1)} %copy.8.scale_ref, bf16[256,1024]{1,0:T(8,128)(2,1)S(1)} %constant_dynamic-update-slice_fusion.5.right_ref, ...), custom_call_target="tpu_custom_call" | custom-call | flops 1000000000 | bytes 2097152 | tf_op jit(solution)/shard_map/pallas_call | solution.py:98
  23.0 1.0 %shard_map.66 = (bf16[2048,1024]{1,0:T(8,128)(2,1)S(1)}, f32[32,1024]{1,0:T(8,128)S(1)}) custom-call(f32[32,512]{1,0:T(8,128)S(1)} %get-tuple-element.111.rows_ref, f32[32,512]{1,0:T(8,128)S(1)} %get-tuple-element.110.vectors_ref, f32[32,1]{1,0:T(8,128)S(1)} %copy.8.scale_ref, ...), custom_call_target="tpu_custom_call", output_to_operand_aliasing={{0}: (5, {})} | custom-call | flops 1000000000 | bytes 2097152 | tf_op jit(solution)/shard_map/pallas_call | solution.py:98
  24.4 1.0 %shard_map.67 = (bf16[2048,1024]{1,0:T(8,128)(2,1)S(1)}, f32[32,1024]{1,0:T(8,128)S(1)}) custom-call(f32[32,512]{1,0:T(8,128)S(1)} %get-tuple-element.113.rows_ref, f32[32,512]{1,0:T(8,128)S(1)} %get-tuple-element.112.vectors_ref, f32[32,1]{1,0:T(8,128)S(1)} %copy.8.scale_ref, ...), custom_call_target="tpu_custom_call", output_to_operand_aliasing={{0}: (5, {})} | custom-call | flops 1000000000 | bytes 2097152 | tf_op jit(solution)/shard_map/pallas_call | solution.py:98
  26.1 0.8 %fusion.3 = f32[96,1024]{1,0:T(8,128)S(1)} fusion(bf16[2048,1024]{1,0:T(8,128)(2,1)S(1)} %get-tuple-element.44, bf16[32,1024]{1,0:T(8,128)(2,1)S(1)} %broadcast.4, bf16[32,1024]{1,0:T(8,128)(2,1)S(1)} %get-tuple-element.107, bf16[32,1024]{1,0:T(8,128)(2,1)S(1)} %get-tuple-element.108, bf16[32,1024]{1,0:T(8,128)(2,1)S(1)} %get-tuple-element.106), kind=kOutput, calls=%fused_computation.42 | convolution fusion | flops 405012480 | bytes 4849664 | tf_op jit(solution)/shard_map/dot_general | solution.py:132
  26.9 0.8 %convolution_add_fusion.8 = f32[96,1024]{1,0:T(8,128)S(1)} fusion(f32[96,1024]{1,0:T(8,128)S(1)} %fusion.3, bf16[2048,1024]{1,0:T(8,128)(2,1)S(1)} %get-tuple-element.45, bf16[32,1024]{1,0:T(8,128)(2,1)S(1)} %broadcast.4, bf16[32,1024]{1,0:T(8,128)(2,1)S(1)} %get-tuple-element.103, bf16[32,1024]{1,0:T(8,128)(2,1)S(1)} %get-tuple-element.104, ...), kind=kOutput, calls=%fused_computation.20 | convolution fusion | flops 405110784 | bytes 5242880 | tf_op jit(solution)/shard_map/dot_general | solution.py:132
  27.8 3.7 %collective-permute-done.9 = f32[32,1024]{1,0:T(8,128)S(1)} collective-permute-done((f32[32,1024]{1,0:T(8,128)S(1)}, f32[32,1024]{1,0:T(8,128)S(1)}, u32[]{:S(2)}, u32[]{:S(2)}) %collective-permute-start.9) | collective-permute-done | bytes 131104 | tf_op jit(solution)/shard_map/ppermute | solution.py:21
  31.5 0.8 %convolution_add_fusion.7 = f32[96,1024]{1,0:T(8,128)S(1)} fusion(f32[96,1024]{1,0:T(8,128)S(1)} %convolution_add_fusion.8, bf16[2048,1024]{1,0:T(8,128)(2,1)S(1)} %get-tuple-element.46, bf16[32,1024]{1,0:T(8,128)(2,1)S(1)} %broadcast.4, bf16[32,1024]{1,0:T(8,128)(2,1)S(1)} %get-tuple-element.99, bf16[32,1024]{1,0:T(8,128)(2,1)S(1)} %get-tuple-element.100, ...), kind=kOutput, calls=%fused_computation.19 | convolution fusion | flops 405110784 | bytes 5242880 | tf_op jit(solution)/shard_map/dot_general | solution.py:132
  32.8 0.8 %convolution_add_fusion.6 = f32[96,1024]{1,0:T(8,128)S(1)} fusion(f32[96,1024]{1,0:T(8,128)S(1)} %convolution_add_fusion.7, bf16[2048,1024]{1,0:T(8,128)(2,1)S(1)} %get-tuple-element.47, bf16[32,1024]{1,0:T(8,128)(2,1)S(1)} %broadcast.4, bf16[32,1024]{1,0:T(8,128)(2,1)S(1)} %get-tuple-element.95, bf16[32,1024]{1,0:T(8,128)(2,1)S(1)} %get-tuple-element.96, ...), kind=kOutput, calls=%fused_computation.18 | convolution fusion | flops 405110784 | bytes 5242880 | tf_op jit(solution)/shard_map/dot_general | solution.py:132
  34.8 0.8 %fusion.12 = f32[96,1024]{1,0:T(8,128)S(1)} fusion(bf16[2048,1024]{1,0:T(8,128)(2,1)S(1)} %get-tuple-element.44, bf16[32,1024]{1,0:T(8,128)(2,1)S(1)} %broadcast.4, bf16[32,1024]{1,0:T(8,128)(2,1)S(1)} %get-tuple-element.93, bf16[32,1024]{1,0:T(8,128)(2,1)S(1)} %get-tuple-element.92, bf16[32,1024]{1,0:T(8,128)(2,1)S(1)} %get-tuple-element.61), kind=kOutput, calls=%fused_computation.47 | convolution fusion | flops 405012480 | bytes 4849664 | tf_op jit(solution)/shard_map/dot_general | solution.py:132
  35.7 0.8 %convolution_add_fusion.5 = f32[96,1024]{1,0:T(8,128)S(1)} fusion(f32[96,1024]{1,0:T(8,128)S(1)} %fusion.12, bf16[2048,1024]{1,0:T(8,128)(2,1)S(1)} %get-tuple-element.45, bf16[32,1024]{1,0:T(8,128)(2,1)S(1)} %broadcast.4, bf16[32,1024]{1,0:T(8,128)(2,1)S(1)} %get-tuple-element.90, bf16[32,1024]{1,0:T(8,128)(2,1)S(1)} %get-tuple-element.91, ...), kind=kOutput, calls=%fused_computation.17 | convolution fusion | flops 405110784 | bytes 5242880 | tf_op jit(solution)/shard_map/dot_general | solution.py:132
  36.6 3.7 %collective-permute-done.12 = f32[32,1024]{1,0:T(8,128)S(1)} collective-permute-done((f32[32,1024]{1,0:T(8,128)S(1)}, f32[32,1024]{1,0:T(8,128)S(1)}, u32[]{:S(2)}, u32[]{:S(2)}) %collective-permute-start.12) | collective-permute-done | bytes 131104 | tf_op jit(solution)/shard_map/ppermute | solution.py:21
  40.4 1.0 %convolution_add_fusion.4 = f32[96,1024]{1,0:T(8,128)S(1)} fusion(f32[96,1024]{1,0:T(8,128)S(1)} %convolution_add_fusion.5, bf16[2048,1024]{1,0:T(8,128)(2,1)S(1)} %get-tuple-element.46, bf16[32,1024]{1,0:T(8,128)(2,1)S(1)} %broadcast.4, bf16[32,1024]{1,0:T(8,128)(2,1)S(1)} %get-tuple-element.87, bf16[32,1024]{1,0:T(8,128)(2,1)S(1)} %get-tuple-element.88, ...), kind=kOutput, calls=%fused_computation.16 | convolution fusion | flops 405110784 | bytes 5242880 | tf_op jit(solution)/shard_map/dot_general | solution.py:132
  41.7 0.8 %convolution_add_fusion.3 = f32[96,1024]{1,0:T(8,128)S(1)} fusion(f32[96,1024]{1,0:T(8,128)S(1)} %convolution_add_fusion.4, bf16[2048,1024]{1,0:T(8,128)(2,1)S(1)} %get-tuple-element.47, bf16[32,1024]{1,0:T(8,128)(2,1)S(1)} %broadcast.4, bf16[32,1024]{1,0:T(8,128)(2,1)S(1)} %get-tuple-element.84, bf16[32,1024]{1,0:T(8,128)(2,1)S(1)} %get-tuple-element.85, ...), kind=kOutput, calls=%fused_computation.15 | convolution fusion | flops 405110784 | bytes 5242880 | tf_op jit(solution)/shard_map/dot_general | solution.py:132
  43.9 0.8 %fusion.21 = f32[96,1024]{1,0:T(8,128)S(1)} fusion(bf16[2048,1024]{1,0:T(8,128)(2,1)S(1)} %get-tuple-element.44, bf16[32,1024]{1,0:T(8,128)(2,1)S(1)} %broadcast.4, bf16[32,1024]{1,0:T(8,128)(2,1)S(1)} %get-tuple-element.82, bf16[32,1024]{1,0:T(8,128)(2,1)S(1)} %get-tuple-element.81, bf16[32,1024]{1,0:T(8,128)(2,1)S(1)} %get-tuple-element.52), kind=kOutput, calls=%fused_computation.52 | convolution fusion | flops 405012480 | bytes 4849664 | tf_op jit(solution)/shard_map/dot_general | solution.py:132
  44.8 0.8 %convolution_add_fusion.2 = f32[96,1024]{1,0:T(8,128)S(1)} fusion(f32[96,1024]{1,0:T(8,128)S(1)} %fusion.21, bf16[2048,1024]{1,0:T(8,128)(2,1)S(1)} %get-tuple-element.45, bf16[32,1024]{1,0:T(8,128)(2,1)S(1)} %broadcast.4, bf16[32,1024]{1,0:T(8,128)(2,1)S(1)} %get-tuple-element.79, bf16[32,1024]{1,0:T(8,128)(2,1)S(1)} %get-tuple-element.80, ...), kind=kOutput, calls=%fused_computation.14 | convolution fusion | flops 405110784 | bytes 5242880 | tf_op jit(solution)/shard_map/dot_general | solution.py:132
  45.6 3.7 %collective-permute-done.15 = f32[32,1024]{1,0:T(8,128)S(1)} collective-permute-done((f32[32,1024]{1,0:T(8,128)S(1)}, f32[32,1024]{1,0:T(8,128)S(1)}, u32[]{:S(2)}, u32[]{:S(2)}) %collective-permute-start.15) | collective-permute-done | bytes 131104 | tf_op jit(solution)/shard_map/ppermute | solution.py:21
  49.4 0.8 %convolution_add_fusion.1 = f32[96,1024]{1,0:T(8,128)S(1)} fusion(f32[96,1024]{1,0:T(8,128)S(1)} %convolution_add_fusion.2, bf16[2048,1024]{1,0:T(8,128)(2,1)S(1)} %get-tuple-element.46, bf16[32,1024]{1,0:T(8,128)(2,1)S(1)} %broadcast.4, bf16[32,1024]{1,0:T(8,128)(2,1)S(1)} %get-tuple-element.76, bf16[32,1024]{1,0:T(8,128)(2,1)S(1)} %get-tuple-element.77, ...), kind=kOutput, calls=%fused_computation.13 | convolution fusion | flops 405110784 | bytes 5242880 | tf_op jit(solution)/shard_map/dot_general | solution.py:132
  50.8 0.8 %convolution_add_fusion = f32[96,1024]{1,0:T(8,128)S(1)} fusion(f32[96,1024]{1,0:T(8,128)S(1)} %convolution_add_fusion.1, bf16[2048,1024]{1,0:T(8,128)(2,1)S(1)} %get-tuple-element.47, bf16[32,1024]{1,0:T(8,128)(2,1)S(1)} %broadcast.4, bf16[32,1024]{1,0:T(8,128)(2,1)S(1)} %get-tuple-element.73, bf16[32,1024]{1,0:T(8,128)(2,1)S(1)} %get-tuple-element.74, ...), kind=kOutput, calls=%fused_computation.12 | convolution fusion | flops 405110784 | bytes 5242880 | tf_op jit(solution)/shard_map/dot_general | solution.py:132
  52.9 3.2 %collective-permute-done.17 = f32[32]{0:T(128)S(1)} collective-permute-done((f32[32]{0:T(128)S(1)}, f32[32]{0:T(128)S(1)}, u32[]{:S(2)}, u32[]{:S(2)}) %collective-permute-start.17) | collective-permute-done | bytes 160 | tf_op jit(solution)/shard_map/ppermute | solution.py:21
  56.1 1.1 %collective-permute-done.18 = f32[32]{0:T(128)S(1)} collective-permute-done((f32[32]{0:T(128)S(1)}, f32[32]{0:T(128)S(1)}, u32[]{:S(2)}, u32[]{:S(2)}) %collective-permute-start.18) | collective-permute-done | bytes 160 | tf_op jit(solution)/shard_map/ppermute | solution.py:21
  57.3 0.7 %fusion.163 = (f32[32,256]{1,0:T(8,128)}, f32[32,256]{1,0:T(8,128)}) fusion(f32[32,1024]{1,0:T(8,128)S(1)} %get-tuple-element.51, f32[32,4096]{1,0:T(8,128)S(1)} %get-tuple-element.56, f32[32]{0:T(128)S(1)} %add_divide_fusion, f32[32,4096]{1,0:T(8,128)S(1)} %multiply_add_fusion, f32[32,4096]{1,0:T(8,128)S(1)} %get-tuple-element.58, f32[32]{0:T(128)S(1)} %div.57, ...), kind=kLoop, calls=%fused_computation.248 | loop fusion | flops 73728 | bytes 262656 | tf_op jit(solution)/shard_map/sub | solution.py:215
  (81 shorter events, 8.5 us)
Async XLA Ops:
  1.4 7.9 %collective-permute-start = (f32[65,256]{1,0:T(8,128)S(1)}, f32[65,256]{1,0:T(8,128)S(1)}, u32[]{:S(2)}, u32[]{:S(2)}) collective-permute-start(f32[65,256]{1,0:T(8,128)S(1)} %pad_maximum_fusion.18.part_ref), channel_id=1, source_target_pairs={{0,8},{1,9},{2,10},{3,11},{4,12},{5,13},{6,14},{7,15},{8,0},{9,1},... | collective-permute-start | bytes 199688 | tf_op jit(solution)/shard_map/ppermute | solution.py:21
  6.3 8.4 %collective-permute-start.3 = (f32[64,256]{1,0:T(8,128)S(1)}, f32[64,256]{1,0:T(8,128)S(1)}, u32[]{:S(2)}, u32[]{:S(2)}) collective-permute-start(f32[64,256]{1,0:T(8,128)S(1)} %get-tuple-element.25), channel_id=1, source_target_pairs={{0,2},{1,3},{2,0},{3,1},{4,6},{5,7},{6,4},{7,5},{8,10},{9,11},{10,... | collective-permute-start | bytes 196616 | tf_op jit(solution)/shard_map/ppermute | solution.py:21
  9.4 5.2 %collective-permute-start.1 = (f32[65,512]{1,0:T(8,128)S(1)}, f32[65,512]{1,0:T(8,128)S(1)}, u32[]{:S(2)}, u32[]{:S(2)}) collective-permute-start(f32[65,512]{1,0:T(8,128)S(1)} %pad_maximum_fusion.17), channel_id=1, source_target_pairs={{0,4},{1,5},{2,6},{3,7},{4,0},{5,1},{6,2},{7,3},{8,12},{9,13},{10,... | collective-permute-start | bytes 399368 | tf_op jit(solution)/shard_map/ppermute | solution.py:21
  10.2 4.5 %collective-permute-start.4 = (f32[64,256]{1,0:T(8,128)S(1)}, f32[64,256]{1,0:T(8,128)S(1)}, u32[]{:S(2)}, u32[]{:S(2)}) collective-permute-start(f32[64,256]{1,0:T(8,128)S(1)} %get-tuple-element.26), channel_id=1, source_target_pairs={{0,2},{1,3},{2,0},{3,1},{4,6},{5,7},{6,4},{7,5},{8,10},{9,11},{10,... | collective-permute-start | bytes 196616 | tf_op jit(solution)/shard_map/ppermute | solution.py:21
  14.8 4.3 %collective-permute-start.6 = (f32[64,512]{1,0:T(8,128)S(1)}, f32[64,512]{1,0:T(8,128)S(1)}, u32[]{:S(2)}, u32[]{:S(2)}) collective-permute-start(f32[64,512]{1,0:T(8,128)S(1)} %constant_dynamic-update-slice_fusion.3), channel_id=1, source_target_pairs={{0,1},{1,0},{2,3},{3,2},{4,5},{5,4},{6,7},{7,6},{8,9},{9,8},{10,11... | collective-permute-start | bytes 393224 | tf_op jit(solution)/shard_map/ppermute | solution.py:21
  14.9 4.2 %collective-permute-start.2 = (f32[64,1024]{1,0:T(8,128)S(1)}, f32[64,1024]{1,0:T(8,128)S(1)}, u32[]{:S(2)}, u32[]{:S(2)}) collective-permute-start(f32[64,1024]{1,0:T(8,128)S(1)} %constant_dynamic-update-slice_fusion), channel_id=1, source_target_pairs={{0,1},{1,0},{2,3},{3,2},{4,5},{5,4},{6,7},{7,6},{8,9},{9,8},{10,11... | collective-permute-start | bytes 786440 | tf_op jit(solution)/shard_map/ppermute | solution.py:21
  15.5 7.5 %collective-permute-start.5 = (f32[64,512]{1,0:T(8,128)S(1)}, f32[64,512]{1,0:T(8,128)S(1)}, u32[]{:S(2)}, u32[]{:S(2)}) collective-permute-start(f32[64,512]{1,0:T(8,128)S(1)} %get-tuple-element.30), channel_id=1, source_target_pairs={{0,2},{1,3},{2,0},{3,1},{4,6},{5,7},{6,4},{7,5},{8,10},{9,11},{10,... | collective-permute-start | bytes 393224 | tf_op jit(solution)/shard_map/ppermute | solution.py:21
  22.9 1.4 %collective-permute-start.7 = (f32[64,512]{1,0:T(8,128)S(1)}, f32[64,512]{1,0:T(8,128)S(1)}, u32[]{:S(2)}, u32[]{:S(2)}) collective-permute-start(f32[64,512]{1,0:T(8,128)S(1)} %collective-permute-done.5), channel_id=1, source_target_pairs={{0,1},{1,0},{2,3},{3,2},{4,5},{5,4},{6,7},{7,6},{8,9},{9,8},{10,11... | collective-permute-start | bytes 393224 | tf_op jit(solution)/shard_map/ppermute | solution.py:21
  25.5 1.4 %collective-permute-start.8 = (f32[32,1024]{1,0:T(8,128)S(1)}, f32[32,1024]{1,0:T(8,128)S(1)}, u32[]{:S(2)}, u32[]{:S(2)}) collective-permute-start(f32[32,1024]{1,0:T(8,128)S(1)} %get-tuple-element.43), channel_id=1, source_target_pairs={{0,1},{1,0},{2,3},{3,2},{4,5},{5,4},{6,7},{7,6},{8,9},{9,8},{10,11... | collective-permute-start | bytes 393224 | tf_op jit(solution)/shard_map/ppermute | solution.py:21
  25.8 5.7 %collective-permute-start.9 = (f32[32,1024]{1,0:T(8,128)S(1)}, f32[32,1024]{1,0:T(8,128)S(1)}, u32[]{:S(2)}, u32[]{:S(2)}) collective-permute-start(f32[32,1024]{1,0:T(8,128)S(1)} %get-tuple-element.43), channel_id=1, source_target_pairs={{0,2},{1,3},{2,0},{3,1},{4,6},{5,7},{6,4},{7,5},{8,10},{9,11},{10,... | collective-permute-start | bytes 393224 | tf_op jit(solution)/shard_map/ppermute | solution.py:21
  31.4 1.3 %collective-permute-start.10 = (f32[32,1024]{1,0:T(8,128)S(1)}, f32[32,1024]{1,0:T(8,128)S(1)}, u32[]{:S(2)}, u32[]{:S(2)}) collective-permute-start(f32[32,1024]{1,0:T(8,128)S(1)} %collective-permute-done.9), channel_id=1, source_target_pairs={{0,1},{1,0},{2,3},{3,2},{4,5},{5,4},{6,7},{7,6},{8,9},{9,8},{10,11... | collective-permute-start | bytes 393224 | tf_op jit(solution)/shard_map/ppermute | solution.py:21
  34.3 1.4 %collective-permute-start.11 = (f32[32,1024]{1,0:T(8,128)S(1)}, f32[32,1024]{1,0:T(8,128)S(1)}, u32[]{:S(2)}, u32[]{:S(2)}) collective-permute-start(f32[32,1024]{1,0:T(8,128)S(1)} %get-tuple-element.62), channel_id=1, source_target_pairs={{0,1},{1,0},{2,3},{3,2},{4,5},{5,4},{6,7},{7,6},{8,9},{9,8},{10,11... | collective-permute-start | bytes 393224 | tf_op jit(solution)/shard_map/ppermute | solution.py:21
  34.5 5.8 %collective-permute-start.12 = (f32[32,1024]{1,0:T(8,128)S(1)}, f32[32,1024]{1,0:T(8,128)S(1)}, u32[]{:S(2)}, u32[]{:S(2)}) collective-permute-start(f32[32,1024]{1,0:T(8,128)S(1)} %get-tuple-element.62), channel_id=1, source_target_pairs={{0,2},{1,3},{2,0},{3,1},{4,6},{5,7},{6,4},{7,5},{8,10},{9,11},{10,... | collective-permute-start | bytes 393224 | tf_op jit(solution)/shard_map/ppermute | solution.py:21
  40.3 1.4 %collective-permute-start.13 = (f32[32,1024]{1,0:T(8,128)S(1)}, f32[32,1024]{1,0:T(8,128)S(1)}, u32[]{:S(2)}, u32[]{:S(2)}) collective-permute-start(f32[32,1024]{1,0:T(8,128)S(1)} %collective-permute-done.12), channel_id=1, source_target_pairs={{0,1},{1,0},{2,3},{3,2},{4,5},{5,4},{6,7},{7,6},{8,9},{9,8},{10,11... | collective-permute-start | bytes 393224 | tf_op jit(solution)/shard_map/ppermute | solution.py:21
  43.4 1.4 %collective-permute-start.14 = (f32[32,1024]{1,0:T(8,128)S(1)}, f32[32,1024]{1,0:T(8,128)S(1)}, u32[]{:S(2)}, u32[]{:S(2)}) collective-permute-start(f32[32,1024]{1,0:T(8,128)S(1)} %get-tuple-element.53), channel_id=1, source_target_pairs={{0,1},{1,0},{2,3},{3,2},{4,5},{5,4},{6,7},{7,6},{8,9},{9,8},{10,11... | collective-permute-start | bytes 393224 | tf_op jit(solution)/shard_map/ppermute | solution.py:21
  43.6 5.7 %collective-permute-start.15 = (f32[32,1024]{1,0:T(8,128)S(1)}, f32[32,1024]{1,0:T(8,128)S(1)}, u32[]{:S(2)}, u32[]{:S(2)}) collective-permute-start(f32[32,1024]{1,0:T(8,128)S(1)} %get-tuple-element.53), channel_id=1, source_target_pairs={{0,2},{1,3},{2,0},{3,1},{4,6},{5,7},{6,4},{7,5},{8,10},{9,11},{10,... | collective-permute-start | bytes 393224 | tf_op jit(solution)/shard_map/ppermute | solution.py:21
  49.4 1.4 %collective-permute-start.16 = (f32[32,1024]{1,0:T(8,128)S(1)}, f32[32,1024]{1,0:T(8,128)S(1)}, u32[]{:S(2)}, u32[]{:S(2)}) collective-permute-start(f32[32,1024]{1,0:T(8,128)S(1)} %collective-permute-done.15), channel_id=1, source_target_pairs={{0,1},{1,0},{2,3},{3,2},{4,5},{5,4},{6,7},{7,6},{8,9},{9,8},{10,11... | collective-permute-start | bytes 393224 | tf_op jit(solution)/shard_map/ppermute | solution.py:21
  52.5 3.6 %collective-permute-start.17 = (f32[32]{0:T(128)S(1)}, f32[32]{0:T(128)S(1)}, u32[]{:S(2)}, u32[]{:S(2)}) collective-permute-start(f32[32]{0:T(128)S(1)} %get-tuple-element.50), channel_id=1, source_target_pairs={{0,2},{1,3},{2,0},{3,1},{4,6},{5,7},{6,4},{7,5},{8,10},{9,11},{10,... | collective-permute-start | bytes 392 | tf_op jit(solution)/shard_map/ppermute | solution.py:21
  56.1 1.1 %collective-permute-start.18 = (f32[32]{0:T(128)S(1)}, f32[32]{0:T(128)S(1)}, u32[]{:S(2)}, u32[]{:S(2)}) collective-permute-start(f32[32]{0:T(128)S(1)} %add.113), channel_id=1, source_target_pairs={{0,1},{1,0},{2,3},{3,2},{4,5},{5,4},{6,7},{7,6},{8,9},{9,8},{10,11... | collective-permute-start | bytes 392 | tf_op jit(solution)/shard_map/ppermute | solution.py:21

commit v11 on v9

--- a/solution.py
+++ b/solution.py
@@ -8,7 +8,7 @@
 from jax.sharding import PartitionSpec as P
 
 ITERS = 4
-TILE_BYTES = 16 << 20
+TILE_BYTES = 32 << 20
 VMEM_BYTES = 16 << 20
 NORM_ROWS = 64
 BUILD_ROWS = 1024
@@ -107,11 +107,25 @@
     return call(build_kernel, outs, rows, vectors, scale, right, total, **cost)
 
 
-def apply_piece(vectors, piece):
-    high, mid, low = split(vectors, 3)
-    left = jnp.concatenate([high, mid, low], axis=0)
-    right = jnp.concatenate([high, mid, jnp.zeros_like(low)], axis=0)
-    return jnp.dot(jnp.concatenate([left, right], axis=1), piece, preferred_element_type=jnp.float32)
+def parts_of(vectors):
+    return jnp.concatenate(split(vectors, 3), axis=0)
+
+
+def apply_piece(parts, piece):
+    probes = parts.shape[0] // 3
+    right = jnp.where(lax.broadcasted_iota(jnp.int32, parts.shape, 0) < 2 * probes, parts, 0)
+    return jnp.dot(jnp.concatenate([parts, right], axis=1), piece, preferred_element_type=jnp.float32)
+
+
+def apply_transposed(parts, piece):
+    both = lax.dot_general(parts, piece, (((1,), (1,)), ((), ())), preferred_element_type=jnp.float32)
+    half = both.shape[1] // 2
+    return both[:, :half] + both[:, half:]
+
+
+def collect(total):
+    probes = total.shape[0] // 3
+    return total[:probes] + (total[probes : 2 * probes] + total[2 * probes :])
 
 
 def solution(mesh):
@@ -120,71 +134,97 @@
 
     def body(points, lengthscale, noise_var, targets):
         feats, width = points.shape
-        probes = targets.shape[0]
-        team = min(n, 4)
+        team = min(n, 2)
         while team < n and (n * width) * (n * width) // team * 4 > TILE_BYTES:
             team *= 2
         outer, inner = [s for s in strides if s >= team], [s for s in strides if s < team]
 
-        def arrivals(x):
-            pieces, sent = [x, swap(x, n, 1)], [x]
+        def others(own):
+            if len(inner) == 1:
+                return [swap(x, n, 1) for x in own]
+            sent = list(own)
+            pieces = [swap(x, n, 1) for x in own]
             for stride in inner[:-1]:
                 came = swap(sent[0] if len(sent) == 1 else jnp.concatenate(sent, axis=1), n, stride)
                 sent.append(came)
                 pieces += [came, swap(came, n, 1)]
             return pieces
 
+        scale = (POINT_SCALE / lengthscale)[:, None]
         mine = lax.optimization_barrier(jnp.concatenate([points, targets, noise_var[None, :]], axis=0))
-        for stride in outer:
+        for stride in outer[:-1]:
             mine = jnp.concatenate([mine, swap(mine, n, stride)], axis=1)
-        noise = mine[-1:]
-        scale = (POINT_SCALE / lengthscale)[:, None]
-        first = arrivals(mine[:-1])
-        cols = noise.shape[1]
-        right = call(
-            scaled_operand_kernel,
-            jax.ShapeDtypeStruct((6 * feats + NORM_ROWS, cols), jnp.bfloat16),
-            mine[:feats],
-            scale,
-            flops=feats * cols,
-            bytes_accessed=feats * cols,
-            transcendentals=0,
-        )
-        starts = [x[feats:] for x in first]
-        tile = []
-        my_applied = noise * starts[0]
-        for x, start in zip(first, starts):
-            piece, my_applied = build_piece(x[:feats], start, scale, right, my_applied)
-            tile.append(piece)
-
-        def operator(pieces):
-            total = apply_piece(pieces[0], tile[0])
-            for x, piece in zip(pieces[1:], tile[1:]):
-                total = lax.optimization_barrier(total + apply_piece(x, piece))
-            return total[:probes] + (total[probes : 2 * probes] + total[2 * probes :]) + noise * pieces[0]
-
-        residual = direction = jnp.concatenate(starts, axis=1)
+        groups = [mine] + [swap(mine, n, stride) for stride in outer[-1:]]
+        noise = [x[-1:] for x in groups]
+        own = [x[:-1] for x in groups]
+        rest = others(own)
+        rights = [
+            call(
+                scaled_operand_kernel,
+                jax.ShapeDtypeStruct((6 * feats + NORM_ROWS, x.shape[1]), jnp.bfloat16),
+                x[:feats],
+                scale,
+                flops=feats * x.shape[1],
+                bytes_accessed=feats * x.shape[1],
+                transcendentals=0,
+            )
+            for x in own
+        ]
+        my_applied = [a * x[feats:] for a, x in zip(noise, own)]
+        tile = {}
+
+        def build(rows, name, j):
+            tile[name, j], my_applied[j] = build_piece(rows[:feats], rows[feats:], scale, rights[j], my_applied[j])
+
+        build(own[0], 0, 0)
+        build(rest[0], 2, 0)
+        if len(own) == 2:
+            build(own[1], 1, 0)
+            my_applied[1] += collect(apply_transposed(parts_of(own[0][feats:]), tile[1, 0]))
+            build(own[1], 1, 1)
+            build(rest[0], 2, 1)
+        for k in range(1, len(rest)):
+            for j in range(len(own)):
+                build(rest[k], 2 + k, j)
+
+        def operator(own, rest):
+            left = [parts_of(x) for x in own]
+            totals = [apply_piece(left[0], tile[0, 0])]
+            if len(own) == 2:
+                totals[0] += apply_piece(left[1], tile[1, 0])
+                totals.append(apply_transposed(left[0], tile[1, 0]) + apply_piece(left[1], tile[1, 1]))
+            totals, rest = lax.optimization_barrier((totals, rest))
+            for k, x in enumerate(rest):
+                totals = lax.optimization_barrier(totals) if k else totals
+                left = parts_of(x)
+                totals = [total + apply_piece(left, tile[2 + k, j]) for j, total in enumerate(totals)]
+            return [collect(total) + a * x for total, a, x in zip(totals, noise, own)], rest
+
+        def whole(own, rest):
+            return jnp.concatenate([*own, *rest], axis=1)
+
+        residual = direction = whole(own, rest)[feats:]
+        cols = sum(x.shape[1] for x in own)
         my_solution = jnp.zeros_like(direction[:, :width])
         norm_now = jnp.sum(residual * residual, axis=1)
         my_image = my_applied
         for iteration in range(ITERS - 1):
-            pieces = arrivals(my_applied)
-            my_next = operator(pieces)
-            applied = jnp.concatenate(pieces, axis=1)
+            my_next, came = operator(my_applied, others(my_applied))
+            applied = whole(my_applied, came)
             curve = jnp.sum(direction * applied, axis=1)
             step_size = (norm_now / curve)[:, None]
             my_solution = my_solution + step_size * direction[:, :width]
             residual = residual - step_size * applied
             norm_next = jnp.sum(residual * residual, axis=1)
             ratio = (norm_next / norm_now)[:, None]
-            my_image = my_image - step_size * my_next
-            my_applied = my_image + ratio * my_applied
+            my_image = [x - step_size * y for x, y in zip(my_image, my_next)]
+            my_applied = [x + ratio * y for x, y in zip(my_image, my_applied)]
             direction = residual + ratio * direction
             norm_now = norm_next
-        curve = add_up(jnp.sum(direction[:, :cols] * my_applied, axis=1), n, inner)
+        curve = add_up(jnp.sum(direction[:, :cols] * jnp.concatenate(my_applied, axis=1), axis=1), n, inner)
         step_size = (norm_now / curve)[:, None]
         my_solution = my_solution + step_size * direction[:, :width]
-        return my_solution, residual[:, :width] - step_size * my_applied[:, :width]
+        return my_solution, residual[:, :width] - step_size * my_applied[0][:, :width]
 
     in_specs = (P("groups", "blk"), P("groups"), P(("groups", "blk")), P("groups", "blk"))
     out_specs = (P("groups", "blk"), P("groups", "blk"))

time: 56.5 us -> 62.5 us (1.11)
  matrix products: 9.83 us -> 23.1 us
  waiting for transfers between devices: 19.7 us -> 9.72 us
  Pallas kernels: 6.97 us -> 12.5 us
  starting transfers between devices: 13.9 us -> 9.13 us
  other arithmetic: 4.77 us -> 6.12 us
    dot_general x12 -> x25, matrix products: 9.83 us -> 23.1 us  [the longest x21 17.4 us: apply_piece(): jnp.dot(jnp.concatenate([parts, right], axis=1), piece, preferred_element...]
    ppermute x16 -> x12, waiting for transfers between devices: 19.7 us -> 9.72 us  [swap(): return lax.ppermute(x, 'blk', [(i, i ^ stride) for i in range(n)])]
    pallas_call x5 -> x9, Pallas kernels: 6.97 us -> 12.5 us  [call(): pl.pallas_call(kernel, out_shape=outs, in_specs=[whole] * len(args), out_...]
    ppermute x16 -> x12, starting transfers between devices: 13.9 us -> 9.13 us  [swap(): return lax.ppermute(x, 'blk', [(i, i ^ stride) for i in range(n)])]
    select_n x0 -> x6, other arithmetic: none -> 0.83 us  [apply_piece(): jnp.where(lax.broadcasted_iota(jnp.int32, parts.shape, 0) < 2 * probes, p...]
  transfers between devices with their start and end apart: 16 -> 12, of which waited for: 14 -> 4; matrix products, arithmetic and copies ran while one was open for 15% -> 23% of each run, Pallas kernels for 9% -> 17%
where the time goes in v11:
time: 62.5 us; the launch traced here: 61.8 us
  matrix products  23.1 us (37%)
  Pallas kernels  12.5 us (20%)
  waiting for transfers between devices  9.72 us (16%)
  starting transfers between devices  9.13 us (15%)
  other arithmetic  6.12 us (10%)
  between operations  1.05 us (2%)
    dot_general x21, matrix products, apply_piece(): jnp.dot(jnp.concatenate([parts, right], axis=1), piece, preferred_element...  17.4 us
    pallas_call x9, Pallas kernels, call(): pl.pallas_call(kernel, out_shape=outs, in_specs=[whole] * len(args), out_...  12.5 us
    ppermute x12, waiting for transfers between devices, swap(): return lax.ppermute(x, 'blk', [(i, i ^ stride) for i in range(n)])  9.72 us
    ppermute x12, starting transfers between devices, swap(): return lax.ppermute(x, 'blk', [(i, i ^ stride) for i in range(n)])  9.13 us
    dot_general x4, matrix products, apply_transposed(): lax.dot_general(parts, piece, (((1,), (1,)), ((), ())), preferred_element...  5.66 us
  transfers between devices with their start and end apart: 12, of which 4 were waited for; matrix products, arithmetic and copies ran while one was open for 23% of the time, Pallas kernels for 17%

profile of v11, /device:TPU:0, one launch (start us, length us, event | category | flops | bytes accessed | tf_op | source)
XLA Modules:
  0.0 61.8 jit_solution(14654627882793360166)
XLA Ops:
  1.4 4.0 %collective-permute-start = (f32[65,256]{1,0:T(8,128)S(1)}, f32[65,256]{1,0:T(8,128)S(1)}, u32[]{:S(2)}, u32[]{:S(2)}) collective-permute-start(f32[65,256]{1,0:T(8,128)S(1)} %pad_maximum_fusion.22), channel_id=1, source_target_pairs={{0,8},{1,9},{2,10},{3,11},{4,12},{5,13},{6,14},{7,15},{8,0},{9,1},... | collective-permute-start | bytes 199688 | tf_op jit(solution)/shard_map/ppermute | solution.py:19
  5.5 3.9 %collective-permute-done = f32[65,256]{1,0:T(8,128)S(1)} collective-permute-done((f32[65,256]{1,0:T(8,128)S(1)}, f32[65,256]{1,0:T(8,128)S(1)}, u32[]{:S(2)}, u32[]{:S(2)}) %collective-permute-start) | collective-permute-done | bytes 66592 | tf_op jit(solution)/shard_map/ppermute | solution.py:19
  10.9 3.7 %collective-permute-done.1 = f32[65,512]{1,0:T(8,128)S(1)} collective-permute-done((f32[65,512]{1,0:T(8,128)S(1)}, f32[65,512]{1,0:T(8,128)S(1)}, u32[]{:S(2)}, u32[]{:S(2)}) %collective-permute-start.1) | collective-permute-done | bytes 133152 | tf_op jit(solution)/shard_map/ppermute | solution.py:19
  14.6 1.8 %collective-permute-start.2 = (f32[65,1024]{1,0:T(8,128)S(1)}, f32[65,1024]{1,0:T(8,128)S(1)}, u32[]{:S(2)}, u32[]{:S(2)}) collective-permute-start(f32[65,1024]{1,0:T(8,128)S(1)} %pad_maximum_fusion.14), channel_id=1, source_target_pairs={{0,2},{1,3},{2,0},{3,1},{4,6},{5,7},{6,4},{7,5},{8,10},{9,11},{10,... | collective-permute-start | bytes 798728 | tf_op jit(solution)/shard_map/ppermute | solution.py:19
  16.7 1.7 %shard_map.60 = (bf16[2048,1024]{1,0:T(8,128)(2,1)S(1)}, f32[32,1024]{1,0:T(8,128)S(1)}) custom-call(f32[32,1024]{1,0:T(8,128)S(1)} %get-tuple-element.94.mine_ref.rows_ref, f32[32,1024]{1,0:T(8,128)S(1)} %get-tuple-element.93.vectors_ref, f32[32,1]{1,0:T(8,128)S(1)} %copy.10.scale_ref, bf16[256,1024]{1,0:T(8,128)(2,1)S(1)} %shard_map.59.right_ref, ...), custom_call_target="tpu_custom_call" | custom-call | flops 872415232 | bytes 4194304 | tf_op jit(solution)/shard_map/pallas_call | solution.py:93
  18.5 1.7 %shard_map.61 = (bf16[2048,1024]{1,0:T(8,128)(2,1)S(1)}, f32[32,1024]{1,0:T(8,128)S(1)}) custom-call(f32[32,1024]{1,0:T(8,128)S(1)} %get-tuple-element.98.rows_ref, f32[32,1024]{1,0:T(8,128)S(1)} %get-tuple-element.97.vectors_ref, f32[32,1]{1,0:T(8,128)S(1)} %copy.10.scale_ref, bf16[256,1024]{1,0:T(8,128)(2,1)S(1)} %shard_map.59.right_ref, ...), custom_call_target="tpu_custom_call" | custom-call | flops 872415232 | bytes 4194304 | tf_op jit(solution)/shard_map/pallas_call | solution.py:93
  20.2 1.2 %collective-permute-done.2 = f32[65,1024]{1,0:T(8,128)S(1)} collective-permute-done((f32[65,1024]{1,0:T(8,128)S(1)}, f32[65,1024]{1,0:T(8,128)S(1)}, u32[]{:S(2)}, u32[]{:S(2)}) %collective-permute-start.2) | collective-permute-done | bytes 266272 | tf_op jit(solution)/shard_map/ppermute | solution.py:19
  21.5 1.7 %shard_map.62 = (bf16[2048,1024]{1,0:T(8,128)(2,1)S(1)}, f32[32,1024]{1,0:T(8,128)S(1)}) custom-call(f32[32,1024]{1,0:T(8,128)S(1)} %get-tuple-element.96.rows_ref.mine_ref, f32[32,1024]{1,0:T(8,128)S(1)} %get-tuple-element.95.vectors_ref, f32[32,1]{1,0:T(8,128)S(1)} %copy.10.scale_ref, bf16[256,1024]{1,0:T(8,128)(2,1)S(1)} %shard_map.59.right_ref, ...), custom_call_target="tpu_custom_call" | custom-call | flops 872415232 | bytes 4194304 | tf_op jit(solution)/shard_map/pallas_call | solution.py:93
  23.2 1.4 %fusion.25 = f32[96,2048]{1,0:T(8,128)S(1)} fusion(bf16[2048,1024]{1,0:T(8,128)(2,1)S(1)} %get-tuple-element.38, bf16[32,1024]{1,0:T(8,128)(2,1)S(1)} %get-tuple-element.92, bf16[32,1024]{1,0:T(8,128)(2,1)S(1)} %get-tuple-element.91, bf16[32,1024]{1,0:T(8,128)(2,1)S(1)} %get-tuple-element.89), kind=kOutput, calls=%fused_computation.70 | convolution fusion | flops 403243008 | bytes 5177344 | tf_op jit(solution)/shard_map/dot_general | solution.py:121
  24.9 1.7 %shard_map.65 = (bf16[2048,1024]{1,0:T(8,128)(2,1)S(1)}, f32[32,1024]{1,0:T(8,128)S(1)}) custom-call(f32[32,1024]{1,0:T(8,128)S(1)} %get-tuple-element.96.rows_ref.mine_ref, f32[32,1024]{1,0:T(8,128)S(1)} %get-tuple-element.95.vectors_ref, f32[32,1]{1,0:T(8,128)S(1)} %copy.10.scale_ref, bf16[256,1024]{1,0:T(8,128)(2,1)S(1)} %shard_map.64.right_ref, ...), custom_call_target="tpu_custom_call" | custom-call | flops 872415232 | bytes 4194304 | tf_op jit(solution)/shard_map/pallas_call | solution.py:93
  26.6 1.7 %shard_map.66 = (bf16[2048,1024]{1,0:T(8,128)(2,1)S(1)}, f32[32,1024]{1,0:T(8,128)S(1)}) custom-call(f32[32,1024]{1,0:T(8,128)S(1)} %get-tuple-element.98.rows_ref, f32[32,1024]{1,0:T(8,128)S(1)} %get-tuple-element.97.vectors_ref, f32[32,1]{1,0:T(8,128)S(1)} %copy.10.scale_ref, bf16[256,1024]{1,0:T(8,128)(2,1)S(1)} %shard_map.64.right_ref, ...), custom_call_target="tpu_custom_call" | custom-call | flops 872415232 | bytes 4194304 | tf_op jit(solution)/shard_map/pallas_call | solution.py:93
  28.4 1.7 %shard_map.63 = (bf16[2048,1024]{1,0:T(8,128)(2,1)S(1)}, f32[32,1024]{1,0:T(8,128)S(1)}) custom-call(f32[32,1024]{1,0:T(8,128)S(1)} %get-tuple-element.100.rows_ref, f32[32,1024]{1,0:T(8,128)S(1)} %get-tuple-element.99.vectors_ref, f32[32,1]{1,0:T(8,128)S(1)} %copy.10.scale_ref, bf16[256,1024]{1,0:T(8,128)(2,1)S(1)} %shard_map.59.right_ref, ...), custom_call_target="tpu_custom_call" | custom-call | flops 872415232 | bytes 4194304 | tf_op jit(solution)/shard_map/pallas_call | solution.py:93
  30.8 1.9 %shard_map.67 = (bf16[2048,1024]{1,0:T(8,128)(2,1)S(1)}, f32[32,1024]{1,0:T(8,128)S(1)}) custom-call(f32[32,1024]{1,0:T(8,128)S(1)} %get-tuple-element.100.rows_ref, f32[32,1024]{1,0:T(8,128)S(1)} %get-tuple-element.99.vectors_ref, f32[32,1]{1,0:T(8,128)S(1)} %copy.10.scale_ref, bf16[256,1024]{1,0:T(8,128)(2,1)S(1)} %shard_map.64.right_ref, ...), custom_call_target="tpu_custom_call" | custom-call | flops 872415232 | bytes 4194304 | tf_op jit(solution)/shard_map/pallas_call | solution.py:93
  32.7 1.4 %fusion.87 = f32[96,2048]{1,0:T(8,128)S(1)} fusion(bf16[2048,1024]{1,0:T(8,128)(2,1)S(1)} %get-tuple-element.38, bf16[32,1024]{1,0:T(8,128)(2,1)S(1)} %get-tuple-element.134, bf16[32,1024]{1,0:T(8,128)(2,1)S(1)} %get-tuple-element.136, bf16[32,1024]{1,0:T(8,128)(2,1)S(1)} %get-tuple-element.133), kind=kOutput, calls=%fused_computation.211 | convolution fusion | flops 403243008 | bytes 5177344 | tf_op jit(solution)/shard_map/dot_general | solution.py:121
  34.3 0.8 %fusion = f32[96,1024]{1,0:T(8,128)S(1)} fusion(bf16[2048,1024]{1,0:T(8,128)(2,1)S(1)} %get-tuple-element.42, bf16[96,1024]{1,0:T(8,128)(2,1)S(1)} %get-tuple-element.158, bf16[32,1024]{1,0:T(8,128)(2,1)S(1)} %get-tuple-element.134, bf16[32,1024]{1,0:T(8,128)(2,1)S(1)} %get-tuple-element.136, bf16[32,1024]{1,0:T(8,128)(2,1)S(1)} %get-tuple-element.133), kind=kOutput, calls=%fused_computation.34 | convolution fusion | flops 404226048 | bytes 4980736 | tf_op jit(solution)/shard_map/dot_general | solution.py:117
  35.1 0.8 %convolution_add_fusion.10 = f32[96,1024]{1,0:T(8,128)S(1)} fusion(bf16[2048,1024]{1,0:T(8,128)(2,1)S(1)} %get-tuple-element.43, f32[96,2048]{1,0:T(8,128)S(1)} %fusion.87, bf16[96,1024]{1,0:T(8,128)(2,1)S(1)} %get-tuple-element.157, bf16[32,1024]{1,0:T(8,128)(2,1)S(1)} %get-tuple-element.130, bf16[32,1024]{1,0:T(8,128)(2,1)S(1)} %get-tuple-element.132, ...), kind=kOutput, calls=%fused_computation.10 | convolution fusion | flops 404422656 | bytes 5767168 | tf_op jit(solution)/shard_map/dot_general | solution.py:117
  35.9 0.8 %convolution_add_fusion.11 = f32[96,1024]{1,0:T(8,128)S(1)} fusion(f32[96,1024]{1,0:T(8,128)S(1)} %fusion, bf16[2048,1024]{1,0:T(8,128)(2,1)S(1)} %get-tuple-element.38, bf16[96,1024]{1,0:T(8,128)(2,1)S(1)} %get-tuple-element.157, bf16[32,1024]{1,0:T(8,128)(2,1)S(1)} %get-tuple-element.130, bf16[32,1024]{1,0:T(8,128)(2,1)S(1)} %get-tuple-element.132, ...), kind=kOutput, calls=%fused_computation.11 | convolution fusion | flops 404324352 | bytes 5373952 | tf_op jit(solution)/shard_map/dot_general | solution.py:117
  37.5 0.8 %fusion.93 = f32[96,1024]{1,0:T(8,128)S(1)} fusion(bf16[2048,1024]{1,0:T(8,128)(2,1)S(1)} %get-tuple-element.47, bf16[96,1024]{1,0:T(8,128)(2,1)S(1)} %get-tuple-element.156, bf16[32,1024]{1,0:T(8,128)(2,1)S(1)} %get-tuple-element.126, bf16[32,1024]{1,0:T(8,128)(2,1)S(1)} %get-tuple-element.127, bf16[32,1024]{1,0:T(8,128)(2,1)S(1)} %get-tuple-element.125), kind=kOutput, calls=%fused_computation.218 | convolution fusion | flops 404226048 | bytes 4980736 | tf_op jit(solution)/shard_map/dot_general | solution.py:117
  38.3 0.8 %fusion.92 = f32[96,1024]{1,0:T(8,128)S(1)} fusion(bf16[2048,1024]{1,0:T(8,128)(2,1)S(1)} %get-tuple-element.49, bf16[96,1024]{1,0:T(8,128)(2,1)S(1)} %get-tuple-element.156, bf16[32,1024]{1,0:T(8,128)(2,1)S(1)} %get-tuple-element.126, bf16[32,1024]{1,0:T(8,128)(2,1)S(1)} %get-tuple-element.127, bf16[32,1024]{1,0:T(8,128)(2,1)S(1)} %get-tuple-element.125), kind=kOutput, calls=%fused_computation.217 | convolution fusion | flops 404226048 | bytes 4980736 | tf_op jit(solution)/shard_map/dot_general | solution.py:117
  39.3 0.8 %convolution_add_fusion.8 = f32[96,1024]{1,0:T(8,128)S(1)} fusion(f32[96,1024]{1,0:T(8,128)S(1)} %add.177, bf16[2048,1024]{1,0:T(8,128)(2,1)S(1)} %get-tuple-element.53, bf16[96,1024]{1,0:T(8,128)(2,1)S(1)} %get-tuple-element.155, bf16[32,1024]{1,0:T(8,128)(2,1)S(1)} %get-tuple-element.122, bf16[32,1024]{1,0:T(8,128)(2,1)S(1)} %get-tuple-element.123, ...), kind=kOutput, calls=%fused_computation.8 | convolution fusion | flops 404324352 | bytes 5373952 | tf_op jit(solution)/shard_map/dot_general | solution.py:117
  40.1 0.8 %convolution_add_fusion.9 = f32[96,1024]{1,0:T(8,128)S(1)} fusion(f32[96,1024]{1,0:T(8,128)S(1)} %add.176, bf16[2048,1024]{1,0:T(8,128)(2,1)S(1)} %get-tuple-element.51, bf16[96,1024]{1,0:T(8,128)(2,1)S(1)} %get-tuple-element.155, bf16[32,1024]{1,0:T(8,128)(2,1)S(1)} %get-tuple-element.122, bf16[32,1024]{1,0:T(8,128)(2,1)S(1)} %get-tuple-element.123, ...), kind=kOutput, calls=%fused_computation.9 | convolution fusion | flops 404324352 | bytes 5373952 | tf_op jit(solution)/shard_map/dot_general | solution.py:117
  41.8 1.4 %fusion.86 = f32[96,2048]{1,0:T(8,128)S(1)} fusion(bf16[2048,1024]{1,0:T(8,128)(2,1)S(1)} %get-tuple-element.38, bf16[32,1024]{1,0:T(8,128)(2,1)S(1)} %get-tuple-element.159, bf16[32,1024]{1,0:T(8,128)(2,1)S(1)} %get-tuple-element.160, bf16[32,1024]{1,0:T(8,128)(2,1)S(1)} %get-tuple-element.142), kind=kOutput, calls=%fused_computation.210 | convolution fusion | flops 403243008 | bytes 5177344 | tf_op jit(solution)/shard_map/dot_general | solution.py:121
  43.3 0.8 %fusion.8 = f32[96,1024]{1,0:T(8,128)S(1)} fusion(bf16[2048,1024]{1,0:T(8,128)(2,1)S(1)} %get-tuple-element.42, bf16[96,1024]{1,0:T(8,128)(2,1)S(1)} %get-tuple-element.154, bf16[32,1024]{1,0:T(8,128)(2,1)S(1)} %get-tuple-element.159, bf16[32,1024]{1,0:T(8,128)(2,1)S(1)} %get-tuple-element.160, bf16[32,1024]{1,0:T(8,128)(2,1)S(1)} %get-tuple-element.142), kind=kOutput, calls=%fused_computation.45 | convolution fusion | flops 404226048 | bytes 4980736 | tf_op jit(solution)/shard_map/dot_general | solution.py:117
  44.1 0.8 %convolution_add_fusion.6 = f32[96,1024]{1,0:T(8,128)S(1)} fusion(bf16[2048,1024]{1,0:T(8,128)(2,1)S(1)} %get-tuple-element.43, f32[96,2048]{1,0:T(8,128)S(1)} %fusion.86, bf16[96,1024]{1,0:T(8,128)(2,1)S(1)} %get-tuple-element.153, bf16[32,1024]{1,0:T(8,128)(2,1)S(1)} %get-tuple-element.118, bf16[32,1024]{1,0:T(8,128)(2,1)S(1)} %get-tuple-element.117, ...), kind=kOutput, calls=%fused_computation.6 | convolution fusion | flops 404422656 | bytes 5767168 | tf_op jit(solution)/shard_map/dot_general | solution.py:117
  48.3 0.8 %convolution_add_fusion.4 = f32[96,1024]{1,0:T(8,128)S(1)} fusion(f32[96,1024]{1,0:T(8,128)S(1)} %add.194, bf16[2048,1024]{1,0:T(8,128)(2,1)S(1)} %get-tuple-element.53, bf16[96,1024]{1,0:T(8,128)(2,1)S(1)} %get-tuple-element.151, bf16[32,1024]{1,0:T(8,128)(2,1)S(1)} %get-tuple-element.112, bf16[32,1024]{1,0:T(8,128)(2,1)S(1)} %get-tuple-element.113, ...), kind=kOutput, calls=%fused_computation.4 | convolution fusion | flops 404324352 | bytes 5373952 | tf_op jit(solution)/shard_map/dot_general | solution.py:117
  49.2 1.1 %convolution_add_fusion.5 = f32[96,1024]{1,0:T(8,128)S(1)} fusion(f32[96,1024]{1,0:T(8,128)S(1)} %add.193, bf16[2048,1024]{1,0:T(8,128)(2,1)S(1)} %get-tuple-element.51, bf16[96,1024]{1,0:T(8,128)(2,1)S(1)} %get-tuple-element.151, bf16[32,1024]{1,0:T(8,128)(2,1)S(1)} %get-tuple-element.112, bf16[32,1024]{1,0:T(8,128)(2,1)S(1)} %get-tuple-element.113, ...), kind=kOutput, calls=%fused_computation.5 | convolution fusion | flops 404324352 | bytes 5373952 | tf_op jit(solution)/shard_map/dot_general | solution.py:117
  51.1 1.4 %fusion.85 = f32[96,2048]{1,0:T(8,128)S(1)} fusion(bf16[2048,1024]{1,0:T(8,128)(2,1)S(1)} %get-tuple-element.38, bf16[32,1024]{1,0:T(8,128)(2,1)S(1)} %get-tuple-element.110, bf16[32,1024]{1,0:T(8,128)(2,1)S(1)} %get-tuple-element.109, bf16[32,1024]{1,0:T(8,128)(2,1)S(1)} %get-tuple-element.139), kind=kOutput, calls=%fused_computation.209 | convolution fusion | flops 403243008 | bytes 5177344 | tf_op jit(solution)/shard_map/dot_general | solution.py:121
  52.7 0.8 %fusion.16 = f32[96,1024]{1,0:T(8,128)S(1)} fusion(bf16[2048,1024]{1,0:T(8,128)(2,1)S(1)} %get-tuple-element.42, bf16[96,1024]{1,0:T(8,128)(2,1)S(1)} %get-tuple-element.150, bf16[32,1024]{1,0:T(8,128)(2,1)S(1)} %get-tuple-element.110, bf16[32,1024]{1,0:T(8,128)(2,1)S(1)} %get-tuple-element.109, bf16[32,1024]{1,0:T(8,128)(2,1)S(1)} %get-tuple-element.139), kind=kOutput, calls=%fused_computation.56 | convolution fusion | flops 404226048 | bytes 4980736 | tf_op jit(solution)/shard_map/dot_general | solution.py:117
  53.5 0.8 %convolution_add_fusion.2 = f32[96,1024]{1,0:T(8,128)S(1)} fusion(bf16[2048,1024]{1,0:T(8,128)(2,1)S(1)} %get-tuple-element.43, f32[96,2048]{1,0:T(8,128)S(1)} %fusion.85, bf16[96,1024]{1,0:T(8,128)(2,1)S(1)} %get-tuple-element.149, bf16[32,1024]{1,0:T(8,128)(2,1)S(1)} %get-tuple-element.108, bf16[32,1024]{1,0:T(8,128)(2,1)S(1)} %get-tuple-element.107, ...), kind=kOutput, calls=%fused_computation.2 | convolution fusion | flops 404422656 | bytes 5767168 | tf_op jit(solution)/shard_map/dot_general | solution.py:117
  54.3 0.8 %convolution_add_fusion.3 = f32[96,1024]{1,0:T(8,128)S(1)} fusion(f32[96,1024]{1,0:T(8,128)S(1)} %fusion.16, bf16[2048,1024]{1,0:T(8,128)(2,1)S(1)} %get-tuple-element.38, bf16[96,1024]{1,0:T(8,128)(2,1)S(1)} %get-tuple-element.149, bf16[32,1024]{1,0:T(8,128)(2,1)S(1)} %get-tuple-element.108, bf16[32,1024]{1,0:T(8,128)(2,1)S(1)} %get-tuple-element.107, ...), kind=kOutput, calls=%fused_computation.3 | convolution fusion | flops 404324352 | bytes 5373952 | tf_op jit(solution)/shard_map/dot_general | solution.py:117
  57.7 0.8 %convolution_add_fusion.1 = f32[96,1024]{1,0:T(8,128)S(1)} fusion(f32[96,1024]{1,0:T(8,128)S(1)} %add.210, bf16[2048,1024]{1,0:T(8,128)(2,1)S(1)} %get-tuple-element.51, bf16[96,1024]{1,0:T(8,128)(2,1)S(1)} %get-tuple-element.147, bf16[32,1024]{1,0:T(8,128)(2,1)S(1)} %get-tuple-element.102, bf16[32,1024]{1,0:T(8,128)(2,1)S(1)} %get-tuple-element.103, ...), kind=kOutput, calls=%fused_computation.1 | convolution fusion | flops 404324352 | bytes 5373952 | tf_op jit(solution)/shard_map/dot_general | solution.py:117
  60.2 0.8 %collective-permute-done.11 = f32[32]{0:T(128)S(1)} collective-permute-done((f32[32]{0:T(128)S(1)}, f32[32]{0:T(128)S(1)}, u32[]{:S(2)}, u32[]{:S(2)}) %collective-permute-start.11) | collective-permute-done | bytes 160 | tf_op jit(solution)/shard_map/ppermute | solution.py:19
  (84 shorter events, 14.8 us)
Async XLA Ops:
  1.4 7.9 %collective-permute-start = (f32[65,256]{1,0:T(8,128)S(1)}, f32[65,256]{1,0:T(8,128)S(1)}, u32[]{:S(2)}, u32[]{:S(2)}) collective-permute-start(f32[65,256]{1,0:T(8,128)S(1)} %pad_maximum_fusion.22), channel_id=1, source_target_pairs={{0,8},{1,9},{2,10},{3,11},{4,12},{5,13},{6,14},{7,15},{8,0},{9,1},... | collective-permute-start | bytes 199688 | tf_op jit(solution)/shard_map/ppermute | solution.py:19
  9.4 5.2 %collective-permute-start.1 = (f32[65,512]{1,0:T(8,128)S(1)}, f32[65,512]{1,0:T(8,128)S(1)}, u32[]{:S(2)}, u32[]{:S(2)}) collective-permute-start(f32[65,512]{1,0:T(8,128)S(1)} %pad_maximum_fusion.18), channel_id=1, source_target_pairs={{0,4},{1,5},{2,6},{3,7},{4,0},{5,1},{6,2},{7,3},{8,12},{9,13},{10,... | collective-permute-start | bytes 399368 | tf_op jit(solution)/shard_map/ppermute | solution.py:19
  14.6 6.8 %collective-permute-start.2 = (f32[65,1024]{1,0:T(8,128)S(1)}, f32[65,1024]{1,0:T(8,128)S(1)}, u32[]{:S(2)}, u32[]{:S(2)}) collective-permute-start(f32[65,1024]{1,0:T(8,128)S(1)} %pad_maximum_fusion.14), channel_id=1, source_target_pairs={{0,2},{1,3},{2,0},{3,1},{4,6},{5,7},{6,4},{7,5},{8,10},{9,11},{10,... | collective-permute-start | bytes 798728 | tf_op jit(solution)/shard_map/ppermute | solution.py:19
  16.5 2.0 %collective-permute-start.3 = (f32[64,1024]{1,0:T(8,128)S(1)}, f32[64,1024]{1,0:T(8,128)S(1)}, u32[]{:S(2)}, u32[]{:S(2)}) collective-permute-start(f32[64,1024]{1,0:T(8,128)S(1)} %slice.215), channel_id=1, source_target_pairs={{0,1},{1,0},{2,3},{3,2},{4,5},{5,4},{6,7},{7,6},{8,9},{9,8},{10,11... | collective-permute-start | bytes 786440 | tf_op jit(solution)/shard_map/ppermute | solution.py:19
  21.4 7.0 %collective-permute-start.4 = (f32[64,1024]{1,0:T(8,128)S(1)}, f32[64,1024]{1,0:T(8,128)S(1)}, u32[]{:S(2)}, u32[]{:S(2)}) collective-permute-start(f32[64,1024]{1,0:T(8,128)S(1)} %slice.216), channel_id=1, source_target_pairs={{0,1},{1,0},{2,3},{3,2},{4,5},{5,4},{6,7},{7,6},{8,9},{9,8},{10,11... | collective-permute-start | bytes 786440 | tf_op jit(solution)/shard_map/ppermute | solution.py:19
  30.2 6.6 %collective-permute-start.5 = (f32[32,1024]{1,0:T(8,128)S(1)}, f32[32,1024]{1,0:T(8,128)S(1)}, u32[]{:S(2)}, u32[]{:S(2)}) collective-permute-start(f32[32,1024]{1,0:T(8,128)S(1)} %get-tuple-element.37), channel_id=1, source_target_pairs={{0,1},{1,0},{2,3},{3,2},{4,5},{5,4},{6,7},{7,6},{8,9},{9,8},{10,11... | collective-permute-start | bytes 393224 | tf_op jit(solution)/shard_map/ppermute | solution.py:19
  32.7 4.1 %collective-permute-start.6 = (f32[32,1024]{1,0:T(8,128)S(1)}, f32[32,1024]{1,0:T(8,128)S(1)}, u32[]{:S(2)}, u32[]{:S(2)}) collective-permute-start(f32[32,1024]{1,0:T(8,128)S(1)} %get-tuple-element.41), channel_id=1, source_target_pairs={{0,1},{1,0},{2,3},{3,2},{4,5},{5,4},{6,7},{7,6},{8,9},{9,8},{10,11... | collective-permute-start | bytes 393224 | tf_op jit(solution)/shard_map/ppermute | solution.py:19
  41.1 4.7 %collective-permute-start.7 = (f32[32,1024]{1,0:T(8,128)S(1)}, f32[32,1024]{1,0:T(8,128)S(1)}, u32[]{:S(2)}, u32[]{:S(2)}) collective-permute-start(f32[32,1024]{1,0:T(8,128)S(1)} %get-tuple-element.143), channel_id=1, source_target_pairs={{0,1},{1,0},{2,3},{3,2},{4,5},{5,4},{6,7},{7,6},{8,9},{9,8},{10,11... | collective-permute-start | bytes 393224 | tf_op jit(solution)/shard_map/ppermute | solution.py:19
  41.7 4.1 %collective-permute-start.8 = (f32[32,1024]{1,0:T(8,128)S(1)}, f32[32,1024]{1,0:T(8,128)S(1)}, u32[]{:S(2)}, u32[]{:S(2)}) collective-permute-start(f32[32,1024]{1,0:T(8,128)S(1)} %get-tuple-element.83), channel_id=1, source_target_pairs={{0,1},{1,0},{2,3},{3,2},{4,5},{5,4},{6,7},{7,6},{8,9},{9,8},{10,11... | collective-permute-start | bytes 393224 | tf_op jit(solution)/shard_map/ppermute | solution.py:19
  50.4 4.7 %collective-permute-start.9 = (f32[32,1024]{1,0:T(8,128)S(1)}, f32[32,1024]{1,0:T(8,128)S(1)}, u32[]{:S(2)}, u32[]{:S(2)}) collective-permute-start(f32[32,1024]{1,0:T(8,128)S(1)} %get-tuple-element.140), channel_id=1, source_target_pairs={{0,1},{1,0},{2,3},{3,2},{4,5},{5,4},{6,7},{7,6},{8,9},{9,8},{10,11... | collective-permute-start | bytes 393224 | tf_op jit(solution)/shard_map/ppermute | solution.py:19
  51.0 4.1 %collective-permute-start.10 = (f32[32,1024]{1,0:T(8,128)S(1)}, f32[32,1024]{1,0:T(8,128)S(1)}, u32[]{:S(2)}, u32[]{:S(2)}) collective-permute-start(f32[32,1024]{1,0:T(8,128)S(1)} %get-tuple-element.73), channel_id=1, source_target_pairs={{0,1},{1,0},{2,3},{3,2},{4,5},{5,4},{6,7},{7,6},{8,9},{9,8},{10,11... | collective-permute-start | bytes 393224 | tf_op jit(solution)/shard_map/ppermute | solution.py:19
  59.7 1.4 %collective-permute-start.11 = (f32[32]{0:T(128)S(1)}, f32[32]{0:T(128)S(1)}, u32[]{:S(2)}, u32[]{:S(2)}) collective-permute-start(f32[32]{0:T(128)S(1)} %fusion.24), channel_id=1, source_target_pairs={{0,1},{1,0},{2,3},{3,2},{4,5},{5,4},{6,7},{7,6},{8,9},{9,8},{10,11... | collective-permute-start | bytes 392 | tf_op jit(solution)/shard_map/ppermute | solution.py:19

commit v12 on v9

--- a/solution.py
+++ b/solution.py
@@ -57,8 +57,10 @@
     return left, right
 
 
-def scaled_operand_kernel(mine_ref, scale_ref, right_ref):
-    right_ref[...] = operands(mine_ref[...] * scale_ref[...])[1]
+def prepare_kernel(part_ref, scale_ref, right_ref, copy_ref):
+    feats = scale_ref.shape[0]
+    right_ref[...] = operands(part_ref[:feats] * scale_ref[...])[1]
+    copy_ref[...] = part_ref[...]
 
 
 def build_kernel(rows_ref, vectors_ref, scale_ref, right_ref, sum_ref, tile_ref, out_ref):
@@ -100,6 +102,16 @@
     )(*args)
 
 
+def prepare(part, scale):
+    feats, cols = scale.shape[0], part.shape[1]
+    outs = (jax.ShapeDtypeStruct((6 * feats + NORM_ROWS, cols), jnp.bfloat16), jax.ShapeDtypeStruct(part.shape, part.dtype))
+    return call(prepare_kernel, outs, part, scale, flops=10**9, bytes_accessed=feats * cols, transcendentals=0)
+
+
+def join(*xs):
+    return jnp.concatenate(xs, axis=1)
+
+
 def build_piece(rows, vectors, scale, right, total):
     count, cols = rows.shape[1], right.shape[1]
     outs = (jax.ShapeDtypeStruct((2 * count, cols), jnp.bfloat16), jax.ShapeDtypeStruct(total.shape, jnp.float32))
@@ -134,28 +146,50 @@
                 pieces += [came, swap(came, n, 1)]
             return pieces
 
-        mine = lax.optimization_barrier(jnp.concatenate([points, targets, noise_var[None, :]], axis=0))
-        for stride in outer:
-            mine = jnp.concatenate([mine, swap(mine, n, stride)], axis=1)
-        noise = mine[-1:]
         scale = (POINT_SCALE / lengthscale)[:, None]
-        first = arrivals(mine[:-1])
+        block = lax.optimization_barrier(jnp.concatenate([points, targets, noise_var[None, :]], axis=0))
+        fence = lax.optimization_barrier
+        tile = []
+
+        def build(x, total):
+            piece, total = build_piece(x[:feats], x[feats:], scale, right, total)
+            tile.append(piece)
+            return total
+
+        if len(outer) == 2 and len(inner) == 2:
+            far, near, side = outer[0], outer[1], inner[0]
+            by_far = swap(block, n, far)
+            right_own, copy = prepare(block, scale)
+            by_near = swap(copy, n, near)
+            side_own = swap(copy[:-1], n, side)
+            by_both = swap(by_far, n, near)
+            right_far = prepare(by_far, scale)[0]
+            last, side_own = fence((join(by_far, by_near, by_both)[:-1], side_own))
+            side_last = swap(last, n, side)
+            right = join(right_own, right_far, prepare(join(by_near, by_both), scale)[0])
+            mine = join(block, by_far, by_near, by_both)
+            noise, mine = mine[-1:], mine[:-1]
+            early = side_own
+            across, early_across = swap(mine, n, 1), swap(early, n, 1)
+            my_applied = build(mine, noise * mine[feats:])
+            my_applied = build(across, my_applied)
+            side_last, my_applied = fence((side_last, my_applied))
+            last_across = swap(side_last, n, 1)
+            beside = join(early, side_last)
+            my_applied = build(beside, my_applied)
+            beside_across = join(early_across, last_across)
+            my_applied = build(beside_across, my_applied)
+            first = [mine, across, beside, beside_across]
+        else:
+            mine = block
+            for stride in outer:
+                mine = join(mine, swap(mine, n, stride))
+            right, noise, first = prepare(mine, scale)[0], mine[-1:], arrivals(mine[:-1])
+            my_applied = noise * first[0][feats:]
+            for x in first:
+                my_applied = build(x, my_applied)
         cols = noise.shape[1]
-        right = call(
-            scaled_operand_kernel,
-            jax.ShapeDtypeStruct((6 * feats + NORM_ROWS, cols), jnp.bfloat16),
-            mine[:feats],
-            scale,
-            flops=feats * cols,
-            bytes_accessed=feats * cols,
-            transcendentals=0,
-        )
         starts = [x[feats:] for x in first]
-        tile = []
-        my_applied = noise * starts[0]
-        for x, start in zip(first, starts):
-            piece, my_applied = build_piece(x[:feats], start, scale, right, my_applied)
-            tile.append(piece)
 
         def operator(pieces):
             total = apply_piece(pieces[0], tile[0])

time: 56.5 us -> 56.6 us (level)
  waiting for transfers between devices: 19.7 us -> 17.6 us
  Pallas kernels: 6.97 us -> 8.25 us
  starting transfers between devices: 13.9 us -> 14.8 us
    ppermute x16 -> x19, waiting for transfers between devices: 19.7 us -> 17.6 us  [swap(): return lax.ppermute(x, 'blk', [(i, i ^ stride) for i in range(n)])]
    pallas_call x5 -> x7, Pallas kernels: 6.97 us -> 8.25 us  [call(): pl.pallas_call(kernel, out_shape=outs, in_specs=[whole] * len(args), out_...]
    ppermute x16 -> x19, starting transfers between devices: 13.9 us -> 14.8 us  [swap(): return lax.ppermute(x, 'blk', [(i, i ^ stride) for i in range(n)])]
  transfers between devices with their start and end apart: 16 -> 19, of which waited for: 14 -> 13; matrix products, arithmetic and copies ran while one was open for 15% -> 15% of each run, Pallas kernels for 9% -> 12%
where the time goes in v12:
time: 56.6 us; the launch traced here: 56.4 us
  waiting for transfers between devices  17.6 us (31%)
  starting transfers between devices  14.8 us (26%)
  matrix products  9.83 us (17%)
  Pallas kernels  8.25 us (15%)
  other arithmetic  4.78 us (8%)
  between operations  0.92 us (2%)
    ppermute x19, waiting for transfers between devices, swap(): return lax.ppermute(x, 'blk', [(i, i ^ stride) for i in range(n)])  17.6 us
    ppermute x19, starting transfers between devices, swap(): return lax.ppermute(x, 'blk', [(i, i ^ stride) for i in range(n)])  14.8 us
    dot_general x12, matrix products, apply_piece(): jnp.dot(jnp.concatenate([left, right], axis=1), piece, preferred_element_...  9.83 us
    pallas_call x7, Pallas kernels, call(): pl.pallas_call(kernel, out_shape=outs, in_specs=[whole] * len(args), out_...  8.25 us
  transfers between devices with their start and end apart: 19, of which 13 were waited for; matrix products, arithmetic and copies ran while one was open for 15% of the time, Pallas kernels for 12%

profile of v12, /device:TPU:0, one launch (start us, length us, event | category | flops | bytes accessed | tf_op | source)
XLA Modules:
  0.0 56.4 jit_solution(15201156458549589894)
XLA Ops:
  1.4 4.0 %collective-permute-start = (f32[65,256]{1,0:T(8,128)S(1)}, f32[65,256]{1,0:T(8,128)S(1)}, u32[]{:S(2)}, u32[]{:S(2)}) collective-permute-start(f32[65,256]{1,0:T(8,128)S(1)} %pad_maximum_fusion.19.part_ref), channel_id=1, source_target_pairs={{0,8},{1,9},{2,10},{3,11},{4,12},{5,13},{6,14},{7,15},{8,0},{9,1},... | collective-permute-start | bytes 199688 | tf_op jit(solution)/shard_map/ppermute | solution.py:19
  6.3 1.6 %collective-permute-start.1 = (f32[65,256]{1,0:T(8,128)S(1)}, f32[65,256]{1,0:T(8,128)S(1)}, u32[]{:S(2)}, u32[]{:S(2)}) collective-permute-start(f32[65,256]{1,0:T(8,128)S(1)} %get-tuple-element.18), channel_id=1, source_target_pairs={{0,4},{1,5},{2,6},{3,7},{4,0},{5,1},{6,2},{7,3},{8,12},{9,13},{10,... | collective-permute-start | bytes 199688 | tf_op jit(solution)/shard_map/ppermute | solution.py:19
  8.0 1.5 %collective-permute-start.4 = (f32[64,256]{1,0:T(8,128)S(1)}, f32[64,256]{1,0:T(8,128)S(1)}, u32[]{:S(2)}, u32[]{:S(2)}) collective-permute-start(f32[64,256]{1,0:T(8,128)S(1)} %slice.97), channel_id=1, source_target_pairs={{0,2},{1,3},{2,0},{3,1},{4,6},{5,7},{6,4},{7,5},{8,10},{9,11},{10,... | collective-permute-start | bytes 196616 | tf_op jit(solution)/shard_map/ppermute | solution.py:19
  9.5 0.9 %collective-permute-start.2 = (f32[65,256]{1,0:T(8,128)S(1)}, f32[65,256]{1,0:T(8,128)S(1)}, u32[]{:S(2)}, u32[]{:S(2)}) collective-permute-start(f32[65,256]{1,0:T(8,128)S(1)} %collective-permute-done.part_ref), channel_id=1, source_target_pairs={{0,4},{1,5},{2,6},{3,7},{4,0},{5,1},{6,2},{7,3},{8,12},{9,13},{10,... | collective-permute-start | bytes 199688 | tf_op jit(solution)/shard_map/ppermute | solution.py:19
  11.0 2.9 %collective-permute-done.2 = f32[65,256]{1,0:T(8,128)S(1)} collective-permute-done((f32[65,256]{1,0:T(8,128)S(1)}, f32[65,256]{1,0:T(8,128)S(1)}, u32[]{:S(2)}, u32[]{:S(2)}) %collective-permute-start.2) | collective-permute-done | bytes 66592 | tf_op jit(solution)/shard_map/ppermute | solution.py:19
  14.0 1.2 %collective-permute-start.5 = (f32[64,768]{1,0:T(8,128)S(1)}, f32[64,768]{1,0:T(8,128)S(1)}, u32[]{:S(2)}, u32[]{:S(2)}) collective-permute-start(f32[64,768]{1,0:T(8,128)S(1)} %pad_maximum_fusion.16), channel_id=1, source_target_pairs={{0,2},{1,3},{2,0},{3,1},{4,6},{5,7},{6,4},{7,5},{8,10},{9,11},{10,... | collective-permute-start | bytes 589832 | tf_op jit(solution)/shard_map/ppermute | solution.py:19
  16.3 1.7 %shard_map.62 = (bf16[2048,1024]{1,0:T(8,128)(2,1)S(1)}, f32[32,1024]{1,0:T(8,128)S(1)}) custom-call(f32[32,1024]{1,0:T(8,128)S(1)} %get-tuple-element.53.rows_ref, f32[32,1024]{1,0:T(8,128)S(1)} %get-tuple-element.54.vectors_ref, f32[32,1]{1,0:T(8,128)S(1)} %copy.6.scale_ref, bf16[256,1024]{1,0:T(8,128)(2,1)S(1)} %constant_dynamic-update-slice_fusion.right_ref, ...), custom_call_target="tpu_custom_call" | custom-call | flops 872415232 | bytes 4194304 | tf_op jit(solution)/shard_map/pallas_call | solution.py:95
  18.1 1.7 %shard_map.63 = (bf16[2048,1024]{1,0:T(8,128)(2,1)S(1)}, f32[32,1024]{1,0:T(8,128)S(1)}) custom-call(f32[32,1024]{1,0:T(8,128)S(1)} %get-tuple-element.60.rows_ref, f32[32,1024]{1,0:T(8,128)S(1)} %get-tuple-element.59.vectors_ref, f32[32,1]{1,0:T(8,128)S(1)} %copy.6.scale_ref, bf16[256,1024]{1,0:T(8,128)(2,1)S(1)} %constant_dynamic-update-slice_fusion.right_ref, ...), custom_call_target="tpu_custom_call" | custom-call | flops 872415232 | bytes 4194304 | tf_op jit(solution)/shard_map/pallas_call | solution.py:95
  19.8 1.6 %collective-permute-done.5 = f32[64,768]{1,0:T(8,128)S(1)} collective-permute-done((f32[64,768]{1,0:T(8,128)S(1)}, f32[64,768]{1,0:T(8,128)S(1)}, u32[]{:S(2)}, u32[]{:S(2)}) %collective-permute-start.5) | collective-permute-done | bytes 196640 | tf_op jit(solution)/shard_map/ppermute | solution.py:19
  21.4 1.7 %shard_map.64 = (bf16[2048,1024]{1,0:T(8,128)(2,1)S(1)}, f32[32,1024]{1,0:T(8,128)S(1)}) custom-call(f32[32,1024]{1,0:T(8,128)S(1)} %get-tuple-element.56.rows_ref, f32[32,1024]{1,0:T(8,128)S(1)} %get-tuple-element.55.vectors_ref, f32[32,1]{1,0:T(8,128)S(1)} %copy.6.scale_ref, bf16[256,1024]{1,0:T(8,128)(2,1)S(1)} %constant_dynamic-update-slice_fusion.right_ref, ...), custom_call_target="tpu_custom_call" | custom-call | flops 872415232 | bytes 4194304 | tf_op jit(solution)/shard_map/pallas_call | solution.py:95
  23.2 1.7 %shard_map.65 = (bf16[2048,1024]{1,0:T(8,128)(2,1)S(1)}, f32[32,1024]{1,0:T(8,128)S(1)}) custom-call(f32[32,1024]{1,0:T(8,128)S(1)} %get-tuple-element.58.rows_ref, f32[32,1024]{1,0:T(8,128)S(1)} %get-tuple-element.57.vectors_ref, f32[32,1]{1,0:T(8,128)S(1)} %copy.6.scale_ref, bf16[256,1024]{1,0:T(8,128)(2,1)S(1)} %constant_dynamic-update-slice_fusion.right_ref, ...), custom_call_target="tpu_custom_call" | custom-call | flops 872415232 | bytes 4194304 | tf_op jit(solution)/shard_map/pallas_call | solution.py:95
  24.9 1.2 %collective-permute-start.9 = (f32[32,1024]{1,0:T(8,128)S(1)}, f32[32,1024]{1,0:T(8,128)S(1)}, u32[]{:S(2)}, u32[]{:S(2)}) collective-permute-start(f32[32,1024]{1,0:T(8,128)S(1)} %get-tuple-element.29), channel_id=1, source_target_pairs={{0,2},{1,3},{2,0},{3,1},{4,6},{5,7},{6,4},{7,5},{8,10},{9,11},{10,... | collective-permute-start | bytes 393224 | tf_op jit(solution)/shard_map/ppermute | solution.py:19
  26.4 0.8 %fusion.1 = f32[96,1024]{1,0:T(8,128)S(1)} fusion(bf16[2048,1024]{1,0:T(8,128)(2,1)S(1)} %get-tuple-element.30, bf16[32,1024]{1,0:T(8,128)(2,1)S(1)} %broadcast.4, bf16[32,1024]{1,0:T(8,128)(2,1)S(1)} %get-tuple-element.96, bf16[32,1024]{1,0:T(8,128)(2,1)S(1)} %get-tuple-element.97, bf16[32,1024]{1,0:T(8,128)(2,1)S(1)} %get-tuple-element.95), kind=kOutput, calls=%fused_computation.38 | convolution fusion | flops 405012480 | bytes 4849664 | tf_op jit(solution)/shard_map/dot_general | solution.py:126
  27.5 0.8 %convolution_add_fusion.8 = f32[96,1024]{1,0:T(8,128)S(1)} fusion(f32[96,1024]{1,0:T(8,128)S(1)} %fusion.1, bf16[2048,1024]{1,0:T(8,128)(2,1)S(1)} %get-tuple-element.31, bf16[32,1024]{1,0:T(8,128)(2,1)S(1)} %broadcast.4, bf16[32,1024]{1,0:T(8,128)(2,1)S(1)} %get-tuple-element.92, bf16[32,1024]{1,0:T(8,128)(2,1)S(1)} %get-tuple-element.93, ...), kind=kOutput, calls=%fused_computation.20 | convolution fusion | flops 405110784 | bytes 5242880 | tf_op jit(solution)/shard_map/dot_general | solution.py:126
  28.3 2.5 %collective-permute-done.9 = f32[32,1024]{1,0:T(8,128)S(1)} collective-permute-done((f32[32,1024]{1,0:T(8,128)S(1)}, f32[32,1024]{1,0:T(8,128)S(1)}, u32[]{:S(2)}, u32[]{:S(2)}) %collective-permute-start.9) | collective-permute-done | bytes 131104 | tf_op jit(solution)/shard_map/ppermute | solution.py:19
  30.9 0.8 %convolution_add_fusion.7 = f32[96,1024]{1,0:T(8,128)S(1)} fusion(f32[96,1024]{1,0:T(8,128)S(1)} %convolution_add_fusion.8, bf16[2048,1024]{1,0:T(8,128)(2,1)S(1)} %get-tuple-element.32, bf16[32,1024]{1,0:T(8,128)(2,1)S(1)} %broadcast.4, bf16[32,1024]{1,0:T(8,128)(2,1)S(1)} %get-tuple-element.88, bf16[32,1024]{1,0:T(8,128)(2,1)S(1)} %get-tuple-element.89, ...), kind=kOutput, calls=%fused_computation.19 | convolution fusion | flops 405110784 | bytes 5242880 | tf_op jit(solution)/shard_map/dot_general | solution.py:126
  32.2 0.8 %convolution_add_fusion.6 = f32[96,1024]{1,0:T(8,128)S(1)} fusion(f32[96,1024]{1,0:T(8,128)S(1)} %convolution_add_fusion.7, bf16[2048,1024]{1,0:T(8,128)(2,1)S(1)} %get-tuple-element.33, bf16[32,1024]{1,0:T(8,128)(2,1)S(1)} %broadcast.4, bf16[32,1024]{1,0:T(8,128)(2,1)S(1)} %get-tuple-element.84, bf16[32,1024]{1,0:T(8,128)(2,1)S(1)} %get-tuple-element.85, ...), kind=kOutput, calls=%fused_computation.18 | convolution fusion | flops 405110784 | bytes 5242880 | tf_op jit(solution)/shard_map/dot_general | solution.py:126
  33.6 1.3 %collective-permute-start.12 = (f32[32,1024]{1,0:T(8,128)S(1)}, f32[32,1024]{1,0:T(8,128)S(1)}, u32[]{:S(2)}, u32[]{:S(2)}) collective-permute-start(f32[32,1024]{1,0:T(8,128)S(1)} %get-tuple-element.48), channel_id=1, source_target_pairs={{0,2},{1,3},{2,0},{3,1},{4,6},{5,7},{6,4},{7,5},{8,10},{9,11},{10,... | collective-permute-start | bytes 393224 | tf_op jit(solution)/shard_map/ppermute | solution.py:19
  34.9 0.8 %fusion.10 = f32[96,1024]{1,0:T(8,128)S(1)} fusion(bf16[2048,1024]{1,0:T(8,128)(2,1)S(1)} %get-tuple-element.30, bf16[32,1024]{1,0:T(8,128)(2,1)S(1)} %broadcast.4, bf16[32,1024]{1,0:T(8,128)(2,1)S(1)} %get-tuple-element.82, bf16[32,1024]{1,0:T(8,128)(2,1)S(1)} %get-tuple-element.81, bf16[32,1024]{1,0:T(8,128)(2,1)S(1)} %get-tuple-element.47), kind=kOutput, calls=%fused_computation.43 | convolution fusion | flops 405012480 | bytes 4849664 | tf_op jit(solution)/shard_map/dot_general | solution.py:126
  36.3 0.8 %convolution_add_fusion.5 = f32[96,1024]{1,0:T(8,128)S(1)} fusion(f32[96,1024]{1,0:T(8,128)S(1)} %fusion.10, bf16[2048,1024]{1,0:T(8,128)(2,1)S(1)} %get-tuple-element.31, bf16[32,1024]{1,0:T(8,128)(2,1)S(1)} %broadcast.4, bf16[32,1024]{1,0:T(8,128)(2,1)S(1)} %get-tuple-element.79, bf16[32,1024]{1,0:T(8,128)(2,1)S(1)} %get-tuple-element.80, ...), kind=kOutput, calls=%fused_computation.17 | convolution fusion | flops 405110784 | bytes 5242880 | tf_op jit(solution)/shard_map/dot_general | solution.py:126
  37.1 2.2 %collective-permute-done.12 = f32[32,1024]{1,0:T(8,128)S(1)} collective-permute-done((f32[32,1024]{1,0:T(8,128)S(1)}, f32[32,1024]{1,0:T(8,128)S(1)}, u32[]{:S(2)}, u32[]{:S(2)}) %collective-permute-start.12) | collective-permute-done | bytes 131104 | tf_op jit(solution)/shard_map/ppermute | solution.py:19
  39.3 1.0 %convolution_add_fusion.4 = f32[96,1024]{1,0:T(8,128)S(1)} fusion(f32[96,1024]{1,0:T(8,128)S(1)} %convolution_add_fusion.5, bf16[2048,1024]{1,0:T(8,128)(2,1)S(1)} %get-tuple-element.32, bf16[32,1024]{1,0:T(8,128)(2,1)S(1)} %broadcast.4, bf16[32,1024]{1,0:T(8,128)(2,1)S(1)} %get-tuple-element.76, bf16[32,1024]{1,0:T(8,128)(2,1)S(1)} %get-tuple-element.77, ...), kind=kOutput, calls=%fused_computation.16 | convolution fusion | flops 405110784 | bytes 5242880 | tf_op jit(solution)/shard_map/dot_general | solution.py:126
  40.6 0.8 %convolution_add_fusion.3 = f32[96,1024]{1,0:T(8,128)S(1)} fusion(f32[96,1024]{1,0:T(8,128)S(1)} %convolution_add_fusion.4, bf16[2048,1024]{1,0:T(8,128)(2,1)S(1)} %get-tuple-element.33, bf16[32,1024]{1,0:T(8,128)(2,1)S(1)} %broadcast.4, bf16[32,1024]{1,0:T(8,128)(2,1)S(1)} %get-tuple-element.73, bf16[32,1024]{1,0:T(8,128)(2,1)S(1)} %get-tuple-element.74, ...), kind=kOutput, calls=%fused_computation.15 | convolution fusion | flops 405110784 | bytes 5242880 | tf_op jit(solution)/shard_map/dot_general | solution.py:126
  42.2 1.3 %collective-permute-start.15 = (f32[32,1024]{1,0:T(8,128)S(1)}, f32[32,1024]{1,0:T(8,128)S(1)}, u32[]{:S(2)}, u32[]{:S(2)}) collective-permute-start(f32[32,1024]{1,0:T(8,128)S(1)} %get-tuple-element.39), channel_id=1, source_target_pairs={{0,2},{1,3},{2,0},{3,1},{4,6},{5,7},{6,4},{7,5},{8,10},{9,11},{10,... | collective-permute-start | bytes 393224 | tf_op jit(solution)/shard_map/ppermute | solution.py:19
  43.5 0.8 %fusion.19 = f32[96,1024]{1,0:T(8,128)S(1)} fusion(bf16[2048,1024]{1,0:T(8,128)(2,1)S(1)} %get-tuple-element.30, bf16[32,1024]{1,0:T(8,128)(2,1)S(1)} %broadcast.4, bf16[32,1024]{1,0:T(8,128)(2,1)S(1)} %get-tuple-element.71, bf16[32,1024]{1,0:T(8,128)(2,1)S(1)} %get-tuple-element.70, bf16[32,1024]{1,0:T(8,128)(2,1)S(1)} %get-tuple-element.38), kind=kOutput, calls=%fused_computation.48 | convolution fusion | flops 405012480 | bytes 4849664 | tf_op jit(solution)/shard_map/dot_general | solution.py:126
  44.8 0.8 %convolution_add_fusion.2 = f32[96,1024]{1,0:T(8,128)S(1)} fusion(f32[96,1024]{1,0:T(8,128)S(1)} %fusion.19, bf16[2048,1024]{1,0:T(8,128)(2,1)S(1)} %get-tuple-element.31, bf16[32,1024]{1,0:T(8,128)(2,1)S(1)} %broadcast.4, bf16[32,1024]{1,0:T(8,128)(2,1)S(1)} %get-tuple-element.68, bf16[32,1024]{1,0:T(8,128)(2,1)S(1)} %get-tuple-element.69, ...), kind=kOutput, calls=%fused_computation.14 | convolution fusion | flops 405110784 | bytes 5242880 | tf_op jit(solution)/shard_map/dot_general | solution.py:126
  45.6 2.2 %collective-permute-done.15 = f32[32,1024]{1,0:T(8,128)S(1)} collective-permute-done((f32[32,1024]{1,0:T(8,128)S(1)}, f32[32,1024]{1,0:T(8,128)S(1)}, u32[]{:S(2)}, u32[]{:S(2)}) %collective-permute-start.15) | collective-permute-done | bytes 131104 | tf_op jit(solution)/shard_map/ppermute | solution.py:19
  47.9 0.8 %convolution_add_fusion.1 = f32[96,1024]{1,0:T(8,128)S(1)} fusion(f32[96,1024]{1,0:T(8,128)S(1)} %convolution_add_fusion.2, bf16[2048,1024]{1,0:T(8,128)(2,1)S(1)} %get-tuple-element.32, bf16[32,1024]{1,0:T(8,128)(2,1)S(1)} %broadcast.4, bf16[32,1024]{1,0:T(8,128)(2,1)S(1)} %get-tuple-element.65, bf16[32,1024]{1,0:T(8,128)(2,1)S(1)} %get-tuple-element.66, ...), kind=kOutput, calls=%fused_computation.13 | convolution fusion | flops 405110784 | bytes 5242880 | tf_op jit(solution)/shard_map/dot_general | solution.py:126
  49.2 0.8 %convolution_add_fusion = f32[96,1024]{1,0:T(8,128)S(1)} fusion(f32[96,1024]{1,0:T(8,128)S(1)} %convolution_add_fusion.1, bf16[2048,1024]{1,0:T(8,128)(2,1)S(1)} %get-tuple-element.33, bf16[32,1024]{1,0:T(8,128)(2,1)S(1)} %broadcast.4, bf16[32,1024]{1,0:T(8,128)(2,1)S(1)} %get-tuple-element.62, bf16[32,1024]{1,0:T(8,128)(2,1)S(1)} %get-tuple-element.63, ...), kind=kOutput, calls=%fused_computation.12 | convolution fusion | flops 405110784 | bytes 5242880 | tf_op jit(solution)/shard_map/dot_general | solution.py:126
  50.9 1.2 %collective-permute-start.17 = (f32[32]{0:T(128)S(1)}, f32[32]{0:T(128)S(1)}, u32[]{:S(2)}, u32[]{:S(2)}) collective-permute-start(f32[32]{0:T(128)S(1)} %get-tuple-element.36), channel_id=1, source_target_pairs={{0,2},{1,3},{2,0},{3,1},{4,6},{5,7},{6,4},{7,5},{8,10},{9,11},{10,... | collective-permute-start | bytes 392 | tf_op jit(solution)/shard_map/ppermute | solution.py:19
  52.2 2.4 %collective-permute-done.17 = f32[32]{0:T(128)S(1)} collective-permute-done((f32[32]{0:T(128)S(1)}, f32[32]{0:T(128)S(1)}, u32[]{:S(2)}, u32[]{:S(2)}) %collective-permute-start.17) | collective-permute-done | bytes 160 | tf_op jit(solution)/shard_map/ppermute | solution.py:19
  54.6 1.1 %collective-permute-done.18 = f32[32]{0:T(128)S(1)} collective-permute-done((f32[32]{0:T(128)S(1)}, f32[32]{0:T(128)S(1)}, u32[]{:S(2)}, u32[]{:S(2)}) %collective-permute-start.18) | collective-permute-done | bytes 160 | tf_op jit(solution)/shard_map/ppermute | solution.py:19
  (77 shorter events, 9.7 us)
Async XLA Ops:
  1.4 8.1 %collective-permute-start = (f32[65,256]{1,0:T(8,128)S(1)}, f32[65,256]{1,0:T(8,128)S(1)}, u32[]{:S(2)}, u32[]{:S(2)}) collective-permute-start(f32[65,256]{1,0:T(8,128)S(1)} %pad_maximum_fusion.19.part_ref), channel_id=1, source_target_pairs={{0,8},{1,9},{2,10},{3,11},{4,12},{5,13},{6,14},{7,15},{8,0},{9,1},... | collective-permute-start | bytes 199688 | tf_op jit(solution)/shard_map/ppermute | solution.py:19
  6.3 4.7 %collective-permute-start.1 = (f32[65,256]{1,0:T(8,128)S(1)}, f32[65,256]{1,0:T(8,128)S(1)}, u32[]{:S(2)}, u32[]{:S(2)}) collective-permute-start(f32[65,256]{1,0:T(8,128)S(1)} %get-tuple-element.18), channel_id=1, source_target_pairs={{0,4},{1,5},{2,6},{3,7},{4,0},{5,1},{6,2},{7,3},{8,12},{9,13},{10,... | collective-permute-start | bytes 199688 | tf_op jit(solution)/shard_map/ppermute | solution.py:19
  8.0 6.0 %collective-permute-start.4 = (f32[64,256]{1,0:T(8,128)S(1)}, f32[64,256]{1,0:T(8,128)S(1)}, u32[]{:S(2)}, u32[]{:S(2)}) collective-permute-start(f32[64,256]{1,0:T(8,128)S(1)} %slice.97), channel_id=1, source_target_pairs={{0,2},{1,3},{2,0},{3,1},{4,6},{5,7},{6,4},{7,5},{8,10},{9,11},{10,... | collective-permute-start | bytes 196616 | tf_op jit(solution)/shard_map/ppermute | solution.py:19
  9.5 4.4 %collective-permute-start.2 = (f32[65,256]{1,0:T(8,128)S(1)}, f32[65,256]{1,0:T(8,128)S(1)}, u32[]{:S(2)}, u32[]{:S(2)}) collective-permute-start(f32[65,256]{1,0:T(8,128)S(1)} %collective-permute-done.part_ref), channel_id=1, source_target_pairs={{0,4},{1,5},{2,6},{3,7},{4,0},{5,1},{6,2},{7,3},{8,12},{9,13},{10,... | collective-permute-start | bytes 199688 | tf_op jit(solution)/shard_map/ppermute | solution.py:19
  14.0 4.1 %collective-permute-start.6 = (f32[64,256]{1,0:T(8,128)S(1)}, f32[64,256]{1,0:T(8,128)S(1)}, u32[]{:S(2)}, u32[]{:S(2)}) collective-permute-start(f32[64,256]{1,0:T(8,128)S(1)} %collective-permute-done.4), channel_id=1, source_target_pairs={{0,1},{1,0},{2,3},{3,2},{4,5},{5,4},{6,7},{7,6},{8,9},{9,8},{10,11... | collective-permute-start | bytes 196616 | tf_op jit(solution)/shard_map/ppermute | solution.py:19
  14.0 7.3 %collective-permute-start.5 = (f32[64,768]{1,0:T(8,128)S(1)}, f32[64,768]{1,0:T(8,128)S(1)}, u32[]{:S(2)}, u32[]{:S(2)}) collective-permute-start(f32[64,768]{1,0:T(8,128)S(1)} %pad_maximum_fusion.16), channel_id=1, source_target_pairs={{0,2},{1,3},{2,0},{3,1},{4,6},{5,7},{6,4},{7,5},{8,10},{9,11},{10,... | collective-permute-start | bytes 589832 | tf_op jit(solution)/shard_map/ppermute | solution.py:19
  16.1 2.0 %collective-permute-start.3 = (f32[64,1024]{1,0:T(8,128)S(1)}, f32[64,1024]{1,0:T(8,128)S(1)}, u32[]{:S(2)}, u32[]{:S(2)}) collective-permute-start(f32[64,1024]{1,0:T(8,128)S(1)} %slice.122), channel_id=1, source_target_pairs={{0,1},{1,0},{2,3},{3,2},{4,5},{5,4},{6,7},{7,6},{8,9},{9,8},{10,11... | collective-permute-start | bytes 786440 | tf_op jit(solution)/shard_map/ppermute | solution.py:19
  21.4 1.8 %collective-permute-start.7 = (f32[64,768]{1,0:T(8,128)S(1)}, f32[64,768]{1,0:T(8,128)S(1)}, u32[]{:S(2)}, u32[]{:S(2)}) collective-permute-start(f32[64,768]{1,0:T(8,128)S(1)} %collective-permute-done.5), channel_id=1, source_target_pairs={{0,1},{1,0},{2,3},{3,2},{4,5},{5,4},{6,7},{7,6},{8,9},{9,8},{10,11... | collective-permute-start | bytes 589832 | tf_op jit(solution)/shard_map/ppermute | solution.py:19
  24.9 5.9 %collective-permute-start.9 = (f32[32,1024]{1,0:T(8,128)S(1)}, f32[32,1024]{1,0:T(8,128)S(1)}, u32[]{:S(2)}, u32[]{:S(2)}) collective-permute-start(f32[32,1024]{1,0:T(8,128)S(1)} %get-tuple-element.29), channel_id=1, source_target_pairs={{0,2},{1,3},{2,0},{3,1},{4,6},{5,7},{6,4},{7,5},{8,10},{9,11},{10,... | collective-permute-start | bytes 393224 | tf_op jit(solution)/shard_map/ppermute | solution.py:19
  26.1 1.3 %collective-permute-start.8 = (f32[32,1024]{1,0:T(8,128)S(1)}, f32[32,1024]{1,0:T(8,128)S(1)}, u32[]{:S(2)}, u32[]{:S(2)}) collective-permute-start(f32[32,1024]{1,0:T(8,128)S(1)} %get-tuple-element.29), channel_id=1, source_target_pairs={{0,1},{1,0},{2,3},{3,2},{4,5},{5,4},{6,7},{7,6},{8,9},{9,8},{10,11... | collective-permute-start | bytes 393224 | tf_op jit(solution)/shard_map/ppermute | solution.py:19
  30.8 1.3 %collective-permute-start.10 = (f32[32,1024]{1,0:T(8,128)S(1)}, f32[32,1024]{1,0:T(8,128)S(1)}, u32[]{:S(2)}, u32[]{:S(2)}) collective-permute-start(f32[32,1024]{1,0:T(8,128)S(1)} %collective-permute-done.9), channel_id=1, source_target_pairs={{0,1},{1,0},{2,3},{3,2},{4,5},{5,4},{6,7},{7,6},{8,9},{9,8},{10,11... | collective-permute-start | bytes 393224 | tf_op jit(solution)/shard_map/ppermute | solution.py:19
  33.6 5.6 %collective-permute-start.12 = (f32[32,1024]{1,0:T(8,128)S(1)}, f32[32,1024]{1,0:T(8,128)S(1)}, u32[]{:S(2)}, u32[]{:S(2)}) collective-permute-start(f32[32,1024]{1,0:T(8,128)S(1)} %get-tuple-element.48), channel_id=1, source_target_pairs={{0,2},{1,3},{2,0},{3,1},{4,6},{5,7},{6,4},{7,5},{8,10},{9,11},{10,... | collective-permute-start | bytes 393224 | tf_op jit(solution)/shard_map/ppermute | solution.py:19
  34.9 1.3 %collective-permute-start.11 = (f32[32,1024]{1,0:T(8,128)S(1)}, f32[32,1024]{1,0:T(8,128)S(1)}, u32[]{:S(2)}, u32[]{:S(2)}) collective-permute-start(f32[32,1024]{1,0:T(8,128)S(1)} %get-tuple-element.48), channel_id=1, source_target_pairs={{0,1},{1,0},{2,3},{3,2},{4,5},{5,4},{6,7},{7,6},{8,9},{9,8},{10,11... | collective-permute-start | bytes 393224 | tf_op jit(solution)/shard_map/ppermute | solution.py:19
  39.3 1.3 %collective-permute-start.13 = (f32[32,1024]{1,0:T(8,128)S(1)}, f32[32,1024]{1,0:T(8,128)S(1)}, u32[]{:S(2)}, u32[]{:S(2)}) collective-permute-start(f32[32,1024]{1,0:T(8,128)S(1)} %collective-permute-done.12), channel_id=1, source_target_pairs={{0,1},{1,0},{2,3},{3,2},{4,5},{5,4},{6,7},{7,6},{8,9},{9,8},{10,11... | collective-permute-start | bytes 393224 | tf_op jit(solution)/shard_map/ppermute | solution.py:19
  42.2 5.7 %collective-permute-start.15 = (f32[32,1024]{1,0:T(8,128)S(1)}, f32[32,1024]{1,0:T(8,128)S(1)}, u32[]{:S(2)}, u32[]{:S(2)}) collective-permute-start(f32[32,1024]{1,0:T(8,128)S(1)} %get-tuple-element.39), channel_id=1, source_target_pairs={{0,2},{1,3},{2,0},{3,1},{4,6},{5,7},{6,4},{7,5},{8,10},{9,11},{10,... | collective-permute-start | bytes 393224 | tf_op jit(solution)/shard_map/ppermute | solution.py:19
  43.4 1.3 %collective-permute-start.14 = (f32[32,1024]{1,0:T(8,128)S(1)}, f32[32,1024]{1,0:T(8,128)S(1)}, u32[]{:S(2)}, u32[]{:S(2)}) collective-permute-start(f32[32,1024]{1,0:T(8,128)S(1)} %get-tuple-element.39), channel_id=1, source_target_pairs={{0,1},{1,0},{2,3},{3,2},{4,5},{5,4},{6,7},{7,6},{8,9},{9,8},{10,11... | collective-permute-start | bytes 393224 | tf_op jit(solution)/shard_map/ppermute | solution.py:19
  47.9 1.3 %collective-permute-start.16 = (f32[32,1024]{1,0:T(8,128)S(1)}, f32[32,1024]{1,0:T(8,128)S(1)}, u32[]{:S(2)}, u32[]{:S(2)}) collective-permute-start(f32[32,1024]{1,0:T(8,128)S(1)} %collective-permute-done.15), channel_id=1, source_target_pairs={{0,1},{1,0},{2,3},{3,2},{4,5},{5,4},{6,7},{7,6},{8,9},{9,8},{10,11... | collective-permute-start | bytes 393224 | tf_op jit(solution)/shard_map/ppermute | solution.py:19
  50.9 3.6 %collective-permute-start.17 = (f32[32]{0:T(128)S(1)}, f32[32]{0:T(128)S(1)}, u32[]{:S(2)}, u32[]{:S(2)}) collective-permute-start(f32[32]{0:T(128)S(1)} %get-tuple-element.36), channel_id=1, source_target_pairs={{0,2},{1,3},{2,0},{3,1},{4,6},{5,7},{6,4},{7,5},{8,10},{9,11},{10,... | collective-permute-start | bytes 392 | tf_op jit(solution)/shard_map/ppermute | solution.py:19
  54.5 1.1 %collective-permute-start.18 = (f32[32]{0:T(128)S(1)}, f32[32]{0:T(128)S(1)}, u32[]{:S(2)}, u32[]{:S(2)}) collective-permute-start(f32[32]{0:T(128)S(1)} %add.113), channel_id=1, source_target_pairs={{0,1},{1,0},{2,3},{3,2},{4,5},{5,4},{6,7},{7,6},{8,9},{9,8},{10,11... | collective-permute-start | bytes 392 | tf_op jit(solution)/shard_map/ppermute | solution.py:19

commit v13 on v9

--- a/solution.py
+++ b/solution.py
@@ -69,23 +69,38 @@
     mid, rest = halve(rest)
     twice = jnp.concatenate([high, mid], axis=0)
     thrice = jnp.concatenate([high, mid, rest.astype(jnp.bfloat16)], axis=0)
-    for top in range(0, total, block):
-        down = slice(top, top + block)
-        left = jnp.transpose(operands(rows_ref[:, down] * scale_ref[...])[0])
-        for at in range(0, cols, step):
-            here = slice(at, at + step)
-            power = jnp.dot(left, right_ref[:, here], preferred_element_type=jnp.float32)
-            high, rest = halve(jnp.exp2(power))
-            low = rest.astype(jnp.bfloat16)
-            tile_ref[down, here] = high
-            tile_ref[total + top : total + top + block, here] = low
-            large = jnp.dot(thrice[:, down], high, preferred_element_type=jnp.float32)
-            small = jnp.dot(twice[:, down], low, preferred_element_type=jnp.float32)
-            term = large[:probes] + (
-                (large[probes : 2 * probes] + small[:probes]) + (large[2 * probes :] + small[probes:])
-            )
-            before = sum_ref if top == 0 else out_ref
-            out_ref[:, here] = before[:, here] + term
+    steps = [(top, at) for top in range(0, total, block) for at in range(0, cols, step)]
+    lefts, powers, parts = {}, {}, {}
+
+    def contract(top, at):
+        if top not in lefts:
+            lefts[top] = jnp.transpose(operands(rows_ref[:, top : top + block] * scale_ref[...])[0])
+        powers[top, at] = jnp.dot(lefts[top], right_ref[:, at : at + step], preferred_element_type=jnp.float32)
+
+    def raise_power(top, at):
+        high, rest = halve(jnp.exp2(powers.pop((top, at))))
+        low = rest.astype(jnp.bfloat16)
+        tile_ref[top : top + block, at : at + step] = high
+        tile_ref[total + top : total + top + block, at : at + step] = low
+        parts[top, at] = high, low
+
+    def apply(top, at):
+        down, here = slice(top, top + block), slice(at, at + step)
+        high, low = parts.pop((top, at))
+        large = jnp.dot(thrice[:, down], high, preferred_element_type=jnp.float32)
+        small = jnp.dot(twice[:, down], low, preferred_element_type=jnp.float32)
+        term = large[:probes] + ((large[probes : 2 * probes] + small[:probes]) + (large[2 * probes :] + small[probes:]))
+        before = sum_ref if top == 0 else out_ref
+        out_ref[:, here] = before[:, here] + term
+
+    contract(*steps[0])
+    for k, chunk in enumerate(steps):
+        if k + 1 < len(steps):
+            contract(*steps[k + 1])
+        raise_power(*chunk)
+        if k:
+            apply(*steps[k - 1])
+    apply(*steps[-1])
 
 
 def call(kernel, outs, *args, **cost):

time: 56.5 us -> 56.2 us (level)
  Pallas kernels: 6.97 us -> 6.36 us
    pallas_call x5, Pallas kernels: 6.97 us -> 6.36 us  [call(): pl.pallas_call(kernel, out_shape=outs, in_specs=[whole] * len(args), out_...]
where the time goes in v13:
time: 56.2 us; the launch traced here: 56 us
  waiting for transfers between devices  20 us (36%)
  starting transfers between devices  14 us (25%)
  matrix products  9.65 us (17%)
  Pallas kernels  6.36 us (11%)
  other arithmetic  4.94 us (9%)
  between operations  0.85 us (2%)
    ppermute x16, waiting for transfers between devices, swap(): return lax.ppermute(x, 'blk', [(i, i ^ stride) for i in range(n)])  20 us
    ppermute x16, starting transfers between devices, swap(): return lax.ppermute(x, 'blk', [(i, i ^ stride) for i in range(n)])  14 us
    dot_general x12, matrix products, apply_piece(): jnp.dot(jnp.concatenate([left, right], axis=1), piece, preferred_element_...  9.65 us
    pallas_call x5, Pallas kernels, call(): pl.pallas_call(kernel, out_shape=outs, in_specs=[whole] * len(args), out_...  6.36 us
  transfers between devices with their start and end apart: 16, of which 14 were waited for; matrix products, arithmetic and copies ran while one was open for 15% of the time, Pallas kernels for 9%

profile of v13, /device:TPU:0, one launch (start us, length us, event | category | flops | bytes accessed | tf_op | source)
XLA Modules:
  0.0 56.0 jit_solution(18390173883891329563)
XLA Ops:
  0.6 0.8 %pad_maximum_fusion.17 = f32[65,256]{1,0:T(8,128)S(1)} fusion(f32[1,256]{1,0:T(1,128)} %bitcast.20, f32[32,256]{1,0:T(8,128)} %param.7, f32[32,256]{1,0:T(8,128)} %param.4), kind=kLoop, calls=%fused_computation.242 | loop fusion | flops 33280 | bytes 133120 | tf_op jit(solution)/shard_map/concatenate | solution.py:152
  1.4 4.0 %collective-permute-start = (f32[65,256]{1,0:T(8,128)S(1)}, f32[65,256]{1,0:T(8,128)S(1)}, u32[]{:S(2)}, u32[]{:S(2)}) collective-permute-start(f32[65,256]{1,0:T(8,128)S(1)} %pad_maximum_fusion.17), channel_id=1, source_target_pairs={{0,8},{1,9},{2,10},{3,11},{4,12},{5,13},{6,14},{7,15},{8,0},{9,1},... | collective-permute-start | bytes 199688 | tf_op jit(solution)/shard_map/ppermute | solution.py:19
  5.5 3.9 %collective-permute-done = f32[65,256]{1,0:T(8,128)S(1)} collective-permute-done((f32[65,256]{1,0:T(8,128)S(1)}, f32[65,256]{1,0:T(8,128)S(1)}, u32[]{:S(2)}, u32[]{:S(2)}) %collective-permute-start) | collective-permute-done | bytes 66592 | tf_op jit(solution)/shard_map/ppermute | solution.py:19
  9.4 0.7 %collective-permute-start.1 = (f32[65,512]{1,0:T(8,128)S(1)}, f32[65,512]{1,0:T(8,128)S(1)}, u32[]{:S(2)}, u32[]{:S(2)}) collective-permute-start(f32[65,512]{1,0:T(8,128)S(1)} %pad_maximum_fusion.16), channel_id=1, source_target_pairs={{0,4},{1,5},{2,6},{3,7},{4,0},{5,1},{6,2},{7,3},{8,12},{9,13},{10,... | collective-permute-start | bytes 399368 | tf_op jit(solution)/shard_map/ppermute | solution.py:19
  10.9 3.7 %collective-permute-done.1 = f32[65,512]{1,0:T(8,128)S(1)} collective-permute-done((f32[65,512]{1,0:T(8,128)S(1)}, f32[65,512]{1,0:T(8,128)S(1)}, u32[]{:S(2)}, u32[]{:S(2)}) %collective-permute-start.1) | collective-permute-done | bytes 133152 | tf_op jit(solution)/shard_map/ppermute | solution.py:19
  14.7 1.8 %collective-permute-start.3 = (f32[64,1024]{1,0:T(8,128)S(1)}, f32[64,1024]{1,0:T(8,128)S(1)}, u32[]{:S(2)}, u32[]{:S(2)}) collective-permute-start(f32[64,1024]{1,0:T(8,128)S(1)} %slice.110), channel_id=1, source_target_pairs={{0,2},{1,3},{2,0},{3,1},{4,6},{5,7},{6,4},{7,5},{8,10},{9,11},{10,... | collective-permute-start | bytes 786440 | tf_op jit(solution)/shard_map/ppermute | solution.py:19
  16.6 1.6 %shard_map.60 = (bf16[2048,1024]{1,0:T(8,128)(2,1)S(1)}, f32[32,1024]{1,0:T(8,128)S(1)}) custom-call(f32[32,1024]{1,0:T(8,128)S(1)} %get-tuple-element.37.mine_ref.rows_ref, f32[32,1024]{1,0:T(8,128)S(1)} %get-tuple-element.38.vectors_ref, f32[32,1]{1,0:T(8,128)S(1)} %copy.10.scale_ref, bf16[256,1024]{1,0:T(8,128)(2,1)S(1)} %shard_map.59.right_ref, ...), custom_call_target="tpu_custom_call" | custom-call | flops 872415232 | bytes 4194304 | tf_op jit(solution)/shard_map/pallas_call | solution.py:108
  18.2 1.6 %shard_map.61 = (bf16[2048,1024]{1,0:T(8,128)(2,1)S(1)}, f32[32,1024]{1,0:T(8,128)S(1)}) custom-call(f32[32,1024]{1,0:T(8,128)S(1)} %get-tuple-element.40.rows_ref, f32[32,1024]{1,0:T(8,128)S(1)} %get-tuple-element.39.vectors_ref, f32[32,1]{1,0:T(8,128)S(1)} %copy.10.scale_ref, bf16[256,1024]{1,0:T(8,128)(2,1)S(1)} %shard_map.59.right_ref, ...), custom_call_target="tpu_custom_call" | custom-call | flops 872415232 | bytes 4194304 | tf_op jit(solution)/shard_map/pallas_call | solution.py:108
  19.8 1.3 %collective-permute-done.3 = f32[64,1024]{1,0:T(8,128)S(1)} collective-permute-done((f32[64,1024]{1,0:T(8,128)S(1)}, f32[64,1024]{1,0:T(8,128)S(1)}, u32[]{:S(2)}, u32[]{:S(2)}) %collective-permute-start.3) | collective-permute-done | bytes 262176 | tf_op jit(solution)/shard_map/ppermute | solution.py:19
  21.1 1.5 %shard_map.62 = (bf16[2048,1024]{1,0:T(8,128)(2,1)S(1)}, f32[32,1024]{1,0:T(8,128)S(1)}) custom-call(f32[32,1024]{1,0:T(8,128)S(1)} %get-tuple-element.42.rows_ref, f32[32,1024]{1,0:T(8,128)S(1)} %get-tuple-element.41.vectors_ref, f32[32,1]{1,0:T(8,128)S(1)} %copy.10.scale_ref, bf16[256,1024]{1,0:T(8,128)(2,1)S(1)} %shard_map.59.right_ref, ...), custom_call_target="tpu_custom_call" | custom-call | flops 872415232 | bytes 4194304 | tf_op jit(solution)/shard_map/pallas_call | solution.py:108
  22.7 1.6 %shard_map.63 = (bf16[2048,1024]{1,0:T(8,128)(2,1)S(1)}, f32[32,1024]{1,0:T(8,128)S(1)}) custom-call(f32[32,1024]{1,0:T(8,128)S(1)} %get-tuple-element.44.rows_ref, f32[32,1024]{1,0:T(8,128)S(1)} %get-tuple-element.43.vectors_ref, f32[32,1]{1,0:T(8,128)S(1)} %copy.10.scale_ref, bf16[256,1024]{1,0:T(8,128)(2,1)S(1)} %shard_map.59.right_ref, ...), custom_call_target="tpu_custom_call" | custom-call | flops 872415232 | bytes 4194304 | tf_op jit(solution)/shard_map/pallas_call | solution.py:108
  24.3 1.8 %collective-permute-start.6 = (f32[32,1024]{1,0:T(8,128)S(1)}, f32[32,1024]{1,0:T(8,128)S(1)}, u32[]{:S(2)}, u32[]{:S(2)}) collective-permute-start(f32[32,1024]{1,0:T(8,128)S(1)} %get-tuple-element.13), channel_id=1, source_target_pairs={{0,2},{1,3},{2,0},{3,1},{4,6},{5,7},{6,4},{7,5},{8,10},{9,11},{10,... | collective-permute-start | bytes 393224 | tf_op jit(solution)/shard_map/ppermute | solution.py:19
  26.4 0.8 %fusion.1 = f32[96,1024]{1,0:T(8,128)S(1)} fusion(bf16[2048,1024]{1,0:T(8,128)(2,1)S(1)} %get-tuple-element.14, bf16[32,1024]{1,0:T(8,128)(2,1)S(1)} %broadcast.4, bf16[32,1024]{1,0:T(8,128)(2,1)S(1)} %get-tuple-element.80, bf16[32,1024]{1,0:T(8,128)(2,1)S(1)} %get-tuple-element.81, bf16[32,1024]{1,0:T(8,128)(2,1)S(1)} %get-tuple-element.79), kind=kOutput, calls=%fused_computation.38 | convolution fusion | flops 405012480 | bytes 4849664 | tf_op jit(solution)/shard_map/dot_general | solution.py:129
  27.5 0.8 %convolution_add_fusion.8 = f32[96,1024]{1,0:T(8,128)S(1)} fusion(f32[96,1024]{1,0:T(8,128)S(1)} %fusion.1, bf16[2048,1024]{1,0:T(8,128)(2,1)S(1)} %get-tuple-element.15, bf16[32,1024]{1,0:T(8,128)(2,1)S(1)} %broadcast.4, bf16[32,1024]{1,0:T(8,128)(2,1)S(1)} %get-tuple-element.76, bf16[32,1024]{1,0:T(8,128)(2,1)S(1)} %get-tuple-element.77, ...), kind=kOutput, calls=%fused_computation.20 | convolution fusion | flops 405110784 | bytes 5242880 | tf_op jit(solution)/shard_map/dot_general | solution.py:129
  28.3 2.0 %collective-permute-done.6 = f32[32,1024]{1,0:T(8,128)S(1)} collective-permute-done((f32[32,1024]{1,0:T(8,128)S(1)}, f32[32,1024]{1,0:T(8,128)S(1)}, u32[]{:S(2)}, u32[]{:S(2)}) %collective-permute-start.6) | collective-permute-done | bytes 131104 | tf_op jit(solution)/shard_map/ppermute | solution.py:19
  30.3 0.8 %convolution_add_fusion.7 = f32[96,1024]{1,0:T(8,128)S(1)} fusion(f32[96,1024]{1,0:T(8,128)S(1)} %convolution_add_fusion.8, bf16[2048,1024]{1,0:T(8,128)(2,1)S(1)} %get-tuple-element.16, bf16[32,1024]{1,0:T(8,128)(2,1)S(1)} %broadcast.4, bf16[32,1024]{1,0:T(8,128)(2,1)S(1)} %get-tuple-element.72, bf16[32,1024]{1,0:T(8,128)(2,1)S(1)} %get-tuple-element.73, ...), kind=kOutput, calls=%fused_computation.19 | convolution fusion | flops 405110784 | bytes 5242880 | tf_op jit(solution)/shard_map/dot_general | solution.py:129
  31.6 0.8 %convolution_add_fusion.6 = f32[96,1024]{1,0:T(8,128)S(1)} fusion(f32[96,1024]{1,0:T(8,128)S(1)} %convolution_add_fusion.7, bf16[2048,1024]{1,0:T(8,128)(2,1)S(1)} %get-tuple-element.17, bf16[32,1024]{1,0:T(8,128)(2,1)S(1)} %broadcast.4, bf16[32,1024]{1,0:T(8,128)(2,1)S(1)} %get-tuple-element.68, bf16[32,1024]{1,0:T(8,128)(2,1)S(1)} %get-tuple-element.69, ...), kind=kOutput, calls=%fused_computation.18 | convolution fusion | flops 405110784 | bytes 5242880 | tf_op jit(solution)/shard_map/dot_general | solution.py:129
  33.1 1.8 %collective-permute-start.9 = (f32[32,1024]{1,0:T(8,128)S(1)}, f32[32,1024]{1,0:T(8,128)S(1)}, u32[]{:S(2)}, u32[]{:S(2)}) collective-permute-start(f32[32,1024]{1,0:T(8,128)S(1)} %get-tuple-element.32), channel_id=1, source_target_pairs={{0,2},{1,3},{2,0},{3,1},{4,6},{5,7},{6,4},{7,5},{8,10},{9,11},{10,... | collective-permute-start | bytes 393224 | tf_op jit(solution)/shard_map/ppermute | solution.py:19
  34.9 0.8 %fusion.10 = f32[96,1024]{1,0:T(8,128)S(1)} fusion(bf16[2048,1024]{1,0:T(8,128)(2,1)S(1)} %get-tuple-element.14, bf16[32,1024]{1,0:T(8,128)(2,1)S(1)} %broadcast.4, bf16[32,1024]{1,0:T(8,128)(2,1)S(1)} %get-tuple-element.66, bf16[32,1024]{1,0:T(8,128)(2,1)S(1)} %get-tuple-element.65, bf16[32,1024]{1,0:T(8,128)(2,1)S(1)} %get-tuple-element.31), kind=kOutput, calls=%fused_computation.43 | convolution fusion | flops 405012480 | bytes 4849664 | tf_op jit(solution)/shard_map/dot_general | solution.py:129
  36.3 0.8 %convolution_add_fusion.5 = f32[96,1024]{1,0:T(8,128)S(1)} fusion(f32[96,1024]{1,0:T(8,128)S(1)} %fusion.10, bf16[2048,1024]{1,0:T(8,128)(2,1)S(1)} %get-tuple-element.15, bf16[32,1024]{1,0:T(8,128)(2,1)S(1)} %broadcast.4, bf16[32,1024]{1,0:T(8,128)(2,1)S(1)} %get-tuple-element.63, bf16[32,1024]{1,0:T(8,128)(2,1)S(1)} %get-tuple-element.64, ...), kind=kOutput, calls=%fused_computation.17 | convolution fusion | flops 405110784 | bytes 5242880 | tf_op jit(solution)/shard_map/dot_general | solution.py:129
  37.1 1.6 %collective-permute-done.9 = f32[32,1024]{1,0:T(8,128)S(1)} collective-permute-done((f32[32,1024]{1,0:T(8,128)S(1)}, f32[32,1024]{1,0:T(8,128)S(1)}, u32[]{:S(2)}, u32[]{:S(2)}) %collective-permute-start.9) | collective-permute-done | bytes 131104 | tf_op jit(solution)/shard_map/ppermute | solution.py:19
  38.7 0.8 %convolution_add_fusion.4 = f32[96,1024]{1,0:T(8,128)S(1)} fusion(f32[96,1024]{1,0:T(8,128)S(1)} %convolution_add_fusion.5, bf16[2048,1024]{1,0:T(8,128)(2,1)S(1)} %get-tuple-element.16, bf16[32,1024]{1,0:T(8,128)(2,1)S(1)} %broadcast.4, bf16[32,1024]{1,0:T(8,128)(2,1)S(1)} %get-tuple-element.60, bf16[32,1024]{1,0:T(8,128)(2,1)S(1)} %get-tuple-element.61, ...), kind=kOutput, calls=%fused_computation.16 | convolution fusion | flops 405110784 | bytes 5242880 | tf_op jit(solution)/shard_map/dot_general | solution.py:129
  40.1 0.8 %convolution_add_fusion.3 = f32[96,1024]{1,0:T(8,128)S(1)} fusion(f32[96,1024]{1,0:T(8,128)S(1)} %convolution_add_fusion.4, bf16[2048,1024]{1,0:T(8,128)(2,1)S(1)} %get-tuple-element.17, bf16[32,1024]{1,0:T(8,128)(2,1)S(1)} %broadcast.4, bf16[32,1024]{1,0:T(8,128)(2,1)S(1)} %get-tuple-element.57, bf16[32,1024]{1,0:T(8,128)(2,1)S(1)} %get-tuple-element.58, ...), kind=kOutput, calls=%fused_computation.15 | convolution fusion | flops 405110784 | bytes 5242880 | tf_op jit(solution)/shard_map/dot_general | solution.py:129
  41.8 1.8 %collective-permute-start.12 = (f32[32,1024]{1,0:T(8,128)S(1)}, f32[32,1024]{1,0:T(8,128)S(1)}, u32[]{:S(2)}, u32[]{:S(2)}) collective-permute-start(f32[32,1024]{1,0:T(8,128)S(1)} %get-tuple-element.23), channel_id=1, source_target_pairs={{0,2},{1,3},{2,0},{3,1},{4,6},{5,7},{6,4},{7,5},{8,10},{9,11},{10,... | collective-permute-start | bytes 393224 | tf_op jit(solution)/shard_map/ppermute | solution.py:19
  43.6 0.8 %fusion.19 = f32[96,1024]{1,0:T(8,128)S(1)} fusion(bf16[2048,1024]{1,0:T(8,128)(2,1)S(1)} %get-tuple-element.14, bf16[32,1024]{1,0:T(8,128)(2,1)S(1)} %broadcast.4, bf16[32,1024]{1,0:T(8,128)(2,1)S(1)} %get-tuple-element.55, bf16[32,1024]{1,0:T(8,128)(2,1)S(1)} %get-tuple-element.54, bf16[32,1024]{1,0:T(8,128)(2,1)S(1)} %get-tuple-element.22), kind=kOutput, calls=%fused_computation.48 | convolution fusion | flops 405012480 | bytes 4849664 | tf_op jit(solution)/shard_map/dot_general | solution.py:129
  45.0 0.8 %convolution_add_fusion.2 = f32[96,1024]{1,0:T(8,128)S(1)} fusion(f32[96,1024]{1,0:T(8,128)S(1)} %fusion.19, bf16[2048,1024]{1,0:T(8,128)(2,1)S(1)} %get-tuple-element.15, bf16[32,1024]{1,0:T(8,128)(2,1)S(1)} %broadcast.4, bf16[32,1024]{1,0:T(8,128)(2,1)S(1)} %get-tuple-element.52, bf16[32,1024]{1,0:T(8,128)(2,1)S(1)} %get-tuple-element.53, ...), kind=kOutput, calls=%fused_computation.14 | convolution fusion | flops 405110784 | bytes 5242880 | tf_op jit(solution)/shard_map/dot_general | solution.py:129
  45.8 1.6 %collective-permute-done.12 = f32[32,1024]{1,0:T(8,128)S(1)} collective-permute-done((f32[32,1024]{1,0:T(8,128)S(1)}, f32[32,1024]{1,0:T(8,128)S(1)}, u32[]{:S(2)}, u32[]{:S(2)}) %collective-permute-start.12) | collective-permute-done | bytes 131104 | tf_op jit(solution)/shard_map/ppermute | solution.py:19
  47.5 0.8 %convolution_add_fusion.1 = f32[96,1024]{1,0:T(8,128)S(1)} fusion(f32[96,1024]{1,0:T(8,128)S(1)} %convolution_add_fusion.2, bf16[2048,1024]{1,0:T(8,128)(2,1)S(1)} %get-tuple-element.16, bf16[32,1024]{1,0:T(8,128)(2,1)S(1)} %broadcast.4, bf16[32,1024]{1,0:T(8,128)(2,1)S(1)} %get-tuple-element.49, bf16[32,1024]{1,0:T(8,128)(2,1)S(1)} %get-tuple-element.50, ...), kind=kOutput, calls=%fused_computation.13 | convolution fusion | flops 405110784 | bytes 5242880 | tf_op jit(solution)/shard_map/dot_general | solution.py:129
  48.8 0.8 %convolution_add_fusion = f32[96,1024]{1,0:T(8,128)S(1)} fusion(f32[96,1024]{1,0:T(8,128)S(1)} %convolution_add_fusion.1, bf16[2048,1024]{1,0:T(8,128)(2,1)S(1)} %get-tuple-element.17, bf16[32,1024]{1,0:T(8,128)(2,1)S(1)} %broadcast.4, bf16[32,1024]{1,0:T(8,128)(2,1)S(1)} %get-tuple-element.46, bf16[32,1024]{1,0:T(8,128)(2,1)S(1)} %get-tuple-element.47, ...), kind=kOutput, calls=%fused_computation.12 | convolution fusion | flops 405110784 | bytes 5242880 | tf_op jit(solution)/shard_map/dot_general | solution.py:129
  50.5 1.8 %collective-permute-start.14 = (f32[32]{0:T(128)S(1)}, f32[32]{0:T(128)S(1)}, u32[]{:S(2)}, u32[]{:S(2)}) collective-permute-start(f32[32]{0:T(128)S(1)} %get-tuple-element.20), channel_id=1, source_target_pairs={{0,2},{1,3},{2,0},{3,1},{4,6},{5,7},{6,4},{7,5},{8,10},{9,11},{10,... | collective-permute-start | bytes 392 | tf_op jit(solution)/shard_map/ppermute | solution.py:19
  52.3 1.8 %collective-permute-done.14 = f32[32]{0:T(128)S(1)} collective-permute-done((f32[32]{0:T(128)S(1)}, f32[32]{0:T(128)S(1)}, u32[]{:S(2)}, u32[]{:S(2)}) %collective-permute-start.14) | collective-permute-done | bytes 160 | tf_op jit(solution)/shard_map/ppermute | solution.py:19
  54.1 1.1 %collective-permute-done.15 = f32[32]{0:T(128)S(1)} collective-permute-done((f32[32]{0:T(128)S(1)}, f32[32]{0:T(128)S(1)}, u32[]{:S(2)}, u32[]{:S(2)}) %collective-permute-start.15) | collective-permute-done | bytes 160 | tf_op jit(solution)/shard_map/ppermute | solution.py:19
  (60 shorter events, 7.6 us)
Async XLA Ops:
  1.4 7.9 %collective-permute-start = (f32[65,256]{1,0:T(8,128)S(1)}, f32[65,256]{1,0:T(8,128)S(1)}, u32[]{:S(2)}, u32[]{:S(2)}) collective-permute-start(f32[65,256]{1,0:T(8,128)S(1)} %pad_maximum_fusion.17), channel_id=1, source_target_pairs={{0,8},{1,9},{2,10},{3,11},{4,12},{5,13},{6,14},{7,15},{8,0},{9,1},... | collective-permute-start | bytes 199688 | tf_op jit(solution)/shard_map/ppermute | solution.py:19
  9.4 5.2 %collective-permute-start.1 = (f32[65,512]{1,0:T(8,128)S(1)}, f32[65,512]{1,0:T(8,128)S(1)}, u32[]{:S(2)}, u32[]{:S(2)}) collective-permute-start(f32[65,512]{1,0:T(8,128)S(1)} %pad_maximum_fusion.16), channel_id=1, source_target_pairs={{0,4},{1,5},{2,6},{3,7},{4,0},{5,1},{6,2},{7,3},{8,12},{9,13},{10,... | collective-permute-start | bytes 399368 | tf_op jit(solution)/shard_map/ppermute | solution.py:19
  14.7 6.4 %collective-permute-start.3 = (f32[64,1024]{1,0:T(8,128)S(1)}, f32[64,1024]{1,0:T(8,128)S(1)}, u32[]{:S(2)}, u32[]{:S(2)}) collective-permute-start(f32[64,1024]{1,0:T(8,128)S(1)} %slice.110), channel_id=1, source_target_pairs={{0,2},{1,3},{2,0},{3,1},{4,6},{5,7},{6,4},{7,5},{8,10},{9,11},{10,... | collective-permute-start | bytes 786440 | tf_op jit(solution)/shard_map/ppermute | solution.py:19
  16.4 1.8 %collective-permute-start.2 = (f32[64,1024]{1,0:T(8,128)S(1)}, f32[64,1024]{1,0:T(8,128)S(1)}, u32[]{:S(2)}, u32[]{:S(2)}) collective-permute-start(f32[64,1024]{1,0:T(8,128)S(1)} %slice.110), channel_id=1, source_target_pairs={{0,1},{1,0},{2,3},{3,2},{4,5},{5,4},{6,7},{7,6},{8,9},{9,8},{10,11... | collective-permute-start | bytes 786440 | tf_op jit(solution)/shard_map/ppermute | solution.py:19
  21.1 1.6 %collective-permute-start.4 = (f32[64,1024]{1,0:T(8,128)S(1)}, f32[64,1024]{1,0:T(8,128)S(1)}, u32[]{:S(2)}, u32[]{:S(2)}) collective-permute-start(f32[64,1024]{1,0:T(8,128)S(1)} %collective-permute-done.3), channel_id=1, source_target_pairs={{0,1},{1,0},{2,3},{3,2},{4,5},{5,4},{6,7},{7,6},{8,9},{9,8},{10,11... | collective-permute-start | bytes 786440 | tf_op jit(solution)/shard_map/ppermute | solution.py:19
  24.3 6.0 %collective-permute-start.6 = (f32[32,1024]{1,0:T(8,128)S(1)}, f32[32,1024]{1,0:T(8,128)S(1)}, u32[]{:S(2)}, u32[]{:S(2)}) collective-permute-start(f32[32,1024]{1,0:T(8,128)S(1)} %get-tuple-element.13), channel_id=1, source_target_pairs={{0,2},{1,3},{2,0},{3,1},{4,6},{5,7},{6,4},{7,5},{8,10},{9,11},{10,... | collective-permute-start | bytes 393224 | tf_op jit(solution)/shard_map/ppermute | solution.py:19
  26.1 1.3 %collective-permute-start.5 = (f32[32,1024]{1,0:T(8,128)S(1)}, f32[32,1024]{1,0:T(8,128)S(1)}, u32[]{:S(2)}, u32[]{:S(2)}) collective-permute-start(f32[32,1024]{1,0:T(8,128)S(1)} %get-tuple-element.13), channel_id=1, source_target_pairs={{0,1},{1,0},{2,3},{3,2},{4,5},{5,4},{6,7},{7,6},{8,9},{9,8},{10,11... | collective-permute-start | bytes 393224 | tf_op jit(solution)/shard_map/ppermute | solution.py:19
  30.3 1.3 %collective-permute-start.7 = (f32[32,1024]{1,0:T(8,128)S(1)}, f32[32,1024]{1,0:T(8,128)S(1)}, u32[]{:S(2)}, u32[]{:S(2)}) collective-permute-start(f32[32,1024]{1,0:T(8,128)S(1)} %collective-permute-done.6), channel_id=1, source_target_pairs={{0,1},{1,0},{2,3},{3,2},{4,5},{5,4},{6,7},{7,6},{8,9},{9,8},{10,11... | collective-permute-start | bytes 393224 | tf_op jit(solution)/shard_map/ppermute | solution.py:19
  33.1 5.6 %collective-permute-start.9 = (f32[32,1024]{1,0:T(8,128)S(1)}, f32[32,1024]{1,0:T(8,128)S(1)}, u32[]{:S(2)}, u32[]{:S(2)}) collective-permute-start(f32[32,1024]{1,0:T(8,128)S(1)} %get-tuple-element.32), channel_id=1, source_target_pairs={{0,2},{1,3},{2,0},{3,1},{4,6},{5,7},{6,4},{7,5},{8,10},{9,11},{10,... | collective-permute-start | bytes 393224 | tf_op jit(solution)/shard_map/ppermute | solution.py:19
  34.9 1.3 %collective-permute-start.8 = (f32[32,1024]{1,0:T(8,128)S(1)}, f32[32,1024]{1,0:T(8,128)S(1)}, u32[]{:S(2)}, u32[]{:S(2)}) collective-permute-start(f32[32,1024]{1,0:T(8,128)S(1)} %get-tuple-element.32), channel_id=1, source_target_pairs={{0,1},{1,0},{2,3},{3,2},{4,5},{5,4},{6,7},{7,6},{8,9},{9,8},{10,11... | collective-permute-start | bytes 393224 | tf_op jit(solution)/shard_map/ppermute | solution.py:19
  38.7 1.3 %collective-permute-start.10 = (f32[32,1024]{1,0:T(8,128)S(1)}, f32[32,1024]{1,0:T(8,128)S(1)}, u32[]{:S(2)}, u32[]{:S(2)}) collective-permute-start(f32[32,1024]{1,0:T(8,128)S(1)} %collective-permute-done.9), channel_id=1, source_target_pairs={{0,1},{1,0},{2,3},{3,2},{4,5},{5,4},{6,7},{7,6},{8,9},{9,8},{10,11... | collective-permute-start | bytes 393224 | tf_op jit(solution)/shard_map/ppermute | solution.py:19
  41.8 5.6 %collective-permute-start.12 = (f32[32,1024]{1,0:T(8,128)S(1)}, f32[32,1024]{1,0:T(8,128)S(1)}, u32[]{:S(2)}, u32[]{:S(2)}) collective-permute-start(f32[32,1024]{1,0:T(8,128)S(1)} %get-tuple-element.23), channel_id=1, source_target_pairs={{0,2},{1,3},{2,0},{3,1},{4,6},{5,7},{6,4},{7,5},{8,10},{9,11},{10,... | collective-permute-start | bytes 393224 | tf_op jit(solution)/shard_map/ppermute | solution.py:19
  43.6 1.3 %collective-permute-start.11 = (f32[32,1024]{1,0:T(8,128)S(1)}, f32[32,1024]{1,0:T(8,128)S(1)}, u32[]{:S(2)}, u32[]{:S(2)}) collective-permute-start(f32[32,1024]{1,0:T(8,128)S(1)} %get-tuple-element.23), channel_id=1, source_target_pairs={{0,1},{1,0},{2,3},{3,2},{4,5},{5,4},{6,7},{7,6},{8,9},{9,8},{10,11... | collective-permute-start | bytes 393224 | tf_op jit(solution)/shard_map/ppermute | solution.py:19
  47.4 1.3 %collective-permute-start.13 = (f32[32,1024]{1,0:T(8,128)S(1)}, f32[32,1024]{1,0:T(8,128)S(1)}, u32[]{:S(2)}, u32[]{:S(2)}) collective-permute-start(f32[32,1024]{1,0:T(8,128)S(1)} %collective-permute-done.12), channel_id=1, source_target_pairs={{0,1},{1,0},{2,3},{3,2},{4,5},{5,4},{6,7},{7,6},{8,9},{9,8},{10,11... | collective-permute-start | bytes 393224 | tf_op jit(solution)/shard_map/ppermute | solution.py:19
  50.5 3.6 %collective-permute-start.14 = (f32[32]{0:T(128)S(1)}, f32[32]{0:T(128)S(1)}, u32[]{:S(2)}, u32[]{:S(2)}) collective-permute-start(f32[32]{0:T(128)S(1)} %get-tuple-element.20), channel_id=1, source_target_pairs={{0,2},{1,3},{2,0},{3,1},{4,6},{5,7},{6,4},{7,5},{8,10},{9,11},{10,... | collective-permute-start | bytes 392 | tf_op jit(solution)/shard_map/ppermute | solution.py:19
  54.1 1.1 %collective-permute-start.15 = (f32[32]{0:T(128)S(1)}, f32[32]{0:T(128)S(1)}, u32[]{:S(2)}, u32[]{:S(2)}) collective-permute-start(f32[32]{0:T(128)S(1)} %add.113), channel_id=1, source_target_pairs={{0,1},{1,0},{2,3},{3,2},{4,5},{5,4},{6,7},{7,6},{8,9},{9,8},{10,11... | collective-permute-start | bytes 392 | tf_op jit(solution)/shard_map/ppermute | solution.py:19

commit v14 on v13

--- a/solution.py
+++ b/solution.py
@@ -1,3 +1,4 @@
+import functools
 import math
 
 import jax
@@ -120,6 +121,66 @@
     outs = (jax.ShapeDtypeStruct((2 * count, cols), jnp.bfloat16), jax.ShapeDtypeStruct(total.shape, jnp.float32))
     cost = dict(flops=2 * count * cols * 416, bytes_accessed=4 * count * cols, transcendentals=count * cols)
     return call(build_kernel, outs, rows, vectors, scale, right, total, **cost)
+
+
+def finish_kernel(count, last, *refs):
+    came = refs[:count]
+    tile_ref, sum_ref, noise_ref, norm_ref, residual_ref, direction_ref, image_ref, solution_ref = refs[count : count + 8]
+    new_norm, new_residual, new_direction, new_solution, new_applied, extra = refs[count + 8 :]
+    probes, cols = image_ref.shape
+    width, size, step = solution_ref.shape[1], came[-1].shape[1], min(cols, 256)
+
+    high, rest = halve(came[-1][...])
+    mid, rest = halve(rest)
+    twice = jnp.concatenate([high, mid], axis=0)
+    thrice = jnp.concatenate([high, mid, rest.astype(jnp.bfloat16)], axis=0)
+    terms = []
+    for at in range(0, cols, step):
+        here = slice(at, at + step)
+        large = sum_ref[:, here] + jnp.dot(thrice, tile_ref[:size, here], preferred_element_type=jnp.float32)
+        small = jnp.dot(twice, tile_ref[size:, here], preferred_element_type=jnp.float32)
+        terms.append(
+            large[:probes] + ((large[probes : 2 * probes] + small[:probes]) + (large[2 * probes :] + small[probes:]))
+        )
+
+    def over(pieces):
+        at = 0
+        for ref in pieces:
+            yield slice(at, at + ref.shape[1]), ref
+            at += ref.shape[1]
+
+    curve = sum(jnp.sum(direction_ref[:, here] * ref[...], axis=1, keepdims=True) for here, ref in over(came))
+    norm = norm_ref[...]
+    step_size = norm / curve
+    for here, ref in over(came):
+        new_residual[:, here] = residual_ref[:, here] - step_size * ref[...]
+    norm_next = sum(jnp.sum(new_residual[:, here] * new_residual[:, here], axis=1, keepdims=True) for here, _ in over(came))
+    new_norm[...] = norm_next
+    ratio = norm_next / norm
+    new_solution[...] = solution_ref[...] + step_size * direction_ref[:, :width]
+    for here, _ in over(came):
+        new_direction[:, here] = new_residual[:, here] + ratio * direction_ref[:, here]
+    inner = jnp.zeros_like(norm)
+    for at, term in zip(range(0, cols, step), terms):
+        here = slice(at, at + step)
+        mine = came[0][:, here]
+        image = image_ref[:, here] - step_size * (term + noise_ref[:, here] * mine)
+        applied = image + ratio * mine
+        new_applied[:, here] = applied
+        if last:
+            inner += jnp.sum(new_direction[:, here] * applied, axis=1, keepdims=True)
+        else:
+            extra[:, here] = image
+    if last:
+        extra[...] = inner
+
+
+def finish(last, came, tile, total, noise, norm, residual, direction, image, answer):
+    outs = (norm, residual, direction, answer, image, norm if last else image)
+    outs = tuple(jax.ShapeDtypeStruct(x.shape, jnp.float32) for x in outs)
+    args = (*came, tile, total, noise, norm, residual, direction, image, answer)
+    cost = dict(flops=2 * 96 * tile.size, bytes_accessed=2 * tile.size, transcendentals=0)
+    return call(functools.partial(finish_kernel, len(came), last), outs, *args, **cost)
 
 
 def apply_piece(vectors, piece):
@@ -172,32 +233,23 @@
             piece, my_applied = build_piece(x[:feats], start, scale, right, my_applied)
             tile.append(piece)
 
-        def operator(pieces):
+        def all_but_last(pieces):
             total = apply_piece(pieces[0], tile[0])
-            for x, piece in zip(pieces[1:], tile[1:]):
+            for x, piece in zip(pieces[1:-1], tile[1:-1]):
                 total = lax.optimization_barrier(total + apply_piece(x, piece))
-            return total[:probes] + (total[probes : 2 * probes] + total[2 * probes :]) + noise * pieces[0]
+            return total
 
         residual = direction = jnp.concatenate(starts, axis=1)
         my_solution = jnp.zeros_like(direction[:, :width])
-        norm_now = jnp.sum(residual * residual, axis=1)
+        norm = jnp.sum(residual * residual, axis=1, keepdims=True)
         my_image = my_applied
         for iteration in range(ITERS - 1):
-            pieces = arrivals(my_applied)
-            my_next = operator(pieces)
-            applied = jnp.concatenate(pieces, axis=1)
-            curve = jnp.sum(direction * applied, axis=1)
-            step_size = (norm_now / curve)[:, None]
-            my_solution = my_solution + step_size * direction[:, :width]
-            residual = residual - step_size * applied
-            norm_next = jnp.sum(residual * residual, axis=1)
-            ratio = (norm_next / norm_now)[:, None]
-            my_image = my_image - step_size * my_next
-            my_applied = my_image + ratio * my_applied
-            direction = residual + ratio * direction
-            norm_now = norm_next
-        curve = add_up(jnp.sum(direction[:, :cols] * my_applied, axis=1), n, inner)
-        step_size = (norm_now / curve)[:, None]
+            came, last = arrivals(my_applied), iteration == ITERS - 2
+            norm, residual, direction, my_solution, my_applied, extra = finish(
+                last, came, tile[-1], all_but_last(came), noise, norm, residual, direction, my_image, my_solution
+            )
+            my_image = extra
+        step_size = norm / add_up(extra, n, inner)
         my_solution = my_solution + step_size * direction[:, :width]
         return my_solution, residual[:, :width] - step_size * my_applied[:, :width]
 

time: 56.2 us -> 62.4 us (1.11)
  local copies, waits for them, and re-layouts: 0.17 us -> 7.41 us
  starting transfers between devices: 14 us -> 10.4 us
  Pallas kernels: 6.36 us -> 9.33 us
  other arithmetic: 4.94 us -> 2.78 us
  waiting for transfers between devices: 20 us -> 21.7 us
    unnamed x0 -> x16, local copies, waits for them, and re-layouts: none -> 7.15 us
    ppermute x16, starting transfers between devices: 14 us -> 10.4 us  [swap(): return lax.ppermute(x, 'blk', [(i, i ^ stride) for i in range(n)])]
    pallas_call x5 -> x8, Pallas kernels: 6.36 us -> 9.33 us  [call(): pl.pallas_call(kernel, out_shape=outs, in_specs=[whole] * len(args), out_...]
    reduce_sum x7 -> x0, other arithmetic: 1.96 us -> none  [the longest x3 0.93 us: body(): curve = jnp.sum(direction * applied, axis=1)]
    ppermute x16, waiting for transfers between devices: 20 us -> 21.7 us  [swap(): return lax.ppermute(x, 'blk', [(i, i ^ stride) for i in range(n)])]
    dot_general x12 -> x9, matrix products: 9.65 us -> 9.69 us  [apply_piece(): jnp.dot(jnp.concatenate([left, right], axis=1), piece, preferred_element_...]
  transfers between devices with their start and end apart: 16 -> 16, of which waited for: 14 -> 12; matrix products, arithmetic and copies ran while one was open for 15% -> 18% of each run, Pallas kernels for 9% -> 8%
where the time goes in v14:
time: 62.4 us; the launch traced here: 62.2 us
  waiting for transfers between devices  21.7 us (35%)
  starting transfers between devices  10.4 us (17%)
  matrix products  9.69 us (16%)
  Pallas kernels  9.33 us (15%)
  local copies, waits for them, and re-layouts  7.41 us (12%)
  other arithmetic  2.78 us (4%)
  between operations  0.91 us (1%)
    ppermute x16, waiting for transfers between devices, swap(): return lax.ppermute(x, 'blk', [(i, i ^ stride) for i in range(n)])  21.7 us
    ppermute x16, starting transfers between devices, swap(): return lax.ppermute(x, 'blk', [(i, i ^ stride) for i in range(n)])  10.4 us
    dot_general x9, matrix products, apply_piece(): jnp.dot(jnp.concatenate([left, right], axis=1), piece, preferred_element_...  9.69 us
    pallas_call x8, Pallas kernels, call(): pl.pallas_call(kernel, out_shape=outs, in_specs=[whole] * len(args), out_...  9.33 us
    unnamed x16, local copies, waits for them, and re-layouts  7.15 us
  transfers between devices with their start and end apart: 16, of which 12 were waited for; matrix products, arithmetic and copies ran while one was open for 18% of the time, Pallas kernels for 8%

profile of v14, /device:TPU:0, one launch (start us, length us, event | category | flops | bytes accessed | tf_op | source)
XLA Modules:
  0.0 62.2 jit_solution(16933862749892588283)
XLA Ops:
  0.6 0.8 %pad_maximum_fusion.12 = f32[65,256]{1,0:T(8,128)S(1)} fusion(f32[1,256]{1,0:T(1,128)} %bitcast.16, f32[32,256]{1,0:T(8,128)} %param.7, f32[32,256]{1,0:T(8,128)} %param.4), kind=kLoop, calls=%fused_computation.157 | loop fusion | flops 33280 | bytes 133120 | tf_op jit(solution)/shard_map/concatenate | solution.py:213
  1.4 4.0 %collective-permute-start = (f32[65,256]{1,0:T(8,128)S(1)}, f32[65,256]{1,0:T(8,128)S(1)}, u32[]{:S(2)}, u32[]{:S(2)}) collective-permute-start(f32[65,256]{1,0:T(8,128)S(1)} %pad_maximum_fusion.12), channel_id=1, source_target_pairs={{0,8},{1,9},{2,10},{3,11},{4,12},{5,13},{6,14},{7,15},{8,0},{9,1},... | collective-permute-start | bytes 199688 | tf_op jit(solution)/shard_map/ppermute | solution.py:20
  5.5 3.9 %collective-permute-done = f32[65,256]{1,0:T(8,128)S(1)} collective-permute-done((f32[65,256]{1,0:T(8,128)S(1)}, f32[65,256]{1,0:T(8,128)S(1)}, u32[]{:S(2)}, u32[]{:S(2)}) %collective-permute-start) | collective-permute-done | bytes 66592 | tf_op jit(solution)/shard_map/ppermute | solution.py:20
  9.4 0.7 %collective-permute-start.1 = (f32[65,512]{1,0:T(8,128)S(1)}, f32[65,512]{1,0:T(8,128)S(1)}, u32[]{:S(2)}, u32[]{:S(2)}) collective-permute-start(f32[65,512]{1,0:T(8,128)S(1)} %pad_maximum_fusion.11), channel_id=1, source_target_pairs={{0,4},{1,5},{2,6},{3,7},{4,0},{5,1},{6,2},{7,3},{8,12},{9,13},{10,... | collective-permute-start | bytes 399368 | tf_op jit(solution)/shard_map/ppermute | solution.py:20
  10.9 3.7 %collective-permute-done.1 = f32[65,512]{1,0:T(8,128)S(1)} collective-permute-done((f32[65,512]{1,0:T(8,128)S(1)}, f32[65,512]{1,0:T(8,128)S(1)}, u32[]{:S(2)}, u32[]{:S(2)}) %collective-permute-start.1) | collective-permute-done | bytes 133152 | tf_op jit(solution)/shard_map/ppermute | solution.py:20
  14.7 1.8 %collective-permute-start.2 = (f32[64,1024]{1,0:T(8,128)S(1)}, f32[64,1024]{1,0:T(8,128)S(1)}, u32[]{:S(2)}, u32[]{:S(2)}) collective-permute-start(f32[64,1024]{1,0:T(8,128)S(1)} %slice.55), channel_id=1, source_target_pairs={{0,2},{1,3},{2,0},{3,1},{4,6},{5,7},{6,4},{7,5},{8,10},{9,11},{10,... | collective-permute-start | bytes 786440 | tf_op jit(solution)/shard_map/ppermute | solution.py:20
  16.7 1.5 %shard_map.60 = (bf16[2048,1024]{1,0:T(8,128)(2,1)S(1)}, f32[32,1024]{1,0:T(8,128)S(1)}) custom-call(f32[32,1024]{1,0:T(8,128)S(1)} %get-tuple-element.58.mine_ref.rows_ref, f32[32,1024]{1,0:T(8,128)S(1)} %get-tuple-element.57.vectors_ref, f32[32,1]{1,0:T(8,128)S(1)} %copy.16.scale_ref, bf16[256,1024]{1,0:T(8,128)(2,1)S(1)} %shard_map.59.right_ref, ...), custom_call_target="tpu_custom_call" | custom-call | flops 872415232 | bytes 4194304 | tf_op jit(solution)/shard_map/pallas_call | solution.py:109
  18.3 1.6 %shard_map.61 = (bf16[2048,1024]{1,0:T(8,128)(2,1)S(1)}, f32[32,1024]{1,0:T(8,128)S(1)}) custom-call(f32[32,1024]{1,0:T(8,128)S(1)} %get-tuple-element.60.rows_ref, f32[32,1024]{1,0:T(8,128)S(1)} %get-tuple-element.59.vectors_ref, f32[32,1]{1,0:T(8,128)S(1)} %copy.16.scale_ref, bf16[256,1024]{1,0:T(8,128)(2,1)S(1)} %shard_map.59.right_ref, ...), custom_call_target="tpu_custom_call" | custom-call | flops 872415232 | bytes 4194304 | tf_op jit(solution)/shard_map/pallas_call | solution.py:109
  19.9 2.0 %copy-done.4 = bf16[2048,1024]{1,0:T(8,128)(2,1)} copy-done((bf16[2048,1024]{1,0:T(8,128)(2,1)}, bf16[2048,1024]{1,0:T(8,128)(2,1)S(1)}, u32[]{:S(2)}) %copy-start.4) | copy-done | bytes 4194328
  21.9 1.6 %collective-permute-done.2 = f32[64,1024]{1,0:T(8,128)S(1)} collective-permute-done((f32[64,1024]{1,0:T(8,128)S(1)}, f32[64,1024]{1,0:T(8,128)S(1)}, u32[]{:S(2)}, u32[]{:S(2)}) %collective-permute-start.2) | collective-permute-done | bytes 262176 | tf_op jit(solution)/shard_map/ppermute | solution.py:20
  23.5 1.5 %shard_map.62 = (bf16[2048,1024]{1,0:T(8,128)(2,1)S(1)}, f32[32,1024]{1,0:T(8,128)S(1)}) custom-call(f32[32,1024]{1,0:T(8,128)S(1)} %get-tuple-element.62.rows_ref, f32[32,1024]{1,0:T(8,128)S(1)} %get-tuple-element.61.vectors_ref, f32[32,1]{1,0:T(8,128)S(1)} %copy.16.scale_ref, bf16[256,1024]{1,0:T(8,128)(2,1)S(1)} %shard_map.59.right_ref, ...), custom_call_target="tpu_custom_call" | custom-call | flops 872415232 | bytes 4194304 | tf_op jit(solution)/shard_map/pallas_call | solution.py:109
  25.0 1.9 %copy-done.2 = bf16[2048,1024]{1,0:T(8,128)(2,1)} copy-done((bf16[2048,1024]{1,0:T(8,128)(2,1)}, bf16[2048,1024]{1,0:T(8,128)(2,1)S(1)}, u32[]{:S(2)}) %copy-start.2) | copy-done | bytes 4194328
  27.0 1.5 %shard_map.63 = (bf16[2048,1024]{1,0:T(8,128)(2,1)S(1)}, f32[32,1024]{1,0:T(8,128)S(1)}) custom-call(f32[32,1024]{1,0:T(8,128)S(1)} %get-tuple-element.64.rows_ref, f32[32,1024]{1,0:T(8,128)S(1)} %get-tuple-element.63.vectors_ref, f32[32,1]{1,0:T(8,128)S(1)} %copy.16.scale_ref, bf16[256,1024]{1,0:T(8,128)(2,1)S(1)} %shard_map.59.right_ref, ...), custom_call_target="tpu_custom_call" | custom-call | flops 872415232 | bytes 4194304 | tf_op jit(solution)/shard_map/pallas_call | solution.py:109
  28.6 2.0 %copy-done = bf16[2048,1024]{1,0:T(8,128)(2,1)} copy-done((bf16[2048,1024]{1,0:T(8,128)(2,1)}, bf16[2048,1024]{1,0:T(8,128)(2,1)S(1)}, u32[]{:S(2)}) %copy-start) | copy-done | bytes 4194328
  30.6 1.7 %collective-permute-start.6 = (f32[32,1024]{1,0:T(8,128)S(1)}, f32[32,1024]{1,0:T(8,128)S(1)}, u32[]{:S(2)}, u32[]{:S(2)}) collective-permute-start(f32[32,1024]{1,0:T(8,128)S(1)} %get-tuple-element.31.refs_0_.refs_10_), channel_id=1, source_target_pairs={{0,2},{1,3},{2,0},{3,1},{4,6},{5,7},{6,4},{7,5},{8,10},{9,11},{10,... | collective-permute-start | bytes 393224 | tf_op jit(solution)/shard_map/ppermute | solution.py:20
  32.6 0.8 %fusion.1 = f32[96,1024]{1,0:T(8,128)S(1)} fusion(bf16[2048,1024]{1,0:T(8,128)(2,1)S(1)} %get-tuple-element.33, bf16[32,1024]{1,0:T(8,128)(2,1)S(1)} %broadcast.3, bf16[32,1024]{1,0:T(8,128)(2,1)S(1)} %get-tuple-element.90, bf16[32,1024]{1,0:T(8,128)(2,1)S(1)} %get-tuple-element.91, bf16[32,1024]{1,0:T(8,128)(2,1)S(1)} %get-tuple-element.89), kind=kOutput, calls=%fused_computation.18 | convolution fusion | flops 405012480 | bytes 4849664 | tf_op jit(solution)/shard_map/dot_general | solution.py:190
  33.7 3.2 %convolution_add_fusion.5 = f32[96,1024]{1,0:T(8,128)S(1)} fusion(f32[96,1024]{1,0:T(8,128)S(1)} %fusion.1, bf16[2048,1024]{1,0:T(8,128)(2,1)} %copy-done.4, bf16[32,1024]{1,0:T(8,128)(2,1)S(1)} %broadcast.3, bf16[32,1024]{1,0:T(8,128)(2,1)S(1)} %get-tuple-element.87, bf16[32,1024]{1,0:T(8,128)(2,1)S(1)} %get-tuple-element.88, ...), kind=kOutput, calls=%fused_computation.14 | convolution fusion | flops 405110784 | bytes 5242880 | tf_op jit(solution)/shard_map/dot_general | solution.py:190
  37.3 0.8 %convolution_add_fusion.4.refs_5_ = f32[96,1024]{1,0:T(8,128)S(1)} fusion(f32[96,1024]{1,0:T(8,128)S(1)} %convolution_add_fusion.5, bf16[2048,1024]{1,0:T(8,128)(2,1)S(1)} %copy-done.3, bf16[32,1024]{1,0:T(8,128)(2,1)S(1)} %broadcast.3, bf16[32,1024]{1,0:T(8,128)(2,1)S(1)} %get-tuple-element.84, bf16[32,1024]{1,0:T(8,128)(2,1)S(1)} %get-tuple-element.85, ...), kind=kOutput, calls=%fused_computation.13 | convolution fusion | flops 405110784 | bytes 5242880 | tf_op jit(solution)/shard_map/dot_general | solution.py:190
  38.3 0.8 %copy-done.1 = bf16[2048,1024]{1,0:T(8,128)(2,1)S(1)} copy-done((bf16[2048,1024]{1,0:T(8,128)(2,1)S(1)}, bf16[2048,1024]{1,0:T(8,128)(2,1)}, u32[]{:S(2)}) %copy-start.1) | copy-done | bytes 4194328
  39.1 1.0 %shard_map.64 = (f32[32,1]{1,0:T(8,128)S(1)}, f32[32,4096]{1,0:T(8,128)S(1)}, f32[32,4096]{1,0:T(8,128)S(1)}, f32[32,256]{1,0:T(8,128)S(1)}, f32[32,1024]{1,0:T(8,128)S(1)}, /*index=5*/f32[32,1024]{1,0:T(8,128)S(1)}) custom-call(f32[32,1024]{1,0:T(8,128)S(1)} %get-tuple-element.31.refs_0_.refs_10_, f32[32,1024]{1,0:T(8,128)S(1)} %collective-permute-done.5.refs_1_, ...), custom_call_target="tpu_custom_call" | custom-call | flops 402653184 | bytes 4194304 | tf_op jit(solution)/shard_map/pallas_call | solution.py:109
  40.7 0.8 %fusion.8 = f32[96,1024]{1,0:T(8,128)S(1)} fusion(bf16[2048,1024]{1,0:T(8,128)(2,1)S(1)} %copy-done.7, bf16[32,1024]{1,0:T(8,128)(2,1)S(1)} %broadcast.3, bf16[32,1024]{1,0:T(8,128)(2,1)S(1)} %get-tuple-element.81, bf16[32,1024]{1,0:T(8,128)(2,1)S(1)} %get-tuple-element.82, bf16[32,1024]{1,0:T(8,128)(2,1)S(1)} %get-tuple-element.80), kind=kOutput, calls=%fused_computation.22 | convolution fusion | flops 405012480 | bytes 4849664 | tf_op jit(solution)/shard_map/dot_general | solution.py:190
  42.4 0.8 %convolution_add_fusion.3 = f32[96,1024]{1,0:T(8,128)S(1)} fusion(f32[96,1024]{1,0:T(8,128)S(1)} %fusion.8, bf16[2048,1024]{1,0:T(8,128)(2,1)S(1)} %copy-done.5, bf16[32,1024]{1,0:T(8,128)(2,1)S(1)} %broadcast.3, bf16[32,1024]{1,0:T(8,128)(2,1)S(1)} %get-tuple-element.78, bf16[32,1024]{1,0:T(8,128)(2,1)S(1)} %get-tuple-element.79, ...), kind=kOutput, calls=%fused_computation.12 | convolution fusion | flops 405110784 | bytes 5242880 | tf_op jit(solution)/shard_map/dot_general | solution.py:190
  43.2 2.7 %collective-permute-done.9.refs_2_ = f32[32,1024]{1,0:T(8,128)S(1)} collective-permute-done((f32[32,1024]{1,0:T(8,128)S(1)}, f32[32,1024]{1,0:T(8,128)S(1)}, u32[]{:S(2)}, u32[]{:S(2)}) %collective-permute-start.9) | collective-permute-done | bytes 131104 | tf_op jit(solution)/shard_map/ppermute | solution.py:20
  45.9 0.8 %convolution_add_fusion.2.refs_5_ = f32[96,1024]{1,0:T(8,128)S(1)} fusion(f32[96,1024]{1,0:T(8,128)S(1)} %convolution_add_fusion.3, bf16[2048,1024]{1,0:T(8,128)(2,1)S(1)} %copy-done.3, bf16[32,1024]{1,0:T(8,128)(2,1)S(1)} %broadcast.3, bf16[32,1024]{1,0:T(8,128)(2,1)S(1)} %get-tuple-element.75, bf16[32,1024]{1,0:T(8,128)(2,1)S(1)} %get-tuple-element.76, ...), kind=kOutput, calls=%fused_computation.11 | convolution fusion | flops 405110784 | bytes 5242880 | tf_op jit(solution)/shard_map/dot_general | solution.py:190
  47.3 1.0 %shard_map.65 = (f32[32,1]{1,0:T(8,128)S(1)}, f32[32,4096]{1,0:T(8,128)S(1)}, f32[32,4096]{1,0:T(8,128)S(1)}, f32[32,256]{1,0:T(8,128)S(1)}, f32[32,1024]{1,0:T(8,128)S(1)}, /*index=5*/f32[32,1024]{1,0:T(8,128)S(1)}) custom-call(f32[32,1024]{1,0:T(8,128)S(1)} %get-tuple-element.36.refs_0_, f32[32,1024]{1,0:T(8,128)S(1)} %collective-permute-done.8.refs_1_, ...), custom_call_target="tpu_custom_call" | custom-call | flops 402653184 | bytes 4194304 | tf_op jit(solution)/shard_map/pallas_call | solution.py:109
  48.8 0.8 %fusion.15 = f32[96,1024]{1,0:T(8,128)S(1)} fusion(bf16[2048,1024]{1,0:T(8,128)(2,1)S(1)} %copy-done.7, bf16[32,1024]{1,0:T(8,128)(2,1)S(1)} %broadcast.3, bf16[32,1024]{1,0:T(8,128)(2,1)S(1)} %get-tuple-element.72, bf16[32,1024]{1,0:T(8,128)(2,1)S(1)} %get-tuple-element.73, bf16[32,1024]{1,0:T(8,128)(2,1)S(1)} %get-tuple-element.71), kind=kOutput, calls=%fused_computation.26 | convolution fusion | flops 405012480 | bytes 4849664 | tf_op jit(solution)/shard_map/dot_general | solution.py:190
  50.2 0.8 %convolution_add_fusion.1 = f32[96,1024]{1,0:T(8,128)S(1)} fusion(f32[96,1024]{1,0:T(8,128)S(1)} %fusion.15, bf16[2048,1024]{1,0:T(8,128)(2,1)S(1)} %copy-done.5, bf16[32,1024]{1,0:T(8,128)(2,1)S(1)} %broadcast.3, bf16[32,1024]{1,0:T(8,128)(2,1)S(1)} %get-tuple-element.69, bf16[32,1024]{1,0:T(8,128)(2,1)S(1)} %get-tuple-element.70, ...), kind=kOutput, calls=%fused_computation.10 | convolution fusion | flops 405110784 | bytes 5242880 | tf_op jit(solution)/shard_map/dot_general | solution.py:190
  51.0 3.0 %collective-permute-done.12.refs_2_ = f32[32,1024]{1,0:T(8,128)S(1)} collective-permute-done((f32[32,1024]{1,0:T(8,128)S(1)}, f32[32,1024]{1,0:T(8,128)S(1)}, u32[]{:S(2)}, u32[]{:S(2)}) %collective-permute-start.12) | collective-permute-done | bytes 131104 | tf_op jit(solution)/shard_map/ppermute | solution.py:20
  54.1 0.8 %convolution_add_fusion.refs_5_ = f32[96,1024]{1,0:T(8,128)S(1)} fusion(f32[96,1024]{1,0:T(8,128)S(1)} %convolution_add_fusion.1, bf16[2048,1024]{1,0:T(8,128)(2,1)S(1)} %copy-done.3, bf16[32,1024]{1,0:T(8,128)(2,1)S(1)} %broadcast.3, bf16[32,1024]{1,0:T(8,128)(2,1)S(1)} %get-tuple-element.66, bf16[32,1024]{1,0:T(8,128)(2,1)S(1)} %get-tuple-element.67, ...), kind=kOutput, calls=%fused_computation.9 | convolution fusion | flops 405110784 | bytes 5242880 | tf_op jit(solution)/shard_map/dot_general | solution.py:190
  55.4 1.0 %shard_map.66 = (f32[32,1]{1,0:T(8,128)S(1)}, f32[32,4096]{1,0:T(8,128)S(1)}, f32[32,4096]{1,0:T(8,128)S(1)}, f32[32,256]{1,0:T(8,128)S(1)}, f32[32,1024]{1,0:T(8,128)S(1)}, /*index=5*/f32[32,1]{1,0:T(8,128)S(1)}) custom-call(f32[32,1024]{1,0:T(8,128)S(1)} %get-tuple-element.42.refs_0_, f32[32,1024]{1,0:T(8,128)S(1)} %collective-permute-done.11.refs_1_, ...), custom_call_target="tpu_custom_call" | custom-call | flops 402653184 | bytes 4194304 | tf_op jit(solution)/shard_map/pallas_call | solution.py:109
  56.8 3.4 %collective-permute-done.14 = f32[32,1]{1,0:T(8,128)S(1)} collective-permute-done((f32[32,1]{1,0:T(8,128)S(1)}, f32[32,1]{1,0:T(8,128)S(1)}, u32[]{:S(2)}, u32[]{:S(2)}) %collective-permute-start.14) | collective-permute-done | bytes 160 | tf_op jit(solution)/shard_map/ppermute | solution.py:20
  60.2 1.2 %collective-permute-done.15 = f32[32,1]{1,0:T(8,128)S(1)} collective-permute-done((f32[32,1]{1,0:T(8,128)S(1)}, f32[32,1]{1,0:T(8,128)S(1)}, u32[]{:S(2)}, u32[]{:S(2)}) %collective-permute-start.15) | collective-permute-done | bytes 160 | tf_op jit(solution)/shard_map/ppermute | solution.py:20
  (60 shorter events, 7.1 us)
Async XLA Ops:
  1.4 7.9 %collective-permute-start = (f32[65,256]{1,0:T(8,128)S(1)}, f32[65,256]{1,0:T(8,128)S(1)}, u32[]{:S(2)}, u32[]{:S(2)}) collective-permute-start(f32[65,256]{1,0:T(8,128)S(1)} %pad_maximum_fusion.12), channel_id=1, source_target_pairs={{0,8},{1,9},{2,10},{3,11},{4,12},{5,13},{6,14},{7,15},{8,0},{9,1},... | collective-permute-start | bytes 199688 | tf_op jit(solution)/shard_map/ppermute | solution.py:20
  9.4 5.2 %collective-permute-start.1 = (f32[65,512]{1,0:T(8,128)S(1)}, f32[65,512]{1,0:T(8,128)S(1)}, u32[]{:S(2)}, u32[]{:S(2)}) collective-permute-start(f32[65,512]{1,0:T(8,128)S(1)} %pad_maximum_fusion.11), channel_id=1, source_target_pairs={{0,4},{1,5},{2,6},{3,7},{4,0},{5,1},{6,2},{7,3},{8,12},{9,13},{10,... | collective-permute-start | bytes 399368 | tf_op jit(solution)/shard_map/ppermute | solution.py:20
  14.7 3.6 %collective-permute-start.4 = (f32[64,1024]{1,0:T(8,128)S(1)}, f32[64,1024]{1,0:T(8,128)S(1)}, u32[]{:S(2)}, u32[]{:S(2)}) collective-permute-start(f32[64,1024]{1,0:T(8,128)S(1)} %slice.55), channel_id=1, source_target_pairs={{0,1},{1,0},{2,3},{3,2},{4,5},{5,4},{6,7},{7,6},{8,9},{9,8},{10,11... | collective-permute-start | bytes 786440 | tf_op jit(solution)/shard_map/ppermute | solution.py:20
  14.7 8.7 %collective-permute-start.2 = (f32[64,1024]{1,0:T(8,128)S(1)}, f32[64,1024]{1,0:T(8,128)S(1)}, u32[]{:S(2)}, u32[]{:S(2)}) collective-permute-start(f32[64,1024]{1,0:T(8,128)S(1)} %slice.55), channel_id=1, source_target_pairs={{0,2},{1,3},{2,0},{3,1},{4,6},{5,7},{6,4},{7,5},{8,10},{9,11},{10,... | collective-permute-start | bytes 786440 | tf_op jit(solution)/shard_map/ppermute | solution.py:20
  18.3 15.3 %copy-start.6 = (bf16[2048,1024]{1,0:T(8,128)(2,1)}, bf16[2048,1024]{1,0:T(8,128)(2,1)S(1)}, u32[]{:S(2)}) copy-start(bf16[2048,1024]{1,0:T(8,128)(2,1)S(1)} %get-tuple-element.33) | copy-start | bytes 12582916
  19.9 2.0 %copy-start.4 = (bf16[2048,1024]{1,0:T(8,128)(2,1)}, bf16[2048,1024]{1,0:T(8,128)(2,1)S(1)}, u32[]{:S(2)}) copy-start(bf16[2048,1024]{1,0:T(8,128)(2,1)S(1)} %get-tuple-element.34) | copy-start | bytes 12582916
  23.5 3.5 %collective-permute-start.3 = (f32[64,1024]{1,0:T(8,128)S(1)}, f32[64,1024]{1,0:T(8,128)S(1)}, u32[]{:S(2)}, u32[]{:S(2)}) collective-permute-start(f32[64,1024]{1,0:T(8,128)S(1)} %collective-permute-done.2), channel_id=1, source_target_pairs={{0,1},{1,0},{2,3},{3,2},{4,5},{5,4},{6,7},{7,6},{8,9},{9,8},{10,11... | collective-permute-start | bytes 786440 | tf_op jit(solution)/shard_map/ppermute | solution.py:20
  25.0 1.9 %copy-start.2 = (bf16[2048,1024]{1,0:T(8,128)(2,1)}, bf16[2048,1024]{1,0:T(8,128)(2,1)S(1)}, u32[]{:S(2)}) copy-start(bf16[2048,1024]{1,0:T(8,128)(2,1)S(1)} %get-tuple-element.35) | copy-start | bytes 12582916
  28.6 2.0 %copy-start = (bf16[2048,1024]{1,0:T(8,128)(2,1)}, bf16[2048,1024]{1,0:T(8,128)(2,1)S(1)}, u32[]{:S(2)}) copy-start(bf16[2048,1024]{1,0:T(8,128)(2,1)S(1)} %get-tuple-element.32.refs_4_) | copy-start | bytes 12582916
  30.6 6.3 %collective-permute-start.6 = (f32[32,1024]{1,0:T(8,128)S(1)}, f32[32,1024]{1,0:T(8,128)S(1)}, u32[]{:S(2)}, u32[]{:S(2)}) collective-permute-start(f32[32,1024]{1,0:T(8,128)S(1)} %get-tuple-element.31.refs_0_.refs_10_), channel_id=1, source_target_pairs={{0,2},{1,3},{2,0},{3,1},{4,6},{5,7},{6,4},{7,5},{8,10},{9,11},{10,... | collective-permute-start | bytes 393224 | tf_op jit(solution)/shard_map/ppermute | solution.py:20
  32.3 1.4 %collective-permute-start.5 = (f32[32,1024]{1,0:T(8,128)S(1)}, f32[32,1024]{1,0:T(8,128)S(1)}, u32[]{:S(2)}, u32[]{:S(2)}) collective-permute-start(f32[32,1024]{1,0:T(8,128)S(1)} %get-tuple-element.31.refs_0_.refs_10_), channel_id=1, source_target_pairs={{0,1},{1,0},{2,3},{3,2},{4,5},{5,4},{6,7},{7,6},{8,9},{9,8},{10,11... | collective-permute-start | bytes 393224 | tf_op jit(solution)/shard_map/ppermute | solution.py:20
  33.7 3.6 %copy-start.3 = (bf16[2048,1024]{1,0:T(8,128)(2,1)S(1)}, bf16[2048,1024]{1,0:T(8,128)(2,1)}, u32[]{:S(2)}) copy-start(bf16[2048,1024]{1,0:T(8,128)(2,1)} %copy-done.2) | copy-start | bytes 12582916
  36.9 2.2 %copy-start.1 = (bf16[2048,1024]{1,0:T(8,128)(2,1)S(1)}, bf16[2048,1024]{1,0:T(8,128)(2,1)}, u32[]{:S(2)}) copy-start(bf16[2048,1024]{1,0:T(8,128)(2,1)} %copy-done) | copy-start | bytes 12582916
  36.9 1.4 %collective-permute-start.7 = (f32[32,1024]{1,0:T(8,128)S(1)}, f32[32,1024]{1,0:T(8,128)S(1)}, u32[]{:S(2)}, u32[]{:S(2)}) collective-permute-start(f32[32,1024]{1,0:T(8,128)S(1)} %collective-permute-done.6.refs_2_), channel_id=1, source_target_pairs={{0,1},{1,0},{2,3},{3,2},{4,5},{5,4},{6,7},{7,6},{8,9},{9,8},{10,11... | collective-permute-start | bytes 393224 | tf_op jit(solution)/shard_map/ppermute | solution.py:20
  38.1 2.6 %copy-start.7 = (bf16[2048,1024]{1,0:T(8,128)(2,1)S(1)}, bf16[2048,1024]{1,0:T(8,128)(2,1)}, u32[]{:S(2)}) copy-start(bf16[2048,1024]{1,0:T(8,128)(2,1)} %copy-done.6) | copy-start | bytes 12582916
  40.2 2.3 %copy-start.5 = (bf16[2048,1024]{1,0:T(8,128)(2,1)S(1)}, bf16[2048,1024]{1,0:T(8,128)(2,1)}, u32[]{:S(2)}) copy-start(bf16[2048,1024]{1,0:T(8,128)(2,1)} %copy-done.4) | copy-start | bytes 12582916
  40.2 5.7 %collective-permute-start.9 = (f32[32,1024]{1,0:T(8,128)S(1)}, f32[32,1024]{1,0:T(8,128)S(1)}, u32[]{:S(2)}, u32[]{:S(2)}) collective-permute-start(f32[32,1024]{1,0:T(8,128)S(1)} %get-tuple-element.36.refs_0_), channel_id=1, source_target_pairs={{0,2},{1,3},{2,0},{3,1},{4,6},{5,7},{6,4},{7,5},{8,10},{9,11},{10,... | collective-permute-start | bytes 393224 | tf_op jit(solution)/shard_map/ppermute | solution.py:20
  40.7 1.3 %collective-permute-start.8 = (f32[32,1024]{1,0:T(8,128)S(1)}, f32[32,1024]{1,0:T(8,128)S(1)}, u32[]{:S(2)}, u32[]{:S(2)}) collective-permute-start(f32[32,1024]{1,0:T(8,128)S(1)} %get-tuple-element.36.refs_0_), channel_id=1, source_target_pairs={{0,1},{1,0},{2,3},{3,2},{4,5},{5,4},{6,7},{7,6},{8,9},{9,8},{10,11... | collective-permute-start | bytes 393224 | tf_op jit(solution)/shard_map/ppermute | solution.py:20
  45.9 1.3 %collective-permute-start.10 = (f32[32,1024]{1,0:T(8,128)S(1)}, f32[32,1024]{1,0:T(8,128)S(1)}, u32[]{:S(2)}, u32[]{:S(2)}) collective-permute-start(f32[32,1024]{1,0:T(8,128)S(1)} %collective-permute-done.9.refs_2_), channel_id=1, source_target_pairs={{0,1},{1,0},{2,3},{3,2},{4,5},{5,4},{6,7},{7,6},{8,9},{9,8},{10,11... | collective-permute-start | bytes 393224 | tf_op jit(solution)/shard_map/ppermute | solution.py:20
  48.2 5.8 %collective-permute-start.12 = (f32[32,1024]{1,0:T(8,128)S(1)}, f32[32,1024]{1,0:T(8,128)S(1)}, u32[]{:S(2)}, u32[]{:S(2)}) collective-permute-start(f32[32,1024]{1,0:T(8,128)S(1)} %get-tuple-element.42.refs_0_), channel_id=1, source_target_pairs={{0,2},{1,3},{2,0},{3,1},{4,6},{5,7},{6,4},{7,5},{8,10},{9,11},{10,... | collective-permute-start | bytes 393224 | tf_op jit(solution)/shard_map/ppermute | solution.py:20
  48.8 1.3 %collective-permute-start.11 = (f32[32,1024]{1,0:T(8,128)S(1)}, f32[32,1024]{1,0:T(8,128)S(1)}, u32[]{:S(2)}, u32[]{:S(2)}) collective-permute-start(f32[32,1024]{1,0:T(8,128)S(1)} %get-tuple-element.42.refs_0_), channel_id=1, source_target_pairs={{0,1},{1,0},{2,3},{3,2},{4,5},{5,4},{6,7},{7,6},{8,9},{9,8},{10,11... | collective-permute-start | bytes 393224 | tf_op jit(solution)/shard_map/ppermute | solution.py:20
  54.0 1.3 %collective-permute-start.13 = (f32[32,1024]{1,0:T(8,128)S(1)}, f32[32,1024]{1,0:T(8,128)S(1)}, u32[]{:S(2)}, u32[]{:S(2)}) collective-permute-start(f32[32,1024]{1,0:T(8,128)S(1)} %collective-permute-done.12.refs_2_), channel_id=1, source_target_pairs={{0,1},{1,0},{2,3},{3,2},{4,5},{5,4},{6,7},{7,6},{8,9},{9,8},{10,11... | collective-permute-start | bytes 393224 | tf_op jit(solution)/shard_map/ppermute | solution.py:20
  56.4 3.8 %collective-permute-start.14 = (f32[32,1]{1,0:T(8,128)S(1)}, f32[32,1]{1,0:T(8,128)S(1)}, u32[]{:S(2)}, u32[]{:S(2)}) collective-permute-start(f32[32,1]{1,0:T(8,128)S(1)} %get-tuple-element.50), channel_id=1, source_target_pairs={{0,2},{1,3},{2,0},{3,1},{4,6},{5,7},{6,4},{7,5},{8,10},{9,11},{10,... | collective-permute-start | bytes 392 | tf_op jit(solution)/shard_map/ppermute | solution.py:20
  60.2 1.2 %collective-permute-start.15 = (f32[32,1]{1,0:T(8,128)S(1)}, f32[32,1]{1,0:T(8,128)S(1)}, u32[]{:S(2)}, u32[]{:S(2)}) collective-permute-start(f32[32,1]{1,0:T(8,128)S(1)} %add.33), channel_id=1, source_target_pairs={{0,1},{1,0},{2,3},{3,2},{4,5},{5,4},{6,7},{7,6},{8,9},{9,8},{10,11... | collective-permute-start | bytes 392 | tf_op jit(solution)/shard_map/ppermute | solution.py:20

commit v15 on v14

--- a/solution.py
+++ b/solution.py
@@ -10,7 +10,7 @@
 
 ITERS = 4
 TILE_BYTES = 16 << 20
-VMEM_BYTES = 16 << 20
+VMEM_BYTES = 4 << 20
 NORM_ROWS = 64
 BUILD_ROWS = 1024
 POINT_SCALE = math.sqrt(math.log2(math.e))

time: 62.4 us -> 62.5 us (level)
  no operation moved by 1% of the time
where the time goes in v15:
time: 62.5 us; the launch traced here: 62.2 us
  waiting for transfers between devices  21.7 us (35%)
  starting transfers between devices  10.4 us (17%)
  matrix products  9.67 us (15%)
  Pallas kernels  9.36 us (15%)
  local copies, waits for them, and re-layouts  7.41 us (12%)
  other arithmetic  2.78 us (4%)
  between operations  0.91 us (1%)
    ppermute x16, waiting for transfers between devices, swap(): return lax.ppermute(x, 'blk', [(i, i ^ stride) for i in range(n)])  21.7 us
    ppermute x16, starting transfers between devices, swap(): return lax.ppermute(x, 'blk', [(i, i ^ stride) for i in range(n)])  10.4 us
    dot_general x9, matrix products, apply_piece(): jnp.dot(jnp.concatenate([left, right], axis=1), piece, preferred_element_...  9.67 us
    pallas_call x8, Pallas kernels, call(): pl.pallas_call(kernel, out_shape=outs, in_specs=[whole] * len(args), out_...  9.36 us
    unnamed x16, local copies, waits for them, and re-layouts  7.15 us
  transfers between devices with their start and end apart: 16, of which 12 were waited for; matrix products, arithmetic and copies ran while one was open for 18% of the time, Pallas kernels for 8%

profile of v15, /device:TPU:0, one launch (start us, length us, event | category | flops | bytes accessed | tf_op | source)
XLA Modules:
  0.0 62.2 jit_solution(10294346812454917944)
XLA Ops:
  0.6 0.8 %pad_maximum_fusion.12 = f32[65,256]{1,0:T(8,128)S(1)} fusion(f32[1,256]{1,0:T(1,128)} %bitcast.16, f32[32,256]{1,0:T(8,128)} %param.7, f32[32,256]{1,0:T(8,128)} %param.4), kind=kLoop, calls=%fused_computation.157 | loop fusion | flops 33280 | bytes 133120 | tf_op jit(solution)/shard_map/concatenate | solution.py:213
  1.4 4.0 %collective-permute-start = (f32[65,256]{1,0:T(8,128)S(1)}, f32[65,256]{1,0:T(8,128)S(1)}, u32[]{:S(2)}, u32[]{:S(2)}) collective-permute-start(f32[65,256]{1,0:T(8,128)S(1)} %pad_maximum_fusion.12), channel_id=1, source_target_pairs={{0,8},{1,9},{2,10},{3,11},{4,12},{5,13},{6,14},{7,15},{8,0},{9,1},... | collective-permute-start | bytes 199688 | tf_op jit(solution)/shard_map/ppermute | solution.py:20
  5.5 3.9 %collective-permute-done = f32[65,256]{1,0:T(8,128)S(1)} collective-permute-done((f32[65,256]{1,0:T(8,128)S(1)}, f32[65,256]{1,0:T(8,128)S(1)}, u32[]{:S(2)}, u32[]{:S(2)}) %collective-permute-start) | collective-permute-done | bytes 66592 | tf_op jit(solution)/shard_map/ppermute | solution.py:20
  9.4 0.7 %collective-permute-start.1 = (f32[65,512]{1,0:T(8,128)S(1)}, f32[65,512]{1,0:T(8,128)S(1)}, u32[]{:S(2)}, u32[]{:S(2)}) collective-permute-start(f32[65,512]{1,0:T(8,128)S(1)} %pad_maximum_fusion.11), channel_id=1, source_target_pairs={{0,4},{1,5},{2,6},{3,7},{4,0},{5,1},{6,2},{7,3},{8,12},{9,13},{10,... | collective-permute-start | bytes 399368 | tf_op jit(solution)/shard_map/ppermute | solution.py:20
  10.9 3.7 %collective-permute-done.1 = f32[65,512]{1,0:T(8,128)S(1)} collective-permute-done((f32[65,512]{1,0:T(8,128)S(1)}, f32[65,512]{1,0:T(8,128)S(1)}, u32[]{:S(2)}, u32[]{:S(2)}) %collective-permute-start.1) | collective-permute-done | bytes 133152 | tf_op jit(solution)/shard_map/ppermute | solution.py:20
  14.7 1.8 %collective-permute-start.2 = (f32[64,1024]{1,0:T(8,128)S(1)}, f32[64,1024]{1,0:T(8,128)S(1)}, u32[]{:S(2)}, u32[]{:S(2)}) collective-permute-start(f32[64,1024]{1,0:T(8,128)S(1)} %slice.55), channel_id=1, source_target_pairs={{0,2},{1,3},{2,0},{3,1},{4,6},{5,7},{6,4},{7,5},{8,10},{9,11},{10,... | collective-permute-start | bytes 786440 | tf_op jit(solution)/shard_map/ppermute | solution.py:20
  16.7 1.5 %shard_map.60 = (bf16[2048,1024]{1,0:T(8,128)(2,1)S(1)}, f32[32,1024]{1,0:T(8,128)S(1)}) custom-call(f32[32,1024]{1,0:T(8,128)S(1)} %get-tuple-element.58.mine_ref.rows_ref, f32[32,1024]{1,0:T(8,128)S(1)} %get-tuple-element.57.vectors_ref, f32[32,1]{1,0:T(8,128)S(1)} %copy.16.scale_ref, bf16[256,1024]{1,0:T(8,128)(2,1)S(1)} %shard_map.59.right_ref, ...), custom_call_target="tpu_custom_call" | custom-call | flops 872415232 | bytes 4194304 | tf_op jit(solution)/shard_map/pallas_call | solution.py:109
  18.3 1.6 %shard_map.61 = (bf16[2048,1024]{1,0:T(8,128)(2,1)S(1)}, f32[32,1024]{1,0:T(8,128)S(1)}) custom-call(f32[32,1024]{1,0:T(8,128)S(1)} %get-tuple-element.60.rows_ref, f32[32,1024]{1,0:T(8,128)S(1)} %get-tuple-element.59.vectors_ref, f32[32,1]{1,0:T(8,128)S(1)} %copy.16.scale_ref, bf16[256,1024]{1,0:T(8,128)(2,1)S(1)} %shard_map.59.right_ref, ...), custom_call_target="tpu_custom_call" | custom-call | flops 872415232 | bytes 4194304 | tf_op jit(solution)/shard_map/pallas_call | solution.py:109
  19.9 2.0 %copy-done.4 = bf16[2048,1024]{1,0:T(8,128)(2,1)} copy-done((bf16[2048,1024]{1,0:T(8,128)(2,1)}, bf16[2048,1024]{1,0:T(8,128)(2,1)S(1)}, u32[]{:S(2)}) %copy-start.4) | copy-done | bytes 4194328
  21.9 1.6 %collective-permute-done.2 = f32[64,1024]{1,0:T(8,128)S(1)} collective-permute-done((f32[64,1024]{1,0:T(8,128)S(1)}, f32[64,1024]{1,0:T(8,128)S(1)}, u32[]{:S(2)}, u32[]{:S(2)}) %collective-permute-start.2) | collective-permute-done | bytes 262176 | tf_op jit(solution)/shard_map/ppermute | solution.py:20
  23.5 1.6 %shard_map.62 = (bf16[2048,1024]{1,0:T(8,128)(2,1)S(1)}, f32[32,1024]{1,0:T(8,128)S(1)}) custom-call(f32[32,1024]{1,0:T(8,128)S(1)} %get-tuple-element.62.rows_ref, f32[32,1024]{1,0:T(8,128)S(1)} %get-tuple-element.61.vectors_ref, f32[32,1]{1,0:T(8,128)S(1)} %copy.16.scale_ref, bf16[256,1024]{1,0:T(8,128)(2,1)S(1)} %shard_map.59.right_ref, ...), custom_call_target="tpu_custom_call" | custom-call | flops 872415232 | bytes 4194304 | tf_op jit(solution)/shard_map/pallas_call | solution.py:109
  25.1 1.9 %copy-done.2 = bf16[2048,1024]{1,0:T(8,128)(2,1)} copy-done((bf16[2048,1024]{1,0:T(8,128)(2,1)}, bf16[2048,1024]{1,0:T(8,128)(2,1)S(1)}, u32[]{:S(2)}) %copy-start.2) | copy-done | bytes 4194328
  27.0 1.6 %shard_map.63 = (bf16[2048,1024]{1,0:T(8,128)(2,1)S(1)}, f32[32,1024]{1,0:T(8,128)S(1)}) custom-call(f32[32,1024]{1,0:T(8,128)S(1)} %get-tuple-element.64.rows_ref, f32[32,1024]{1,0:T(8,128)S(1)} %get-tuple-element.63.vectors_ref, f32[32,1]{1,0:T(8,128)S(1)} %copy.16.scale_ref, bf16[256,1024]{1,0:T(8,128)(2,1)S(1)} %shard_map.59.right_ref, ...), custom_call_target="tpu_custom_call" | custom-call | flops 872415232 | bytes 4194304 | tf_op jit(solution)/shard_map/pallas_call | solution.py:109
  28.6 2.0 %copy-done = bf16[2048,1024]{1,0:T(8,128)(2,1)} copy-done((bf16[2048,1024]{1,0:T(8,128)(2,1)}, bf16[2048,1024]{1,0:T(8,128)(2,1)S(1)}, u32[]{:S(2)}) %copy-start) | copy-done | bytes 4194328
  30.6 1.7 %collective-permute-start.6 = (f32[32,1024]{1,0:T(8,128)S(1)}, f32[32,1024]{1,0:T(8,128)S(1)}, u32[]{:S(2)}, u32[]{:S(2)}) collective-permute-start(f32[32,1024]{1,0:T(8,128)S(1)} %get-tuple-element.31.refs_0_.refs_10_), channel_id=1, source_target_pairs={{0,2},{1,3},{2,0},{3,1},{4,6},{5,7},{6,4},{7,5},{8,10},{9,11},{10,... | collective-permute-start | bytes 393224 | tf_op jit(solution)/shard_map/ppermute | solution.py:20
  32.6 0.8 %fusion.1 = f32[96,1024]{1,0:T(8,128)S(1)} fusion(bf16[2048,1024]{1,0:T(8,128)(2,1)S(1)} %get-tuple-element.33, bf16[32,1024]{1,0:T(8,128)(2,1)S(1)} %broadcast.3, bf16[32,1024]{1,0:T(8,128)(2,1)S(1)} %get-tuple-element.90, bf16[32,1024]{1,0:T(8,128)(2,1)S(1)} %get-tuple-element.91, bf16[32,1024]{1,0:T(8,128)(2,1)S(1)} %get-tuple-element.89), kind=kOutput, calls=%fused_computation.18 | convolution fusion | flops 405012480 | bytes 4849664 | tf_op jit(solution)/shard_map/dot_general | solution.py:190
  33.7 3.2 %convolution_add_fusion.5 = f32[96,1024]{1,0:T(8,128)S(1)} fusion(f32[96,1024]{1,0:T(8,128)S(1)} %fusion.1, bf16[2048,1024]{1,0:T(8,128)(2,1)} %copy-done.4, bf16[32,1024]{1,0:T(8,128)(2,1)S(1)} %broadcast.3, bf16[32,1024]{1,0:T(8,128)(2,1)S(1)} %get-tuple-element.87, bf16[32,1024]{1,0:T(8,128)(2,1)S(1)} %get-tuple-element.88, ...), kind=kOutput, calls=%fused_computation.14 | convolution fusion | flops 405110784 | bytes 5242880 | tf_op jit(solution)/shard_map/dot_general | solution.py:190
  37.3 0.8 %convolution_add_fusion.4.refs_5_ = f32[96,1024]{1,0:T(8,128)S(1)} fusion(f32[96,1024]{1,0:T(8,128)S(1)} %convolution_add_fusion.5, bf16[2048,1024]{1,0:T(8,128)(2,1)S(1)} %copy-done.3, bf16[32,1024]{1,0:T(8,128)(2,1)S(1)} %broadcast.3, bf16[32,1024]{1,0:T(8,128)(2,1)S(1)} %get-tuple-element.84, bf16[32,1024]{1,0:T(8,128)(2,1)S(1)} %get-tuple-element.85, ...), kind=kOutput, calls=%fused_computation.13 | convolution fusion | flops 405110784 | bytes 5242880 | tf_op jit(solution)/shard_map/dot_general | solution.py:190
  38.4 0.8 %copy-done.1 = bf16[2048,1024]{1,0:T(8,128)(2,1)S(1)} copy-done((bf16[2048,1024]{1,0:T(8,128)(2,1)S(1)}, bf16[2048,1024]{1,0:T(8,128)(2,1)}, u32[]{:S(2)}) %copy-start.1) | copy-done | bytes 4194328
  39.2 1.0 %shard_map.64 = (f32[32,1]{1,0:T(8,128)S(1)}, f32[32,4096]{1,0:T(8,128)S(1)}, f32[32,4096]{1,0:T(8,128)S(1)}, f32[32,256]{1,0:T(8,128)S(1)}, f32[32,1024]{1,0:T(8,128)S(1)}, /*index=5*/f32[32,1024]{1,0:T(8,128)S(1)}) custom-call(f32[32,1024]{1,0:T(8,128)S(1)} %get-tuple-element.31.refs_0_.refs_10_, f32[32,1024]{1,0:T(8,128)S(1)} %collective-permute-done.5.refs_1_, ...), custom_call_target="tpu_custom_call" | custom-call | flops 402653184 | bytes 4194304 | tf_op jit(solution)/shard_map/pallas_call | solution.py:109
  40.7 0.8 %fusion.8 = f32[96,1024]{1,0:T(8,128)S(1)} fusion(bf16[2048,1024]{1,0:T(8,128)(2,1)S(1)} %copy-done.7, bf16[32,1024]{1,0:T(8,128)(2,1)S(1)} %broadcast.3, bf16[32,1024]{1,0:T(8,128)(2,1)S(1)} %get-tuple-element.81, bf16[32,1024]{1,0:T(8,128)(2,1)S(1)} %get-tuple-element.82, bf16[32,1024]{1,0:T(8,128)(2,1)S(1)} %get-tuple-element.80), kind=kOutput, calls=%fused_computation.22 | convolution fusion | flops 405012480 | bytes 4849664 | tf_op jit(solution)/shard_map/dot_general | solution.py:190
  42.5 0.8 %convolution_add_fusion.3 = f32[96,1024]{1,0:T(8,128)S(1)} fusion(f32[96,1024]{1,0:T(8,128)S(1)} %fusion.8, bf16[2048,1024]{1,0:T(8,128)(2,1)S(1)} %copy-done.5, bf16[32,1024]{1,0:T(8,128)(2,1)S(1)} %broadcast.3, bf16[32,1024]{1,0:T(8,128)(2,1)S(1)} %get-tuple-element.78, bf16[32,1024]{1,0:T(8,128)(2,1)S(1)} %get-tuple-element.79, ...), kind=kOutput, calls=%fused_computation.12 | convolution fusion | flops 405110784 | bytes 5242880 | tf_op jit(solution)/shard_map/dot_general | solution.py:190
  43.3 2.7 %collective-permute-done.9.refs_2_ = f32[32,1024]{1,0:T(8,128)S(1)} collective-permute-done((f32[32,1024]{1,0:T(8,128)S(1)}, f32[32,1024]{1,0:T(8,128)S(1)}, u32[]{:S(2)}, u32[]{:S(2)}) %collective-permute-start.9) | collective-permute-done | bytes 131104 | tf_op jit(solution)/shard_map/ppermute | solution.py:20
  46.0 0.8 %convolution_add_fusion.2.refs_5_ = f32[96,1024]{1,0:T(8,128)S(1)} fusion(f32[96,1024]{1,0:T(8,128)S(1)} %convolution_add_fusion.3, bf16[2048,1024]{1,0:T(8,128)(2,1)S(1)} %copy-done.3, bf16[32,1024]{1,0:T(8,128)(2,1)S(1)} %broadcast.3, bf16[32,1024]{1,0:T(8,128)(2,1)S(1)} %get-tuple-element.75, bf16[32,1024]{1,0:T(8,128)(2,1)S(1)} %get-tuple-element.76, ...), kind=kOutput, calls=%fused_computation.11 | convolution fusion | flops 405110784 | bytes 5242880 | tf_op jit(solution)/shard_map/dot_general | solution.py:190
  47.3 1.0 %shard_map.65 = (f32[32,1]{1,0:T(8,128)S(1)}, f32[32,4096]{1,0:T(8,128)S(1)}, f32[32,4096]{1,0:T(8,128)S(1)}, f32[32,256]{1,0:T(8,128)S(1)}, f32[32,1024]{1,0:T(8,128)S(1)}, /*index=5*/f32[32,1024]{1,0:T(8,128)S(1)}) custom-call(f32[32,1024]{1,0:T(8,128)S(1)} %get-tuple-element.36.refs_0_, f32[32,1024]{1,0:T(8,128)S(1)} %collective-permute-done.8.refs_1_, ...), custom_call_target="tpu_custom_call" | custom-call | flops 402653184 | bytes 4194304 | tf_op jit(solution)/shard_map/pallas_call | solution.py:109
  48.8 0.8 %fusion.15 = f32[96,1024]{1,0:T(8,128)S(1)} fusion(bf16[2048,1024]{1,0:T(8,128)(2,1)S(1)} %copy-done.7, bf16[32,1024]{1,0:T(8,128)(2,1)S(1)} %broadcast.3, bf16[32,1024]{1,0:T(8,128)(2,1)S(1)} %get-tuple-element.72, bf16[32,1024]{1,0:T(8,128)(2,1)S(1)} %get-tuple-element.73, bf16[32,1024]{1,0:T(8,128)(2,1)S(1)} %get-tuple-element.71), kind=kOutput, calls=%fused_computation.26 | convolution fusion | flops 405012480 | bytes 4849664 | tf_op jit(solution)/shard_map/dot_general | solution.py:190
  50.2 0.8 %convolution_add_fusion.1 = f32[96,1024]{1,0:T(8,128)S(1)} fusion(f32[96,1024]{1,0:T(8,128)S(1)} %fusion.15, bf16[2048,1024]{1,0:T(8,128)(2,1)S(1)} %copy-done.5, bf16[32,1024]{1,0:T(8,128)(2,1)S(1)} %broadcast.3, bf16[32,1024]{1,0:T(8,128)(2,1)S(1)} %get-tuple-element.69, bf16[32,1024]{1,0:T(8,128)(2,1)S(1)} %get-tuple-element.70, ...), kind=kOutput, calls=%fused_computation.10 | convolution fusion | flops 405110784 | bytes 5242880 | tf_op jit(solution)/shard_map/dot_general | solution.py:190
  51.0 3.0 %collective-permute-done.12.refs_2_ = f32[32,1024]{1,0:T(8,128)S(1)} collective-permute-done((f32[32,1024]{1,0:T(8,128)S(1)}, f32[32,1024]{1,0:T(8,128)S(1)}, u32[]{:S(2)}, u32[]{:S(2)}) %collective-permute-start.12) | collective-permute-done | bytes 131104 | tf_op jit(solution)/shard_map/ppermute | solution.py:20
  54.1 0.8 %convolution_add_fusion.refs_5_ = f32[96,1024]{1,0:T(8,128)S(1)} fusion(f32[96,1024]{1,0:T(8,128)S(1)} %convolution_add_fusion.1, bf16[2048,1024]{1,0:T(8,128)(2,1)S(1)} %copy-done.3, bf16[32,1024]{1,0:T(8,128)(2,1)S(1)} %broadcast.3, bf16[32,1024]{1,0:T(8,128)(2,1)S(1)} %get-tuple-element.66, bf16[32,1024]{1,0:T(8,128)(2,1)S(1)} %get-tuple-element.67, ...), kind=kOutput, calls=%fused_computation.9 | convolution fusion | flops 405110784 | bytes 5242880 | tf_op jit(solution)/shard_map/dot_general | solution.py:190
  55.4 1.0 %shard_map.66 = (f32[32,1]{1,0:T(8,128)S(1)}, f32[32,4096]{1,0:T(8,128)S(1)}, f32[32,4096]{1,0:T(8,128)S(1)}, f32[32,256]{1,0:T(8,128)S(1)}, f32[32,1024]{1,0:T(8,128)S(1)}, /*index=5*/f32[32,1]{1,0:T(8,128)S(1)}) custom-call(f32[32,1024]{1,0:T(8,128)S(1)} %get-tuple-element.42.refs_0_, f32[32,1024]{1,0:T(8,128)S(1)} %collective-permute-done.11.refs_1_, ...), custom_call_target="tpu_custom_call" | custom-call | flops 402653184 | bytes 4194304 | tf_op jit(solution)/shard_map/pallas_call | solution.py:109
  56.8 3.4 %collective-permute-done.14 = f32[32,1]{1,0:T(8,128)S(1)} collective-permute-done((f32[32,1]{1,0:T(8,128)S(1)}, f32[32,1]{1,0:T(8,128)S(1)}, u32[]{:S(2)}, u32[]{:S(2)}) %collective-permute-start.14) | collective-permute-done | bytes 160 | tf_op jit(solution)/shard_map/ppermute | solution.py:20
  60.2 1.2 %collective-permute-done.15 = f32[32,1]{1,0:T(8,128)S(1)} collective-permute-done((f32[32,1]{1,0:T(8,128)S(1)}, f32[32,1]{1,0:T(8,128)S(1)}, u32[]{:S(2)}, u32[]{:S(2)}) %collective-permute-start.15) | collective-permute-done | bytes 160 | tf_op jit(solution)/shard_map/ppermute | solution.py:20
  (60 shorter events, 7.1 us)
Async XLA Ops:
  1.4 7.9 %collective-permute-start = (f32[65,256]{1,0:T(8,128)S(1)}, f32[65,256]{1,0:T(8,128)S(1)}, u32[]{:S(2)}, u32[]{:S(2)}) collective-permute-start(f32[65,256]{1,0:T(8,128)S(1)} %pad_maximum_fusion.12), channel_id=1, source_target_pairs={{0,8},{1,9},{2,10},{3,11},{4,12},{5,13},{6,14},{7,15},{8,0},{9,1},... | collective-permute-start | bytes 199688 | tf_op jit(solution)/shard_map/ppermute | solution.py:20
  9.4 5.2 %collective-permute-start.1 = (f32[65,512]{1,0:T(8,128)S(1)}, f32[65,512]{1,0:T(8,128)S(1)}, u32[]{:S(2)}, u32[]{:S(2)}) collective-permute-start(f32[65,512]{1,0:T(8,128)S(1)} %pad_maximum_fusion.11), channel_id=1, source_target_pairs={{0,4},{1,5},{2,6},{3,7},{4,0},{5,1},{6,2},{7,3},{8,12},{9,13},{10,... | collective-permute-start | bytes 399368 | tf_op jit(solution)/shard_map/ppermute | solution.py:20
  14.7 3.6 %collective-permute-start.4 = (f32[64,1024]{1,0:T(8,128)S(1)}, f32[64,1024]{1,0:T(8,128)S(1)}, u32[]{:S(2)}, u32[]{:S(2)}) collective-permute-start(f32[64,1024]{1,0:T(8,128)S(1)} %slice.55), channel_id=1, source_target_pairs={{0,1},{1,0},{2,3},{3,2},{4,5},{5,4},{6,7},{7,6},{8,9},{9,8},{10,11... | collective-permute-start | bytes 786440 | tf_op jit(solution)/shard_map/ppermute | solution.py:20
  14.7 8.7 %collective-permute-start.2 = (f32[64,1024]{1,0:T(8,128)S(1)}, f32[64,1024]{1,0:T(8,128)S(1)}, u32[]{:S(2)}, u32[]{:S(2)}) collective-permute-start(f32[64,1024]{1,0:T(8,128)S(1)} %slice.55), channel_id=1, source_target_pairs={{0,2},{1,3},{2,0},{3,1},{4,6},{5,7},{6,4},{7,5},{8,10},{9,11},{10,... | collective-permute-start | bytes 786440 | tf_op jit(solution)/shard_map/ppermute | solution.py:20
  18.3 15.3 %copy-start.6 = (bf16[2048,1024]{1,0:T(8,128)(2,1)}, bf16[2048,1024]{1,0:T(8,128)(2,1)S(1)}, u32[]{:S(2)}) copy-start(bf16[2048,1024]{1,0:T(8,128)(2,1)S(1)} %get-tuple-element.33) | copy-start | bytes 12582916
  19.9 2.0 %copy-start.4 = (bf16[2048,1024]{1,0:T(8,128)(2,1)}, bf16[2048,1024]{1,0:T(8,128)(2,1)S(1)}, u32[]{:S(2)}) copy-start(bf16[2048,1024]{1,0:T(8,128)(2,1)S(1)} %get-tuple-element.34) | copy-start | bytes 12582916
  23.5 3.5 %collective-permute-start.3 = (f32[64,1024]{1,0:T(8,128)S(1)}, f32[64,1024]{1,0:T(8,128)S(1)}, u32[]{:S(2)}, u32[]{:S(2)}) collective-permute-start(f32[64,1024]{1,0:T(8,128)S(1)} %collective-permute-done.2), channel_id=1, source_target_pairs={{0,1},{1,0},{2,3},{3,2},{4,5},{5,4},{6,7},{7,6},{8,9},{9,8},{10,11... | collective-permute-start | bytes 786440 | tf_op jit(solution)/shard_map/ppermute | solution.py:20
  25.0 1.9 %copy-start.2 = (bf16[2048,1024]{1,0:T(8,128)(2,1)}, bf16[2048,1024]{1,0:T(8,128)(2,1)S(1)}, u32[]{:S(2)}) copy-start(bf16[2048,1024]{1,0:T(8,128)(2,1)S(1)} %get-tuple-element.35) | copy-start | bytes 12582916
  28.6 2.0 %copy-start = (bf16[2048,1024]{1,0:T(8,128)(2,1)}, bf16[2048,1024]{1,0:T(8,128)(2,1)S(1)}, u32[]{:S(2)}) copy-start(bf16[2048,1024]{1,0:T(8,128)(2,1)S(1)} %get-tuple-element.32.refs_4_) | copy-start | bytes 12582916
  30.6 6.3 %collective-permute-start.6 = (f32[32,1024]{1,0:T(8,128)S(1)}, f32[32,1024]{1,0:T(8,128)S(1)}, u32[]{:S(2)}, u32[]{:S(2)}) collective-permute-start(f32[32,1024]{1,0:T(8,128)S(1)} %get-tuple-element.31.refs_0_.refs_10_), channel_id=1, source_target_pairs={{0,2},{1,3},{2,0},{3,1},{4,6},{5,7},{6,4},{7,5},{8,10},{9,11},{10,... | collective-permute-start | bytes 393224 | tf_op jit(solution)/shard_map/ppermute | solution.py:20
  32.3 1.4 %collective-permute-start.5 = (f32[32,1024]{1,0:T(8,128)S(1)}, f32[32,1024]{1,0:T(8,128)S(1)}, u32[]{:S(2)}, u32[]{:S(2)}) collective-permute-start(f32[32,1024]{1,0:T(8,128)S(1)} %get-tuple-element.31.refs_0_.refs_10_), channel_id=1, source_target_pairs={{0,1},{1,0},{2,3},{3,2},{4,5},{5,4},{6,7},{7,6},{8,9},{9,8},{10,11... | collective-permute-start | bytes 393224 | tf_op jit(solution)/shard_map/ppermute | solution.py:20
  33.7 3.6 %copy-start.3 = (bf16[2048,1024]{1,0:T(8,128)(2,1)S(1)}, bf16[2048,1024]{1,0:T(8,128)(2,1)}, u32[]{:S(2)}) copy-start(bf16[2048,1024]{1,0:T(8,128)(2,1)} %copy-done.2) | copy-start | bytes 12582916
  36.9 2.2 %copy-start.1 = (bf16[2048,1024]{1,0:T(8,128)(2,1)S(1)}, bf16[2048,1024]{1,0:T(8,128)(2,1)}, u32[]{:S(2)}) copy-start(bf16[2048,1024]{1,0:T(8,128)(2,1)} %copy-done) | copy-start | bytes 12582916
  36.9 1.4 %collective-permute-start.7 = (f32[32,1024]{1,0:T(8,128)S(1)}, f32[32,1024]{1,0:T(8,128)S(1)}, u32[]{:S(2)}, u32[]{:S(2)}) collective-permute-start(f32[32,1024]{1,0:T(8,128)S(1)} %collective-permute-done.6.refs_2_), channel_id=1, source_target_pairs={{0,1},{1,0},{2,3},{3,2},{4,5},{5,4},{6,7},{7,6},{8,9},{9,8},{10,11... | collective-permute-start | bytes 393224 | tf_op jit(solution)/shard_map/ppermute | solution.py:20
  38.1 2.6 %copy-start.7 = (bf16[2048,1024]{1,0:T(8,128)(2,1)S(1)}, bf16[2048,1024]{1,0:T(8,128)(2,1)}, u32[]{:S(2)}) copy-start(bf16[2048,1024]{1,0:T(8,128)(2,1)} %copy-done.6) | copy-start | bytes 12582916
  40.2 2.3 %copy-start.5 = (bf16[2048,1024]{1,0:T(8,128)(2,1)S(1)}, bf16[2048,1024]{1,0:T(8,128)(2,1)}, u32[]{:S(2)}) copy-start(bf16[2048,1024]{1,0:T(8,128)(2,1)} %copy-done.4) | copy-start | bytes 12582916
  40.2 5.7 %collective-permute-start.9 = (f32[32,1024]{1,0:T(8,128)S(1)}, f32[32,1024]{1,0:T(8,128)S(1)}, u32[]{:S(2)}, u32[]{:S(2)}) collective-permute-start(f32[32,1024]{1,0:T(8,128)S(1)} %get-tuple-element.36.refs_0_), channel_id=1, source_target_pairs={{0,2},{1,3},{2,0},{3,1},{4,6},{5,7},{6,4},{7,5},{8,10},{9,11},{10,... | collective-permute-start | bytes 393224 | tf_op jit(solution)/shard_map/ppermute | solution.py:20
  40.7 1.3 %collective-permute-start.8 = (f32[32,1024]{1,0:T(8,128)S(1)}, f32[32,1024]{1,0:T(8,128)S(1)}, u32[]{:S(2)}, u32[]{:S(2)}) collective-permute-start(f32[32,1024]{1,0:T(8,128)S(1)} %get-tuple-element.36.refs_0_), channel_id=1, source_target_pairs={{0,1},{1,0},{2,3},{3,2},{4,5},{5,4},{6,7},{7,6},{8,9},{9,8},{10,11... | collective-permute-start | bytes 393224 | tf_op jit(solution)/shard_map/ppermute | solution.py:20
  45.9 1.3 %collective-permute-start.10 = (f32[32,1024]{1,0:T(8,128)S(1)}, f32[32,1024]{1,0:T(8,128)S(1)}, u32[]{:S(2)}, u32[]{:S(2)}) collective-permute-start(f32[32,1024]{1,0:T(8,128)S(1)} %collective-permute-done.9.refs_2_), channel_id=1, source_target_pairs={{0,1},{1,0},{2,3},{3,2},{4,5},{5,4},{6,7},{7,6},{8,9},{9,8},{10,11... | collective-permute-start | bytes 393224 | tf_op jit(solution)/shard_map/ppermute | solution.py:20
  48.2 5.8 %collective-permute-start.12 = (f32[32,1024]{1,0:T(8,128)S(1)}, f32[32,1024]{1,0:T(8,128)S(1)}, u32[]{:S(2)}, u32[]{:S(2)}) collective-permute-start(f32[32,1024]{1,0:T(8,128)S(1)} %get-tuple-element.42.refs_0_), channel_id=1, source_target_pairs={{0,2},{1,3},{2,0},{3,1},{4,6},{5,7},{6,4},{7,5},{8,10},{9,11},{10,... | collective-permute-start | bytes 393224 | tf_op jit(solution)/shard_map/ppermute | solution.py:20
  48.8 1.3 %collective-permute-start.11 = (f32[32,1024]{1,0:T(8,128)S(1)}, f32[32,1024]{1,0:T(8,128)S(1)}, u32[]{:S(2)}, u32[]{:S(2)}) collective-permute-start(f32[32,1024]{1,0:T(8,128)S(1)} %get-tuple-element.42.refs_0_), channel_id=1, source_target_pairs={{0,1},{1,0},{2,3},{3,2},{4,5},{5,4},{6,7},{7,6},{8,9},{9,8},{10,11... | collective-permute-start | bytes 393224 | tf_op jit(solution)/shard_map/ppermute | solution.py:20
  54.0 1.3 %collective-permute-start.13 = (f32[32,1024]{1,0:T(8,128)S(1)}, f32[32,1024]{1,0:T(8,128)S(1)}, u32[]{:S(2)}, u32[]{:S(2)}) collective-permute-start(f32[32,1024]{1,0:T(8,128)S(1)} %collective-permute-done.12.refs_2_), channel_id=1, source_target_pairs={{0,1},{1,0},{2,3},{3,2},{4,5},{5,4},{6,7},{7,6},{8,9},{9,8},{10,11... | collective-permute-start | bytes 393224 | tf_op jit(solution)/shard_map/ppermute | solution.py:20
  56.4 3.8 %collective-permute-start.14 = (f32[32,1]{1,0:T(8,128)S(1)}, f32[32,1]{1,0:T(8,128)S(1)}, u32[]{:S(2)}, u32[]{:S(2)}) collective-permute-start(f32[32,1]{1,0:T(8,128)S(1)} %get-tuple-element.50), channel_id=1, source_target_pairs={{0,2},{1,3},{2,0},{3,1},{4,6},{5,7},{6,4},{7,5},{8,10},{9,11},{10,... | collective-permute-start | bytes 392 | tf_op jit(solution)/shard_map/ppermute | solution.py:20
  60.2 1.2 %collective-permute-start.15 = (f32[32,1]{1,0:T(8,128)S(1)}, f32[32,1]{1,0:T(8,128)S(1)}, u32[]{:S(2)}, u32[]{:S(2)}) collective-permute-start(f32[32,1]{1,0:T(8,128)S(1)} %add.33), channel_id=1, source_target_pairs={{0,1},{1,0},{2,3},{3,2},{4,5},{5,4},{6,7},{7,6},{8,9},{9,8},{10,11... | collective-permute-start | bytes 392 | tf_op jit(solution)/shard_map/ppermute | solution.py:20

commit v16 on v13

--- a/solution.py
+++ b/solution.py
@@ -57,8 +57,11 @@
     return left, right
 
 
-def scaled_operand_kernel(mine_ref, scale_ref, right_ref):
-    right_ref[...] = operands(mine_ref[...] * scale_ref[...])[1]
+def prepare_kernel(part_ref, scale_ref, right_ref, *copy_ref):
+    feats = scale_ref.shape[0]
+    right_ref[...] = operands(part_ref[:feats] * scale_ref[...])[1]
+    for ref in copy_ref:
+        ref[...] = part_ref[:-1]
 
 
 def build_kernel(rows_ref, vectors_ref, scale_ref, right_ref, sum_ref, tile_ref, out_ref):
@@ -115,6 +118,18 @@
     )(*args)
 
 
+def prepare(part, scale, copy=False):
+    feats, cols = scale.shape[0], part.shape[1]
+    outs = (jax.ShapeDtypeStruct((6 * feats + NORM_ROWS, cols), jnp.bfloat16),)
+    if copy:
+        outs += (jax.ShapeDtypeStruct((part.shape[0] - 1, cols), part.dtype),)
+    return call(prepare_kernel, outs, part, scale, flops=10**9, bytes_accessed=feats * cols, transcendentals=0)
+
+
+def join(*xs):
+    return jnp.concatenate(xs, axis=1)
+
+
 def build_piece(rows, vectors, scale, right, total):
     count, cols = rows.shape[1], right.shape[1]
     outs = (jax.ShapeDtypeStruct((2 * count, cols), jnp.bfloat16), jax.ShapeDtypeStruct(total.shape, jnp.float32))
@@ -149,28 +164,53 @@
                 pieces += [came, swap(came, n, 1)]
             return pieces
 
-        mine = lax.optimization_barrier(jnp.concatenate([points, targets, noise_var[None, :]], axis=0))
-        for stride in outer:
-            mine = jnp.concatenate([mine, swap(mine, n, stride)], axis=1)
-        noise = mine[-1:]
         scale = (POINT_SCALE / lengthscale)[:, None]
-        first = arrivals(mine[:-1])
+        block = lax.optimization_barrier(jnp.concatenate([points, targets, noise_var[None, :]], axis=0))
+        fence = lax.optimization_barrier
+        tile = []
+
+        def build(x, total):
+            piece, total = build_piece(x[:feats], x[feats:], scale, right, total)
+            tile.append(piece)
+            return total
+
+        if len(outer) == 2 and len(inner) == 2:
+            far, near, side = outer[0], outer[1], inner[0]
+            by_far = swap(block, n, far)
+            right_own, copy = prepare(block, scale, True)
+            side_own = swap(copy, n, side)
+            by_near = swap(join(block, by_far), n, near)
+            right_far, copy = prepare(by_far, scale, True)
+            side_far = swap(copy, n, side)
+            last, side_own, side_far = fence((by_near[:-1], side_own, side_far))
+            side_last = swap(last, n, side)
+            right = join(right_own, right_far, *prepare(by_near, scale))
+            mine = join(block, by_far, by_near)
+            noise, mine = mine[-1:], mine[:-1]
+            across = swap(mine, n, 1)
+            my_applied = build(mine, noise * mine[feats:])
+            side_own, side_far, my_applied = fence((side_own, side_far, my_applied))
+            early = join(side_own, side_far)
+            early_across = swap(early, n, 1)
+            my_applied = build(across, my_applied)
+            side_last, my_applied = fence((side_last, my_applied))
+            last_across = swap(side_last, n, 1)
+            beside = join(early, side_last)
+            my_applied = build(beside, my_applied)
+            early_across, last_across, my_applied = fence((early_across, last_across, my_applied))
+            beside_across = join(early_across, last_across)
+            my_applied = build(beside_across, my_applied)
+            first = [mine, across, beside, beside_across]
+        else:
+            mine = block
+            for stride in outer:
+                mine = join(mine, swap(mine, n, stride))
+            (right,), noise, first = prepare(mine, scale), mine[-1:], arrivals(mine[:-1])
+            my_applied = noise * first[0][feats:]
+            for x in first:
+                my_applied = build(x, my_applied)
         cols = noise.shape[1]
-        right = call(
-            scaled_operand_kernel,
-            jax.ShapeDtypeStruct((6 * feats + NORM_ROWS, cols), jnp.bfloat16),
-            mine[:feats],
-            scale,
-            flops=feats * cols,
-            bytes_accessed=feats * cols,
-            transcendentals=0,
-        )
         starts = [x[feats:] for x in first]
-        tile = []
-        my_applied = noise * starts[0]
-        for x, start in zip(first, starts):
-            piece, my_applied = build_piece(x[:feats], start, scale, right, my_applied)
-            tile.append(piece)
 
         def operator(pieces):
             total = apply_piece(pieces[0], tile[0])

time: 56.2 us -> 55.8 us (level)
  waiting for transfers between devices: 20 us -> 19.2 us
    ppermute x16 -> x19, waiting for transfers between devices: 20 us -> 19.2 us  [swap(): return lax.ppermute(x, 'blk', [(i, i ^ stride) for i in range(n)])]
    pallas_call x5 -> x7, Pallas kernels: 6.36 us -> 6.53 us  [call(): pl.pallas_call(kernel, out_shape=outs, in_specs=[whole] * len(args), out_...]
    ppermute x16 -> x19, starting transfers between devices: 14 us -> 14 us  [swap(): return lax.ppermute(x, 'blk', [(i, i ^ stride) for i in range(n)])]
  transfers between devices with their start and end apart: 16 -> 19, of which waited for: 14 -> 13; matrix products, arithmetic and copies ran while one was open for 15% -> 15% of each run, Pallas kernels for 9% -> 9%
where the time goes in v16:
time: 55.8 us; the launch traced here: 55.6 us
  waiting for transfers between devices  19.2 us (34%)
  starting transfers between devices  14 us (25%)
  matrix products  9.82 us (18%)
  Pallas kernels  6.53 us (12%)
  other arithmetic  4.84 us (9%)
  between operations  0.95 us (2%)
    ppermute x19, waiting for transfers between devices, swap(): return lax.ppermute(x, 'blk', [(i, i ^ stride) for i in range(n)])  19.2 us
    ppermute x19, starting transfers between devices, swap(): return lax.ppermute(x, 'blk', [(i, i ^ stride) for i in range(n)])  14 us
    dot_general x12, matrix products, apply_piece(): jnp.dot(jnp.concatenate([left, right], axis=1), piece, preferred_element_...  9.82 us
    pallas_call x7, Pallas kernels, call(): pl.pallas_call(kernel, out_shape=outs, in_specs=[whole] * len(args), out_...  6.53 us
  transfers between devices with their start and end apart: 19, of which 13 were waited for; matrix products, arithmetic and copies ran while one was open for 15% of the time, Pallas kernels for 9%

profile of v16, /device:TPU:0, one launch (start us, length us, event | category | flops | bytes accessed | tf_op | source)
XLA Modules:
  0.0 55.6 jit_solution(15686311697314733079)
XLA Ops:
  0.6 0.8 %pad_maximum_fusion.19.part_ref = f32[65,256]{1,0:T(8,128)S(1)} fusion(f32[1,256]{1,0:T(1,128)} %bitcast.20, f32[32,256]{1,0:T(8,128)} %param.7, f32[32,256]{1,0:T(8,128)} %param.4), kind=kLoop, calls=%fused_computation.244 | loop fusion | flops 33280 | bytes 133120 | tf_op jit(solution)/shard_map/concatenate | solution.py:168
  1.4 4.0 %collective-permute-start = (f32[65,256]{1,0:T(8,128)S(1)}, f32[65,256]{1,0:T(8,128)S(1)}, u32[]{:S(2)}, u32[]{:S(2)}) collective-permute-start(f32[65,256]{1,0:T(8,128)S(1)} %pad_maximum_fusion.19.part_ref), channel_id=1, source_target_pairs={{0,8},{1,9},{2,10},{3,11},{4,12},{5,13},{6,14},{7,15},{8,0},{9,1},... | collective-permute-start | bytes 199688 | tf_op jit(solution)/shard_map/ppermute | solution.py:19
  6.3 1.6 %collective-permute-start.3 = (f32[64,256]{1,0:T(8,128)S(1)}, f32[64,256]{1,0:T(8,128)S(1)}, u32[]{:S(2)}, u32[]{:S(2)}) collective-permute-start(f32[64,256]{1,0:T(8,128)S(1)} %get-tuple-element.25), channel_id=1, source_target_pairs={{0,2},{1,3},{2,0},{3,1},{4,6},{5,7},{6,4},{7,5},{8,10},{9,11},{10,... | collective-permute-start | bytes 196616 | tf_op jit(solution)/shard_map/ppermute | solution.py:19
  7.9 1.5 %collective-permute-done.part_ref = f32[65,256]{1,0:T(8,128)S(1)} collective-permute-done((f32[65,256]{1,0:T(8,128)S(1)}, f32[65,256]{1,0:T(8,128)S(1)}, u32[]{:S(2)}, u32[]{:S(2)}) %collective-permute-start) | collective-permute-done | bytes 66592 | tf_op jit(solution)/shard_map/ppermute | solution.py:19
  10.2 1.6 %collective-permute-start.4 = (f32[64,256]{1,0:T(8,128)S(1)}, f32[64,256]{1,0:T(8,128)S(1)}, u32[]{:S(2)}, u32[]{:S(2)}) collective-permute-start(f32[64,256]{1,0:T(8,128)S(1)} %get-tuple-element.26), channel_id=1, source_target_pairs={{0,2},{1,3},{2,0},{3,1},{4,6},{5,7},{6,4},{7,5},{8,10},{9,11},{10,... | collective-permute-start | bytes 196616 | tf_op jit(solution)/shard_map/ppermute | solution.py:19
  11.8 2.8 %collective-permute-done.1.part_ref = f32[65,512]{1,0:T(8,128)S(1)} collective-permute-done((f32[65,512]{1,0:T(8,128)S(1)}, f32[65,512]{1,0:T(8,128)S(1)}, u32[]{:S(2)}, u32[]{:S(2)}) %collective-permute-start.1) | collective-permute-done | bytes 133152 | tf_op jit(solution)/shard_map/ppermute | solution.py:19
  14.6 1.8 %collective-permute-start.5 = (f32[64,512]{1,0:T(8,128)S(1)}, f32[64,512]{1,0:T(8,128)S(1)}, u32[]{:S(2)}, u32[]{:S(2)}) collective-permute-start(f32[64,512]{1,0:T(8,128)S(1)} %slice.120), channel_id=1, source_target_pairs={{0,2},{1,3},{2,0},{3,1},{4,6},{5,7},{6,4},{7,5},{8,10},{9,11},{10,... | collective-permute-start | bytes 393224 | tf_op jit(solution)/shard_map/ppermute | solution.py:19
  16.8 1.6 %shard_map.62 = (bf16[2048,1024]{1,0:T(8,128)(2,1)S(1)}, f32[32,1024]{1,0:T(8,128)S(1)}) custom-call(f32[32,1024]{1,0:T(8,128)S(1)} %get-tuple-element.67.rows_ref, f32[32,1024]{1,0:T(8,128)S(1)} %get-tuple-element.68.vectors_ref, f32[32,1]{1,0:T(8,128)S(1)} %copy.6.scale_ref, bf16[256,1024]{1,0:T(8,128)(2,1)S(1)} %pad_maximum_fusion.12.right_ref, ...), custom_call_target="tpu_custom_call" | custom-call | flops 872415232 | bytes 4194304 | tf_op jit(solution)/shard_map/pallas_call | solution.py:111
  19.0 1.6 %shard_map.63 = (bf16[2048,1024]{1,0:T(8,128)(2,1)S(1)}, f32[32,1024]{1,0:T(8,128)S(1)}) custom-call(f32[32,1024]{1,0:T(8,128)S(1)} %get-tuple-element.74.rows_ref, f32[32,1024]{1,0:T(8,128)S(1)} %get-tuple-element.73.vectors_ref, f32[32,1]{1,0:T(8,128)S(1)} %copy.6.scale_ref, bf16[256,1024]{1,0:T(8,128)(2,1)S(1)} %pad_maximum_fusion.12.right_ref, ...), custom_call_target="tpu_custom_call" | custom-call | flops 872415232 | bytes 4194304 | tf_op jit(solution)/shard_map/pallas_call | solution.py:111
  20.7 1.6 %shard_map.64 = (bf16[2048,1024]{1,0:T(8,128)(2,1)S(1)}, f32[32,1024]{1,0:T(8,128)S(1)}) custom-call(f32[32,1024]{1,0:T(8,128)S(1)} %get-tuple-element.72.rows_ref, f32[32,1024]{1,0:T(8,128)S(1)} %get-tuple-element.71.vectors_ref, f32[32,1]{1,0:T(8,128)S(1)} %copy.6.scale_ref, bf16[256,1024]{1,0:T(8,128)(2,1)S(1)} %pad_maximum_fusion.12.right_ref, ...), custom_call_target="tpu_custom_call" | custom-call | flops 872415232 | bytes 4194304 | tf_op jit(solution)/shard_map/pallas_call | solution.py:111
  22.4 1.6 %shard_map.65 = (bf16[2048,1024]{1,0:T(8,128)(2,1)S(1)}, f32[32,1024]{1,0:T(8,128)S(1)}) custom-call(f32[32,1024]{1,0:T(8,128)S(1)} %get-tuple-element.70.rows_ref, f32[32,1024]{1,0:T(8,128)S(1)} %get-tuple-element.69.vectors_ref, f32[32,1]{1,0:T(8,128)S(1)} %copy.6.scale_ref, bf16[256,1024]{1,0:T(8,128)(2,1)S(1)} %pad_maximum_fusion.12.right_ref, ...), custom_call_target="tpu_custom_call" | custom-call | flops 872415232 | bytes 4194304 | tf_op jit(solution)/shard_map/pallas_call | solution.py:111
  23.9 0.8 %collective-permute-start.9 = (f32[32,1024]{1,0:T(8,128)S(1)}, f32[32,1024]{1,0:T(8,128)S(1)}, u32[]{:S(2)}, u32[]{:S(2)}) collective-permute-start(f32[32,1024]{1,0:T(8,128)S(1)} %get-tuple-element.43), channel_id=1, source_target_pairs={{0,2},{1,3},{2,0},{3,1},{4,6},{5,7},{6,4},{7,5},{8,10},{9,11},{10,... | collective-permute-start | bytes 393224 | tf_op jit(solution)/shard_map/ppermute | solution.py:19
  25.0 0.8 %fusion.1 = f32[96,1024]{1,0:T(8,128)S(1)} fusion(bf16[2048,1024]{1,0:T(8,128)(2,1)S(1)} %get-tuple-element.44, bf16[32,1024]{1,0:T(8,128)(2,1)S(1)} %broadcast.4, bf16[32,1024]{1,0:T(8,128)(2,1)S(1)} %get-tuple-element.110, bf16[32,1024]{1,0:T(8,128)(2,1)S(1)} %get-tuple-element.111, bf16[32,1024]{1,0:T(8,128)(2,1)S(1)} %get-tuple-element.109), kind=kOutput, calls=%fused_computation.39 | convolution fusion | flops 405012480 | bytes 4849664 | tf_op jit(solution)/shard_map/dot_general | solution.py:144
  26.1 0.8 %convolution_add_fusion.8 = f32[96,1024]{1,0:T(8,128)S(1)} fusion(f32[96,1024]{1,0:T(8,128)S(1)} %fusion.1, bf16[2048,1024]{1,0:T(8,128)(2,1)S(1)} %get-tuple-element.45, bf16[32,1024]{1,0:T(8,128)(2,1)S(1)} %broadcast.4, bf16[32,1024]{1,0:T(8,128)(2,1)S(1)} %get-tuple-element.106, bf16[32,1024]{1,0:T(8,128)(2,1)S(1)} %get-tuple-element.107, ...), kind=kOutput, calls=%fused_computation.20 | convolution fusion | flops 405110784 | bytes 5242880 | tf_op jit(solution)/shard_map/dot_general | solution.py:144
  26.9 3.0 %collective-permute-done.9 = f32[32,1024]{1,0:T(8,128)S(1)} collective-permute-done((f32[32,1024]{1,0:T(8,128)S(1)}, f32[32,1024]{1,0:T(8,128)S(1)}, u32[]{:S(2)}, u32[]{:S(2)}) %collective-permute-start.9) | collective-permute-done | bytes 131104 | tf_op jit(solution)/shard_map/ppermute | solution.py:19
  29.9 0.8 %convolution_add_fusion.7 = f32[96,1024]{1,0:T(8,128)S(1)} fusion(f32[96,1024]{1,0:T(8,128)S(1)} %convolution_add_fusion.8, bf16[2048,1024]{1,0:T(8,128)(2,1)S(1)} %get-tuple-element.46, bf16[32,1024]{1,0:T(8,128)(2,1)S(1)} %broadcast.4, bf16[32,1024]{1,0:T(8,128)(2,1)S(1)} %get-tuple-element.102, bf16[32,1024]{1,0:T(8,128)(2,1)S(1)} %get-tuple-element.103, ...), kind=kOutput, calls=%fused_computation.19 | convolution fusion | flops 405110784 | bytes 5242880 | tf_op jit(solution)/shard_map/dot_general | solution.py:144
  31.3 0.8 %convolution_add_fusion.6 = f32[96,1024]{1,0:T(8,128)S(1)} fusion(f32[96,1024]{1,0:T(8,128)S(1)} %convolution_add_fusion.7, bf16[2048,1024]{1,0:T(8,128)(2,1)S(1)} %get-tuple-element.47, bf16[32,1024]{1,0:T(8,128)(2,1)S(1)} %broadcast.4, bf16[32,1024]{1,0:T(8,128)(2,1)S(1)} %get-tuple-element.98, bf16[32,1024]{1,0:T(8,128)(2,1)S(1)} %get-tuple-element.99, ...), kind=kOutput, calls=%fused_computation.18 | convolution fusion | flops 405110784 | bytes 5242880 | tf_op jit(solution)/shard_map/dot_general | solution.py:144
  32.7 0.8 %collective-permute-start.12 = (f32[32,1024]{1,0:T(8,128)S(1)}, f32[32,1024]{1,0:T(8,128)S(1)}, u32[]{:S(2)}, u32[]{:S(2)}) collective-permute-start(f32[32,1024]{1,0:T(8,128)S(1)} %get-tuple-element.62), channel_id=1, source_target_pairs={{0,2},{1,3},{2,0},{3,1},{4,6},{5,7},{6,4},{7,5},{8,10},{9,11},{10,... | collective-permute-start | bytes 393224 | tf_op jit(solution)/shard_map/ppermute | solution.py:19
  33.5 0.8 %fusion.10 = f32[96,1024]{1,0:T(8,128)S(1)} fusion(bf16[2048,1024]{1,0:T(8,128)(2,1)S(1)} %get-tuple-element.44, bf16[32,1024]{1,0:T(8,128)(2,1)S(1)} %broadcast.4, bf16[32,1024]{1,0:T(8,128)(2,1)S(1)} %get-tuple-element.96, bf16[32,1024]{1,0:T(8,128)(2,1)S(1)} %get-tuple-element.95, bf16[32,1024]{1,0:T(8,128)(2,1)S(1)} %get-tuple-element.61), kind=kOutput, calls=%fused_computation.44 | convolution fusion | flops 405012480 | bytes 4849664 | tf_op jit(solution)/shard_map/dot_general | solution.py:144
  34.9 0.8 %convolution_add_fusion.5 = f32[96,1024]{1,0:T(8,128)S(1)} fusion(f32[96,1024]{1,0:T(8,128)S(1)} %fusion.10, bf16[2048,1024]{1,0:T(8,128)(2,1)S(1)} %get-tuple-element.45, bf16[32,1024]{1,0:T(8,128)(2,1)S(1)} %broadcast.4, bf16[32,1024]{1,0:T(8,128)(2,1)S(1)} %get-tuple-element.93, bf16[32,1024]{1,0:T(8,128)(2,1)S(1)} %get-tuple-element.94, ...), kind=kOutput, calls=%fused_computation.17 | convolution fusion | flops 405110784 | bytes 5242880 | tf_op jit(solution)/shard_map/dot_general | solution.py:144
  35.7 2.6 %collective-permute-done.12 = f32[32,1024]{1,0:T(8,128)S(1)} collective-permute-done((f32[32,1024]{1,0:T(8,128)S(1)}, f32[32,1024]{1,0:T(8,128)S(1)}, u32[]{:S(2)}, u32[]{:S(2)}) %collective-permute-start.12) | collective-permute-done | bytes 131104 | tf_op jit(solution)/shard_map/ppermute | solution.py:19
  38.3 0.8 %convolution_add_fusion.4 = f32[96,1024]{1,0:T(8,128)S(1)} fusion(f32[96,1024]{1,0:T(8,128)S(1)} %convolution_add_fusion.5, bf16[2048,1024]{1,0:T(8,128)(2,1)S(1)} %get-tuple-element.46, bf16[32,1024]{1,0:T(8,128)(2,1)S(1)} %broadcast.4, bf16[32,1024]{1,0:T(8,128)(2,1)S(1)} %get-tuple-element.90, bf16[32,1024]{1,0:T(8,128)(2,1)S(1)} %get-tuple-element.91, ...), kind=kOutput, calls=%fused_computation.16 | convolution fusion | flops 405110784 | bytes 5242880 | tf_op jit(solution)/shard_map/dot_general | solution.py:144
  39.7 1.0 %convolution_add_fusion.3 = f32[96,1024]{1,0:T(8,128)S(1)} fusion(f32[96,1024]{1,0:T(8,128)S(1)} %convolution_add_fusion.4, bf16[2048,1024]{1,0:T(8,128)(2,1)S(1)} %get-tuple-element.47, bf16[32,1024]{1,0:T(8,128)(2,1)S(1)} %broadcast.4, bf16[32,1024]{1,0:T(8,128)(2,1)S(1)} %get-tuple-element.87, bf16[32,1024]{1,0:T(8,128)(2,1)S(1)} %get-tuple-element.88, ...), kind=kOutput, calls=%fused_computation.15 | convolution fusion | flops 405110784 | bytes 5242880 | tf_op jit(solution)/shard_map/dot_general | solution.py:144
  41.4 0.8 %collective-permute-start.15 = (f32[32,1024]{1,0:T(8,128)S(1)}, f32[32,1024]{1,0:T(8,128)S(1)}, u32[]{:S(2)}, u32[]{:S(2)}) collective-permute-start(f32[32,1024]{1,0:T(8,128)S(1)} %get-tuple-element.53), channel_id=1, source_target_pairs={{0,2},{1,3},{2,0},{3,1},{4,6},{5,7},{6,4},{7,5},{8,10},{9,11},{10,... | collective-permute-start | bytes 393224 | tf_op jit(solution)/shard_map/ppermute | solution.py:19
  42.2 0.8 %fusion.19 = f32[96,1024]{1,0:T(8,128)S(1)} fusion(bf16[2048,1024]{1,0:T(8,128)(2,1)S(1)} %get-tuple-element.44, bf16[32,1024]{1,0:T(8,128)(2,1)S(1)} %broadcast.4, bf16[32,1024]{1,0:T(8,128)(2,1)S(1)} %get-tuple-element.85, bf16[32,1024]{1,0:T(8,128)(2,1)S(1)} %get-tuple-element.84, bf16[32,1024]{1,0:T(8,128)(2,1)S(1)} %get-tuple-element.52), kind=kOutput, calls=%fused_computation.49 | convolution fusion | flops 405012480 | bytes 4849664 | tf_op jit(solution)/shard_map/dot_general | solution.py:144
  43.6 0.8 %convolution_add_fusion.2 = f32[96,1024]{1,0:T(8,128)S(1)} fusion(f32[96,1024]{1,0:T(8,128)S(1)} %fusion.19, bf16[2048,1024]{1,0:T(8,128)(2,1)S(1)} %get-tuple-element.45, bf16[32,1024]{1,0:T(8,128)(2,1)S(1)} %broadcast.4, bf16[32,1024]{1,0:T(8,128)(2,1)S(1)} %get-tuple-element.82, bf16[32,1024]{1,0:T(8,128)(2,1)S(1)} %get-tuple-element.83, ...), kind=kOutput, calls=%fused_computation.14 | convolution fusion | flops 405110784 | bytes 5242880 | tf_op jit(solution)/shard_map/dot_general | solution.py:144
  44.4 2.6 %collective-permute-done.15 = f32[32,1024]{1,0:T(8,128)S(1)} collective-permute-done((f32[32,1024]{1,0:T(8,128)S(1)}, f32[32,1024]{1,0:T(8,128)S(1)}, u32[]{:S(2)}, u32[]{:S(2)}) %collective-permute-start.15) | collective-permute-done | bytes 131104 | tf_op jit(solution)/shard_map/ppermute | solution.py:19
  47.1 0.8 %convolution_add_fusion.1 = f32[96,1024]{1,0:T(8,128)S(1)} fusion(f32[96,1024]{1,0:T(8,128)S(1)} %convolution_add_fusion.2, bf16[2048,1024]{1,0:T(8,128)(2,1)S(1)} %get-tuple-element.46, bf16[32,1024]{1,0:T(8,128)(2,1)S(1)} %broadcast.4, bf16[32,1024]{1,0:T(8,128)(2,1)S(1)} %get-tuple-element.79, bf16[32,1024]{1,0:T(8,128)(2,1)S(1)} %get-tuple-element.80, ...), kind=kOutput, calls=%fused_computation.13 | convolution fusion | flops 405110784 | bytes 5242880 | tf_op jit(solution)/shard_map/dot_general | solution.py:144
  48.4 0.8 %convolution_add_fusion = f32[96,1024]{1,0:T(8,128)S(1)} fusion(f32[96,1024]{1,0:T(8,128)S(1)} %convolution_add_fusion.1, bf16[2048,1024]{1,0:T(8,128)(2,1)S(1)} %get-tuple-element.47, bf16[32,1024]{1,0:T(8,128)(2,1)S(1)} %broadcast.4, bf16[32,1024]{1,0:T(8,128)(2,1)S(1)} %get-tuple-element.76, bf16[32,1024]{1,0:T(8,128)(2,1)S(1)} %get-tuple-element.77, ...), kind=kOutput, calls=%fused_computation.12 | convolution fusion | flops 405110784 | bytes 5242880 | tf_op jit(solution)/shard_map/dot_general | solution.py:144
  50.1 0.8 %collective-permute-start.17 = (f32[32]{0:T(128)S(1)}, f32[32]{0:T(128)S(1)}, u32[]{:S(2)}, u32[]{:S(2)}) collective-permute-start(f32[32]{0:T(128)S(1)} %get-tuple-element.50), channel_id=1, source_target_pairs={{0,2},{1,3},{2,0},{3,1},{4,6},{5,7},{6,4},{7,5},{8,10},{9,11},{10,... | collective-permute-start | bytes 392 | tf_op jit(solution)/shard_map/ppermute | solution.py:19
  50.9 2.8 %collective-permute-done.17 = f32[32]{0:T(128)S(1)} collective-permute-done((f32[32]{0:T(128)S(1)}, f32[32]{0:T(128)S(1)}, u32[]{:S(2)}, u32[]{:S(2)}) %collective-permute-start.17) | collective-permute-done | bytes 160 | tf_op jit(solution)/shard_map/ppermute | solution.py:19
  53.7 1.1 %collective-permute-done.18 = f32[32]{0:T(128)S(1)} collective-permute-done((f32[32]{0:T(128)S(1)}, f32[32]{0:T(128)S(1)}, u32[]{:S(2)}, u32[]{:S(2)}) %collective-permute-start.18) | collective-permute-done | bytes 160 | tf_op jit(solution)/shard_map/ppermute | solution.py:19
  (76 shorter events, 9.2 us)
Async XLA Ops:
  1.4 7.9 %collective-permute-start = (f32[65,256]{1,0:T(8,128)S(1)}, f32[65,256]{1,0:T(8,128)S(1)}, u32[]{:S(2)}, u32[]{:S(2)}) collective-permute-start(f32[65,256]{1,0:T(8,128)S(1)} %pad_maximum_fusion.19.part_ref), channel_id=1, source_target_pairs={{0,8},{1,9},{2,10},{3,11},{4,12},{5,13},{6,14},{7,15},{8,0},{9,1},... | collective-permute-start | bytes 199688 | tf_op jit(solution)/shard_map/ppermute | solution.py:19
  6.3 8.3 %collective-permute-start.3 = (f32[64,256]{1,0:T(8,128)S(1)}, f32[64,256]{1,0:T(8,128)S(1)}, u32[]{:S(2)}, u32[]{:S(2)}) collective-permute-start(f32[64,256]{1,0:T(8,128)S(1)} %get-tuple-element.25), channel_id=1, source_target_pairs={{0,2},{1,3},{2,0},{3,1},{4,6},{5,7},{6,4},{7,5},{8,10},{9,11},{10,... | collective-permute-start | bytes 196616 | tf_op jit(solution)/shard_map/ppermute | solution.py:19
  9.4 5.2 %collective-permute-start.1 = (f32[65,512]{1,0:T(8,128)S(1)}, f32[65,512]{1,0:T(8,128)S(1)}, u32[]{:S(2)}, u32[]{:S(2)}) collective-permute-start(f32[65,512]{1,0:T(8,128)S(1)} %pad_maximum_fusion.17), channel_id=1, source_target_pairs={{0,4},{1,5},{2,6},{3,7},{4,0},{5,1},{6,2},{7,3},{8,12},{9,13},{10,... | collective-permute-start | bytes 399368 | tf_op jit(solution)/shard_map/ppermute | solution.py:19
  10.2 4.4 %collective-permute-start.4 = (f32[64,256]{1,0:T(8,128)S(1)}, f32[64,256]{1,0:T(8,128)S(1)}, u32[]{:S(2)}, u32[]{:S(2)}) collective-permute-start(f32[64,256]{1,0:T(8,128)S(1)} %get-tuple-element.26), channel_id=1, source_target_pairs={{0,2},{1,3},{2,0},{3,1},{4,6},{5,7},{6,4},{7,5},{8,10},{9,11},{10,... | collective-permute-start | bytes 196616 | tf_op jit(solution)/shard_map/ppermute | solution.py:19
  14.6 5.9 %collective-permute-start.5 = (f32[64,512]{1,0:T(8,128)S(1)}, f32[64,512]{1,0:T(8,128)S(1)}, u32[]{:S(2)}, u32[]{:S(2)}) collective-permute-start(f32[64,512]{1,0:T(8,128)S(1)} %slice.120), channel_id=1, source_target_pairs={{0,2},{1,3},{2,0},{3,1},{4,6},{5,7},{6,4},{7,5},{8,10},{9,11},{10,... | collective-permute-start | bytes 393224 | tf_op jit(solution)/shard_map/ppermute | solution.py:19
  16.5 2.4 %collective-permute-start.2 = (f32[64,1024]{1,0:T(8,128)S(1)}, f32[64,1024]{1,0:T(8,128)S(1)}, u32[]{:S(2)}, u32[]{:S(2)}) collective-permute-start(f32[64,1024]{1,0:T(8,128)S(1)} %slice.118), channel_id=1, source_target_pairs={{0,1},{1,0},{2,3},{3,2},{4,5},{5,4},{6,7},{7,6},{8,9},{9,8},{10,11... | collective-permute-start | bytes 786440 | tf_op jit(solution)/shard_map/ppermute | solution.py:19
  18.4 3.9 %collective-permute-start.6 = (f32[64,512]{1,0:T(8,128)S(1)}, f32[64,512]{1,0:T(8,128)S(1)}, u32[]{:S(2)}, u32[]{:S(2)}) collective-permute-start(f32[64,512]{1,0:T(8,128)S(1)} %pad_maximum_fusion.18), channel_id=1, source_target_pairs={{0,1},{1,0},{2,3},{3,2},{4,5},{5,4},{6,7},{7,6},{8,9},{9,8},{10,11... | collective-permute-start | bytes 393224 | tf_op jit(solution)/shard_map/ppermute | solution.py:19
  20.6 1.7 %collective-permute-start.7 = (f32[64,512]{1,0:T(8,128)S(1)}, f32[64,512]{1,0:T(8,128)S(1)}, u32[]{:S(2)}, u32[]{:S(2)}) collective-permute-start(f32[64,512]{1,0:T(8,128)S(1)} %collective-permute-done.5), channel_id=1, source_target_pairs={{0,1},{1,0},{2,3},{3,2},{4,5},{5,4},{6,7},{7,6},{8,9},{9,8},{10,11... | collective-permute-start | bytes 393224 | tf_op jit(solution)/shard_map/ppermute | solution.py:19
  23.9 5.9 %collective-permute-start.9 = (f32[32,1024]{1,0:T(8,128)S(1)}, f32[32,1024]{1,0:T(8,128)S(1)}, u32[]{:S(2)}, u32[]{:S(2)}) collective-permute-start(f32[32,1024]{1,0:T(8,128)S(1)} %get-tuple-element.43), channel_id=1, source_target_pairs={{0,2},{1,3},{2,0},{3,1},{4,6},{5,7},{6,4},{7,5},{8,10},{9,11},{10,... | collective-permute-start | bytes 393224 | tf_op jit(solution)/shard_map/ppermute | solution.py:19
  24.7 1.3 %collective-permute-start.8 = (f32[32,1024]{1,0:T(8,128)S(1)}, f32[32,1024]{1,0:T(8,128)S(1)}, u32[]{:S(2)}, u32[]{:S(2)}) collective-permute-start(f32[32,1024]{1,0:T(8,128)S(1)} %get-tuple-element.43), channel_id=1, source_target_pairs={{0,1},{1,0},{2,3},{3,2},{4,5},{5,4},{6,7},{7,6},{8,9},{9,8},{10,11... | collective-permute-start | bytes 393224 | tf_op jit(solution)/shard_map/ppermute | solution.py:19
  29.9 1.3 %collective-permute-start.10 = (f32[32,1024]{1,0:T(8,128)S(1)}, f32[32,1024]{1,0:T(8,128)S(1)}, u32[]{:S(2)}, u32[]{:S(2)}) collective-permute-start(f32[32,1024]{1,0:T(8,128)S(1)} %collective-permute-done.9), channel_id=1, source_target_pairs={{0,1},{1,0},{2,3},{3,2},{4,5},{5,4},{6,7},{7,6},{8,9},{9,8},{10,11... | collective-permute-start | bytes 393224 | tf_op jit(solution)/shard_map/ppermute | solution.py:19
  32.7 5.6 %collective-permute-start.12 = (f32[32,1024]{1,0:T(8,128)S(1)}, f32[32,1024]{1,0:T(8,128)S(1)}, u32[]{:S(2)}, u32[]{:S(2)}) collective-permute-start(f32[32,1024]{1,0:T(8,128)S(1)} %get-tuple-element.62), channel_id=1, source_target_pairs={{0,2},{1,3},{2,0},{3,1},{4,6},{5,7},{6,4},{7,5},{8,10},{9,11},{10,... | collective-permute-start | bytes 393224 | tf_op jit(solution)/shard_map/ppermute | solution.py:19
  33.5 1.3 %collective-permute-start.11 = (f32[32,1024]{1,0:T(8,128)S(1)}, f32[32,1024]{1,0:T(8,128)S(1)}, u32[]{:S(2)}, u32[]{:S(2)}) collective-permute-start(f32[32,1024]{1,0:T(8,128)S(1)} %get-tuple-element.62), channel_id=1, source_target_pairs={{0,1},{1,0},{2,3},{3,2},{4,5},{5,4},{6,7},{7,6},{8,9},{9,8},{10,11... | collective-permute-start | bytes 393224 | tf_op jit(solution)/shard_map/ppermute | solution.py:19
  38.3 1.3 %collective-permute-start.13 = (f32[32,1024]{1,0:T(8,128)S(1)}, f32[32,1024]{1,0:T(8,128)S(1)}, u32[]{:S(2)}, u32[]{:S(2)}) collective-permute-start(f32[32,1024]{1,0:T(8,128)S(1)} %collective-permute-done.12), channel_id=1, source_target_pairs={{0,1},{1,0},{2,3},{3,2},{4,5},{5,4},{6,7},{7,6},{8,9},{9,8},{10,11... | collective-permute-start | bytes 393224 | tf_op jit(solution)/shard_map/ppermute | solution.py:19
  41.4 5.6 %collective-permute-start.15 = (f32[32,1024]{1,0:T(8,128)S(1)}, f32[32,1024]{1,0:T(8,128)S(1)}, u32[]{:S(2)}, u32[]{:S(2)}) collective-permute-start(f32[32,1024]{1,0:T(8,128)S(1)} %get-tuple-element.53), channel_id=1, source_target_pairs={{0,2},{1,3},{2,0},{3,1},{4,6},{5,7},{6,4},{7,5},{8,10},{9,11},{10,... | collective-permute-start | bytes 393224 | tf_op jit(solution)/shard_map/ppermute | solution.py:19
  42.2 1.3 %collective-permute-start.14 = (f32[32,1024]{1,0:T(8,128)S(1)}, f32[32,1024]{1,0:T(8,128)S(1)}, u32[]{:S(2)}, u32[]{:S(2)}) collective-permute-start(f32[32,1024]{1,0:T(8,128)S(1)} %get-tuple-element.53), channel_id=1, source_target_pairs={{0,1},{1,0},{2,3},{3,2},{4,5},{5,4},{6,7},{7,6},{8,9},{9,8},{10,11... | collective-permute-start | bytes 393224 | tf_op jit(solution)/shard_map/ppermute | solution.py:19
  47.0 1.3 %collective-permute-start.16 = (f32[32,1024]{1,0:T(8,128)S(1)}, f32[32,1024]{1,0:T(8,128)S(1)}, u32[]{:S(2)}, u32[]{:S(2)}) collective-permute-start(f32[32,1024]{1,0:T(8,128)S(1)} %collective-permute-done.15), channel_id=1, source_target_pairs={{0,1},{1,0},{2,3},{3,2},{4,5},{5,4},{6,7},{7,6},{8,9},{9,8},{10,11... | collective-permute-start | bytes 393224 | tf_op jit(solution)/shard_map/ppermute | solution.py:19
  50.1 3.6 %collective-permute-start.17 = (f32[32]{0:T(128)S(1)}, f32[32]{0:T(128)S(1)}, u32[]{:S(2)}, u32[]{:S(2)}) collective-permute-start(f32[32]{0:T(128)S(1)} %get-tuple-element.50), channel_id=1, source_target_pairs={{0,2},{1,3},{2,0},{3,1},{4,6},{5,7},{6,4},{7,5},{8,10},{9,11},{10,... | collective-permute-start | bytes 392 | tf_op jit(solution)/shard_map/ppermute | solution.py:19
  53.7 1.1 %collective-permute-start.18 = (f32[32]{0:T(128)S(1)}, f32[32]{0:T(128)S(1)}, u32[]{:S(2)}, u32[]{:S(2)}) collective-permute-start(f32[32]{0:T(128)S(1)} %add.113), channel_id=1, source_target_pairs={{0,1},{1,0},{2,3},{3,2},{4,5},{5,4},{6,7},{7,6},{8,9},{9,8},{10,11... | collective-permute-start | bytes 392 | tf_op jit(solution)/shard_map/ppermute | solution.py:19

commit v17 on v16

--- a/solution.py
+++ b/solution.py
@@ -123,7 +123,7 @@
     outs = (jax.ShapeDtypeStruct((6 * feats + NORM_ROWS, cols), jnp.bfloat16),)
     if copy:
         outs += (jax.ShapeDtypeStruct((part.shape[0] - 1, cols), part.dtype),)
-    return call(prepare_kernel, outs, part, scale, flops=10**9, bytes_accessed=feats * cols, transcendentals=0)
+    return call(prepare_kernel, outs, part, scale, flops=10**10, bytes_accessed=feats * cols, transcendentals=0)
 
 
 def join(*xs):
@@ -157,11 +157,10 @@
         outer, inner = [s for s in strides if s >= team], [s for s in strides if s < team]
 
         def arrivals(x):
-            pieces, sent = [x, swap(x, n, 1)], [x]
+            pieces, sent = [join(x, swap(x, n, 1))], [x]
             for stride in inner[:-1]:
-                came = swap(sent[0] if len(sent) == 1 else jnp.concatenate(sent, axis=1), n, stride)
-                sent.append(came)
-                pieces += [came, swap(came, n, 1)]
+                sent.append(swap(join(*sent), n, stride))
+                pieces += [sent[-1], swap(sent[-1], n, 1)]
             return pieces
 
         scale = (POINT_SCALE / lengthscale)[:, None]
@@ -187,55 +186,76 @@
             right = join(right_own, right_far, *prepare(by_near, scale))
             mine = join(block, by_far, by_near)
             noise, mine = mine[-1:], mine[:-1]
-            across = swap(mine, n, 1)
-            my_applied = build(mine, noise * mine[feats:])
-            side_own, side_far, my_applied = fence((side_own, side_far, my_applied))
-            early = join(side_own, side_far)
-            early_across = swap(early, n, 1)
-            my_applied = build(across, my_applied)
+            pair = join(mine, swap(mine, n, 1))
+            my_applied = build(pair, noise * mine[feats:])
             side_last, my_applied = fence((side_last, my_applied))
-            last_across = swap(side_last, n, 1)
-            beside = join(early, side_last)
+            beside = join(side_own, side_far, side_last)
+            beside_across = swap(beside, n, 1)
             my_applied = build(beside, my_applied)
-            early_across, last_across, my_applied = fence((early_across, last_across, my_applied))
-            beside_across = join(early_across, last_across)
             my_applied = build(beside_across, my_applied)
-            first = [mine, across, beside, beside_across]
+            first = [pair, beside, beside_across]
         else:
             mine = block
             for stride in outer:
                 mine = join(mine, swap(mine, n, stride))
             (right,), noise, first = prepare(mine, scale), mine[-1:], arrivals(mine[:-1])
-            my_applied = noise * first[0][feats:]
+            my_applied = noise * mine[feats:-1]
             for x in first:
                 my_applied = build(x, my_applied)
         cols = noise.shape[1]
         starts = [x[feats:] for x in first]
 
-        def operator(pieces):
-            total = apply_piece(pieces[0], tile[0])
-            for x, piece in zip(pieces[1:], tile[1:]):
-                total = lax.optimization_barrier(total + apply_piece(x, piece))
-            return total[:probes] + (total[probes : 2 * probes] + total[2 * probes :]) + noise * pieces[0]
+        def exchange(x, turn):
+            raw, pieces, total = [x], [], None
+
+            def add(k, piece):
+                nonlocal total
+                if k:
+                    piece, total = fence((piece, total))
+                pieces.append(turn(k, piece))
+                term = apply_piece(pieces[-1], tile[k])
+                total = term if total is None else total + term
+                return piece
+
+            came = [swap(x, n, stride) for stride in inner[:1] if stride > 1]
+            beside = swap(x, n, 1)
+            add(0, join(x, beside))
+            for k, stride in enumerate(inner[:-1]):
+                arrived, total = fence((came[0] if k == 0 else swap(join(*raw), n, stride), total))
+                raw.append(arrived)
+                beside = swap(arrived, n, 1)
+                add(1 + 2 * k, arrived)
+                add(2 + 2 * k, beside)
+            return total[:probes] + (total[probes : 2 * probes] + total[2 * probes :]) + noise * pieces[0][:, :cols], pieces
 
         residual = direction = jnp.concatenate(starts, axis=1)
         my_solution = jnp.zeros_like(direction[:, :width])
         norm_now = jnp.sum(residual * residual, axis=1)
-        my_image = my_applied
+        my_next, applied = exchange(my_applied, lambda k, piece: piece)
+        image = applied
         for iteration in range(ITERS - 1):
-            pieces = arrivals(my_applied)
-            my_next = operator(pieces)
-            applied = jnp.concatenate(pieces, axis=1)
-            curve = jnp.sum(direction * applied, axis=1)
+            last = iteration == ITERS - 2
+            pieces, sent = (applied, my_next) if last else fence((applied, my_next))
+            whole = jnp.concatenate(pieces, axis=1)
+            curve = jnp.sum(direction * whole, axis=1)
             step_size = (norm_now / curve)[:, None]
             my_solution = my_solution + step_size * direction[:, :width]
-            residual = residual - step_size * applied
+            residual = residual - step_size * whole
             norm_next = jnp.sum(residual * residual, axis=1)
             ratio = (norm_next / norm_now)[:, None]
-            my_image = my_image - step_size * my_next
-            my_applied = my_image + ratio * my_applied
             direction = residual + ratio * direction
             norm_now = norm_next
+            new_image = []
+
+            def turn(k, piece):
+                new_image.append(image[k] - step_size * piece)
+                return new_image[k] + ratio * applied[k]
+
+            if last:
+                my_applied = image[0][:, :cols] - step_size * my_next + ratio * applied[0][:, :cols]
+            else:
+                my_next, applied = exchange(sent, turn)
+                image = new_image
         curve = add_up(jnp.sum(direction[:, :cols] * my_applied, axis=1), n, inner)
         step_size = (norm_now / curve)[:, None]
         my_solution = my_solution + step_size * direction[:, :width]

time: 55.8 us -> 56.3 us (level)
  starting transfers between devices: 14 us -> 18.1 us
  waiting for transfers between devices: 19.2 us -> 15.1 us
  other arithmetic: 4.84 us -> 5.74 us
    ppermute x19 -> x18, starting transfers between devices: 14 us -> 18.1 us  [swap(): return lax.ppermute(x, 'blk', [(i, i ^ stride) for i in range(n)])]
    ppermute x19 -> x18, waiting for transfers between devices: 19.2 us -> 15.1 us  [swap(): return lax.ppermute(x, 'blk', [(i, i ^ stride) for i in range(n)])]
    dot_general x12 -> x9, matrix products: 9.82 us -> 9.4 us  [apply_piece(): jnp.dot(jnp.concatenate([left, right], axis=1), piece, preferred_element_...]
    pallas_call x7 -> x6, Pallas kernels: 6.53 us -> 6.36 us  [call(): pl.pallas_call(kernel, out_shape=outs, in_specs=[whole] * len(args), out_...]
  transfers between devices with their start and end apart: 19 -> 18, of which waited for: 13 -> 11; matrix products, arithmetic and copies ran while one was open for 15% -> 17% of each run, Pallas kernels for 9% -> 9%
where the time goes in v17:
time: 56.3 us; the launch traced here: 56.1 us
  starting transfers between devices  18.1 us (32%)
  waiting for transfers between devices  15.1 us (27%)
  matrix products  9.4 us (17%)
  Pallas kernels  6.36 us (11%)
  other arithmetic  5.74 us (10%)
  between operations  1.07 us (2%)
    ppermute x18, starting transfers between devices, swap(): return lax.ppermute(x, 'blk', [(i, i ^ stride) for i in range(n)])  18.1 us
    ppermute x18, waiting for transfers between devices, swap(): return lax.ppermute(x, 'blk', [(i, i ^ stride) for i in range(n)])  15.1 us
    dot_general x9, matrix products, apply_piece(): jnp.dot(jnp.concatenate([left, right], axis=1), piece, preferred_element_...  9.4 us
    pallas_call x6, Pallas kernels, call(): pl.pallas_call(kernel, out_shape=outs, in_specs=[whole] * len(args), out_...  6.36 us
  transfers between devices with their start and end apart: 18, of which 11 were waited for; matrix products, arithmetic and copies ran while one was open for 17% of the time, Pallas kernels for 9%

profile of v17, /device:TPU:0, one launch (start us, length us, event | category | flops | bytes accessed | tf_op | source)
XLA Modules:
  0.0 56.1 jit_solution(13589832492540731068)
XLA Ops:
  0.6 0.8 %pad_maximum_fusion.15.part_ref = f32[65,256]{1,0:T(8,128)S(1)} fusion(f32[1,256]{1,0:T(1,128)} %bitcast.17, f32[32,256]{1,0:T(8,128)} %param.7, f32[32,256]{1,0:T(8,128)} %param.4), kind=kLoop, calls=%fused_computation.203 | loop fusion | flops 33280 | bytes 133120 | tf_op jit(solution)/shard_map/concatenate | solution.py:167
  1.4 4.0 %collective-permute-start = (f32[65,256]{1,0:T(8,128)S(1)}, f32[65,256]{1,0:T(8,128)S(1)}, u32[]{:S(2)}, u32[]{:S(2)}) collective-permute-start(f32[65,256]{1,0:T(8,128)S(1)} %pad_maximum_fusion.15.part_ref), channel_id=1, source_target_pairs={{0,8},{1,9},{2,10},{3,11},{4,12},{5,13},{6,14},{7,15},{8,0},{9,1},... | collective-permute-start | bytes 199688 | tf_op jit(solution)/shard_map/ppermute | solution.py:19
  5.5 0.7 %divide_bitcast_fusion = f32[32,1]{0,1:T(1,128)S(1)} fusion(f32[32]{0:T(128)} %param.5), kind=kLoop, calls=%fused_computation.226 | loop fusion | flops 32 | bytes 256 | tf_op jit(solution)/shard_map/broadcast_in_dim | solution.py:166
  6.3 1.6 %collective-permute-start.3 = (f32[64,256]{1,0:T(8,128)S(1)}, f32[64,256]{1,0:T(8,128)S(1)}, u32[]{:S(2)}, u32[]{:S(2)}) collective-permute-start(f32[64,256]{1,0:T(8,128)S(1)} %get-tuple-element.40), channel_id=1, source_target_pairs={{0,2},{1,3},{2,0},{3,1},{4,6},{5,7},{6,4},{7,5},{8,10},{9,11},{10,... | collective-permute-start | bytes 196616 | tf_op jit(solution)/shard_map/ppermute | solution.py:19
  7.9 1.5 %collective-permute-done.part_ref = f32[65,256]{1,0:T(8,128)S(1)} collective-permute-done((f32[65,256]{1,0:T(8,128)S(1)}, f32[65,256]{1,0:T(8,128)S(1)}, u32[]{:S(2)}, u32[]{:S(2)}) %collective-permute-start) | collective-permute-done | bytes 66592 | tf_op jit(solution)/shard_map/ppermute | solution.py:19
  9.4 0.7 %collective-permute-start.1 = (f32[65,512]{1,0:T(8,128)S(1)}, f32[65,512]{1,0:T(8,128)S(1)}, u32[]{:S(2)}, u32[]{:S(2)}) collective-permute-start(f32[65,512]{1,0:T(8,128)S(1)} %pad_maximum_fusion.14), channel_id=1, source_target_pairs={{0,4},{1,5},{2,6},{3,7},{4,0},{5,1},{6,2},{7,3},{8,12},{9,13},{10,... | collective-permute-start | bytes 399368 | tf_op jit(solution)/shard_map/ppermute | solution.py:19
  10.2 1.6 %collective-permute-start.4 = (f32[64,256]{1,0:T(8,128)S(1)}, f32[64,256]{1,0:T(8,128)S(1)}, u32[]{:S(2)}, u32[]{:S(2)}) collective-permute-start(f32[64,256]{1,0:T(8,128)S(1)} %get-tuple-element.41), channel_id=1, source_target_pairs={{0,2},{1,3},{2,0},{3,1},{4,6},{5,7},{6,4},{7,5},{8,10},{9,11},{10,... | collective-permute-start | bytes 196616 | tf_op jit(solution)/shard_map/ppermute | solution.py:19
  11.8 2.8 %collective-permute-done.1.part_ref = f32[65,512]{1,0:T(8,128)S(1)} collective-permute-done((f32[65,512]{1,0:T(8,128)S(1)}, f32[65,512]{1,0:T(8,128)S(1)}, u32[]{:S(2)}, u32[]{:S(2)}) %collective-permute-start.1) | collective-permute-done | bytes 133152 | tf_op jit(solution)/shard_map/ppermute | solution.py:19
  14.8 1.8 %collective-permute-start.5 = (f32[64,512]{1,0:T(8,128)S(1)}, f32[64,512]{1,0:T(8,128)S(1)}, u32[]{:S(2)}, u32[]{:S(2)}) collective-permute-start(f32[64,512]{1,0:T(8,128)S(1)} %slice.128), channel_id=1, source_target_pairs={{0,2},{1,3},{2,0},{3,1},{4,6},{5,7},{6,4},{7,5},{8,10},{9,11},{10,... | collective-permute-start | bytes 393224 | tf_op jit(solution)/shard_map/ppermute | solution.py:19
  16.8 2.9 %shard_map.62 = (bf16[4096,1024]{1,0:T(8,128)(2,1)S(1)}, f32[32,1024]{1,0:T(8,128)S(1)}) custom-call(f32[32,2048]{1,0:T(8,128)S(1)} %get-tuple-element.104.rows_ref, f32[32,2048]{1,0:T(8,128)S(1)} %get-tuple-element.103.vectors_ref, f32[32,1]{1,0:T(8,128)S(1)} %copy.6.scale_ref, bf16[256,1024]{1,0:T(8,128)(2,1)S(1)} %pad_maximum_fusion.9.right_ref, ...), custom_call_target="tpu_custom_call" | custom-call | flops 1744830464 | bytes 8388608 | tf_op jit(solution)/shard_map/pallas_call | solution.py:111
  19.8 0.9 %collective-permute-done.5 = f32[64,512]{1,0:T(8,128)S(1)} collective-permute-done((f32[64,512]{1,0:T(8,128)S(1)}, f32[64,512]{1,0:T(8,128)S(1)}, u32[]{:S(2)}, u32[]{:S(2)}) %collective-permute-start.5) | collective-permute-done | bytes 131104 | tf_op jit(solution)/shard_map/ppermute | solution.py:19
  20.8 1.6 %shard_map.63 = (bf16[2048,1024]{1,0:T(8,128)(2,1)S(1)}, f32[32,1024]{1,0:T(8,128)S(1)}) custom-call(f32[32,1024]{1,0:T(8,128)S(1)} %get-tuple-element.113.rows_ref, f32[32,1024]{1,0:T(8,128)S(1)} %get-tuple-element.112.vectors_ref, f32[32,1]{1,0:T(8,128)S(1)} %copy.6.scale_ref, bf16[256,1024]{1,0:T(8,128)(2,1)S(1)} %pad_maximum_fusion.9.right_ref, ...), custom_call_target="tpu_custom_call" | custom-call | flops 872415232 | bytes 4194304 | tf_op jit(solution)/shard_map/pallas_call | solution.py:111
  22.5 1.6 %shard_map.64 = (bf16[2048,1024]{1,0:T(8,128)(2,1)S(1)}, f32[32,1024]{1,0:T(8,128)S(1)}) custom-call(f32[32,1024]{1,0:T(8,128)S(1)} %get-tuple-element.115.rows_ref, f32[32,1024]{1,0:T(8,128)S(1)} %get-tuple-element.114.vectors_ref, f32[32,1]{1,0:T(8,128)S(1)} %copy.6.scale_ref, bf16[256,1024]{1,0:T(8,128)(2,1)S(1)} %pad_maximum_fusion.9.right_ref, ...), custom_call_target="tpu_custom_call" | custom-call | flops 872415232 | bytes 4194304 | tf_op jit(solution)/shard_map/pallas_call | solution.py:111
  24.6 1.7 %collective-permute-start.8 = (f32[32,1024]{1,0:T(8,128)S(1)}, f32[32,1024]{1,0:T(8,128)S(1)}, u32[]{:S(2)}, u32[]{:S(2)}) collective-permute-start(f32[32,1024]{1,0:T(8,128)S(1)} %get-tuple-element.51), channel_id=1, source_target_pairs={{0,2},{1,3},{2,0},{3,1},{4,6},{5,7},{6,4},{7,5},{8,10},{9,11},{10,... | collective-permute-start | bytes 393224 | tf_op jit(solution)/shard_map/ppermute | solution.py:19
  26.4 1.5 %fusion.1 = f32[96,1024]{1,0:T(8,128)S(1)} fusion(bf16[4096,1024]{1,0:T(8,128)(2,1)S(1)} %get-tuple-element.52, bf16[32,2048]{1,0:T(8,128)(2,1)S(1)} %broadcast.7, bf16[32,2048]{1,0:T(8,128)(2,1)S(1)} %get-tuple-element.110, bf16[32,2048]{1,0:T(8,128)(2,1)S(1)} %get-tuple-element.111, bf16[32,2048]{1,0:T(8,128)(2,1)S(1)} %get-tuple-element.109), kind=kOutput, calls=%fused_computation.10 | convolution fusion | flops 810024960 | bytes 9306112 | tf_op jit(solution)/shard_map/dot_general | solution.py:144
  27.9 2.1 %collective-permute-done.8 = f32[32,1024]{1,0:T(8,128)S(1)} collective-permute-done((f32[32,1024]{1,0:T(8,128)S(1)}, f32[32,1024]{1,0:T(8,128)S(1)}, u32[]{:S(2)}, u32[]{:S(2)}) %collective-permute-start.8) | collective-permute-done | bytes 131104 | tf_op jit(solution)/shard_map/ppermute | solution.py:19
  30.2 0.8 %fusion.34 = f32[96,1024]{1,0:T(8,128)S(1)} fusion(bf16[2048,1024]{1,0:T(8,128)(2,1)S(1)} %get-tuple-element.56, bf16[32,1024]{1,0:T(8,128)(2,1)S(1)} %broadcast.8, bf16[32,1024]{1,0:T(8,128)(2,1)S(1)} %get-tuple-element.128, bf16[32,1024]{1,0:T(8,128)(2,1)S(1)} %get-tuple-element.129, bf16[32,1024]{1,0:T(8,128)(2,1)S(1)} %get-tuple-element.127), kind=kOutput, calls=%fused_computation.58 | convolution fusion | flops 405012480 | bytes 4849664 | tf_op jit(solution)/shard_map/dot_general | solution.py:144
  31.5 0.8 %fusion.37 = f32[96,1024]{1,0:T(8,128)S(1)} fusion(bf16[2048,1024]{1,0:T(8,128)(2,1)S(1)} %get-tuple-element.59, bf16[32,1024]{1,0:T(8,128)(2,1)S(1)} %broadcast.8, bf16[32,1024]{1,0:T(8,128)(2,1)S(1)} %get-tuple-element.125, bf16[32,1024]{1,0:T(8,128)(2,1)S(1)} %get-tuple-element.126, bf16[32,1024]{1,0:T(8,128)(2,1)S(1)} %get-tuple-element.124), kind=kOutput, calls=%fused_computation.60 | convolution fusion | flops 405012480 | bytes 4849664 | tf_op jit(solution)/shard_map/dot_general | solution.py:144
  32.7 1.7 %collective-permute-start.11 = (f32[32,1024]{1,0:T(8,128)S(1)}, f32[32,1024]{1,0:T(8,128)S(1)}, u32[]{:S(2)}, u32[]{:S(2)}) collective-permute-start(f32[32,1024]{1,0:T(8,128)S(1)} %fusion.129), channel_id=1, source_target_pairs={{0,2},{1,3},{2,0},{3,1},{4,6},{5,7},{6,4},{7,5},{8,10},{9,11},{10,... | collective-permute-start | bytes 393224 | tf_op jit(solution)/shard_map/ppermute | solution.py:19
  35.2 1.5 %fusion.4 = f32[96,1024]{1,0:T(8,128)S(1)} fusion(bf16[4096,1024]{1,0:T(8,128)(2,1)S(1)} %get-tuple-element.52, bf16[32,2048]{1,0:T(8,128)(2,1)S(1)} %broadcast.7, bf16[32,2048]{1,0:T(8,128)(2,1)S(1)} %get-tuple-element.108, bf16[32,2048]{1,0:T(8,128)(2,1)S(1)} %get-tuple-element.107, bf16[32,2048]{1,0:T(8,128)(2,1)S(1)} %get-tuple-element.101), kind=kOutput, calls=%fused_computation.12 | convolution fusion | flops 810024960 | bytes 9306112 | tf_op jit(solution)/shard_map/dot_general | solution.py:144
  36.6 1.8 %collective-permute-done.11 = f32[32,1024]{1,0:T(8,128)S(1)} collective-permute-done((f32[32,1024]{1,0:T(8,128)S(1)}, f32[32,1024]{1,0:T(8,128)S(1)}, u32[]{:S(2)}, u32[]{:S(2)}) %collective-permute-start.11) | collective-permute-done | bytes 131104 | tf_op jit(solution)/shard_map/ppermute | solution.py:19
  38.6 0.8 %fusion.40 = f32[96,1024]{1,0:T(8,128)S(1)} fusion(bf16[2048,1024]{1,0:T(8,128)(2,1)S(1)} %get-tuple-element.56, bf16[32,1024]{1,0:T(8,128)(2,1)S(1)} %broadcast.8, bf16[32,1024]{1,0:T(8,128)(2,1)S(1)} %get-tuple-element.123, bf16[32,1024]{1,0:T(8,128)(2,1)S(1)} %get-tuple-element.122, bf16[32,1024]{1,0:T(8,128)(2,1)S(1)} %get-tuple-element.99), kind=kOutput, calls=%fused_computation.62 | convolution fusion | flops 405012480 | bytes 4849664 | tf_op jit(solution)/shard_map/dot_general | solution.py:144
  40.1 1.0 %fusion.43 = f32[96,1024]{1,0:T(8,128)S(1)} fusion(bf16[2048,1024]{1,0:T(8,128)(2,1)S(1)} %get-tuple-element.59, bf16[32,1024]{1,0:T(8,128)(2,1)S(1)} %broadcast.8, bf16[32,1024]{1,0:T(8,128)(2,1)S(1)} %get-tuple-element.121, bf16[32,1024]{1,0:T(8,128)(2,1)S(1)} %get-tuple-element.120, bf16[32,1024]{1,0:T(8,128)(2,1)S(1)} %get-tuple-element.97), kind=kOutput, calls=%fused_computation.64 | convolution fusion | flops 405012480 | bytes 4849664 | tf_op jit(solution)/shard_map/dot_general | solution.py:144
  41.4 1.7 %collective-permute-start.14 = (f32[32,1024]{1,0:T(8,128)S(1)}, f32[32,1024]{1,0:T(8,128)S(1)}, u32[]{:S(2)}, u32[]{:S(2)}) collective-permute-start(f32[32,1024]{1,0:T(8,128)S(1)} %fusion.126), channel_id=1, source_target_pairs={{0,2},{1,3},{2,0},{3,1},{4,6},{5,7},{6,4},{7,5},{8,10},{9,11},{10,... | collective-permute-start | bytes 393224 | tf_op jit(solution)/shard_map/ppermute | solution.py:19
  44.1 1.5 %fusion.7 = f32[96,1024]{1,0:T(8,128)S(1)} fusion(bf16[4096,1024]{1,0:T(8,128)(2,1)S(1)} %get-tuple-element.52, bf16[32,2048]{1,0:T(8,128)(2,1)S(1)} %broadcast.7, bf16[32,2048]{1,0:T(8,128)(2,1)S(1)} %get-tuple-element.106, bf16[32,2048]{1,0:T(8,128)(2,1)S(1)} %get-tuple-element.105, bf16[32,2048]{1,0:T(8,128)(2,1)S(1)} %get-tuple-element.90), kind=kOutput, calls=%fused_computation.14 | convolution fusion | flops 810024960 | bytes 9306112 | tf_op jit(solution)/shard_map/dot_general | solution.py:144
  45.6 1.6 %collective-permute-done.14 = f32[32,1024]{1,0:T(8,128)S(1)} collective-permute-done((f32[32,1024]{1,0:T(8,128)S(1)}, f32[32,1024]{1,0:T(8,128)S(1)}, u32[]{:S(2)}, u32[]{:S(2)}) %collective-permute-start.14) | collective-permute-done | bytes 131104 | tf_op jit(solution)/shard_map/ppermute | solution.py:19
  47.4 0.8 %fusion.46 = f32[96,1024]{1,0:T(8,128)S(1)} fusion(bf16[2048,1024]{1,0:T(8,128)(2,1)S(1)} %get-tuple-element.56, bf16[32,1024]{1,0:T(8,128)(2,1)S(1)} %broadcast.8, bf16[32,1024]{1,0:T(8,128)(2,1)S(1)} %get-tuple-element.119, bf16[32,1024]{1,0:T(8,128)(2,1)S(1)} %get-tuple-element.118, bf16[32,1024]{1,0:T(8,128)(2,1)S(1)} %get-tuple-element.88), kind=kOutput, calls=%fused_computation.66 | convolution fusion | flops 405012480 | bytes 4849664 | tf_op jit(solution)/shard_map/dot_general | solution.py:144
  49.4 0.8 %fusion.49 = f32[96,1024]{1,0:T(8,128)S(1)} fusion(bf16[2048,1024]{1,0:T(8,128)(2,1)S(1)} %get-tuple-element.59, bf16[32,1024]{1,0:T(8,128)(2,1)S(1)} %broadcast.8, bf16[32,1024]{1,0:T(8,128)(2,1)S(1)} %get-tuple-element.117, bf16[32,1024]{1,0:T(8,128)(2,1)S(1)} %get-tuple-element.116, bf16[32,1024]{1,0:T(8,128)(2,1)S(1)} %get-tuple-element.82), kind=kOutput, calls=%fused_computation.68 | convolution fusion | flops 405012480 | bytes 4849664 | tf_op jit(solution)/shard_map/dot_general | solution.py:144
  50.6 1.8 %collective-permute-start.16 = (f32[32]{0:T(128)S(1)}, f32[32]{0:T(128)S(1)}, u32[]{:S(2)}, u32[]{:S(2)}) collective-permute-start(f32[32]{0:T(128)S(1)} %get-tuple-element.80), channel_id=1, source_target_pairs={{0,2},{1,3},{2,0},{3,1},{4,6},{5,7},{6,4},{7,5},{8,10},{9,11},{10,... | collective-permute-start | bytes 392 | tf_op jit(solution)/shard_map/ppermute | solution.py:19
  52.4 1.8 %collective-permute-done.16 = f32[32]{0:T(128)S(1)} collective-permute-done((f32[32]{0:T(128)S(1)}, f32[32]{0:T(128)S(1)}, u32[]{:S(2)}, u32[]{:S(2)}) %collective-permute-start.16) | collective-permute-done | bytes 160 | tf_op jit(solution)/shard_map/ppermute | solution.py:19
  54.2 1.1 %collective-permute-done.17 = f32[32]{0:T(128)S(1)} collective-permute-done((f32[32]{0:T(128)S(1)}, f32[32]{0:T(128)S(1)}, u32[]{:S(2)}, u32[]{:S(2)}) %collective-permute-start.17) | collective-permute-done | bytes 160 | tf_op jit(solution)/shard_map/ppermute | solution.py:19
  55.4 0.7 %fusion.130 = (f32[32,256]{1,0:T(8,128)}, f32[32,256]{1,0:T(8,128)}) fusion(f32[32,1024]{1,0:T(8,128)S(1)} %get-tuple-element.81, f32[32,4096]{1,0:T(8,128)S(1)} %get-tuple-element.85, f32[32]{0:T(128)S(1)} %add_divide_fusion, f32[32,4096]{1,0:T(8,128)S(1)} %multiply_add_fusion, f32[32,4096]{1,0:T(8,128)S(1)} %get-tuple-element.87, f32[32]{0:T(128)S(1)} %div.57, ...), kind=kLoop, calls=%fused_computation.205 | loop fusion | flops 73728 | bytes 262656 | tf_op jit(solution)/shard_map/sub | solution.py:262
  (85 shorter events, 6.9 us)
Async XLA Ops:
  1.4 7.9 %collective-permute-start = (f32[65,256]{1,0:T(8,128)S(1)}, f32[65,256]{1,0:T(8,128)S(1)}, u32[]{:S(2)}, u32[]{:S(2)}) collective-permute-start(f32[65,256]{1,0:T(8,128)S(1)} %pad_maximum_fusion.15.part_ref), channel_id=1, source_target_pairs={{0,8},{1,9},{2,10},{3,11},{4,12},{5,13},{6,14},{7,15},{8,0},{9,1},... | collective-permute-start | bytes 199688 | tf_op jit(solution)/shard_map/ppermute | solution.py:19
  6.3 8.4 %collective-permute-start.3 = (f32[64,256]{1,0:T(8,128)S(1)}, f32[64,256]{1,0:T(8,128)S(1)}, u32[]{:S(2)}, u32[]{:S(2)}) collective-permute-start(f32[64,256]{1,0:T(8,128)S(1)} %get-tuple-element.40), channel_id=1, source_target_pairs={{0,2},{1,3},{2,0},{3,1},{4,6},{5,7},{6,4},{7,5},{8,10},{9,11},{10,... | collective-permute-start | bytes 196616 | tf_op jit(solution)/shard_map/ppermute | solution.py:19
  9.4 5.2 %collective-permute-start.1 = (f32[65,512]{1,0:T(8,128)S(1)}, f32[65,512]{1,0:T(8,128)S(1)}, u32[]{:S(2)}, u32[]{:S(2)}) collective-permute-start(f32[65,512]{1,0:T(8,128)S(1)} %pad_maximum_fusion.14), channel_id=1, source_target_pairs={{0,4},{1,5},{2,6},{3,7},{4,0},{5,1},{6,2},{7,3},{8,12},{9,13},{10,... | collective-permute-start | bytes 399368 | tf_op jit(solution)/shard_map/ppermute | solution.py:19
  10.2 4.5 %collective-permute-start.4 = (f32[64,256]{1,0:T(8,128)S(1)}, f32[64,256]{1,0:T(8,128)S(1)}, u32[]{:S(2)}, u32[]{:S(2)}) collective-permute-start(f32[64,256]{1,0:T(8,128)S(1)} %get-tuple-element.41), channel_id=1, source_target_pairs={{0,2},{1,3},{2,0},{3,1},{4,6},{5,7},{6,4},{7,5},{8,10},{9,11},{10,... | collective-permute-start | bytes 196616 | tf_op jit(solution)/shard_map/ppermute | solution.py:19
  14.7 2.1 %collective-permute-start.2 = (f32[64,1024]{1,0:T(8,128)S(1)}, f32[64,1024]{1,0:T(8,128)S(1)}, u32[]{:S(2)}, u32[]{:S(2)}) collective-permute-start(f32[64,1024]{1,0:T(8,128)S(1)} %slice.125), channel_id=1, source_target_pairs={{0,1},{1,0},{2,3},{3,2},{4,5},{5,4},{6,7},{7,6},{8,9},{9,8},{10,11... | collective-permute-start | bytes 786440 | tf_op jit(solution)/shard_map/ppermute | solution.py:19
  14.8 6.0 %collective-permute-start.5 = (f32[64,512]{1,0:T(8,128)S(1)}, f32[64,512]{1,0:T(8,128)S(1)}, u32[]{:S(2)}, u32[]{:S(2)}) collective-permute-start(f32[64,512]{1,0:T(8,128)S(1)} %slice.128), channel_id=1, source_target_pairs={{0,2},{1,3},{2,0},{3,1},{4,6},{5,7},{6,4},{7,5},{8,10},{9,11},{10,... | collective-permute-start | bytes 393224 | tf_op jit(solution)/shard_map/ppermute | solution.py:19
  20.7 1.7 %collective-permute-start.6 = (f32[64,1024]{1,0:T(8,128)S(1)}, f32[64,1024]{1,0:T(8,128)S(1)}, u32[]{:S(2)}, u32[]{:S(2)}) collective-permute-start(f32[64,1024]{1,0:T(8,128)S(1)} %constant_dynamic-update-slice_fusion), channel_id=1, source_target_pairs={{0,1},{1,0},{2,3},{3,2},{4,5},{5,4},{6,7},{7,6},{8,9},{9,8},{10,11... | collective-permute-start | bytes 786440 | tf_op jit(solution)/shard_map/ppermute | solution.py:19
  24.0 2.3 %collective-permute-start.7 = (f32[32,1024]{1,0:T(8,128)S(1)}, f32[32,1024]{1,0:T(8,128)S(1)}, u32[]{:S(2)}, u32[]{:S(2)}) collective-permute-start(f32[32,1024]{1,0:T(8,128)S(1)} %get-tuple-element.51), channel_id=1, source_target_pairs={{0,1},{1,0},{2,3},{3,2},{4,5},{5,4},{6,7},{7,6},{8,9},{9,8},{10,11... | collective-permute-start | bytes 393224 | tf_op jit(solution)/shard_map/ppermute | solution.py:19
  24.6 5.5 %collective-permute-start.8 = (f32[32,1024]{1,0:T(8,128)S(1)}, f32[32,1024]{1,0:T(8,128)S(1)}, u32[]{:S(2)}, u32[]{:S(2)}) collective-permute-start(f32[32,1024]{1,0:T(8,128)S(1)} %get-tuple-element.51), channel_id=1, source_target_pairs={{0,2},{1,3},{2,0},{3,1},{4,6},{5,7},{6,4},{7,5},{8,10},{9,11},{10,... | collective-permute-start | bytes 393224 | tf_op jit(solution)/shard_map/ppermute | solution.py:19
  30.1 1.4 %collective-permute-start.9 = (f32[32,1024]{1,0:T(8,128)S(1)}, f32[32,1024]{1,0:T(8,128)S(1)}, u32[]{:S(2)}, u32[]{:S(2)}) collective-permute-start(f32[32,1024]{1,0:T(8,128)S(1)} %collective-permute-done.8), channel_id=1, source_target_pairs={{0,1},{1,0},{2,3},{3,2},{4,5},{5,4},{6,7},{7,6},{8,9},{9,8},{10,11... | collective-permute-start | bytes 393224 | tf_op jit(solution)/shard_map/ppermute | solution.py:19
  32.4 2.5 %collective-permute-start.10 = (f32[32,1024]{1,0:T(8,128)S(1)}, f32[32,1024]{1,0:T(8,128)S(1)}, u32[]{:S(2)}, u32[]{:S(2)}) collective-permute-start(f32[32,1024]{1,0:T(8,128)S(1)} %fusion.129), channel_id=1, source_target_pairs={{0,1},{1,0},{2,3},{3,2},{4,5},{5,4},{6,7},{7,6},{8,9},{9,8},{10,11... | collective-permute-start | bytes 393224 | tf_op jit(solution)/shard_map/ppermute | solution.py:19
  32.7 5.8 %collective-permute-start.11 = (f32[32,1024]{1,0:T(8,128)S(1)}, f32[32,1024]{1,0:T(8,128)S(1)}, u32[]{:S(2)}, u32[]{:S(2)}) collective-permute-start(f32[32,1024]{1,0:T(8,128)S(1)} %fusion.129), channel_id=1, source_target_pairs={{0,2},{1,3},{2,0},{3,1},{4,6},{5,7},{6,4},{7,5},{8,10},{9,11},{10,... | collective-permute-start | bytes 393224 | tf_op jit(solution)/shard_map/ppermute | solution.py:19
  38.6 1.4 %collective-permute-start.12 = (f32[32,1024]{1,0:T(8,128)S(1)}, f32[32,1024]{1,0:T(8,128)S(1)}, u32[]{:S(2)}, u32[]{:S(2)}) collective-permute-start(f32[32,1024]{1,0:T(8,128)S(1)} %collective-permute-done.11), channel_id=1, source_target_pairs={{0,1},{1,0},{2,3},{3,2},{4,5},{5,4},{6,7},{7,6},{8,9},{9,8},{10,11... | collective-permute-start | bytes 393224 | tf_op jit(solution)/shard_map/ppermute | solution.py:19
  41.2 2.7 %collective-permute-start.13 = (f32[32,1024]{1,0:T(8,128)S(1)}, f32[32,1024]{1,0:T(8,128)S(1)}, u32[]{:S(2)}, u32[]{:S(2)}) collective-permute-start(f32[32,1024]{1,0:T(8,128)S(1)} %fusion.126), channel_id=1, source_target_pairs={{0,1},{1,0},{2,3},{3,2},{4,5},{5,4},{6,7},{7,6},{8,9},{9,8},{10,11... | collective-permute-start | bytes 393224 | tf_op jit(solution)/shard_map/ppermute | solution.py:19
  41.4 5.8 %collective-permute-start.14 = (f32[32,1024]{1,0:T(8,128)S(1)}, f32[32,1024]{1,0:T(8,128)S(1)}, u32[]{:S(2)}, u32[]{:S(2)}) collective-permute-start(f32[32,1024]{1,0:T(8,128)S(1)} %fusion.126), channel_id=1, source_target_pairs={{0,2},{1,3},{2,0},{3,1},{4,6},{5,7},{6,4},{7,5},{8,10},{9,11},{10,... | collective-permute-start | bytes 393224 | tf_op jit(solution)/shard_map/ppermute | solution.py:19
  47.3 1.4 %collective-permute-start.15 = (f32[32,1024]{1,0:T(8,128)S(1)}, f32[32,1024]{1,0:T(8,128)S(1)}, u32[]{:S(2)}, u32[]{:S(2)}) collective-permute-start(f32[32,1024]{1,0:T(8,128)S(1)} %collective-permute-done.14), channel_id=1, source_target_pairs={{0,1},{1,0},{2,3},{3,2},{4,5},{5,4},{6,7},{7,6},{8,9},{9,8},{10,11... | collective-permute-start | bytes 393224 | tf_op jit(solution)/shard_map/ppermute | solution.py:19
  50.6 3.6 %collective-permute-start.16 = (f32[32]{0:T(128)S(1)}, f32[32]{0:T(128)S(1)}, u32[]{:S(2)}, u32[]{:S(2)}) collective-permute-start(f32[32]{0:T(128)S(1)} %get-tuple-element.80), channel_id=1, source_target_pairs={{0,2},{1,3},{2,0},{3,1},{4,6},{5,7},{6,4},{7,5},{8,10},{9,11},{10,... | collective-permute-start | bytes 392 | tf_op jit(solution)/shard_map/ppermute | solution.py:19
  54.2 1.1 %collective-permute-start.17 = (f32[32]{0:T(128)S(1)}, f32[32]{0:T(128)S(1)}, u32[]{:S(2)}, u32[]{:S(2)}) collective-permute-start(f32[32]{0:T(128)S(1)} %add.117), channel_id=1, source_target_pairs={{0,1},{1,0},{2,3},{3,2},{4,5},{5,4},{6,7},{7,6},{8,9},{9,8},{10,11... | collective-permute-start | bytes 392 | tf_op jit(solution)/shard_map/ppermute | solution.py:19

commit v18 on v16

--- a/solution.py
+++ b/solution.py
@@ -61,17 +61,20 @@
     feats = scale_ref.shape[0]
     right_ref[...] = operands(part_ref[:feats] * scale_ref[...])[1]
     for ref in copy_ref:
-        ref[...] = part_ref[:-1]
-
-
-def build_kernel(rows_ref, vectors_ref, scale_ref, right_ref, sum_ref, tile_ref, out_ref):
+        ref[...] = part_ref[...]
+
+
+def build_kernel(rows_ref, scale_ref, right_ref, *refs):
+    applies = len(refs) > 1
+    vectors_ref, sum_ref, tile_ref, out_ref = refs if applies else (None, None, *refs, None)
     total, cols = rows_ref.shape[1], right_ref.shape[1]
-    probes = vectors_ref.shape[0]
     block, step = min(total, BUILD_ROWS), min(cols, 256)
-    high, rest = halve(vectors_ref[...])
-    mid, rest = halve(rest)
-    twice = jnp.concatenate([high, mid], axis=0)
-    thrice = jnp.concatenate([high, mid, rest.astype(jnp.bfloat16)], axis=0)
+    if applies:
+        probes = vectors_ref.shape[0]
+        high, rest = halve(vectors_ref[...])
+        mid, rest = halve(rest)
+        twice = jnp.concatenate([high, mid], axis=0)
+        thrice = jnp.concatenate([high, mid, rest.astype(jnp.bfloat16)], axis=0)
     steps = [(top, at) for top in range(0, total, block) for at in range(0, cols, step)]
     lefts, powers, parts = {}, {}, {}
 
@@ -101,9 +104,10 @@
         if k + 1 < len(steps):
             contract(*steps[k + 1])
         raise_power(*chunk)
-        if k:
+        if k and applies:
             apply(*steps[k - 1])
-    apply(*steps[-1])
+    if applies:
+        apply(*steps[-1])
 
 
 def call(kernel, outs, *args, **cost):
@@ -122,7 +126,7 @@
     feats, cols = scale.shape[0], part.shape[1]
     outs = (jax.ShapeDtypeStruct((6 * feats + NORM_ROWS, cols), jnp.bfloat16),)
     if copy:
-        outs += (jax.ShapeDtypeStruct((part.shape[0] - 1, cols), part.dtype),)
+        outs += (jax.ShapeDtypeStruct(part.shape, part.dtype),)
     return call(prepare_kernel, outs, part, scale, flops=10**9, bytes_accessed=feats * cols, transcendentals=0)
 
 
@@ -130,18 +134,34 @@
     return jnp.concatenate(xs, axis=1)
 
 
-def build_piece(rows, vectors, scale, right, total):
+def build_piece(rows, scale, right, vectors=None, total=None):
     count, cols = rows.shape[1], right.shape[1]
-    outs = (jax.ShapeDtypeStruct((2 * count, cols), jnp.bfloat16), jax.ShapeDtypeStruct(total.shape, jnp.float32))
+    outs = (jax.ShapeDtypeStruct((2 * count, cols), jnp.bfloat16),)
     cost = dict(flops=2 * count * cols * 416, bytes_accessed=4 * count * cols, transcendentals=count * cols)
-    return call(build_kernel, outs, rows, vectors, scale, right, total, **cost)
+    args = (rows, scale, right)
+    if vectors is not None:
+        outs, args = (*outs, jax.ShapeDtypeStruct(total.shape, jnp.float32)), (*args, vectors, total)
+    return call(build_kernel, outs, *args, **cost)
+
+
+def parts_of(vectors):
+    high, mid, low = split(vectors, 3)
+    return jnp.concatenate([high, mid, low], axis=0)
+
+
+def apply_parts(parts, piece):
+    probes = parts.shape[0] // 3
+    right = jnp.concatenate([parts[: 2 * probes], jnp.zeros_like(parts[2 * probes :])], axis=0)
+    return jnp.dot(jnp.concatenate([parts, right], axis=1), piece, preferred_element_type=jnp.float32)
 
 
 def apply_piece(vectors, piece):
-    high, mid, low = split(vectors, 3)
-    left = jnp.concatenate([high, mid, low], axis=0)
-    right = jnp.concatenate([high, mid, jnp.zeros_like(low)], axis=0)
-    return jnp.dot(jnp.concatenate([left, right], axis=1), piece, preferred_element_type=jnp.float32)
+    return apply_parts(parts_of(vectors), piece)
+
+
+def collect(total):
+    probes = total.shape[0] // 3
+    return total[:probes] + (total[probes : 2 * probes] + total[2 * probes :])
 
 
 def solution(mesh):
@@ -170,7 +190,7 @@
         tile = []
 
         def build(x, total):
-            piece, total = build_piece(x[:feats], x[feats:], scale, right, total)
+            piece, total = build_piece(x[:feats], scale, right, x[feats:], total)
             tile.append(piece)
             return total
 
@@ -182,7 +202,7 @@
             by_near = swap(join(block, by_far), n, near)
             right_far, copy = prepare(by_far, scale, True)
             side_far = swap(copy, n, side)
-            last, side_own, side_far = fence((by_near[:-1], side_own, side_far))
+            last, side_own, side_far = fence((by_near, side_own, side_far))
             side_last = swap(last, n, side)
             right = join(right_own, right_far, *prepare(by_near, scale))
             mine = join(block, by_far, by_near)
@@ -191,16 +211,19 @@
             my_applied = build(mine, noise * mine[feats:])
             side_own, side_far, my_applied = fence((side_own, side_far, my_applied))
             early = join(side_own, side_far)
-            early_across = swap(early, n, 1)
+            early_across = swap(early[:-1], n, 1)
             my_applied = build(across, my_applied)
             side_last, my_applied = fence((side_last, my_applied))
-            last_across = swap(side_last, n, 1)
+            last_across = swap(side_last[:-1], n, 1)
             beside = join(early, side_last)
-            my_applied = build(beside, my_applied)
-            early_across, last_across, my_applied = fence((early_across, last_across, my_applied))
+            noise_beside, beside = beside[-1:], beside[:-1]
+            my_far = build(beside, jnp.zeros_like(my_applied))
+            early_across, last_across, my_far = fence((early_across, last_across, my_far))
             beside_across = join(early_across, last_across)
-            my_applied = build(beside_across, my_applied)
+            my_far = build(beside_across, my_far)
+            my_applied = my_applied + my_far
             first = [mine, across, beside, beside_across]
+            far_rows = [beside[:feats], beside_across[:feats]]
         else:
             mine = block
             for stride in outer:
@@ -209,23 +232,41 @@
             my_applied = noise * first[0][feats:]
             for x in first:
                 my_applied = build(x, my_applied)
+            my_far, far_rows = my_applied, []
         cols = noise.shape[1]
         starts = [x[feats:] for x in first]
 
-        def operator(pieces):
-            total = apply_piece(pieces[0], tile[0])
-            for x, piece in zip(pieces[1:], tile[1:]):
-                total = lax.optimization_barrier(total + apply_piece(x, piece))
-            return total[:probes] + (total[probes : 2 * probes] + total[2 * probes :]) + noise * pieces[0]
-
-        residual = direction = jnp.concatenate(starts, axis=1)
+        far_tile, right_far = [], None
+
+        def exchange(x):
+            nonlocal right_far
+            parts, passed = fence((parts_of(x), x))
+            pieces, sent = [x, swap(passed, n, 1)], [x]
+            total = fence(apply_parts(parts, tile[0]))
+            total = near = fence(total + apply_piece(pieces[1], tile[1]))
+            for k, stride in enumerate(inner[:-1]):
+                arrived = swap(join(*sent), n, stride)
+                if len(far_tile) < len(far_rows):
+                    rows, columns, total = fence((far_rows[len(far_tile)], far_rows[0], total))
+                    if right_far is None:
+                        (right_far,) = prepare(columns, scale)
+                    (piece,) = build_piece(rows, scale, right_far)
+                    arrived, piece, right_far, total = fence((arrived, piece, right_far, total))
+                    far_tile.append(piece)
+                sent.append(arrived)
+                pieces += [arrived, swap(arrived, n, 1)]
+                for at in (2 + 2 * k, 3 + 2 * k):
+                    total = total + apply_piece(pieces[at], tile[at])
+                    total = fence(total) if at < len(tile) - 1 else total
+            return collect(total - near), collect(total) + noise * x, pieces
+
+        residual = direction = join(*starts)
         my_solution = jnp.zeros_like(direction[:, :width])
         norm_now = jnp.sum(residual * residual, axis=1)
-        my_image = my_applied
+        my_image, far_image = my_applied, my_far
         for iteration in range(ITERS - 1):
-            pieces = arrivals(my_applied)
-            my_next = operator(pieces)
-            applied = jnp.concatenate(pieces, axis=1)
+            far_next, my_next, pieces = exchange(my_applied)
+            applied = join(*pieces)
             curve = jnp.sum(direction * applied, axis=1)
             step_size = (norm_now / curve)[:, None]
             my_solution = my_solution + step_size * direction[:, :width]
@@ -234,9 +275,17 @@
             ratio = (norm_next / norm_now)[:, None]
             my_image = my_image - step_size * my_next
             my_applied = my_image + ratio * my_applied
+            far_image = far_image - step_size * far_next
+            my_far = far_image + ratio * my_far
             direction = residual + ratio * direction
             norm_now = norm_next
-        curve = add_up(jnp.sum(direction[:, :cols] * my_applied, axis=1), n, inner)
+        mine = direction[:, :cols]
+        if far_rows:
+            side, beside = direction[:, 2 * cols : 3 * cols], direction[:, 3 * cols :]
+            image = collect(apply_piece(side, far_tile[0]) + apply_piece(beside, far_tile[1])) + noise_beside * side
+            curve = add_up(jnp.sum(mine * (my_applied + my_far) + side * image, axis=1), n, [1])
+        else:
+            curve = add_up(jnp.sum(mine * my_applied, axis=1), n, inner)
         step_size = (norm_now / curve)[:, None]
         my_solution = my_solution + step_size * direction[:, :width]
         return my_solution, residual[:, :width] - step_size * my_applied[:, :width]

time: 55.8 us -> 54.3 us (0.973)
  waiting for transfers between devices: 19.2 us -> 12.3 us
  Pallas kernels: 6.53 us -> 8.82 us
  matrix products: 9.82 us -> 11.7 us
  other arithmetic: 4.84 us -> 5.71 us
    ppermute x19 -> x18, waiting for transfers between devices: 19.2 us -> 12.3 us  [swap(): return lax.ppermute(x, 'blk', [(i, i ^ stride) for i in range(n)])]
    pallas_call x7 -> x10, Pallas kernels: 6.53 us -> 8.82 us  [call(): pl.pallas_call(kernel, out_shape=outs, in_specs=[whole] * len(args), out_...]
    dot_general x12 -> x14, matrix products: 9.82 us -> 11.7 us  [apply_parts(): jnp.dot(jnp.concatenate([parts, right], axis=1), piece, preferred_element...]
    ppermute x19 -> x18, starting transfers between devices: 14 us -> 14.2 us  [swap(): return lax.ppermute(x, 'blk', [(i, i ^ stride) for i in range(n)])]
  transfers between devices with their start and end apart: 19 -> 18, of which waited for: 13 -> 12; matrix products, arithmetic and copies ran while one was open for 15% -> 17% of each run, Pallas kernels for 9% -> 13%
where the time goes in v18:
time: 54.3 us; the launch traced here: 54.2 us
  starting transfers between devices  14.2 us (26%)
  waiting for transfers between devices  12.3 us (23%)
  matrix products  11.7 us (22%)
  Pallas kernels  8.82 us (16%)
  other arithmetic  5.71 us (11%)
  between operations  1.16 us (2%)
    ppermute x18, starting transfers between devices, swap(): return lax.ppermute(x, 'blk', [(i, i ^ stride) for i in range(n)])  14.2 us
    ppermute x18, waiting for transfers between devices, swap(): return lax.ppermute(x, 'blk', [(i, i ^ stride) for i in range(n)])  12.3 us
    dot_general x14, matrix products, apply_parts(): jnp.dot(jnp.concatenate([parts, right], axis=1), piece, preferred_element...  11.7 us
    pallas_call x10, Pallas kernels, call(): pl.pallas_call(kernel, out_shape=outs, in_specs=[whole] * len(args), out_...  8.82 us
  transfers between devices with their start and end apart: 18, of which 12 were waited for; matrix products, arithmetic and copies ran while one was open for 17% of the time, Pallas kernels for 13%

profile of v18, /device:TPU:0, one launch (start us, length us, event | category | flops | bytes accessed | tf_op | source)
XLA Modules:
  0.0 54.2 jit_solution(4035296676833855699)
XLA Ops:
  1.4 4.0 %collective-permute-start = (f32[65,256]{1,0:T(8,128)S(1)}, f32[65,256]{1,0:T(8,128)S(1)}, u32[]{:S(2)}, u32[]{:S(2)}) collective-permute-start(f32[65,256]{1,0:T(8,128)S(1)} %pad_maximum_fusion.11.part_ref), channel_id=1, source_target_pairs={{0,8},{1,9},{2,10},{3,11},{4,12},{5,13},{6,14},{7,15},{8,0},{9,1},... | collective-permute-start | bytes 199688 | tf_op jit(solution)/shard_map/ppermute | solution.py:19
  6.3 1.6 %collective-permute-start.3 = (f32[65,256]{1,0:T(8,128)S(1)}, f32[65,256]{1,0:T(8,128)S(1)}, u32[]{:S(2)}, u32[]{:S(2)}) collective-permute-start(f32[65,256]{1,0:T(8,128)S(1)} %get-tuple-element.43), channel_id=1, source_target_pairs={{0,2},{1,3},{2,0},{3,1},{4,6},{5,7},{6,4},{7,5},{8,10},{9,11},{10,... | collective-permute-start | bytes 199688 | tf_op jit(solution)/shard_map/ppermute | solution.py:19
  7.9 1.5 %collective-permute-done.part_ref = f32[65,256]{1,0:T(8,128)S(1)} collective-permute-done((f32[65,256]{1,0:T(8,128)S(1)}, f32[65,256]{1,0:T(8,128)S(1)}, u32[]{:S(2)}, u32[]{:S(2)}) %collective-permute-start) | collective-permute-done | bytes 66592 | tf_op jit(solution)/shard_map/ppermute | solution.py:19
  10.2 1.6 %collective-permute-start.4 = (f32[65,256]{1,0:T(8,128)S(1)}, f32[65,256]{1,0:T(8,128)S(1)}, u32[]{:S(2)}, u32[]{:S(2)}) collective-permute-start(f32[65,256]{1,0:T(8,128)S(1)} %get-tuple-element.44), channel_id=1, source_target_pairs={{0,2},{1,3},{2,0},{3,1},{4,6},{5,7},{6,4},{7,5},{8,10},{9,11},{10,... | collective-permute-start | bytes 199688 | tf_op jit(solution)/shard_map/ppermute | solution.py:19
  11.8 2.8 %collective-permute-done.4 = f32[65,256]{1,0:T(8,128)S(1)} collective-permute-done((f32[65,256]{1,0:T(8,128)S(1)}, f32[65,256]{1,0:T(8,128)S(1)}, u32[]{:S(2)}, u32[]{:S(2)}) %collective-permute-start.4) | collective-permute-done | bytes 66592 | tf_op jit(solution)/shard_map/ppermute | solution.py:19
  14.6 1.7 %collective-permute-start.5 = (f32[65,512]{1,0:T(8,128)S(1)}, f32[65,512]{1,0:T(8,128)S(1)}, u32[]{:S(2)}, u32[]{:S(2)}) collective-permute-start(f32[65,512]{1,0:T(8,128)S(1)} %collective-permute-done.1.part_ref), channel_id=1, source_target_pairs={{0,2},{1,3},{2,0},{3,1},{4,6},{5,7},{6,4},{7,5},{8,10},{9,11},{10,... | collective-permute-start | bytes 399368 | tf_op jit(solution)/shard_map/ppermute | solution.py:19
  16.7 1.6 %shard_map.62 = (bf16[2048,1024]{1,0:T(8,128)(2,1)S(1)}, f32[32,1024]{1,0:T(8,128)S(1)}) custom-call(f32[32,1024]{1,0:T(8,128)S(1)} %get-tuple-element.119.rows_ref, f32[32,1]{1,0:T(8,128)S(1)} %copy.6.scale_ref, bf16[256,1024]{1,0:T(8,128)(2,1)S(1)} %pad_maximum_fusion.right_ref, f32[32,1024]{1,0:T(8,128)S(1)} %get-tuple-element.120.refs_0_, ...), custom_call_target="tpu_custom_call" | custom-call | flops 872415232 | bytes 4194304 | tf_op jit(solution)/shard_map/pallas_call | solution.py:115
  18.9 1.6 %shard_map.63 = (bf16[2048,1024]{1,0:T(8,128)(2,1)S(1)}, f32[32,1024]{1,0:T(8,128)S(1)}) custom-call(f32[32,1024]{1,0:T(8,128)S(1)} %get-tuple-element.124.rows_ref, f32[32,1]{1,0:T(8,128)S(1)} %copy.6.scale_ref, bf16[256,1024]{1,0:T(8,128)(2,1)S(1)} %pad_maximum_fusion.right_ref, f32[32,1024]{1,0:T(8,128)S(1)} %get-tuple-element.123.refs_0_, ...), custom_call_target="tpu_custom_call" | custom-call | flops 872415232 | bytes 4194304 | tf_op jit(solution)/shard_map/pallas_call | solution.py:115
  20.7 1.6 %shard_map.64 = (bf16[2048,1024]{1,0:T(8,128)(2,1)S(1)}, f32[32,1024]{1,0:T(8,128)S(1)}) custom-call(f32[32,1024]{1,0:T(8,128)S(1)} %get-tuple-element.67.rows_ref.part_ref, f32[32,1]{1,0:T(8,128)S(1)} %copy.6.scale_ref, bf16[256,1024]{1,0:T(8,128)(2,1)S(1)} %pad_maximum_fusion.right_ref, f32[32,1024]{1,0:T(8,128)S(1)} %get-tuple-element.116.refs_0_, ...), custom_call_target="tpu_custom_call" | custom-call | flops 872415232 | bytes 4194304 | tf_op jit(solution)/shard_map/pallas_call | solution.py:115
  22.3 1.6 %shard_map.65 = (bf16[2048,1024]{1,0:T(8,128)(2,1)S(1)}, f32[32,1024]{1,0:T(8,128)S(1)}) custom-call(f32[32,1024]{1,0:T(8,128)S(1)} %get-tuple-element.75.rows_ref, f32[32,1]{1,0:T(8,128)S(1)} %copy.6.scale_ref, bf16[256,1024]{1,0:T(8,128)(2,1)S(1)} %pad_maximum_fusion.right_ref, f32[32,1024]{1,0:T(8,128)S(1)} %get-tuple-element.121.refs_0_, ...), custom_call_target="tpu_custom_call" | custom-call | flops 872415232 | bytes 4194304 | tf_op jit(solution)/shard_map/pallas_call | solution.py:115
  24.0 1.0 %collective-permute-start.9 = (f32[32,1024]{1,0:T(8,128)S(1)}, f32[32,1024]{1,0:T(8,128)S(1)}, u32[]{:S(2)}, u32[]{:S(2)}) collective-permute-start(f32[32,1024]{1,0:T(8,128)S(1)} %get-tuple-element.62), channel_id=1, source_target_pairs={{0,2},{1,3},{2,0},{3,1},{4,6},{5,7},{6,4},{7,5},{8,10},{9,11},{10,... | collective-permute-start | bytes 393224 | tf_op jit(solution)/shard_map/ppermute | solution.py:19
  25.4 0.8 %fusion.22 = f32[96,1024]{1,0:T(8,128)S(1)} fusion(bf16[2048,1024]{1,0:T(8,128)(2,1)S(1)} %get-tuple-element.64, bf16[96,1024]{1,0:T(8,128)(2,1)S(1)} %broadcast_select_fusion.2, bf16[96,1024]{1,0:T(8,128)(2,1)S(1)} %pad_maximum_fusion.6), kind=kOutput, calls=%fused_computation.47 | convolution fusion | flops 403439616 | bytes 4980736 | tf_op jit(solution)/shard_map/dot_general | solution.py:155
  26.5 0.8 %convolution_add_fusion.5 = f32[96,1024]{1,0:T(8,128)S(1)} fusion(f32[96,1024]{1,0:T(8,128)S(1)} %fusion.22, bf16[2048,1024]{1,0:T(8,128)(2,1)S(1)} %get-tuple-element.65, bf16[96,1024]{1,0:T(8,128)(2,1)S(1)} %fusion.116, bf16[32,1024]{1,0:T(8,128)(2,1)S(1)} %get-tuple-element.153, bf16[32,1024]{1,0:T(8,128)(2,1)S(1)} %get-tuple-element.154, ...), kind=kOutput, calls=%fused_computation.5 | convolution fusion | flops 404324352 | bytes 5373952 | tf_op jit(solution)/shard_map/dot_general | solution.py:155
  27.5 1.1 %shard_map.67 = bf16[2048,1024]{1,0:T(8,128)(2,1)S(1)} custom-call(f32[32,1024]{1,0:T(8,128)S(1)} %get-tuple-element.67.rows_ref.part_ref, f32[32,1]{1,0:T(8,128)S(1)} %copy.6.scale_ref, bf16[256,1024]{1,0:T(8,128)(2,1)S(1)} %shard_map.66.right_ref), custom_call_target="tpu_custom_call" | custom-call | flops 872415232 | bytes 4194304 | tf_op jit(solution)/shard_map/pallas_call | solution.py:115
  28.5 1.4 %collective-permute-done.9 = f32[32,1024]{1,0:T(8,128)S(1)} collective-permute-done((f32[32,1024]{1,0:T(8,128)S(1)}, f32[32,1024]{1,0:T(8,128)S(1)}, u32[]{:S(2)}, u32[]{:S(2)}) %collective-permute-start.9) | collective-permute-done | bytes 131104 | tf_op jit(solution)/shard_map/ppermute | solution.py:19
  30.0 0.8 %fusion.33 = f32[96,1024]{1,0:T(8,128)S(1)} fusion(bf16[2048,1024]{1,0:T(8,128)(2,1)S(1)} %get-tuple-element.71, bf16[96,1024]{1,0:T(8,128)(2,1)S(1)} %fusion.117, bf16[32,1024]{1,0:T(8,128)(2,1)S(1)} %get-tuple-element.150, bf16[32,1024]{1,0:T(8,128)(2,1)S(1)} %get-tuple-element.151, bf16[32,1024]{1,0:T(8,128)(2,1)S(1)} %get-tuple-element.152), kind=kOutput, calls=%fused_computation.58 | convolution fusion | flops 404226048 | bytes 4980736 | tf_op jit(solution)/shard_map/dot_general | solution.py:155
  31.8 0.8 %fusion.41 = f32[96,1024]{1,0:T(8,128)S(1)} fusion(bf16[2048,1024]{1,0:T(8,128)(2,1)S(1)} %get-tuple-element.72, bf16[96,1024]{1,0:T(8,128)(2,1)S(1)} %fusion.118, bf16[32,1024]{1,0:T(8,128)(2,1)S(1)} %get-tuple-element.147, bf16[32,1024]{1,0:T(8,128)(2,1)S(1)} %get-tuple-element.148, bf16[32,1024]{1,0:T(8,128)(2,1)S(1)} %get-tuple-element.149), kind=kOutput, calls=%fused_computation.66 | convolution fusion | flops 404226048 | bytes 4980736 | tf_op jit(solution)/shard_map/dot_general | solution.py:155
  32.9 1.1 %collective-permute-start.12 = (f32[32,1024]{1,0:T(8,128)S(1)}, f32[32,1024]{1,0:T(8,128)S(1)}, u32[]{:S(2)}, u32[]{:S(2)}) collective-permute-start(f32[32,1024]{1,0:T(8,128)S(1)} %get-tuple-element.73), channel_id=1, source_target_pairs={{0,2},{1,3},{2,0},{3,1},{4,6},{5,7},{6,4},{7,5},{8,10},{9,11},{10,... | collective-permute-start | bytes 393224 | tf_op jit(solution)/shard_map/ppermute | solution.py:19
  34.1 0.8 %fusion.49 = f32[96,1024]{1,0:T(8,128)S(1)} fusion(bf16[2048,1024]{1,0:T(8,128)(2,1)S(1)} %get-tuple-element.64, bf16[96,1024]{1,0:T(8,128)(2,1)S(1)} %broadcast_select_fusion.1, bf16[96,1024]{1,0:T(8,128)(2,1)S(1)} %pad_maximum_fusion.7), kind=kOutput, calls=%fused_computation.74 | convolution fusion | flops 403439616 | bytes 4980736 | tf_op jit(solution)/shard_map/dot_general | solution.py:155
  35.4 1.0 %convolution_add_fusion.4 = f32[96,1024]{1,0:T(8,128)S(1)} fusion(f32[96,1024]{1,0:T(8,128)S(1)} %fusion.49, bf16[2048,1024]{1,0:T(8,128)(2,1)S(1)} %get-tuple-element.65, bf16[96,1024]{1,0:T(8,128)(2,1)S(1)} %fusion.119, bf16[32,1024]{1,0:T(8,128)(2,1)S(1)} %get-tuple-element.142, bf16[32,1024]{1,0:T(8,128)(2,1)S(1)} %get-tuple-element.143, ...), kind=kOutput, calls=%fused_computation.4 | convolution fusion | flops 404324352 | bytes 5373952 | tf_op jit(solution)/shard_map/dot_general | solution.py:155
  36.4 1.1 %shard_map.68 = bf16[2048,1024]{1,0:T(8,128)(2,1)S(1)} custom-call(f32[32,1024]{1,0:T(8,128)S(1)} %get-tuple-element.75.rows_ref, f32[32,1]{1,0:T(8,128)S(1)} %copy.6.scale_ref, bf16[256,1024]{1,0:T(8,128)(2,1)S(1)} %shard_map.66.right_ref), custom_call_target="tpu_custom_call" | custom-call | flops 872415232 | bytes 4194304 | tf_op jit(solution)/shard_map/pallas_call | solution.py:115
  37.5 1.0 %collective-permute-done.12 = f32[32,1024]{1,0:T(8,128)S(1)} collective-permute-done((f32[32,1024]{1,0:T(8,128)S(1)}, f32[32,1024]{1,0:T(8,128)S(1)}, u32[]{:S(2)}, u32[]{:S(2)}) %collective-permute-start.12) | collective-permute-done | bytes 131104 | tf_op jit(solution)/shard_map/ppermute | solution.py:19
  38.5 0.8 %fusion.60 = f32[96,1024]{1,0:T(8,128)S(1)} fusion(bf16[2048,1024]{1,0:T(8,128)(2,1)S(1)} %get-tuple-element.71, bf16[96,1024]{1,0:T(8,128)(2,1)S(1)} %fusion.120, bf16[32,1024]{1,0:T(8,128)(2,1)S(1)} %get-tuple-element.139, bf16[32,1024]{1,0:T(8,128)(2,1)S(1)} %get-tuple-element.140, bf16[32,1024]{1,0:T(8,128)(2,1)S(1)} %get-tuple-element.141), kind=kOutput, calls=%fused_computation.85 | convolution fusion | flops 404226048 | bytes 4980736 | tf_op jit(solution)/shard_map/dot_general | solution.py:155
  40.4 0.8 %fusion.68 = f32[96,1024]{1,0:T(8,128)S(1)} fusion(bf16[2048,1024]{1,0:T(8,128)(2,1)S(1)} %get-tuple-element.72, bf16[96,1024]{1,0:T(8,128)(2,1)S(1)} %fusion.121, bf16[32,1024]{1,0:T(8,128)(2,1)S(1)} %get-tuple-element.136, bf16[32,1024]{1,0:T(8,128)(2,1)S(1)} %get-tuple-element.137, bf16[32,1024]{1,0:T(8,128)(2,1)S(1)} %get-tuple-element.138), kind=kOutput, calls=%fused_computation.93 | convolution fusion | flops 404226048 | bytes 4980736 | tf_op jit(solution)/shard_map/dot_general | solution.py:155
  41.5 1.1 %collective-permute-start.15 = (f32[32,1024]{1,0:T(8,128)S(1)}, f32[32,1024]{1,0:T(8,128)S(1)}, u32[]{:S(2)}, u32[]{:S(2)}) collective-permute-start(f32[32,1024]{1,0:T(8,128)S(1)} %get-tuple-element.80), channel_id=1, source_target_pairs={{0,2},{1,3},{2,0},{3,1},{4,6},{5,7},{6,4},{7,5},{8,10},{9,11},{10,... | collective-permute-start | bytes 393224 | tf_op jit(solution)/shard_map/ppermute | solution.py:19
  42.7 0.8 %fusion.76 = f32[96,1024]{1,0:T(8,128)S(1)} fusion(bf16[2048,1024]{1,0:T(8,128)(2,1)S(1)} %get-tuple-element.64, bf16[96,1024]{1,0:T(8,128)(2,1)S(1)} %broadcast_select_fusion, bf16[96,1024]{1,0:T(8,128)(2,1)S(1)} %pad_maximum_fusion.8), kind=kOutput, calls=%fused_computation.101 | convolution fusion | flops 403439616 | bytes 4980736 | tf_op jit(solution)/shard_map/dot_general | solution.py:155
  44.0 0.8 %convolution_add_fusion.3 = f32[96,1024]{1,0:T(8,128)S(1)} fusion(f32[96,1024]{1,0:T(8,128)S(1)} %fusion.76, bf16[2048,1024]{1,0:T(8,128)(2,1)S(1)} %get-tuple-element.65, bf16[96,1024]{1,0:T(8,128)(2,1)S(1)} %fusion.122, bf16[32,1024]{1,0:T(8,128)(2,1)S(1)} %get-tuple-element.131, bf16[32,1024]{1,0:T(8,128)(2,1)S(1)} %get-tuple-element.132, ...), kind=kOutput, calls=%fused_computation.3 | convolution fusion | flops 404324352 | bytes 5373952 | tf_op jit(solution)/shard_map/dot_general | solution.py:155
  44.9 2.2 %collective-permute-done.15 = f32[32,1024]{1,0:T(8,128)S(1)} collective-permute-done((f32[32,1024]{1,0:T(8,128)S(1)}, f32[32,1024]{1,0:T(8,128)S(1)}, u32[]{:S(2)}, u32[]{:S(2)}) %collective-permute-start.15) | collective-permute-done | bytes 131104 | tf_op jit(solution)/shard_map/ppermute | solution.py:19
  47.2 0.8 %convolution_add_fusion.2 = f32[96,1024]{1,0:T(8,128)S(1)} fusion(f32[96,1024]{1,0:T(8,128)S(1)} %convolution_add_fusion.3, bf16[2048,1024]{1,0:T(8,128)(2,1)S(1)} %get-tuple-element.71, bf16[96,1024]{1,0:T(8,128)(2,1)S(1)} %fusion.123, bf16[32,1024]{1,0:T(8,128)(2,1)S(1)} %get-tuple-element.128, bf16[32,1024]{1,0:T(8,128)(2,1)S(1)} %get-tuple-element.129, ...), kind=kOutput, calls=%fused_computation.2 | convolution fusion | flops 404324352 | bytes 5373952 | tf_op jit(solution)/shard_map/dot_general | solution.py:155
  49.4 0.8 %fusion.211 = (f32[96,1024]{1,0:T(8,128)S(1)}, f32[96,1024]{1,0:T(8,128)S(1)}) fusion(f32[96,1024]{1,0:T(8,128)S(1)} %convolution_add_fusion.3, f32[96,1024]{1,0:T(8,128)S(1)} %convolution_add_fusion.2, bf16[2048,1024]{1,0:T(8,128)(2,1)S(1)} %get-tuple-element.72, bf16[96,1024]{1,0:T(8,128)(2,1)S(1)} %fusion.124, ...), kind=kOutput, calls=%fused_computation.322 | convolution fusion | flops 404422656 | bytes 6160384 | tf_op jit(solution)/shard_map/dot_general | solution.py:155
  51.1 0.8 %convolution_add_fusion = f32[96,1024]{1,0:T(8,128)S(1)} fusion(f32[96,1024]{1,0:T(8,128)S(1)} %fusion.108, bf16[2048,1024]{1,0:T(8,128)(2,1)S(1)} %shard_map.67, bf16[96,1024]{1,0:T(8,128)(2,1)S(1)} %get-tuple-element.162, bf16[32,1024]{1,0:T(8,128)(2,1)S(1)} %get-tuple-element.110, bf16[32,1024]{1,0:T(8,128)(2,1)S(1)} %get-tuple-element.111, ...), kind=kOutput, calls=%fused_computation | convolution fusion | flops 404324352 | bytes 5373952 | tf_op jit(solution)/shard_map/dot_general | solution.py:155
  52.5 1.0 %collective-permute-done.17 = f32[32]{0:T(128)S(1)} collective-permute-done((f32[32]{0:T(128)S(1)}, f32[32]{0:T(128)S(1)}, u32[]{:S(2)}, u32[]{:S(2)}) %collective-permute-start.17) | collective-permute-done | bytes 160 | tf_op jit(solution)/shard_map/ppermute | solution.py:19
  (103 shorter events, 11.8 us)
Async XLA Ops:
  1.4 7.9 %collective-permute-start = (f32[65,256]{1,0:T(8,128)S(1)}, f32[65,256]{1,0:T(8,128)S(1)}, u32[]{:S(2)}, u32[]{:S(2)}) collective-permute-start(f32[65,256]{1,0:T(8,128)S(1)} %pad_maximum_fusion.11.part_ref), channel_id=1, source_target_pairs={{0,8},{1,9},{2,10},{3,11},{4,12},{5,13},{6,14},{7,15},{8,0},{9,1},... | collective-permute-start | bytes 199688 | tf_op jit(solution)/shard_map/ppermute | solution.py:19
  6.3 5.5 %collective-permute-start.3 = (f32[65,256]{1,0:T(8,128)S(1)}, f32[65,256]{1,0:T(8,128)S(1)}, u32[]{:S(2)}, u32[]{:S(2)}) collective-permute-start(f32[65,256]{1,0:T(8,128)S(1)} %get-tuple-element.43), channel_id=1, source_target_pairs={{0,2},{1,3},{2,0},{3,1},{4,6},{5,7},{6,4},{7,5},{8,10},{9,11},{10,... | collective-permute-start | bytes 199688 | tf_op jit(solution)/shard_map/ppermute | solution.py:19
  9.4 5.2 %collective-permute-start.1 = (f32[65,512]{1,0:T(8,128)S(1)}, f32[65,512]{1,0:T(8,128)S(1)}, u32[]{:S(2)}, u32[]{:S(2)}) collective-permute-start(f32[65,512]{1,0:T(8,128)S(1)} %pad_maximum_fusion.9), channel_id=1, source_target_pairs={{0,4},{1,5},{2,6},{3,7},{4,0},{5,1},{6,2},{7,3},{8,12},{9,13},{10,... | collective-permute-start | bytes 399368 | tf_op jit(solution)/shard_map/ppermute | solution.py:19
  10.2 4.4 %collective-permute-start.4 = (f32[65,256]{1,0:T(8,128)S(1)}, f32[65,256]{1,0:T(8,128)S(1)}, u32[]{:S(2)}, u32[]{:S(2)}) collective-permute-start(f32[65,256]{1,0:T(8,128)S(1)} %get-tuple-element.44), channel_id=1, source_target_pairs={{0,2},{1,3},{2,0},{3,1},{4,6},{5,7},{6,4},{7,5},{8,10},{9,11},{10,... | collective-permute-start | bytes 199688 | tf_op jit(solution)/shard_map/ppermute | solution.py:19
  14.6 5.8 %collective-permute-start.5 = (f32[65,512]{1,0:T(8,128)S(1)}, f32[65,512]{1,0:T(8,128)S(1)}, u32[]{:S(2)}, u32[]{:S(2)}) collective-permute-start(f32[65,512]{1,0:T(8,128)S(1)} %collective-permute-done.1.part_ref), channel_id=1, source_target_pairs={{0,2},{1,3},{2,0},{3,1},{4,6},{5,7},{6,4},{7,5},{8,10},{9,11},{10,... | collective-permute-start | bytes 399368 | tf_op jit(solution)/shard_map/ppermute | solution.py:19
  16.4 2.4 %collective-permute-start.2 = (f32[64,1024]{1,0:T(8,128)S(1)}, f32[64,1024]{1,0:T(8,128)S(1)}, u32[]{:S(2)}, u32[]{:S(2)}) collective-permute-start(f32[64,1024]{1,0:T(8,128)S(1)} %slice.215), channel_id=1, source_target_pairs={{0,1},{1,0},{2,3},{3,2},{4,5},{5,4},{6,7},{7,6},{8,9},{9,8},{10,11... | collective-permute-start | bytes 786440 | tf_op jit(solution)/shard_map/ppermute | solution.py:19
  18.3 4.0 %collective-permute-start.6 = (f32[64,512]{1,0:T(8,128)S(1)}, f32[64,512]{1,0:T(8,128)S(1)}, u32[]{:S(2)}, u32[]{:S(2)}) collective-permute-start(f32[64,512]{1,0:T(8,128)S(1)} %pad_maximum_fusion.10), channel_id=1, source_target_pairs={{0,1},{1,0},{2,3},{3,2},{4,5},{5,4},{6,7},{7,6},{8,9},{9,8},{10,11... | collective-permute-start | bytes 393224 | tf_op jit(solution)/shard_map/ppermute | solution.py:19
  20.5 1.7 %collective-permute-start.7 = (f32[64,512]{1,0:T(8,128)S(1)}, f32[64,512]{1,0:T(8,128)S(1)}, u32[]{:S(2)}, u32[]{:S(2)}) collective-permute-start(f32[64,512]{1,0:T(8,128)S(1)} %slice.179), channel_id=1, source_target_pairs={{0,1},{1,0},{2,3},{3,2},{4,5},{5,4},{6,7},{7,6},{8,9},{9,8},{10,11... | collective-permute-start | bytes 393224 | tf_op jit(solution)/shard_map/ppermute | solution.py:19
  20.7 4.6 %copy-start = (pred[96]{0:T(512)(128)(4,1)S(1)}, pred[96]{0:T(512)(128)(4,1)}, u32[]{:S(2)}) copy-start(pred[96]{0:T(512)(128)(4,1)} %constant.9.clone.1) | copy-start | bytes 292
  24.0 6.0 %collective-permute-start.9 = (f32[32,1024]{1,0:T(8,128)S(1)}, f32[32,1024]{1,0:T(8,128)S(1)}, u32[]{:S(2)}, u32[]{:S(2)}) collective-permute-start(f32[32,1024]{1,0:T(8,128)S(1)} %get-tuple-element.62), channel_id=1, source_target_pairs={{0,2},{1,3},{2,0},{3,1},{4,6},{5,7},{6,4},{7,5},{8,10},{9,11},{10,... | collective-permute-start | bytes 393224 | tf_op jit(solution)/shard_map/ppermute | solution.py:19
  25.0 1.4 %collective-permute-start.8 = (f32[32,1024]{1,0:T(8,128)S(1)}, f32[32,1024]{1,0:T(8,128)S(1)}, u32[]{:S(2)}, u32[]{:S(2)}) collective-permute-start(f32[32,1024]{1,0:T(8,128)S(1)} %get-tuple-element.62), channel_id=1, source_target_pairs={{0,1},{1,0},{2,3},{3,2},{4,5},{5,4},{6,7},{7,6},{8,9},{9,8},{10,11... | collective-permute-start | bytes 393224 | tf_op jit(solution)/shard_map/ppermute | solution.py:19
  29.9 1.3 %collective-permute-start.10 = (f32[32,1024]{1,0:T(8,128)S(1)}, f32[32,1024]{1,0:T(8,128)S(1)}, u32[]{:S(2)}, u32[]{:S(2)}) collective-permute-start(f32[32,1024]{1,0:T(8,128)S(1)} %collective-permute-done.9), channel_id=1, source_target_pairs={{0,1},{1,0},{2,3},{3,2},{4,5},{5,4},{6,7},{7,6},{8,9},{9,8},{10,11... | collective-permute-start | bytes 393224 | tf_op jit(solution)/shard_map/ppermute | solution.py:19
  32.9 5.6 %collective-permute-start.12 = (f32[32,1024]{1,0:T(8,128)S(1)}, f32[32,1024]{1,0:T(8,128)S(1)}, u32[]{:S(2)}, u32[]{:S(2)}) collective-permute-start(f32[32,1024]{1,0:T(8,128)S(1)} %get-tuple-element.73), channel_id=1, source_target_pairs={{0,2},{1,3},{2,0},{3,1},{4,6},{5,7},{6,4},{7,5},{8,10},{9,11},{10,... | collective-permute-start | bytes 393224 | tf_op jit(solution)/shard_map/ppermute | solution.py:19
  33.9 1.4 %collective-permute-start.11 = (f32[32,1024]{1,0:T(8,128)S(1)}, f32[32,1024]{1,0:T(8,128)S(1)}, u32[]{:S(2)}, u32[]{:S(2)}) collective-permute-start(f32[32,1024]{1,0:T(8,128)S(1)} %get-tuple-element.73), channel_id=1, source_target_pairs={{0,1},{1,0},{2,3},{3,2},{4,5},{5,4},{6,7},{7,6},{8,9},{9,8},{10,11... | collective-permute-start | bytes 393224 | tf_op jit(solution)/shard_map/ppermute | solution.py:19
  38.5 1.3 %collective-permute-start.13 = (f32[32,1024]{1,0:T(8,128)S(1)}, f32[32,1024]{1,0:T(8,128)S(1)}, u32[]{:S(2)}, u32[]{:S(2)}) collective-permute-start(f32[32,1024]{1,0:T(8,128)S(1)} %collective-permute-done.12), channel_id=1, source_target_pairs={{0,1},{1,0},{2,3},{3,2},{4,5},{5,4},{6,7},{7,6},{8,9},{9,8},{10,11... | collective-permute-start | bytes 393224 | tf_op jit(solution)/shard_map/ppermute | solution.py:19
  41.5 5.6 %collective-permute-start.15 = (f32[32,1024]{1,0:T(8,128)S(1)}, f32[32,1024]{1,0:T(8,128)S(1)}, u32[]{:S(2)}, u32[]{:S(2)}) collective-permute-start(f32[32,1024]{1,0:T(8,128)S(1)} %get-tuple-element.80), channel_id=1, source_target_pairs={{0,2},{1,3},{2,0},{3,1},{4,6},{5,7},{6,4},{7,5},{8,10},{9,11},{10,... | collective-permute-start | bytes 393224 | tf_op jit(solution)/shard_map/ppermute | solution.py:19
  42.6 1.4 %collective-permute-start.14 = (f32[32,1024]{1,0:T(8,128)S(1)}, f32[32,1024]{1,0:T(8,128)S(1)}, u32[]{:S(2)}, u32[]{:S(2)}) collective-permute-start(f32[32,1024]{1,0:T(8,128)S(1)} %get-tuple-element.80), channel_id=1, source_target_pairs={{0,1},{1,0},{2,3},{3,2},{4,5},{5,4},{6,7},{7,6},{8,9},{9,8},{10,11... | collective-permute-start | bytes 393224 | tf_op jit(solution)/shard_map/ppermute | solution.py:19
  47.1 1.4 %collective-permute-start.16 = (f32[32,1024]{1,0:T(8,128)S(1)}, f32[32,1024]{1,0:T(8,128)S(1)}, u32[]{:S(2)}, u32[]{:S(2)}) collective-permute-start(f32[32,1024]{1,0:T(8,128)S(1)} %collective-permute-done.15), channel_id=1, source_target_pairs={{0,1},{1,0},{2,3},{3,2},{4,5},{5,4},{6,7},{7,6},{8,9},{9,8},{10,11... | collective-permute-start | bytes 393224 | tf_op jit(solution)/shard_map/ppermute | solution.py:19
  52.2 1.2 %collective-permute-start.17 = (f32[32]{0:T(128)S(1)}, f32[32]{0:T(128)S(1)}, u32[]{:S(2)}, u32[]{:S(2)}) collective-permute-start(f32[32]{0:T(128)S(1)} %get-tuple-element.86), channel_id=1, source_target_pairs={{0,1},{1,0},{2,3},{3,2},{4,5},{5,4},{6,7},{7,6},{8,9},{9,8},{10,11... | collective-permute-start | bytes 392 | tf_op jit(solution)/shard_map/ppermute | solution.py:19

commit v19 on v18

--- a/solution.py
+++ b/solution.py
@@ -150,9 +150,7 @@
 
 
 def apply_parts(parts, piece):
-    probes = parts.shape[0] // 3
-    right = jnp.concatenate([parts[: 2 * probes], jnp.zeros_like(parts[2 * probes :])], axis=0)
-    return jnp.dot(jnp.concatenate([parts, right], axis=1), piece, preferred_element_type=jnp.float32)
+    return jnp.dot(jnp.concatenate([parts, parts], axis=1), piece, preferred_element_type=jnp.float32)
 
 
 def apply_piece(vectors, piece):
@@ -238,36 +236,44 @@
 
         far_tile, right_far = [], None
 
-        def exchange(x):
+        def exchange(x, direction):
             nonlocal right_far
             parts, passed = fence((parts_of(x), x))
             pieces, sent = [x, swap(passed, n, 1)], [x]
-            total = fence(apply_parts(parts, tile[0]))
-            total = near = fence(total + apply_piece(pieces[1], tile[1]))
+            near = fence(apply_parts(parts, tile[0]))
+            near = fence(near + apply_piece(pieces[1], tile[1]))
+            far = jnp.zeros_like(near) if len(inner) == 1 else None
             for k, stride in enumerate(inner[:-1]):
                 arrived = swap(join(*sent), n, stride)
                 if len(far_tile) < len(far_rows):
-                    rows, columns, total = fence((far_rows[len(far_tile)], far_rows[0], total))
+                    rows, columns, near = fence((far_rows[len(far_tile)], far_rows[0], near))
                     if right_far is None:
                         (right_far,) = prepare(columns, scale)
                     (piece,) = build_piece(rows, scale, right_far)
-                    arrived, piece, right_far, total = fence((arrived, piece, right_far, total))
+                    piece, right_far, near = fence((piece, right_far, near))
                     far_tile.append(piece)
+                arrived, near = fence((arrived, near))
                 sent.append(arrived)
-                pieces += [arrived, swap(arrived, n, 1)]
-                for at in (2 + 2 * k, 3 + 2 * k):
-                    total = total + apply_piece(pieces[at], tile[at])
-                    total = fence(total) if at < len(tile) - 1 else total
-            return collect(total - near), collect(total) + noise * x, pieces
+                pieces.append(arrived)
+                term = apply_piece(arrived, tile[2 + 2 * k])
+                far = fence(term if far is None else far + term)
+                pieces.append(swap(arrived, n, 1))
+                if k < len(inner) - 2:
+                    far = fence(far + apply_piece(pieces[-1], tile[3 + 2 * k]))
+            before = join(*pieces[:-1])
+            curve = jnp.sum(direction[:, : before.shape[1]] * before, axis=1)
+            curve, far = fence((curve, far))
+            curve = curve + jnp.sum(direction[:, before.shape[1] :] * pieces[-1], axis=1)
+            if len(inner) > 1:
+                far = far + apply_piece(pieces[-1], tile[-1])
+            return collect(far), collect(near) + collect(far) + noise * x, join(*pieces), curve
 
         residual = direction = join(*starts)
         my_solution = jnp.zeros_like(direction[:, :width])
         norm_now = jnp.sum(residual * residual, axis=1)
         my_image, far_image = my_applied, my_far
         for iteration in range(ITERS - 1):
-            far_next, my_next, pieces = exchange(my_applied)
-            applied = join(*pieces)
-            curve = jnp.sum(direction * applied, axis=1)
+            far_next, my_next, applied, curve = exchange(my_applied, direction)
             step_size = (norm_now / curve)[:, None]
             my_solution = my_solution + step_size * direction[:, :width]
             residual = residual - step_size * applied

time: 54.3 us -> 53.5 us (0.985)
  transfers between devices with their start and end apart: 18 -> 18, of which waited for: 12 -> 12; matrix products, arithmetic and copies ran while one was open for 17% -> 18% of each run, Pallas kernels for 13% -> 14%
where the time goes in v19:
time: 53.5 us; the launch traced here: 53.3 us
  starting transfers between devices  14.2 us (27%)
  waiting for transfers between devices  12 us (22%)
  matrix products  11.5 us (21%)
  Pallas kernels  8.8 us (16%)
  other arithmetic  5.48 us (10%)
  between operations  1.01 us (2%)
    ppermute x18, starting transfers between devices, swap(): return lax.ppermute(x, 'blk', [(i, i ^ stride) for i in range(n)])  14.2 us
    ppermute x18, waiting for transfers between devices, swap(): return lax.ppermute(x, 'blk', [(i, i ^ stride) for i in range(n)])  12 us
    dot_general x14, matrix products, apply_parts(): jnp.dot(jnp.concatenate([parts, parts], axis=1), piece, preferred_element...  11.5 us
    pallas_call x10, Pallas kernels, call(): pl.pallas_call(kernel, out_shape=outs, in_specs=[whole] * len(args), out_...  8.8 us
  transfers between devices with their start and end apart: 18, of which 12 were waited for; matrix products, arithmetic and copies ran while one was open for 18% of the time, Pallas kernels for 14%

profile of v19, /device:TPU:0, one launch (start us, length us, event | category | flops | bytes accessed | tf_op | source)
XLA Modules:
  0.0 53.3 jit_solution(7203213664647010053)
XLA Ops:
  0.6 0.8 %pad_maximum_fusion.8.part_ref = f32[65,256]{1,0:T(8,128)S(1)} fusion(f32[1,256]{1,0:T(1,128)} %bitcast.24, f32[32,256]{1,0:T(8,128)} %param.7, f32[32,256]{1,0:T(8,128)} %param.4), kind=kLoop, calls=%fused_computation.278 | loop fusion | flops 33280 | bytes 133120 | tf_op jit(solution)/shard_map/concatenate | solution.py:186
  1.4 4.0 %collective-permute-start = (f32[65,256]{1,0:T(8,128)S(1)}, f32[65,256]{1,0:T(8,128)S(1)}, u32[]{:S(2)}, u32[]{:S(2)}) collective-permute-start(f32[65,256]{1,0:T(8,128)S(1)} %pad_maximum_fusion.8.part_ref), channel_id=1, source_target_pairs={{0,8},{1,9},{2,10},{3,11},{4,12},{5,13},{6,14},{7,15},{8,0},{9,1},... | collective-permute-start | bytes 199688 | tf_op jit(solution)/shard_map/ppermute | solution.py:19
  6.3 1.6 %collective-permute-start.3 = (f32[65,256]{1,0:T(8,128)S(1)}, f32[65,256]{1,0:T(8,128)S(1)}, u32[]{:S(2)}, u32[]{:S(2)}) collective-permute-start(f32[65,256]{1,0:T(8,128)S(1)} %get-tuple-element.53), channel_id=1, source_target_pairs={{0,2},{1,3},{2,0},{3,1},{4,6},{5,7},{6,4},{7,5},{8,10},{9,11},{10,... | collective-permute-start | bytes 199688 | tf_op jit(solution)/shard_map/ppermute | solution.py:19
  7.9 1.5 %collective-permute-done.part_ref = f32[65,256]{1,0:T(8,128)S(1)} collective-permute-done((f32[65,256]{1,0:T(8,128)S(1)}, f32[65,256]{1,0:T(8,128)S(1)}, u32[]{:S(2)}, u32[]{:S(2)}) %collective-permute-start) | collective-permute-done | bytes 66592 | tf_op jit(solution)/shard_map/ppermute | solution.py:19
  10.2 1.6 %collective-permute-start.4 = (f32[65,256]{1,0:T(8,128)S(1)}, f32[65,256]{1,0:T(8,128)S(1)}, u32[]{:S(2)}, u32[]{:S(2)}) collective-permute-start(f32[65,256]{1,0:T(8,128)S(1)} %get-tuple-element.54), channel_id=1, source_target_pairs={{0,2},{1,3},{2,0},{3,1},{4,6},{5,7},{6,4},{7,5},{8,10},{9,11},{10,... | collective-permute-start | bytes 199688 | tf_op jit(solution)/shard_map/ppermute | solution.py:19
  11.8 2.8 %collective-permute-done.4 = f32[65,256]{1,0:T(8,128)S(1)} collective-permute-done((f32[65,256]{1,0:T(8,128)S(1)}, f32[65,256]{1,0:T(8,128)S(1)}, u32[]{:S(2)}, u32[]{:S(2)}) %collective-permute-start.4) | collective-permute-done | bytes 66592 | tf_op jit(solution)/shard_map/ppermute | solution.py:19
  14.6 1.7 %collective-permute-start.5 = (f32[65,512]{1,0:T(8,128)S(1)}, f32[65,512]{1,0:T(8,128)S(1)}, u32[]{:S(2)}, u32[]{:S(2)}) collective-permute-start(f32[65,512]{1,0:T(8,128)S(1)} %collective-permute-done.1.part_ref), channel_id=1, source_target_pairs={{0,2},{1,3},{2,0},{3,1},{4,6},{5,7},{6,4},{7,5},{8,10},{9,11},{10,... | collective-permute-start | bytes 399368 | tf_op jit(solution)/shard_map/ppermute | solution.py:19
  16.7 1.6 %shard_map.62 = (bf16[2048,1024]{1,0:T(8,128)(2,1)S(1)}, f32[32,1024]{1,0:T(8,128)S(1)}) custom-call(f32[32,1024]{1,0:T(8,128)S(1)} %get-tuple-element.129.rows_ref, f32[32,1]{1,0:T(8,128)S(1)} %copy.6.scale_ref, bf16[256,1024]{1,0:T(8,128)(2,1)S(1)} %pad_maximum_fusion.right_ref, f32[32,1024]{1,0:T(8,128)S(1)} %get-tuple-element.130.refs_0_, ...), custom_call_target="tpu_custom_call" | custom-call | flops 872415232 | bytes 4194304 | tf_op jit(solution)/shard_map/pallas_call | solution.py:115
  18.9 1.5 %shard_map.63 = (bf16[2048,1024]{1,0:T(8,128)(2,1)S(1)}, f32[32,1024]{1,0:T(8,128)S(1)}) custom-call(f32[32,1024]{1,0:T(8,128)S(1)} %get-tuple-element.134.rows_ref, f32[32,1]{1,0:T(8,128)S(1)} %copy.6.scale_ref, bf16[256,1024]{1,0:T(8,128)(2,1)S(1)} %pad_maximum_fusion.right_ref, f32[32,1024]{1,0:T(8,128)S(1)} %get-tuple-element.133.refs_0_, ...), custom_call_target="tpu_custom_call" | custom-call | flops 872415232 | bytes 4194304 | tf_op jit(solution)/shard_map/pallas_call | solution.py:115
  20.6 1.6 %shard_map.64 = (bf16[2048,1024]{1,0:T(8,128)(2,1)S(1)}, f32[32,1024]{1,0:T(8,128)S(1)}) custom-call(f32[32,1024]{1,0:T(8,128)S(1)} %get-tuple-element.77.rows_ref.part_ref, f32[32,1]{1,0:T(8,128)S(1)} %copy.6.scale_ref, bf16[256,1024]{1,0:T(8,128)(2,1)S(1)} %pad_maximum_fusion.right_ref, f32[32,1024]{1,0:T(8,128)S(1)} %get-tuple-element.126.refs_0_, ...), custom_call_target="tpu_custom_call" | custom-call | flops 872415232 | bytes 4194304 | tf_op jit(solution)/shard_map/pallas_call | solution.py:115
  22.3 1.6 %shard_map.65 = (bf16[2048,1024]{1,0:T(8,128)(2,1)S(1)}, f32[32,1024]{1,0:T(8,128)S(1)}) custom-call(f32[32,1024]{1,0:T(8,128)S(1)} %get-tuple-element.88.rows_ref, f32[32,1]{1,0:T(8,128)S(1)} %copy.6.scale_ref, bf16[256,1024]{1,0:T(8,128)(2,1)S(1)} %pad_maximum_fusion.right_ref, f32[32,1024]{1,0:T(8,128)S(1)} %get-tuple-element.131.refs_0_, ...), custom_call_target="tpu_custom_call" | custom-call | flops 872415232 | bytes 4194304 | tf_op jit(solution)/shard_map/pallas_call | solution.py:115
  23.9 1.1 %collective-permute-start.9 = (f32[32,1024]{1,0:T(8,128)S(1)}, f32[32,1024]{1,0:T(8,128)S(1)}, u32[]{:S(2)}, u32[]{:S(2)}) collective-permute-start(f32[32,1024]{1,0:T(8,128)S(1)} %get-tuple-element.72), channel_id=1, source_target_pairs={{0,2},{1,3},{2,0},{3,1},{4,6},{5,7},{6,4},{7,5},{8,10},{9,11},{10,... | collective-permute-start | bytes 393224 | tf_op jit(solution)/shard_map/ppermute | solution.py:19
  26.5 0.8 %convolution_add_fusion.6 = f32[96,1024]{1,0:T(8,128)S(1)} fusion(f32[96,1024]{1,0:T(8,128)S(1)} %fusion.6, bf16[2048,1024]{1,0:T(8,128)(2,1)S(1)} %get-tuple-element.75, bf16[32,1024]{1,0:T(8,128)(2,1)S(1)} %get-tuple-element.167, bf16[32,1024]{1,0:T(8,128)(2,1)S(1)} %get-tuple-element.168, bf16[32,1024]{1,0:T(8,128)(2,1)S(1)} %get-tuple-element.166), kind=kOutput, calls=%fused_computation.6 | convolution fusion | flops 405110784 | bytes 5177344 | tf_op jit(solution)/shard_map/dot_general | solution.py:153
  27.4 1.1 %shard_map.67 = bf16[2048,1024]{1,0:T(8,128)(2,1)S(1)} custom-call(f32[32,1024]{1,0:T(8,128)S(1)} %get-tuple-element.77.rows_ref.part_ref, f32[32,1]{1,0:T(8,128)S(1)} %copy.6.scale_ref, bf16[256,1024]{1,0:T(8,128)(2,1)S(1)} %shard_map.66.right_ref), custom_call_target="tpu_custom_call" | custom-call | flops 872415232 | bytes 4194304 | tf_op jit(solution)/shard_map/pallas_call | solution.py:115
  28.5 1.4 %collective-permute-done.9 = f32[32,1024]{1,0:T(8,128)S(1)} collective-permute-done((f32[32,1024]{1,0:T(8,128)S(1)}, f32[32,1024]{1,0:T(8,128)S(1)}, u32[]{:S(2)}, u32[]{:S(2)}) %collective-permute-start.9) | collective-permute-done | bytes 131104 | tf_op jit(solution)/shard_map/ppermute | solution.py:19
  29.9 0.8 %fusion.21 = f32[96,1024]{1,0:T(8,128)S(1)} fusion(bf16[2048,1024]{1,0:T(8,128)(2,1)S(1)} %get-tuple-element.81, bf16[32,1024]{1,0:T(8,128)(2,1)S(1)} %get-tuple-element.164, bf16[32,1024]{1,0:T(8,128)(2,1)S(1)} %get-tuple-element.165, bf16[32,1024]{1,0:T(8,128)(2,1)S(1)} %get-tuple-element.163), kind=kOutput, calls=%fused_computation.43 | convolution fusion | flops 405012480 | bytes 4784128 | tf_op jit(solution)/shard_map/dot_general | solution.py:153
  31.6 0.8 %convolution_add_fusion.5 = f32[96,1024]{1,0:T(8,128)S(1)} fusion(f32[96,1024]{1,0:T(8,128)S(1)} %fusion.21, bf16[2048,1024]{1,0:T(8,128)(2,1)S(1)} %get-tuple-element.85, bf16[32,1024]{1,0:T(8,128)(2,1)S(1)} %get-tuple-element.160, bf16[32,1024]{1,0:T(8,128)(2,1)S(1)} %get-tuple-element.161, bf16[32,1024]{1,0:T(8,128)(2,1)S(1)} %get-tuple-element.159), kind=kOutput, calls=%fused_computation.5 | convolution fusion | flops 405110784 | bytes 5177344 | tf_op jit(solution)/shard_map/dot_general | solution.py:153
  32.6 1.1 %collective-permute-start.12 = (f32[32,1024]{1,0:T(8,128)S(1)}, f32[32,1024]{1,0:T(8,128)S(1)}, u32[]{:S(2)}, u32[]{:S(2)}) collective-permute-start(f32[32,1024]{1,0:T(8,128)S(1)} %get-tuple-element.86), channel_id=1, source_target_pairs={{0,2},{1,3},{2,0},{3,1},{4,6},{5,7},{6,4},{7,5},{8,10},{9,11},{10,... | collective-permute-start | bytes 393224 | tf_op jit(solution)/shard_map/ppermute | solution.py:19
  35.3 1.0 %convolution_add_fusion.4 = f32[96,1024]{1,0:T(8,128)S(1)} fusion(f32[96,1024]{1,0:T(8,128)S(1)} %fusion.44, bf16[2048,1024]{1,0:T(8,128)(2,1)S(1)} %get-tuple-element.75, bf16[32,1024]{1,0:T(8,128)(2,1)S(1)} %get-tuple-element.155, bf16[32,1024]{1,0:T(8,128)(2,1)S(1)} %get-tuple-element.156, bf16[32,1024]{1,0:T(8,128)(2,1)S(1)} %get-tuple-element.154), kind=kOutput, calls=%fused_computation.4 | convolution fusion | flops 405110784 | bytes 5177344 | tf_op jit(solution)/shard_map/dot_general | solution.py:153
  36.3 1.1 %shard_map.68 = bf16[2048,1024]{1,0:T(8,128)(2,1)S(1)} custom-call(f32[32,1024]{1,0:T(8,128)S(1)} %get-tuple-element.88.rows_ref, f32[32,1]{1,0:T(8,128)S(1)} %copy.6.scale_ref, bf16[256,1024]{1,0:T(8,128)(2,1)S(1)} %shard_map.66.right_ref), custom_call_target="tpu_custom_call" | custom-call | flops 872415232 | bytes 4194304 | tf_op jit(solution)/shard_map/pallas_call | solution.py:115
  37.4 0.9 %collective-permute-done.12 = f32[32,1024]{1,0:T(8,128)S(1)} collective-permute-done((f32[32,1024]{1,0:T(8,128)S(1)}, f32[32,1024]{1,0:T(8,128)S(1)}, u32[]{:S(2)}, u32[]{:S(2)}) %collective-permute-start.12) | collective-permute-done | bytes 131104 | tf_op jit(solution)/shard_map/ppermute | solution.py:19
  38.3 0.8 %fusion.59 = f32[96,1024]{1,0:T(8,128)S(1)} fusion(bf16[2048,1024]{1,0:T(8,128)(2,1)S(1)} %get-tuple-element.81, bf16[32,1024]{1,0:T(8,128)(2,1)S(1)} %get-tuple-element.152, bf16[32,1024]{1,0:T(8,128)(2,1)S(1)} %get-tuple-element.153, bf16[32,1024]{1,0:T(8,128)(2,1)S(1)} %get-tuple-element.151), kind=kOutput, calls=%fused_computation.81 | convolution fusion | flops 405012480 | bytes 4784128 | tf_op jit(solution)/shard_map/dot_general | solution.py:153
  40.0 0.8 %convolution_add_fusion.3 = f32[96,1024]{1,0:T(8,128)S(1)} fusion(f32[96,1024]{1,0:T(8,128)S(1)} %fusion.59, bf16[2048,1024]{1,0:T(8,128)(2,1)S(1)} %get-tuple-element.85, bf16[32,1024]{1,0:T(8,128)(2,1)S(1)} %get-tuple-element.148, bf16[32,1024]{1,0:T(8,128)(2,1)S(1)} %get-tuple-element.149, bf16[32,1024]{1,0:T(8,128)(2,1)S(1)} %get-tuple-element.147), kind=kOutput, calls=%fused_computation.3 | convolution fusion | flops 405110784 | bytes 5177344 | tf_op jit(solution)/shard_map/dot_general | solution.py:153
  41.0 1.1 %collective-permute-start.15 = (f32[32,1024]{1,0:T(8,128)S(1)}, f32[32,1024]{1,0:T(8,128)S(1)}, u32[]{:S(2)}, u32[]{:S(2)}) collective-permute-start(f32[32,1024]{1,0:T(8,128)S(1)} %get-tuple-element.96), channel_id=1, source_target_pairs={{0,2},{1,3},{2,0},{3,1},{4,6},{5,7},{6,4},{7,5},{8,10},{9,11},{10,... | collective-permute-start | bytes 393224 | tf_op jit(solution)/shard_map/ppermute | solution.py:19
  42.3 0.8 %fusion.82 = f32[96,1024]{1,0:T(8,128)S(1)} fusion(bf16[2048,1024]{1,0:T(8,128)(2,1)S(1)} %get-tuple-element.74, bf16[96,1024]{1,0:T(8,128)(2,1)S(1)} %pad_maximum_fusion.5), kind=kOutput, calls=%fused_computation.104 | convolution fusion | flops 403439616 | bytes 4784128 | tf_op jit(solution)/shard_map/dot_general | solution.py:153
  43.5 0.8 %convolution_add_fusion.2 = f32[96,1024]{1,0:T(8,128)S(1)} fusion(f32[96,1024]{1,0:T(8,128)S(1)} %fusion.82, bf16[2048,1024]{1,0:T(8,128)(2,1)S(1)} %get-tuple-element.75, bf16[32,1024]{1,0:T(8,128)(2,1)S(1)} %get-tuple-element.143, bf16[32,1024]{1,0:T(8,128)(2,1)S(1)} %get-tuple-element.144, bf16[32,1024]{1,0:T(8,128)(2,1)S(1)} %get-tuple-element.142), kind=kOutput, calls=%fused_computation.2 | convolution fusion | flops 405110784 | bytes 5177344 | tf_op jit(solution)/shard_map/dot_general | solution.py:153
  44.3 2.3 %collective-permute-done.15 = f32[32,1024]{1,0:T(8,128)S(1)} collective-permute-done((f32[32,1024]{1,0:T(8,128)S(1)}, f32[32,1024]{1,0:T(8,128)S(1)}, u32[]{:S(2)}, u32[]{:S(2)}) %collective-permute-start.15) | collective-permute-done | bytes 131104 | tf_op jit(solution)/shard_map/ppermute | solution.py:19
  46.6 0.8 %fusion.97 = f32[96,1024]{1,0:T(8,128)S(1)} fusion(bf16[2048,1024]{1,0:T(8,128)(2,1)S(1)} %get-tuple-element.81, bf16[32,1024]{1,0:T(8,128)(2,1)S(1)} %get-tuple-element.140, bf16[32,1024]{1,0:T(8,128)(2,1)S(1)} %get-tuple-element.141, bf16[32,1024]{1,0:T(8,128)(2,1)S(1)} %get-tuple-element.139), kind=kOutput, calls=%fused_computation.119 | convolution fusion | flops 405012480 | bytes 4784128 | tf_op jit(solution)/shard_map/dot_general | solution.py:153
  48.6 0.8 %convolution_add_fusion.1 = f32[96,1024]{1,0:T(8,128)S(1)} fusion(f32[96,1024]{1,0:T(8,128)S(1)} %fusion.97, bf16[2048,1024]{1,0:T(8,128)(2,1)S(1)} %get-tuple-element.85, bf16[32,1024]{1,0:T(8,128)(2,1)S(1)} %get-tuple-element.136, bf16[32,1024]{1,0:T(8,128)(2,1)S(1)} %get-tuple-element.137, bf16[32,1024]{1,0:T(8,128)(2,1)S(1)} %get-tuple-element.135), kind=kOutput, calls=%fused_computation.1 | convolution fusion | flops 405110784 | bytes 5177344 | tf_op jit(solution)/shard_map/dot_general | solution.py:153
  49.4 0.8 %fusion.120 = f32[96,1024]{1,0:T(8,128)S(1)} fusion(bf16[2048,1024]{1,0:T(8,128)(2,1)S(1)} %shard_map.67, bf16[32,1024]{1,0:T(8,128)(2,1)S(1)} %get-tuple-element.122, bf16[32,1024]{1,0:T(8,128)(2,1)S(1)} %get-tuple-element.121, bf16[32,1024]{1,0:T(8,128)(2,1)S(1)} %get-tuple-element.125), kind=kOutput, calls=%fused_computation.142 | convolution fusion | flops 405012480 | bytes 4784128 | tf_op jit(solution)/shard_map/dot_general | solution.py:153
  50.2 0.8 %convolution_add_fusion = f32[96,1024]{1,0:T(8,128)S(1)} fusion(f32[96,1024]{1,0:T(8,128)S(1)} %fusion.120, bf16[2048,1024]{1,0:T(8,128)(2,1)S(1)} %shard_map.68, bf16[32,1024]{1,0:T(8,128)(2,1)S(1)} %get-tuple-element.123, bf16[32,1024]{1,0:T(8,128)(2,1)S(1)} %get-tuple-element.124, bf16[32,1024]{1,0:T(8,128)(2,1)S(1)} %get-tuple-element.120), kind=kOutput, calls=%fused_computation | convolution fusion | flops 405110784 | bytes 5177344 | tf_op jit(solution)/shard_map/dot_general | solution.py:153
  51.6 0.9 %collective-permute-done.17 = f32[32]{0:T(128)S(1)} collective-permute-done((f32[32]{0:T(128)S(1)}, f32[32]{0:T(128)S(1)}, u32[]{:S(2)}, u32[]{:S(2)}) %collective-permute-start.17) | collective-permute-done | bytes 160 | tf_op jit(solution)/shard_map/ppermute | solution.py:19
  (87 shorter events, 11.3 us)
Async XLA Ops:
  1.4 7.9 %collective-permute-start = (f32[65,256]{1,0:T(8,128)S(1)}, f32[65,256]{1,0:T(8,128)S(1)}, u32[]{:S(2)}, u32[]{:S(2)}) collective-permute-start(f32[65,256]{1,0:T(8,128)S(1)} %pad_maximum_fusion.8.part_ref), channel_id=1, source_target_pairs={{0,8},{1,9},{2,10},{3,11},{4,12},{5,13},{6,14},{7,15},{8,0},{9,1},... | collective-permute-start | bytes 199688 | tf_op jit(solution)/shard_map/ppermute | solution.py:19
  6.3 5.5 %collective-permute-start.3 = (f32[65,256]{1,0:T(8,128)S(1)}, f32[65,256]{1,0:T(8,128)S(1)}, u32[]{:S(2)}, u32[]{:S(2)}) collective-permute-start(f32[65,256]{1,0:T(8,128)S(1)} %get-tuple-element.53), channel_id=1, source_target_pairs={{0,2},{1,3},{2,0},{3,1},{4,6},{5,7},{6,4},{7,5},{8,10},{9,11},{10,... | collective-permute-start | bytes 199688 | tf_op jit(solution)/shard_map/ppermute | solution.py:19
  9.4 5.2 %collective-permute-start.1 = (f32[65,512]{1,0:T(8,128)S(1)}, f32[65,512]{1,0:T(8,128)S(1)}, u32[]{:S(2)}, u32[]{:S(2)}) collective-permute-start(f32[65,512]{1,0:T(8,128)S(1)} %pad_maximum_fusion.6), channel_id=1, source_target_pairs={{0,4},{1,5},{2,6},{3,7},{4,0},{5,1},{6,2},{7,3},{8,12},{9,13},{10,... | collective-permute-start | bytes 399368 | tf_op jit(solution)/shard_map/ppermute | solution.py:19
  10.2 4.4 %collective-permute-start.4 = (f32[65,256]{1,0:T(8,128)S(1)}, f32[65,256]{1,0:T(8,128)S(1)}, u32[]{:S(2)}, u32[]{:S(2)}) collective-permute-start(f32[65,256]{1,0:T(8,128)S(1)} %get-tuple-element.54), channel_id=1, source_target_pairs={{0,2},{1,3},{2,0},{3,1},{4,6},{5,7},{6,4},{7,5},{8,10},{9,11},{10,... | collective-permute-start | bytes 199688 | tf_op jit(solution)/shard_map/ppermute | solution.py:19
  14.6 5.8 %collective-permute-start.5 = (f32[65,512]{1,0:T(8,128)S(1)}, f32[65,512]{1,0:T(8,128)S(1)}, u32[]{:S(2)}, u32[]{:S(2)}) collective-permute-start(f32[65,512]{1,0:T(8,128)S(1)} %collective-permute-done.1.part_ref), channel_id=1, source_target_pairs={{0,2},{1,3},{2,0},{3,1},{4,6},{5,7},{6,4},{7,5},{8,10},{9,11},{10,... | collective-permute-start | bytes 399368 | tf_op jit(solution)/shard_map/ppermute | solution.py:19
  16.4 2.4 %collective-permute-start.2 = (f32[64,1024]{1,0:T(8,128)S(1)}, f32[64,1024]{1,0:T(8,128)S(1)}, u32[]{:S(2)}, u32[]{:S(2)}) collective-permute-start(f32[64,1024]{1,0:T(8,128)S(1)} %slice.214), channel_id=1, source_target_pairs={{0,1},{1,0},{2,3},{3,2},{4,5},{5,4},{6,7},{7,6},{8,9},{9,8},{10,11... | collective-permute-start | bytes 786440 | tf_op jit(solution)/shard_map/ppermute | solution.py:19
  18.3 3.9 %collective-permute-start.6 = (f32[64,512]{1,0:T(8,128)S(1)}, f32[64,512]{1,0:T(8,128)S(1)}, u32[]{:S(2)}, u32[]{:S(2)}) collective-permute-start(f32[64,512]{1,0:T(8,128)S(1)} %pad_maximum_fusion.7), channel_id=1, source_target_pairs={{0,1},{1,0},{2,3},{3,2},{4,5},{5,4},{6,7},{7,6},{8,9},{9,8},{10,11... | collective-permute-start | bytes 393224 | tf_op jit(solution)/shard_map/ppermute | solution.py:19
  20.5 1.7 %collective-permute-start.7 = (f32[64,512]{1,0:T(8,128)S(1)}, f32[64,512]{1,0:T(8,128)S(1)}, u32[]{:S(2)}, u32[]{:S(2)}) collective-permute-start(f32[64,512]{1,0:T(8,128)S(1)} %slice.174), channel_id=1, source_target_pairs={{0,1},{1,0},{2,3},{3,2},{4,5},{5,4},{6,7},{7,6},{8,9},{9,8},{10,11... | collective-permute-start | bytes 393224 | tf_op jit(solution)/shard_map/ppermute | solution.py:19
  23.9 5.9 %collective-permute-start.9 = (f32[32,1024]{1,0:T(8,128)S(1)}, f32[32,1024]{1,0:T(8,128)S(1)}, u32[]{:S(2)}, u32[]{:S(2)}) collective-permute-start(f32[32,1024]{1,0:T(8,128)S(1)} %get-tuple-element.72), channel_id=1, source_target_pairs={{0,2},{1,3},{2,0},{3,1},{4,6},{5,7},{6,4},{7,5},{8,10},{9,11},{10,... | collective-permute-start | bytes 393224 | tf_op jit(solution)/shard_map/ppermute | solution.py:19
  25.0 1.4 %collective-permute-start.8 = (f32[32,1024]{1,0:T(8,128)S(1)}, f32[32,1024]{1,0:T(8,128)S(1)}, u32[]{:S(2)}, u32[]{:S(2)}) collective-permute-start(f32[32,1024]{1,0:T(8,128)S(1)} %get-tuple-element.72), channel_id=1, source_target_pairs={{0,1},{1,0},{2,3},{3,2},{4,5},{5,4},{6,7},{7,6},{8,9},{9,8},{10,11... | collective-permute-start | bytes 393224 | tf_op jit(solution)/shard_map/ppermute | solution.py:19
  29.9 1.3 %collective-permute-start.10 = (f32[32,1024]{1,0:T(8,128)S(1)}, f32[32,1024]{1,0:T(8,128)S(1)}, u32[]{:S(2)}, u32[]{:S(2)}) collective-permute-start(f32[32,1024]{1,0:T(8,128)S(1)} %collective-permute-done.9), channel_id=1, source_target_pairs={{0,1},{1,0},{2,3},{3,2},{4,5},{5,4},{6,7},{7,6},{8,9},{9,8},{10,11... | collective-permute-start | bytes 393224 | tf_op jit(solution)/shard_map/ppermute | solution.py:19
  32.6 5.6 %collective-permute-start.12 = (f32[32,1024]{1,0:T(8,128)S(1)}, f32[32,1024]{1,0:T(8,128)S(1)}, u32[]{:S(2)}, u32[]{:S(2)}) collective-permute-start(f32[32,1024]{1,0:T(8,128)S(1)} %get-tuple-element.86), channel_id=1, source_target_pairs={{0,2},{1,3},{2,0},{3,1},{4,6},{5,7},{6,4},{7,5},{8,10},{9,11},{10,... | collective-permute-start | bytes 393224 | tf_op jit(solution)/shard_map/ppermute | solution.py:19
  33.8 1.4 %collective-permute-start.11 = (f32[32,1024]{1,0:T(8,128)S(1)}, f32[32,1024]{1,0:T(8,128)S(1)}, u32[]{:S(2)}, u32[]{:S(2)}) collective-permute-start(f32[32,1024]{1,0:T(8,128)S(1)} %get-tuple-element.86), channel_id=1, source_target_pairs={{0,1},{1,0},{2,3},{3,2},{4,5},{5,4},{6,7},{7,6},{8,9},{9,8},{10,11... | collective-permute-start | bytes 393224 | tf_op jit(solution)/shard_map/ppermute | solution.py:19
  38.2 1.3 %collective-permute-start.13 = (f32[32,1024]{1,0:T(8,128)S(1)}, f32[32,1024]{1,0:T(8,128)S(1)}, u32[]{:S(2)}, u32[]{:S(2)}) collective-permute-start(f32[32,1024]{1,0:T(8,128)S(1)} %collective-permute-done.12), channel_id=1, source_target_pairs={{0,1},{1,0},{2,3},{3,2},{4,5},{5,4},{6,7},{7,6},{8,9},{9,8},{10,11... | collective-permute-start | bytes 393224 | tf_op jit(solution)/shard_map/ppermute | solution.py:19
  41.0 5.6 %collective-permute-start.15 = (f32[32,1024]{1,0:T(8,128)S(1)}, f32[32,1024]{1,0:T(8,128)S(1)}, u32[]{:S(2)}, u32[]{:S(2)}) collective-permute-start(f32[32,1024]{1,0:T(8,128)S(1)} %get-tuple-element.96), channel_id=1, source_target_pairs={{0,2},{1,3},{2,0},{3,1},{4,6},{5,7},{6,4},{7,5},{8,10},{9,11},{10,... | collective-permute-start | bytes 393224 | tf_op jit(solution)/shard_map/ppermute | solution.py:19
  42.1 1.4 %collective-permute-start.14 = (f32[32,1024]{1,0:T(8,128)S(1)}, f32[32,1024]{1,0:T(8,128)S(1)}, u32[]{:S(2)}, u32[]{:S(2)}) collective-permute-start(f32[32,1024]{1,0:T(8,128)S(1)} %get-tuple-element.96), channel_id=1, source_target_pairs={{0,1},{1,0},{2,3},{3,2},{4,5},{5,4},{6,7},{7,6},{8,9},{9,8},{10,11... | collective-permute-start | bytes 393224 | tf_op jit(solution)/shard_map/ppermute | solution.py:19
  46.6 1.3 %collective-permute-start.16 = (f32[32,1024]{1,0:T(8,128)S(1)}, f32[32,1024]{1,0:T(8,128)S(1)}, u32[]{:S(2)}, u32[]{:S(2)}) collective-permute-start(f32[32,1024]{1,0:T(8,128)S(1)} %collective-permute-done.15), channel_id=1, source_target_pairs={{0,1},{1,0},{2,3},{3,2},{4,5},{5,4},{6,7},{7,6},{8,9},{9,8},{10,11... | collective-permute-start | bytes 393224 | tf_op jit(solution)/shard_map/ppermute | solution.py:19
  51.4 1.2 %collective-permute-start.17 = (f32[32]{0:T(128)S(1)}, f32[32]{0:T(128)S(1)}, u32[]{:S(2)}, u32[]{:S(2)}) collective-permute-start(f32[32]{0:T(128)S(1)} %get-tuple-element.104), channel_id=1, source_target_pairs={{0,1},{1,0},{2,3},{3,2},{4,5},{5,4},{6,7},{7,6},{8,9},{9,8},{10,11... | collective-permute-start | bytes 392 | tf_op jit(solution)/shard_map/ppermute | solution.py:19

commit v20 on v19

--- a/solution.py
+++ b/solution.py
@@ -207,17 +207,12 @@
             noise, mine = mine[-1:], mine[:-1]
             across = swap(mine, n, 1)
             my_applied = build(mine, noise * mine[feats:])
-            side_own, side_far, my_applied = fence((side_own, side_far, my_applied))
-            early = join(side_own, side_far)
-            early_across = swap(early[:-1], n, 1)
             my_applied = build(across, my_applied)
             side_last, my_applied = fence((side_last, my_applied))
-            last_across = swap(side_last[:-1], n, 1)
-            beside = join(early, side_last)
+            beside = join(side_own, side_far, side_last)
             noise_beside, beside = beside[-1:], beside[:-1]
+            beside_across = swap(beside, n, 1)
             my_far = build(beside, jnp.zeros_like(my_applied))
-            early_across, last_across, my_far = fence((early_across, last_across, my_far))
-            beside_across = join(early_across, last_across)
             my_far = build(beside_across, my_far)
             my_applied = my_applied + my_far
             first = [mine, across, beside, beside_across]

time: 53.5 us -> 52.9 us (0.989)
  waiting for transfers between devices: 12 us -> 10.3 us
  starting transfers between devices: 14.2 us -> 15.3 us
    ppermute x18 -> x17, waiting for transfers between devices: 12 us -> 10.3 us  [swap(): return lax.ppermute(x, 'blk', [(i, i ^ stride) for i in range(n)])]
    ppermute x18 -> x17, starting transfers between devices: 14.2 us -> 15.3 us  [swap(): return lax.ppermute(x, 'blk', [(i, i ^ stride) for i in range(n)])]
  transfers between devices with their start and end apart: 18 -> 17, of which waited for: 12 -> 12; matrix products, arithmetic and copies ran while one was open for 18% -> 18% of each run, Pallas kernels for 14% -> 14%
where the time goes in v20:
time: 52.9 us; the launch traced here: 52.7 us
  starting transfers between devices  15.3 us (29%)
  matrix products  11.5 us (22%)
  waiting for transfers between devices  10.3 us (19%)
  Pallas kernels  8.81 us (17%)
  other arithmetic  5.47 us (10%)
  between operations  0.99 us (2%)
    ppermute x17, starting transfers between devices, swap(): return lax.ppermute(x, 'blk', [(i, i ^ stride) for i in range(n)])  15.3 us
    dot_general x14, matrix products, apply_parts(): jnp.dot(jnp.concatenate([parts, parts], axis=1), piece, preferred_element...  11.5 us
    ppermute x17, waiting for transfers between devices, swap(): return lax.ppermute(x, 'blk', [(i, i ^ stride) for i in range(n)])  10.3 us
    pallas_call x10, Pallas kernels, call(): pl.pallas_call(kernel, out_shape=outs, in_specs=[whole] * len(args), out_...  8.81 us
  transfers between devices with their start and end apart: 17, of which 12 were waited for; matrix products, arithmetic and copies ran while one was open for 18% of the time, Pallas kernels for 14%

profile of v20, /device:TPU:0, one launch (start us, length us, event | category | flops | bytes accessed | tf_op | source)
XLA Modules:
  0.0 52.7 jit_solution(10398306299386124310)
XLA Ops:
  0.6 0.8 %pad_maximum_fusion.7.part_ref = f32[65,256]{1,0:T(8,128)S(1)} fusion(f32[1,256]{1,0:T(1,128)} %bitcast.24, f32[32,256]{1,0:T(8,128)} %param.7, f32[32,256]{1,0:T(8,128)} %param.4), kind=kLoop, calls=%fused_computation.277 | loop fusion | flops 33280 | bytes 133120 | tf_op jit(solution)/shard_map/concatenate | solution.py:186
  1.4 4.0 %collective-permute-start = (f32[65,256]{1,0:T(8,128)S(1)}, f32[65,256]{1,0:T(8,128)S(1)}, u32[]{:S(2)}, u32[]{:S(2)}) collective-permute-start(f32[65,256]{1,0:T(8,128)S(1)} %pad_maximum_fusion.7.part_ref), channel_id=1, source_target_pairs={{0,8},{1,9},{2,10},{3,11},{4,12},{5,13},{6,14},{7,15},{8,0},{9,1},... | collective-permute-start | bytes 199688 | tf_op jit(solution)/shard_map/ppermute | solution.py:19
  6.3 1.6 %collective-permute-start.3 = (f32[65,256]{1,0:T(8,128)S(1)}, f32[65,256]{1,0:T(8,128)S(1)}, u32[]{:S(2)}, u32[]{:S(2)}) collective-permute-start(f32[65,256]{1,0:T(8,128)S(1)} %get-tuple-element.47), channel_id=1, source_target_pairs={{0,2},{1,3},{2,0},{3,1},{4,6},{5,7},{6,4},{7,5},{8,10},{9,11},{10,... | collective-permute-start | bytes 199688 | tf_op jit(solution)/shard_map/ppermute | solution.py:19
  7.9 1.5 %collective-permute-done.part_ref = f32[65,256]{1,0:T(8,128)S(1)} collective-permute-done((f32[65,256]{1,0:T(8,128)S(1)}, f32[65,256]{1,0:T(8,128)S(1)}, u32[]{:S(2)}, u32[]{:S(2)}) %collective-permute-start) | collective-permute-done | bytes 66592 | tf_op jit(solution)/shard_map/ppermute | solution.py:19
  10.2 1.6 %collective-permute-start.4 = (f32[65,256]{1,0:T(8,128)S(1)}, f32[65,256]{1,0:T(8,128)S(1)}, u32[]{:S(2)}, u32[]{:S(2)}) collective-permute-start(f32[65,256]{1,0:T(8,128)S(1)} %get-tuple-element.48), channel_id=1, source_target_pairs={{0,2},{1,3},{2,0},{3,1},{4,6},{5,7},{6,4},{7,5},{8,10},{9,11},{10,... | collective-permute-start | bytes 199688 | tf_op jit(solution)/shard_map/ppermute | solution.py:19
  11.8 2.8 %collective-permute-done.4 = f32[65,256]{1,0:T(8,128)S(1)} collective-permute-done((f32[65,256]{1,0:T(8,128)S(1)}, f32[65,256]{1,0:T(8,128)S(1)}, u32[]{:S(2)}, u32[]{:S(2)}) %collective-permute-start.4) | collective-permute-done | bytes 66592 | tf_op jit(solution)/shard_map/ppermute | solution.py:19
  14.6 1.7 %collective-permute-start.5 = (f32[65,512]{1,0:T(8,128)S(1)}, f32[65,512]{1,0:T(8,128)S(1)}, u32[]{:S(2)}, u32[]{:S(2)}) collective-permute-start(f32[65,512]{1,0:T(8,128)S(1)} %collective-permute-done.1.part_ref), channel_id=1, source_target_pairs={{0,2},{1,3},{2,0},{3,1},{4,6},{5,7},{6,4},{7,5},{8,10},{9,11},{10,... | collective-permute-start | bytes 399368 | tf_op jit(solution)/shard_map/ppermute | solution.py:19
  16.7 1.6 %shard_map.62 = (bf16[2048,1024]{1,0:T(8,128)(2,1)S(1)}, f32[32,1024]{1,0:T(8,128)S(1)}) custom-call(f32[32,1024]{1,0:T(8,128)S(1)} %get-tuple-element.117.rows_ref, f32[32,1]{1,0:T(8,128)S(1)} %copy.6.scale_ref, bf16[256,1024]{1,0:T(8,128)(2,1)S(1)} %pad_maximum_fusion.right_ref, f32[32,1024]{1,0:T(8,128)S(1)} %get-tuple-element.118.refs_0_, ...), custom_call_target="tpu_custom_call" | custom-call | flops 872415232 | bytes 4194304 | tf_op jit(solution)/shard_map/pallas_call | solution.py:115
  18.3 1.6 %shard_map.63 = (bf16[2048,1024]{1,0:T(8,128)(2,1)S(1)}, f32[32,1024]{1,0:T(8,128)S(1)}) custom-call(f32[32,1024]{1,0:T(8,128)S(1)} %get-tuple-element.122.rows_ref, f32[32,1]{1,0:T(8,128)S(1)} %copy.6.scale_ref, bf16[256,1024]{1,0:T(8,128)(2,1)S(1)} %pad_maximum_fusion.right_ref, f32[32,1024]{1,0:T(8,128)S(1)} %get-tuple-element.121.refs_0_, ...), custom_call_target="tpu_custom_call" | custom-call | flops 872415232 | bytes 4194304 | tf_op jit(solution)/shard_map/pallas_call | solution.py:115
  20.6 1.6 %shard_map.64 = (bf16[2048,1024]{1,0:T(8,128)(2,1)S(1)}, f32[32,1024]{1,0:T(8,128)S(1)}) custom-call(f32[32,1024]{1,0:T(8,128)S(1)} %get-tuple-element.65.rows_ref.part_ref, f32[32,1]{1,0:T(8,128)S(1)} %copy.6.scale_ref, bf16[256,1024]{1,0:T(8,128)(2,1)S(1)} %pad_maximum_fusion.right_ref, f32[32,1024]{1,0:T(8,128)S(1)} %get-tuple-element.114.refs_0_, ...), custom_call_target="tpu_custom_call" | custom-call | flops 872415232 | bytes 4194304 | tf_op jit(solution)/shard_map/pallas_call | solution.py:115
  22.2 1.6 %shard_map.65 = (bf16[2048,1024]{1,0:T(8,128)(2,1)S(1)}, f32[32,1024]{1,0:T(8,128)S(1)}) custom-call(f32[32,1024]{1,0:T(8,128)S(1)} %get-tuple-element.76.rows_ref, f32[32,1]{1,0:T(8,128)S(1)} %copy.6.scale_ref, bf16[256,1024]{1,0:T(8,128)(2,1)S(1)} %pad_maximum_fusion.right_ref, f32[32,1024]{1,0:T(8,128)S(1)} %get-tuple-element.119.refs_0_, ...), custom_call_target="tpu_custom_call" | custom-call | flops 872415232 | bytes 4194304 | tf_op jit(solution)/shard_map/pallas_call | solution.py:115
  23.8 1.2 %collective-permute-start.8 = (f32[32,1024]{1,0:T(8,128)S(1)}, f32[32,1024]{1,0:T(8,128)S(1)}, u32[]{:S(2)}, u32[]{:S(2)}) collective-permute-start(f32[32,1024]{1,0:T(8,128)S(1)} %get-tuple-element.60), channel_id=1, source_target_pairs={{0,2},{1,3},{2,0},{3,1},{4,6},{5,7},{6,4},{7,5},{8,10},{9,11},{10,... | collective-permute-start | bytes 393224 | tf_op jit(solution)/shard_map/ppermute | solution.py:19
  26.4 0.8 %convolution_add_fusion.6 = f32[96,1024]{1,0:T(8,128)S(1)} fusion(f32[96,1024]{1,0:T(8,128)S(1)} %fusion.6, bf16[2048,1024]{1,0:T(8,128)(2,1)S(1)} %get-tuple-element.63, bf16[32,1024]{1,0:T(8,128)(2,1)S(1)} %get-tuple-element.155, bf16[32,1024]{1,0:T(8,128)(2,1)S(1)} %get-tuple-element.156, bf16[32,1024]{1,0:T(8,128)(2,1)S(1)} %get-tuple-element.154), kind=kOutput, calls=%fused_computation.6 | convolution fusion | flops 405110784 | bytes 5177344 | tf_op jit(solution)/shard_map/dot_general | solution.py:153
  27.4 1.1 %shard_map.67 = bf16[2048,1024]{1,0:T(8,128)(2,1)S(1)} custom-call(f32[32,1024]{1,0:T(8,128)S(1)} %get-tuple-element.65.rows_ref.part_ref, f32[32,1]{1,0:T(8,128)S(1)} %copy.6.scale_ref, bf16[256,1024]{1,0:T(8,128)(2,1)S(1)} %shard_map.66.right_ref), custom_call_target="tpu_custom_call" | custom-call | flops 872415232 | bytes 4194304 | tf_op jit(solution)/shard_map/pallas_call | solution.py:115
  28.4 0.8 %collective-permute-done.8 = f32[32,1024]{1,0:T(8,128)S(1)} collective-permute-done((f32[32,1024]{1,0:T(8,128)S(1)}, f32[32,1024]{1,0:T(8,128)S(1)}, u32[]{:S(2)}, u32[]{:S(2)}) %collective-permute-start.8) | collective-permute-done | bytes 131104 | tf_op jit(solution)/shard_map/ppermute | solution.py:19
  29.3 0.8 %fusion.21 = f32[96,1024]{1,0:T(8,128)S(1)} fusion(bf16[2048,1024]{1,0:T(8,128)(2,1)S(1)} %get-tuple-element.69, bf16[32,1024]{1,0:T(8,128)(2,1)S(1)} %get-tuple-element.152, bf16[32,1024]{1,0:T(8,128)(2,1)S(1)} %get-tuple-element.153, bf16[32,1024]{1,0:T(8,128)(2,1)S(1)} %get-tuple-element.151), kind=kOutput, calls=%fused_computation.43 | convolution fusion | flops 405012480 | bytes 4784128 | tf_op jit(solution)/shard_map/dot_general | solution.py:153
  31.1 0.8 %convolution_add_fusion.5 = f32[96,1024]{1,0:T(8,128)S(1)} fusion(f32[96,1024]{1,0:T(8,128)S(1)} %fusion.21, bf16[2048,1024]{1,0:T(8,128)(2,1)S(1)} %get-tuple-element.73, bf16[32,1024]{1,0:T(8,128)(2,1)S(1)} %get-tuple-element.148, bf16[32,1024]{1,0:T(8,128)(2,1)S(1)} %get-tuple-element.149, bf16[32,1024]{1,0:T(8,128)(2,1)S(1)} %get-tuple-element.147), kind=kOutput, calls=%fused_computation.5 | convolution fusion | flops 405110784 | bytes 5177344 | tf_op jit(solution)/shard_map/dot_general | solution.py:153
  32.0 1.6 %collective-permute-start.11 = (f32[32,1024]{1,0:T(8,128)S(1)}, f32[32,1024]{1,0:T(8,128)S(1)}, u32[]{:S(2)}, u32[]{:S(2)}) collective-permute-start(f32[32,1024]{1,0:T(8,128)S(1)} %get-tuple-element.74), channel_id=1, source_target_pairs={{0,2},{1,3},{2,0},{3,1},{4,6},{5,7},{6,4},{7,5},{8,10},{9,11},{10,... | collective-permute-start | bytes 393224 | tf_op jit(solution)/shard_map/ppermute | solution.py:19
  33.9 0.8 %fusion.44 = f32[96,1024]{1,0:T(8,128)S(1)} fusion(bf16[2048,1024]{1,0:T(8,128)(2,1)S(1)} %get-tuple-element.62, bf16[96,1024]{1,0:T(8,128)(2,1)S(1)} %pad_maximum_fusion.4), kind=kOutput, calls=%fused_computation.66 | convolution fusion | flops 403439616 | bytes 4784128 | tf_op jit(solution)/shard_map/dot_general | solution.py:153
  35.2 1.0 %convolution_add_fusion.4 = f32[96,1024]{1,0:T(8,128)S(1)} fusion(f32[96,1024]{1,0:T(8,128)S(1)} %fusion.44, bf16[2048,1024]{1,0:T(8,128)(2,1)S(1)} %get-tuple-element.63, bf16[32,1024]{1,0:T(8,128)(2,1)S(1)} %get-tuple-element.143, bf16[32,1024]{1,0:T(8,128)(2,1)S(1)} %get-tuple-element.144, bf16[32,1024]{1,0:T(8,128)(2,1)S(1)} %get-tuple-element.142), kind=kOutput, calls=%fused_computation.4 | convolution fusion | flops 405110784 | bytes 5177344 | tf_op jit(solution)/shard_map/dot_general | solution.py:153
  36.2 1.1 %shard_map.68 = bf16[2048,1024]{1,0:T(8,128)(2,1)S(1)} custom-call(f32[32,1024]{1,0:T(8,128)S(1)} %get-tuple-element.76.rows_ref, f32[32,1]{1,0:T(8,128)S(1)} %copy.6.scale_ref, bf16[256,1024]{1,0:T(8,128)(2,1)S(1)} %shard_map.66.right_ref), custom_call_target="tpu_custom_call" | custom-call | flops 872415232 | bytes 4194304 | tf_op jit(solution)/shard_map/pallas_call | solution.py:115
  37.7 0.8 %fusion.59 = f32[96,1024]{1,0:T(8,128)S(1)} fusion(bf16[2048,1024]{1,0:T(8,128)(2,1)S(1)} %get-tuple-element.69, bf16[32,1024]{1,0:T(8,128)(2,1)S(1)} %get-tuple-element.140, bf16[32,1024]{1,0:T(8,128)(2,1)S(1)} %get-tuple-element.141, bf16[32,1024]{1,0:T(8,128)(2,1)S(1)} %get-tuple-element.139), kind=kOutput, calls=%fused_computation.81 | convolution fusion | flops 405012480 | bytes 4784128 | tf_op jit(solution)/shard_map/dot_general | solution.py:153
  39.4 0.8 %convolution_add_fusion.3 = f32[96,1024]{1,0:T(8,128)S(1)} fusion(f32[96,1024]{1,0:T(8,128)S(1)} %fusion.59, bf16[2048,1024]{1,0:T(8,128)(2,1)S(1)} %get-tuple-element.73, bf16[32,1024]{1,0:T(8,128)(2,1)S(1)} %get-tuple-element.136, bf16[32,1024]{1,0:T(8,128)(2,1)S(1)} %get-tuple-element.137, bf16[32,1024]{1,0:T(8,128)(2,1)S(1)} %get-tuple-element.135), kind=kOutput, calls=%fused_computation.3 | convolution fusion | flops 405110784 | bytes 5177344 | tf_op jit(solution)/shard_map/dot_general | solution.py:153
  40.4 1.6 %collective-permute-start.14 = (f32[32,1024]{1,0:T(8,128)S(1)}, f32[32,1024]{1,0:T(8,128)S(1)}, u32[]{:S(2)}, u32[]{:S(2)}) collective-permute-start(f32[32,1024]{1,0:T(8,128)S(1)} %get-tuple-element.84), channel_id=1, source_target_pairs={{0,2},{1,3},{2,0},{3,1},{4,6},{5,7},{6,4},{7,5},{8,10},{9,11},{10,... | collective-permute-start | bytes 393224 | tf_op jit(solution)/shard_map/ppermute | solution.py:19
  42.2 0.8 %fusion.82 = f32[96,1024]{1,0:T(8,128)S(1)} fusion(bf16[2048,1024]{1,0:T(8,128)(2,1)S(1)} %get-tuple-element.62, bf16[96,1024]{1,0:T(8,128)(2,1)S(1)} %pad_maximum_fusion.5), kind=kOutput, calls=%fused_computation.104 | convolution fusion | flops 403439616 | bytes 4784128 | tf_op jit(solution)/shard_map/dot_general | solution.py:153
  43.5 0.8 %convolution_add_fusion.2 = f32[96,1024]{1,0:T(8,128)S(1)} fusion(f32[96,1024]{1,0:T(8,128)S(1)} %fusion.82, bf16[2048,1024]{1,0:T(8,128)(2,1)S(1)} %get-tuple-element.63, bf16[32,1024]{1,0:T(8,128)(2,1)S(1)} %get-tuple-element.131, bf16[32,1024]{1,0:T(8,128)(2,1)S(1)} %get-tuple-element.132, bf16[32,1024]{1,0:T(8,128)(2,1)S(1)} %get-tuple-element.130), kind=kOutput, calls=%fused_computation.2 | convolution fusion | flops 405110784 | bytes 5177344 | tf_op jit(solution)/shard_map/dot_general | solution.py:153
  44.3 1.7 %collective-permute-done.14 = f32[32,1024]{1,0:T(8,128)S(1)} collective-permute-done((f32[32,1024]{1,0:T(8,128)S(1)}, f32[32,1024]{1,0:T(8,128)S(1)}, u32[]{:S(2)}, u32[]{:S(2)}) %collective-permute-start.14) | collective-permute-done | bytes 131104 | tf_op jit(solution)/shard_map/ppermute | solution.py:19
  46.0 0.8 %fusion.97 = f32[96,1024]{1,0:T(8,128)S(1)} fusion(bf16[2048,1024]{1,0:T(8,128)(2,1)S(1)} %get-tuple-element.69, bf16[32,1024]{1,0:T(8,128)(2,1)S(1)} %get-tuple-element.128, bf16[32,1024]{1,0:T(8,128)(2,1)S(1)} %get-tuple-element.129, bf16[32,1024]{1,0:T(8,128)(2,1)S(1)} %get-tuple-element.127), kind=kOutput, calls=%fused_computation.119 | convolution fusion | flops 405012480 | bytes 4784128 | tf_op jit(solution)/shard_map/dot_general | solution.py:153
  48.0 0.8 %convolution_add_fusion.1 = f32[96,1024]{1,0:T(8,128)S(1)} fusion(f32[96,1024]{1,0:T(8,128)S(1)} %fusion.97, bf16[2048,1024]{1,0:T(8,128)(2,1)S(1)} %get-tuple-element.73, bf16[32,1024]{1,0:T(8,128)(2,1)S(1)} %get-tuple-element.124, bf16[32,1024]{1,0:T(8,128)(2,1)S(1)} %get-tuple-element.125, bf16[32,1024]{1,0:T(8,128)(2,1)S(1)} %get-tuple-element.123), kind=kOutput, calls=%fused_computation.1 | convolution fusion | flops 405110784 | bytes 5177344 | tf_op jit(solution)/shard_map/dot_general | solution.py:153
  48.8 0.8 %fusion.120 = f32[96,1024]{1,0:T(8,128)S(1)} fusion(bf16[2048,1024]{1,0:T(8,128)(2,1)S(1)} %shard_map.67, bf16[32,1024]{1,0:T(8,128)(2,1)S(1)} %get-tuple-element.110, bf16[32,1024]{1,0:T(8,128)(2,1)S(1)} %get-tuple-element.109, bf16[32,1024]{1,0:T(8,128)(2,1)S(1)} %get-tuple-element.113), kind=kOutput, calls=%fused_computation.142 | convolution fusion | flops 405012480 | bytes 4784128 | tf_op jit(solution)/shard_map/dot_general | solution.py:153
  49.6 0.8 %convolution_add_fusion = f32[96,1024]{1,0:T(8,128)S(1)} fusion(f32[96,1024]{1,0:T(8,128)S(1)} %fusion.120, bf16[2048,1024]{1,0:T(8,128)(2,1)S(1)} %shard_map.68, bf16[32,1024]{1,0:T(8,128)(2,1)S(1)} %get-tuple-element.111, bf16[32,1024]{1,0:T(8,128)(2,1)S(1)} %get-tuple-element.112, bf16[32,1024]{1,0:T(8,128)(2,1)S(1)} %get-tuple-element.108), kind=kOutput, calls=%fused_computation | convolution fusion | flops 405110784 | bytes 5177344 | tf_op jit(solution)/shard_map/dot_general | solution.py:153
  51.0 0.9 %collective-permute-done.16 = f32[32]{0:T(128)S(1)} collective-permute-done((f32[32]{0:T(128)S(1)}, f32[32]{0:T(128)S(1)}, u32[]{:S(2)}, u32[]{:S(2)}) %collective-permute-start.16) | collective-permute-done | bytes 160 | tf_op jit(solution)/shard_map/ppermute | solution.py:19
  (82 shorter events, 10.7 us)
Async XLA Ops:
  1.4 7.9 %collective-permute-start = (f32[65,256]{1,0:T(8,128)S(1)}, f32[65,256]{1,0:T(8,128)S(1)}, u32[]{:S(2)}, u32[]{:S(2)}) collective-permute-start(f32[65,256]{1,0:T(8,128)S(1)} %pad_maximum_fusion.7.part_ref), channel_id=1, source_target_pairs={{0,8},{1,9},{2,10},{3,11},{4,12},{5,13},{6,14},{7,15},{8,0},{9,1},... | collective-permute-start | bytes 199688 | tf_op jit(solution)/shard_map/ppermute | solution.py:19
  6.3 5.5 %collective-permute-start.3 = (f32[65,256]{1,0:T(8,128)S(1)}, f32[65,256]{1,0:T(8,128)S(1)}, u32[]{:S(2)}, u32[]{:S(2)}) collective-permute-start(f32[65,256]{1,0:T(8,128)S(1)} %get-tuple-element.47), channel_id=1, source_target_pairs={{0,2},{1,3},{2,0},{3,1},{4,6},{5,7},{6,4},{7,5},{8,10},{9,11},{10,... | collective-permute-start | bytes 199688 | tf_op jit(solution)/shard_map/ppermute | solution.py:19
  9.4 5.2 %collective-permute-start.1 = (f32[65,512]{1,0:T(8,128)S(1)}, f32[65,512]{1,0:T(8,128)S(1)}, u32[]{:S(2)}, u32[]{:S(2)}) collective-permute-start(f32[65,512]{1,0:T(8,128)S(1)} %pad_maximum_fusion.6), channel_id=1, source_target_pairs={{0,4},{1,5},{2,6},{3,7},{4,0},{5,1},{6,2},{7,3},{8,12},{9,13},{10,... | collective-permute-start | bytes 399368 | tf_op jit(solution)/shard_map/ppermute | solution.py:19
  10.2 4.4 %collective-permute-start.4 = (f32[65,256]{1,0:T(8,128)S(1)}, f32[65,256]{1,0:T(8,128)S(1)}, u32[]{:S(2)}, u32[]{:S(2)}) collective-permute-start(f32[65,256]{1,0:T(8,128)S(1)} %get-tuple-element.48), channel_id=1, source_target_pairs={{0,2},{1,3},{2,0},{3,1},{4,6},{5,7},{6,4},{7,5},{8,10},{9,11},{10,... | collective-permute-start | bytes 199688 | tf_op jit(solution)/shard_map/ppermute | solution.py:19
  14.6 5.3 %collective-permute-start.5 = (f32[65,512]{1,0:T(8,128)S(1)}, f32[65,512]{1,0:T(8,128)S(1)}, u32[]{:S(2)}, u32[]{:S(2)}) collective-permute-start(f32[65,512]{1,0:T(8,128)S(1)} %collective-permute-done.1.part_ref), channel_id=1, source_target_pairs={{0,2},{1,3},{2,0},{3,1},{4,6},{5,7},{6,4},{7,5},{8,10},{9,11},{10,... | collective-permute-start | bytes 399368 | tf_op jit(solution)/shard_map/ppermute | solution.py:19
  16.4 1.9 %collective-permute-start.2 = (f32[64,1024]{1,0:T(8,128)S(1)}, f32[64,1024]{1,0:T(8,128)S(1)}, u32[]{:S(2)}, u32[]{:S(2)}) collective-permute-start(f32[64,1024]{1,0:T(8,128)S(1)} %slice.209), channel_id=1, source_target_pairs={{0,1},{1,0},{2,3},{3,2},{4,5},{5,4},{6,7},{7,6},{8,9},{9,8},{10,11... | collective-permute-start | bytes 786440 | tf_op jit(solution)/shard_map/ppermute | solution.py:19
  20.0 2.2 %collective-permute-start.6 = (f32[64,1024]{1,0:T(8,128)S(1)}, f32[64,1024]{1,0:T(8,128)S(1)}, u32[]{:S(2)}, u32[]{:S(2)}) collective-permute-start(f32[64,1024]{1,0:T(8,128)S(1)} %slice.214), channel_id=1, source_target_pairs={{0,1},{1,0},{2,3},{3,2},{4,5},{5,4},{6,7},{7,6},{8,9},{9,8},{10,11... | collective-permute-start | bytes 786440 | tf_op jit(solution)/shard_map/ppermute | solution.py:19
  23.8 5.5 %collective-permute-start.8 = (f32[32,1024]{1,0:T(8,128)S(1)}, f32[32,1024]{1,0:T(8,128)S(1)}, u32[]{:S(2)}, u32[]{:S(2)}) collective-permute-start(f32[32,1024]{1,0:T(8,128)S(1)} %get-tuple-element.60), channel_id=1, source_target_pairs={{0,2},{1,3},{2,0},{3,1},{4,6},{5,7},{6,4},{7,5},{8,10},{9,11},{10,... | collective-permute-start | bytes 393224 | tf_op jit(solution)/shard_map/ppermute | solution.py:19
  25.0 1.4 %collective-permute-start.7 = (f32[32,1024]{1,0:T(8,128)S(1)}, f32[32,1024]{1,0:T(8,128)S(1)}, u32[]{:S(2)}, u32[]{:S(2)}) collective-permute-start(f32[32,1024]{1,0:T(8,128)S(1)} %get-tuple-element.60), channel_id=1, source_target_pairs={{0,1},{1,0},{2,3},{3,2},{4,5},{5,4},{6,7},{7,6},{8,9},{9,8},{10,11... | collective-permute-start | bytes 393224 | tf_op jit(solution)/shard_map/ppermute | solution.py:19
  29.3 1.3 %collective-permute-start.9 = (f32[32,1024]{1,0:T(8,128)S(1)}, f32[32,1024]{1,0:T(8,128)S(1)}, u32[]{:S(2)}, u32[]{:S(2)}) collective-permute-start(f32[32,1024]{1,0:T(8,128)S(1)} %collective-permute-done.8), channel_id=1, source_target_pairs={{0,1},{1,0},{2,3},{3,2},{4,5},{5,4},{6,7},{7,6},{8,9},{9,8},{10,11... | collective-permute-start | bytes 393224 | tf_op jit(solution)/shard_map/ppermute | solution.py:19
  32.0 5.6 %collective-permute-start.11 = (f32[32,1024]{1,0:T(8,128)S(1)}, f32[32,1024]{1,0:T(8,128)S(1)}, u32[]{:S(2)}, u32[]{:S(2)}) collective-permute-start(f32[32,1024]{1,0:T(8,128)S(1)} %get-tuple-element.74), channel_id=1, source_target_pairs={{0,2},{1,3},{2,0},{3,1},{4,6},{5,7},{6,4},{7,5},{8,10},{9,11},{10,... | collective-permute-start | bytes 393224 | tf_op jit(solution)/shard_map/ppermute | solution.py:19
  33.8 1.4 %collective-permute-start.10 = (f32[32,1024]{1,0:T(8,128)S(1)}, f32[32,1024]{1,0:T(8,128)S(1)}, u32[]{:S(2)}, u32[]{:S(2)}) collective-permute-start(f32[32,1024]{1,0:T(8,128)S(1)} %get-tuple-element.74), channel_id=1, source_target_pairs={{0,1},{1,0},{2,3},{3,2},{4,5},{5,4},{6,7},{7,6},{8,9},{9,8},{10,11... | collective-permute-start | bytes 393224 | tf_op jit(solution)/shard_map/ppermute | solution.py:19
  37.6 1.3 %collective-permute-start.12 = (f32[32,1024]{1,0:T(8,128)S(1)}, f32[32,1024]{1,0:T(8,128)S(1)}, u32[]{:S(2)}, u32[]{:S(2)}) collective-permute-start(f32[32,1024]{1,0:T(8,128)S(1)} %collective-permute-done.11), channel_id=1, source_target_pairs={{0,1},{1,0},{2,3},{3,2},{4,5},{5,4},{6,7},{7,6},{8,9},{9,8},{10,11... | collective-permute-start | bytes 393224 | tf_op jit(solution)/shard_map/ppermute | solution.py:19
  40.4 5.6 %collective-permute-start.14 = (f32[32,1024]{1,0:T(8,128)S(1)}, f32[32,1024]{1,0:T(8,128)S(1)}, u32[]{:S(2)}, u32[]{:S(2)}) collective-permute-start(f32[32,1024]{1,0:T(8,128)S(1)} %get-tuple-element.84), channel_id=1, source_target_pairs={{0,2},{1,3},{2,0},{3,1},{4,6},{5,7},{6,4},{7,5},{8,10},{9,11},{10,... | collective-permute-start | bytes 393224 | tf_op jit(solution)/shard_map/ppermute | solution.py:19
  42.0 1.4 %collective-permute-start.13 = (f32[32,1024]{1,0:T(8,128)S(1)}, f32[32,1024]{1,0:T(8,128)S(1)}, u32[]{:S(2)}, u32[]{:S(2)}) collective-permute-start(f32[32,1024]{1,0:T(8,128)S(1)} %get-tuple-element.84), channel_id=1, source_target_pairs={{0,1},{1,0},{2,3},{3,2},{4,5},{5,4},{6,7},{7,6},{8,9},{9,8},{10,11... | collective-permute-start | bytes 393224 | tf_op jit(solution)/shard_map/ppermute | solution.py:19
  46.0 1.3 %collective-permute-start.15 = (f32[32,1024]{1,0:T(8,128)S(1)}, f32[32,1024]{1,0:T(8,128)S(1)}, u32[]{:S(2)}, u32[]{:S(2)}) collective-permute-start(f32[32,1024]{1,0:T(8,128)S(1)} %collective-permute-done.14), channel_id=1, source_target_pairs={{0,1},{1,0},{2,3},{3,2},{4,5},{5,4},{6,7},{7,6},{8,9},{9,8},{10,11... | collective-permute-start | bytes 393224 | tf_op jit(solution)/shard_map/ppermute | solution.py:19
  50.8 1.2 %collective-permute-start.16 = (f32[32]{0:T(128)S(1)}, f32[32]{0:T(128)S(1)}, u32[]{:S(2)}, u32[]{:S(2)}) collective-permute-start(f32[32]{0:T(128)S(1)} %get-tuple-element.92), channel_id=1, source_target_pairs={{0,1},{1,0},{2,3},{3,2},{4,5},{5,4},{6,7},{7,6},{8,9},{9,8},{10,11... | collective-permute-start | bytes 392 | tf_op jit(solution)/shard_map/ppermute | solution.py:19

commit v21 on v20

--- a/solution.py
+++ b/solution.py
@@ -61,7 +61,7 @@
     feats = scale_ref.shape[0]
     right_ref[...] = operands(part_ref[:feats] * scale_ref[...])[1]
     for ref in copy_ref:
-        ref[...] = part_ref[...]
+        ref[...] = part_ref[: ref.shape[0]]
 
 
 def build_kernel(rows_ref, scale_ref, right_ref, *refs):
@@ -122,12 +122,12 @@
     )(*args)
 
 
-def prepare(part, scale, copy=False):
+def prepare(part, scale, copy=0):
     feats, cols = scale.shape[0], part.shape[1]
     outs = (jax.ShapeDtypeStruct((6 * feats + NORM_ROWS, cols), jnp.bfloat16),)
     if copy:
-        outs += (jax.ShapeDtypeStruct(part.shape, part.dtype),)
-    return call(prepare_kernel, outs, part, scale, flops=10**9, bytes_accessed=feats * cols, transcendentals=0)
+        outs += (jax.ShapeDtypeStruct((copy, cols), part.dtype),)
+    return call(prepare_kernel, outs, part, scale, flops=10**0, bytes_accessed=feats * cols, transcendentals=0)
 
 
 def join(*xs):
@@ -183,7 +183,9 @@
             return pieces
 
         scale = (POINT_SCALE / lengthscale)[:, None]
-        block = lax.optimization_barrier(jnp.concatenate([points, targets, noise_var[None, :]], axis=0))
+        rows = [points, targets, noise_var[None, :]]
+        used = sum(x.shape[0] for x in rows)
+        block = lax.optimization_barrier(jnp.concatenate([*rows, jnp.zeros((-used % 8, width), jnp.float32)], axis=0))
         fence = lax.optimization_barrier
         tile = []
 
@@ -195,15 +197,17 @@
         if len(outer) == 2 and len(inner) == 2:
             far, near, side = outer[0], outer[1], inner[0]
             by_far = swap(block, n, far)
-            right_own, copy = prepare(block, scale, True)
+            right_own, copy = prepare(block, scale, used)
+            near_own = swap(copy, n, near)
             side_own = swap(copy, n, side)
-            by_near = swap(join(block, by_far), n, near)
-            right_far, copy = prepare(by_far, scale, True)
+            near_far = swap(by_far, n, near)
+            right_far, copy = prepare(by_far, scale, used)
             side_far = swap(copy, n, side)
+            right_near, by_near = prepare(join(near_own, near_far[:used]), scale, used)
             last, side_own, side_far = fence((by_near, side_own, side_far))
             side_last = swap(last, n, side)
-            right = join(right_own, right_far, *prepare(by_near, scale))
-            mine = join(block, by_far, by_near)
+            right = join(right_own, right_far, right_near)
+            mine = join(block[:used], by_far[:used], by_near)
             noise, mine = mine[-1:], mine[:-1]
             across = swap(mine, n, 1)
             my_applied = build(mine, noise * mine[feats:])
@@ -221,6 +225,7 @@
             mine = block
             for stride in outer:
                 mine = join(mine, swap(mine, n, stride))
+            mine = mine[:used]
             (right,), noise, first = prepare(mine, scale), mine[-1:], arrivals(mine[:-1])
             my_applied = noise * first[0][feats:]
             for x in first:

time: 52.9 us -> 53 us (level)
  starting transfers between devices: 15.3 us -> 17.8 us
  waiting for transfers between devices: 10.3 us -> 7.81 us
    ppermute x17 -> x18, waiting for transfers between devices: 10.3 us -> 7.81 us  [swap(): return lax.ppermute(x, 'blk', [(i, i ^ stride) for i in range(n)])]
    ppermute x17 -> x18, starting transfers between devices: 15.3 us -> 17.8 us  [swap(): return lax.ppermute(x, 'blk', [(i, i ^ stride) for i in range(n)])]
  transfers between devices with their start and end apart: 17 -> 18, of which waited for: 12 -> 13; matrix products, arithmetic and copies ran while one was open for 18% -> 18% of each run, Pallas kernels for 14% -> 14%
where the time goes in v21:
time: 53 us; the launch traced here: 52.8 us
  starting transfers between devices  17.8 us (34%)
  matrix products  11.5 us (22%)
  Pallas kernels  8.82 us (17%)
  waiting for transfers between devices  7.81 us (15%)
  other arithmetic  5.47 us (10%)
  between operations  1.02 us (2%)
    ppermute x18, starting transfers between devices, swap(): return lax.ppermute(x, 'blk', [(i, i ^ stride) for i in range(n)])  17.8 us
    dot_general x14, matrix products, apply_parts(): jnp.dot(jnp.concatenate([parts, parts], axis=1), piece, preferred_element...  11.5 us
    pallas_call x10, Pallas kernels, call(): pl.pallas_call(kernel, out_shape=outs, in_specs=[whole] * len(args), out_...  8.82 us
    ppermute x18, waiting for transfers between devices, swap(): return lax.ppermute(x, 'blk', [(i, i ^ stride) for i in range(n)])  7.81 us
  transfers between devices with their start and end apart: 18, of which 13 were waited for; matrix products, arithmetic and copies ran while one was open for 18% of the time, Pallas kernels for 14%

profile of v21, /device:TPU:0, one launch (start us, length us, event | category | flops | bytes accessed | tf_op | source)
XLA Modules:
  0.0 52.8 jit_solution(7466204463330392759)
XLA Ops:
  0.7 0.9 %maximum_maximum_fusion.part_ref = f32[72,256]{1,0:T(8,128)S(1)} fusion(f32[1,256]{1,0:T(1,128)} %bitcast.32, f32[32,256]{1,0:T(8,128)} %param.7, f32[32,256]{1,0:T(8,128)} %param.4, f32[72]{0:T(128)S(1)} %pad.117.clone), kind=kLoop, calls=%fused_computation.276 | loop fusion | flops 55296 | bytes 140576 | tf_op jit(solution)/shard_map/concatenate | solution.py:188
  1.6 4.1 %collective-permute-start = (f32[72,256]{1,0:T(8,128)S(1)}, f32[72,256]{1,0:T(8,128)S(1)}, u32[]{:S(2)}, u32[]{:S(2)}) collective-permute-start(f32[72,256]{1,0:T(8,128)S(1)} %maximum_maximum_fusion.part_ref), channel_id=1, source_target_pairs={{0,8},{1,9},{2,10},{3,11},{4,12},{5,13},{6,14},{7,15},{8,0},{9,1},... | collective-permute-start | bytes 221192 | tf_op jit(solution)/shard_map/ppermute | solution.py:19
  6.5 1.6 %collective-permute-start.4 = (f32[65,256]{1,0:T(8,128)S(1)}, f32[65,256]{1,0:T(8,128)S(1)}, u32[]{:S(2)}, u32[]{:S(2)}) collective-permute-start(f32[65,256]{1,0:T(8,128)S(1)} %get-tuple-element.49), channel_id=1, source_target_pairs={{0,2},{1,3},{2,0},{3,1},{4,6},{5,7},{6,4},{7,5},{8,10},{9,11},{10,... | collective-permute-start | bytes 199688 | tf_op jit(solution)/shard_map/ppermute | solution.py:19
  8.1 1.6 %collective-permute-start.1 = (f32[65,256]{1,0:T(8,128)S(1)}, f32[65,256]{1,0:T(8,128)S(1)}, u32[]{:S(2)}, u32[]{:S(2)}) collective-permute-start(f32[65,256]{1,0:T(8,128)S(1)} %get-tuple-element.49), channel_id=1, source_target_pairs={{0,4},{1,5},{2,6},{3,7},{4,0},{5,1},{6,2},{7,3},{8,12},{9,13},{10,... | collective-permute-start | bytes 199688 | tf_op jit(solution)/shard_map/ppermute | solution.py:19
  10.4 1.9 %collective-permute-start.5 = (f32[65,256]{1,0:T(8,128)S(1)}, f32[65,256]{1,0:T(8,128)S(1)}, u32[]{:S(2)}, u32[]{:S(2)}) collective-permute-start(f32[65,256]{1,0:T(8,128)S(1)} %get-tuple-element.51), channel_id=1, source_target_pairs={{0,2},{1,3},{2,0},{3,1},{4,6},{5,7},{6,4},{7,5},{8,10},{9,11},{10,... | collective-permute-start | bytes 199688 | tf_op jit(solution)/shard_map/ppermute | solution.py:19
  12.8 1.2 %collective-permute-done.2 = f32[72,256]{1,0:T(8,128)S(1)} collective-permute-done((f32[72,256]{1,0:T(8,128)S(1)}, f32[72,256]{1,0:T(8,128)S(1)}, u32[]{:S(2)}, u32[]{:S(2)}) %collective-permute-start.2) | collective-permute-done | bytes 73760 | tf_op jit(solution)/shard_map/ppermute | solution.py:19
  14.8 1.8 %collective-permute-start.6 = (f32[65,512]{1,0:T(8,128)S(1)}, f32[65,512]{1,0:T(8,128)S(1)}, u32[]{:S(2)}, u32[]{:S(2)}) collective-permute-start(f32[65,512]{1,0:T(8,128)S(1)} %get-tuple-element.54), channel_id=1, source_target_pairs={{0,2},{1,3},{2,0},{3,1},{4,6},{5,7},{6,4},{7,5},{8,10},{9,11},{10,... | collective-permute-start | bytes 399368 | tf_op jit(solution)/shard_map/ppermute | solution.py:19
  16.8 1.6 %shard_map.62 = (bf16[2048,1024]{1,0:T(8,128)(2,1)S(1)}, f32[32,1024]{1,0:T(8,128)S(1)}) custom-call(f32[32,1024]{1,0:T(8,128)S(1)} %get-tuple-element.121.rows_ref, f32[32,1]{1,0:T(8,128)S(1)} %copy.6.scale_ref, bf16[256,1024]{1,0:T(8,128)(2,1)S(1)} %constant_dynamic-update-slice_fusion.right_ref, f32[32,1024]{1,0:T(8,128)S(1)} %get-tuple-element.122.refs_0_, ...), custom_call_target="tpu_custom_call" | custom-call | flops 872415232 | bytes 4194304 | tf_op jit(solution)/shard_map/pallas_call | solution.py:115
  18.4 1.6 %shard_map.63 = (bf16[2048,1024]{1,0:T(8,128)(2,1)S(1)}, f32[32,1024]{1,0:T(8,128)S(1)}) custom-call(f32[32,1024]{1,0:T(8,128)S(1)} %get-tuple-element.126.rows_ref, f32[32,1]{1,0:T(8,128)S(1)} %copy.6.scale_ref, bf16[256,1024]{1,0:T(8,128)(2,1)S(1)} %constant_dynamic-update-slice_fusion.right_ref, f32[32,1024]{1,0:T(8,128)S(1)} %get-tuple-element.125.refs_0_, ...), custom_call_target="tpu_custom_call" | custom-call | flops 872415232 | bytes 4194304 | tf_op jit(solution)/shard_map/pallas_call | solution.py:115
  20.6 1.6 %shard_map.64 = (bf16[2048,1024]{1,0:T(8,128)(2,1)S(1)}, f32[32,1024]{1,0:T(8,128)S(1)}) custom-call(f32[32,1024]{1,0:T(8,128)S(1)} %get-tuple-element.69.rows_ref.part_ref, f32[32,1]{1,0:T(8,128)S(1)} %copy.6.scale_ref, bf16[256,1024]{1,0:T(8,128)(2,1)S(1)} %constant_dynamic-update-slice_fusion.right_ref, f32[32,1024]{1,0:T(8,128)S(1)} %get-tuple-element.118.refs_0_, ...), custom_call_target="tpu_custom_call" | custom-call | flops 872415232 | bytes 4194304 | tf_op jit(solution)/shard_map/pallas_call | solution.py:115
  22.2 1.6 %shard_map.65 = (bf16[2048,1024]{1,0:T(8,128)(2,1)S(1)}, f32[32,1024]{1,0:T(8,128)S(1)}) custom-call(f32[32,1024]{1,0:T(8,128)S(1)} %get-tuple-element.80.rows_ref, f32[32,1]{1,0:T(8,128)S(1)} %copy.6.scale_ref, bf16[256,1024]{1,0:T(8,128)(2,1)S(1)} %constant_dynamic-update-slice_fusion.right_ref, f32[32,1024]{1,0:T(8,128)S(1)} %get-tuple-element.123.refs_0_, ...), custom_call_target="tpu_custom_call" | custom-call | flops 872415232 | bytes 4194304 | tf_op jit(solution)/shard_map/pallas_call | solution.py:115
  23.9 1.3 %collective-permute-start.9 = (f32[32,1024]{1,0:T(8,128)S(1)}, f32[32,1024]{1,0:T(8,128)S(1)}, u32[]{:S(2)}, u32[]{:S(2)}) collective-permute-start(f32[32,1024]{1,0:T(8,128)S(1)} %get-tuple-element.64), channel_id=1, source_target_pairs={{0,2},{1,3},{2,0},{3,1},{4,6},{5,7},{6,4},{7,5},{8,10},{9,11},{10,... | collective-permute-start | bytes 393224 | tf_op jit(solution)/shard_map/ppermute | solution.py:19
  25.5 0.8 %fusion.6 = f32[96,1024]{1,0:T(8,128)S(1)} fusion(bf16[2048,1024]{1,0:T(8,128)(2,1)S(1)} %get-tuple-element.66, bf16[96,1024]{1,0:T(8,128)(2,1)S(1)} %pad_maximum_fusion.2), kind=kOutput, calls=%fused_computation.27 | convolution fusion | flops 403439616 | bytes 4784128 | tf_op jit(solution)/shard_map/dot_general | solution.py:153
  26.7 0.8 %convolution_add_fusion.6 = f32[96,1024]{1,0:T(8,128)S(1)} fusion(f32[96,1024]{1,0:T(8,128)S(1)} %fusion.6, bf16[2048,1024]{1,0:T(8,128)(2,1)S(1)} %get-tuple-element.67, bf16[32,1024]{1,0:T(8,128)(2,1)S(1)} %get-tuple-element.159, bf16[32,1024]{1,0:T(8,128)(2,1)S(1)} %get-tuple-element.160, bf16[32,1024]{1,0:T(8,128)(2,1)S(1)} %get-tuple-element.158), kind=kOutput, calls=%fused_computation.6 | convolution fusion | flops 405110784 | bytes 5177344 | tf_op jit(solution)/shard_map/dot_general | solution.py:153
  27.6 1.1 %shard_map.67 = bf16[2048,1024]{1,0:T(8,128)(2,1)S(1)} custom-call(f32[32,1024]{1,0:T(8,128)S(1)} %get-tuple-element.69.rows_ref.part_ref, f32[32,1]{1,0:T(8,128)S(1)} %copy.6.scale_ref, bf16[256,1024]{1,0:T(8,128)(2,1)S(1)} %shard_map.66.right_ref), custom_call_target="tpu_custom_call" | custom-call | flops 872415232 | bytes 4194304 | tf_op jit(solution)/shard_map/pallas_call | solution.py:115
  29.4 0.8 %fusion.21 = f32[96,1024]{1,0:T(8,128)S(1)} fusion(bf16[2048,1024]{1,0:T(8,128)(2,1)S(1)} %get-tuple-element.73, bf16[32,1024]{1,0:T(8,128)(2,1)S(1)} %get-tuple-element.156, bf16[32,1024]{1,0:T(8,128)(2,1)S(1)} %get-tuple-element.157, bf16[32,1024]{1,0:T(8,128)(2,1)S(1)} %get-tuple-element.155), kind=kOutput, calls=%fused_computation.42 | convolution fusion | flops 405012480 | bytes 4784128 | tf_op jit(solution)/shard_map/dot_general | solution.py:153
  31.2 0.8 %convolution_add_fusion.5 = f32[96,1024]{1,0:T(8,128)S(1)} fusion(f32[96,1024]{1,0:T(8,128)S(1)} %fusion.21, bf16[2048,1024]{1,0:T(8,128)(2,1)S(1)} %get-tuple-element.77, bf16[32,1024]{1,0:T(8,128)(2,1)S(1)} %get-tuple-element.152, bf16[32,1024]{1,0:T(8,128)(2,1)S(1)} %get-tuple-element.153, bf16[32,1024]{1,0:T(8,128)(2,1)S(1)} %get-tuple-element.151), kind=kOutput, calls=%fused_computation.5 | convolution fusion | flops 405110784 | bytes 5177344 | tf_op jit(solution)/shard_map/dot_general | solution.py:153
  32.1 1.8 %collective-permute-start.12 = (f32[32,1024]{1,0:T(8,128)S(1)}, f32[32,1024]{1,0:T(8,128)S(1)}, u32[]{:S(2)}, u32[]{:S(2)}) collective-permute-start(f32[32,1024]{1,0:T(8,128)S(1)} %get-tuple-element.78), channel_id=1, source_target_pairs={{0,2},{1,3},{2,0},{3,1},{4,6},{5,7},{6,4},{7,5},{8,10},{9,11},{10,... | collective-permute-start | bytes 393224 | tf_op jit(solution)/shard_map/ppermute | solution.py:19
  34.1 0.8 %fusion.44 = f32[96,1024]{1,0:T(8,128)S(1)} fusion(bf16[2048,1024]{1,0:T(8,128)(2,1)S(1)} %get-tuple-element.66, bf16[96,1024]{1,0:T(8,128)(2,1)S(1)} %pad_maximum_fusion.3), kind=kOutput, calls=%fused_computation.65 | convolution fusion | flops 403439616 | bytes 4784128 | tf_op jit(solution)/shard_map/dot_general | solution.py:153
  35.5 1.0 %convolution_add_fusion.4 = f32[96,1024]{1,0:T(8,128)S(1)} fusion(f32[96,1024]{1,0:T(8,128)S(1)} %fusion.44, bf16[2048,1024]{1,0:T(8,128)(2,1)S(1)} %get-tuple-element.67, bf16[32,1024]{1,0:T(8,128)(2,1)S(1)} %get-tuple-element.147, bf16[32,1024]{1,0:T(8,128)(2,1)S(1)} %get-tuple-element.148, bf16[32,1024]{1,0:T(8,128)(2,1)S(1)} %get-tuple-element.146), kind=kOutput, calls=%fused_computation.4 | convolution fusion | flops 405110784 | bytes 5177344 | tf_op jit(solution)/shard_map/dot_general | solution.py:153
  36.5 1.1 %shard_map.68 = bf16[2048,1024]{1,0:T(8,128)(2,1)S(1)} custom-call(f32[32,1024]{1,0:T(8,128)S(1)} %get-tuple-element.80.rows_ref, f32[32,1]{1,0:T(8,128)S(1)} %copy.6.scale_ref, bf16[256,1024]{1,0:T(8,128)(2,1)S(1)} %shard_map.66.right_ref), custom_call_target="tpu_custom_call" | custom-call | flops 872415232 | bytes 4194304 | tf_op jit(solution)/shard_map/pallas_call | solution.py:115
  37.8 0.8 %fusion.59 = f32[96,1024]{1,0:T(8,128)S(1)} fusion(bf16[2048,1024]{1,0:T(8,128)(2,1)S(1)} %get-tuple-element.73, bf16[32,1024]{1,0:T(8,128)(2,1)S(1)} %get-tuple-element.144, bf16[32,1024]{1,0:T(8,128)(2,1)S(1)} %get-tuple-element.145, bf16[32,1024]{1,0:T(8,128)(2,1)S(1)} %get-tuple-element.143), kind=kOutput, calls=%fused_computation.80 | convolution fusion | flops 405012480 | bytes 4784128 | tf_op jit(solution)/shard_map/dot_general | solution.py:153
  39.5 0.8 %convolution_add_fusion.3 = f32[96,1024]{1,0:T(8,128)S(1)} fusion(f32[96,1024]{1,0:T(8,128)S(1)} %fusion.59, bf16[2048,1024]{1,0:T(8,128)(2,1)S(1)} %get-tuple-element.77, bf16[32,1024]{1,0:T(8,128)(2,1)S(1)} %get-tuple-element.140, bf16[32,1024]{1,0:T(8,128)(2,1)S(1)} %get-tuple-element.141, bf16[32,1024]{1,0:T(8,128)(2,1)S(1)} %get-tuple-element.139), kind=kOutput, calls=%fused_computation.3 | convolution fusion | flops 405110784 | bytes 5177344 | tf_op jit(solution)/shard_map/dot_general | solution.py:153
  40.5 1.8 %collective-permute-start.15 = (f32[32,1024]{1,0:T(8,128)S(1)}, f32[32,1024]{1,0:T(8,128)S(1)}, u32[]{:S(2)}, u32[]{:S(2)}) collective-permute-start(f32[32,1024]{1,0:T(8,128)S(1)} %get-tuple-element.88), channel_id=1, source_target_pairs={{0,2},{1,3},{2,0},{3,1},{4,6},{5,7},{6,4},{7,5},{8,10},{9,11},{10,... | collective-permute-start | bytes 393224 | tf_op jit(solution)/shard_map/ppermute | solution.py:19
  42.5 0.8 %fusion.82 = f32[96,1024]{1,0:T(8,128)S(1)} fusion(bf16[2048,1024]{1,0:T(8,128)(2,1)S(1)} %get-tuple-element.66, bf16[96,1024]{1,0:T(8,128)(2,1)S(1)} %pad_maximum_fusion.4), kind=kOutput, calls=%fused_computation.103 | convolution fusion | flops 403439616 | bytes 4784128 | tf_op jit(solution)/shard_map/dot_general | solution.py:153
  43.7 0.8 %convolution_add_fusion.2 = f32[96,1024]{1,0:T(8,128)S(1)} fusion(f32[96,1024]{1,0:T(8,128)S(1)} %fusion.82, bf16[2048,1024]{1,0:T(8,128)(2,1)S(1)} %get-tuple-element.67, bf16[32,1024]{1,0:T(8,128)(2,1)S(1)} %get-tuple-element.135, bf16[32,1024]{1,0:T(8,128)(2,1)S(1)} %get-tuple-element.136, bf16[32,1024]{1,0:T(8,128)(2,1)S(1)} %get-tuple-element.134), kind=kOutput, calls=%fused_computation.2 | convolution fusion | flops 405110784 | bytes 5177344 | tf_op jit(solution)/shard_map/dot_general | solution.py:153
  44.6 1.6 %collective-permute-done.15 = f32[32,1024]{1,0:T(8,128)S(1)} collective-permute-done((f32[32,1024]{1,0:T(8,128)S(1)}, f32[32,1024]{1,0:T(8,128)S(1)}, u32[]{:S(2)}, u32[]{:S(2)}) %collective-permute-start.15) | collective-permute-done | bytes 131104 | tf_op jit(solution)/shard_map/ppermute | solution.py:19
  46.2 0.8 %fusion.97 = f32[96,1024]{1,0:T(8,128)S(1)} fusion(bf16[2048,1024]{1,0:T(8,128)(2,1)S(1)} %get-tuple-element.73, bf16[32,1024]{1,0:T(8,128)(2,1)S(1)} %get-tuple-element.132, bf16[32,1024]{1,0:T(8,128)(2,1)S(1)} %get-tuple-element.133, bf16[32,1024]{1,0:T(8,128)(2,1)S(1)} %get-tuple-element.131), kind=kOutput, calls=%fused_computation.118 | convolution fusion | flops 405012480 | bytes 4784128 | tf_op jit(solution)/shard_map/dot_general | solution.py:153
  48.1 0.8 %convolution_add_fusion.1 = f32[96,1024]{1,0:T(8,128)S(1)} fusion(f32[96,1024]{1,0:T(8,128)S(1)} %fusion.97, bf16[2048,1024]{1,0:T(8,128)(2,1)S(1)} %get-tuple-element.77, bf16[32,1024]{1,0:T(8,128)(2,1)S(1)} %get-tuple-element.128, bf16[32,1024]{1,0:T(8,128)(2,1)S(1)} %get-tuple-element.129, bf16[32,1024]{1,0:T(8,128)(2,1)S(1)} %get-tuple-element.127), kind=kOutput, calls=%fused_computation.1 | convolution fusion | flops 405110784 | bytes 5177344 | tf_op jit(solution)/shard_map/dot_general | solution.py:153
  48.9 0.8 %fusion.120 = f32[96,1024]{1,0:T(8,128)S(1)} fusion(bf16[2048,1024]{1,0:T(8,128)(2,1)S(1)} %shard_map.67, bf16[32,1024]{1,0:T(8,128)(2,1)S(1)} %get-tuple-element.114, bf16[32,1024]{1,0:T(8,128)(2,1)S(1)} %get-tuple-element.113, bf16[32,1024]{1,0:T(8,128)(2,1)S(1)} %get-tuple-element.117), kind=kOutput, calls=%fused_computation.141 | convolution fusion | flops 405012480 | bytes 4784128 | tf_op jit(solution)/shard_map/dot_general | solution.py:153
  49.7 0.8 %convolution_add_fusion = f32[96,1024]{1,0:T(8,128)S(1)} fusion(f32[96,1024]{1,0:T(8,128)S(1)} %fusion.120, bf16[2048,1024]{1,0:T(8,128)(2,1)S(1)} %shard_map.68, bf16[32,1024]{1,0:T(8,128)(2,1)S(1)} %get-tuple-element.115, bf16[32,1024]{1,0:T(8,128)(2,1)S(1)} %get-tuple-element.116, bf16[32,1024]{1,0:T(8,128)(2,1)S(1)} %get-tuple-element.112), kind=kOutput, calls=%fused_computation | convolution fusion | flops 405110784 | bytes 5177344 | tf_op jit(solution)/shard_map/dot_general | solution.py:153
  51.1 0.9 %collective-permute-done.17 = f32[32]{0:T(128)S(1)} collective-permute-done((f32[32]{0:T(128)S(1)}, f32[32]{0:T(128)S(1)}, u32[]{:S(2)}, u32[]{:S(2)}) %collective-permute-start.17) | collective-permute-done | bytes 160 | tf_op jit(solution)/shard_map/ppermute | solution.py:19
  (88 shorter events, 11.5 us)
Async XLA Ops:
  1.6 8.1 %collective-permute-start = (f32[72,256]{1,0:T(8,128)S(1)}, f32[72,256]{1,0:T(8,128)S(1)}, u32[]{:S(2)}, u32[]{:S(2)}) collective-permute-start(f32[72,256]{1,0:T(8,128)S(1)} %maximum_maximum_fusion.part_ref), channel_id=1, source_target_pairs={{0,8},{1,9},{2,10},{3,11},{4,12},{5,13},{6,14},{7,15},{8,0},{9,1},... | collective-permute-start | bytes 221192 | tf_op jit(solution)/shard_map/ppermute | solution.py:19
  6.5 7.7 %collective-permute-start.4 = (f32[65,256]{1,0:T(8,128)S(1)}, f32[65,256]{1,0:T(8,128)S(1)}, u32[]{:S(2)}, u32[]{:S(2)}) collective-permute-start(f32[65,256]{1,0:T(8,128)S(1)} %get-tuple-element.49), channel_id=1, source_target_pairs={{0,2},{1,3},{2,0},{3,1},{4,6},{5,7},{6,4},{7,5},{8,10},{9,11},{10,... | collective-permute-start | bytes 199688 | tf_op jit(solution)/shard_map/ppermute | solution.py:19
  8.1 4.7 %collective-permute-start.1 = (f32[65,256]{1,0:T(8,128)S(1)}, f32[65,256]{1,0:T(8,128)S(1)}, u32[]{:S(2)}, u32[]{:S(2)}) collective-permute-start(f32[65,256]{1,0:T(8,128)S(1)} %get-tuple-element.49), channel_id=1, source_target_pairs={{0,4},{1,5},{2,6},{3,7},{4,0},{5,1},{6,2},{7,3},{8,12},{9,13},{10,... | collective-permute-start | bytes 199688 | tf_op jit(solution)/shard_map/ppermute | solution.py:19
  9.7 4.4 %collective-permute-start.2 = (f32[72,256]{1,0:T(8,128)S(1)}, f32[72,256]{1,0:T(8,128)S(1)}, u32[]{:S(2)}, u32[]{:S(2)}) collective-permute-start(f32[72,256]{1,0:T(8,128)S(1)} %collective-permute-done.part_ref), channel_id=1, source_target_pairs={{0,4},{1,5},{2,6},{3,7},{4,0},{5,1},{6,2},{7,3},{8,12},{9,13},{10,... | collective-permute-start | bytes 221192 | tf_op jit(solution)/shard_map/ppermute | solution.py:19
  10.4 4.4 %collective-permute-start.5 = (f32[65,256]{1,0:T(8,128)S(1)}, f32[65,256]{1,0:T(8,128)S(1)}, u32[]{:S(2)}, u32[]{:S(2)}) collective-permute-start(f32[65,256]{1,0:T(8,128)S(1)} %get-tuple-element.51), channel_id=1, source_target_pairs={{0,2},{1,3},{2,0},{3,1},{4,6},{5,7},{6,4},{7,5},{8,10},{9,11},{10,... | collective-permute-start | bytes 199688 | tf_op jit(solution)/shard_map/ppermute | solution.py:19
  14.8 5.2 %collective-permute-start.6 = (f32[65,512]{1,0:T(8,128)S(1)}, f32[65,512]{1,0:T(8,128)S(1)}, u32[]{:S(2)}, u32[]{:S(2)}) collective-permute-start(f32[65,512]{1,0:T(8,128)S(1)} %get-tuple-element.54), channel_id=1, source_target_pairs={{0,2},{1,3},{2,0},{3,1},{4,6},{5,7},{6,4},{7,5},{8,10},{9,11},{10,... | collective-permute-start | bytes 399368 | tf_op jit(solution)/shard_map/ppermute | solution.py:19
  16.7 1.7 %collective-permute-start.3 = (f32[64,1024]{1,0:T(8,128)S(1)}, f32[64,1024]{1,0:T(8,128)S(1)}, u32[]{:S(2)}, u32[]{:S(2)}) collective-permute-start(f32[64,1024]{1,0:T(8,128)S(1)} %slice.225), channel_id=1, source_target_pairs={{0,1},{1,0},{2,3},{3,2},{4,5},{5,4},{6,7},{7,6},{8,9},{9,8},{10,11... | collective-permute-start | bytes 786440 | tf_op jit(solution)/shard_map/ppermute | solution.py:19
  20.0 2.2 %collective-permute-start.7 = (f32[64,1024]{1,0:T(8,128)S(1)}, f32[64,1024]{1,0:T(8,128)S(1)}, u32[]{:S(2)}, u32[]{:S(2)}) collective-permute-start(f32[64,1024]{1,0:T(8,128)S(1)} %slice.230), channel_id=1, source_target_pairs={{0,1},{1,0},{2,3},{3,2},{4,5},{5,4},{6,7},{7,6},{8,9},{9,8},{10,11... | collective-permute-start | bytes 786440 | tf_op jit(solution)/shard_map/ppermute | solution.py:19
  23.9 5.5 %collective-permute-start.9 = (f32[32,1024]{1,0:T(8,128)S(1)}, f32[32,1024]{1,0:T(8,128)S(1)}, u32[]{:S(2)}, u32[]{:S(2)}) collective-permute-start(f32[32,1024]{1,0:T(8,128)S(1)} %get-tuple-element.64), channel_id=1, source_target_pairs={{0,2},{1,3},{2,0},{3,1},{4,6},{5,7},{6,4},{7,5},{8,10},{9,11},{10,... | collective-permute-start | bytes 393224 | tf_op jit(solution)/shard_map/ppermute | solution.py:19
  25.2 1.4 %collective-permute-start.8 = (f32[32,1024]{1,0:T(8,128)S(1)}, f32[32,1024]{1,0:T(8,128)S(1)}, u32[]{:S(2)}, u32[]{:S(2)}) collective-permute-start(f32[32,1024]{1,0:T(8,128)S(1)} %get-tuple-element.64), channel_id=1, source_target_pairs={{0,1},{1,0},{2,3},{3,2},{4,5},{5,4},{6,7},{7,6},{8,9},{9,8},{10,11... | collective-permute-start | bytes 393224 | tf_op jit(solution)/shard_map/ppermute | solution.py:19
  29.4 1.3 %collective-permute-start.10 = (f32[32,1024]{1,0:T(8,128)S(1)}, f32[32,1024]{1,0:T(8,128)S(1)}, u32[]{:S(2)}, u32[]{:S(2)}) collective-permute-start(f32[32,1024]{1,0:T(8,128)S(1)} %collective-permute-done.9), channel_id=1, source_target_pairs={{0,1},{1,0},{2,3},{3,2},{4,5},{5,4},{6,7},{7,6},{8,9},{9,8},{10,11... | collective-permute-start | bytes 393224 | tf_op jit(solution)/shard_map/ppermute | solution.py:19
  32.1 5.6 %collective-permute-start.12 = (f32[32,1024]{1,0:T(8,128)S(1)}, f32[32,1024]{1,0:T(8,128)S(1)}, u32[]{:S(2)}, u32[]{:S(2)}) collective-permute-start(f32[32,1024]{1,0:T(8,128)S(1)} %get-tuple-element.78), channel_id=1, source_target_pairs={{0,2},{1,3},{2,0},{3,1},{4,6},{5,7},{6,4},{7,5},{8,10},{9,11},{10,... | collective-permute-start | bytes 393224 | tf_op jit(solution)/shard_map/ppermute | solution.py:19
  34.1 1.4 %collective-permute-start.11 = (f32[32,1024]{1,0:T(8,128)S(1)}, f32[32,1024]{1,0:T(8,128)S(1)}, u32[]{:S(2)}, u32[]{:S(2)}) collective-permute-start(f32[32,1024]{1,0:T(8,128)S(1)} %get-tuple-element.78), channel_id=1, source_target_pairs={{0,1},{1,0},{2,3},{3,2},{4,5},{5,4},{6,7},{7,6},{8,9},{9,8},{10,11... | collective-permute-start | bytes 393224 | tf_op jit(solution)/shard_map/ppermute | solution.py:19
  37.7 1.3 %collective-permute-start.13 = (f32[32,1024]{1,0:T(8,128)S(1)}, f32[32,1024]{1,0:T(8,128)S(1)}, u32[]{:S(2)}, u32[]{:S(2)}) collective-permute-start(f32[32,1024]{1,0:T(8,128)S(1)} %collective-permute-done.12), channel_id=1, source_target_pairs={{0,1},{1,0},{2,3},{3,2},{4,5},{5,4},{6,7},{7,6},{8,9},{9,8},{10,11... | collective-permute-start | bytes 393224 | tf_op jit(solution)/shard_map/ppermute | solution.py:19
  40.5 5.6 %collective-permute-start.15 = (f32[32,1024]{1,0:T(8,128)S(1)}, f32[32,1024]{1,0:T(8,128)S(1)}, u32[]{:S(2)}, u32[]{:S(2)}) collective-permute-start(f32[32,1024]{1,0:T(8,128)S(1)} %get-tuple-element.88), channel_id=1, source_target_pairs={{0,2},{1,3},{2,0},{3,1},{4,6},{5,7},{6,4},{7,5},{8,10},{9,11},{10,... | collective-permute-start | bytes 393224 | tf_op jit(solution)/shard_map/ppermute | solution.py:19
  42.3 1.4 %collective-permute-start.14 = (f32[32,1024]{1,0:T(8,128)S(1)}, f32[32,1024]{1,0:T(8,128)S(1)}, u32[]{:S(2)}, u32[]{:S(2)}) collective-permute-start(f32[32,1024]{1,0:T(8,128)S(1)} %get-tuple-element.88), channel_id=1, source_target_pairs={{0,1},{1,0},{2,3},{3,2},{4,5},{5,4},{6,7},{7,6},{8,9},{9,8},{10,11... | collective-permute-start | bytes 393224 | tf_op jit(solution)/shard_map/ppermute | solution.py:19
  46.1 1.3 %collective-permute-start.16 = (f32[32,1024]{1,0:T(8,128)S(1)}, f32[32,1024]{1,0:T(8,128)S(1)}, u32[]{:S(2)}, u32[]{:S(2)}) collective-permute-start(f32[32,1024]{1,0:T(8,128)S(1)} %collective-permute-done.15), channel_id=1, source_target_pairs={{0,1},{1,0},{2,3},{3,2},{4,5},{5,4},{6,7},{7,6},{8,9},{9,8},{10,11... | collective-permute-start | bytes 393224 | tf_op jit(solution)/shard_map/ppermute | solution.py:19
  50.9 1.2 %collective-permute-start.17 = (f32[32]{0:T(128)S(1)}, f32[32]{0:T(128)S(1)}, u32[]{:S(2)}, u32[]{:S(2)}) collective-permute-start(f32[32]{0:T(128)S(1)} %get-tuple-element.96), channel_id=1, source_target_pairs={{0,1},{1,0},{2,3},{3,2},{4,5},{5,4},{6,7},{7,6},{8,9},{9,8},{10,11... | collective-permute-start | bytes 392 | tf_op jit(solution)/shard_map/ppermute | solution.py:19

commit v22 on v21

--- a/solution.py
+++ b/solution.py
@@ -183,9 +183,9 @@
             return pieces
 
         scale = (POINT_SCALE / lengthscale)[:, None]
-        rows = [points, targets, noise_var[None, :]]
-        used = sum(x.shape[0] for x in rows)
-        block = lax.optimization_barrier(jnp.concatenate([*rows, jnp.zeros((-used % 8, width), jnp.float32)], axis=0))
+        used = feats + probes + 1
+        rest = jnp.broadcast_to(noise_var[None, :], (1 + -used % 8, width))
+        block = lax.optimization_barrier(jnp.concatenate([points, targets, rest], axis=0))
         fence = lax.optimization_barrier
         tile = []
 
@@ -204,7 +204,7 @@
             right_far, copy = prepare(by_far, scale, used)
             side_far = swap(copy, n, side)
             right_near, by_near = prepare(join(near_own, near_far[:used]), scale, used)
-            last, side_own, side_far = fence((by_near, side_own, side_far))
+            last, side_own = fence((by_near, side_own))
             side_last = swap(last, n, side)
             right = join(right_own, right_far, right_near)
             mine = join(block[:used], by_far[:used], by_near)
@@ -212,7 +212,7 @@
             across = swap(mine, n, 1)
             my_applied = build(mine, noise * mine[feats:])
             my_applied = build(across, my_applied)
-            side_last, my_applied = fence((side_last, my_applied))
+            side_last, side_far, my_applied = fence((side_last, side_far, my_applied))
             beside = join(side_own, side_far, side_last)
             noise_beside, beside = beside[-1:], beside[:-1]
             beside_across = swap(beside, n, 1)

time: 53 us -> 52.9 us (level)
  starting transfers between devices: 17.8 us -> 16.4 us
  waiting for transfers between devices: 7.81 us -> 8.63 us
  local copies, waits for them, and re-layouts: 0.35 us -> 0.95 us
    ppermute x18, starting transfers between devices: 17.8 us -> 16.4 us  [swap(): return lax.ppermute(x, 'blk', [(i, i ^ stride) for i in range(n)])]
    ppermute x18, waiting for transfers between devices: 7.81 us -> 8.63 us  [swap(): return lax.ppermute(x, 'blk', [(i, i ^ stride) for i in range(n)])]
    broadcast_in_dim x1, local copies, waits for them, and re-layouts: 0.01 us -> 0.68 us  [body(): rest = jnp.broadcast_to(noise_var[None, :], (1 + -used % 8, width))]
where the time goes in v22:
time: 52.9 us; the launch traced here: 52.7 us
  starting transfers between devices  16.4 us (31%)
  matrix products  11.5 us (22%)
  Pallas kernels  8.82 us (17%)
  waiting for transfers between devices  8.63 us (16%)
  other arithmetic  5.39 us (10%)
  between operations  1 us (2%)
  local copies, waits for them, and re-layouts  0.95 us (2%)
    ppermute x18, starting transfers between devices, swap(): return lax.ppermute(x, 'blk', [(i, i ^ stride) for i in range(n)])  16.4 us
    dot_general x14, matrix products, apply_parts(): jnp.dot(jnp.concatenate([parts, parts], axis=1), piece, preferred_element...  11.5 us
    pallas_call x10, Pallas kernels, call(): pl.pallas_call(kernel, out_shape=outs, in_specs=[whole] * len(args), out_...  8.82 us
    ppermute x18, waiting for transfers between devices, swap(): return lax.ppermute(x, 'blk', [(i, i ^ stride) for i in range(n)])  8.63 us
  transfers between devices with their start and end apart: 18, of which 13 were waited for; matrix products, arithmetic and copies ran while one was open for 18% of the time, Pallas kernels for 14%

profile of v22, /device:TPU:0, one launch (start us, length us, event | category | flops | bytes accessed | tf_op | source)
XLA Modules:
  0.0 52.7 jit_solution(14361100510424923936)
XLA Ops:
  2.1 4.0 %collective-permute-start = (f32[72,256]{1,0:T(8,128)S(1)}, f32[72,256]{1,0:T(8,128)S(1)}, u32[]{:S(2)}, u32[]{:S(2)}) collective-permute-start(f32[72,256]{1,0:T(8,128)S(1)} %pad_maximum_fusion.6.part_ref), channel_id=1, source_target_pairs={{0,8},{1,9},{2,10},{3,11},{4,12},{5,13},{6,14},{7,15},{8,0},{9,1},... | collective-permute-start | bytes 221192 | tf_op jit(solution)/shard_map/ppermute | solution.py:19
  7.0 1.6 %collective-permute-start.4 = (f32[65,256]{1,0:T(8,128)S(1)}, f32[65,256]{1,0:T(8,128)S(1)}, u32[]{:S(2)}, u32[]{:S(2)}) collective-permute-start(f32[65,256]{1,0:T(8,128)S(1)} %get-tuple-element.49), channel_id=1, source_target_pairs={{0,2},{1,3},{2,0},{3,1},{4,6},{5,7},{6,4},{7,5},{8,10},{9,11},{10,... | collective-permute-start | bytes 199688 | tf_op jit(solution)/shard_map/ppermute | solution.py:19
  8.6 1.6 %collective-permute-start.1 = (f32[65,256]{1,0:T(8,128)S(1)}, f32[65,256]{1,0:T(8,128)S(1)}, u32[]{:S(2)}, u32[]{:S(2)}) collective-permute-start(f32[65,256]{1,0:T(8,128)S(1)} %get-tuple-element.49), channel_id=1, source_target_pairs={{0,4},{1,5},{2,6},{3,7},{4,0},{5,1},{6,2},{7,3},{8,12},{9,13},{10,... | collective-permute-start | bytes 199688 | tf_op jit(solution)/shard_map/ppermute | solution.py:19
  10.9 1.9 %collective-permute-start.6 = (f32[65,256]{1,0:T(8,128)S(1)}, f32[65,256]{1,0:T(8,128)S(1)}, u32[]{:S(2)}, u32[]{:S(2)}) collective-permute-start(f32[65,256]{1,0:T(8,128)S(1)} %get-tuple-element.53), channel_id=1, source_target_pairs={{0,2},{1,3},{2,0},{3,1},{4,6},{5,7},{6,4},{7,5},{8,10},{9,11},{10,... | collective-permute-start | bytes 199688 | tf_op jit(solution)/shard_map/ppermute | solution.py:19
  13.3 1.2 %collective-permute-done.2 = f32[72,256]{1,0:T(8,128)S(1)} collective-permute-done((f32[72,256]{1,0:T(8,128)S(1)}, f32[72,256]{1,0:T(8,128)S(1)}, u32[]{:S(2)}, u32[]{:S(2)}) %collective-permute-start.2) | collective-permute-done | bytes 73760 | tf_op jit(solution)/shard_map/ppermute | solution.py:19
  14.7 1.5 %collective-permute-start.5 = (f32[65,512]{1,0:T(8,128)S(1)}, f32[65,512]{1,0:T(8,128)S(1)}, u32[]{:S(2)}, u32[]{:S(2)}) collective-permute-start(f32[65,512]{1,0:T(8,128)S(1)} %get-tuple-element.52), channel_id=1, source_target_pairs={{0,2},{1,3},{2,0},{3,1},{4,6},{5,7},{6,4},{7,5},{8,10},{9,11},{10,... | collective-permute-start | bytes 399368 | tf_op jit(solution)/shard_map/ppermute | solution.py:19
  16.3 1.6 %shard_map.62 = (bf16[2048,1024]{1,0:T(8,128)(2,1)S(1)}, f32[32,1024]{1,0:T(8,128)S(1)}) custom-call(f32[32,1024]{1,0:T(8,128)S(1)} %get-tuple-element.121.rows_ref, f32[32,1]{1,0:T(8,128)S(1)} %copy.6.scale_ref, bf16[256,1024]{1,0:T(8,128)(2,1)S(1)} %constant_dynamic-update-slice_fusion.right_ref, f32[32,1024]{1,0:T(8,128)S(1)} %get-tuple-element.122.refs_0_, ...), custom_call_target="tpu_custom_call" | custom-call | flops 872415232 | bytes 4194304 | tf_op jit(solution)/shard_map/pallas_call | solution.py:115
  18.0 1.6 %shard_map.63 = (bf16[2048,1024]{1,0:T(8,128)(2,1)S(1)}, f32[32,1024]{1,0:T(8,128)S(1)}) custom-call(f32[32,1024]{1,0:T(8,128)S(1)} %get-tuple-element.126.rows_ref, f32[32,1]{1,0:T(8,128)S(1)} %copy.6.scale_ref, bf16[256,1024]{1,0:T(8,128)(2,1)S(1)} %constant_dynamic-update-slice_fusion.right_ref, f32[32,1024]{1,0:T(8,128)S(1)} %get-tuple-element.125.refs_0_, ...), custom_call_target="tpu_custom_call" | custom-call | flops 872415232 | bytes 4194304 | tf_op jit(solution)/shard_map/pallas_call | solution.py:115
  20.2 1.6 %shard_map.64 = (bf16[2048,1024]{1,0:T(8,128)(2,1)S(1)}, f32[32,1024]{1,0:T(8,128)S(1)}) custom-call(f32[32,1024]{1,0:T(8,128)S(1)} %get-tuple-element.69.rows_ref.part_ref, f32[32,1]{1,0:T(8,128)S(1)} %copy.6.scale_ref, bf16[256,1024]{1,0:T(8,128)(2,1)S(1)} %constant_dynamic-update-slice_fusion.right_ref, f32[32,1024]{1,0:T(8,128)S(1)} %get-tuple-element.118.refs_0_, ...), custom_call_target="tpu_custom_call" | custom-call | flops 872415232 | bytes 4194304 | tf_op jit(solution)/shard_map/pallas_call | solution.py:115
  21.8 1.6 %shard_map.65 = (bf16[2048,1024]{1,0:T(8,128)(2,1)S(1)}, f32[32,1024]{1,0:T(8,128)S(1)}) custom-call(f32[32,1024]{1,0:T(8,128)S(1)} %get-tuple-element.80.rows_ref, f32[32,1]{1,0:T(8,128)S(1)} %copy.6.scale_ref, bf16[256,1024]{1,0:T(8,128)(2,1)S(1)} %constant_dynamic-update-slice_fusion.right_ref, f32[32,1024]{1,0:T(8,128)S(1)} %get-tuple-element.123.refs_0_, ...), custom_call_target="tpu_custom_call" | custom-call | flops 872415232 | bytes 4194304 | tf_op jit(solution)/shard_map/pallas_call | solution.py:115
  23.5 1.3 %collective-permute-start.9 = (f32[32,1024]{1,0:T(8,128)S(1)}, f32[32,1024]{1,0:T(8,128)S(1)}, u32[]{:S(2)}, u32[]{:S(2)}) collective-permute-start(f32[32,1024]{1,0:T(8,128)S(1)} %get-tuple-element.64), channel_id=1, source_target_pairs={{0,2},{1,3},{2,0},{3,1},{4,6},{5,7},{6,4},{7,5},{8,10},{9,11},{10,... | collective-permute-start | bytes 393224 | tf_op jit(solution)/shard_map/ppermute | solution.py:19
  25.1 0.8 %fusion.6 = f32[96,1024]{1,0:T(8,128)S(1)} fusion(bf16[2048,1024]{1,0:T(8,128)(2,1)S(1)} %get-tuple-element.66, bf16[96,1024]{1,0:T(8,128)(2,1)S(1)} %pad_maximum_fusion.2), kind=kOutput, calls=%fused_computation.27 | convolution fusion | flops 403439616 | bytes 4784128 | tf_op jit(solution)/shard_map/dot_general | solution.py:153
  26.3 0.8 %convolution_add_fusion.6 = f32[96,1024]{1,0:T(8,128)S(1)} fusion(f32[96,1024]{1,0:T(8,128)S(1)} %fusion.6, bf16[2048,1024]{1,0:T(8,128)(2,1)S(1)} %get-tuple-element.67, bf16[32,1024]{1,0:T(8,128)(2,1)S(1)} %get-tuple-element.159, bf16[32,1024]{1,0:T(8,128)(2,1)S(1)} %get-tuple-element.160, bf16[32,1024]{1,0:T(8,128)(2,1)S(1)} %get-tuple-element.158), kind=kOutput, calls=%fused_computation.6 | convolution fusion | flops 405110784 | bytes 5177344 | tf_op jit(solution)/shard_map/dot_general | solution.py:153
  27.2 1.1 %shard_map.67 = bf16[2048,1024]{1,0:T(8,128)(2,1)S(1)} custom-call(f32[32,1024]{1,0:T(8,128)S(1)} %get-tuple-element.69.rows_ref.part_ref, f32[32,1]{1,0:T(8,128)S(1)} %copy.6.scale_ref, bf16[256,1024]{1,0:T(8,128)(2,1)S(1)} %shard_map.66.right_ref), custom_call_target="tpu_custom_call" | custom-call | flops 872415232 | bytes 4194304 | tf_op jit(solution)/shard_map/pallas_call | solution.py:115
  28.3 1.0 %collective-permute-done.9 = f32[32,1024]{1,0:T(8,128)S(1)} collective-permute-done((f32[32,1024]{1,0:T(8,128)S(1)}, f32[32,1024]{1,0:T(8,128)S(1)}, u32[]{:S(2)}, u32[]{:S(2)}) %collective-permute-start.9) | collective-permute-done | bytes 131104 | tf_op jit(solution)/shard_map/ppermute | solution.py:19
  29.3 0.8 %fusion.21 = f32[96,1024]{1,0:T(8,128)S(1)} fusion(bf16[2048,1024]{1,0:T(8,128)(2,1)S(1)} %get-tuple-element.73, bf16[32,1024]{1,0:T(8,128)(2,1)S(1)} %get-tuple-element.156, bf16[32,1024]{1,0:T(8,128)(2,1)S(1)} %get-tuple-element.157, bf16[32,1024]{1,0:T(8,128)(2,1)S(1)} %get-tuple-element.155), kind=kOutput, calls=%fused_computation.42 | convolution fusion | flops 405012480 | bytes 4784128 | tf_op jit(solution)/shard_map/dot_general | solution.py:153
  31.1 0.8 %convolution_add_fusion.5 = f32[96,1024]{1,0:T(8,128)S(1)} fusion(f32[96,1024]{1,0:T(8,128)S(1)} %fusion.21, bf16[2048,1024]{1,0:T(8,128)(2,1)S(1)} %get-tuple-element.77, bf16[32,1024]{1,0:T(8,128)(2,1)S(1)} %get-tuple-element.152, bf16[32,1024]{1,0:T(8,128)(2,1)S(1)} %get-tuple-element.153, bf16[32,1024]{1,0:T(8,128)(2,1)S(1)} %get-tuple-element.151), kind=kOutput, calls=%fused_computation.5 | convolution fusion | flops 405110784 | bytes 5177344 | tf_op jit(solution)/shard_map/dot_general | solution.py:153
  32.0 1.5 %collective-permute-start.12 = (f32[32,1024]{1,0:T(8,128)S(1)}, f32[32,1024]{1,0:T(8,128)S(1)}, u32[]{:S(2)}, u32[]{:S(2)}) collective-permute-start(f32[32,1024]{1,0:T(8,128)S(1)} %get-tuple-element.78), channel_id=1, source_target_pairs={{0,2},{1,3},{2,0},{3,1},{4,6},{5,7},{6,4},{7,5},{8,10},{9,11},{10,... | collective-permute-start | bytes 393224 | tf_op jit(solution)/shard_map/ppermute | solution.py:19
  33.7 0.8 %fusion.44 = f32[96,1024]{1,0:T(8,128)S(1)} fusion(bf16[2048,1024]{1,0:T(8,128)(2,1)S(1)} %get-tuple-element.66, bf16[96,1024]{1,0:T(8,128)(2,1)S(1)} %pad_maximum_fusion.3), kind=kOutput, calls=%fused_computation.65 | convolution fusion | flops 403439616 | bytes 4784128 | tf_op jit(solution)/shard_map/dot_general | solution.py:153
  35.1 1.0 %convolution_add_fusion.4 = f32[96,1024]{1,0:T(8,128)S(1)} fusion(f32[96,1024]{1,0:T(8,128)S(1)} %fusion.44, bf16[2048,1024]{1,0:T(8,128)(2,1)S(1)} %get-tuple-element.67, bf16[32,1024]{1,0:T(8,128)(2,1)S(1)} %get-tuple-element.147, bf16[32,1024]{1,0:T(8,128)(2,1)S(1)} %get-tuple-element.148, bf16[32,1024]{1,0:T(8,128)(2,1)S(1)} %get-tuple-element.146), kind=kOutput, calls=%fused_computation.4 | convolution fusion | flops 405110784 | bytes 5177344 | tf_op jit(solution)/shard_map/dot_general | solution.py:153
  36.1 1.1 %shard_map.68 = bf16[2048,1024]{1,0:T(8,128)(2,1)S(1)} custom-call(f32[32,1024]{1,0:T(8,128)S(1)} %get-tuple-element.80.rows_ref, f32[32,1]{1,0:T(8,128)S(1)} %copy.6.scale_ref, bf16[256,1024]{1,0:T(8,128)(2,1)S(1)} %shard_map.66.right_ref), custom_call_target="tpu_custom_call" | custom-call | flops 872415232 | bytes 4194304 | tf_op jit(solution)/shard_map/pallas_call | solution.py:115
  37.7 0.8 %fusion.59 = f32[96,1024]{1,0:T(8,128)S(1)} fusion(bf16[2048,1024]{1,0:T(8,128)(2,1)S(1)} %get-tuple-element.73, bf16[32,1024]{1,0:T(8,128)(2,1)S(1)} %get-tuple-element.144, bf16[32,1024]{1,0:T(8,128)(2,1)S(1)} %get-tuple-element.145, bf16[32,1024]{1,0:T(8,128)(2,1)S(1)} %get-tuple-element.143), kind=kOutput, calls=%fused_computation.80 | convolution fusion | flops 405012480 | bytes 4784128 | tf_op jit(solution)/shard_map/dot_general | solution.py:153
  39.4 0.8 %convolution_add_fusion.3 = f32[96,1024]{1,0:T(8,128)S(1)} fusion(f32[96,1024]{1,0:T(8,128)S(1)} %fusion.59, bf16[2048,1024]{1,0:T(8,128)(2,1)S(1)} %get-tuple-element.77, bf16[32,1024]{1,0:T(8,128)(2,1)S(1)} %get-tuple-element.140, bf16[32,1024]{1,0:T(8,128)(2,1)S(1)} %get-tuple-element.141, bf16[32,1024]{1,0:T(8,128)(2,1)S(1)} %get-tuple-element.139), kind=kOutput, calls=%fused_computation.3 | convolution fusion | flops 405110784 | bytes 5177344 | tf_op jit(solution)/shard_map/dot_general | solution.py:153
  40.4 1.5 %collective-permute-start.15 = (f32[32,1024]{1,0:T(8,128)S(1)}, f32[32,1024]{1,0:T(8,128)S(1)}, u32[]{:S(2)}, u32[]{:S(2)}) collective-permute-start(f32[32,1024]{1,0:T(8,128)S(1)} %get-tuple-element.88), channel_id=1, source_target_pairs={{0,2},{1,3},{2,0},{3,1},{4,6},{5,7},{6,4},{7,5},{8,10},{9,11},{10,... | collective-permute-start | bytes 393224 | tf_op jit(solution)/shard_map/ppermute | solution.py:19
  42.1 0.8 %fusion.82 = f32[96,1024]{1,0:T(8,128)S(1)} fusion(bf16[2048,1024]{1,0:T(8,128)(2,1)S(1)} %get-tuple-element.66, bf16[96,1024]{1,0:T(8,128)(2,1)S(1)} %pad_maximum_fusion.4), kind=kOutput, calls=%fused_computation.103 | convolution fusion | flops 403439616 | bytes 4784128 | tf_op jit(solution)/shard_map/dot_general | solution.py:153
  43.3 0.8 %convolution_add_fusion.2 = f32[96,1024]{1,0:T(8,128)S(1)} fusion(f32[96,1024]{1,0:T(8,128)S(1)} %fusion.82, bf16[2048,1024]{1,0:T(8,128)(2,1)S(1)} %get-tuple-element.67, bf16[32,1024]{1,0:T(8,128)(2,1)S(1)} %get-tuple-element.135, bf16[32,1024]{1,0:T(8,128)(2,1)S(1)} %get-tuple-element.136, bf16[32,1024]{1,0:T(8,128)(2,1)S(1)} %get-tuple-element.134), kind=kOutput, calls=%fused_computation.2 | convolution fusion | flops 405110784 | bytes 5177344 | tf_op jit(solution)/shard_map/dot_general | solution.py:153
  44.1 1.9 %collective-permute-done.15 = f32[32,1024]{1,0:T(8,128)S(1)} collective-permute-done((f32[32,1024]{1,0:T(8,128)S(1)}, f32[32,1024]{1,0:T(8,128)S(1)}, u32[]{:S(2)}, u32[]{:S(2)}) %collective-permute-start.15) | collective-permute-done | bytes 131104 | tf_op jit(solution)/shard_map/ppermute | solution.py:19
  46.1 0.8 %fusion.97 = f32[96,1024]{1,0:T(8,128)S(1)} fusion(bf16[2048,1024]{1,0:T(8,128)(2,1)S(1)} %get-tuple-element.73, bf16[32,1024]{1,0:T(8,128)(2,1)S(1)} %get-tuple-element.132, bf16[32,1024]{1,0:T(8,128)(2,1)S(1)} %get-tuple-element.133, bf16[32,1024]{1,0:T(8,128)(2,1)S(1)} %get-tuple-element.131), kind=kOutput, calls=%fused_computation.118 | convolution fusion | flops 405012480 | bytes 4784128 | tf_op jit(solution)/shard_map/dot_general | solution.py:153
  48.0 0.8 %convolution_add_fusion.1 = f32[96,1024]{1,0:T(8,128)S(1)} fusion(f32[96,1024]{1,0:T(8,128)S(1)} %fusion.97, bf16[2048,1024]{1,0:T(8,128)(2,1)S(1)} %get-tuple-element.77, bf16[32,1024]{1,0:T(8,128)(2,1)S(1)} %get-tuple-element.128, bf16[32,1024]{1,0:T(8,128)(2,1)S(1)} %get-tuple-element.129, bf16[32,1024]{1,0:T(8,128)(2,1)S(1)} %get-tuple-element.127), kind=kOutput, calls=%fused_computation.1 | convolution fusion | flops 405110784 | bytes 5177344 | tf_op jit(solution)/shard_map/dot_general | solution.py:153
  48.8 0.8 %fusion.120 = f32[96,1024]{1,0:T(8,128)S(1)} fusion(bf16[2048,1024]{1,0:T(8,128)(2,1)S(1)} %shard_map.67, bf16[32,1024]{1,0:T(8,128)(2,1)S(1)} %get-tuple-element.114, bf16[32,1024]{1,0:T(8,128)(2,1)S(1)} %get-tuple-element.113, bf16[32,1024]{1,0:T(8,128)(2,1)S(1)} %get-tuple-element.117), kind=kOutput, calls=%fused_computation.141 | convolution fusion | flops 405012480 | bytes 4784128 | tf_op jit(solution)/shard_map/dot_general | solution.py:153
  49.6 0.8 %convolution_add_fusion = f32[96,1024]{1,0:T(8,128)S(1)} fusion(f32[96,1024]{1,0:T(8,128)S(1)} %fusion.120, bf16[2048,1024]{1,0:T(8,128)(2,1)S(1)} %shard_map.68, bf16[32,1024]{1,0:T(8,128)(2,1)S(1)} %get-tuple-element.115, bf16[32,1024]{1,0:T(8,128)(2,1)S(1)} %get-tuple-element.116, bf16[32,1024]{1,0:T(8,128)(2,1)S(1)} %get-tuple-element.112), kind=kOutput, calls=%fused_computation | convolution fusion | flops 405110784 | bytes 5177344 | tf_op jit(solution)/shard_map/dot_general | solution.py:153
  51.0 0.9 %collective-permute-done.17 = f32[32]{0:T(128)S(1)} collective-permute-done((f32[32]{0:T(128)S(1)}, f32[32]{0:T(128)S(1)}, u32[]{:S(2)}, u32[]{:S(2)}) %collective-permute-start.17) | collective-permute-done | bytes 160 | tf_op jit(solution)/shard_map/ppermute | solution.py:19
  (87 shorter events, 12.0 us)
Async XLA Ops:
  2.1 8.1 %collective-permute-start = (f32[72,256]{1,0:T(8,128)S(1)}, f32[72,256]{1,0:T(8,128)S(1)}, u32[]{:S(2)}, u32[]{:S(2)}) collective-permute-start(f32[72,256]{1,0:T(8,128)S(1)} %pad_maximum_fusion.6.part_ref), channel_id=1, source_target_pairs={{0,8},{1,9},{2,10},{3,11},{4,12},{5,13},{6,14},{7,15},{8,0},{9,1},... | collective-permute-start | bytes 221192 | tf_op jit(solution)/shard_map/ppermute | solution.py:19
  7.0 7.7 %collective-permute-start.4 = (f32[65,256]{1,0:T(8,128)S(1)}, f32[65,256]{1,0:T(8,128)S(1)}, u32[]{:S(2)}, u32[]{:S(2)}) collective-permute-start(f32[65,256]{1,0:T(8,128)S(1)} %get-tuple-element.49), channel_id=1, source_target_pairs={{0,2},{1,3},{2,0},{3,1},{4,6},{5,7},{6,4},{7,5},{8,10},{9,11},{10,... | collective-permute-start | bytes 199688 | tf_op jit(solution)/shard_map/ppermute | solution.py:19
  8.6 4.7 %collective-permute-start.1 = (f32[65,256]{1,0:T(8,128)S(1)}, f32[65,256]{1,0:T(8,128)S(1)}, u32[]{:S(2)}, u32[]{:S(2)}) collective-permute-start(f32[65,256]{1,0:T(8,128)S(1)} %get-tuple-element.49), channel_id=1, source_target_pairs={{0,4},{1,5},{2,6},{3,7},{4,0},{5,1},{6,2},{7,3},{8,12},{9,13},{10,... | collective-permute-start | bytes 199688 | tf_op jit(solution)/shard_map/ppermute | solution.py:19
  10.1 4.4 %collective-permute-start.2 = (f32[72,256]{1,0:T(8,128)S(1)}, f32[72,256]{1,0:T(8,128)S(1)}, u32[]{:S(2)}, u32[]{:S(2)}) collective-permute-start(f32[72,256]{1,0:T(8,128)S(1)} %collective-permute-done.part_ref), channel_id=1, source_target_pairs={{0,4},{1,5},{2,6},{3,7},{4,0},{5,1},{6,2},{7,3},{8,12},{9,13},{10,... | collective-permute-start | bytes 221192 | tf_op jit(solution)/shard_map/ppermute | solution.py:19
  10.9 8.7 %collective-permute-start.6 = (f32[65,256]{1,0:T(8,128)S(1)}, f32[65,256]{1,0:T(8,128)S(1)}, u32[]{:S(2)}, u32[]{:S(2)}) collective-permute-start(f32[65,256]{1,0:T(8,128)S(1)} %get-tuple-element.53), channel_id=1, source_target_pairs={{0,2},{1,3},{2,0},{3,1},{4,6},{5,7},{6,4},{7,5},{8,10},{9,11},{10,... | collective-permute-start | bytes 199688 | tf_op jit(solution)/shard_map/ppermute | solution.py:19
  14.7 5.2 %collective-permute-start.5 = (f32[65,512]{1,0:T(8,128)S(1)}, f32[65,512]{1,0:T(8,128)S(1)}, u32[]{:S(2)}, u32[]{:S(2)}) collective-permute-start(f32[65,512]{1,0:T(8,128)S(1)} %get-tuple-element.52), channel_id=1, source_target_pairs={{0,2},{1,3},{2,0},{3,1},{4,6},{5,7},{6,4},{7,5},{8,10},{9,11},{10,... | collective-permute-start | bytes 399368 | tf_op jit(solution)/shard_map/ppermute | solution.py:19
  16.2 1.7 %collective-permute-start.3 = (f32[64,1024]{1,0:T(8,128)S(1)}, f32[64,1024]{1,0:T(8,128)S(1)}, u32[]{:S(2)}, u32[]{:S(2)}) collective-permute-start(f32[64,1024]{1,0:T(8,128)S(1)} %slice.225), channel_id=1, source_target_pairs={{0,1},{1,0},{2,3},{3,2},{4,5},{5,4},{6,7},{7,6},{8,9},{9,8},{10,11... | collective-permute-start | bytes 786440 | tf_op jit(solution)/shard_map/ppermute | solution.py:19
  20.0 1.8 %collective-permute-start.7 = (f32[64,1024]{1,0:T(8,128)S(1)}, f32[64,1024]{1,0:T(8,128)S(1)}, u32[]{:S(2)}, u32[]{:S(2)}) collective-permute-start(f32[64,1024]{1,0:T(8,128)S(1)} %slice.230), channel_id=1, source_target_pairs={{0,1},{1,0},{2,3},{3,2},{4,5},{5,4},{6,7},{7,6},{8,9},{9,8},{10,11... | collective-permute-start | bytes 786440 | tf_op jit(solution)/shard_map/ppermute | solution.py:19
  23.5 5.8 %collective-permute-start.9 = (f32[32,1024]{1,0:T(8,128)S(1)}, f32[32,1024]{1,0:T(8,128)S(1)}, u32[]{:S(2)}, u32[]{:S(2)}) collective-permute-start(f32[32,1024]{1,0:T(8,128)S(1)} %get-tuple-element.64), channel_id=1, source_target_pairs={{0,2},{1,3},{2,0},{3,1},{4,6},{5,7},{6,4},{7,5},{8,10},{9,11},{10,... | collective-permute-start | bytes 393224 | tf_op jit(solution)/shard_map/ppermute | solution.py:19
  24.8 1.4 %collective-permute-start.8 = (f32[32,1024]{1,0:T(8,128)S(1)}, f32[32,1024]{1,0:T(8,128)S(1)}, u32[]{:S(2)}, u32[]{:S(2)}) collective-permute-start(f32[32,1024]{1,0:T(8,128)S(1)} %get-tuple-element.64), channel_id=1, source_target_pairs={{0,1},{1,0},{2,3},{3,2},{4,5},{5,4},{6,7},{7,6},{8,9},{9,8},{10,11... | collective-permute-start | bytes 393224 | tf_op jit(solution)/shard_map/ppermute | solution.py:19
  29.3 1.3 %collective-permute-start.10 = (f32[32,1024]{1,0:T(8,128)S(1)}, f32[32,1024]{1,0:T(8,128)S(1)}, u32[]{:S(2)}, u32[]{:S(2)}) collective-permute-start(f32[32,1024]{1,0:T(8,128)S(1)} %collective-permute-done.9), channel_id=1, source_target_pairs={{0,1},{1,0},{2,3},{3,2},{4,5},{5,4},{6,7},{7,6},{8,9},{9,8},{10,11... | collective-permute-start | bytes 393224 | tf_op jit(solution)/shard_map/ppermute | solution.py:19
  32.0 5.6 %collective-permute-start.12 = (f32[32,1024]{1,0:T(8,128)S(1)}, f32[32,1024]{1,0:T(8,128)S(1)}, u32[]{:S(2)}, u32[]{:S(2)}) collective-permute-start(f32[32,1024]{1,0:T(8,128)S(1)} %get-tuple-element.78), channel_id=1, source_target_pairs={{0,2},{1,3},{2,0},{3,1},{4,6},{5,7},{6,4},{7,5},{8,10},{9,11},{10,... | collective-permute-start | bytes 393224 | tf_op jit(solution)/shard_map/ppermute | solution.py:19
  33.6 1.4 %collective-permute-start.11 = (f32[32,1024]{1,0:T(8,128)S(1)}, f32[32,1024]{1,0:T(8,128)S(1)}, u32[]{:S(2)}, u32[]{:S(2)}) collective-permute-start(f32[32,1024]{1,0:T(8,128)S(1)} %get-tuple-element.78), channel_id=1, source_target_pairs={{0,1},{1,0},{2,3},{3,2},{4,5},{5,4},{6,7},{7,6},{8,9},{9,8},{10,11... | collective-permute-start | bytes 393224 | tf_op jit(solution)/shard_map/ppermute | solution.py:19
  37.7 1.3 %collective-permute-start.13 = (f32[32,1024]{1,0:T(8,128)S(1)}, f32[32,1024]{1,0:T(8,128)S(1)}, u32[]{:S(2)}, u32[]{:S(2)}) collective-permute-start(f32[32,1024]{1,0:T(8,128)S(1)} %collective-permute-done.12), channel_id=1, source_target_pairs={{0,1},{1,0},{2,3},{3,2},{4,5},{5,4},{6,7},{7,6},{8,9},{9,8},{10,11... | collective-permute-start | bytes 393224 | tf_op jit(solution)/shard_map/ppermute | solution.py:19
  40.4 5.6 %collective-permute-start.15 = (f32[32,1024]{1,0:T(8,128)S(1)}, f32[32,1024]{1,0:T(8,128)S(1)}, u32[]{:S(2)}, u32[]{:S(2)}) collective-permute-start(f32[32,1024]{1,0:T(8,128)S(1)} %get-tuple-element.88), channel_id=1, source_target_pairs={{0,2},{1,3},{2,0},{3,1},{4,6},{5,7},{6,4},{7,5},{8,10},{9,11},{10,... | collective-permute-start | bytes 393224 | tf_op jit(solution)/shard_map/ppermute | solution.py:19
  41.9 1.4 %collective-permute-start.14 = (f32[32,1024]{1,0:T(8,128)S(1)}, f32[32,1024]{1,0:T(8,128)S(1)}, u32[]{:S(2)}, u32[]{:S(2)}) collective-permute-start(f32[32,1024]{1,0:T(8,128)S(1)} %get-tuple-element.88), channel_id=1, source_target_pairs={{0,1},{1,0},{2,3},{3,2},{4,5},{5,4},{6,7},{7,6},{8,9},{9,8},{10,11... | collective-permute-start | bytes 393224 | tf_op jit(solution)/shard_map/ppermute | solution.py:19
  46.0 1.3 %collective-permute-start.16 = (f32[32,1024]{1,0:T(8,128)S(1)}, f32[32,1024]{1,0:T(8,128)S(1)}, u32[]{:S(2)}, u32[]{:S(2)}) collective-permute-start(f32[32,1024]{1,0:T(8,128)S(1)} %collective-permute-done.15), channel_id=1, source_target_pairs={{0,1},{1,0},{2,3},{3,2},{4,5},{5,4},{6,7},{7,6},{8,9},{9,8},{10,11... | collective-permute-start | bytes 393224 | tf_op jit(solution)/shard_map/ppermute | solution.py:19
  50.8 1.2 %collective-permute-start.17 = (f32[32]{0:T(128)S(1)}, f32[32]{0:T(128)S(1)}, u32[]{:S(2)}, u32[]{:S(2)}) collective-permute-start(f32[32]{0:T(128)S(1)} %get-tuple-element.96), channel_id=1, source_target_pairs={{0,1},{1,0},{2,3},{3,2},{4,5},{5,4},{6,7},{7,6},{8,9},{9,8},{10,11... | collective-permute-start | bytes 392 | tf_op jit(solution)/shard_map/ppermute | solution.py:19

commit v23 on v22

--- a/solution.py
+++ b/solution.py
@@ -184,8 +184,8 @@
 
         scale = (POINT_SCALE / lengthscale)[:, None]
         used = feats + probes + 1
-        rest = jnp.broadcast_to(noise_var[None, :], (1 + -used % 8, width))
-        block = lax.optimization_barrier(jnp.concatenate([points, targets, rest], axis=0))
+        spare = points[: -used % 8]
+        block = lax.optimization_barrier(jnp.concatenate([points, targets, noise_var[None, :], spare], axis=0))
         fence = lax.optimization_barrier
         tile = []
 

time: 52.9 us -> 53 us (level)
    slice x0 -> x1, local copies, waits for them, and re-layouts: none -> 0.7 us  [body(): spare = points[:-used % 8]]
    broadcast_in_dim x1 -> x0, local copies, waits for them, and re-layouts: 0.68 us -> none  [body(): rest = jnp.broadcast_to(noise_var[None, :], (1 + -used % 8, width))]
where the time goes in v23:
time: 53 us; the launch traced here: 52.8 us
  starting transfers between devices  16.5 us (31%)
  matrix products  11.5 us (22%)
  Pallas kernels  8.81 us (17%)
  waiting for transfers between devices  8.6 us (16%)
  other arithmetic  5.41 us (10%)
  between operations  1 us (2%)
  local copies, waits for them, and re-layouts  0.97 us (2%)
    ppermute x18, starting transfers between devices, swap(): return lax.ppermute(x, 'blk', [(i, i ^ stride) for i in range(n)])  16.5 us
    dot_general x14, matrix products, apply_parts(): jnp.dot(jnp.concatenate([parts, parts], axis=1), piece, preferred_element...  11.5 us
    pallas_call x10, Pallas kernels, call(): pl.pallas_call(kernel, out_shape=outs, in_specs=[whole] * len(args), out_...  8.81 us
    ppermute x18, waiting for transfers between devices, swap(): return lax.ppermute(x, 'blk', [(i, i ^ stride) for i in range(n)])  8.6 us
  transfers between devices with their start and end apart: 18, of which 13 were waited for; matrix products, arithmetic and copies ran while one was open for 18% of the time, Pallas kernels for 14%

profile of v23, /device:TPU:0, one launch (start us, length us, event | category | flops | bytes accessed | tf_op | source)
XLA Modules:
  0.0 52.8 jit_solution(16188975532900078335)
XLA Ops:
  1.3 0.8 %pad_maximum_fusion.6.part_ref = f32[72,256]{1,0:T(8,128)S(1)} fusion(f32[7,256]{1,0:T(8,128)S(1)} %slice.175, f32[1,256]{1,0:T(1,128)} %bitcast.32, f32[32,256]{1,0:T(8,128)} %param.7, f32[32,256]{1,0:T(8,128)} %param.4), kind=kLoop, calls=%fused_computation.276 | loop fusion | flops 55296 | bytes 147456 | tf_op jit(solution)/shard_map/concatenate | solution.py:188
  2.1 4.1 %collective-permute-start = (f32[72,256]{1,0:T(8,128)S(1)}, f32[72,256]{1,0:T(8,128)S(1)}, u32[]{:S(2)}, u32[]{:S(2)}) collective-permute-start(f32[72,256]{1,0:T(8,128)S(1)} %pad_maximum_fusion.6.part_ref), channel_id=1, source_target_pairs={{0,8},{1,9},{2,10},{3,11},{4,12},{5,13},{6,14},{7,15},{8,0},{9,1},... | collective-permute-start | bytes 221192 | tf_op jit(solution)/shard_map/ppermute | solution.py:19
  7.1 1.6 %collective-permute-start.4 = (f32[65,256]{1,0:T(8,128)S(1)}, f32[65,256]{1,0:T(8,128)S(1)}, u32[]{:S(2)}, u32[]{:S(2)}) collective-permute-start(f32[65,256]{1,0:T(8,128)S(1)} %get-tuple-element.49), channel_id=1, source_target_pairs={{0,2},{1,3},{2,0},{3,1},{4,6},{5,7},{6,4},{7,5},{8,10},{9,11},{10,... | collective-permute-start | bytes 199688 | tf_op jit(solution)/shard_map/ppermute | solution.py:19
  8.7 1.6 %collective-permute-start.1 = (f32[65,256]{1,0:T(8,128)S(1)}, f32[65,256]{1,0:T(8,128)S(1)}, u32[]{:S(2)}, u32[]{:S(2)}) collective-permute-start(f32[65,256]{1,0:T(8,128)S(1)} %get-tuple-element.49), channel_id=1, source_target_pairs={{0,4},{1,5},{2,6},{3,7},{4,0},{5,1},{6,2},{7,3},{8,12},{9,13},{10,... | collective-permute-start | bytes 199688 | tf_op jit(solution)/shard_map/ppermute | solution.py:19
  11.0 1.9 %collective-permute-start.6 = (f32[65,256]{1,0:T(8,128)S(1)}, f32[65,256]{1,0:T(8,128)S(1)}, u32[]{:S(2)}, u32[]{:S(2)}) collective-permute-start(f32[65,256]{1,0:T(8,128)S(1)} %get-tuple-element.53), channel_id=1, source_target_pairs={{0,2},{1,3},{2,0},{3,1},{4,6},{5,7},{6,4},{7,5},{8,10},{9,11},{10,... | collective-permute-start | bytes 199688 | tf_op jit(solution)/shard_map/ppermute | solution.py:19
  13.4 1.2 %collective-permute-done.2 = f32[72,256]{1,0:T(8,128)S(1)} collective-permute-done((f32[72,256]{1,0:T(8,128)S(1)}, f32[72,256]{1,0:T(8,128)S(1)}, u32[]{:S(2)}, u32[]{:S(2)}) %collective-permute-start.2) | collective-permute-done | bytes 73760 | tf_op jit(solution)/shard_map/ppermute | solution.py:19
  14.8 1.5 %collective-permute-start.5 = (f32[65,512]{1,0:T(8,128)S(1)}, f32[65,512]{1,0:T(8,128)S(1)}, u32[]{:S(2)}, u32[]{:S(2)}) collective-permute-start(f32[65,512]{1,0:T(8,128)S(1)} %get-tuple-element.52), channel_id=1, source_target_pairs={{0,2},{1,3},{2,0},{3,1},{4,6},{5,7},{6,4},{7,5},{8,10},{9,11},{10,... | collective-permute-start | bytes 399368 | tf_op jit(solution)/shard_map/ppermute | solution.py:19
  16.4 1.6 %shard_map.62 = (bf16[2048,1024]{1,0:T(8,128)(2,1)S(1)}, f32[32,1024]{1,0:T(8,128)S(1)}) custom-call(f32[32,1024]{1,0:T(8,128)S(1)} %get-tuple-element.121.rows_ref, f32[32,1]{1,0:T(8,128)S(1)} %copy.6.scale_ref, bf16[256,1024]{1,0:T(8,128)(2,1)S(1)} %constant_dynamic-update-slice_fusion.right_ref, f32[32,1024]{1,0:T(8,128)S(1)} %get-tuple-element.122.refs_0_, ...), custom_call_target="tpu_custom_call" | custom-call | flops 872415232 | bytes 4194304 | tf_op jit(solution)/shard_map/pallas_call | solution.py:115
  18.1 1.6 %shard_map.63 = (bf16[2048,1024]{1,0:T(8,128)(2,1)S(1)}, f32[32,1024]{1,0:T(8,128)S(1)}) custom-call(f32[32,1024]{1,0:T(8,128)S(1)} %get-tuple-element.126.rows_ref, f32[32,1]{1,0:T(8,128)S(1)} %copy.6.scale_ref, bf16[256,1024]{1,0:T(8,128)(2,1)S(1)} %constant_dynamic-update-slice_fusion.right_ref, f32[32,1024]{1,0:T(8,128)S(1)} %get-tuple-element.125.refs_0_, ...), custom_call_target="tpu_custom_call" | custom-call | flops 872415232 | bytes 4194304 | tf_op jit(solution)/shard_map/pallas_call | solution.py:115
  20.3 1.6 %shard_map.64 = (bf16[2048,1024]{1,0:T(8,128)(2,1)S(1)}, f32[32,1024]{1,0:T(8,128)S(1)}) custom-call(f32[32,1024]{1,0:T(8,128)S(1)} %get-tuple-element.69.rows_ref.part_ref, f32[32,1]{1,0:T(8,128)S(1)} %copy.6.scale_ref, bf16[256,1024]{1,0:T(8,128)(2,1)S(1)} %constant_dynamic-update-slice_fusion.right_ref, f32[32,1024]{1,0:T(8,128)S(1)} %get-tuple-element.118.refs_0_, ...), custom_call_target="tpu_custom_call" | custom-call | flops 872415232 | bytes 4194304 | tf_op jit(solution)/shard_map/pallas_call | solution.py:115
  21.9 1.6 %shard_map.65 = (bf16[2048,1024]{1,0:T(8,128)(2,1)S(1)}, f32[32,1024]{1,0:T(8,128)S(1)}) custom-call(f32[32,1024]{1,0:T(8,128)S(1)} %get-tuple-element.80.rows_ref, f32[32,1]{1,0:T(8,128)S(1)} %copy.6.scale_ref, bf16[256,1024]{1,0:T(8,128)(2,1)S(1)} %constant_dynamic-update-slice_fusion.right_ref, f32[32,1024]{1,0:T(8,128)S(1)} %get-tuple-element.123.refs_0_, ...), custom_call_target="tpu_custom_call" | custom-call | flops 872415232 | bytes 4194304 | tf_op jit(solution)/shard_map/pallas_call | solution.py:115
  23.6 1.3 %collective-permute-start.9 = (f32[32,1024]{1,0:T(8,128)S(1)}, f32[32,1024]{1,0:T(8,128)S(1)}, u32[]{:S(2)}, u32[]{:S(2)}) collective-permute-start(f32[32,1024]{1,0:T(8,128)S(1)} %get-tuple-element.64), channel_id=1, source_target_pairs={{0,2},{1,3},{2,0},{3,1},{4,6},{5,7},{6,4},{7,5},{8,10},{9,11},{10,... | collective-permute-start | bytes 393224 | tf_op jit(solution)/shard_map/ppermute | solution.py:19
  26.4 0.8 %convolution_add_fusion.6 = f32[96,1024]{1,0:T(8,128)S(1)} fusion(f32[96,1024]{1,0:T(8,128)S(1)} %fusion.6, bf16[2048,1024]{1,0:T(8,128)(2,1)S(1)} %get-tuple-element.67, bf16[32,1024]{1,0:T(8,128)(2,1)S(1)} %get-tuple-element.159, bf16[32,1024]{1,0:T(8,128)(2,1)S(1)} %get-tuple-element.160, bf16[32,1024]{1,0:T(8,128)(2,1)S(1)} %get-tuple-element.158), kind=kOutput, calls=%fused_computation.6 | convolution fusion | flops 405110784 | bytes 5177344 | tf_op jit(solution)/shard_map/dot_general | solution.py:153
  27.3 1.1 %shard_map.67 = bf16[2048,1024]{1,0:T(8,128)(2,1)S(1)} custom-call(f32[32,1024]{1,0:T(8,128)S(1)} %get-tuple-element.69.rows_ref.part_ref, f32[32,1]{1,0:T(8,128)S(1)} %copy.6.scale_ref, bf16[256,1024]{1,0:T(8,128)(2,1)S(1)} %shard_map.66.right_ref), custom_call_target="tpu_custom_call" | custom-call | flops 872415232 | bytes 4194304 | tf_op jit(solution)/shard_map/pallas_call | solution.py:115
  28.4 1.0 %collective-permute-done.9 = f32[32,1024]{1,0:T(8,128)S(1)} collective-permute-done((f32[32,1024]{1,0:T(8,128)S(1)}, f32[32,1024]{1,0:T(8,128)S(1)}, u32[]{:S(2)}, u32[]{:S(2)}) %collective-permute-start.9) | collective-permute-done | bytes 131104 | tf_op jit(solution)/shard_map/ppermute | solution.py:19
  29.4 0.8 %fusion.21 = f32[96,1024]{1,0:T(8,128)S(1)} fusion(bf16[2048,1024]{1,0:T(8,128)(2,1)S(1)} %get-tuple-element.73, bf16[32,1024]{1,0:T(8,128)(2,1)S(1)} %get-tuple-element.156, bf16[32,1024]{1,0:T(8,128)(2,1)S(1)} %get-tuple-element.157, bf16[32,1024]{1,0:T(8,128)(2,1)S(1)} %get-tuple-element.155), kind=kOutput, calls=%fused_computation.42 | convolution fusion | flops 405012480 | bytes 4784128 | tf_op jit(solution)/shard_map/dot_general | solution.py:153
  31.2 0.8 %convolution_add_fusion.5 = f32[96,1024]{1,0:T(8,128)S(1)} fusion(f32[96,1024]{1,0:T(8,128)S(1)} %fusion.21, bf16[2048,1024]{1,0:T(8,128)(2,1)S(1)} %get-tuple-element.77, bf16[32,1024]{1,0:T(8,128)(2,1)S(1)} %get-tuple-element.152, bf16[32,1024]{1,0:T(8,128)(2,1)S(1)} %get-tuple-element.153, bf16[32,1024]{1,0:T(8,128)(2,1)S(1)} %get-tuple-element.151), kind=kOutput, calls=%fused_computation.5 | convolution fusion | flops 405110784 | bytes 5177344 | tf_op jit(solution)/shard_map/dot_general | solution.py:153
  32.1 1.5 %collective-permute-start.12 = (f32[32,1024]{1,0:T(8,128)S(1)}, f32[32,1024]{1,0:T(8,128)S(1)}, u32[]{:S(2)}, u32[]{:S(2)}) collective-permute-start(f32[32,1024]{1,0:T(8,128)S(1)} %get-tuple-element.78), channel_id=1, source_target_pairs={{0,2},{1,3},{2,0},{3,1},{4,6},{5,7},{6,4},{7,5},{8,10},{9,11},{10,... | collective-permute-start | bytes 393224 | tf_op jit(solution)/shard_map/ppermute | solution.py:19
  33.8 0.8 %fusion.44 = f32[96,1024]{1,0:T(8,128)S(1)} fusion(bf16[2048,1024]{1,0:T(8,128)(2,1)S(1)} %get-tuple-element.66, bf16[96,1024]{1,0:T(8,128)(2,1)S(1)} %pad_maximum_fusion.3), kind=kOutput, calls=%fused_computation.65 | convolution fusion | flops 403439616 | bytes 4784128 | tf_op jit(solution)/shard_map/dot_general | solution.py:153
  35.2 1.0 %convolution_add_fusion.4 = f32[96,1024]{1,0:T(8,128)S(1)} fusion(f32[96,1024]{1,0:T(8,128)S(1)} %fusion.44, bf16[2048,1024]{1,0:T(8,128)(2,1)S(1)} %get-tuple-element.67, bf16[32,1024]{1,0:T(8,128)(2,1)S(1)} %get-tuple-element.147, bf16[32,1024]{1,0:T(8,128)(2,1)S(1)} %get-tuple-element.148, bf16[32,1024]{1,0:T(8,128)(2,1)S(1)} %get-tuple-element.146), kind=kOutput, calls=%fused_computation.4 | convolution fusion | flops 405110784 | bytes 5177344 | tf_op jit(solution)/shard_map/dot_general | solution.py:153
  36.2 1.1 %shard_map.68 = bf16[2048,1024]{1,0:T(8,128)(2,1)S(1)} custom-call(f32[32,1024]{1,0:T(8,128)S(1)} %get-tuple-element.80.rows_ref, f32[32,1]{1,0:T(8,128)S(1)} %copy.6.scale_ref, bf16[256,1024]{1,0:T(8,128)(2,1)S(1)} %shard_map.66.right_ref), custom_call_target="tpu_custom_call" | custom-call | flops 872415232 | bytes 4194304 | tf_op jit(solution)/shard_map/pallas_call | solution.py:115
  37.8 0.8 %fusion.59 = f32[96,1024]{1,0:T(8,128)S(1)} fusion(bf16[2048,1024]{1,0:T(8,128)(2,1)S(1)} %get-tuple-element.73, bf16[32,1024]{1,0:T(8,128)(2,1)S(1)} %get-tuple-element.144, bf16[32,1024]{1,0:T(8,128)(2,1)S(1)} %get-tuple-element.145, bf16[32,1024]{1,0:T(8,128)(2,1)S(1)} %get-tuple-element.143), kind=kOutput, calls=%fused_computation.80 | convolution fusion | flops 405012480 | bytes 4784128 | tf_op jit(solution)/shard_map/dot_general | solution.py:153
  39.5 0.8 %convolution_add_fusion.3 = f32[96,1024]{1,0:T(8,128)S(1)} fusion(f32[96,1024]{1,0:T(8,128)S(1)} %fusion.59, bf16[2048,1024]{1,0:T(8,128)(2,1)S(1)} %get-tuple-element.77, bf16[32,1024]{1,0:T(8,128)(2,1)S(1)} %get-tuple-element.140, bf16[32,1024]{1,0:T(8,128)(2,1)S(1)} %get-tuple-element.141, bf16[32,1024]{1,0:T(8,128)(2,1)S(1)} %get-tuple-element.139), kind=kOutput, calls=%fused_computation.3 | convolution fusion | flops 405110784 | bytes 5177344 | tf_op jit(solution)/shard_map/dot_general | solution.py:153
  40.5 1.5 %collective-permute-start.15 = (f32[32,1024]{1,0:T(8,128)S(1)}, f32[32,1024]{1,0:T(8,128)S(1)}, u32[]{:S(2)}, u32[]{:S(2)}) collective-permute-start(f32[32,1024]{1,0:T(8,128)S(1)} %get-tuple-element.88), channel_id=1, source_target_pairs={{0,2},{1,3},{2,0},{3,1},{4,6},{5,7},{6,4},{7,5},{8,10},{9,11},{10,... | collective-permute-start | bytes 393224 | tf_op jit(solution)/shard_map/ppermute | solution.py:19
  42.2 0.8 %fusion.82 = f32[96,1024]{1,0:T(8,128)S(1)} fusion(bf16[2048,1024]{1,0:T(8,128)(2,1)S(1)} %get-tuple-element.66, bf16[96,1024]{1,0:T(8,128)(2,1)S(1)} %pad_maximum_fusion.4), kind=kOutput, calls=%fused_computation.103 | convolution fusion | flops 403439616 | bytes 4784128 | tf_op jit(solution)/shard_map/dot_general | solution.py:153
  43.4 0.8 %convolution_add_fusion.2 = f32[96,1024]{1,0:T(8,128)S(1)} fusion(f32[96,1024]{1,0:T(8,128)S(1)} %fusion.82, bf16[2048,1024]{1,0:T(8,128)(2,1)S(1)} %get-tuple-element.67, bf16[32,1024]{1,0:T(8,128)(2,1)S(1)} %get-tuple-element.135, bf16[32,1024]{1,0:T(8,128)(2,1)S(1)} %get-tuple-element.136, bf16[32,1024]{1,0:T(8,128)(2,1)S(1)} %get-tuple-element.134), kind=kOutput, calls=%fused_computation.2 | convolution fusion | flops 405110784 | bytes 5177344 | tf_op jit(solution)/shard_map/dot_general | solution.py:153
  44.2 1.9 %collective-permute-done.15 = f32[32,1024]{1,0:T(8,128)S(1)} collective-permute-done((f32[32,1024]{1,0:T(8,128)S(1)}, f32[32,1024]{1,0:T(8,128)S(1)}, u32[]{:S(2)}, u32[]{:S(2)}) %collective-permute-start.15) | collective-permute-done | bytes 131104 | tf_op jit(solution)/shard_map/ppermute | solution.py:19
  46.2 0.8 %fusion.97 = f32[96,1024]{1,0:T(8,128)S(1)} fusion(bf16[2048,1024]{1,0:T(8,128)(2,1)S(1)} %get-tuple-element.73, bf16[32,1024]{1,0:T(8,128)(2,1)S(1)} %get-tuple-element.132, bf16[32,1024]{1,0:T(8,128)(2,1)S(1)} %get-tuple-element.133, bf16[32,1024]{1,0:T(8,128)(2,1)S(1)} %get-tuple-element.131), kind=kOutput, calls=%fused_computation.118 | convolution fusion | flops 405012480 | bytes 4784128 | tf_op jit(solution)/shard_map/dot_general | solution.py:153
  48.1 0.8 %convolution_add_fusion.1 = f32[96,1024]{1,0:T(8,128)S(1)} fusion(f32[96,1024]{1,0:T(8,128)S(1)} %fusion.97, bf16[2048,1024]{1,0:T(8,128)(2,1)S(1)} %get-tuple-element.77, bf16[32,1024]{1,0:T(8,128)(2,1)S(1)} %get-tuple-element.128, bf16[32,1024]{1,0:T(8,128)(2,1)S(1)} %get-tuple-element.129, bf16[32,1024]{1,0:T(8,128)(2,1)S(1)} %get-tuple-element.127), kind=kOutput, calls=%fused_computation.1 | convolution fusion | flops 405110784 | bytes 5177344 | tf_op jit(solution)/shard_map/dot_general | solution.py:153
  48.9 0.8 %fusion.120 = f32[96,1024]{1,0:T(8,128)S(1)} fusion(bf16[2048,1024]{1,0:T(8,128)(2,1)S(1)} %shard_map.67, bf16[32,1024]{1,0:T(8,128)(2,1)S(1)} %get-tuple-element.114, bf16[32,1024]{1,0:T(8,128)(2,1)S(1)} %get-tuple-element.113, bf16[32,1024]{1,0:T(8,128)(2,1)S(1)} %get-tuple-element.117), kind=kOutput, calls=%fused_computation.141 | convolution fusion | flops 405012480 | bytes 4784128 | tf_op jit(solution)/shard_map/dot_general | solution.py:153
  49.7 0.8 %convolution_add_fusion = f32[96,1024]{1,0:T(8,128)S(1)} fusion(f32[96,1024]{1,0:T(8,128)S(1)} %fusion.120, bf16[2048,1024]{1,0:T(8,128)(2,1)S(1)} %shard_map.68, bf16[32,1024]{1,0:T(8,128)(2,1)S(1)} %get-tuple-element.115, bf16[32,1024]{1,0:T(8,128)(2,1)S(1)} %get-tuple-element.116, bf16[32,1024]{1,0:T(8,128)(2,1)S(1)} %get-tuple-element.112), kind=kOutput, calls=%fused_computation | convolution fusion | flops 405110784 | bytes 5177344 | tf_op jit(solution)/shard_map/dot_general | solution.py:153
  51.1 0.9 %collective-permute-done.17 = f32[32]{0:T(128)S(1)} collective-permute-done((f32[32]{0:T(128)S(1)}, f32[32]{0:T(128)S(1)}, u32[]{:S(2)}, u32[]{:S(2)}) %collective-permute-start.17) | collective-permute-done | bytes 160 | tf_op jit(solution)/shard_map/ppermute | solution.py:19
  (87 shorter events, 12.0 us)
Async XLA Ops:
  2.1 8.1 %collective-permute-start = (f32[72,256]{1,0:T(8,128)S(1)}, f32[72,256]{1,0:T(8,128)S(1)}, u32[]{:S(2)}, u32[]{:S(2)}) collective-permute-start(f32[72,256]{1,0:T(8,128)S(1)} %pad_maximum_fusion.6.part_ref), channel_id=1, source_target_pairs={{0,8},{1,9},{2,10},{3,11},{4,12},{5,13},{6,14},{7,15},{8,0},{9,1},... | collective-permute-start | bytes 221192 | tf_op jit(solution)/shard_map/ppermute | solution.py:19
  7.1 7.7 %collective-permute-start.4 = (f32[65,256]{1,0:T(8,128)S(1)}, f32[65,256]{1,0:T(8,128)S(1)}, u32[]{:S(2)}, u32[]{:S(2)}) collective-permute-start(f32[65,256]{1,0:T(8,128)S(1)} %get-tuple-element.49), channel_id=1, source_target_pairs={{0,2},{1,3},{2,0},{3,1},{4,6},{5,7},{6,4},{7,5},{8,10},{9,11},{10,... | collective-permute-start | bytes 199688 | tf_op jit(solution)/shard_map/ppermute | solution.py:19
  8.7 4.7 %collective-permute-start.1 = (f32[65,256]{1,0:T(8,128)S(1)}, f32[65,256]{1,0:T(8,128)S(1)}, u32[]{:S(2)}, u32[]{:S(2)}) collective-permute-start(f32[65,256]{1,0:T(8,128)S(1)} %get-tuple-element.49), channel_id=1, source_target_pairs={{0,4},{1,5},{2,6},{3,7},{4,0},{5,1},{6,2},{7,3},{8,12},{9,13},{10,... | collective-permute-start | bytes 199688 | tf_op jit(solution)/shard_map/ppermute | solution.py:19
  10.2 4.4 %collective-permute-start.2 = (f32[72,256]{1,0:T(8,128)S(1)}, f32[72,256]{1,0:T(8,128)S(1)}, u32[]{:S(2)}, u32[]{:S(2)}) collective-permute-start(f32[72,256]{1,0:T(8,128)S(1)} %collective-permute-done.part_ref), channel_id=1, source_target_pairs={{0,4},{1,5},{2,6},{3,7},{4,0},{5,1},{6,2},{7,3},{8,12},{9,13},{10,... | collective-permute-start | bytes 221192 | tf_op jit(solution)/shard_map/ppermute | solution.py:19
  11.0 8.7 %collective-permute-start.6 = (f32[65,256]{1,0:T(8,128)S(1)}, f32[65,256]{1,0:T(8,128)S(1)}, u32[]{:S(2)}, u32[]{:S(2)}) collective-permute-start(f32[65,256]{1,0:T(8,128)S(1)} %get-tuple-element.53), channel_id=1, source_target_pairs={{0,2},{1,3},{2,0},{3,1},{4,6},{5,7},{6,4},{7,5},{8,10},{9,11},{10,... | collective-permute-start | bytes 199688 | tf_op jit(solution)/shard_map/ppermute | solution.py:19
  14.8 5.2 %collective-permute-start.5 = (f32[65,512]{1,0:T(8,128)S(1)}, f32[65,512]{1,0:T(8,128)S(1)}, u32[]{:S(2)}, u32[]{:S(2)}) collective-permute-start(f32[65,512]{1,0:T(8,128)S(1)} %get-tuple-element.52), channel_id=1, source_target_pairs={{0,2},{1,3},{2,0},{3,1},{4,6},{5,7},{6,4},{7,5},{8,10},{9,11},{10,... | collective-permute-start | bytes 399368 | tf_op jit(solution)/shard_map/ppermute | solution.py:19
  16.3 1.7 %collective-permute-start.3 = (f32[64,1024]{1,0:T(8,128)S(1)}, f32[64,1024]{1,0:T(8,128)S(1)}, u32[]{:S(2)}, u32[]{:S(2)}) collective-permute-start(f32[64,1024]{1,0:T(8,128)S(1)} %slice.229), channel_id=1, source_target_pairs={{0,1},{1,0},{2,3},{3,2},{4,5},{5,4},{6,7},{7,6},{8,9},{9,8},{10,11... | collective-permute-start | bytes 786440 | tf_op jit(solution)/shard_map/ppermute | solution.py:19
  20.1 1.8 %collective-permute-start.7 = (f32[64,1024]{1,0:T(8,128)S(1)}, f32[64,1024]{1,0:T(8,128)S(1)}, u32[]{:S(2)}, u32[]{:S(2)}) collective-permute-start(f32[64,1024]{1,0:T(8,128)S(1)} %slice.234), channel_id=1, source_target_pairs={{0,1},{1,0},{2,3},{3,2},{4,5},{5,4},{6,7},{7,6},{8,9},{9,8},{10,11... | collective-permute-start | bytes 786440 | tf_op jit(solution)/shard_map/ppermute | solution.py:19
  23.6 5.8 %collective-permute-start.9 = (f32[32,1024]{1,0:T(8,128)S(1)}, f32[32,1024]{1,0:T(8,128)S(1)}, u32[]{:S(2)}, u32[]{:S(2)}) collective-permute-start(f32[32,1024]{1,0:T(8,128)S(1)} %get-tuple-element.64), channel_id=1, source_target_pairs={{0,2},{1,3},{2,0},{3,1},{4,6},{5,7},{6,4},{7,5},{8,10},{9,11},{10,... | collective-permute-start | bytes 393224 | tf_op jit(solution)/shard_map/ppermute | solution.py:19
  24.9 1.4 %collective-permute-start.8 = (f32[32,1024]{1,0:T(8,128)S(1)}, f32[32,1024]{1,0:T(8,128)S(1)}, u32[]{:S(2)}, u32[]{:S(2)}) collective-permute-start(f32[32,1024]{1,0:T(8,128)S(1)} %get-tuple-element.64), channel_id=1, source_target_pairs={{0,1},{1,0},{2,3},{3,2},{4,5},{5,4},{6,7},{7,6},{8,9},{9,8},{10,11... | collective-permute-start | bytes 393224 | tf_op jit(solution)/shard_map/ppermute | solution.py:19
  29.4 1.3 %collective-permute-start.10 = (f32[32,1024]{1,0:T(8,128)S(1)}, f32[32,1024]{1,0:T(8,128)S(1)}, u32[]{:S(2)}, u32[]{:S(2)}) collective-permute-start(f32[32,1024]{1,0:T(8,128)S(1)} %collective-permute-done.9), channel_id=1, source_target_pairs={{0,1},{1,0},{2,3},{3,2},{4,5},{5,4},{6,7},{7,6},{8,9},{9,8},{10,11... | collective-permute-start | bytes 393224 | tf_op jit(solution)/shard_map/ppermute | solution.py:19
  32.1 5.6 %collective-permute-start.12 = (f32[32,1024]{1,0:T(8,128)S(1)}, f32[32,1024]{1,0:T(8,128)S(1)}, u32[]{:S(2)}, u32[]{:S(2)}) collective-permute-start(f32[32,1024]{1,0:T(8,128)S(1)} %get-tuple-element.78), channel_id=1, source_target_pairs={{0,2},{1,3},{2,0},{3,1},{4,6},{5,7},{6,4},{7,5},{8,10},{9,11},{10,... | collective-permute-start | bytes 393224 | tf_op jit(solution)/shard_map/ppermute | solution.py:19
  33.7 1.4 %collective-permute-start.11 = (f32[32,1024]{1,0:T(8,128)S(1)}, f32[32,1024]{1,0:T(8,128)S(1)}, u32[]{:S(2)}, u32[]{:S(2)}) collective-permute-start(f32[32,1024]{1,0:T(8,128)S(1)} %get-tuple-element.78), channel_id=1, source_target_pairs={{0,1},{1,0},{2,3},{3,2},{4,5},{5,4},{6,7},{7,6},{8,9},{9,8},{10,11... | collective-permute-start | bytes 393224 | tf_op jit(solution)/shard_map/ppermute | solution.py:19
  37.8 1.3 %collective-permute-start.13 = (f32[32,1024]{1,0:T(8,128)S(1)}, f32[32,1024]{1,0:T(8,128)S(1)}, u32[]{:S(2)}, u32[]{:S(2)}) collective-permute-start(f32[32,1024]{1,0:T(8,128)S(1)} %collective-permute-done.12), channel_id=1, source_target_pairs={{0,1},{1,0},{2,3},{3,2},{4,5},{5,4},{6,7},{7,6},{8,9},{9,8},{10,11... | collective-permute-start | bytes 393224 | tf_op jit(solution)/shard_map/ppermute | solution.py:19
  40.5 5.6 %collective-permute-start.15 = (f32[32,1024]{1,0:T(8,128)S(1)}, f32[32,1024]{1,0:T(8,128)S(1)}, u32[]{:S(2)}, u32[]{:S(2)}) collective-permute-start(f32[32,1024]{1,0:T(8,128)S(1)} %get-tuple-element.88), channel_id=1, source_target_pairs={{0,2},{1,3},{2,0},{3,1},{4,6},{5,7},{6,4},{7,5},{8,10},{9,11},{10,... | collective-permute-start | bytes 393224 | tf_op jit(solution)/shard_map/ppermute | solution.py:19
  42.0 1.4 %collective-permute-start.14 = (f32[32,1024]{1,0:T(8,128)S(1)}, f32[32,1024]{1,0:T(8,128)S(1)}, u32[]{:S(2)}, u32[]{:S(2)}) collective-permute-start(f32[32,1024]{1,0:T(8,128)S(1)} %get-tuple-element.88), channel_id=1, source_target_pairs={{0,1},{1,0},{2,3},{3,2},{4,5},{5,4},{6,7},{7,6},{8,9},{9,8},{10,11... | collective-permute-start | bytes 393224 | tf_op jit(solution)/shard_map/ppermute | solution.py:19
  46.1 1.3 %collective-permute-start.16 = (f32[32,1024]{1,0:T(8,128)S(1)}, f32[32,1024]{1,0:T(8,128)S(1)}, u32[]{:S(2)}, u32[]{:S(2)}) collective-permute-start(f32[32,1024]{1,0:T(8,128)S(1)} %collective-permute-done.15), channel_id=1, source_target_pairs={{0,1},{1,0},{2,3},{3,2},{4,5},{5,4},{6,7},{7,6},{8,9},{9,8},{10,11... | collective-permute-start | bytes 393224 | tf_op jit(solution)/shard_map/ppermute | solution.py:19
  50.9 1.2 %collective-permute-start.17 = (f32[32]{0:T(128)S(1)}, f32[32]{0:T(128)S(1)}, u32[]{:S(2)}, u32[]{:S(2)}) collective-permute-start(f32[32]{0:T(128)S(1)} %get-tuple-element.96), channel_id=1, source_target_pairs={{0,1},{1,0},{2,3},{3,2},{4,5},{5,4},{6,7},{7,6},{8,9},{9,8},{10,11... | collective-permute-start | bytes 392 | tf_op jit(solution)/shard_map/ppermute | solution.py:19

commit v24 on v23

--- a/solution.py
+++ b/solution.py
@@ -184,8 +184,8 @@
 
         scale = (POINT_SCALE / lengthscale)[:, None]
         used = feats + probes + 1
-        spare = points[: -used % 8]
-        block = lax.optimization_barrier(jnp.concatenate([points, targets, noise_var[None, :], spare], axis=0))
+        spare = jnp.zeros((-used % 8, width), jnp.float32)
+        block = lax.optimization_barrier(jnp.concatenate([points, targets, jnp.pad(noise_var[None, :], ((0, -used % 8), (0, 0)))], axis=0))
         fence = lax.optimization_barrier
         tile = []
 

time: 53 us -> 52.2 us (0.985)
  local copies, waits for them, and re-layouts: 0.97 us -> 0.27 us
    slice x1 -> x0, local copies, waits for them, and re-layouts: 0.7 us -> none  [body(): spare = points[:-used % 8]]
where the time goes in v24:
time: 52.2 us; the launch traced here: 52 us
  starting transfers between devices  16.4 us (31%)
  matrix products  11.5 us (22%)
  Pallas kernels  8.81 us (17%)
  waiting for transfers between devices  8.65 us (17%)
  other arithmetic  5.41 us (10%)
  between operations  1 us (2%)
    ppermute x18, starting transfers between devices, swap(): return lax.ppermute(x, 'blk', [(i, i ^ stride) for i in range(n)])  16.4 us
    dot_general x14, matrix products, apply_parts(): jnp.dot(jnp.concatenate([parts, parts], axis=1), piece, preferred_element...  11.5 us
    pallas_call x10, Pallas kernels, call(): pl.pallas_call(kernel, out_shape=outs, in_specs=[whole] * len(args), out_...  8.81 us
    ppermute x18, waiting for transfers between devices, swap(): return lax.ppermute(x, 'blk', [(i, i ^ stride) for i in range(n)])  8.65 us
  transfers between devices with their start and end apart: 18, of which 13 were waited for; matrix products, arithmetic and copies ran while one was open for 18% of the time, Pallas kernels for 14%

profile of v24, /device:TPU:0, one launch (start us, length us, event | category | flops | bytes accessed | tf_op | source)
XLA Modules:
  0.0 52.0 jit_solution(4865620212245730624)
XLA Ops:
  0.6 0.8 %select_maximum_fusion.part_ref = f32[72,256]{1,0:T(8,128)S(1)} fusion(f32[1,256]{1,0:T(1,128)} %bitcast.32, f32[32,256]{1,0:T(8,128)} %param.7, f32[32,256]{1,0:T(8,128)} %param.4), kind=kLoop, calls=%fused_computation.276 | loop fusion | flops 73728 | bytes 140288 | tf_op jit(solution)/shard_map/concatenate | solution.py:188
  1.4 4.0 %collective-permute-start = (f32[72,256]{1,0:T(8,128)S(1)}, f32[72,256]{1,0:T(8,128)S(1)}, u32[]{:S(2)}, u32[]{:S(2)}) collective-permute-start(f32[72,256]{1,0:T(8,128)S(1)} %select_maximum_fusion.part_ref), channel_id=1, source_target_pairs={{0,8},{1,9},{2,10},{3,11},{4,12},{5,13},{6,14},{7,15},{8,0},{9,1},... | collective-permute-start | bytes 221192 | tf_op jit(solution)/shard_map/ppermute | solution.py:19
  6.3 1.6 %collective-permute-start.4 = (f32[65,256]{1,0:T(8,128)S(1)}, f32[65,256]{1,0:T(8,128)S(1)}, u32[]{:S(2)}, u32[]{:S(2)}) collective-permute-start(f32[65,256]{1,0:T(8,128)S(1)} %get-tuple-element.49), channel_id=1, source_target_pairs={{0,2},{1,3},{2,0},{3,1},{4,6},{5,7},{6,4},{7,5},{8,10},{9,11},{10,... | collective-permute-start | bytes 199688 | tf_op jit(solution)/shard_map/ppermute | solution.py:19
  7.9 1.6 %collective-permute-start.1 = (f32[65,256]{1,0:T(8,128)S(1)}, f32[65,256]{1,0:T(8,128)S(1)}, u32[]{:S(2)}, u32[]{:S(2)}) collective-permute-start(f32[65,256]{1,0:T(8,128)S(1)} %get-tuple-element.49), channel_id=1, source_target_pairs={{0,4},{1,5},{2,6},{3,7},{4,0},{5,1},{6,2},{7,3},{8,12},{9,13},{10,... | collective-permute-start | bytes 199688 | tf_op jit(solution)/shard_map/ppermute | solution.py:19
  10.2 1.9 %collective-permute-start.6 = (f32[65,256]{1,0:T(8,128)S(1)}, f32[65,256]{1,0:T(8,128)S(1)}, u32[]{:S(2)}, u32[]{:S(2)}) collective-permute-start(f32[65,256]{1,0:T(8,128)S(1)} %get-tuple-element.53), channel_id=1, source_target_pairs={{0,2},{1,3},{2,0},{3,1},{4,6},{5,7},{6,4},{7,5},{8,10},{9,11},{10,... | collective-permute-start | bytes 199688 | tf_op jit(solution)/shard_map/ppermute | solution.py:19
  12.6 1.2 %collective-permute-done.2 = f32[72,256]{1,0:T(8,128)S(1)} collective-permute-done((f32[72,256]{1,0:T(8,128)S(1)}, f32[72,256]{1,0:T(8,128)S(1)}, u32[]{:S(2)}, u32[]{:S(2)}) %collective-permute-start.2) | collective-permute-done | bytes 73760 | tf_op jit(solution)/shard_map/ppermute | solution.py:19
  14.0 1.5 %collective-permute-start.5 = (f32[65,512]{1,0:T(8,128)S(1)}, f32[65,512]{1,0:T(8,128)S(1)}, u32[]{:S(2)}, u32[]{:S(2)}) collective-permute-start(f32[65,512]{1,0:T(8,128)S(1)} %get-tuple-element.52), channel_id=1, source_target_pairs={{0,2},{1,3},{2,0},{3,1},{4,6},{5,7},{6,4},{7,5},{8,10},{9,11},{10,... | collective-permute-start | bytes 399368 | tf_op jit(solution)/shard_map/ppermute | solution.py:19
  15.7 1.6 %shard_map.62 = (bf16[2048,1024]{1,0:T(8,128)(2,1)S(1)}, f32[32,1024]{1,0:T(8,128)S(1)}) custom-call(f32[32,1024]{1,0:T(8,128)S(1)} %get-tuple-element.121.rows_ref, f32[32,1]{1,0:T(8,128)S(1)} %copy.6.scale_ref, bf16[256,1024]{1,0:T(8,128)(2,1)S(1)} %constant_dynamic-update-slice_fusion.right_ref, f32[32,1024]{1,0:T(8,128)S(1)} %get-tuple-element.122.refs_0_, ...), custom_call_target="tpu_custom_call" | custom-call | flops 872415232 | bytes 4194304 | tf_op jit(solution)/shard_map/pallas_call | solution.py:115
  17.3 1.5 %shard_map.63 = (bf16[2048,1024]{1,0:T(8,128)(2,1)S(1)}, f32[32,1024]{1,0:T(8,128)S(1)}) custom-call(f32[32,1024]{1,0:T(8,128)S(1)} %get-tuple-element.126.rows_ref, f32[32,1]{1,0:T(8,128)S(1)} %copy.6.scale_ref, bf16[256,1024]{1,0:T(8,128)(2,1)S(1)} %constant_dynamic-update-slice_fusion.right_ref, f32[32,1024]{1,0:T(8,128)S(1)} %get-tuple-element.125.refs_0_, ...), custom_call_target="tpu_custom_call" | custom-call | flops 872415232 | bytes 4194304 | tf_op jit(solution)/shard_map/pallas_call | solution.py:115
  19.6 1.6 %shard_map.64 = (bf16[2048,1024]{1,0:T(8,128)(2,1)S(1)}, f32[32,1024]{1,0:T(8,128)S(1)}) custom-call(f32[32,1024]{1,0:T(8,128)S(1)} %get-tuple-element.69.rows_ref.part_ref, f32[32,1]{1,0:T(8,128)S(1)} %copy.6.scale_ref, bf16[256,1024]{1,0:T(8,128)(2,1)S(1)} %constant_dynamic-update-slice_fusion.right_ref, f32[32,1024]{1,0:T(8,128)S(1)} %get-tuple-element.118.refs_0_, ...), custom_call_target="tpu_custom_call" | custom-call | flops 872415232 | bytes 4194304 | tf_op jit(solution)/shard_map/pallas_call | solution.py:115
  21.2 1.6 %shard_map.65 = (bf16[2048,1024]{1,0:T(8,128)(2,1)S(1)}, f32[32,1024]{1,0:T(8,128)S(1)}) custom-call(f32[32,1024]{1,0:T(8,128)S(1)} %get-tuple-element.80.rows_ref, f32[32,1]{1,0:T(8,128)S(1)} %copy.6.scale_ref, bf16[256,1024]{1,0:T(8,128)(2,1)S(1)} %constant_dynamic-update-slice_fusion.right_ref, f32[32,1024]{1,0:T(8,128)S(1)} %get-tuple-element.123.refs_0_, ...), custom_call_target="tpu_custom_call" | custom-call | flops 872415232 | bytes 4194304 | tf_op jit(solution)/shard_map/pallas_call | solution.py:115
  22.8 1.3 %collective-permute-start.9 = (f32[32,1024]{1,0:T(8,128)S(1)}, f32[32,1024]{1,0:T(8,128)S(1)}, u32[]{:S(2)}, u32[]{:S(2)}) collective-permute-start(f32[32,1024]{1,0:T(8,128)S(1)} %get-tuple-element.64), channel_id=1, source_target_pairs={{0,2},{1,3},{2,0},{3,1},{4,6},{5,7},{6,4},{7,5},{8,10},{9,11},{10,... | collective-permute-start | bytes 393224 | tf_op jit(solution)/shard_map/ppermute | solution.py:19
  25.6 0.8 %convolution_add_fusion.6 = f32[96,1024]{1,0:T(8,128)S(1)} fusion(f32[96,1024]{1,0:T(8,128)S(1)} %fusion.6, bf16[2048,1024]{1,0:T(8,128)(2,1)S(1)} %get-tuple-element.67, bf16[32,1024]{1,0:T(8,128)(2,1)S(1)} %get-tuple-element.159, bf16[32,1024]{1,0:T(8,128)(2,1)S(1)} %get-tuple-element.160, bf16[32,1024]{1,0:T(8,128)(2,1)S(1)} %get-tuple-element.158), kind=kOutput, calls=%fused_computation.6 | convolution fusion | flops 405110784 | bytes 5177344 | tf_op jit(solution)/shard_map/dot_general | solution.py:153
  26.6 1.1 %shard_map.67 = bf16[2048,1024]{1,0:T(8,128)(2,1)S(1)} custom-call(f32[32,1024]{1,0:T(8,128)S(1)} %get-tuple-element.69.rows_ref.part_ref, f32[32,1]{1,0:T(8,128)S(1)} %copy.6.scale_ref, bf16[256,1024]{1,0:T(8,128)(2,1)S(1)} %shard_map.66.right_ref), custom_call_target="tpu_custom_call" | custom-call | flops 872415232 | bytes 4194304 | tf_op jit(solution)/shard_map/pallas_call | solution.py:115
  27.6 1.0 %collective-permute-done.9 = f32[32,1024]{1,0:T(8,128)S(1)} collective-permute-done((f32[32,1024]{1,0:T(8,128)S(1)}, f32[32,1024]{1,0:T(8,128)S(1)}, u32[]{:S(2)}, u32[]{:S(2)}) %collective-permute-start.9) | collective-permute-done | bytes 131104 | tf_op jit(solution)/shard_map/ppermute | solution.py:19
  28.7 0.8 %fusion.21 = f32[96,1024]{1,0:T(8,128)S(1)} fusion(bf16[2048,1024]{1,0:T(8,128)(2,1)S(1)} %get-tuple-element.73, bf16[32,1024]{1,0:T(8,128)(2,1)S(1)} %get-tuple-element.156, bf16[32,1024]{1,0:T(8,128)(2,1)S(1)} %get-tuple-element.157, bf16[32,1024]{1,0:T(8,128)(2,1)S(1)} %get-tuple-element.155), kind=kOutput, calls=%fused_computation.42 | convolution fusion | flops 405012480 | bytes 4784128 | tf_op jit(solution)/shard_map/dot_general | solution.py:153
  30.4 0.8 %convolution_add_fusion.5 = f32[96,1024]{1,0:T(8,128)S(1)} fusion(f32[96,1024]{1,0:T(8,128)S(1)} %fusion.21, bf16[2048,1024]{1,0:T(8,128)(2,1)S(1)} %get-tuple-element.77, bf16[32,1024]{1,0:T(8,128)(2,1)S(1)} %get-tuple-element.152, bf16[32,1024]{1,0:T(8,128)(2,1)S(1)} %get-tuple-element.153, bf16[32,1024]{1,0:T(8,128)(2,1)S(1)} %get-tuple-element.151), kind=kOutput, calls=%fused_computation.5 | convolution fusion | flops 405110784 | bytes 5177344 | tf_op jit(solution)/shard_map/dot_general | solution.py:153
  31.4 1.5 %collective-permute-start.12 = (f32[32,1024]{1,0:T(8,128)S(1)}, f32[32,1024]{1,0:T(8,128)S(1)}, u32[]{:S(2)}, u32[]{:S(2)}) collective-permute-start(f32[32,1024]{1,0:T(8,128)S(1)} %get-tuple-element.78), channel_id=1, source_target_pairs={{0,2},{1,3},{2,0},{3,1},{4,6},{5,7},{6,4},{7,5},{8,10},{9,11},{10,... | collective-permute-start | bytes 393224 | tf_op jit(solution)/shard_map/ppermute | solution.py:19
  33.1 0.8 %fusion.44 = f32[96,1024]{1,0:T(8,128)S(1)} fusion(bf16[2048,1024]{1,0:T(8,128)(2,1)S(1)} %get-tuple-element.66, bf16[96,1024]{1,0:T(8,128)(2,1)S(1)} %pad_maximum_fusion.3), kind=kOutput, calls=%fused_computation.65 | convolution fusion | flops 403439616 | bytes 4784128 | tf_op jit(solution)/shard_map/dot_general | solution.py:153
  34.4 1.0 %convolution_add_fusion.4 = f32[96,1024]{1,0:T(8,128)S(1)} fusion(f32[96,1024]{1,0:T(8,128)S(1)} %fusion.44, bf16[2048,1024]{1,0:T(8,128)(2,1)S(1)} %get-tuple-element.67, bf16[32,1024]{1,0:T(8,128)(2,1)S(1)} %get-tuple-element.147, bf16[32,1024]{1,0:T(8,128)(2,1)S(1)} %get-tuple-element.148, bf16[32,1024]{1,0:T(8,128)(2,1)S(1)} %get-tuple-element.146), kind=kOutput, calls=%fused_computation.4 | convolution fusion | flops 405110784 | bytes 5177344 | tf_op jit(solution)/shard_map/dot_general | solution.py:153
  35.4 1.1 %shard_map.68 = bf16[2048,1024]{1,0:T(8,128)(2,1)S(1)} custom-call(f32[32,1024]{1,0:T(8,128)S(1)} %get-tuple-element.80.rows_ref, f32[32,1]{1,0:T(8,128)S(1)} %copy.6.scale_ref, bf16[256,1024]{1,0:T(8,128)(2,1)S(1)} %shard_map.66.right_ref), custom_call_target="tpu_custom_call" | custom-call | flops 872415232 | bytes 4194304 | tf_op jit(solution)/shard_map/pallas_call | solution.py:115
  37.0 0.8 %fusion.59 = f32[96,1024]{1,0:T(8,128)S(1)} fusion(bf16[2048,1024]{1,0:T(8,128)(2,1)S(1)} %get-tuple-element.73, bf16[32,1024]{1,0:T(8,128)(2,1)S(1)} %get-tuple-element.144, bf16[32,1024]{1,0:T(8,128)(2,1)S(1)} %get-tuple-element.145, bf16[32,1024]{1,0:T(8,128)(2,1)S(1)} %get-tuple-element.143), kind=kOutput, calls=%fused_computation.80 | convolution fusion | flops 405012480 | bytes 4784128 | tf_op jit(solution)/shard_map/dot_general | solution.py:153
  38.8 0.8 %convolution_add_fusion.3 = f32[96,1024]{1,0:T(8,128)S(1)} fusion(f32[96,1024]{1,0:T(8,128)S(1)} %fusion.59, bf16[2048,1024]{1,0:T(8,128)(2,1)S(1)} %get-tuple-element.77, bf16[32,1024]{1,0:T(8,128)(2,1)S(1)} %get-tuple-element.140, bf16[32,1024]{1,0:T(8,128)(2,1)S(1)} %get-tuple-element.141, bf16[32,1024]{1,0:T(8,128)(2,1)S(1)} %get-tuple-element.139), kind=kOutput, calls=%fused_computation.3 | convolution fusion | flops 405110784 | bytes 5177344 | tf_op jit(solution)/shard_map/dot_general | solution.py:153
  39.7 1.5 %collective-permute-start.15 = (f32[32,1024]{1,0:T(8,128)S(1)}, f32[32,1024]{1,0:T(8,128)S(1)}, u32[]{:S(2)}, u32[]{:S(2)}) collective-permute-start(f32[32,1024]{1,0:T(8,128)S(1)} %get-tuple-element.88), channel_id=1, source_target_pairs={{0,2},{1,3},{2,0},{3,1},{4,6},{5,7},{6,4},{7,5},{8,10},{9,11},{10,... | collective-permute-start | bytes 393224 | tf_op jit(solution)/shard_map/ppermute | solution.py:19
  41.4 0.8 %fusion.82 = f32[96,1024]{1,0:T(8,128)S(1)} fusion(bf16[2048,1024]{1,0:T(8,128)(2,1)S(1)} %get-tuple-element.66, bf16[96,1024]{1,0:T(8,128)(2,1)S(1)} %pad_maximum_fusion.4), kind=kOutput, calls=%fused_computation.103 | convolution fusion | flops 403439616 | bytes 4784128 | tf_op jit(solution)/shard_map/dot_general | solution.py:153
  42.7 0.8 %convolution_add_fusion.2 = f32[96,1024]{1,0:T(8,128)S(1)} fusion(f32[96,1024]{1,0:T(8,128)S(1)} %fusion.82, bf16[2048,1024]{1,0:T(8,128)(2,1)S(1)} %get-tuple-element.67, bf16[32,1024]{1,0:T(8,128)(2,1)S(1)} %get-tuple-element.135, bf16[32,1024]{1,0:T(8,128)(2,1)S(1)} %get-tuple-element.136, bf16[32,1024]{1,0:T(8,128)(2,1)S(1)} %get-tuple-element.134), kind=kOutput, calls=%fused_computation.2 | convolution fusion | flops 405110784 | bytes 5177344 | tf_op jit(solution)/shard_map/dot_general | solution.py:153
  43.5 1.9 %collective-permute-done.15 = f32[32,1024]{1,0:T(8,128)S(1)} collective-permute-done((f32[32,1024]{1,0:T(8,128)S(1)}, f32[32,1024]{1,0:T(8,128)S(1)}, u32[]{:S(2)}, u32[]{:S(2)}) %collective-permute-start.15) | collective-permute-done | bytes 131104 | tf_op jit(solution)/shard_map/ppermute | solution.py:19
  45.4 0.8 %fusion.97 = f32[96,1024]{1,0:T(8,128)S(1)} fusion(bf16[2048,1024]{1,0:T(8,128)(2,1)S(1)} %get-tuple-element.73, bf16[32,1024]{1,0:T(8,128)(2,1)S(1)} %get-tuple-element.132, bf16[32,1024]{1,0:T(8,128)(2,1)S(1)} %get-tuple-element.133, bf16[32,1024]{1,0:T(8,128)(2,1)S(1)} %get-tuple-element.131), kind=kOutput, calls=%fused_computation.118 | convolution fusion | flops 405012480 | bytes 4784128 | tf_op jit(solution)/shard_map/dot_general | solution.py:153
  47.3 0.8 %convolution_add_fusion.1 = f32[96,1024]{1,0:T(8,128)S(1)} fusion(f32[96,1024]{1,0:T(8,128)S(1)} %fusion.97, bf16[2048,1024]{1,0:T(8,128)(2,1)S(1)} %get-tuple-element.77, bf16[32,1024]{1,0:T(8,128)(2,1)S(1)} %get-tuple-element.128, bf16[32,1024]{1,0:T(8,128)(2,1)S(1)} %get-tuple-element.129, bf16[32,1024]{1,0:T(8,128)(2,1)S(1)} %get-tuple-element.127), kind=kOutput, calls=%fused_computation.1 | convolution fusion | flops 405110784 | bytes 5177344 | tf_op jit(solution)/shard_map/dot_general | solution.py:153
  48.1 0.8 %fusion.120 = f32[96,1024]{1,0:T(8,128)S(1)} fusion(bf16[2048,1024]{1,0:T(8,128)(2,1)S(1)} %shard_map.67, bf16[32,1024]{1,0:T(8,128)(2,1)S(1)} %get-tuple-element.114, bf16[32,1024]{1,0:T(8,128)(2,1)S(1)} %get-tuple-element.113, bf16[32,1024]{1,0:T(8,128)(2,1)S(1)} %get-tuple-element.117), kind=kOutput, calls=%fused_computation.141 | convolution fusion | flops 405012480 | bytes 4784128 | tf_op jit(solution)/shard_map/dot_general | solution.py:153
  49.0 0.8 %convolution_add_fusion = f32[96,1024]{1,0:T(8,128)S(1)} fusion(f32[96,1024]{1,0:T(8,128)S(1)} %fusion.120, bf16[2048,1024]{1,0:T(8,128)(2,1)S(1)} %shard_map.68, bf16[32,1024]{1,0:T(8,128)(2,1)S(1)} %get-tuple-element.115, bf16[32,1024]{1,0:T(8,128)(2,1)S(1)} %get-tuple-element.116, bf16[32,1024]{1,0:T(8,128)(2,1)S(1)} %get-tuple-element.112), kind=kOutput, calls=%fused_computation | convolution fusion | flops 405110784 | bytes 5177344 | tf_op jit(solution)/shard_map/dot_general | solution.py:153
  50.3 0.9 %collective-permute-done.17 = f32[32]{0:T(128)S(1)} collective-permute-done((f32[32]{0:T(128)S(1)}, f32[32]{0:T(128)S(1)}, u32[]{:S(2)}, u32[]{:S(2)}) %collective-permute-start.17) | collective-permute-done | bytes 160 | tf_op jit(solution)/shard_map/ppermute | solution.py:19
  (86 shorter events, 11.3 us)
Async XLA Ops:
  1.4 8.1 %collective-permute-start = (f32[72,256]{1,0:T(8,128)S(1)}, f32[72,256]{1,0:T(8,128)S(1)}, u32[]{:S(2)}, u32[]{:S(2)}) collective-permute-start(f32[72,256]{1,0:T(8,128)S(1)} %select_maximum_fusion.part_ref), channel_id=1, source_target_pairs={{0,8},{1,9},{2,10},{3,11},{4,12},{5,13},{6,14},{7,15},{8,0},{9,1},... | collective-permute-start | bytes 221192 | tf_op jit(solution)/shard_map/ppermute | solution.py:19
  6.3 7.7 %collective-permute-start.4 = (f32[65,256]{1,0:T(8,128)S(1)}, f32[65,256]{1,0:T(8,128)S(1)}, u32[]{:S(2)}, u32[]{:S(2)}) collective-permute-start(f32[65,256]{1,0:T(8,128)S(1)} %get-tuple-element.49), channel_id=1, source_target_pairs={{0,2},{1,3},{2,0},{3,1},{4,6},{5,7},{6,4},{7,5},{8,10},{9,11},{10,... | collective-permute-start | bytes 199688 | tf_op jit(solution)/shard_map/ppermute | solution.py:19
  7.9 4.7 %collective-permute-start.1 = (f32[65,256]{1,0:T(8,128)S(1)}, f32[65,256]{1,0:T(8,128)S(1)}, u32[]{:S(2)}, u32[]{:S(2)}) collective-permute-start(f32[65,256]{1,0:T(8,128)S(1)} %get-tuple-element.49), channel_id=1, source_target_pairs={{0,4},{1,5},{2,6},{3,7},{4,0},{5,1},{6,2},{7,3},{8,12},{9,13},{10,... | collective-permute-start | bytes 199688 | tf_op jit(solution)/shard_map/ppermute | solution.py:19
  9.5 4.4 %collective-permute-start.2 = (f32[72,256]{1,0:T(8,128)S(1)}, f32[72,256]{1,0:T(8,128)S(1)}, u32[]{:S(2)}, u32[]{:S(2)}) collective-permute-start(f32[72,256]{1,0:T(8,128)S(1)} %collective-permute-done.part_ref), channel_id=1, source_target_pairs={{0,4},{1,5},{2,6},{3,7},{4,0},{5,1},{6,2},{7,3},{8,12},{9,13},{10,... | collective-permute-start | bytes 221192 | tf_op jit(solution)/shard_map/ppermute | solution.py:19
  10.2 8.7 %collective-permute-start.6 = (f32[65,256]{1,0:T(8,128)S(1)}, f32[65,256]{1,0:T(8,128)S(1)}, u32[]{:S(2)}, u32[]{:S(2)}) collective-permute-start(f32[65,256]{1,0:T(8,128)S(1)} %get-tuple-element.53), channel_id=1, source_target_pairs={{0,2},{1,3},{2,0},{3,1},{4,6},{5,7},{6,4},{7,5},{8,10},{9,11},{10,... | collective-permute-start | bytes 199688 | tf_op jit(solution)/shard_map/ppermute | solution.py:19
  14.0 5.2 %collective-permute-start.5 = (f32[65,512]{1,0:T(8,128)S(1)}, f32[65,512]{1,0:T(8,128)S(1)}, u32[]{:S(2)}, u32[]{:S(2)}) collective-permute-start(f32[65,512]{1,0:T(8,128)S(1)} %get-tuple-element.52), channel_id=1, source_target_pairs={{0,2},{1,3},{2,0},{3,1},{4,6},{5,7},{6,4},{7,5},{8,10},{9,11},{10,... | collective-permute-start | bytes 399368 | tf_op jit(solution)/shard_map/ppermute | solution.py:19
  15.6 1.7 %collective-permute-start.3 = (f32[64,1024]{1,0:T(8,128)S(1)}, f32[64,1024]{1,0:T(8,128)S(1)}, u32[]{:S(2)}, u32[]{:S(2)}) collective-permute-start(f32[64,1024]{1,0:T(8,128)S(1)} %slice.225), channel_id=1, source_target_pairs={{0,1},{1,0},{2,3},{3,2},{4,5},{5,4},{6,7},{7,6},{8,9},{9,8},{10,11... | collective-permute-start | bytes 786440 | tf_op jit(solution)/shard_map/ppermute | solution.py:19
  19.3 1.8 %collective-permute-start.7 = (f32[64,1024]{1,0:T(8,128)S(1)}, f32[64,1024]{1,0:T(8,128)S(1)}, u32[]{:S(2)}, u32[]{:S(2)}) collective-permute-start(f32[64,1024]{1,0:T(8,128)S(1)} %slice.230), channel_id=1, source_target_pairs={{0,1},{1,0},{2,3},{3,2},{4,5},{5,4},{6,7},{7,6},{8,9},{9,8},{10,11... | collective-permute-start | bytes 786440 | tf_op jit(solution)/shard_map/ppermute | solution.py:19
  22.8 5.8 %collective-permute-start.9 = (f32[32,1024]{1,0:T(8,128)S(1)}, f32[32,1024]{1,0:T(8,128)S(1)}, u32[]{:S(2)}, u32[]{:S(2)}) collective-permute-start(f32[32,1024]{1,0:T(8,128)S(1)} %get-tuple-element.64), channel_id=1, source_target_pairs={{0,2},{1,3},{2,0},{3,1},{4,6},{5,7},{6,4},{7,5},{8,10},{9,11},{10,... | collective-permute-start | bytes 393224 | tf_op jit(solution)/shard_map/ppermute | solution.py:19
  24.2 1.4 %collective-permute-start.8 = (f32[32,1024]{1,0:T(8,128)S(1)}, f32[32,1024]{1,0:T(8,128)S(1)}, u32[]{:S(2)}, u32[]{:S(2)}) collective-permute-start(f32[32,1024]{1,0:T(8,128)S(1)} %get-tuple-element.64), channel_id=1, source_target_pairs={{0,1},{1,0},{2,3},{3,2},{4,5},{5,4},{6,7},{7,6},{8,9},{9,8},{10,11... | collective-permute-start | bytes 393224 | tf_op jit(solution)/shard_map/ppermute | solution.py:19
  28.6 1.3 %collective-permute-start.10 = (f32[32,1024]{1,0:T(8,128)S(1)}, f32[32,1024]{1,0:T(8,128)S(1)}, u32[]{:S(2)}, u32[]{:S(2)}) collective-permute-start(f32[32,1024]{1,0:T(8,128)S(1)} %collective-permute-done.9), channel_id=1, source_target_pairs={{0,1},{1,0},{2,3},{3,2},{4,5},{5,4},{6,7},{7,6},{8,9},{9,8},{10,11... | collective-permute-start | bytes 393224 | tf_op jit(solution)/shard_map/ppermute | solution.py:19
  31.4 5.6 %collective-permute-start.12 = (f32[32,1024]{1,0:T(8,128)S(1)}, f32[32,1024]{1,0:T(8,128)S(1)}, u32[]{:S(2)}, u32[]{:S(2)}) collective-permute-start(f32[32,1024]{1,0:T(8,128)S(1)} %get-tuple-element.78), channel_id=1, source_target_pairs={{0,2},{1,3},{2,0},{3,1},{4,6},{5,7},{6,4},{7,5},{8,10},{9,11},{10,... | collective-permute-start | bytes 393224 | tf_op jit(solution)/shard_map/ppermute | solution.py:19
  33.0 1.4 %collective-permute-start.11 = (f32[32,1024]{1,0:T(8,128)S(1)}, f32[32,1024]{1,0:T(8,128)S(1)}, u32[]{:S(2)}, u32[]{:S(2)}) collective-permute-start(f32[32,1024]{1,0:T(8,128)S(1)} %get-tuple-element.78), channel_id=1, source_target_pairs={{0,1},{1,0},{2,3},{3,2},{4,5},{5,4},{6,7},{7,6},{8,9},{9,8},{10,11... | collective-permute-start | bytes 393224 | tf_op jit(solution)/shard_map/ppermute | solution.py:19
  37.0 1.3 %collective-permute-start.13 = (f32[32,1024]{1,0:T(8,128)S(1)}, f32[32,1024]{1,0:T(8,128)S(1)}, u32[]{:S(2)}, u32[]{:S(2)}) collective-permute-start(f32[32,1024]{1,0:T(8,128)S(1)} %collective-permute-done.12), channel_id=1, source_target_pairs={{0,1},{1,0},{2,3},{3,2},{4,5},{5,4},{6,7},{7,6},{8,9},{9,8},{10,11... | collective-permute-start | bytes 393224 | tf_op jit(solution)/shard_map/ppermute | solution.py:19
  39.7 5.6 %collective-permute-start.15 = (f32[32,1024]{1,0:T(8,128)S(1)}, f32[32,1024]{1,0:T(8,128)S(1)}, u32[]{:S(2)}, u32[]{:S(2)}) collective-permute-start(f32[32,1024]{1,0:T(8,128)S(1)} %get-tuple-element.88), channel_id=1, source_target_pairs={{0,2},{1,3},{2,0},{3,1},{4,6},{5,7},{6,4},{7,5},{8,10},{9,11},{10,... | collective-permute-start | bytes 393224 | tf_op jit(solution)/shard_map/ppermute | solution.py:19
  41.2 1.4 %collective-permute-start.14 = (f32[32,1024]{1,0:T(8,128)S(1)}, f32[32,1024]{1,0:T(8,128)S(1)}, u32[]{:S(2)}, u32[]{:S(2)}) collective-permute-start(f32[32,1024]{1,0:T(8,128)S(1)} %get-tuple-element.88), channel_id=1, source_target_pairs={{0,1},{1,0},{2,3},{3,2},{4,5},{5,4},{6,7},{7,6},{8,9},{9,8},{10,11... | collective-permute-start | bytes 393224 | tf_op jit(solution)/shard_map/ppermute | solution.py:19
  45.4 1.3 %collective-permute-start.16 = (f32[32,1024]{1,0:T(8,128)S(1)}, f32[32,1024]{1,0:T(8,128)S(1)}, u32[]{:S(2)}, u32[]{:S(2)}) collective-permute-start(f32[32,1024]{1,0:T(8,128)S(1)} %collective-permute-done.15), channel_id=1, source_target_pairs={{0,1},{1,0},{2,3},{3,2},{4,5},{5,4},{6,7},{7,6},{8,9},{9,8},{10,11... | collective-permute-start | bytes 393224 | tf_op jit(solution)/shard_map/ppermute | solution.py:19
  50.1 1.2 %collective-permute-start.17 = (f32[32]{0:T(128)S(1)}, f32[32]{0:T(128)S(1)}, u32[]{:S(2)}, u32[]{:S(2)}) collective-permute-start(f32[32]{0:T(128)S(1)} %get-tuple-element.96), channel_id=1, source_target_pairs={{0,1},{1,0},{2,3},{3,2},{4,5},{5,4},{6,7},{7,6},{8,9},{9,8},{10,11... | collective-permute-start | bytes 392 | tf_op jit(solution)/shard_map/ppermute | solution.py:19

commit v25 on v24

--- a/solution.py
+++ b/solution.py
@@ -189,7 +189,7 @@
         fence = lax.optimization_barrier
         tile = []
 
-        def build(x, total):
+        def build(x, total, right):
             piece, total = build_piece(x[:feats], scale, right, x[feats:], total)
             tile.append(piece)
             return total
@@ -210,15 +210,22 @@
             mine = join(block[:used], by_far[:used], by_near)
             noise, mine = mine[-1:], mine[:-1]
             across = swap(mine, n, 1)
-            my_applied = build(mine, noise * mine[feats:])
-            my_applied = build(across, my_applied)
-            side_last, side_far, my_applied = fence((side_last, side_far, my_applied))
+            zeros = jnp.zeros((probes, mine.shape[1]), jnp.float32)
+            near_own = build(mine, noise * mine[feats:], right)
+            across, near_own = fence((across, near_own))
+            (right_across,) = prepare(across, scale)
+            near_other = build(mine, zeros, right_across)
+            near_came = swap(near_other, n, 1)
+            side_last, side_far, near_other = fence((side_last, side_far, near_other))
             beside = join(side_own, side_far, side_last)
             noise_beside, beside = beside[-1:], beside[:-1]
             beside_across = swap(beside, n, 1)
-            my_far = build(beside, jnp.zeros_like(my_applied))
-            my_far = build(beside_across, my_far)
-            my_applied = my_applied + my_far
+            far_other = build(beside, zeros, right_across)
+            far_came = swap(far_other, n, 1)
+            far_own = build(beside, zeros, right)
+            far_came, near_came, far_own = fence((far_came, near_came, far_own))
+            my_far = far_own + far_came
+            my_applied = near_own + near_came + my_far
             first = [mine, across, beside, beside_across]
             far_rows = [beside[:feats], beside_across[:feats]]
         else:
@@ -229,7 +236,7 @@
             (right,), noise, first = prepare(mine, scale), mine[-1:], arrivals(mine[:-1])
             my_applied = noise * first[0][feats:]
             for x in first:
-                my_applied = build(x, my_applied)
+                my_applied = build(x, my_applied, right)
             my_far, far_rows = my_applied, []
         cols = noise.shape[1]
         starts = [x[feats:] for x in first]
@@ -268,12 +275,42 @@
                 far = far + apply_piece(pieces[-1], tile[-1])
             return collect(far), collect(near) + collect(far) + noise * x, join(*pieces), curve
 
+        def exchange_sums(x, direction):
+            nonlocal right_far
+            arrived = swap(x, n, inner[0])
+            parts, passed = fence((parts_of(x), x))
+            across = swap(passed, n, 1)
+            near_other = collect(apply_parts(parts, tile[1]))
+            near_came = swap(near_other, n, 1)
+            parts, near_other = fence((parts, near_other))
+            near_own = apply_parts(parts, tile[0])
+            if len(far_tile) < len(far_rows):
+                rows, columns, near_own = fence((far_rows[len(far_tile)], far_rows[0], near_own))
+                if right_far is None:
+                    (right_far,) = prepare(columns, scale)
+                (piece,) = build_piece(rows, scale, right_far)
+                piece, right_far, near_own = fence((piece, right_far, near_own))
+                far_tile.append(piece)
+            arrived, near_own = fence((arrived, near_own))
+            arrived_across = swap(arrived, n, 1)
+            parts = parts_of(arrived)
+            far_other = collect(apply_parts(parts, tile[2]))
+            far_came = swap(far_other, n, 1)
+            parts, far_other = fence((parts, far_other))
+            far_own = apply_parts(parts, tile[3])
+            before = join(x, across, arrived)
+            curve = jnp.sum(direction[:, : before.shape[1]] * before, axis=1)
+            curve, far_own, arrived_across = fence((curve, far_own, arrived_across))
+            curve = curve + jnp.sum(direction[:, before.shape[1] :] * arrived_across, axis=1)
+            far = collect(far_own) + far_came
+            return far, collect(near_own) + near_came + far + noise * x, join(before, arrived_across), curve
+
         residual = direction = join(*starts)
         my_solution = jnp.zeros_like(direction[:, :width])
         norm_now = jnp.sum(residual * residual, axis=1)
         my_image, far_image = my_applied, my_far
         for iteration in range(ITERS - 1):
-            far_next, my_next, applied, curve = exchange(my_applied, direction)
+            far_next, my_next, applied, curve = (exchange_sums if far_rows else exchange)(my_applied, direction)
             step_size = (norm_now / curve)[:, None]
             my_solution = my_solution + step_size * direction[:, :width]
             residual = residual - step_size * applied

time: 52.2 us -> 54.8 us (1.050)
  starting transfers between devices: 16.4 us -> 19 us
    ppermute x18 -> x26, starting transfers between devices: 16.4 us -> 19 us  [swap(): return lax.ppermute(x, 'blk', [(i, i ^ stride) for i in range(n)])]
    ppermute x18 -> x26, waiting for transfers between devices: 8.65 us -> 8.34 us  [swap(): return lax.ppermute(x, 'blk', [(i, i ^ stride) for i in range(n)])]
    pallas_call x10 -> x11, Pallas kernels: 8.81 us -> 8.95 us  [call(): pl.pallas_call(kernel, out_shape=outs, in_specs=[whole] * len(args), out_...]
  transfers between devices with their start and end apart: 18 -> 26, of which waited for: 13 -> 6; matrix products, arithmetic and copies ran while one was open for 18% -> 26% of each run, Pallas kernels for 14% -> 16%
where the time goes in v25:
time: 54.8 us; the launch traced here: 54.6 us
  starting transfers between devices  19 us (35%)
  matrix products  11.3 us (21%)
  Pallas kernels  8.95 us (16%)
  waiting for transfers between devices  8.34 us (15%)
  other arithmetic  5.52 us (10%)
  between operations  1.13 us (2%)
    ppermute x26, starting transfers between devices, swap(): return lax.ppermute(x, 'blk', [(i, i ^ stride) for i in range(n)])  19 us
    dot_general x14, matrix products, apply_parts(): jnp.dot(jnp.concatenate([parts, parts], axis=1), piece, preferred_element...  11.3 us
    pallas_call x11, Pallas kernels, call(): pl.pallas_call(kernel, out_shape=outs, in_specs=[whole] * len(args), out_...  8.95 us
    ppermute x26, waiting for transfers between devices, swap(): return lax.ppermute(x, 'blk', [(i, i ^ stride) for i in range(n)])  8.34 us
  transfers between devices with their start and end apart: 26, of which 6 were waited for; matrix products, arithmetic and copies ran while one was open for 26% of the time, Pallas kernels for 16%

profile of v25, /device:TPU:0, one launch (start us, length us, event | category | flops | bytes accessed | tf_op | source)
XLA Modules:
  0.0 54.6 jit_solution(10367998587583072778)
XLA Ops:
  0.6 0.8 %select_maximum_fusion.part_ref = f32[72,256]{1,0:T(8,128)S(1)} fusion(f32[1,256]{1,0:T(1,128)} %bitcast.32, f32[32,256]{1,0:T(8,128)} %param.7, f32[32,256]{1,0:T(8,128)} %param.4), kind=kLoop, calls=%fused_computation.205 | loop fusion | flops 73728 | bytes 140288 | tf_op jit(solution)/shard_map/concatenate | solution.py:188
  1.4 4.0 %collective-permute-start = (f32[72,256]{1,0:T(8,128)S(1)}, f32[72,256]{1,0:T(8,128)S(1)}, u32[]{:S(2)}, u32[]{:S(2)}) collective-permute-start(f32[72,256]{1,0:T(8,128)S(1)} %select_maximum_fusion.part_ref), channel_id=1, source_target_pairs={{0,8},{1,9},{2,10},{3,11},{4,12},{5,13},{6,14},{7,15},{8,0},{9,1},... | collective-permute-start | bytes 221192 | tf_op jit(solution)/shard_map/ppermute | solution.py:19
  6.3 1.6 %collective-permute-start.4 = (f32[65,256]{1,0:T(8,128)S(1)}, f32[65,256]{1,0:T(8,128)S(1)}, u32[]{:S(2)}, u32[]{:S(2)}) collective-permute-start(f32[65,256]{1,0:T(8,128)S(1)} %get-tuple-element.62), channel_id=1, source_target_pairs={{0,2},{1,3},{2,0},{3,1},{4,6},{5,7},{6,4},{7,5},{8,10},{9,11},{10,... | collective-permute-start | bytes 199688 | tf_op jit(solution)/shard_map/ppermute | solution.py:19
  7.9 1.6 %collective-permute-start.1 = (f32[65,256]{1,0:T(8,128)S(1)}, f32[65,256]{1,0:T(8,128)S(1)}, u32[]{:S(2)}, u32[]{:S(2)}) collective-permute-start(f32[65,256]{1,0:T(8,128)S(1)} %get-tuple-element.62), channel_id=1, source_target_pairs={{0,4},{1,5},{2,6},{3,7},{4,0},{5,1},{6,2},{7,3},{8,12},{9,13},{10,... | collective-permute-start | bytes 199688 | tf_op jit(solution)/shard_map/ppermute | solution.py:19
  10.2 1.9 %collective-permute-start.6 = (f32[65,256]{1,0:T(8,128)S(1)}, f32[65,256]{1,0:T(8,128)S(1)}, u32[]{:S(2)}, u32[]{:S(2)}) collective-permute-start(f32[65,256]{1,0:T(8,128)S(1)} %get-tuple-element.71), channel_id=1, source_target_pairs={{0,2},{1,3},{2,0},{3,1},{4,6},{5,7},{6,4},{7,5},{8,10},{9,11},{10,... | collective-permute-start | bytes 199688 | tf_op jit(solution)/shard_map/ppermute | solution.py:19
  12.6 1.2 %collective-permute-done.2 = f32[72,256]{1,0:T(8,128)S(1)} collective-permute-done((f32[72,256]{1,0:T(8,128)S(1)}, f32[72,256]{1,0:T(8,128)S(1)}, u32[]{:S(2)}, u32[]{:S(2)}) %collective-permute-start.2) | collective-permute-done | bytes 73760 | tf_op jit(solution)/shard_map/ppermute | solution.py:19
  14.0 1.5 %collective-permute-start.5 = (f32[65,512]{1,0:T(8,128)S(1)}, f32[65,512]{1,0:T(8,128)S(1)}, u32[]{:S(2)}, u32[]{:S(2)}) collective-permute-start(f32[65,512]{1,0:T(8,128)S(1)} %get-tuple-element.70), channel_id=1, source_target_pairs={{0,2},{1,3},{2,0},{3,1},{4,6},{5,7},{6,4},{7,5},{8,10},{9,11},{10,... | collective-permute-start | bytes 399368 | tf_op jit(solution)/shard_map/ppermute | solution.py:19
  15.7 1.6 %shard_map.62 = (bf16[2048,1024]{1,0:T(8,128)(2,1)S(1)}, f32[32,1024]{1,0:T(8,128)S(1)}) custom-call(f32[32,1024]{1,0:T(8,128)S(1)} %get-tuple-element.150.rows_ref, f32[32,1]{1,0:T(8,128)S(1)} %copy.6.scale_ref, bf16[256,1024]{1,0:T(8,128)(2,1)S(1)} %constant_dynamic-update-slice_fusion.right_ref, f32[32,1024]{1,0:T(8,128)S(1)} %get-tuple-element.151.refs_0_, ...), custom_call_target="tpu_custom_call" | custom-call | flops 872415232 | bytes 4194304 | tf_op jit(solution)/shard_map/pallas_call | solution.py:115
  17.4 1.6 %shard_map.64 = (bf16[2048,1024]{1,0:T(8,128)(2,1)S(1)}, f32[32,1024]{1,0:T(8,128)S(1)}) custom-call(f32[32,1024]{1,0:T(8,128)S(1)} %get-tuple-element.150.rows_ref, f32[32,1]{1,0:T(8,128)S(1)} %copy.6.scale_ref, bf16[256,1024]{1,0:T(8,128)(2,1)S(1)} %shard_map.63.right_ref, f32[32,1024]{1,0:T(8,128)S(1)} %get-tuple-element.151.refs_0_, ...), custom_call_target="tpu_custom_call" | custom-call | flops 872415232 | bytes 4194304 | tf_op jit(solution)/shard_map/pallas_call | solution.py:115
  19.6 1.6 %shard_map.65 = (bf16[2048,1024]{1,0:T(8,128)(2,1)S(1)}, f32[32,1024]{1,0:T(8,128)S(1)}) custom-call(f32[32,1024]{1,0:T(8,128)S(1)} %get-tuple-element.87.rows_ref.part_ref, f32[32,1]{1,0:T(8,128)S(1)} %copy.6.scale_ref, bf16[256,1024]{1,0:T(8,128)(2,1)S(1)} %shard_map.63.right_ref, f32[32,1024]{1,0:T(8,128)S(1)} %get-tuple-element.148.refs_0_, ...), custom_call_target="tpu_custom_call" | custom-call | flops 872415232 | bytes 4194304 | tf_op jit(solution)/shard_map/pallas_call | solution.py:115
  21.9 1.6 %shard_map.66 = (bf16[2048,1024]{1,0:T(8,128)(2,1)S(1)}, f32[32,1024]{1,0:T(8,128)S(1)}) custom-call(f32[32,1024]{1,0:T(8,128)S(1)} %get-tuple-element.87.rows_ref.part_ref, f32[32,1]{1,0:T(8,128)S(1)} %copy.6.scale_ref, bf16[256,1024]{1,0:T(8,128)(2,1)S(1)} %constant_dynamic-update-slice_fusion.right_ref, f32[32,1024]{1,0:T(8,128)S(1)} %get-tuple-element.148.refs_0_, ...), custom_call_target="tpu_custom_call" | custom-call | flops 872415232 | bytes 4194304 | tf_op jit(solution)/shard_map/pallas_call | solution.py:115
  23.5 1.1 %collective-permute-start.11 = (f32[32,1024]{1,0:T(8,128)S(1)}, f32[32,1024]{1,0:T(8,128)S(1)}, u32[]{:S(2)}, u32[]{:S(2)}) collective-permute-start(f32[32,1024]{1,0:T(8,128)S(1)} %get-tuple-element.81), channel_id=1, source_target_pairs={{0,2},{1,3},{2,0},{3,1},{4,6},{5,7},{6,4},{7,5},{8,10},{9,11},{10,... | collective-permute-start | bytes 393224 | tf_op jit(solution)/shard_map/ppermute | solution.py:19
  24.7 0.8 %fusion.6 = f32[96,1024]{1,0:T(8,128)S(1)} fusion(bf16[2048,1024]{1,0:T(8,128)(2,1)S(1)} %get-tuple-element.83, bf16[96,1024]{1,0:T(8,128)(2,1)S(1)} %pad_maximum_fusion.2), kind=kOutput, calls=%fused_computation.21 | convolution fusion | flops 403439616 | bytes 4784128 | tf_op jit(solution)/shard_map/dot_general | solution.py:153
  26.1 0.8 %fusion.10 = f32[96,1024]{1,0:T(8,128)S(1)} fusion(bf16[2048,1024]{1,0:T(8,128)(2,1)S(1)} %get-tuple-element.85, bf16[96,1024]{1,0:T(8,128)(2,1)S(1)} %pad_maximum_fusion.2), kind=kOutput, calls=%fused_computation.25 | convolution fusion | flops 403439616 | bytes 4784128 | tf_op jit(solution)/shard_map/dot_general | solution.py:153
  27.1 1.1 %shard_map.68 = bf16[2048,1024]{1,0:T(8,128)(2,1)S(1)} custom-call(f32[32,1024]{1,0:T(8,128)S(1)} %get-tuple-element.87.rows_ref.part_ref, f32[32,1]{1,0:T(8,128)S(1)} %copy.6.scale_ref, bf16[256,1024]{1,0:T(8,128)(2,1)S(1)} %shard_map.67.right_ref), custom_call_target="tpu_custom_call" | custom-call | flops 872415232 | bytes 4194304 | tf_op jit(solution)/shard_map/pallas_call | solution.py:115
  28.1 0.9 %collective-permute-done.11 = f32[32,1024]{1,0:T(8,128)S(1)} collective-permute-done((f32[32,1024]{1,0:T(8,128)S(1)}, f32[32,1024]{1,0:T(8,128)S(1)}, u32[]{:S(2)}, u32[]{:S(2)}) %collective-permute-start.11) | collective-permute-done | bytes 131104 | tf_op jit(solution)/shard_map/ppermute | solution.py:19
  29.1 0.8 %fusion.14 = f32[96,1024]{1,0:T(8,128)S(1)} fusion(bf16[2048,1024]{1,0:T(8,128)(2,1)S(1)} %get-tuple-element.91, bf16[32,1024]{1,0:T(8,128)(2,1)S(1)} %get-tuple-element.166, bf16[32,1024]{1,0:T(8,128)(2,1)S(1)} %get-tuple-element.167, bf16[32,1024]{1,0:T(8,128)(2,1)S(1)} %get-tuple-element.165), kind=kOutput, calls=%fused_computation.29 | convolution fusion | flops 405012480 | bytes 4784128 | tf_op jit(solution)/shard_map/dot_general | solution.py:153
  30.5 0.8 %fusion.26 = f32[96,1024]{1,0:T(8,128)S(1)} fusion(bf16[2048,1024]{1,0:T(8,128)(2,1)S(1)} %get-tuple-element.93, bf16[96,1024]{1,0:T(8,128)(2,1)S(1)} %pad_maximum_fusion.3), kind=kOutput, calls=%fused_computation.41 | convolution fusion | flops 403439616 | bytes 4784128 | tf_op jit(solution)/shard_map/dot_general | solution.py:153
  32.3 1.1 %collective-permute-start.16 = (f32[32,1024]{1,0:T(8,128)S(1)}, f32[32,1024]{1,0:T(8,128)S(1)}, u32[]{:S(2)}, u32[]{:S(2)}) collective-permute-start(f32[32,1024]{1,0:T(8,128)S(1)} %get-tuple-element.98), channel_id=1, source_target_pairs={{0,2},{1,3},{2,0},{3,1},{4,6},{5,7},{6,4},{7,5},{8,10},{9,11},{10,... | collective-permute-start | bytes 393224 | tf_op jit(solution)/shard_map/ppermute | solution.py:19
  33.4 0.8 %fusion.30 = f32[96,1024]{1,0:T(8,128)S(1)} fusion(bf16[2048,1024]{1,0:T(8,128)(2,1)S(1)} %get-tuple-element.83, bf16[96,1024]{1,0:T(8,128)(2,1)S(1)} %pad_maximum_fusion.4), kind=kOutput, calls=%fused_computation.45 | convolution fusion | flops 403439616 | bytes 4784128 | tf_op jit(solution)/shard_map/dot_general | solution.py:153
  35.0 0.8 %fusion.34 = f32[96,1024]{1,0:T(8,128)S(1)} fusion(bf16[2048,1024]{1,0:T(8,128)(2,1)S(1)} %get-tuple-element.85, bf16[96,1024]{1,0:T(8,128)(2,1)S(1)} %pad_maximum_fusion.4), kind=kOutput, calls=%fused_computation.49 | convolution fusion | flops 403439616 | bytes 4784128 | tf_op jit(solution)/shard_map/dot_general | solution.py:153
  35.8 1.1 %shard_map.69 = bf16[2048,1024]{1,0:T(8,128)(2,1)S(1)} custom-call(f32[32,1024]{1,0:T(8,128)S(1)} %get-tuple-element.101.rows_ref, f32[32,1]{1,0:T(8,128)S(1)} %copy.6.scale_ref, bf16[256,1024]{1,0:T(8,128)(2,1)S(1)} %shard_map.67.right_ref), custom_call_target="tpu_custom_call" | custom-call | flops 872415232 | bytes 4194304 | tf_op jit(solution)/shard_map/pallas_call | solution.py:115
  36.9 0.8 %collective-permute-done.16 = f32[32,1024]{1,0:T(8,128)S(1)} collective-permute-done((f32[32,1024]{1,0:T(8,128)S(1)}, f32[32,1024]{1,0:T(8,128)S(1)}, u32[]{:S(2)}, u32[]{:S(2)}) %collective-permute-start.16) | collective-permute-done | bytes 131104 | tf_op jit(solution)/shard_map/ppermute | solution.py:19
  37.8 0.8 %fusion.38 = f32[96,1024]{1,0:T(8,128)S(1)} fusion(bf16[2048,1024]{1,0:T(8,128)(2,1)S(1)} %get-tuple-element.91, bf16[32,1024]{1,0:T(8,128)(2,1)S(1)} %get-tuple-element.161, bf16[32,1024]{1,0:T(8,128)(2,1)S(1)} %get-tuple-element.162, bf16[32,1024]{1,0:T(8,128)(2,1)S(1)} %get-tuple-element.160), kind=kOutput, calls=%fused_computation.53 | convolution fusion | flops 405012480 | bytes 4784128 | tf_op jit(solution)/shard_map/dot_general | solution.py:153
  40.8 0.8 %fusion.54 = f32[96,1024]{1,0:T(8,128)S(1)} fusion(bf16[2048,1024]{1,0:T(8,128)(2,1)S(1)} %get-tuple-element.83, bf16[96,1024]{1,0:T(8,128)(2,1)S(1)} %pad_maximum_fusion.6), kind=kOutput, calls=%fused_computation.69 | convolution fusion | flops 403439616 | bytes 4784128 | tf_op jit(solution)/shard_map/dot_general | solution.py:153
  41.7 1.1 %collective-permute-start.21 = (f32[32,1024]{1,0:T(8,128)S(1)}, f32[32,1024]{1,0:T(8,128)S(1)}, u32[]{:S(2)}, u32[]{:S(2)}) collective-permute-start(f32[32,1024]{1,0:T(8,128)S(1)} %get-tuple-element.111), channel_id=1, source_target_pairs={{0,2},{1,3},{2,0},{3,1},{4,6},{5,7},{6,4},{7,5},{8,10},{9,11},{10,... | collective-permute-start | bytes 393224 | tf_op jit(solution)/shard_map/ppermute | solution.py:19
  43.1 0.8 %fusion.58 = f32[96,1024]{1,0:T(8,128)S(1)} fusion(bf16[2048,1024]{1,0:T(8,128)(2,1)S(1)} %get-tuple-element.85, bf16[96,1024]{1,0:T(8,128)(2,1)S(1)} %pad_maximum_fusion.6), kind=kOutput, calls=%fused_computation.73 | convolution fusion | flops 403439616 | bytes 4784128 | tf_op jit(solution)/shard_map/dot_general | solution.py:153
  44.0 3.7 %collective-permute-done.21 = f32[32,1024]{1,0:T(8,128)S(1)} collective-permute-done((f32[32,1024]{1,0:T(8,128)S(1)}, f32[32,1024]{1,0:T(8,128)S(1)}, u32[]{:S(2)}, u32[]{:S(2)}) %collective-permute-start.21) | collective-permute-done | bytes 131104 | tf_op jit(solution)/shard_map/ppermute | solution.py:19
  47.7 0.8 %fusion.62 = f32[96,1024]{1,0:T(8,128)S(1)} fusion(bf16[2048,1024]{1,0:T(8,128)(2,1)S(1)} %get-tuple-element.91, bf16[32,1024]{1,0:T(8,128)(2,1)S(1)} %get-tuple-element.156, bf16[32,1024]{1,0:T(8,128)(2,1)S(1)} %get-tuple-element.157, bf16[32,1024]{1,0:T(8,128)(2,1)S(1)} %get-tuple-element.155), kind=kOutput, calls=%fused_computation.77 | convolution fusion | flops 405012480 | bytes 4784128 | tf_op jit(solution)/shard_map/dot_general | solution.py:153
  50.7 0.8 %fusion.78 = f32[96,1024]{1,0:T(8,128)S(1)} fusion(bf16[2048,1024]{1,0:T(8,128)(2,1)S(1)} %shard_map.68, bf16[32,1024]{1,0:T(8,128)(2,1)S(1)} %get-tuple-element.143, bf16[32,1024]{1,0:T(8,128)(2,1)S(1)} %get-tuple-element.142, bf16[32,1024]{1,0:T(8,128)(2,1)S(1)} %get-tuple-element.146), kind=kOutput, calls=%fused_computation.93 | convolution fusion | flops 405012480 | bytes 4784128 | tf_op jit(solution)/shard_map/dot_general | solution.py:153
  51.5 0.8 %convolution_add_fusion = f32[96,1024]{1,0:T(8,128)S(1)} fusion(f32[96,1024]{1,0:T(8,128)S(1)} %fusion.78, bf16[2048,1024]{1,0:T(8,128)(2,1)S(1)} %shard_map.69, bf16[32,1024]{1,0:T(8,128)(2,1)S(1)} %get-tuple-element.144, bf16[32,1024]{1,0:T(8,128)(2,1)S(1)} %get-tuple-element.145, bf16[32,1024]{1,0:T(8,128)(2,1)S(1)} %get-tuple-element.141), kind=kOutput, calls=%fused_computation | convolution fusion | flops 405110784 | bytes 5177344 | tf_op jit(solution)/shard_map/dot_general | solution.py:153
  52.7 1.1 %collective-permute-done.25 = f32[32]{0:T(128)S(1)} collective-permute-done((f32[32]{0:T(128)S(1)}, f32[32]{0:T(128)S(1)}, u32[]{:S(2)}, u32[]{:S(2)}) %collective-permute-start.25) | collective-permute-done | bytes 160 | tf_op jit(solution)/shard_map/ppermute | solution.py:19
  (108 shorter events, 12.9 us)
Async XLA Ops:
  1.4 8.1 %collective-permute-start = (f32[72,256]{1,0:T(8,128)S(1)}, f32[72,256]{1,0:T(8,128)S(1)}, u32[]{:S(2)}, u32[]{:S(2)}) collective-permute-start(f32[72,256]{1,0:T(8,128)S(1)} %select_maximum_fusion.part_ref), channel_id=1, source_target_pairs={{0,8},{1,9},{2,10},{3,11},{4,12},{5,13},{6,14},{7,15},{8,0},{9,1},... | collective-permute-start | bytes 221192 | tf_op jit(solution)/shard_map/ppermute | solution.py:19
  6.3 7.7 %collective-permute-start.4 = (f32[65,256]{1,0:T(8,128)S(1)}, f32[65,256]{1,0:T(8,128)S(1)}, u32[]{:S(2)}, u32[]{:S(2)}) collective-permute-start(f32[65,256]{1,0:T(8,128)S(1)} %get-tuple-element.62), channel_id=1, source_target_pairs={{0,2},{1,3},{2,0},{3,1},{4,6},{5,7},{6,4},{7,5},{8,10},{9,11},{10,... | collective-permute-start | bytes 199688 | tf_op jit(solution)/shard_map/ppermute | solution.py:19
  7.9 4.7 %collective-permute-start.1 = (f32[65,256]{1,0:T(8,128)S(1)}, f32[65,256]{1,0:T(8,128)S(1)}, u32[]{:S(2)}, u32[]{:S(2)}) collective-permute-start(f32[65,256]{1,0:T(8,128)S(1)} %get-tuple-element.62), channel_id=1, source_target_pairs={{0,4},{1,5},{2,6},{3,7},{4,0},{5,1},{6,2},{7,3},{8,12},{9,13},{10,... | collective-permute-start | bytes 199688 | tf_op jit(solution)/shard_map/ppermute | solution.py:19
  9.5 4.4 %collective-permute-start.2 = (f32[72,256]{1,0:T(8,128)S(1)}, f32[72,256]{1,0:T(8,128)S(1)}, u32[]{:S(2)}, u32[]{:S(2)}) collective-permute-start(f32[72,256]{1,0:T(8,128)S(1)} %collective-permute-done.part_ref), channel_id=1, source_target_pairs={{0,4},{1,5},{2,6},{3,7},{4,0},{5,1},{6,2},{7,3},{8,12},{9,13},{10,... | collective-permute-start | bytes 221192 | tf_op jit(solution)/shard_map/ppermute | solution.py:19
  10.2 9.4 %collective-permute-start.6 = (f32[65,256]{1,0:T(8,128)S(1)}, f32[65,256]{1,0:T(8,128)S(1)}, u32[]{:S(2)}, u32[]{:S(2)}) collective-permute-start(f32[65,256]{1,0:T(8,128)S(1)} %get-tuple-element.71), channel_id=1, source_target_pairs={{0,2},{1,3},{2,0},{3,1},{4,6},{5,7},{6,4},{7,5},{8,10},{9,11},{10,... | collective-permute-start | bytes 199688 | tf_op jit(solution)/shard_map/ppermute | solution.py:19
  14.0 5.5 %collective-permute-start.5 = (f32[65,512]{1,0:T(8,128)S(1)}, f32[65,512]{1,0:T(8,128)S(1)}, u32[]{:S(2)}, u32[]{:S(2)}) collective-permute-start(f32[65,512]{1,0:T(8,128)S(1)} %get-tuple-element.70), channel_id=1, source_target_pairs={{0,2},{1,3},{2,0},{3,1},{4,6},{5,7},{6,4},{7,5},{8,10},{9,11},{10,... | collective-permute-start | bytes 399368 | tf_op jit(solution)/shard_map/ppermute | solution.py:19
  15.5 1.7 %collective-permute-start.3 = (f32[64,1024]{1,0:T(8,128)S(1)}, f32[64,1024]{1,0:T(8,128)S(1)}, u32[]{:S(2)}, u32[]{:S(2)}) collective-permute-start(f32[64,1024]{1,0:T(8,128)S(1)} %slice.285), channel_id=1, source_target_pairs={{0,1},{1,0},{2,3},{3,2},{4,5},{5,4},{6,7},{7,6},{8,9},{9,8},{10,11... | collective-permute-start | bytes 786440 | tf_op jit(solution)/shard_map/ppermute | solution.py:19
  19.0 4.5 %collective-permute-start.9 = (f32[32,1024]{1,0:T(8,128)S(1)}, f32[32,1024]{1,0:T(8,128)S(1)}, u32[]{:S(2)}, u32[]{:S(2)}) collective-permute-start(f32[32,1024]{1,0:T(8,128)S(1)} %get-tuple-element.72), channel_id=1, source_target_pairs={{0,1},{1,0},{2,3},{3,2},{4,5},{5,4},{6,7},{7,6},{8,9},{9,8},{10,11... | collective-permute-start | bytes 393224 | tf_op jit(solution)/shard_map/ppermute | solution.py:19
  21.2 2.3 %collective-permute-start.8 = (f32[32,1024]{1,0:T(8,128)S(1)}, f32[32,1024]{1,0:T(8,128)S(1)}, u32[]{:S(2)}, u32[]{:S(2)}) collective-permute-start(f32[32,1024]{1,0:T(8,128)S(1)} %get-tuple-element.76), channel_id=1, source_target_pairs={{0,1},{1,0},{2,3},{3,2},{4,5},{5,4},{6,7},{7,6},{8,9},{9,8},{10,11... | collective-permute-start | bytes 393224 | tf_op jit(solution)/shard_map/ppermute | solution.py:19
  21.3 10.2 %collective-permute-start.7 = (f32[64,1024]{1,0:T(8,128)S(1)}, f32[64,1024]{1,0:T(8,128)S(1)}, u32[]{:S(2)}, u32[]{:S(2)}) collective-permute-start(f32[64,1024]{1,0:T(8,128)S(1)} %slice.288), channel_id=1, source_target_pairs={{0,1},{1,0},{2,3},{3,2},{4,5},{5,4},{6,7},{7,6},{8,9},{9,8},{10,11... | collective-permute-start | bytes 786440 | tf_op jit(solution)/shard_map/ppermute | solution.py:19
  23.5 5.5 %collective-permute-start.11 = (f32[32,1024]{1,0:T(8,128)S(1)}, f32[32,1024]{1,0:T(8,128)S(1)}, u32[]{:S(2)}, u32[]{:S(2)}) collective-permute-start(f32[32,1024]{1,0:T(8,128)S(1)} %get-tuple-element.81), channel_id=1, source_target_pairs={{0,2},{1,3},{2,0},{3,1},{4,6},{5,7},{6,4},{7,5},{8,10},{9,11},{10,... | collective-permute-start | bytes 393224 | tf_op jit(solution)/shard_map/ppermute | solution.py:19
  25.5 6.6 %collective-permute-start.13 = (f32[32,1024]{1,0:T(8,128)S(1)}, f32[32,1024]{1,0:T(8,128)S(1)}, u32[]{:S(2)}, u32[]{:S(2)}) collective-permute-start(f32[32,1024]{1,0:T(8,128)S(1)} %fusion.129), channel_id=1, source_target_pairs={{0,1},{1,0},{2,3},{3,2},{4,5},{5,4},{6,7},{7,6},{8,9},{9,8},{10,11... | collective-permute-start | bytes 393224 | tf_op jit(solution)/shard_map/ppermute | solution.py:19
  25.6 5.7 %collective-permute-start.10 = (f32[32,1024]{1,0:T(8,128)S(1)}, f32[32,1024]{1,0:T(8,128)S(1)}, u32[]{:S(2)}, u32[]{:S(2)}) collective-permute-start(f32[32,1024]{1,0:T(8,128)S(1)} %get-tuple-element.81), channel_id=1, source_target_pairs={{0,1},{1,0},{2,3},{3,2},{4,5},{5,4},{6,7},{7,6},{8,9},{9,8},{10,11... | collective-permute-start | bytes 393224 | tf_op jit(solution)/shard_map/ppermute | solution.py:19
  29.0 2.5 %collective-permute-start.12 = (f32[32,1024]{1,0:T(8,128)S(1)}, f32[32,1024]{1,0:T(8,128)S(1)}, u32[]{:S(2)}, u32[]{:S(2)}) collective-permute-start(f32[32,1024]{1,0:T(8,128)S(1)} %collective-permute-done.11), channel_id=1, source_target_pairs={{0,1},{1,0},{2,3},{3,2},{4,5},{5,4},{6,7},{7,6},{8,9},{9,8},{10,11... | collective-permute-start | bytes 393224 | tf_op jit(solution)/shard_map/ppermute | solution.py:19
  29.9 2.2 %collective-permute-start.14 = (f32[32,1024]{1,0:T(8,128)S(1)}, f32[32,1024]{1,0:T(8,128)S(1)}, u32[]{:S(2)}, u32[]{:S(2)}) collective-permute-start(f32[32,1024]{1,0:T(8,128)S(1)} %fusion.128), channel_id=1, source_target_pairs={{0,1},{1,0},{2,3},{3,2},{4,5},{5,4},{6,7},{7,6},{8,9},{9,8},{10,11... | collective-permute-start | bytes 393224 | tf_op jit(solution)/shard_map/ppermute | solution.py:19
  32.3 5.5 %collective-permute-start.16 = (f32[32,1024]{1,0:T(8,128)S(1)}, f32[32,1024]{1,0:T(8,128)S(1)}, u32[]{:S(2)}, u32[]{:S(2)}) collective-permute-start(f32[32,1024]{1,0:T(8,128)S(1)} %get-tuple-element.98), channel_id=1, source_target_pairs={{0,2},{1,3},{2,0},{3,1},{4,6},{5,7},{6,4},{7,5},{8,10},{9,11},{10,... | collective-permute-start | bytes 393224 | tf_op jit(solution)/shard_map/ppermute | solution.py:19
  34.3 6.3 %collective-permute-start.18 = (f32[32,1024]{1,0:T(8,128)S(1)}, f32[32,1024]{1,0:T(8,128)S(1)}, u32[]{:S(2)}, u32[]{:S(2)}) collective-permute-start(f32[32,1024]{1,0:T(8,128)S(1)} %fusion.127), channel_id=1, source_target_pairs={{0,1},{1,0},{2,3},{3,2},{4,5},{5,4},{6,7},{7,6},{8,9},{9,8},{10,11... | collective-permute-start | bytes 393224 | tf_op jit(solution)/shard_map/ppermute | solution.py:19
  34.6 5.4 %collective-permute-start.15 = (f32[32,1024]{1,0:T(8,128)S(1)}, f32[32,1024]{1,0:T(8,128)S(1)}, u32[]{:S(2)}, u32[]{:S(2)}) collective-permute-start(f32[32,1024]{1,0:T(8,128)S(1)} %get-tuple-element.98), channel_id=1, source_target_pairs={{0,1},{1,0},{2,3},{3,2},{4,5},{5,4},{6,7},{7,6},{8,9},{9,8},{10,11... | collective-permute-start | bytes 393224 | tf_op jit(solution)/shard_map/ppermute | solution.py:19
  37.7 2.4 %collective-permute-start.17 = (f32[32,1024]{1,0:T(8,128)S(1)}, f32[32,1024]{1,0:T(8,128)S(1)}, u32[]{:S(2)}, u32[]{:S(2)}) collective-permute-start(f32[32,1024]{1,0:T(8,128)S(1)} %collective-permute-done.16), channel_id=1, source_target_pairs={{0,1},{1,0},{2,3},{3,2},{4,5},{5,4},{6,7},{7,6},{8,9},{9,8},{10,11... | collective-permute-start | bytes 393224 | tf_op jit(solution)/shard_map/ppermute | solution.py:19
  38.6 2.0 %collective-permute-start.19 = (f32[32,1024]{1,0:T(8,128)S(1)}, f32[32,1024]{1,0:T(8,128)S(1)}, u32[]{:S(2)}, u32[]{:S(2)}) collective-permute-start(f32[32,1024]{1,0:T(8,128)S(1)} %fusion.126), channel_id=1, source_target_pairs={{0,1},{1,0},{2,3},{3,2},{4,5},{5,4},{6,7},{7,6},{8,9},{9,8},{10,11... | collective-permute-start | bytes 393224 | tf_op jit(solution)/shard_map/ppermute | solution.py:19
  41.6 10.7 %collective-permute-start.23 = (f32[32,1024]{1,0:T(8,128)S(1)}, f32[32,1024]{1,0:T(8,128)S(1)}, u32[]{:S(2)}, u32[]{:S(2)}) collective-permute-start(f32[32,1024]{1,0:T(8,128)S(1)} %fusion.124), channel_id=1, source_target_pairs={{0,1},{1,0},{2,3},{3,2},{4,5},{5,4},{6,7},{7,6},{8,9},{9,8},{10,11... | collective-permute-start | bytes 393224 | tf_op jit(solution)/shard_map/ppermute | solution.py:19
  41.7 5.9 %collective-permute-start.21 = (f32[32,1024]{1,0:T(8,128)S(1)}, f32[32,1024]{1,0:T(8,128)S(1)}, u32[]{:S(2)}, u32[]{:S(2)}) collective-permute-start(f32[32,1024]{1,0:T(8,128)S(1)} %get-tuple-element.111), channel_id=1, source_target_pairs={{0,2},{1,3},{2,0},{3,1},{4,6},{5,7},{6,4},{7,5},{8,10},{9,11},{10,... | collective-permute-start | bytes 393224 | tf_op jit(solution)/shard_map/ppermute | solution.py:19
  42.8 7.1 %collective-permute-start.20 = (f32[32,1024]{1,0:T(8,128)S(1)}, f32[32,1024]{1,0:T(8,128)S(1)}, u32[]{:S(2)}, u32[]{:S(2)}) collective-permute-start(f32[32,1024]{1,0:T(8,128)S(1)} %get-tuple-element.111), channel_id=1, source_target_pairs={{0,1},{1,0},{2,3},{3,2},{4,5},{5,4},{6,7},{7,6},{8,9},{9,8},{10,11... | collective-permute-start | bytes 393224 | tf_op jit(solution)/shard_map/ppermute | solution.py:19
  47.6 2.4 %collective-permute-start.22 = (f32[32,1024]{1,0:T(8,128)S(1)}, f32[32,1024]{1,0:T(8,128)S(1)}, u32[]{:S(2)}, u32[]{:S(2)}) collective-permute-start(f32[32,1024]{1,0:T(8,128)S(1)} %collective-permute-done.21), channel_id=1, source_target_pairs={{0,1},{1,0},{2,3},{3,2},{4,5},{5,4},{6,7},{7,6},{8,9},{9,8},{10,11... | collective-permute-start | bytes 393224 | tf_op jit(solution)/shard_map/ppermute | solution.py:19
  48.5 3.8 %collective-permute-start.24 = (f32[32,1024]{1,0:T(8,128)S(1)}, f32[32,1024]{1,0:T(8,128)S(1)}, u32[]{:S(2)}, u32[]{:S(2)}) collective-permute-start(f32[32,1024]{1,0:T(8,128)S(1)} %fusion.123), channel_id=1, source_target_pairs={{0,1},{1,0},{2,3},{3,2},{4,5},{5,4},{6,7},{7,6},{8,9},{9,8},{10,11... | collective-permute-start | bytes 393224 | tf_op jit(solution)/shard_map/ppermute | solution.py:19
  52.7 1.2 %collective-permute-start.25 = (f32[32]{0:T(128)S(1)}, f32[32]{0:T(128)S(1)}, u32[]{:S(2)}, u32[]{:S(2)}) collective-permute-start(f32[32]{0:T(128)S(1)} %get-tuple-element.122), channel_id=1, source_target_pairs={{0,1},{1,0},{2,3},{3,2},{4,5},{5,4},{6,7},{7,6},{8,9},{9,8},{10,11... | collective-permute-start | bytes 392 | tf_op jit(solution)/shard_map/ppermute | solution.py:19

commit v26 on v24

--- a/solution.py
+++ b/solution.py
@@ -144,6 +144,10 @@
     return call(build_kernel, outs, *args, **cost)
 
 
+def stack(vectors):
+    return jnp.concatenate([parts_of(x) for x in vectors], axis=0)
+
+
 def parts_of(vectors):
     high, mid, low = split(vectors, 3)
     return jnp.concatenate([high, mid, low], axis=0)
@@ -155,6 +159,11 @@
 
 def apply_piece(vectors, piece):
     return apply_parts(parts_of(vectors), piece)
+
+
+def cut(x):
+    middle = x.shape[1] // 2
+    return x[:, :middle], x[:, middle:]
 
 
 def collect(total):
@@ -184,8 +193,8 @@
 
         scale = (POINT_SCALE / lengthscale)[:, None]
         used = feats + probes + 1
-        spare = jnp.zeros((-used % 8, width), jnp.float32)
-        block = lax.optimization_barrier(jnp.concatenate([points, targets, jnp.pad(noise_var[None, :], ((0, -used % 8), (0, 0)))], axis=0))
+        spare = jnp.pad(noise_var[None, :], ((0, -used % 8), (0, 0)))
+        block = lax.optimization_barrier(jnp.concatenate([points, targets, spare], axis=0))
         fence = lax.optimization_barrier
         tile = []
 
@@ -235,23 +244,45 @@
         starts = [x[feats:] for x in first]
 
         far_tile, right_far = [], None
-
-        def exchange(x, direction):
+        first_core = lax.axis_index("blk") % 2 == 0
+
+        def paired(x):
+            low, high = cut(x)
+            return jnp.where(first_core, low, high), jnp.where(first_core, high, low)
+
+        def far_own_product(vectors):
+            return [collect(x) for x in jnp.split(apply_parts(stack(vectors), far_tile[0]), len(vectors))]
+
+        def far_cross_product(vectors):
+            low, high = zip(*[cut(x) for x in vectors])
+            terms = [apply_parts(stack(x), piece) for x, piece in zip((low, high), far_tile[1])]
+            return [join(*[collect(x) for x in pair]) for pair in zip(*[jnp.split(x, len(vectors)) for x in terms])]
+
+        def far_build():
             nonlocal right_far
+            if right_far is None:
+                (right_far,) = prepare(far_rows[0], scale)
+                return build_piece(far_rows[0], scale, right_far)[0]
+            return [build_piece(x, scale, y)[0] for x, y in zip(cut(far_rows[1]), paired(right_far))]
+
+        def exchange(x, residual, direction, last):
+            nonlocal far_rows
             parts, passed = fence((parts_of(x), x))
-            pieces, sent = [x, swap(passed, n, 1)], [x]
+            pieces, sent, known = [x, swap(passed, n, 1)], [x], []
             near = fence(apply_parts(parts, tile[0]))
             near = fence(near + apply_piece(pieces[1], tile[1]))
             far = jnp.zeros_like(near) if len(inner) == 1 else None
             for k, stride in enumerate(inner[:-1]):
                 arrived = swap(join(*sent), n, stride)
-                if len(far_tile) < len(far_rows):
-                    rows, columns, near = fence((far_rows[len(far_tile)], far_rows[0], near))
-                    if right_far is None:
-                        (right_far,) = prepare(columns, scale)
-                    (piece,) = build_piece(rows, scale, right_far)
-                    piece, right_far, near = fence((piece, right_far, near))
+                if far_rows and not last:
+                    far_rows, near = fence((far_rows, near))
+                    piece, near = fence((far_build(), near))
                     far_tile.append(piece)
+                elif far_rows:
+                    state, near = fence(([residual, direction], near))
+                    known = [far_own_product([v[:, 2 * cols : 3 * cols] for v in state])]
+                    known.append(far_cross_product([v[:, 3 * cols :] for v in state]))
+                    known, near = fence((known, near))
                 arrived, near = fence((arrived, near))
                 sent.append(arrived)
                 pieces.append(arrived)
@@ -260,20 +291,24 @@
                 pieces.append(swap(arrived, n, 1))
                 if k < len(inner) - 2:
                     far = fence(far + apply_piece(pieces[-1], tile[3 + 2 * k]))
+            if known:
+                own_term, far = fence((far_own_product([arrived])[0], far))
             before = join(*pieces[:-1])
             curve = jnp.sum(direction[:, : before.shape[1]] * before, axis=1)
             curve, far = fence((curve, far))
             curve = curve + jnp.sum(direction[:, before.shape[1] :] * pieces[-1], axis=1)
             if len(inner) > 1:
                 far = far + apply_piece(pieces[-1], tile[-1])
-            return collect(far), collect(near) + collect(far) + noise * x, join(*pieces), curve
+            if known:
+                known = [[*known[0], own_term], [*known[1], *far_cross_product(pieces[-1:])]]
+            return collect(far), collect(near) + collect(far) + noise * x, join(*pieces), curve, known
 
         residual = direction = join(*starts)
         my_solution = jnp.zeros_like(direction[:, :width])
         norm_now = jnp.sum(residual * residual, axis=1)
         my_image, far_image = my_applied, my_far
         for iteration in range(ITERS - 1):
-            far_next, my_next, applied, curve = exchange(my_applied, direction)
+            far_next, my_next, applied, curve, known = exchange(my_applied, residual, direction, iteration == ITERS - 2)
             step_size = (norm_now / curve)[:, None]
             my_solution = my_solution + step_size * direction[:, :width]
             residual = residual - step_size * applied
@@ -287,9 +322,10 @@
             norm_now = norm_next
         mine = direction[:, :cols]
         if far_rows:
-            side, beside = direction[:, 2 * cols : 3 * cols], direction[:, 3 * cols :]
-            image = collect(apply_piece(side, far_tile[0]) + apply_piece(beside, far_tile[1])) + noise_beside * side
-            curve = add_up(jnp.sum(mine * (my_applied + my_far) + side * image, axis=1), n, [1])
+            own_part, cross = [of_res + ratio * of_dir - step_size * of_app for of_res, of_dir, of_app in known]
+            side = direction[:, 2 * cols : 3 * cols]
+            far_terms = side * (own_part + noise_beside * side) + 2.0 * join(*paired(side)) * cross
+            curve = add_up(jnp.sum(mine * (my_applied + my_far) + far_terms, axis=1), n, [1])
         else:
             curve = add_up(jnp.sum(mine * my_applied, axis=1), n, inner)
         step_size = (norm_now / curve)[:, None]

time: 52.2 us -> 52.6 us (level)
  waiting for transfers between devices: 8.65 us -> 6.36 us
  matrix products: 11.5 us -> 13.1 us
  other arithmetic: 5.41 us -> 5.94 us
    ppermute x18, waiting for transfers between devices: 8.65 us -> 6.36 us  [swap(): return lax.ppermute(x, 'blk', [(i, i ^ stride) for i in range(n)])]
    dot_general x14 -> x18, matrix products: 11.5 us -> 13.1 us  [apply_parts(): jnp.dot(jnp.concatenate([parts, parts], axis=1), piece, preferred_element...]
    pallas_call x10 -> x11, Pallas kernels: 8.81 us -> 8.68 us  [call(): pl.pallas_call(kernel, out_shape=outs, in_specs=[whole] * len(args), out_...]
  transfers between devices with their start and end apart: 18 -> 18, of which waited for: 13 -> 11; matrix products, arithmetic and copies ran while one was open for 18% -> 24% of each run, Pallas kernels for 14% -> 14%
where the time goes in v26:
time: 52.6 us; the launch traced here: 52.4 us
  starting transfers between devices  16.8 us (32%)
  matrix products  13.1 us (25%)
  Pallas kernels  8.68 us (17%)
  waiting for transfers between devices  6.36 us (12%)
  other arithmetic  5.94 us (11%)
  between operations  1.21 us (2%)
    ppermute x18, starting transfers between devices, swap(): return lax.ppermute(x, 'blk', [(i, i ^ stride) for i in range(n)])  16.8 us
    dot_general x18, matrix products, apply_parts(): jnp.dot(jnp.concatenate([parts, parts], axis=1), piece, preferred_element...  13.1 us
    pallas_call x11, Pallas kernels, call(): pl.pallas_call(kernel, out_shape=outs, in_specs=[whole] * len(args), out_...  8.68 us
    ppermute x18, waiting for transfers between devices, swap(): return lax.ppermute(x, 'blk', [(i, i ^ stride) for i in range(n)])  6.36 us
  transfers between devices with their start and end apart: 18, of which 11 were waited for; matrix products, arithmetic and copies ran while one was open for 24% of the time, Pallas kernels for 14%

profile of v26, /device:TPU:0, one launch (start us, length us, event | category | flops | bytes accessed | tf_op | source)
XLA Modules:
  0.0 52.4 jit_solution(11273830671046319564)
XLA Ops:
  0.6 0.8 %select_maximum_fusion.part_ref = f32[72,256]{1,0:T(8,128)S(1)} fusion(f32[1,256]{1,0:T(1,128)} %bitcast.36, f32[32,256]{1,0:T(8,128)} %param.7, f32[32,256]{1,0:T(8,128)} %param.4), kind=kLoop, calls=%fused_computation.312 | loop fusion | flops 73728 | bytes 140288 | tf_op jit(solution)/shard_map/concatenate | solution.py:197
  1.4 4.0 %collective-permute-start = (f32[72,256]{1,0:T(8,128)S(1)}, f32[72,256]{1,0:T(8,128)S(1)}, u32[]{:S(2)}, u32[]{:S(2)}) collective-permute-start(f32[72,256]{1,0:T(8,128)S(1)} %select_maximum_fusion.part_ref), channel_id=1, source_target_pairs={{0,8},{1,9},{2,10},{3,11},{4,12},{5,13},{6,14},{7,15},{8,0},{9,1},... | collective-permute-start | bytes 221192 | tf_op jit(solution)/shard_map/ppermute | solution.py:19
  6.3 1.6 %collective-permute-start.4 = (f32[65,256]{1,0:T(8,128)S(1)}, f32[65,256]{1,0:T(8,128)S(1)}, u32[]{:S(2)}, u32[]{:S(2)}) collective-permute-start(f32[65,256]{1,0:T(8,128)S(1)} %get-tuple-element.59), channel_id=1, source_target_pairs={{0,2},{1,3},{2,0},{3,1},{4,6},{5,7},{6,4},{7,5},{8,10},{9,11},{10,... | collective-permute-start | bytes 199688 | tf_op jit(solution)/shard_map/ppermute | solution.py:19
  7.9 1.6 %collective-permute-start.1 = (f32[65,256]{1,0:T(8,128)S(1)}, f32[65,256]{1,0:T(8,128)S(1)}, u32[]{:S(2)}, u32[]{:S(2)}) collective-permute-start(f32[65,256]{1,0:T(8,128)S(1)} %get-tuple-element.59), channel_id=1, source_target_pairs={{0,4},{1,5},{2,6},{3,7},{4,0},{5,1},{6,2},{7,3},{8,12},{9,13},{10,... | collective-permute-start | bytes 199688 | tf_op jit(solution)/shard_map/ppermute | solution.py:19
  10.2 1.9 %collective-permute-start.6 = (f32[65,256]{1,0:T(8,128)S(1)}, f32[65,256]{1,0:T(8,128)S(1)}, u32[]{:S(2)}, u32[]{:S(2)}) collective-permute-start(f32[65,256]{1,0:T(8,128)S(1)} %get-tuple-element.63), channel_id=1, source_target_pairs={{0,2},{1,3},{2,0},{3,1},{4,6},{5,7},{6,4},{7,5},{8,10},{9,11},{10,... | collective-permute-start | bytes 199688 | tf_op jit(solution)/shard_map/ppermute | solution.py:19
  12.6 1.2 %collective-permute-done.2 = f32[72,256]{1,0:T(8,128)S(1)} collective-permute-done((f32[72,256]{1,0:T(8,128)S(1)}, f32[72,256]{1,0:T(8,128)S(1)}, u32[]{:S(2)}, u32[]{:S(2)}) %collective-permute-start.2) | collective-permute-done | bytes 73760 | tf_op jit(solution)/shard_map/ppermute | solution.py:19
  14.0 1.5 %collective-permute-start.5 = (f32[65,512]{1,0:T(8,128)S(1)}, f32[65,512]{1,0:T(8,128)S(1)}, u32[]{:S(2)}, u32[]{:S(2)}) collective-permute-start(f32[65,512]{1,0:T(8,128)S(1)} %get-tuple-element.62), channel_id=1, source_target_pairs={{0,2},{1,3},{2,0},{3,1},{4,6},{5,7},{6,4},{7,5},{8,10},{9,11},{10,... | collective-permute-start | bytes 399368 | tf_op jit(solution)/shard_map/ppermute | solution.py:19
  15.7 1.6 %shard_map.62 = (bf16[2048,1024]{1,0:T(8,128)(2,1)S(1)}, f32[32,1024]{1,0:T(8,128)S(1)}) custom-call(f32[32,1024]{1,0:T(8,128)S(1)} %get-tuple-element.157.rows_ref, f32[32,1]{1,0:T(8,128)S(1)} %copy.6.scale_ref, bf16[256,1024]{1,0:T(8,128)(2,1)S(1)} %constant_dynamic-update-slice_fusion.right_ref, f32[32,1024]{1,0:T(8,128)S(1)} %get-tuple-element.158.refs_0_, ...), custom_call_target="tpu_custom_call" | custom-call | flops 872415232 | bytes 4194304 | tf_op jit(solution)/shard_map/pallas_call | solution.py:115
  17.3 1.5 %shard_map.63 = (bf16[2048,1024]{1,0:T(8,128)(2,1)S(1)}, f32[32,1024]{1,0:T(8,128)S(1)}) custom-call(f32[32,1024]{1,0:T(8,128)S(1)} %get-tuple-element.162.rows_ref, f32[32,1]{1,0:T(8,128)S(1)} %copy.6.scale_ref, bf16[256,1024]{1,0:T(8,128)(2,1)S(1)} %constant_dynamic-update-slice_fusion.right_ref, f32[32,1024]{1,0:T(8,128)S(1)} %get-tuple-element.161.refs_0_, ...), custom_call_target="tpu_custom_call" | custom-call | flops 872415232 | bytes 4194304 | tf_op jit(solution)/shard_map/pallas_call | solution.py:115
  19.6 1.6 %shard_map.64 = (bf16[2048,1024]{1,0:T(8,128)(2,1)S(1)}, f32[32,1024]{1,0:T(8,128)S(1)}) custom-call(f32[32,1024]{1,0:T(8,128)S(1)} %get-tuple-element.78.rows_ref.part_ref, f32[32,1]{1,0:T(8,128)S(1)} %copy.6.scale_ref, bf16[256,1024]{1,0:T(8,128)(2,1)S(1)} %constant_dynamic-update-slice_fusion.right_ref, f32[32,1024]{1,0:T(8,128)S(1)} %get-tuple-element.154.refs_0_, ...), custom_call_target="tpu_custom_call" | custom-call | flops 872415232 | bytes 4194304 | tf_op jit(solution)/shard_map/pallas_call | solution.py:115
  21.2 1.6 %shard_map.65 = (bf16[2048,1024]{1,0:T(8,128)(2,1)S(1)}, f32[32,1024]{1,0:T(8,128)S(1)}) custom-call(f32[32,1024]{1,0:T(8,128)S(1)} %get-tuple-element.90.rows_ref, f32[32,1]{1,0:T(8,128)S(1)} %copy.6.scale_ref, bf16[256,1024]{1,0:T(8,128)(2,1)S(1)} %constant_dynamic-update-slice_fusion.right_ref, f32[32,1024]{1,0:T(8,128)S(1)} %get-tuple-element.159.refs_0_, ...), custom_call_target="tpu_custom_call" | custom-call | flops 872415232 | bytes 4194304 | tf_op jit(solution)/shard_map/pallas_call | solution.py:115
  22.8 1.3 %collective-permute-start.9 = (f32[32,1024]{1,0:T(8,128)S(1)}, f32[32,1024]{1,0:T(8,128)S(1)}, u32[]{:S(2)}, u32[]{:S(2)}) collective-permute-start(f32[32,1024]{1,0:T(8,128)S(1)} %get-tuple-element.74), channel_id=1, source_target_pairs={{0,2},{1,3},{2,0},{3,1},{4,6},{5,7},{6,4},{7,5},{8,10},{9,11},{10,... | collective-permute-start | bytes 393224 | tf_op jit(solution)/shard_map/ppermute | solution.py:19
  24.4 0.8 %fusion.10 = f32[96,1024]{1,0:T(8,128)S(1)} fusion(bf16[2048,1024]{1,0:T(8,128)(2,1)S(1)} %get-tuple-element.76, bf16[96,1024]{1,0:T(8,128)(2,1)S(1)} %pad_maximum_fusion.2), kind=kOutput, calls=%fused_computation.30 | convolution fusion | flops 403439616 | bytes 4784128 | tf_op jit(solution)/shard_map/dot_general | solution.py:157
  25.6 0.8 %convolution_add_fusion.5 = f32[96,1024]{1,0:T(8,128)S(1)} fusion(f32[96,1024]{1,0:T(8,128)S(1)} %fusion.10, bf16[2048,1024]{1,0:T(8,128)(2,1)S(1)} %get-tuple-element.77, bf16[32,1024]{1,0:T(8,128)(2,1)S(1)} %get-tuple-element.203, bf16[32,1024]{1,0:T(8,128)(2,1)S(1)} %get-tuple-element.204, bf16[32,1024]{1,0:T(8,128)(2,1)S(1)} %get-tuple-element.202), kind=kOutput, calls=%fused_computation.5 | convolution fusion | flops 405110784 | bytes 5177344 | tf_op jit(solution)/shard_map/dot_general | solution.py:157
  26.6 1.1 %shard_map.67 = bf16[2048,1024]{1,0:T(8,128)(2,1)S(1)} custom-call(f32[32,1024]{1,0:T(8,128)S(1)} %get-tuple-element.78.rows_ref.part_ref, f32[32,1]{1,0:T(8,128)S(1)} %copy.6.scale_ref, bf16[256,1024]{1,0:T(8,128)(2,1)S(1)} %shard_map.66.right_ref), custom_call_target="tpu_custom_call" | custom-call | flops 872415232 | bytes 4194304 | tf_op jit(solution)/shard_map/pallas_call | solution.py:115
  27.6 1.0 %collective-permute-done.9 = f32[32,1024]{1,0:T(8,128)S(1)} collective-permute-done((f32[32,1024]{1,0:T(8,128)S(1)}, f32[32,1024]{1,0:T(8,128)S(1)}, u32[]{:S(2)}, u32[]{:S(2)}) %collective-permute-start.9) | collective-permute-done | bytes 131104 | tf_op jit(solution)/shard_map/ppermute | solution.py:19
  28.7 0.8 %fusion.25 = f32[96,1024]{1,0:T(8,128)S(1)} fusion(bf16[2048,1024]{1,0:T(8,128)(2,1)S(1)} %get-tuple-element.82, bf16[32,1024]{1,0:T(8,128)(2,1)S(1)} %get-tuple-element.200, bf16[32,1024]{1,0:T(8,128)(2,1)S(1)} %get-tuple-element.201, bf16[32,1024]{1,0:T(8,128)(2,1)S(1)} %get-tuple-element.199), kind=kOutput, calls=%fused_computation.45 | convolution fusion | flops 405012480 | bytes 4784128 | tf_op jit(solution)/shard_map/dot_general | solution.py:157
  30.4 0.8 %convolution_add_fusion.4 = f32[96,1024]{1,0:T(8,128)S(1)} fusion(f32[96,1024]{1,0:T(8,128)S(1)} %fusion.25, bf16[2048,1024]{1,0:T(8,128)(2,1)S(1)} %get-tuple-element.86, bf16[32,1024]{1,0:T(8,128)(2,1)S(1)} %get-tuple-element.196, bf16[32,1024]{1,0:T(8,128)(2,1)S(1)} %get-tuple-element.197, bf16[32,1024]{1,0:T(8,128)(2,1)S(1)} %get-tuple-element.195), kind=kOutput, calls=%fused_computation.4 | convolution fusion | flops 405110784 | bytes 5177344 | tf_op jit(solution)/shard_map/dot_general | solution.py:157
  31.4 1.5 %collective-permute-start.12 = (f32[32,1024]{1,0:T(8,128)S(1)}, f32[32,1024]{1,0:T(8,128)S(1)}, u32[]{:S(2)}, u32[]{:S(2)}) collective-permute-start(f32[32,1024]{1,0:T(8,128)S(1)} %get-tuple-element.87), channel_id=1, source_target_pairs={{0,2},{1,3},{2,0},{3,1},{4,6},{5,7},{6,4},{7,5},{8,10},{9,11},{10,... | collective-permute-start | bytes 393224 | tf_op jit(solution)/shard_map/ppermute | solution.py:19
  33.1 0.8 %fusion.48 = f32[96,1024]{1,0:T(8,128)S(1)} fusion(bf16[2048,1024]{1,0:T(8,128)(2,1)S(1)} %get-tuple-element.76, bf16[96,1024]{1,0:T(8,128)(2,1)S(1)} %pad_maximum_fusion.3), kind=kOutput, calls=%fused_computation.68 | convolution fusion | flops 403439616 | bytes 4784128 | tf_op jit(solution)/shard_map/dot_general | solution.py:157
  34.4 1.0 %convolution_add_fusion.3 = f32[96,1024]{1,0:T(8,128)S(1)} fusion(f32[96,1024]{1,0:T(8,128)S(1)} %fusion.48, bf16[2048,1024]{1,0:T(8,128)(2,1)S(1)} %get-tuple-element.77, bf16[32,1024]{1,0:T(8,128)(2,1)S(1)} %get-tuple-element.191, bf16[32,1024]{1,0:T(8,128)(2,1)S(1)} %get-tuple-element.192, bf16[32,1024]{1,0:T(8,128)(2,1)S(1)} %get-tuple-element.190), kind=kOutput, calls=%fused_computation.3 | convolution fusion | flops 405110784 | bytes 5177344 | tf_op jit(solution)/shard_map/dot_general | solution.py:157
  37.1 0.8 %fusion.63 = f32[96,1024]{1,0:T(8,128)S(1)} fusion(bf16[2048,1024]{1,0:T(8,128)(2,1)S(1)} %get-tuple-element.82, bf16[32,1024]{1,0:T(8,128)(2,1)S(1)} %get-tuple-element.186, bf16[32,1024]{1,0:T(8,128)(2,1)S(1)} %get-tuple-element.187, bf16[32,1024]{1,0:T(8,128)(2,1)S(1)} %get-tuple-element.185), kind=kOutput, calls=%fused_computation.83 | convolution fusion | flops 405012480 | bytes 4784128 | tf_op jit(solution)/shard_map/dot_general | solution.py:157
  38.8 0.8 %convolution_add_fusion.2 = f32[96,1024]{1,0:T(8,128)S(1)} fusion(f32[96,1024]{1,0:T(8,128)S(1)} %fusion.63, bf16[2048,1024]{1,0:T(8,128)(2,1)S(1)} %get-tuple-element.86, bf16[32,1024]{1,0:T(8,128)(2,1)S(1)} %get-tuple-element.182, bf16[32,1024]{1,0:T(8,128)(2,1)S(1)} %get-tuple-element.183, bf16[32,1024]{1,0:T(8,128)(2,1)S(1)} %get-tuple-element.181), kind=kOutput, calls=%fused_computation.2 | convolution fusion | flops 405110784 | bytes 5177344 | tf_op jit(solution)/shard_map/dot_general | solution.py:157
  39.8 1.5 %collective-permute-start.15 = (f32[32,1024]{1,0:T(8,128)S(1)}, f32[32,1024]{1,0:T(8,128)S(1)}, u32[]{:S(2)}, u32[]{:S(2)}) collective-permute-start(f32[32,1024]{1,0:T(8,128)S(1)} %get-tuple-element.97), channel_id=1, source_target_pairs={{0,2},{1,3},{2,0},{3,1},{4,6},{5,7},{6,4},{7,5},{8,10},{9,11},{10,... | collective-permute-start | bytes 393224 | tf_op jit(solution)/shard_map/ppermute | solution.py:19
  41.5 0.8 %fusion.86 = f32[96,1024]{1,0:T(8,128)S(1)} fusion(bf16[2048,1024]{1,0:T(8,128)(2,1)S(1)} %get-tuple-element.76, bf16[96,1024]{1,0:T(8,128)(2,1)S(1)} %pad_maximum_fusion.4), kind=kOutput, calls=%fused_computation.106 | convolution fusion | flops 403439616 | bytes 4784128 | tf_op jit(solution)/shard_map/dot_general | solution.py:157
  42.8 0.8 %convolution_add_fusion.1 = f32[96,1024]{1,0:T(8,128)S(1)} fusion(f32[96,1024]{1,0:T(8,128)S(1)} %fusion.86, bf16[2048,1024]{1,0:T(8,128)(2,1)S(1)} %get-tuple-element.77, bf16[32,1024]{1,0:T(8,128)(2,1)S(1)} %get-tuple-element.177, bf16[32,1024]{1,0:T(8,128)(2,1)S(1)} %get-tuple-element.178, bf16[32,1024]{1,0:T(8,128)(2,1)S(1)} %get-tuple-element.176), kind=kOutput, calls=%fused_computation.1 | convolution fusion | flops 405110784 | bytes 5177344 | tf_op jit(solution)/shard_map/dot_general | solution.py:157
  43.8 1.0 %fusion = f32[192,1024]{1,0:T(8,128)S(1)} fusion(bf16[2048,1024]{1,0:T(8,128)(2,1)S(1)} %shard_map.67, bf16[192,1024]{1,0:T(8,128)(2,1)S(1)} %fusion.197), kind=kOutput, calls=%fused_computation.6 | convolution fusion | flops 806879232 | bytes 5373952 | tf_op jit(solution)/shard_map/dot_general | solution.py:157
  46.0 0.8 %fusion.229 = f32[96,1024]{1,0:T(8,128)S(1)} fusion(bf16[2048,1024]{1,0:T(8,128)(2,1)S(1)} %get-tuple-element.82, bf16[32,1024]{1,0:T(8,128)(2,1)S(1)} %get-tuple-element.174, bf16[32,1024]{1,0:T(8,128)(2,1)S(1)} %get-tuple-element.175, bf16[32,1024]{1,0:T(8,128)(2,1)S(1)} %get-tuple-element.173), kind=kOutput, calls=%fused_computation.396 | convolution fusion | flops 405012480 | bytes 4784128 | tf_op jit(solution)/shard_map/dot_general | solution.py:157
  46.9 0.8 %fusion.230 = f32[96,1024]{1,0:T(8,128)S(1)} fusion(bf16[2048,1024]{1,0:T(8,128)(2,1)S(1)} %shard_map.67, bf16[32,1024]{1,0:T(8,128)(2,1)S(1)} %get-tuple-element.174, bf16[32,1024]{1,0:T(8,128)(2,1)S(1)} %get-tuple-element.175, bf16[32,1024]{1,0:T(8,128)(2,1)S(1)} %get-tuple-element.173), kind=kOutput, calls=%fused_computation.397 | convolution fusion | flops 405012480 | bytes 4784128 | tf_op jit(solution)/shard_map/dot_general | solution.py:157
  49.2 0.8 %convolution_add_fusion = f32[96,1024]{1,0:T(8,128)S(1)} fusion(f32[96,1024]{1,0:T(8,128)S(1)} %fusion.229, bf16[2048,1024]{1,0:T(8,128)(2,1)S(1)} %get-tuple-element.86, bf16[32,1024]{1,0:T(8,128)(2,1)S(1)} %get-tuple-element.164, bf16[32,1024]{1,0:T(8,128)(2,1)S(1)} %get-tuple-element.165, bf16[32,1024]{1,0:T(8,128)(2,1)S(1)} %get-tuple-element.163), kind=kOutput, calls=%fused_computation | convolution fusion | flops 405110784 | bytes 5177344 | tf_op jit(solution)/shard_map/dot_general | solution.py:157
  50.8 0.8 %collective-permute-done.17 = f32[32]{0:T(128)S(1)} collective-permute-done((f32[32]{0:T(128)S(1)}, f32[32]{0:T(128)S(1)}, u32[]{:S(2)}, u32[]{:S(2)}) %collective-permute-start.17) | collective-permute-done | bytes 160 | tf_op jit(solution)/shard_map/ppermute | solution.py:19
  51.6 0.7 %fusion.209 = (f32[32,256]{1,0:T(8,128)}, f32[32,256]{1,0:T(8,128)}) fusion(f32[32,1024]{1,0:T(8,128)S(1)} %get-tuple-element.117, f32[32,4096]{1,0:T(8,128)S(1)} %get-tuple-element.119, f32[32]{0:T(128)S(1)} %add_divide_fusion, f32[32,4096]{1,0:T(8,128)S(1)} %multiply_add_fusion, f32[32,4096]{1,0:T(8,128)S(1)} %multiply_add_fusion.1, ...), kind=kLoop, calls=%fused_computation.366 | loop fusion | flops 73728 | bytes 262656 | tf_op jit(solution)/shard_map/sub | solution.py:333
  (113 shorter events, 12.7 us)
Async XLA Ops:
  1.4 8.1 %collective-permute-start = (f32[72,256]{1,0:T(8,128)S(1)}, f32[72,256]{1,0:T(8,128)S(1)}, u32[]{:S(2)}, u32[]{:S(2)}) collective-permute-start(f32[72,256]{1,0:T(8,128)S(1)} %select_maximum_fusion.part_ref), channel_id=1, source_target_pairs={{0,8},{1,9},{2,10},{3,11},{4,12},{5,13},{6,14},{7,15},{8,0},{9,1},... | collective-permute-start | bytes 221192 | tf_op jit(solution)/shard_map/ppermute | solution.py:19
  6.3 7.7 %collective-permute-start.4 = (f32[65,256]{1,0:T(8,128)S(1)}, f32[65,256]{1,0:T(8,128)S(1)}, u32[]{:S(2)}, u32[]{:S(2)}) collective-permute-start(f32[65,256]{1,0:T(8,128)S(1)} %get-tuple-element.59), channel_id=1, source_target_pairs={{0,2},{1,3},{2,0},{3,1},{4,6},{5,7},{6,4},{7,5},{8,10},{9,11},{10,... | collective-permute-start | bytes 199688 | tf_op jit(solution)/shard_map/ppermute | solution.py:19
  7.9 4.7 %collective-permute-start.1 = (f32[65,256]{1,0:T(8,128)S(1)}, f32[65,256]{1,0:T(8,128)S(1)}, u32[]{:S(2)}, u32[]{:S(2)}) collective-permute-start(f32[65,256]{1,0:T(8,128)S(1)} %get-tuple-element.59), channel_id=1, source_target_pairs={{0,4},{1,5},{2,6},{3,7},{4,0},{5,1},{6,2},{7,3},{8,12},{9,13},{10,... | collective-permute-start | bytes 199688 | tf_op jit(solution)/shard_map/ppermute | solution.py:19
  9.5 4.4 %collective-permute-start.2 = (f32[72,256]{1,0:T(8,128)S(1)}, f32[72,256]{1,0:T(8,128)S(1)}, u32[]{:S(2)}, u32[]{:S(2)}) collective-permute-start(f32[72,256]{1,0:T(8,128)S(1)} %collective-permute-done.part_ref), channel_id=1, source_target_pairs={{0,4},{1,5},{2,6},{3,7},{4,0},{5,1},{6,2},{7,3},{8,12},{9,13},{10,... | collective-permute-start | bytes 221192 | tf_op jit(solution)/shard_map/ppermute | solution.py:19
  10.2 8.7 %collective-permute-start.6 = (f32[65,256]{1,0:T(8,128)S(1)}, f32[65,256]{1,0:T(8,128)S(1)}, u32[]{:S(2)}, u32[]{:S(2)}) collective-permute-start(f32[65,256]{1,0:T(8,128)S(1)} %get-tuple-element.63), channel_id=1, source_target_pairs={{0,2},{1,3},{2,0},{3,1},{4,6},{5,7},{6,4},{7,5},{8,10},{9,11},{10,... | collective-permute-start | bytes 199688 | tf_op jit(solution)/shard_map/ppermute | solution.py:19
  14.0 5.2 %collective-permute-start.5 = (f32[65,512]{1,0:T(8,128)S(1)}, f32[65,512]{1,0:T(8,128)S(1)}, u32[]{:S(2)}, u32[]{:S(2)}) collective-permute-start(f32[65,512]{1,0:T(8,128)S(1)} %get-tuple-element.62), channel_id=1, source_target_pairs={{0,2},{1,3},{2,0},{3,1},{4,6},{5,7},{6,4},{7,5},{8,10},{9,11},{10,... | collective-permute-start | bytes 399368 | tf_op jit(solution)/shard_map/ppermute | solution.py:19
  15.6 1.7 %collective-permute-start.3 = (f32[64,1024]{1,0:T(8,128)S(1)}, f32[64,1024]{1,0:T(8,128)S(1)}, u32[]{:S(2)}, u32[]{:S(2)}) collective-permute-start(f32[64,1024]{1,0:T(8,128)S(1)} %slice.399), channel_id=1, source_target_pairs={{0,1},{1,0},{2,3},{3,2},{4,5},{5,4},{6,7},{7,6},{8,9},{9,8},{10,11... | collective-permute-start | bytes 786440 | tf_op jit(solution)/shard_map/ppermute | solution.py:19
  19.3 1.8 %collective-permute-start.7 = (f32[64,1024]{1,0:T(8,128)S(1)}, f32[64,1024]{1,0:T(8,128)S(1)}, u32[]{:S(2)}, u32[]{:S(2)}) collective-permute-start(f32[64,1024]{1,0:T(8,128)S(1)} %slice.404), channel_id=1, source_target_pairs={{0,1},{1,0},{2,3},{3,2},{4,5},{5,4},{6,7},{7,6},{8,9},{9,8},{10,11... | collective-permute-start | bytes 786440 | tf_op jit(solution)/shard_map/ppermute | solution.py:19
  22.8 5.8 %collective-permute-start.9 = (f32[32,1024]{1,0:T(8,128)S(1)}, f32[32,1024]{1,0:T(8,128)S(1)}, u32[]{:S(2)}, u32[]{:S(2)}) collective-permute-start(f32[32,1024]{1,0:T(8,128)S(1)} %get-tuple-element.74), channel_id=1, source_target_pairs={{0,2},{1,3},{2,0},{3,1},{4,6},{5,7},{6,4},{7,5},{8,10},{9,11},{10,... | collective-permute-start | bytes 393224 | tf_op jit(solution)/shard_map/ppermute | solution.py:19
  24.2 1.4 %collective-permute-start.8 = (f32[32,1024]{1,0:T(8,128)S(1)}, f32[32,1024]{1,0:T(8,128)S(1)}, u32[]{:S(2)}, u32[]{:S(2)}) collective-permute-start(f32[32,1024]{1,0:T(8,128)S(1)} %get-tuple-element.74), channel_id=1, source_target_pairs={{0,1},{1,0},{2,3},{3,2},{4,5},{5,4},{6,7},{7,6},{8,9},{9,8},{10,11... | collective-permute-start | bytes 393224 | tf_op jit(solution)/shard_map/ppermute | solution.py:19
  28.6 1.3 %collective-permute-start.10 = (f32[32,1024]{1,0:T(8,128)S(1)}, f32[32,1024]{1,0:T(8,128)S(1)}, u32[]{:S(2)}, u32[]{:S(2)}) collective-permute-start(f32[32,1024]{1,0:T(8,128)S(1)} %collective-permute-done.9), channel_id=1, source_target_pairs={{0,1},{1,0},{2,3},{3,2},{4,5},{5,4},{6,7},{7,6},{8,9},{9,8},{10,11... | collective-permute-start | bytes 393224 | tf_op jit(solution)/shard_map/ppermute | solution.py:19
  31.4 5.7 %collective-permute-start.12 = (f32[32,1024]{1,0:T(8,128)S(1)}, f32[32,1024]{1,0:T(8,128)S(1)}, u32[]{:S(2)}, u32[]{:S(2)}) collective-permute-start(f32[32,1024]{1,0:T(8,128)S(1)} %get-tuple-element.87), channel_id=1, source_target_pairs={{0,2},{1,3},{2,0},{3,1},{4,6},{5,7},{6,4},{7,5},{8,10},{9,11},{10,... | collective-permute-start | bytes 393224 | tf_op jit(solution)/shard_map/ppermute | solution.py:19
  33.0 1.4 %collective-permute-start.11 = (f32[32,1024]{1,0:T(8,128)S(1)}, f32[32,1024]{1,0:T(8,128)S(1)}, u32[]{:S(2)}, u32[]{:S(2)}) collective-permute-start(f32[32,1024]{1,0:T(8,128)S(1)} %get-tuple-element.87), channel_id=1, source_target_pairs={{0,1},{1,0},{2,3},{3,2},{4,5},{5,4},{6,7},{7,6},{8,9},{9,8},{10,11... | collective-permute-start | bytes 393224 | tf_op jit(solution)/shard_map/ppermute | solution.py:19
  37.1 1.3 %collective-permute-start.13 = (f32[32,1024]{1,0:T(8,128)S(1)}, f32[32,1024]{1,0:T(8,128)S(1)}, u32[]{:S(2)}, u32[]{:S(2)}) collective-permute-start(f32[32,1024]{1,0:T(8,128)S(1)} %collective-permute-done.12), channel_id=1, source_target_pairs={{0,1},{1,0},{2,3},{3,2},{4,5},{5,4},{6,7},{7,6},{8,9},{9,8},{10,11... | collective-permute-start | bytes 393224 | tf_op jit(solution)/shard_map/ppermute | solution.py:19
  39.8 6.0 %collective-permute-start.15 = (f32[32,1024]{1,0:T(8,128)S(1)}, f32[32,1024]{1,0:T(8,128)S(1)}, u32[]{:S(2)}, u32[]{:S(2)}) collective-permute-start(f32[32,1024]{1,0:T(8,128)S(1)} %get-tuple-element.97), channel_id=1, source_target_pairs={{0,2},{1,3},{2,0},{3,1},{4,6},{5,7},{6,4},{7,5},{8,10},{9,11},{10,... | collective-permute-start | bytes 393224 | tf_op jit(solution)/shard_map/ppermute | solution.py:19
  41.3 1.4 %collective-permute-start.14 = (f32[32,1024]{1,0:T(8,128)S(1)}, f32[32,1024]{1,0:T(8,128)S(1)}, u32[]{:S(2)}, u32[]{:S(2)}) collective-permute-start(f32[32,1024]{1,0:T(8,128)S(1)} %get-tuple-element.97), channel_id=1, source_target_pairs={{0,1},{1,0},{2,3},{3,2},{4,5},{5,4},{6,7},{7,6},{8,9},{9,8},{10,11... | collective-permute-start | bytes 393224 | tf_op jit(solution)/shard_map/ppermute | solution.py:19
  45.8 2.1 %collective-permute-start.16 = (f32[32,1024]{1,0:T(8,128)S(1)}, f32[32,1024]{1,0:T(8,128)S(1)}, u32[]{:S(2)}, u32[]{:S(2)}) collective-permute-start(f32[32,1024]{1,0:T(8,128)S(1)} %collective-permute-done.15), channel_id=1, source_target_pairs={{0,1},{1,0},{2,3},{3,2},{4,5},{5,4},{6,7},{7,6},{8,9},{9,8},{10,11... | collective-permute-start | bytes 393224 | tf_op jit(solution)/shard_map/ppermute | solution.py:19
  50.4 1.2 %collective-permute-start.17 = (f32[32]{0:T(128)S(1)}, f32[32]{0:T(128)S(1)}, u32[]{:S(2)}, u32[]{:S(2)}) collective-permute-start(f32[32]{0:T(128)S(1)} %get-tuple-element.116), channel_id=1, source_target_pairs={{0,1},{1,0},{2,3},{3,2},{4,5},{5,4},{6,7},{7,6},{8,9},{9,8},{10,11... | collective-permute-start | bytes 392 | tf_op jit(solution)/shard_map/ppermute | solution.py:19

commit v27 on v24

--- a/solution.py
+++ b/solution.py
@@ -73,7 +73,6 @@
         probes = vectors_ref.shape[0]
         high, rest = halve(vectors_ref[...])
         mid, rest = halve(rest)
-        twice = jnp.concatenate([high, mid], axis=0)
         thrice = jnp.concatenate([high, mid, rest.astype(jnp.bfloat16)], axis=0)
     steps = [(top, at) for top in range(0, total, block) for at in range(0, cols, step)]
     lefts, powers, parts = {}, {}, {}
@@ -92,10 +91,10 @@
 
     def apply(top, at):
         down, here = slice(top, top + block), slice(at, at + step)
-        high, low = parts.pop((top, at))
-        large = jnp.dot(thrice[:, down], high, preferred_element_type=jnp.float32)
-        small = jnp.dot(twice[:, down], low, preferred_element_type=jnp.float32)
-        term = large[:probes] + ((large[probes : 2 * probes] + small[:probes]) + (large[2 * probes :] + small[probes:]))
+        vectors = jnp.concatenate([thrice[:, down]] * 2, axis=1)
+        both = jnp.concatenate(parts.pop((top, at)), axis=0)
+        term = jnp.dot(vectors, both, preferred_element_type=jnp.float32)
+        term = term[:probes] + (term[probes : 2 * probes] + term[2 * probes :])
         before = sum_ref if top == 0 else out_ref
         out_ref[:, here] = before[:, here] + term
 
@@ -184,8 +183,8 @@
 
         scale = (POINT_SCALE / lengthscale)[:, None]
         used = feats + probes + 1
-        spare = jnp.zeros((-used % 8, width), jnp.float32)
-        block = lax.optimization_barrier(jnp.concatenate([points, targets, jnp.pad(noise_var[None, :], ((0, -used % 8), (0, 0)))], axis=0))
+        spare = jnp.pad(noise_var[None, :], ((0, -used % 8), (0, 0)))
+        block = lax.optimization_barrier(jnp.concatenate([points, targets, spare], axis=0))
         fence = lax.optimization_barrier
         tile = []
 

time: 52.2 us -> 52.2 us (level)
  no operation moved by 1% of the time
where the time goes in v27:
time: 52.2 us; the launch traced here: 52 us
  starting transfers between devices  16.4 us (31%)
  matrix products  11.5 us (22%)
  waiting for transfers between devices  8.73 us (17%)
  Pallas kernels  8.69 us (17%)
  other arithmetic  5.41 us (10%)
  between operations  1 us (2%)
    ppermute x18, starting transfers between devices, swap(): return lax.ppermute(x, 'blk', [(i, i ^ stride) for i in range(n)])  16.4 us
    dot_general x14, matrix products, apply_parts(): jnp.dot(jnp.concatenate([parts, parts], axis=1), piece, preferred_element...  11.5 us
    ppermute x18, waiting for transfers between devices, swap(): return lax.ppermute(x, 'blk', [(i, i ^ stride) for i in range(n)])  8.73 us
    pallas_call x10, Pallas kernels, call(): pl.pallas_call(kernel, out_shape=outs, in_specs=[whole] * len(args), out_...  8.69 us
  transfers between devices with their start and end apart: 18, of which 13 were waited for; matrix products, arithmetic and copies ran while one was open for 18% of the time, Pallas kernels for 14%

profile of v27, /device:TPU:0, one launch (start us, length us, event | category | flops | bytes accessed | tf_op | source)
XLA Modules:
  0.0 52.0 jit_solution(11030876968164511337)
XLA Ops:
  0.6 0.8 %select_maximum_fusion.part_ref = f32[72,256]{1,0:T(8,128)S(1)} fusion(f32[1,256]{1,0:T(1,128)} %bitcast.32, f32[32,256]{1,0:T(8,128)} %param.7, f32[32,256]{1,0:T(8,128)} %param.4), kind=kLoop, calls=%fused_computation.276 | loop fusion | flops 73728 | bytes 140288 | tf_op jit(solution)/shard_map/concatenate | solution.py:187
  1.4 4.0 %collective-permute-start = (f32[72,256]{1,0:T(8,128)S(1)}, f32[72,256]{1,0:T(8,128)S(1)}, u32[]{:S(2)}, u32[]{:S(2)}) collective-permute-start(f32[72,256]{1,0:T(8,128)S(1)} %select_maximum_fusion.part_ref), channel_id=1, source_target_pairs={{0,8},{1,9},{2,10},{3,11},{4,12},{5,13},{6,14},{7,15},{8,0},{9,1},... | collective-permute-start | bytes 221192 | tf_op jit(solution)/shard_map/ppermute | solution.py:19
  6.3 1.6 %collective-permute-start.4 = (f32[65,256]{1,0:T(8,128)S(1)}, f32[65,256]{1,0:T(8,128)S(1)}, u32[]{:S(2)}, u32[]{:S(2)}) collective-permute-start(f32[65,256]{1,0:T(8,128)S(1)} %get-tuple-element.49), channel_id=1, source_target_pairs={{0,2},{1,3},{2,0},{3,1},{4,6},{5,7},{6,4},{7,5},{8,10},{9,11},{10,... | collective-permute-start | bytes 199688 | tf_op jit(solution)/shard_map/ppermute | solution.py:19
  7.9 1.6 %collective-permute-start.1 = (f32[65,256]{1,0:T(8,128)S(1)}, f32[65,256]{1,0:T(8,128)S(1)}, u32[]{:S(2)}, u32[]{:S(2)}) collective-permute-start(f32[65,256]{1,0:T(8,128)S(1)} %get-tuple-element.49), channel_id=1, source_target_pairs={{0,4},{1,5},{2,6},{3,7},{4,0},{5,1},{6,2},{7,3},{8,12},{9,13},{10,... | collective-permute-start | bytes 199688 | tf_op jit(solution)/shard_map/ppermute | solution.py:19
  10.2 1.9 %collective-permute-start.6 = (f32[65,256]{1,0:T(8,128)S(1)}, f32[65,256]{1,0:T(8,128)S(1)}, u32[]{:S(2)}, u32[]{:S(2)}) collective-permute-start(f32[65,256]{1,0:T(8,128)S(1)} %get-tuple-element.53), channel_id=1, source_target_pairs={{0,2},{1,3},{2,0},{3,1},{4,6},{5,7},{6,4},{7,5},{8,10},{9,11},{10,... | collective-permute-start | bytes 199688 | tf_op jit(solution)/shard_map/ppermute | solution.py:19
  12.6 1.2 %collective-permute-done.2 = f32[72,256]{1,0:T(8,128)S(1)} collective-permute-done((f32[72,256]{1,0:T(8,128)S(1)}, f32[72,256]{1,0:T(8,128)S(1)}, u32[]{:S(2)}, u32[]{:S(2)}) %collective-permute-start.2) | collective-permute-done | bytes 73760 | tf_op jit(solution)/shard_map/ppermute | solution.py:19
  14.0 1.5 %collective-permute-start.5 = (f32[65,512]{1,0:T(8,128)S(1)}, f32[65,512]{1,0:T(8,128)S(1)}, u32[]{:S(2)}, u32[]{:S(2)}) collective-permute-start(f32[65,512]{1,0:T(8,128)S(1)} %get-tuple-element.52), channel_id=1, source_target_pairs={{0,2},{1,3},{2,0},{3,1},{4,6},{5,7},{6,4},{7,5},{8,10},{9,11},{10,... | collective-permute-start | bytes 399368 | tf_op jit(solution)/shard_map/ppermute | solution.py:19
  15.7 1.5 %shard_map.62 = (bf16[2048,1024]{1,0:T(8,128)(2,1)S(1)}, f32[32,1024]{1,0:T(8,128)S(1)}) custom-call(f32[32,1024]{1,0:T(8,128)S(1)} %get-tuple-element.121.rows_ref, f32[32,1]{1,0:T(8,128)S(1)} %copy.6.scale_ref, bf16[256,1024]{1,0:T(8,128)(2,1)S(1)} %constant_dynamic-update-slice_fusion.right_ref, f32[32,1024]{1,0:T(8,128)S(1)} %get-tuple-element.122.refs_0_, ...), custom_call_target="tpu_custom_call" | custom-call | flops 872415232 | bytes 4194304 | tf_op jit(solution)/shard_map/pallas_call | solution.py:114
  17.3 1.5 %shard_map.63 = (bf16[2048,1024]{1,0:T(8,128)(2,1)S(1)}, f32[32,1024]{1,0:T(8,128)S(1)}) custom-call(f32[32,1024]{1,0:T(8,128)S(1)} %get-tuple-element.126.rows_ref, f32[32,1]{1,0:T(8,128)S(1)} %copy.6.scale_ref, bf16[256,1024]{1,0:T(8,128)(2,1)S(1)} %constant_dynamic-update-slice_fusion.right_ref, f32[32,1024]{1,0:T(8,128)S(1)} %get-tuple-element.125.refs_0_, ...), custom_call_target="tpu_custom_call" | custom-call | flops 872415232 | bytes 4194304 | tf_op jit(solution)/shard_map/pallas_call | solution.py:114
  19.5 1.5 %shard_map.64 = (bf16[2048,1024]{1,0:T(8,128)(2,1)S(1)}, f32[32,1024]{1,0:T(8,128)S(1)}) custom-call(f32[32,1024]{1,0:T(8,128)S(1)} %get-tuple-element.69.rows_ref.part_ref, f32[32,1]{1,0:T(8,128)S(1)} %copy.6.scale_ref, bf16[256,1024]{1,0:T(8,128)(2,1)S(1)} %constant_dynamic-update-slice_fusion.right_ref, f32[32,1024]{1,0:T(8,128)S(1)} %get-tuple-element.118.refs_0_, ...), custom_call_target="tpu_custom_call" | custom-call | flops 872415232 | bytes 4194304 | tf_op jit(solution)/shard_map/pallas_call | solution.py:114
  21.1 1.5 %shard_map.65 = (bf16[2048,1024]{1,0:T(8,128)(2,1)S(1)}, f32[32,1024]{1,0:T(8,128)S(1)}) custom-call(f32[32,1024]{1,0:T(8,128)S(1)} %get-tuple-element.80.rows_ref, f32[32,1]{1,0:T(8,128)S(1)} %copy.6.scale_ref, bf16[256,1024]{1,0:T(8,128)(2,1)S(1)} %constant_dynamic-update-slice_fusion.right_ref, f32[32,1024]{1,0:T(8,128)S(1)} %get-tuple-element.123.refs_0_, ...), custom_call_target="tpu_custom_call" | custom-call | flops 872415232 | bytes 4194304 | tf_op jit(solution)/shard_map/pallas_call | solution.py:114
  22.7 1.4 %collective-permute-start.9 = (f32[32,1024]{1,0:T(8,128)S(1)}, f32[32,1024]{1,0:T(8,128)S(1)}, u32[]{:S(2)}, u32[]{:S(2)}) collective-permute-start(f32[32,1024]{1,0:T(8,128)S(1)} %get-tuple-element.64), channel_id=1, source_target_pairs={{0,2},{1,3},{2,0},{3,1},{4,6},{5,7},{6,4},{7,5},{8,10},{9,11},{10,... | collective-permute-start | bytes 393224 | tf_op jit(solution)/shard_map/ppermute | solution.py:19
  25.5 0.8 %convolution_add_fusion.6 = f32[96,1024]{1,0:T(8,128)S(1)} fusion(f32[96,1024]{1,0:T(8,128)S(1)} %fusion.6, bf16[2048,1024]{1,0:T(8,128)(2,1)S(1)} %get-tuple-element.67, bf16[32,1024]{1,0:T(8,128)(2,1)S(1)} %get-tuple-element.159, bf16[32,1024]{1,0:T(8,128)(2,1)S(1)} %get-tuple-element.160, bf16[32,1024]{1,0:T(8,128)(2,1)S(1)} %get-tuple-element.158), kind=kOutput, calls=%fused_computation.6 | convolution fusion | flops 405110784 | bytes 5177344 | tf_op jit(solution)/shard_map/dot_general | solution.py:152
  26.5 1.1 %shard_map.67 = bf16[2048,1024]{1,0:T(8,128)(2,1)S(1)} custom-call(f32[32,1024]{1,0:T(8,128)S(1)} %get-tuple-element.69.rows_ref.part_ref, f32[32,1]{1,0:T(8,128)S(1)} %copy.6.scale_ref, bf16[256,1024]{1,0:T(8,128)(2,1)S(1)} %shard_map.66.right_ref), custom_call_target="tpu_custom_call" | custom-call | flops 872415232 | bytes 4194304 | tf_op jit(solution)/shard_map/pallas_call | solution.py:114
  27.6 1.0 %collective-permute-done.9 = f32[32,1024]{1,0:T(8,128)S(1)} collective-permute-done((f32[32,1024]{1,0:T(8,128)S(1)}, f32[32,1024]{1,0:T(8,128)S(1)}, u32[]{:S(2)}, u32[]{:S(2)}) %collective-permute-start.9) | collective-permute-done | bytes 131104 | tf_op jit(solution)/shard_map/ppermute | solution.py:19
  28.6 0.8 %fusion.21 = f32[96,1024]{1,0:T(8,128)S(1)} fusion(bf16[2048,1024]{1,0:T(8,128)(2,1)S(1)} %get-tuple-element.73, bf16[32,1024]{1,0:T(8,128)(2,1)S(1)} %get-tuple-element.156, bf16[32,1024]{1,0:T(8,128)(2,1)S(1)} %get-tuple-element.157, bf16[32,1024]{1,0:T(8,128)(2,1)S(1)} %get-tuple-element.155), kind=kOutput, calls=%fused_computation.42 | convolution fusion | flops 405012480 | bytes 4784128 | tf_op jit(solution)/shard_map/dot_general | solution.py:152
  30.4 0.8 %convolution_add_fusion.5 = f32[96,1024]{1,0:T(8,128)S(1)} fusion(f32[96,1024]{1,0:T(8,128)S(1)} %fusion.21, bf16[2048,1024]{1,0:T(8,128)(2,1)S(1)} %get-tuple-element.77, bf16[32,1024]{1,0:T(8,128)(2,1)S(1)} %get-tuple-element.152, bf16[32,1024]{1,0:T(8,128)(2,1)S(1)} %get-tuple-element.153, bf16[32,1024]{1,0:T(8,128)(2,1)S(1)} %get-tuple-element.151), kind=kOutput, calls=%fused_computation.5 | convolution fusion | flops 405110784 | bytes 5177344 | tf_op jit(solution)/shard_map/dot_general | solution.py:152
  31.3 1.5 %collective-permute-start.12 = (f32[32,1024]{1,0:T(8,128)S(1)}, f32[32,1024]{1,0:T(8,128)S(1)}, u32[]{:S(2)}, u32[]{:S(2)}) collective-permute-start(f32[32,1024]{1,0:T(8,128)S(1)} %get-tuple-element.78), channel_id=1, source_target_pairs={{0,2},{1,3},{2,0},{3,1},{4,6},{5,7},{6,4},{7,5},{8,10},{9,11},{10,... | collective-permute-start | bytes 393224 | tf_op jit(solution)/shard_map/ppermute | solution.py:19
  33.0 0.8 %fusion.44 = f32[96,1024]{1,0:T(8,128)S(1)} fusion(bf16[2048,1024]{1,0:T(8,128)(2,1)S(1)} %get-tuple-element.66, bf16[96,1024]{1,0:T(8,128)(2,1)S(1)} %pad_maximum_fusion.3), kind=kOutput, calls=%fused_computation.65 | convolution fusion | flops 403439616 | bytes 4784128 | tf_op jit(solution)/shard_map/dot_general | solution.py:152
  34.4 1.0 %convolution_add_fusion.4 = f32[96,1024]{1,0:T(8,128)S(1)} fusion(f32[96,1024]{1,0:T(8,128)S(1)} %fusion.44, bf16[2048,1024]{1,0:T(8,128)(2,1)S(1)} %get-tuple-element.67, bf16[32,1024]{1,0:T(8,128)(2,1)S(1)} %get-tuple-element.147, bf16[32,1024]{1,0:T(8,128)(2,1)S(1)} %get-tuple-element.148, bf16[32,1024]{1,0:T(8,128)(2,1)S(1)} %get-tuple-element.146), kind=kOutput, calls=%fused_computation.4 | convolution fusion | flops 405110784 | bytes 5177344 | tf_op jit(solution)/shard_map/dot_general | solution.py:152
  35.4 1.1 %shard_map.68 = bf16[2048,1024]{1,0:T(8,128)(2,1)S(1)} custom-call(f32[32,1024]{1,0:T(8,128)S(1)} %get-tuple-element.80.rows_ref, f32[32,1]{1,0:T(8,128)S(1)} %copy.6.scale_ref, bf16[256,1024]{1,0:T(8,128)(2,1)S(1)} %shard_map.66.right_ref), custom_call_target="tpu_custom_call" | custom-call | flops 872415232 | bytes 4194304 | tf_op jit(solution)/shard_map/pallas_call | solution.py:114
  37.0 0.8 %fusion.59 = f32[96,1024]{1,0:T(8,128)S(1)} fusion(bf16[2048,1024]{1,0:T(8,128)(2,1)S(1)} %get-tuple-element.73, bf16[32,1024]{1,0:T(8,128)(2,1)S(1)} %get-tuple-element.144, bf16[32,1024]{1,0:T(8,128)(2,1)S(1)} %get-tuple-element.145, bf16[32,1024]{1,0:T(8,128)(2,1)S(1)} %get-tuple-element.143), kind=kOutput, calls=%fused_computation.80 | convolution fusion | flops 405012480 | bytes 4784128 | tf_op jit(solution)/shard_map/dot_general | solution.py:152
  38.7 0.8 %convolution_add_fusion.3 = f32[96,1024]{1,0:T(8,128)S(1)} fusion(f32[96,1024]{1,0:T(8,128)S(1)} %fusion.59, bf16[2048,1024]{1,0:T(8,128)(2,1)S(1)} %get-tuple-element.77, bf16[32,1024]{1,0:T(8,128)(2,1)S(1)} %get-tuple-element.140, bf16[32,1024]{1,0:T(8,128)(2,1)S(1)} %get-tuple-element.141, bf16[32,1024]{1,0:T(8,128)(2,1)S(1)} %get-tuple-element.139), kind=kOutput, calls=%fused_computation.3 | convolution fusion | flops 405110784 | bytes 5177344 | tf_op jit(solution)/shard_map/dot_general | solution.py:152
  39.7 1.5 %collective-permute-start.15 = (f32[32,1024]{1,0:T(8,128)S(1)}, f32[32,1024]{1,0:T(8,128)S(1)}, u32[]{:S(2)}, u32[]{:S(2)}) collective-permute-start(f32[32,1024]{1,0:T(8,128)S(1)} %get-tuple-element.88), channel_id=1, source_target_pairs={{0,2},{1,3},{2,0},{3,1},{4,6},{5,7},{6,4},{7,5},{8,10},{9,11},{10,... | collective-permute-start | bytes 393224 | tf_op jit(solution)/shard_map/ppermute | solution.py:19
  41.4 0.8 %fusion.82 = f32[96,1024]{1,0:T(8,128)S(1)} fusion(bf16[2048,1024]{1,0:T(8,128)(2,1)S(1)} %get-tuple-element.66, bf16[96,1024]{1,0:T(8,128)(2,1)S(1)} %pad_maximum_fusion.4), kind=kOutput, calls=%fused_computation.103 | convolution fusion | flops 403439616 | bytes 4784128 | tf_op jit(solution)/shard_map/dot_general | solution.py:152
  42.6 0.8 %convolution_add_fusion.2 = f32[96,1024]{1,0:T(8,128)S(1)} fusion(f32[96,1024]{1,0:T(8,128)S(1)} %fusion.82, bf16[2048,1024]{1,0:T(8,128)(2,1)S(1)} %get-tuple-element.67, bf16[32,1024]{1,0:T(8,128)(2,1)S(1)} %get-tuple-element.135, bf16[32,1024]{1,0:T(8,128)(2,1)S(1)} %get-tuple-element.136, bf16[32,1024]{1,0:T(8,128)(2,1)S(1)} %get-tuple-element.134), kind=kOutput, calls=%fused_computation.2 | convolution fusion | flops 405110784 | bytes 5177344 | tf_op jit(solution)/shard_map/dot_general | solution.py:152
  43.4 1.9 %collective-permute-done.15 = f32[32,1024]{1,0:T(8,128)S(1)} collective-permute-done((f32[32,1024]{1,0:T(8,128)S(1)}, f32[32,1024]{1,0:T(8,128)S(1)}, u32[]{:S(2)}, u32[]{:S(2)}) %collective-permute-start.15) | collective-permute-done | bytes 131104 | tf_op jit(solution)/shard_map/ppermute | solution.py:19
  45.4 0.8 %fusion.97 = f32[96,1024]{1,0:T(8,128)S(1)} fusion(bf16[2048,1024]{1,0:T(8,128)(2,1)S(1)} %get-tuple-element.73, bf16[32,1024]{1,0:T(8,128)(2,1)S(1)} %get-tuple-element.132, bf16[32,1024]{1,0:T(8,128)(2,1)S(1)} %get-tuple-element.133, bf16[32,1024]{1,0:T(8,128)(2,1)S(1)} %get-tuple-element.131), kind=kOutput, calls=%fused_computation.118 | convolution fusion | flops 405012480 | bytes 4784128 | tf_op jit(solution)/shard_map/dot_general | solution.py:152
  47.3 0.8 %convolution_add_fusion.1 = f32[96,1024]{1,0:T(8,128)S(1)} fusion(f32[96,1024]{1,0:T(8,128)S(1)} %fusion.97, bf16[2048,1024]{1,0:T(8,128)(2,1)S(1)} %get-tuple-element.77, bf16[32,1024]{1,0:T(8,128)(2,1)S(1)} %get-tuple-element.128, bf16[32,1024]{1,0:T(8,128)(2,1)S(1)} %get-tuple-element.129, bf16[32,1024]{1,0:T(8,128)(2,1)S(1)} %get-tuple-element.127), kind=kOutput, calls=%fused_computation.1 | convolution fusion | flops 405110784 | bytes 5177344 | tf_op jit(solution)/shard_map/dot_general | solution.py:152
  48.1 0.8 %fusion.120 = f32[96,1024]{1,0:T(8,128)S(1)} fusion(bf16[2048,1024]{1,0:T(8,128)(2,1)S(1)} %shard_map.67, bf16[32,1024]{1,0:T(8,128)(2,1)S(1)} %get-tuple-element.114, bf16[32,1024]{1,0:T(8,128)(2,1)S(1)} %get-tuple-element.113, bf16[32,1024]{1,0:T(8,128)(2,1)S(1)} %get-tuple-element.117), kind=kOutput, calls=%fused_computation.141 | convolution fusion | flops 405012480 | bytes 4784128 | tf_op jit(solution)/shard_map/dot_general | solution.py:152
  48.9 0.8 %convolution_add_fusion = f32[96,1024]{1,0:T(8,128)S(1)} fusion(f32[96,1024]{1,0:T(8,128)S(1)} %fusion.120, bf16[2048,1024]{1,0:T(8,128)(2,1)S(1)} %shard_map.68, bf16[32,1024]{1,0:T(8,128)(2,1)S(1)} %get-tuple-element.115, bf16[32,1024]{1,0:T(8,128)(2,1)S(1)} %get-tuple-element.116, bf16[32,1024]{1,0:T(8,128)(2,1)S(1)} %get-tuple-element.112), kind=kOutput, calls=%fused_computation | convolution fusion | flops 405110784 | bytes 5177344 | tf_op jit(solution)/shard_map/dot_general | solution.py:152
  50.3 0.9 %collective-permute-done.17 = f32[32]{0:T(128)S(1)} collective-permute-done((f32[32]{0:T(128)S(1)}, f32[32]{0:T(128)S(1)}, u32[]{:S(2)}, u32[]{:S(2)}) %collective-permute-start.17) | collective-permute-done | bytes 160 | tf_op jit(solution)/shard_map/ppermute | solution.py:19
  (86 shorter events, 11.3 us)
Async XLA Ops:
  1.4 8.1 %collective-permute-start = (f32[72,256]{1,0:T(8,128)S(1)}, f32[72,256]{1,0:T(8,128)S(1)}, u32[]{:S(2)}, u32[]{:S(2)}) collective-permute-start(f32[72,256]{1,0:T(8,128)S(1)} %select_maximum_fusion.part_ref), channel_id=1, source_target_pairs={{0,8},{1,9},{2,10},{3,11},{4,12},{5,13},{6,14},{7,15},{8,0},{9,1},... | collective-permute-start | bytes 221192 | tf_op jit(solution)/shard_map/ppermute | solution.py:19
  6.3 7.7 %collective-permute-start.4 = (f32[65,256]{1,0:T(8,128)S(1)}, f32[65,256]{1,0:T(8,128)S(1)}, u32[]{:S(2)}, u32[]{:S(2)}) collective-permute-start(f32[65,256]{1,0:T(8,128)S(1)} %get-tuple-element.49), channel_id=1, source_target_pairs={{0,2},{1,3},{2,0},{3,1},{4,6},{5,7},{6,4},{7,5},{8,10},{9,11},{10,... | collective-permute-start | bytes 199688 | tf_op jit(solution)/shard_map/ppermute | solution.py:19
  7.9 4.7 %collective-permute-start.1 = (f32[65,256]{1,0:T(8,128)S(1)}, f32[65,256]{1,0:T(8,128)S(1)}, u32[]{:S(2)}, u32[]{:S(2)}) collective-permute-start(f32[65,256]{1,0:T(8,128)S(1)} %get-tuple-element.49), channel_id=1, source_target_pairs={{0,4},{1,5},{2,6},{3,7},{4,0},{5,1},{6,2},{7,3},{8,12},{9,13},{10,... | collective-permute-start | bytes 199688 | tf_op jit(solution)/shard_map/ppermute | solution.py:19
  9.5 4.4 %collective-permute-start.2 = (f32[72,256]{1,0:T(8,128)S(1)}, f32[72,256]{1,0:T(8,128)S(1)}, u32[]{:S(2)}, u32[]{:S(2)}) collective-permute-start(f32[72,256]{1,0:T(8,128)S(1)} %collective-permute-done.part_ref), channel_id=1, source_target_pairs={{0,4},{1,5},{2,6},{3,7},{4,0},{5,1},{6,2},{7,3},{8,12},{9,13},{10,... | collective-permute-start | bytes 221192 | tf_op jit(solution)/shard_map/ppermute | solution.py:19
  10.2 8.6 %collective-permute-start.6 = (f32[65,256]{1,0:T(8,128)S(1)}, f32[65,256]{1,0:T(8,128)S(1)}, u32[]{:S(2)}, u32[]{:S(2)}) collective-permute-start(f32[65,256]{1,0:T(8,128)S(1)} %get-tuple-element.53), channel_id=1, source_target_pairs={{0,2},{1,3},{2,0},{3,1},{4,6},{5,7},{6,4},{7,5},{8,10},{9,11},{10,... | collective-permute-start | bytes 199688 | tf_op jit(solution)/shard_map/ppermute | solution.py:19
  14.0 5.2 %collective-permute-start.5 = (f32[65,512]{1,0:T(8,128)S(1)}, f32[65,512]{1,0:T(8,128)S(1)}, u32[]{:S(2)}, u32[]{:S(2)}) collective-permute-start(f32[65,512]{1,0:T(8,128)S(1)} %get-tuple-element.52), channel_id=1, source_target_pairs={{0,2},{1,3},{2,0},{3,1},{4,6},{5,7},{6,4},{7,5},{8,10},{9,11},{10,... | collective-permute-start | bytes 399368 | tf_op jit(solution)/shard_map/ppermute | solution.py:19
  15.6 1.7 %collective-permute-start.3 = (f32[64,1024]{1,0:T(8,128)S(1)}, f32[64,1024]{1,0:T(8,128)S(1)}, u32[]{:S(2)}, u32[]{:S(2)}) collective-permute-start(f32[64,1024]{1,0:T(8,128)S(1)} %slice.225), channel_id=1, source_target_pairs={{0,1},{1,0},{2,3},{3,2},{4,5},{5,4},{6,7},{7,6},{8,9},{9,8},{10,11... | collective-permute-start | bytes 786440 | tf_op jit(solution)/shard_map/ppermute | solution.py:19
  19.3 1.7 %collective-permute-start.7 = (f32[64,1024]{1,0:T(8,128)S(1)}, f32[64,1024]{1,0:T(8,128)S(1)}, u32[]{:S(2)}, u32[]{:S(2)}) collective-permute-start(f32[64,1024]{1,0:T(8,128)S(1)} %slice.230), channel_id=1, source_target_pairs={{0,1},{1,0},{2,3},{3,2},{4,5},{5,4},{6,7},{7,6},{8,9},{9,8},{10,11... | collective-permute-start | bytes 786440 | tf_op jit(solution)/shard_map/ppermute | solution.py:19
  22.7 5.9 %collective-permute-start.9 = (f32[32,1024]{1,0:T(8,128)S(1)}, f32[32,1024]{1,0:T(8,128)S(1)}, u32[]{:S(2)}, u32[]{:S(2)}) collective-permute-start(f32[32,1024]{1,0:T(8,128)S(1)} %get-tuple-element.64), channel_id=1, source_target_pairs={{0,2},{1,3},{2,0},{3,1},{4,6},{5,7},{6,4},{7,5},{8,10},{9,11},{10,... | collective-permute-start | bytes 393224 | tf_op jit(solution)/shard_map/ppermute | solution.py:19
  24.1 1.4 %collective-permute-start.8 = (f32[32,1024]{1,0:T(8,128)S(1)}, f32[32,1024]{1,0:T(8,128)S(1)}, u32[]{:S(2)}, u32[]{:S(2)}) collective-permute-start(f32[32,1024]{1,0:T(8,128)S(1)} %get-tuple-element.64), channel_id=1, source_target_pairs={{0,1},{1,0},{2,3},{3,2},{4,5},{5,4},{6,7},{7,6},{8,9},{9,8},{10,11... | collective-permute-start | bytes 393224 | tf_op jit(solution)/shard_map/ppermute | solution.py:19
  28.6 1.3 %collective-permute-start.10 = (f32[32,1024]{1,0:T(8,128)S(1)}, f32[32,1024]{1,0:T(8,128)S(1)}, u32[]{:S(2)}, u32[]{:S(2)}) collective-permute-start(f32[32,1024]{1,0:T(8,128)S(1)} %collective-permute-done.9), channel_id=1, source_target_pairs={{0,1},{1,0},{2,3},{3,2},{4,5},{5,4},{6,7},{7,6},{8,9},{9,8},{10,11... | collective-permute-start | bytes 393224 | tf_op jit(solution)/shard_map/ppermute | solution.py:19
  31.3 5.6 %collective-permute-start.12 = (f32[32,1024]{1,0:T(8,128)S(1)}, f32[32,1024]{1,0:T(8,128)S(1)}, u32[]{:S(2)}, u32[]{:S(2)}) collective-permute-start(f32[32,1024]{1,0:T(8,128)S(1)} %get-tuple-element.78), channel_id=1, source_target_pairs={{0,2},{1,3},{2,0},{3,1},{4,6},{5,7},{6,4},{7,5},{8,10},{9,11},{10,... | collective-permute-start | bytes 393224 | tf_op jit(solution)/shard_map/ppermute | solution.py:19
  32.9 1.4 %collective-permute-start.11 = (f32[32,1024]{1,0:T(8,128)S(1)}, f32[32,1024]{1,0:T(8,128)S(1)}, u32[]{:S(2)}, u32[]{:S(2)}) collective-permute-start(f32[32,1024]{1,0:T(8,128)S(1)} %get-tuple-element.78), channel_id=1, source_target_pairs={{0,1},{1,0},{2,3},{3,2},{4,5},{5,4},{6,7},{7,6},{8,9},{9,8},{10,11... | collective-permute-start | bytes 393224 | tf_op jit(solution)/shard_map/ppermute | solution.py:19
  36.9 1.3 %collective-permute-start.13 = (f32[32,1024]{1,0:T(8,128)S(1)}, f32[32,1024]{1,0:T(8,128)S(1)}, u32[]{:S(2)}, u32[]{:S(2)}) collective-permute-start(f32[32,1024]{1,0:T(8,128)S(1)} %collective-permute-done.12), channel_id=1, source_target_pairs={{0,1},{1,0},{2,3},{3,2},{4,5},{5,4},{6,7},{7,6},{8,9},{9,8},{10,11... | collective-permute-start | bytes 393224 | tf_op jit(solution)/shard_map/ppermute | solution.py:19
  39.7 5.6 %collective-permute-start.15 = (f32[32,1024]{1,0:T(8,128)S(1)}, f32[32,1024]{1,0:T(8,128)S(1)}, u32[]{:S(2)}, u32[]{:S(2)}) collective-permute-start(f32[32,1024]{1,0:T(8,128)S(1)} %get-tuple-element.88), channel_id=1, source_target_pairs={{0,2},{1,3},{2,0},{3,1},{4,6},{5,7},{6,4},{7,5},{8,10},{9,11},{10,... | collective-permute-start | bytes 393224 | tf_op jit(solution)/shard_map/ppermute | solution.py:19
  41.2 1.4 %collective-permute-start.14 = (f32[32,1024]{1,0:T(8,128)S(1)}, f32[32,1024]{1,0:T(8,128)S(1)}, u32[]{:S(2)}, u32[]{:S(2)}) collective-permute-start(f32[32,1024]{1,0:T(8,128)S(1)} %get-tuple-element.88), channel_id=1, source_target_pairs={{0,1},{1,0},{2,3},{3,2},{4,5},{5,4},{6,7},{7,6},{8,9},{9,8},{10,11... | collective-permute-start | bytes 393224 | tf_op jit(solution)/shard_map/ppermute | solution.py:19
  45.3 1.3 %collective-permute-start.16 = (f32[32,1024]{1,0:T(8,128)S(1)}, f32[32,1024]{1,0:T(8,128)S(1)}, u32[]{:S(2)}, u32[]{:S(2)}) collective-permute-start(f32[32,1024]{1,0:T(8,128)S(1)} %collective-permute-done.15), channel_id=1, source_target_pairs={{0,1},{1,0},{2,3},{3,2},{4,5},{5,4},{6,7},{7,6},{8,9},{9,8},{10,11... | collective-permute-start | bytes 393224 | tf_op jit(solution)/shard_map/ppermute | solution.py:19
  50.1 1.2 %collective-permute-start.17 = (f32[32]{0:T(128)S(1)}, f32[32]{0:T(128)S(1)}, u32[]{:S(2)}, u32[]{:S(2)}) collective-permute-start(f32[32]{0:T(128)S(1)} %get-tuple-element.96), channel_id=1, source_target_pairs={{0,1},{1,0},{2,3},{3,2},{4,5},{5,4},{6,7},{7,6},{8,9},{9,8},{10,11... | collective-permute-start | bytes 392 | tf_op jit(solution)/shard_map/ppermute | solution.py:19

commit v28 on v27

--- a/solution.py
+++ b/solution.py
@@ -100,11 +100,11 @@
 
     contract(*steps[0])
     for k, chunk in enumerate(steps):
+        if k and applies:
+            apply(*steps[k - 1])
         if k + 1 < len(steps):
             contract(*steps[k + 1])
         raise_power(*chunk)
-        if k and applies:
-            apply(*steps[k - 1])
     if applies:
         apply(*steps[-1])
 

time: 52.2 us -> 52.2 us (level)
  no operation moved by 1% of the time
where the time goes in v28:
time: 52.2 us; the launch traced here: 52 us
  starting transfers between devices  16.4 us (31%)
  matrix products  11.5 us (22%)
  Pallas kernels  8.76 us (17%)
  waiting for transfers between devices  8.67 us (17%)
  other arithmetic  5.42 us (10%)
  between operations  0.97 us (2%)
    ppermute x18, starting transfers between devices, swap(): return lax.ppermute(x, 'blk', [(i, i ^ stride) for i in range(n)])  16.4 us
    dot_general x14, matrix products, apply_parts(): jnp.dot(jnp.concatenate([parts, parts], axis=1), piece, preferred_element...  11.5 us
    pallas_call x10, Pallas kernels, call(): pl.pallas_call(kernel, out_shape=outs, in_specs=[whole] * len(args), out_...  8.76 us
    ppermute x18, waiting for transfers between devices, swap(): return lax.ppermute(x, 'blk', [(i, i ^ stride) for i in range(n)])  8.67 us
  transfers between devices with their start and end apart: 18, of which 13 were waited for; matrix products, arithmetic and copies ran while one was open for 18% of the time, Pallas kernels for 14%

profile of v28, /device:TPU:0, one launch (start us, length us, event | category | flops | bytes accessed | tf_op | source)
XLA Modules:
  0.0 52.0 jit_solution(7190056686937944772)
XLA Ops:
  0.6 0.8 %select_maximum_fusion.part_ref = f32[72,256]{1,0:T(8,128)S(1)} fusion(f32[1,256]{1,0:T(1,128)} %bitcast.32, f32[32,256]{1,0:T(8,128)} %param.7, f32[32,256]{1,0:T(8,128)} %param.4), kind=kLoop, calls=%fused_computation.276 | loop fusion | flops 73728 | bytes 140288 | tf_op jit(solution)/shard_map/concatenate | solution.py:187
  1.4 4.0 %collective-permute-start = (f32[72,256]{1,0:T(8,128)S(1)}, f32[72,256]{1,0:T(8,128)S(1)}, u32[]{:S(2)}, u32[]{:S(2)}) collective-permute-start(f32[72,256]{1,0:T(8,128)S(1)} %select_maximum_fusion.part_ref), channel_id=1, source_target_pairs={{0,8},{1,9},{2,10},{3,11},{4,12},{5,13},{6,14},{7,15},{8,0},{9,1},... | collective-permute-start | bytes 221192 | tf_op jit(solution)/shard_map/ppermute | solution.py:19
  6.3 1.6 %collective-permute-start.4 = (f32[65,256]{1,0:T(8,128)S(1)}, f32[65,256]{1,0:T(8,128)S(1)}, u32[]{:S(2)}, u32[]{:S(2)}) collective-permute-start(f32[65,256]{1,0:T(8,128)S(1)} %get-tuple-element.49), channel_id=1, source_target_pairs={{0,2},{1,3},{2,0},{3,1},{4,6},{5,7},{6,4},{7,5},{8,10},{9,11},{10,... | collective-permute-start | bytes 199688 | tf_op jit(solution)/shard_map/ppermute | solution.py:19
  7.9 1.6 %collective-permute-start.1 = (f32[65,256]{1,0:T(8,128)S(1)}, f32[65,256]{1,0:T(8,128)S(1)}, u32[]{:S(2)}, u32[]{:S(2)}) collective-permute-start(f32[65,256]{1,0:T(8,128)S(1)} %get-tuple-element.49), channel_id=1, source_target_pairs={{0,4},{1,5},{2,6},{3,7},{4,0},{5,1},{6,2},{7,3},{8,12},{9,13},{10,... | collective-permute-start | bytes 199688 | tf_op jit(solution)/shard_map/ppermute | solution.py:19
  10.2 1.9 %collective-permute-start.6 = (f32[65,256]{1,0:T(8,128)S(1)}, f32[65,256]{1,0:T(8,128)S(1)}, u32[]{:S(2)}, u32[]{:S(2)}) collective-permute-start(f32[65,256]{1,0:T(8,128)S(1)} %get-tuple-element.53), channel_id=1, source_target_pairs={{0,2},{1,3},{2,0},{3,1},{4,6},{5,7},{6,4},{7,5},{8,10},{9,11},{10,... | collective-permute-start | bytes 199688 | tf_op jit(solution)/shard_map/ppermute | solution.py:19
  12.6 1.2 %collective-permute-done.2 = f32[72,256]{1,0:T(8,128)S(1)} collective-permute-done((f32[72,256]{1,0:T(8,128)S(1)}, f32[72,256]{1,0:T(8,128)S(1)}, u32[]{:S(2)}, u32[]{:S(2)}) %collective-permute-start.2) | collective-permute-done | bytes 73760 | tf_op jit(solution)/shard_map/ppermute | solution.py:19
  14.0 1.5 %collective-permute-start.5 = (f32[65,512]{1,0:T(8,128)S(1)}, f32[65,512]{1,0:T(8,128)S(1)}, u32[]{:S(2)}, u32[]{:S(2)}) collective-permute-start(f32[65,512]{1,0:T(8,128)S(1)} %get-tuple-element.52), channel_id=1, source_target_pairs={{0,2},{1,3},{2,0},{3,1},{4,6},{5,7},{6,4},{7,5},{8,10},{9,11},{10,... | collective-permute-start | bytes 399368 | tf_op jit(solution)/shard_map/ppermute | solution.py:19
  15.7 1.5 %shard_map.62 = (bf16[2048,1024]{1,0:T(8,128)(2,1)S(1)}, f32[32,1024]{1,0:T(8,128)S(1)}) custom-call(f32[32,1024]{1,0:T(8,128)S(1)} %get-tuple-element.121.rows_ref, f32[32,1]{1,0:T(8,128)S(1)} %copy.6.scale_ref, bf16[256,1024]{1,0:T(8,128)(2,1)S(1)} %constant_dynamic-update-slice_fusion.right_ref, f32[32,1024]{1,0:T(8,128)S(1)} %get-tuple-element.122.refs_0_, ...), custom_call_target="tpu_custom_call" | custom-call | flops 872415232 | bytes 4194304 | tf_op jit(solution)/shard_map/pallas_call | solution.py:114
  17.3 1.5 %shard_map.63 = (bf16[2048,1024]{1,0:T(8,128)(2,1)S(1)}, f32[32,1024]{1,0:T(8,128)S(1)}) custom-call(f32[32,1024]{1,0:T(8,128)S(1)} %get-tuple-element.126.rows_ref, f32[32,1]{1,0:T(8,128)S(1)} %copy.6.scale_ref, bf16[256,1024]{1,0:T(8,128)(2,1)S(1)} %constant_dynamic-update-slice_fusion.right_ref, f32[32,1024]{1,0:T(8,128)S(1)} %get-tuple-element.125.refs_0_, ...), custom_call_target="tpu_custom_call" | custom-call | flops 872415232 | bytes 4194304 | tf_op jit(solution)/shard_map/pallas_call | solution.py:114
  19.6 1.5 %shard_map.64 = (bf16[2048,1024]{1,0:T(8,128)(2,1)S(1)}, f32[32,1024]{1,0:T(8,128)S(1)}) custom-call(f32[32,1024]{1,0:T(8,128)S(1)} %get-tuple-element.69.rows_ref.part_ref, f32[32,1]{1,0:T(8,128)S(1)} %copy.6.scale_ref, bf16[256,1024]{1,0:T(8,128)(2,1)S(1)} %constant_dynamic-update-slice_fusion.right_ref, f32[32,1024]{1,0:T(8,128)S(1)} %get-tuple-element.118.refs_0_, ...), custom_call_target="tpu_custom_call" | custom-call | flops 872415232 | bytes 4194304 | tf_op jit(solution)/shard_map/pallas_call | solution.py:114
  21.2 1.5 %shard_map.65 = (bf16[2048,1024]{1,0:T(8,128)(2,1)S(1)}, f32[32,1024]{1,0:T(8,128)S(1)}) custom-call(f32[32,1024]{1,0:T(8,128)S(1)} %get-tuple-element.80.rows_ref, f32[32,1]{1,0:T(8,128)S(1)} %copy.6.scale_ref, bf16[256,1024]{1,0:T(8,128)(2,1)S(1)} %constant_dynamic-update-slice_fusion.right_ref, f32[32,1024]{1,0:T(8,128)S(1)} %get-tuple-element.123.refs_0_, ...), custom_call_target="tpu_custom_call" | custom-call | flops 872415232 | bytes 4194304 | tf_op jit(solution)/shard_map/pallas_call | solution.py:114
  22.8 1.3 %collective-permute-start.9 = (f32[32,1024]{1,0:T(8,128)S(1)}, f32[32,1024]{1,0:T(8,128)S(1)}, u32[]{:S(2)}, u32[]{:S(2)}) collective-permute-start(f32[32,1024]{1,0:T(8,128)S(1)} %get-tuple-element.64), channel_id=1, source_target_pairs={{0,2},{1,3},{2,0},{3,1},{4,6},{5,7},{6,4},{7,5},{8,10},{9,11},{10,... | collective-permute-start | bytes 393224 | tf_op jit(solution)/shard_map/ppermute | solution.py:19
  25.6 0.8 %convolution_add_fusion.6 = f32[96,1024]{1,0:T(8,128)S(1)} fusion(f32[96,1024]{1,0:T(8,128)S(1)} %fusion.6, bf16[2048,1024]{1,0:T(8,128)(2,1)S(1)} %get-tuple-element.67, bf16[32,1024]{1,0:T(8,128)(2,1)S(1)} %get-tuple-element.159, bf16[32,1024]{1,0:T(8,128)(2,1)S(1)} %get-tuple-element.160, bf16[32,1024]{1,0:T(8,128)(2,1)S(1)} %get-tuple-element.158), kind=kOutput, calls=%fused_computation.6 | convolution fusion | flops 405110784 | bytes 5177344 | tf_op jit(solution)/shard_map/dot_general | solution.py:152
  26.5 1.1 %shard_map.67 = bf16[2048,1024]{1,0:T(8,128)(2,1)S(1)} custom-call(f32[32,1024]{1,0:T(8,128)S(1)} %get-tuple-element.69.rows_ref.part_ref, f32[32,1]{1,0:T(8,128)S(1)} %copy.6.scale_ref, bf16[256,1024]{1,0:T(8,128)(2,1)S(1)} %shard_map.66.right_ref), custom_call_target="tpu_custom_call" | custom-call | flops 872415232 | bytes 4194304 | tf_op jit(solution)/shard_map/pallas_call | solution.py:114
  27.6 1.0 %collective-permute-done.9 = f32[32,1024]{1,0:T(8,128)S(1)} collective-permute-done((f32[32,1024]{1,0:T(8,128)S(1)}, f32[32,1024]{1,0:T(8,128)S(1)}, u32[]{:S(2)}, u32[]{:S(2)}) %collective-permute-start.9) | collective-permute-done | bytes 131104 | tf_op jit(solution)/shard_map/ppermute | solution.py:19
  28.6 0.8 %fusion.21 = f32[96,1024]{1,0:T(8,128)S(1)} fusion(bf16[2048,1024]{1,0:T(8,128)(2,1)S(1)} %get-tuple-element.73, bf16[32,1024]{1,0:T(8,128)(2,1)S(1)} %get-tuple-element.156, bf16[32,1024]{1,0:T(8,128)(2,1)S(1)} %get-tuple-element.157, bf16[32,1024]{1,0:T(8,128)(2,1)S(1)} %get-tuple-element.155), kind=kOutput, calls=%fused_computation.42 | convolution fusion | flops 405012480 | bytes 4784128 | tf_op jit(solution)/shard_map/dot_general | solution.py:152
  30.4 0.8 %convolution_add_fusion.5 = f32[96,1024]{1,0:T(8,128)S(1)} fusion(f32[96,1024]{1,0:T(8,128)S(1)} %fusion.21, bf16[2048,1024]{1,0:T(8,128)(2,1)S(1)} %get-tuple-element.77, bf16[32,1024]{1,0:T(8,128)(2,1)S(1)} %get-tuple-element.152, bf16[32,1024]{1,0:T(8,128)(2,1)S(1)} %get-tuple-element.153, bf16[32,1024]{1,0:T(8,128)(2,1)S(1)} %get-tuple-element.151), kind=kOutput, calls=%fused_computation.5 | convolution fusion | flops 405110784 | bytes 5177344 | tf_op jit(solution)/shard_map/dot_general | solution.py:152
  31.3 1.5 %collective-permute-start.12 = (f32[32,1024]{1,0:T(8,128)S(1)}, f32[32,1024]{1,0:T(8,128)S(1)}, u32[]{:S(2)}, u32[]{:S(2)}) collective-permute-start(f32[32,1024]{1,0:T(8,128)S(1)} %get-tuple-element.78), channel_id=1, source_target_pairs={{0,2},{1,3},{2,0},{3,1},{4,6},{5,7},{6,4},{7,5},{8,10},{9,11},{10,... | collective-permute-start | bytes 393224 | tf_op jit(solution)/shard_map/ppermute | solution.py:19
  33.0 0.8 %fusion.44 = f32[96,1024]{1,0:T(8,128)S(1)} fusion(bf16[2048,1024]{1,0:T(8,128)(2,1)S(1)} %get-tuple-element.66, bf16[96,1024]{1,0:T(8,128)(2,1)S(1)} %pad_maximum_fusion.3), kind=kOutput, calls=%fused_computation.65 | convolution fusion | flops 403439616 | bytes 4784128 | tf_op jit(solution)/shard_map/dot_general | solution.py:152
  34.4 1.0 %convolution_add_fusion.4 = f32[96,1024]{1,0:T(8,128)S(1)} fusion(f32[96,1024]{1,0:T(8,128)S(1)} %fusion.44, bf16[2048,1024]{1,0:T(8,128)(2,1)S(1)} %get-tuple-element.67, bf16[32,1024]{1,0:T(8,128)(2,1)S(1)} %get-tuple-element.147, bf16[32,1024]{1,0:T(8,128)(2,1)S(1)} %get-tuple-element.148, bf16[32,1024]{1,0:T(8,128)(2,1)S(1)} %get-tuple-element.146), kind=kOutput, calls=%fused_computation.4 | convolution fusion | flops 405110784 | bytes 5177344 | tf_op jit(solution)/shard_map/dot_general | solution.py:152
  35.4 1.1 %shard_map.68 = bf16[2048,1024]{1,0:T(8,128)(2,1)S(1)} custom-call(f32[32,1024]{1,0:T(8,128)S(1)} %get-tuple-element.80.rows_ref, f32[32,1]{1,0:T(8,128)S(1)} %copy.6.scale_ref, bf16[256,1024]{1,0:T(8,128)(2,1)S(1)} %shard_map.66.right_ref), custom_call_target="tpu_custom_call" | custom-call | flops 872415232 | bytes 4194304 | tf_op jit(solution)/shard_map/pallas_call | solution.py:114
  37.0 0.8 %fusion.59 = f32[96,1024]{1,0:T(8,128)S(1)} fusion(bf16[2048,1024]{1,0:T(8,128)(2,1)S(1)} %get-tuple-element.73, bf16[32,1024]{1,0:T(8,128)(2,1)S(1)} %get-tuple-element.144, bf16[32,1024]{1,0:T(8,128)(2,1)S(1)} %get-tuple-element.145, bf16[32,1024]{1,0:T(8,128)(2,1)S(1)} %get-tuple-element.143), kind=kOutput, calls=%fused_computation.80 | convolution fusion | flops 405012480 | bytes 4784128 | tf_op jit(solution)/shard_map/dot_general | solution.py:152
  38.8 0.8 %convolution_add_fusion.3 = f32[96,1024]{1,0:T(8,128)S(1)} fusion(f32[96,1024]{1,0:T(8,128)S(1)} %fusion.59, bf16[2048,1024]{1,0:T(8,128)(2,1)S(1)} %get-tuple-element.77, bf16[32,1024]{1,0:T(8,128)(2,1)S(1)} %get-tuple-element.140, bf16[32,1024]{1,0:T(8,128)(2,1)S(1)} %get-tuple-element.141, bf16[32,1024]{1,0:T(8,128)(2,1)S(1)} %get-tuple-element.139), kind=kOutput, calls=%fused_computation.3 | convolution fusion | flops 405110784 | bytes 5177344 | tf_op jit(solution)/shard_map/dot_general | solution.py:152
  39.7 1.5 %collective-permute-start.15 = (f32[32,1024]{1,0:T(8,128)S(1)}, f32[32,1024]{1,0:T(8,128)S(1)}, u32[]{:S(2)}, u32[]{:S(2)}) collective-permute-start(f32[32,1024]{1,0:T(8,128)S(1)} %get-tuple-element.88), channel_id=1, source_target_pairs={{0,2},{1,3},{2,0},{3,1},{4,6},{5,7},{6,4},{7,5},{8,10},{9,11},{10,... | collective-permute-start | bytes 393224 | tf_op jit(solution)/shard_map/ppermute | solution.py:19
  41.4 0.8 %fusion.82 = f32[96,1024]{1,0:T(8,128)S(1)} fusion(bf16[2048,1024]{1,0:T(8,128)(2,1)S(1)} %get-tuple-element.66, bf16[96,1024]{1,0:T(8,128)(2,1)S(1)} %pad_maximum_fusion.4), kind=kOutput, calls=%fused_computation.103 | convolution fusion | flops 403439616 | bytes 4784128 | tf_op jit(solution)/shard_map/dot_general | solution.py:152
  42.7 0.8 %convolution_add_fusion.2 = f32[96,1024]{1,0:T(8,128)S(1)} fusion(f32[96,1024]{1,0:T(8,128)S(1)} %fusion.82, bf16[2048,1024]{1,0:T(8,128)(2,1)S(1)} %get-tuple-element.67, bf16[32,1024]{1,0:T(8,128)(2,1)S(1)} %get-tuple-element.135, bf16[32,1024]{1,0:T(8,128)(2,1)S(1)} %get-tuple-element.136, bf16[32,1024]{1,0:T(8,128)(2,1)S(1)} %get-tuple-element.134), kind=kOutput, calls=%fused_computation.2 | convolution fusion | flops 405110784 | bytes 5177344 | tf_op jit(solution)/shard_map/dot_general | solution.py:152
  43.5 1.9 %collective-permute-done.15 = f32[32,1024]{1,0:T(8,128)S(1)} collective-permute-done((f32[32,1024]{1,0:T(8,128)S(1)}, f32[32,1024]{1,0:T(8,128)S(1)}, u32[]{:S(2)}, u32[]{:S(2)}) %collective-permute-start.15) | collective-permute-done | bytes 131104 | tf_op jit(solution)/shard_map/ppermute | solution.py:19
  45.4 0.8 %fusion.97 = f32[96,1024]{1,0:T(8,128)S(1)} fusion(bf16[2048,1024]{1,0:T(8,128)(2,1)S(1)} %get-tuple-element.73, bf16[32,1024]{1,0:T(8,128)(2,1)S(1)} %get-tuple-element.132, bf16[32,1024]{1,0:T(8,128)(2,1)S(1)} %get-tuple-element.133, bf16[32,1024]{1,0:T(8,128)(2,1)S(1)} %get-tuple-element.131), kind=kOutput, calls=%fused_computation.118 | convolution fusion | flops 405012480 | bytes 4784128 | tf_op jit(solution)/shard_map/dot_general | solution.py:152
  47.3 0.8 %convolution_add_fusion.1 = f32[96,1024]{1,0:T(8,128)S(1)} fusion(f32[96,1024]{1,0:T(8,128)S(1)} %fusion.97, bf16[2048,1024]{1,0:T(8,128)(2,1)S(1)} %get-tuple-element.77, bf16[32,1024]{1,0:T(8,128)(2,1)S(1)} %get-tuple-element.128, bf16[32,1024]{1,0:T(8,128)(2,1)S(1)} %get-tuple-element.129, bf16[32,1024]{1,0:T(8,128)(2,1)S(1)} %get-tuple-element.127), kind=kOutput, calls=%fused_computation.1 | convolution fusion | flops 405110784 | bytes 5177344 | tf_op jit(solution)/shard_map/dot_general | solution.py:152
  48.1 0.8 %fusion.120 = f32[96,1024]{1,0:T(8,128)S(1)} fusion(bf16[2048,1024]{1,0:T(8,128)(2,1)S(1)} %shard_map.67, bf16[32,1024]{1,0:T(8,128)(2,1)S(1)} %get-tuple-element.114, bf16[32,1024]{1,0:T(8,128)(2,1)S(1)} %get-tuple-element.113, bf16[32,1024]{1,0:T(8,128)(2,1)S(1)} %get-tuple-element.117), kind=kOutput, calls=%fused_computation.141 | convolution fusion | flops 405012480 | bytes 4784128 | tf_op jit(solution)/shard_map/dot_general | solution.py:152
  48.9 0.8 %convolution_add_fusion = f32[96,1024]{1,0:T(8,128)S(1)} fusion(f32[96,1024]{1,0:T(8,128)S(1)} %fusion.120, bf16[2048,1024]{1,0:T(8,128)(2,1)S(1)} %shard_map.68, bf16[32,1024]{1,0:T(8,128)(2,1)S(1)} %get-tuple-element.115, bf16[32,1024]{1,0:T(8,128)(2,1)S(1)} %get-tuple-element.116, bf16[32,1024]{1,0:T(8,128)(2,1)S(1)} %get-tuple-element.112), kind=kOutput, calls=%fused_computation | convolution fusion | flops 405110784 | bytes 5177344 | tf_op jit(solution)/shard_map/dot_general | solution.py:152
  50.3 0.9 %collective-permute-done.17 = f32[32]{0:T(128)S(1)} collective-permute-done((f32[32]{0:T(128)S(1)}, f32[32]{0:T(128)S(1)}, u32[]{:S(2)}, u32[]{:S(2)}) %collective-permute-start.17) | collective-permute-done | bytes 160 | tf_op jit(solution)/shard_map/ppermute | solution.py:19
  (86 shorter events, 11.4 us)
Async XLA Ops:
  1.4 8.1 %collective-permute-start = (f32[72,256]{1,0:T(8,128)S(1)}, f32[72,256]{1,0:T(8,128)S(1)}, u32[]{:S(2)}, u32[]{:S(2)}) collective-permute-start(f32[72,256]{1,0:T(8,128)S(1)} %select_maximum_fusion.part_ref), channel_id=1, source_target_pairs={{0,8},{1,9},{2,10},{3,11},{4,12},{5,13},{6,14},{7,15},{8,0},{9,1},... | collective-permute-start | bytes 221192 | tf_op jit(solution)/shard_map/ppermute | solution.py:19
  6.3 7.7 %collective-permute-start.4 = (f32[65,256]{1,0:T(8,128)S(1)}, f32[65,256]{1,0:T(8,128)S(1)}, u32[]{:S(2)}, u32[]{:S(2)}) collective-permute-start(f32[65,256]{1,0:T(8,128)S(1)} %get-tuple-element.49), channel_id=1, source_target_pairs={{0,2},{1,3},{2,0},{3,1},{4,6},{5,7},{6,4},{7,5},{8,10},{9,11},{10,... | collective-permute-start | bytes 199688 | tf_op jit(solution)/shard_map/ppermute | solution.py:19
  7.9 4.7 %collective-permute-start.1 = (f32[65,256]{1,0:T(8,128)S(1)}, f32[65,256]{1,0:T(8,128)S(1)}, u32[]{:S(2)}, u32[]{:S(2)}) collective-permute-start(f32[65,256]{1,0:T(8,128)S(1)} %get-tuple-element.49), channel_id=1, source_target_pairs={{0,4},{1,5},{2,6},{3,7},{4,0},{5,1},{6,2},{7,3},{8,12},{9,13},{10,... | collective-permute-start | bytes 199688 | tf_op jit(solution)/shard_map/ppermute | solution.py:19
  9.5 4.4 %collective-permute-start.2 = (f32[72,256]{1,0:T(8,128)S(1)}, f32[72,256]{1,0:T(8,128)S(1)}, u32[]{:S(2)}, u32[]{:S(2)}) collective-permute-start(f32[72,256]{1,0:T(8,128)S(1)} %collective-permute-done.part_ref), channel_id=1, source_target_pairs={{0,4},{1,5},{2,6},{3,7},{4,0},{5,1},{6,2},{7,3},{8,12},{9,13},{10,... | collective-permute-start | bytes 221192 | tf_op jit(solution)/shard_map/ppermute | solution.py:19
  10.2 8.7 %collective-permute-start.6 = (f32[65,256]{1,0:T(8,128)S(1)}, f32[65,256]{1,0:T(8,128)S(1)}, u32[]{:S(2)}, u32[]{:S(2)}) collective-permute-start(f32[65,256]{1,0:T(8,128)S(1)} %get-tuple-element.53), channel_id=1, source_target_pairs={{0,2},{1,3},{2,0},{3,1},{4,6},{5,7},{6,4},{7,5},{8,10},{9,11},{10,... | collective-permute-start | bytes 199688 | tf_op jit(solution)/shard_map/ppermute | solution.py:19
  14.0 5.2 %collective-permute-start.5 = (f32[65,512]{1,0:T(8,128)S(1)}, f32[65,512]{1,0:T(8,128)S(1)}, u32[]{:S(2)}, u32[]{:S(2)}) collective-permute-start(f32[65,512]{1,0:T(8,128)S(1)} %get-tuple-element.52), channel_id=1, source_target_pairs={{0,2},{1,3},{2,0},{3,1},{4,6},{5,7},{6,4},{7,5},{8,10},{9,11},{10,... | collective-permute-start | bytes 399368 | tf_op jit(solution)/shard_map/ppermute | solution.py:19
  15.6 1.7 %collective-permute-start.3 = (f32[64,1024]{1,0:T(8,128)S(1)}, f32[64,1024]{1,0:T(8,128)S(1)}, u32[]{:S(2)}, u32[]{:S(2)}) collective-permute-start(f32[64,1024]{1,0:T(8,128)S(1)} %slice.225), channel_id=1, source_target_pairs={{0,1},{1,0},{2,3},{3,2},{4,5},{5,4},{6,7},{7,6},{8,9},{9,8},{10,11... | collective-permute-start | bytes 786440 | tf_op jit(solution)/shard_map/ppermute | solution.py:19
  19.3 1.8 %collective-permute-start.7 = (f32[64,1024]{1,0:T(8,128)S(1)}, f32[64,1024]{1,0:T(8,128)S(1)}, u32[]{:S(2)}, u32[]{:S(2)}) collective-permute-start(f32[64,1024]{1,0:T(8,128)S(1)} %slice.230), channel_id=1, source_target_pairs={{0,1},{1,0},{2,3},{3,2},{4,5},{5,4},{6,7},{7,6},{8,9},{9,8},{10,11... | collective-permute-start | bytes 786440 | tf_op jit(solution)/shard_map/ppermute | solution.py:19
  22.8 5.8 %collective-permute-start.9 = (f32[32,1024]{1,0:T(8,128)S(1)}, f32[32,1024]{1,0:T(8,128)S(1)}, u32[]{:S(2)}, u32[]{:S(2)}) collective-permute-start(f32[32,1024]{1,0:T(8,128)S(1)} %get-tuple-element.64), channel_id=1, source_target_pairs={{0,2},{1,3},{2,0},{3,1},{4,6},{5,7},{6,4},{7,5},{8,10},{9,11},{10,... | collective-permute-start | bytes 393224 | tf_op jit(solution)/shard_map/ppermute | solution.py:19
  24.1 1.4 %collective-permute-start.8 = (f32[32,1024]{1,0:T(8,128)S(1)}, f32[32,1024]{1,0:T(8,128)S(1)}, u32[]{:S(2)}, u32[]{:S(2)}) collective-permute-start(f32[32,1024]{1,0:T(8,128)S(1)} %get-tuple-element.64), channel_id=1, source_target_pairs={{0,1},{1,0},{2,3},{3,2},{4,5},{5,4},{6,7},{7,6},{8,9},{9,8},{10,11... | collective-permute-start | bytes 393224 | tf_op jit(solution)/shard_map/ppermute | solution.py:19
  28.6 1.3 %collective-permute-start.10 = (f32[32,1024]{1,0:T(8,128)S(1)}, f32[32,1024]{1,0:T(8,128)S(1)}, u32[]{:S(2)}, u32[]{:S(2)}) collective-permute-start(f32[32,1024]{1,0:T(8,128)S(1)} %collective-permute-done.9), channel_id=1, source_target_pairs={{0,1},{1,0},{2,3},{3,2},{4,5},{5,4},{6,7},{7,6},{8,9},{9,8},{10,11... | collective-permute-start | bytes 393224 | tf_op jit(solution)/shard_map/ppermute | solution.py:19
  31.3 5.6 %collective-permute-start.12 = (f32[32,1024]{1,0:T(8,128)S(1)}, f32[32,1024]{1,0:T(8,128)S(1)}, u32[]{:S(2)}, u32[]{:S(2)}) collective-permute-start(f32[32,1024]{1,0:T(8,128)S(1)} %get-tuple-element.78), channel_id=1, source_target_pairs={{0,2},{1,3},{2,0},{3,1},{4,6},{5,7},{6,4},{7,5},{8,10},{9,11},{10,... | collective-permute-start | bytes 393224 | tf_op jit(solution)/shard_map/ppermute | solution.py:19
  33.0 1.4 %collective-permute-start.11 = (f32[32,1024]{1,0:T(8,128)S(1)}, f32[32,1024]{1,0:T(8,128)S(1)}, u32[]{:S(2)}, u32[]{:S(2)}) collective-permute-start(f32[32,1024]{1,0:T(8,128)S(1)} %get-tuple-element.78), channel_id=1, source_target_pairs={{0,1},{1,0},{2,3},{3,2},{4,5},{5,4},{6,7},{7,6},{8,9},{9,8},{10,11... | collective-permute-start | bytes 393224 | tf_op jit(solution)/shard_map/ppermute | solution.py:19
  37.0 1.3 %collective-permute-start.13 = (f32[32,1024]{1,0:T(8,128)S(1)}, f32[32,1024]{1,0:T(8,128)S(1)}, u32[]{:S(2)}, u32[]{:S(2)}) collective-permute-start(f32[32,1024]{1,0:T(8,128)S(1)} %collective-permute-done.12), channel_id=1, source_target_pairs={{0,1},{1,0},{2,3},{3,2},{4,5},{5,4},{6,7},{7,6},{8,9},{9,8},{10,11... | collective-permute-start | bytes 393224 | tf_op jit(solution)/shard_map/ppermute | solution.py:19
  39.7 5.6 %collective-permute-start.15 = (f32[32,1024]{1,0:T(8,128)S(1)}, f32[32,1024]{1,0:T(8,128)S(1)}, u32[]{:S(2)}, u32[]{:S(2)}) collective-permute-start(f32[32,1024]{1,0:T(8,128)S(1)} %get-tuple-element.88), channel_id=1, source_target_pairs={{0,2},{1,3},{2,0},{3,1},{4,6},{5,7},{6,4},{7,5},{8,10},{9,11},{10,... | collective-permute-start | bytes 393224 | tf_op jit(solution)/shard_map/ppermute | solution.py:19
  41.2 1.4 %collective-permute-start.14 = (f32[32,1024]{1,0:T(8,128)S(1)}, f32[32,1024]{1,0:T(8,128)S(1)}, u32[]{:S(2)}, u32[]{:S(2)}) collective-permute-start(f32[32,1024]{1,0:T(8,128)S(1)} %get-tuple-element.88), channel_id=1, source_target_pairs={{0,1},{1,0},{2,3},{3,2},{4,5},{5,4},{6,7},{7,6},{8,9},{9,8},{10,11... | collective-permute-start | bytes 393224 | tf_op jit(solution)/shard_map/ppermute | solution.py:19
  45.4 1.3 %collective-permute-start.16 = (f32[32,1024]{1,0:T(8,128)S(1)}, f32[32,1024]{1,0:T(8,128)S(1)}, u32[]{:S(2)}, u32[]{:S(2)}) collective-permute-start(f32[32,1024]{1,0:T(8,128)S(1)} %collective-permute-done.15), channel_id=1, source_target_pairs={{0,1},{1,0},{2,3},{3,2},{4,5},{5,4},{6,7},{7,6},{8,9},{9,8},{10,11... | collective-permute-start | bytes 393224 | tf_op jit(solution)/shard_map/ppermute | solution.py:19
  50.1 1.2 %collective-permute-start.17 = (f32[32]{0:T(128)S(1)}, f32[32]{0:T(128)S(1)}, u32[]{:S(2)}, u32[]{:S(2)}) collective-permute-start(f32[32]{0:T(128)S(1)} %get-tuple-element.96), channel_id=1, source_target_pairs={{0,1},{1,0},{2,3},{3,2},{4,5},{5,4},{6,7},{7,6},{8,9},{9,8},{10,11... | collective-permute-start | bytes 392 | tf_op jit(solution)/shard_map/ppermute | solution.py:19

commit v29 on v27

--- a/solution.py
+++ b/solution.py
@@ -11,7 +11,7 @@
 TILE_BYTES = 16 << 20
 VMEM_BYTES = 16 << 20
 NORM_ROWS = 64
-BUILD_ROWS = 1024
+BUILD_ROWS = 512
 POINT_SCALE = math.sqrt(math.log2(math.e))
 
 

time: 52.2 us -> 52.3 us (level)
  no operation moved by 1% of the time
where the time goes in v29:
time: 52.3 us; the launch traced here: 52.1 us
  starting transfers between devices  16.4 us (31%)
  matrix products  11.5 us (22%)
  Pallas kernels  8.89 us (17%)
  waiting for transfers between devices  8.6 us (16%)
  other arithmetic  5.42 us (10%)
  between operations  0.98 us (2%)
    ppermute x18, starting transfers between devices, swap(): return lax.ppermute(x, 'blk', [(i, i ^ stride) for i in range(n)])  16.4 us
    dot_general x14, matrix products, apply_parts(): jnp.dot(jnp.concatenate([parts, parts], axis=1), piece, preferred_element...  11.5 us
    pallas_call x10, Pallas kernels, call(): pl.pallas_call(kernel, out_shape=outs, in_specs=[whole] * len(args), out_...  8.89 us
    ppermute x18, waiting for transfers between devices, swap(): return lax.ppermute(x, 'blk', [(i, i ^ stride) for i in range(n)])  8.6 us
  transfers between devices with their start and end apart: 18, of which 13 were waited for; matrix products, arithmetic and copies ran while one was open for 18% of the time, Pallas kernels for 14%

profile of v29, /device:TPU:0, one launch (start us, length us, event | category | flops | bytes accessed | tf_op | source)
XLA Modules:
  0.0 52.1 jit_solution(16294350651584287762)
XLA Ops:
  0.6 0.8 %select_maximum_fusion.part_ref = f32[72,256]{1,0:T(8,128)S(1)} fusion(f32[1,256]{1,0:T(1,128)} %bitcast.32, f32[32,256]{1,0:T(8,128)} %param.7, f32[32,256]{1,0:T(8,128)} %param.4), kind=kLoop, calls=%fused_computation.276 | loop fusion | flops 73728 | bytes 140288 | tf_op jit(solution)/shard_map/concatenate | solution.py:187
  1.4 4.0 %collective-permute-start = (f32[72,256]{1,0:T(8,128)S(1)}, f32[72,256]{1,0:T(8,128)S(1)}, u32[]{:S(2)}, u32[]{:S(2)}) collective-permute-start(f32[72,256]{1,0:T(8,128)S(1)} %select_maximum_fusion.part_ref), channel_id=1, source_target_pairs={{0,8},{1,9},{2,10},{3,11},{4,12},{5,13},{6,14},{7,15},{8,0},{9,1},... | collective-permute-start | bytes 221192 | tf_op jit(solution)/shard_map/ppermute | solution.py:19
  6.3 1.6 %collective-permute-start.4 = (f32[65,256]{1,0:T(8,128)S(1)}, f32[65,256]{1,0:T(8,128)S(1)}, u32[]{:S(2)}, u32[]{:S(2)}) collective-permute-start(f32[65,256]{1,0:T(8,128)S(1)} %get-tuple-element.49), channel_id=1, source_target_pairs={{0,2},{1,3},{2,0},{3,1},{4,6},{5,7},{6,4},{7,5},{8,10},{9,11},{10,... | collective-permute-start | bytes 199688 | tf_op jit(solution)/shard_map/ppermute | solution.py:19
  7.9 1.6 %collective-permute-start.1 = (f32[65,256]{1,0:T(8,128)S(1)}, f32[65,256]{1,0:T(8,128)S(1)}, u32[]{:S(2)}, u32[]{:S(2)}) collective-permute-start(f32[65,256]{1,0:T(8,128)S(1)} %get-tuple-element.49), channel_id=1, source_target_pairs={{0,4},{1,5},{2,6},{3,7},{4,0},{5,1},{6,2},{7,3},{8,12},{9,13},{10,... | collective-permute-start | bytes 199688 | tf_op jit(solution)/shard_map/ppermute | solution.py:19
  10.2 1.9 %collective-permute-start.6 = (f32[65,256]{1,0:T(8,128)S(1)}, f32[65,256]{1,0:T(8,128)S(1)}, u32[]{:S(2)}, u32[]{:S(2)}) collective-permute-start(f32[65,256]{1,0:T(8,128)S(1)} %get-tuple-element.53), channel_id=1, source_target_pairs={{0,2},{1,3},{2,0},{3,1},{4,6},{5,7},{6,4},{7,5},{8,10},{9,11},{10,... | collective-permute-start | bytes 199688 | tf_op jit(solution)/shard_map/ppermute | solution.py:19
  12.6 1.2 %collective-permute-done.2 = f32[72,256]{1,0:T(8,128)S(1)} collective-permute-done((f32[72,256]{1,0:T(8,128)S(1)}, f32[72,256]{1,0:T(8,128)S(1)}, u32[]{:S(2)}, u32[]{:S(2)}) %collective-permute-start.2) | collective-permute-done | bytes 73760 | tf_op jit(solution)/shard_map/ppermute | solution.py:19
  14.0 1.5 %collective-permute-start.5 = (f32[65,512]{1,0:T(8,128)S(1)}, f32[65,512]{1,0:T(8,128)S(1)}, u32[]{:S(2)}, u32[]{:S(2)}) collective-permute-start(f32[65,512]{1,0:T(8,128)S(1)} %get-tuple-element.52), channel_id=1, source_target_pairs={{0,2},{1,3},{2,0},{3,1},{4,6},{5,7},{6,4},{7,5},{8,10},{9,11},{10,... | collective-permute-start | bytes 399368 | tf_op jit(solution)/shard_map/ppermute | solution.py:19
  15.7 1.6 %shard_map.62 = (bf16[2048,1024]{1,0:T(8,128)(2,1)S(1)}, f32[32,1024]{1,0:T(8,128)S(1)}) custom-call(f32[32,1024]{1,0:T(8,128)S(1)} %get-tuple-element.121.rows_ref, f32[32,1]{1,0:T(8,128)S(1)} %copy.6.scale_ref, bf16[256,1024]{1,0:T(8,128)(2,1)S(1)} %constant_dynamic-update-slice_fusion.right_ref, f32[32,1024]{1,0:T(8,128)S(1)} %get-tuple-element.122.refs_0_, ...), custom_call_target="tpu_custom_call" | custom-call | flops 872415232 | bytes 4194304 | tf_op jit(solution)/shard_map/pallas_call | solution.py:114
  17.3 1.6 %shard_map.63 = (bf16[2048,1024]{1,0:T(8,128)(2,1)S(1)}, f32[32,1024]{1,0:T(8,128)S(1)}) custom-call(f32[32,1024]{1,0:T(8,128)S(1)} %get-tuple-element.126.rows_ref, f32[32,1]{1,0:T(8,128)S(1)} %copy.6.scale_ref, bf16[256,1024]{1,0:T(8,128)(2,1)S(1)} %constant_dynamic-update-slice_fusion.right_ref, f32[32,1024]{1,0:T(8,128)S(1)} %get-tuple-element.125.refs_0_, ...), custom_call_target="tpu_custom_call" | custom-call | flops 872415232 | bytes 4194304 | tf_op jit(solution)/shard_map/pallas_call | solution.py:114
  19.6 1.6 %shard_map.64 = (bf16[2048,1024]{1,0:T(8,128)(2,1)S(1)}, f32[32,1024]{1,0:T(8,128)S(1)}) custom-call(f32[32,1024]{1,0:T(8,128)S(1)} %get-tuple-element.69.rows_ref.part_ref, f32[32,1]{1,0:T(8,128)S(1)} %copy.6.scale_ref, bf16[256,1024]{1,0:T(8,128)(2,1)S(1)} %constant_dynamic-update-slice_fusion.right_ref, f32[32,1024]{1,0:T(8,128)S(1)} %get-tuple-element.118.refs_0_, ...), custom_call_target="tpu_custom_call" | custom-call | flops 872415232 | bytes 4194304 | tf_op jit(solution)/shard_map/pallas_call | solution.py:114
  21.2 1.6 %shard_map.65 = (bf16[2048,1024]{1,0:T(8,128)(2,1)S(1)}, f32[32,1024]{1,0:T(8,128)S(1)}) custom-call(f32[32,1024]{1,0:T(8,128)S(1)} %get-tuple-element.80.rows_ref, f32[32,1]{1,0:T(8,128)S(1)} %copy.6.scale_ref, bf16[256,1024]{1,0:T(8,128)(2,1)S(1)} %constant_dynamic-update-slice_fusion.right_ref, f32[32,1024]{1,0:T(8,128)S(1)} %get-tuple-element.123.refs_0_, ...), custom_call_target="tpu_custom_call" | custom-call | flops 872415232 | bytes 4194304 | tf_op jit(solution)/shard_map/pallas_call | solution.py:114
  22.9 1.3 %collective-permute-start.9 = (f32[32,1024]{1,0:T(8,128)S(1)}, f32[32,1024]{1,0:T(8,128)S(1)}, u32[]{:S(2)}, u32[]{:S(2)}) collective-permute-start(f32[32,1024]{1,0:T(8,128)S(1)} %get-tuple-element.64), channel_id=1, source_target_pairs={{0,2},{1,3},{2,0},{3,1},{4,6},{5,7},{6,4},{7,5},{8,10},{9,11},{10,... | collective-permute-start | bytes 393224 | tf_op jit(solution)/shard_map/ppermute | solution.py:19
  25.6 0.8 %convolution_add_fusion.6 = f32[96,1024]{1,0:T(8,128)S(1)} fusion(f32[96,1024]{1,0:T(8,128)S(1)} %fusion.6, bf16[2048,1024]{1,0:T(8,128)(2,1)S(1)} %get-tuple-element.67, bf16[32,1024]{1,0:T(8,128)(2,1)S(1)} %get-tuple-element.159, bf16[32,1024]{1,0:T(8,128)(2,1)S(1)} %get-tuple-element.160, bf16[32,1024]{1,0:T(8,128)(2,1)S(1)} %get-tuple-element.158), kind=kOutput, calls=%fused_computation.6 | convolution fusion | flops 405110784 | bytes 5177344 | tf_op jit(solution)/shard_map/dot_general | solution.py:152
  26.6 1.1 %shard_map.67 = bf16[2048,1024]{1,0:T(8,128)(2,1)S(1)} custom-call(f32[32,1024]{1,0:T(8,128)S(1)} %get-tuple-element.69.rows_ref.part_ref, f32[32,1]{1,0:T(8,128)S(1)} %copy.6.scale_ref, bf16[256,1024]{1,0:T(8,128)(2,1)S(1)} %shard_map.66.right_ref), custom_call_target="tpu_custom_call" | custom-call | flops 872415232 | bytes 4194304 | tf_op jit(solution)/shard_map/pallas_call | solution.py:114
  27.7 1.0 %collective-permute-done.9 = f32[32,1024]{1,0:T(8,128)S(1)} collective-permute-done((f32[32,1024]{1,0:T(8,128)S(1)}, f32[32,1024]{1,0:T(8,128)S(1)}, u32[]{:S(2)}, u32[]{:S(2)}) %collective-permute-start.9) | collective-permute-done | bytes 131104 | tf_op jit(solution)/shard_map/ppermute | solution.py:19
  28.7 0.8 %fusion.21 = f32[96,1024]{1,0:T(8,128)S(1)} fusion(bf16[2048,1024]{1,0:T(8,128)(2,1)S(1)} %get-tuple-element.73, bf16[32,1024]{1,0:T(8,128)(2,1)S(1)} %get-tuple-element.156, bf16[32,1024]{1,0:T(8,128)(2,1)S(1)} %get-tuple-element.157, bf16[32,1024]{1,0:T(8,128)(2,1)S(1)} %get-tuple-element.155), kind=kOutput, calls=%fused_computation.42 | convolution fusion | flops 405012480 | bytes 4784128 | tf_op jit(solution)/shard_map/dot_general | solution.py:152
  30.4 0.8 %convolution_add_fusion.5 = f32[96,1024]{1,0:T(8,128)S(1)} fusion(f32[96,1024]{1,0:T(8,128)S(1)} %fusion.21, bf16[2048,1024]{1,0:T(8,128)(2,1)S(1)} %get-tuple-element.77, bf16[32,1024]{1,0:T(8,128)(2,1)S(1)} %get-tuple-element.152, bf16[32,1024]{1,0:T(8,128)(2,1)S(1)} %get-tuple-element.153, bf16[32,1024]{1,0:T(8,128)(2,1)S(1)} %get-tuple-element.151), kind=kOutput, calls=%fused_computation.5 | convolution fusion | flops 405110784 | bytes 5177344 | tf_op jit(solution)/shard_map/dot_general | solution.py:152
  31.4 1.5 %collective-permute-start.12 = (f32[32,1024]{1,0:T(8,128)S(1)}, f32[32,1024]{1,0:T(8,128)S(1)}, u32[]{:S(2)}, u32[]{:S(2)}) collective-permute-start(f32[32,1024]{1,0:T(8,128)S(1)} %get-tuple-element.78), channel_id=1, source_target_pairs={{0,2},{1,3},{2,0},{3,1},{4,6},{5,7},{6,4},{7,5},{8,10},{9,11},{10,... | collective-permute-start | bytes 393224 | tf_op jit(solution)/shard_map/ppermute | solution.py:19
  33.1 1.0 %fusion.44 = f32[96,1024]{1,0:T(8,128)S(1)} fusion(bf16[2048,1024]{1,0:T(8,128)(2,1)S(1)} %get-tuple-element.66, bf16[96,1024]{1,0:T(8,128)(2,1)S(1)} %pad_maximum_fusion.3), kind=kOutput, calls=%fused_computation.65 | convolution fusion | flops 403439616 | bytes 4784128 | tf_op jit(solution)/shard_map/dot_general | solution.py:152
  34.5 0.8 %convolution_add_fusion.4 = f32[96,1024]{1,0:T(8,128)S(1)} fusion(f32[96,1024]{1,0:T(8,128)S(1)} %fusion.44, bf16[2048,1024]{1,0:T(8,128)(2,1)S(1)} %get-tuple-element.67, bf16[32,1024]{1,0:T(8,128)(2,1)S(1)} %get-tuple-element.147, bf16[32,1024]{1,0:T(8,128)(2,1)S(1)} %get-tuple-element.148, bf16[32,1024]{1,0:T(8,128)(2,1)S(1)} %get-tuple-element.146), kind=kOutput, calls=%fused_computation.4 | convolution fusion | flops 405110784 | bytes 5177344 | tf_op jit(solution)/shard_map/dot_general | solution.py:152
  35.3 1.1 %shard_map.68 = bf16[2048,1024]{1,0:T(8,128)(2,1)S(1)} custom-call(f32[32,1024]{1,0:T(8,128)S(1)} %get-tuple-element.80.rows_ref, f32[32,1]{1,0:T(8,128)S(1)} %copy.6.scale_ref, bf16[256,1024]{1,0:T(8,128)(2,1)S(1)} %shard_map.66.right_ref), custom_call_target="tpu_custom_call" | custom-call | flops 872415232 | bytes 4194304 | tf_op jit(solution)/shard_map/pallas_call | solution.py:114
  37.1 0.8 %fusion.59 = f32[96,1024]{1,0:T(8,128)S(1)} fusion(bf16[2048,1024]{1,0:T(8,128)(2,1)S(1)} %get-tuple-element.73, bf16[32,1024]{1,0:T(8,128)(2,1)S(1)} %get-tuple-element.144, bf16[32,1024]{1,0:T(8,128)(2,1)S(1)} %get-tuple-element.145, bf16[32,1024]{1,0:T(8,128)(2,1)S(1)} %get-tuple-element.143), kind=kOutput, calls=%fused_computation.80 | convolution fusion | flops 405012480 | bytes 4784128 | tf_op jit(solution)/shard_map/dot_general | solution.py:152
  38.8 0.8 %convolution_add_fusion.3 = f32[96,1024]{1,0:T(8,128)S(1)} fusion(f32[96,1024]{1,0:T(8,128)S(1)} %fusion.59, bf16[2048,1024]{1,0:T(8,128)(2,1)S(1)} %get-tuple-element.77, bf16[32,1024]{1,0:T(8,128)(2,1)S(1)} %get-tuple-element.140, bf16[32,1024]{1,0:T(8,128)(2,1)S(1)} %get-tuple-element.141, bf16[32,1024]{1,0:T(8,128)(2,1)S(1)} %get-tuple-element.139), kind=kOutput, calls=%fused_computation.3 | convolution fusion | flops 405110784 | bytes 5177344 | tf_op jit(solution)/shard_map/dot_general | solution.py:152
  39.8 1.5 %collective-permute-start.15 = (f32[32,1024]{1,0:T(8,128)S(1)}, f32[32,1024]{1,0:T(8,128)S(1)}, u32[]{:S(2)}, u32[]{:S(2)}) collective-permute-start(f32[32,1024]{1,0:T(8,128)S(1)} %get-tuple-element.88), channel_id=1, source_target_pairs={{0,2},{1,3},{2,0},{3,1},{4,6},{5,7},{6,4},{7,5},{8,10},{9,11},{10,... | collective-permute-start | bytes 393224 | tf_op jit(solution)/shard_map/ppermute | solution.py:19
  41.5 0.8 %fusion.82 = f32[96,1024]{1,0:T(8,128)S(1)} fusion(bf16[2048,1024]{1,0:T(8,128)(2,1)S(1)} %get-tuple-element.66, bf16[96,1024]{1,0:T(8,128)(2,1)S(1)} %pad_maximum_fusion.4), kind=kOutput, calls=%fused_computation.103 | convolution fusion | flops 403439616 | bytes 4784128 | tf_op jit(solution)/shard_map/dot_general | solution.py:152
  42.7 0.8 %convolution_add_fusion.2 = f32[96,1024]{1,0:T(8,128)S(1)} fusion(f32[96,1024]{1,0:T(8,128)S(1)} %fusion.82, bf16[2048,1024]{1,0:T(8,128)(2,1)S(1)} %get-tuple-element.67, bf16[32,1024]{1,0:T(8,128)(2,1)S(1)} %get-tuple-element.135, bf16[32,1024]{1,0:T(8,128)(2,1)S(1)} %get-tuple-element.136, bf16[32,1024]{1,0:T(8,128)(2,1)S(1)} %get-tuple-element.134), kind=kOutput, calls=%fused_computation.2 | convolution fusion | flops 405110784 | bytes 5177344 | tf_op jit(solution)/shard_map/dot_general | solution.py:152
  43.5 1.9 %collective-permute-done.15 = f32[32,1024]{1,0:T(8,128)S(1)} collective-permute-done((f32[32,1024]{1,0:T(8,128)S(1)}, f32[32,1024]{1,0:T(8,128)S(1)}, u32[]{:S(2)}, u32[]{:S(2)}) %collective-permute-start.15) | collective-permute-done | bytes 131104 | tf_op jit(solution)/shard_map/ppermute | solution.py:19
  45.4 0.8 %fusion.97 = f32[96,1024]{1,0:T(8,128)S(1)} fusion(bf16[2048,1024]{1,0:T(8,128)(2,1)S(1)} %get-tuple-element.73, bf16[32,1024]{1,0:T(8,128)(2,1)S(1)} %get-tuple-element.132, bf16[32,1024]{1,0:T(8,128)(2,1)S(1)} %get-tuple-element.133, bf16[32,1024]{1,0:T(8,128)(2,1)S(1)} %get-tuple-element.131), kind=kOutput, calls=%fused_computation.118 | convolution fusion | flops 405012480 | bytes 4784128 | tf_op jit(solution)/shard_map/dot_general | solution.py:152
  47.4 0.8 %convolution_add_fusion.1 = f32[96,1024]{1,0:T(8,128)S(1)} fusion(f32[96,1024]{1,0:T(8,128)S(1)} %fusion.97, bf16[2048,1024]{1,0:T(8,128)(2,1)S(1)} %get-tuple-element.77, bf16[32,1024]{1,0:T(8,128)(2,1)S(1)} %get-tuple-element.128, bf16[32,1024]{1,0:T(8,128)(2,1)S(1)} %get-tuple-element.129, bf16[32,1024]{1,0:T(8,128)(2,1)S(1)} %get-tuple-element.127), kind=kOutput, calls=%fused_computation.1 | convolution fusion | flops 405110784 | bytes 5177344 | tf_op jit(solution)/shard_map/dot_general | solution.py:152
  48.2 0.8 %fusion.120 = f32[96,1024]{1,0:T(8,128)S(1)} fusion(bf16[2048,1024]{1,0:T(8,128)(2,1)S(1)} %shard_map.67, bf16[32,1024]{1,0:T(8,128)(2,1)S(1)} %get-tuple-element.114, bf16[32,1024]{1,0:T(8,128)(2,1)S(1)} %get-tuple-element.113, bf16[32,1024]{1,0:T(8,128)(2,1)S(1)} %get-tuple-element.117), kind=kOutput, calls=%fused_computation.141 | convolution fusion | flops 405012480 | bytes 4784128 | tf_op jit(solution)/shard_map/dot_general | solution.py:152
  49.0 0.8 %convolution_add_fusion = f32[96,1024]{1,0:T(8,128)S(1)} fusion(f32[96,1024]{1,0:T(8,128)S(1)} %fusion.120, bf16[2048,1024]{1,0:T(8,128)(2,1)S(1)} %shard_map.68, bf16[32,1024]{1,0:T(8,128)(2,1)S(1)} %get-tuple-element.115, bf16[32,1024]{1,0:T(8,128)(2,1)S(1)} %get-tuple-element.116, bf16[32,1024]{1,0:T(8,128)(2,1)S(1)} %get-tuple-element.112), kind=kOutput, calls=%fused_computation | convolution fusion | flops 405110784 | bytes 5177344 | tf_op jit(solution)/shard_map/dot_general | solution.py:152
  50.4 0.9 %collective-permute-done.17 = f32[32]{0:T(128)S(1)} collective-permute-done((f32[32]{0:T(128)S(1)}, f32[32]{0:T(128)S(1)}, u32[]{:S(2)}, u32[]{:S(2)}) %collective-permute-start.17) | collective-permute-done | bytes 160 | tf_op jit(solution)/shard_map/ppermute | solution.py:19
  (86 shorter events, 11.4 us)
Async XLA Ops:
  1.4 8.1 %collective-permute-start = (f32[72,256]{1,0:T(8,128)S(1)}, f32[72,256]{1,0:T(8,128)S(1)}, u32[]{:S(2)}, u32[]{:S(2)}) collective-permute-start(f32[72,256]{1,0:T(8,128)S(1)} %select_maximum_fusion.part_ref), channel_id=1, source_target_pairs={{0,8},{1,9},{2,10},{3,11},{4,12},{5,13},{6,14},{7,15},{8,0},{9,1},... | collective-permute-start | bytes 221192 | tf_op jit(solution)/shard_map/ppermute | solution.py:19
  6.3 7.7 %collective-permute-start.4 = (f32[65,256]{1,0:T(8,128)S(1)}, f32[65,256]{1,0:T(8,128)S(1)}, u32[]{:S(2)}, u32[]{:S(2)}) collective-permute-start(f32[65,256]{1,0:T(8,128)S(1)} %get-tuple-element.49), channel_id=1, source_target_pairs={{0,2},{1,3},{2,0},{3,1},{4,6},{5,7},{6,4},{7,5},{8,10},{9,11},{10,... | collective-permute-start | bytes 199688 | tf_op jit(solution)/shard_map/ppermute | solution.py:19
  7.9 4.7 %collective-permute-start.1 = (f32[65,256]{1,0:T(8,128)S(1)}, f32[65,256]{1,0:T(8,128)S(1)}, u32[]{:S(2)}, u32[]{:S(2)}) collective-permute-start(f32[65,256]{1,0:T(8,128)S(1)} %get-tuple-element.49), channel_id=1, source_target_pairs={{0,4},{1,5},{2,6},{3,7},{4,0},{5,1},{6,2},{7,3},{8,12},{9,13},{10,... | collective-permute-start | bytes 199688 | tf_op jit(solution)/shard_map/ppermute | solution.py:19
  9.5 4.4 %collective-permute-start.2 = (f32[72,256]{1,0:T(8,128)S(1)}, f32[72,256]{1,0:T(8,128)S(1)}, u32[]{:S(2)}, u32[]{:S(2)}) collective-permute-start(f32[72,256]{1,0:T(8,128)S(1)} %collective-permute-done.part_ref), channel_id=1, source_target_pairs={{0,4},{1,5},{2,6},{3,7},{4,0},{5,1},{6,2},{7,3},{8,12},{9,13},{10,... | collective-permute-start | bytes 221192 | tf_op jit(solution)/shard_map/ppermute | solution.py:19
  10.2 8.7 %collective-permute-start.6 = (f32[65,256]{1,0:T(8,128)S(1)}, f32[65,256]{1,0:T(8,128)S(1)}, u32[]{:S(2)}, u32[]{:S(2)}) collective-permute-start(f32[65,256]{1,0:T(8,128)S(1)} %get-tuple-element.53), channel_id=1, source_target_pairs={{0,2},{1,3},{2,0},{3,1},{4,6},{5,7},{6,4},{7,5},{8,10},{9,11},{10,... | collective-permute-start | bytes 199688 | tf_op jit(solution)/shard_map/ppermute | solution.py:19
  14.0 5.2 %collective-permute-start.5 = (f32[65,512]{1,0:T(8,128)S(1)}, f32[65,512]{1,0:T(8,128)S(1)}, u32[]{:S(2)}, u32[]{:S(2)}) collective-permute-start(f32[65,512]{1,0:T(8,128)S(1)} %get-tuple-element.52), channel_id=1, source_target_pairs={{0,2},{1,3},{2,0},{3,1},{4,6},{5,7},{6,4},{7,5},{8,10},{9,11},{10,... | collective-permute-start | bytes 399368 | tf_op jit(solution)/shard_map/ppermute | solution.py:19
  15.6 1.7 %collective-permute-start.3 = (f32[64,1024]{1,0:T(8,128)S(1)}, f32[64,1024]{1,0:T(8,128)S(1)}, u32[]{:S(2)}, u32[]{:S(2)}) collective-permute-start(f32[64,1024]{1,0:T(8,128)S(1)} %slice.225), channel_id=1, source_target_pairs={{0,1},{1,0},{2,3},{3,2},{4,5},{5,4},{6,7},{7,6},{8,9},{9,8},{10,11... | collective-permute-start | bytes 786440 | tf_op jit(solution)/shard_map/ppermute | solution.py:19
  19.3 1.9 %collective-permute-start.7 = (f32[64,1024]{1,0:T(8,128)S(1)}, f32[64,1024]{1,0:T(8,128)S(1)}, u32[]{:S(2)}, u32[]{:S(2)}) collective-permute-start(f32[64,1024]{1,0:T(8,128)S(1)} %slice.230), channel_id=1, source_target_pairs={{0,1},{1,0},{2,3},{3,2},{4,5},{5,4},{6,7},{7,6},{8,9},{9,8},{10,11... | collective-permute-start | bytes 786440 | tf_op jit(solution)/shard_map/ppermute | solution.py:19
  22.9 5.8 %collective-permute-start.9 = (f32[32,1024]{1,0:T(8,128)S(1)}, f32[32,1024]{1,0:T(8,128)S(1)}, u32[]{:S(2)}, u32[]{:S(2)}) collective-permute-start(f32[32,1024]{1,0:T(8,128)S(1)} %get-tuple-element.64), channel_id=1, source_target_pairs={{0,2},{1,3},{2,0},{3,1},{4,6},{5,7},{6,4},{7,5},{8,10},{9,11},{10,... | collective-permute-start | bytes 393224 | tf_op jit(solution)/shard_map/ppermute | solution.py:19
  24.2 1.4 %collective-permute-start.8 = (f32[32,1024]{1,0:T(8,128)S(1)}, f32[32,1024]{1,0:T(8,128)S(1)}, u32[]{:S(2)}, u32[]{:S(2)}) collective-permute-start(f32[32,1024]{1,0:T(8,128)S(1)} %get-tuple-element.64), channel_id=1, source_target_pairs={{0,1},{1,0},{2,3},{3,2},{4,5},{5,4},{6,7},{7,6},{8,9},{9,8},{10,11... | collective-permute-start | bytes 393224 | tf_op jit(solution)/shard_map/ppermute | solution.py:19
  28.7 1.3 %collective-permute-start.10 = (f32[32,1024]{1,0:T(8,128)S(1)}, f32[32,1024]{1,0:T(8,128)S(1)}, u32[]{:S(2)}, u32[]{:S(2)}) collective-permute-start(f32[32,1024]{1,0:T(8,128)S(1)} %collective-permute-done.9), channel_id=1, source_target_pairs={{0,1},{1,0},{2,3},{3,2},{4,5},{5,4},{6,7},{7,6},{8,9},{9,8},{10,11... | collective-permute-start | bytes 393224 | tf_op jit(solution)/shard_map/ppermute | solution.py:19
  31.4 5.6 %collective-permute-start.12 = (f32[32,1024]{1,0:T(8,128)S(1)}, f32[32,1024]{1,0:T(8,128)S(1)}, u32[]{:S(2)}, u32[]{:S(2)}) collective-permute-start(f32[32,1024]{1,0:T(8,128)S(1)} %get-tuple-element.78), channel_id=1, source_target_pairs={{0,2},{1,3},{2,0},{3,1},{4,6},{5,7},{6,4},{7,5},{8,10},{9,11},{10,... | collective-permute-start | bytes 393224 | tf_op jit(solution)/shard_map/ppermute | solution.py:19
  33.0 1.4 %collective-permute-start.11 = (f32[32,1024]{1,0:T(8,128)S(1)}, f32[32,1024]{1,0:T(8,128)S(1)}, u32[]{:S(2)}, u32[]{:S(2)}) collective-permute-start(f32[32,1024]{1,0:T(8,128)S(1)} %get-tuple-element.78), channel_id=1, source_target_pairs={{0,1},{1,0},{2,3},{3,2},{4,5},{5,4},{6,7},{7,6},{8,9},{9,8},{10,11... | collective-permute-start | bytes 393224 | tf_op jit(solution)/shard_map/ppermute | solution.py:19
  37.0 1.3 %collective-permute-start.13 = (f32[32,1024]{1,0:T(8,128)S(1)}, f32[32,1024]{1,0:T(8,128)S(1)}, u32[]{:S(2)}, u32[]{:S(2)}) collective-permute-start(f32[32,1024]{1,0:T(8,128)S(1)} %collective-permute-done.12), channel_id=1, source_target_pairs={{0,1},{1,0},{2,3},{3,2},{4,5},{5,4},{6,7},{7,6},{8,9},{9,8},{10,11... | collective-permute-start | bytes 393224 | tf_op jit(solution)/shard_map/ppermute | solution.py:19
  39.8 5.6 %collective-permute-start.15 = (f32[32,1024]{1,0:T(8,128)S(1)}, f32[32,1024]{1,0:T(8,128)S(1)}, u32[]{:S(2)}, u32[]{:S(2)}) collective-permute-start(f32[32,1024]{1,0:T(8,128)S(1)} %get-tuple-element.88), channel_id=1, source_target_pairs={{0,2},{1,3},{2,0},{3,1},{4,6},{5,7},{6,4},{7,5},{8,10},{9,11},{10,... | collective-permute-start | bytes 393224 | tf_op jit(solution)/shard_map/ppermute | solution.py:19
  41.3 1.4 %collective-permute-start.14 = (f32[32,1024]{1,0:T(8,128)S(1)}, f32[32,1024]{1,0:T(8,128)S(1)}, u32[]{:S(2)}, u32[]{:S(2)}) collective-permute-start(f32[32,1024]{1,0:T(8,128)S(1)} %get-tuple-element.88), channel_id=1, source_target_pairs={{0,1},{1,0},{2,3},{3,2},{4,5},{5,4},{6,7},{7,6},{8,9},{9,8},{10,11... | collective-permute-start | bytes 393224 | tf_op jit(solution)/shard_map/ppermute | solution.py:19
  45.4 1.3 %collective-permute-start.16 = (f32[32,1024]{1,0:T(8,128)S(1)}, f32[32,1024]{1,0:T(8,128)S(1)}, u32[]{:S(2)}, u32[]{:S(2)}) collective-permute-start(f32[32,1024]{1,0:T(8,128)S(1)} %collective-permute-done.15), channel_id=1, source_target_pairs={{0,1},{1,0},{2,3},{3,2},{4,5},{5,4},{6,7},{7,6},{8,9},{9,8},{10,11... | collective-permute-start | bytes 393224 | tf_op jit(solution)/shard_map/ppermute | solution.py:19
  50.2 1.2 %collective-permute-start.17 = (f32[32]{0:T(128)S(1)}, f32[32]{0:T(128)S(1)}, u32[]{:S(2)}, u32[]{:S(2)}) collective-permute-start(f32[32]{0:T(128)S(1)} %get-tuple-element.96), channel_id=1, source_target_pairs={{0,1},{1,0},{2,3},{3,2},{4,5},{5,4},{6,7},{7,6},{8,9},{9,8},{10,11... | collective-permute-start | bytes 392 | tf_op jit(solution)/shard_map/ppermute | solution.py:19

commit v30 on v26

--- a/solution.py
+++ b/solution.py
@@ -73,7 +73,6 @@
         probes = vectors_ref.shape[0]
         high, rest = halve(vectors_ref[...])
         mid, rest = halve(rest)
-        twice = jnp.concatenate([high, mid], axis=0)
         thrice = jnp.concatenate([high, mid, rest.astype(jnp.bfloat16)], axis=0)
     steps = [(top, at) for top in range(0, total, block) for at in range(0, cols, step)]
     lefts, powers, parts = {}, {}, {}
@@ -92,10 +91,10 @@
 
     def apply(top, at):
         down, here = slice(top, top + block), slice(at, at + step)
-        high, low = parts.pop((top, at))
-        large = jnp.dot(thrice[:, down], high, preferred_element_type=jnp.float32)
-        small = jnp.dot(twice[:, down], low, preferred_element_type=jnp.float32)
-        term = large[:probes] + ((large[probes : 2 * probes] + small[:probes]) + (large[2 * probes :] + small[probes:]))
+        vectors = jnp.concatenate([thrice[:, down]] * 2, axis=1)
+        both = jnp.concatenate(parts.pop((top, at)), axis=0)
+        term = jnp.dot(vectors, both, preferred_element_type=jnp.float32)
+        term = term[:probes] + (term[probes : 2 * probes] + term[2 * probes :])
         before = sum_ref if top == 0 else out_ref
         out_ref[:, here] = before[:, here] + term
 
@@ -254,9 +253,7 @@
             return [collect(x) for x in jnp.split(apply_parts(stack(vectors), far_tile[0]), len(vectors))]
 
         def far_cross_product(vectors):
-            low, high = zip(*[cut(x) for x in vectors])
-            terms = [apply_parts(stack(x), piece) for x, piece in zip((low, high), far_tile[1])]
-            return [join(*[collect(x) for x in pair]) for pair in zip(*[jnp.split(x, len(vectors)) for x in terms])]
+            return join(*[collect(apply_piece(x, piece)) for x, piece in zip(cut(vectors), far_tile[1])])
 
         def far_build():
             nonlocal right_far
@@ -280,9 +277,7 @@
                     far_tile.append(piece)
                 elif far_rows:
                     state, near = fence(([residual, direction], near))
-                    known = [far_own_product([v[:, 2 * cols : 3 * cols] for v in state])]
-                    known.append(far_cross_product([v[:, 3 * cols :] for v in state]))
-                    known, near = fence((known, near))
+                    known, near = fence((far_own_product([v[:, 2 * cols : 3 * cols] for v in state]), near))
                 arrived, near = fence((arrived, near))
                 sent.append(arrived)
                 pieces.append(arrived)
@@ -300,7 +295,7 @@
             if len(inner) > 1:
                 far = far + apply_piece(pieces[-1], tile[-1])
             if known:
-                known = [[*known[0], own_term], [*known[1], *far_cross_product(pieces[-1:])]]
+                known.append(own_term)
             return collect(far), collect(near) + collect(far) + noise * x, join(*pieces), curve, known
 
         residual = direction = join(*starts)
@@ -322,8 +317,9 @@
             norm_now = norm_next
         mine = direction[:, :cols]
         if far_rows:
-            own_part, cross = [of_res + ratio * of_dir - step_size * of_app for of_res, of_dir, of_app in known]
-            side = direction[:, 2 * cols : 3 * cols]
+            of_residual, of_direction, of_applied = known
+            own_part = of_residual + ratio * of_direction - step_size * of_applied
+            side, cross = direction[:, 2 * cols : 3 * cols], far_cross_product(direction[:, 3 * cols :])
             far_terms = side * (own_part + noise_beside * side) + 2.0 * join(*paired(side)) * cross
             curve = add_up(jnp.sum(mine * (my_applied + my_far) + far_terms, axis=1), n, [1])
         else:

time: 52.6 us -> 52 us (0.989)
  waiting for transfers between devices: 6.36 us -> 7.1 us
  matrix products: 13.1 us -> 12.4 us
    ppermute x18, waiting for transfers between devices: 6.36 us -> 7.1 us  [swap(): return lax.ppermute(x, 'blk', [(i, i ^ stride) for i in range(n)])]
    dot_general x18 -> x16, matrix products: 13.1 us -> 12.4 us  [apply_parts(): jnp.dot(jnp.concatenate([parts, parts], axis=1), piece, preferred_element...]
  transfers between devices with their start and end apart: 18 -> 18, of which waited for: 11 -> 12; matrix products, arithmetic and copies ran while one was open for 24% -> 22% of each run, Pallas kernels for 14% -> 14%
where the time goes in v30:
time: 52 us; the launch traced here: 51.8 us
  starting transfers between devices  16.7 us (32%)
  matrix products  12.4 us (24%)
  Pallas kernels  8.56 us (16%)
  waiting for transfers between devices  7.1 us (14%)
  other arithmetic  5.7 us (11%)
  between operations  1.11 us (2%)
    ppermute x18, starting transfers between devices, swap(): return lax.ppermute(x, 'blk', [(i, i ^ stride) for i in range(n)])  16.7 us
    dot_general x16, matrix products, apply_parts(): jnp.dot(jnp.concatenate([parts, parts], axis=1), piece, preferred_element...  12.4 us
    pallas_call x11, Pallas kernels, call(): pl.pallas_call(kernel, out_shape=outs, in_specs=[whole] * len(args), out_...  8.56 us
    ppermute x18, waiting for transfers between devices, swap(): return lax.ppermute(x, 'blk', [(i, i ^ stride) for i in range(n)])  7.1 us
  transfers between devices with their start and end apart: 18, of which 12 were waited for; matrix products, arithmetic and copies ran while one was open for 22% of the time, Pallas kernels for 14%

profile of v30, /device:TPU:0, one launch (start us, length us, event | category | flops | bytes accessed | tf_op | source)
XLA Modules:
  0.0 51.8 jit_solution(14836000530923481263)
XLA Ops:
  0.6 0.8 %select_maximum_fusion.part_ref = f32[72,256]{1,0:T(8,128)S(1)} fusion(f32[1,256]{1,0:T(1,128)} %bitcast.34, f32[32,256]{1,0:T(8,128)} %param.7, f32[32,256]{1,0:T(8,128)} %param.4), kind=kLoop, calls=%fused_computation.284 | loop fusion | flops 73728 | bytes 140288 | tf_op jit(solution)/shard_map/concatenate | solution.py:196
  1.4 4.0 %collective-permute-start = (f32[72,256]{1,0:T(8,128)S(1)}, f32[72,256]{1,0:T(8,128)S(1)}, u32[]{:S(2)}, u32[]{:S(2)}) collective-permute-start(f32[72,256]{1,0:T(8,128)S(1)} %select_maximum_fusion.part_ref), channel_id=1, source_target_pairs={{0,8},{1,9},{2,10},{3,11},{4,12},{5,13},{6,14},{7,15},{8,0},{9,1},... | collective-permute-start | bytes 221192 | tf_op jit(solution)/shard_map/ppermute | solution.py:19
  6.3 1.6 %collective-permute-start.4 = (f32[65,256]{1,0:T(8,128)S(1)}, f32[65,256]{1,0:T(8,128)S(1)}, u32[]{:S(2)}, u32[]{:S(2)}) collective-permute-start(f32[65,256]{1,0:T(8,128)S(1)} %get-tuple-element.57), channel_id=1, source_target_pairs={{0,2},{1,3},{2,0},{3,1},{4,6},{5,7},{6,4},{7,5},{8,10},{9,11},{10,... | collective-permute-start | bytes 199688 | tf_op jit(solution)/shard_map/ppermute | solution.py:19
  7.9 1.6 %collective-permute-start.1 = (f32[65,256]{1,0:T(8,128)S(1)}, f32[65,256]{1,0:T(8,128)S(1)}, u32[]{:S(2)}, u32[]{:S(2)}) collective-permute-start(f32[65,256]{1,0:T(8,128)S(1)} %get-tuple-element.57), channel_id=1, source_target_pairs={{0,4},{1,5},{2,6},{3,7},{4,0},{5,1},{6,2},{7,3},{8,12},{9,13},{10,... | collective-permute-start | bytes 199688 | tf_op jit(solution)/shard_map/ppermute | solution.py:19
  10.2 1.9 %collective-permute-start.6 = (f32[65,256]{1,0:T(8,128)S(1)}, f32[65,256]{1,0:T(8,128)S(1)}, u32[]{:S(2)}, u32[]{:S(2)}) collective-permute-start(f32[65,256]{1,0:T(8,128)S(1)} %get-tuple-element.61), channel_id=1, source_target_pairs={{0,2},{1,3},{2,0},{3,1},{4,6},{5,7},{6,4},{7,5},{8,10},{9,11},{10,... | collective-permute-start | bytes 199688 | tf_op jit(solution)/shard_map/ppermute | solution.py:19
  12.6 1.2 %collective-permute-done.2 = f32[72,256]{1,0:T(8,128)S(1)} collective-permute-done((f32[72,256]{1,0:T(8,128)S(1)}, f32[72,256]{1,0:T(8,128)S(1)}, u32[]{:S(2)}, u32[]{:S(2)}) %collective-permute-start.2) | collective-permute-done | bytes 73760 | tf_op jit(solution)/shard_map/ppermute | solution.py:19
  14.0 1.5 %collective-permute-start.5 = (f32[65,512]{1,0:T(8,128)S(1)}, f32[65,512]{1,0:T(8,128)S(1)}, u32[]{:S(2)}, u32[]{:S(2)}) collective-permute-start(f32[65,512]{1,0:T(8,128)S(1)} %get-tuple-element.60), channel_id=1, source_target_pairs={{0,2},{1,3},{2,0},{3,1},{4,6},{5,7},{6,4},{7,5},{8,10},{9,11},{10,... | collective-permute-start | bytes 399368 | tf_op jit(solution)/shard_map/ppermute | solution.py:19
  15.7 1.5 %shard_map.62 = (bf16[2048,1024]{1,0:T(8,128)(2,1)S(1)}, f32[32,1024]{1,0:T(8,128)S(1)}) custom-call(f32[32,1024]{1,0:T(8,128)S(1)} %get-tuple-element.143.rows_ref, f32[32,1]{1,0:T(8,128)S(1)} %copy.6.scale_ref, bf16[256,1024]{1,0:T(8,128)(2,1)S(1)} %constant_dynamic-update-slice_fusion.right_ref, f32[32,1024]{1,0:T(8,128)S(1)} %get-tuple-element.144.refs_0_, ...), custom_call_target="tpu_custom_call" | custom-call | flops 872415232 | bytes 4194304 | tf_op jit(solution)/shard_map/pallas_call | solution.py:114
  17.3 1.5 %shard_map.63 = (bf16[2048,1024]{1,0:T(8,128)(2,1)S(1)}, f32[32,1024]{1,0:T(8,128)S(1)}) custom-call(f32[32,1024]{1,0:T(8,128)S(1)} %get-tuple-element.148.rows_ref, f32[32,1]{1,0:T(8,128)S(1)} %copy.6.scale_ref, bf16[256,1024]{1,0:T(8,128)(2,1)S(1)} %constant_dynamic-update-slice_fusion.right_ref, f32[32,1024]{1,0:T(8,128)S(1)} %get-tuple-element.147.refs_0_, ...), custom_call_target="tpu_custom_call" | custom-call | flops 872415232 | bytes 4194304 | tf_op jit(solution)/shard_map/pallas_call | solution.py:114
  19.5 1.5 %shard_map.64 = (bf16[2048,1024]{1,0:T(8,128)(2,1)S(1)}, f32[32,1024]{1,0:T(8,128)S(1)}) custom-call(f32[32,1024]{1,0:T(8,128)S(1)} %get-tuple-element.76.rows_ref.part_ref, f32[32,1]{1,0:T(8,128)S(1)} %copy.6.scale_ref, bf16[256,1024]{1,0:T(8,128)(2,1)S(1)} %constant_dynamic-update-slice_fusion.right_ref, f32[32,1024]{1,0:T(8,128)S(1)} %get-tuple-element.140.refs_0_, ...), custom_call_target="tpu_custom_call" | custom-call | flops 872415232 | bytes 4194304 | tf_op jit(solution)/shard_map/pallas_call | solution.py:114
  21.1 1.5 %shard_map.65 = (bf16[2048,1024]{1,0:T(8,128)(2,1)S(1)}, f32[32,1024]{1,0:T(8,128)S(1)}) custom-call(f32[32,1024]{1,0:T(8,128)S(1)} %get-tuple-element.88.rows_ref, f32[32,1]{1,0:T(8,128)S(1)} %copy.6.scale_ref, bf16[256,1024]{1,0:T(8,128)(2,1)S(1)} %constant_dynamic-update-slice_fusion.right_ref, f32[32,1024]{1,0:T(8,128)S(1)} %get-tuple-element.145.refs_0_, ...), custom_call_target="tpu_custom_call" | custom-call | flops 872415232 | bytes 4194304 | tf_op jit(solution)/shard_map/pallas_call | solution.py:114
  22.7 1.4 %collective-permute-start.9 = (f32[32,1024]{1,0:T(8,128)S(1)}, f32[32,1024]{1,0:T(8,128)S(1)}, u32[]{:S(2)}, u32[]{:S(2)}) collective-permute-start(f32[32,1024]{1,0:T(8,128)S(1)} %get-tuple-element.72), channel_id=1, source_target_pairs={{0,2},{1,3},{2,0},{3,1},{4,6},{5,7},{6,4},{7,5},{8,10},{9,11},{10,... | collective-permute-start | bytes 393224 | tf_op jit(solution)/shard_map/ppermute | solution.py:19
  24.4 0.8 %fusion.10 = f32[96,1024]{1,0:T(8,128)S(1)} fusion(bf16[2048,1024]{1,0:T(8,128)(2,1)S(1)} %get-tuple-element.74, bf16[96,1024]{1,0:T(8,128)(2,1)S(1)} %pad_maximum_fusion.2), kind=kOutput, calls=%fused_computation.30 | convolution fusion | flops 403439616 | bytes 4784128 | tf_op jit(solution)/shard_map/dot_general | solution.py:156
  25.5 0.8 %convolution_add_fusion.5 = f32[96,1024]{1,0:T(8,128)S(1)} fusion(f32[96,1024]{1,0:T(8,128)S(1)} %fusion.10, bf16[2048,1024]{1,0:T(8,128)(2,1)S(1)} %get-tuple-element.75, bf16[32,1024]{1,0:T(8,128)(2,1)S(1)} %get-tuple-element.183, bf16[32,1024]{1,0:T(8,128)(2,1)S(1)} %get-tuple-element.184, bf16[32,1024]{1,0:T(8,128)(2,1)S(1)} %get-tuple-element.182), kind=kOutput, calls=%fused_computation.5 | convolution fusion | flops 405110784 | bytes 5177344 | tf_op jit(solution)/shard_map/dot_general | solution.py:156
  26.5 1.1 %shard_map.67 = bf16[2048,1024]{1,0:T(8,128)(2,1)S(1)} custom-call(f32[32,1024]{1,0:T(8,128)S(1)} %get-tuple-element.76.rows_ref.part_ref, f32[32,1]{1,0:T(8,128)S(1)} %copy.6.scale_ref, bf16[256,1024]{1,0:T(8,128)(2,1)S(1)} %shard_map.66.right_ref), custom_call_target="tpu_custom_call" | custom-call | flops 872415232 | bytes 4194304 | tf_op jit(solution)/shard_map/pallas_call | solution.py:114
  27.6 1.0 %collective-permute-done.9 = f32[32,1024]{1,0:T(8,128)S(1)} collective-permute-done((f32[32,1024]{1,0:T(8,128)S(1)}, f32[32,1024]{1,0:T(8,128)S(1)}, u32[]{:S(2)}, u32[]{:S(2)}) %collective-permute-start.9) | collective-permute-done | bytes 131104 | tf_op jit(solution)/shard_map/ppermute | solution.py:19
  28.6 0.8 %fusion.25 = f32[96,1024]{1,0:T(8,128)S(1)} fusion(bf16[2048,1024]{1,0:T(8,128)(2,1)S(1)} %get-tuple-element.80, bf16[32,1024]{1,0:T(8,128)(2,1)S(1)} %get-tuple-element.180, bf16[32,1024]{1,0:T(8,128)(2,1)S(1)} %get-tuple-element.181, bf16[32,1024]{1,0:T(8,128)(2,1)S(1)} %get-tuple-element.179), kind=kOutput, calls=%fused_computation.45 | convolution fusion | flops 405012480 | bytes 4784128 | tf_op jit(solution)/shard_map/dot_general | solution.py:156
  30.4 0.8 %convolution_add_fusion.4 = f32[96,1024]{1,0:T(8,128)S(1)} fusion(f32[96,1024]{1,0:T(8,128)S(1)} %fusion.25, bf16[2048,1024]{1,0:T(8,128)(2,1)S(1)} %get-tuple-element.84, bf16[32,1024]{1,0:T(8,128)(2,1)S(1)} %get-tuple-element.176, bf16[32,1024]{1,0:T(8,128)(2,1)S(1)} %get-tuple-element.177, bf16[32,1024]{1,0:T(8,128)(2,1)S(1)} %get-tuple-element.175), kind=kOutput, calls=%fused_computation.4 | convolution fusion | flops 405110784 | bytes 5177344 | tf_op jit(solution)/shard_map/dot_general | solution.py:156
  31.3 1.5 %collective-permute-start.12 = (f32[32,1024]{1,0:T(8,128)S(1)}, f32[32,1024]{1,0:T(8,128)S(1)}, u32[]{:S(2)}, u32[]{:S(2)}) collective-permute-start(f32[32,1024]{1,0:T(8,128)S(1)} %get-tuple-element.85), channel_id=1, source_target_pairs={{0,2},{1,3},{2,0},{3,1},{4,6},{5,7},{6,4},{7,5},{8,10},{9,11},{10,... | collective-permute-start | bytes 393224 | tf_op jit(solution)/shard_map/ppermute | solution.py:19
  33.0 0.8 %fusion.48 = f32[96,1024]{1,0:T(8,128)S(1)} fusion(bf16[2048,1024]{1,0:T(8,128)(2,1)S(1)} %get-tuple-element.74, bf16[96,1024]{1,0:T(8,128)(2,1)S(1)} %pad_maximum_fusion.3), kind=kOutput, calls=%fused_computation.68 | convolution fusion | flops 403439616 | bytes 4784128 | tf_op jit(solution)/shard_map/dot_general | solution.py:156
  34.4 1.0 %convolution_add_fusion.3 = f32[96,1024]{1,0:T(8,128)S(1)} fusion(f32[96,1024]{1,0:T(8,128)S(1)} %fusion.48, bf16[2048,1024]{1,0:T(8,128)(2,1)S(1)} %get-tuple-element.75, bf16[32,1024]{1,0:T(8,128)(2,1)S(1)} %get-tuple-element.171, bf16[32,1024]{1,0:T(8,128)(2,1)S(1)} %get-tuple-element.172, bf16[32,1024]{1,0:T(8,128)(2,1)S(1)} %get-tuple-element.170), kind=kOutput, calls=%fused_computation.3 | convolution fusion | flops 405110784 | bytes 5177344 | tf_op jit(solution)/shard_map/dot_general | solution.py:156
  37.0 0.8 %fusion.63 = f32[96,1024]{1,0:T(8,128)S(1)} fusion(bf16[2048,1024]{1,0:T(8,128)(2,1)S(1)} %get-tuple-element.80, bf16[32,1024]{1,0:T(8,128)(2,1)S(1)} %get-tuple-element.166, bf16[32,1024]{1,0:T(8,128)(2,1)S(1)} %get-tuple-element.167, bf16[32,1024]{1,0:T(8,128)(2,1)S(1)} %get-tuple-element.165), kind=kOutput, calls=%fused_computation.83 | convolution fusion | flops 405012480 | bytes 4784128 | tf_op jit(solution)/shard_map/dot_general | solution.py:156
  38.8 0.8 %convolution_add_fusion.2 = f32[96,1024]{1,0:T(8,128)S(1)} fusion(f32[96,1024]{1,0:T(8,128)S(1)} %fusion.63, bf16[2048,1024]{1,0:T(8,128)(2,1)S(1)} %get-tuple-element.84, bf16[32,1024]{1,0:T(8,128)(2,1)S(1)} %get-tuple-element.162, bf16[32,1024]{1,0:T(8,128)(2,1)S(1)} %get-tuple-element.163, bf16[32,1024]{1,0:T(8,128)(2,1)S(1)} %get-tuple-element.161), kind=kOutput, calls=%fused_computation.2 | convolution fusion | flops 405110784 | bytes 5177344 | tf_op jit(solution)/shard_map/dot_general | solution.py:156
  39.7 1.5 %collective-permute-start.15 = (f32[32,1024]{1,0:T(8,128)S(1)}, f32[32,1024]{1,0:T(8,128)S(1)}, u32[]{:S(2)}, u32[]{:S(2)}) collective-permute-start(f32[32,1024]{1,0:T(8,128)S(1)} %get-tuple-element.95), channel_id=1, source_target_pairs={{0,2},{1,3},{2,0},{3,1},{4,6},{5,7},{6,4},{7,5},{8,10},{9,11},{10,... | collective-permute-start | bytes 393224 | tf_op jit(solution)/shard_map/ppermute | solution.py:19
  41.4 0.8 %fusion.86 = f32[96,1024]{1,0:T(8,128)S(1)} fusion(bf16[2048,1024]{1,0:T(8,128)(2,1)S(1)} %get-tuple-element.74, bf16[96,1024]{1,0:T(8,128)(2,1)S(1)} %pad_maximum_fusion.4), kind=kOutput, calls=%fused_computation.106 | convolution fusion | flops 403439616 | bytes 4784128 | tf_op jit(solution)/shard_map/dot_general | solution.py:156
  42.7 0.8 %convolution_add_fusion.1 = f32[96,1024]{1,0:T(8,128)S(1)} fusion(f32[96,1024]{1,0:T(8,128)S(1)} %fusion.86, bf16[2048,1024]{1,0:T(8,128)(2,1)S(1)} %get-tuple-element.75, bf16[32,1024]{1,0:T(8,128)(2,1)S(1)} %get-tuple-element.157, bf16[32,1024]{1,0:T(8,128)(2,1)S(1)} %get-tuple-element.158, bf16[32,1024]{1,0:T(8,128)(2,1)S(1)} %get-tuple-element.156), kind=kOutput, calls=%fused_computation.1 | convolution fusion | flops 405110784 | bytes 5177344 | tf_op jit(solution)/shard_map/dot_general | solution.py:156
  43.6 1.0 %fusion = f32[192,1024]{1,0:T(8,128)S(1)} fusion(bf16[2048,1024]{1,0:T(8,128)(2,1)S(1)} %shard_map.67, bf16[192,1024]{1,0:T(8,128)(2,1)S(1)} %fusion.180), kind=kOutput, calls=%fused_computation.6 | convolution fusion | flops 806879232 | bytes 5373952 | tf_op jit(solution)/shard_map/dot_general | solution.py:156
  45.4 0.8 %fusion.206 = f32[96,1024]{1,0:T(8,128)S(1)} fusion(bf16[2048,1024]{1,0:T(8,128)(2,1)S(1)} %get-tuple-element.80, bf16[32,1024]{1,0:T(8,128)(2,1)S(1)} %get-tuple-element.154, bf16[32,1024]{1,0:T(8,128)(2,1)S(1)} %get-tuple-element.155, bf16[32,1024]{1,0:T(8,128)(2,1)S(1)} %get-tuple-element.153), kind=kOutput, calls=%fused_computation.338 | convolution fusion | flops 405012480 | bytes 4784128 | tf_op jit(solution)/shard_map/dot_general | solution.py:156
  46.2 0.8 %fusion.207 = f32[96,1024]{1,0:T(8,128)S(1)} fusion(bf16[2048,1024]{1,0:T(8,128)(2,1)S(1)} %shard_map.67, bf16[32,1024]{1,0:T(8,128)(2,1)S(1)} %get-tuple-element.154, bf16[32,1024]{1,0:T(8,128)(2,1)S(1)} %get-tuple-element.155, bf16[32,1024]{1,0:T(8,128)(2,1)S(1)} %get-tuple-element.153), kind=kOutput, calls=%fused_computation.339 | convolution fusion | flops 405012480 | bytes 4784128 | tf_op jit(solution)/shard_map/dot_general | solution.py:156
  48.5 0.8 %convolution_add_fusion = f32[96,1024]{1,0:T(8,128)S(1)} fusion(f32[96,1024]{1,0:T(8,128)S(1)} %fusion.206, bf16[2048,1024]{1,0:T(8,128)(2,1)S(1)} %get-tuple-element.84, bf16[32,1024]{1,0:T(8,128)(2,1)S(1)} %get-tuple-element.150, bf16[32,1024]{1,0:T(8,128)(2,1)S(1)} %get-tuple-element.151, bf16[32,1024]{1,0:T(8,128)(2,1)S(1)} %get-tuple-element.149), kind=kOutput, calls=%fused_computation | convolution fusion | flops 405110784 | bytes 5177344 | tf_op jit(solution)/shard_map/dot_general | solution.py:156
  50.3 0.8 %collective-permute-done.17 = f32[32]{0:T(128)S(1)} collective-permute-done((f32[32]{0:T(128)S(1)}, f32[32]{0:T(128)S(1)}, u32[]{:S(2)}, u32[]{:S(2)}) %collective-permute-start.17) | collective-permute-done | bytes 160 | tf_op jit(solution)/shard_map/ppermute | solution.py:19
  51.1 0.7 %fusion.188 = (f32[32,256]{1,0:T(8,128)}, f32[32,256]{1,0:T(8,128)}) fusion(f32[32,1024]{1,0:T(8,128)S(1)} %get-tuple-element.113, f32[32,4096]{1,0:T(8,128)S(1)} %get-tuple-element.115, f32[32]{0:T(128)S(1)} %add_divide_fusion, f32[32,4096]{1,0:T(8,128)S(1)} %multiply_add_fusion, f32[32,4096]{1,0:T(8,128)S(1)} %multiply_add_fusion.1, ...), kind=kLoop, calls=%fused_computation.304 | loop fusion | flops 73728 | bytes 262656 | tf_op jit(solution)/shard_map/sub | solution.py:329
  (100 shorter events, 12.4 us)
Async XLA Ops:
  1.4 8.1 %collective-permute-start = (f32[72,256]{1,0:T(8,128)S(1)}, f32[72,256]{1,0:T(8,128)S(1)}, u32[]{:S(2)}, u32[]{:S(2)}) collective-permute-start(f32[72,256]{1,0:T(8,128)S(1)} %select_maximum_fusion.part_ref), channel_id=1, source_target_pairs={{0,8},{1,9},{2,10},{3,11},{4,12},{5,13},{6,14},{7,15},{8,0},{9,1},... | collective-permute-start | bytes 221192 | tf_op jit(solution)/shard_map/ppermute | solution.py:19
  6.3 7.7 %collective-permute-start.4 = (f32[65,256]{1,0:T(8,128)S(1)}, f32[65,256]{1,0:T(8,128)S(1)}, u32[]{:S(2)}, u32[]{:S(2)}) collective-permute-start(f32[65,256]{1,0:T(8,128)S(1)} %get-tuple-element.57), channel_id=1, source_target_pairs={{0,2},{1,3},{2,0},{3,1},{4,6},{5,7},{6,4},{7,5},{8,10},{9,11},{10,... | collective-permute-start | bytes 199688 | tf_op jit(solution)/shard_map/ppermute | solution.py:19
  7.9 4.7 %collective-permute-start.1 = (f32[65,256]{1,0:T(8,128)S(1)}, f32[65,256]{1,0:T(8,128)S(1)}, u32[]{:S(2)}, u32[]{:S(2)}) collective-permute-start(f32[65,256]{1,0:T(8,128)S(1)} %get-tuple-element.57), channel_id=1, source_target_pairs={{0,4},{1,5},{2,6},{3,7},{4,0},{5,1},{6,2},{7,3},{8,12},{9,13},{10,... | collective-permute-start | bytes 199688 | tf_op jit(solution)/shard_map/ppermute | solution.py:19
  9.5 4.4 %collective-permute-start.2 = (f32[72,256]{1,0:T(8,128)S(1)}, f32[72,256]{1,0:T(8,128)S(1)}, u32[]{:S(2)}, u32[]{:S(2)}) collective-permute-start(f32[72,256]{1,0:T(8,128)S(1)} %collective-permute-done.part_ref), channel_id=1, source_target_pairs={{0,4},{1,5},{2,6},{3,7},{4,0},{5,1},{6,2},{7,3},{8,12},{9,13},{10,... | collective-permute-start | bytes 221192 | tf_op jit(solution)/shard_map/ppermute | solution.py:19
  10.2 8.6 %collective-permute-start.6 = (f32[65,256]{1,0:T(8,128)S(1)}, f32[65,256]{1,0:T(8,128)S(1)}, u32[]{:S(2)}, u32[]{:S(2)}) collective-permute-start(f32[65,256]{1,0:T(8,128)S(1)} %get-tuple-element.61), channel_id=1, source_target_pairs={{0,2},{1,3},{2,0},{3,1},{4,6},{5,7},{6,4},{7,5},{8,10},{9,11},{10,... | collective-permute-start | bytes 199688 | tf_op jit(solution)/shard_map/ppermute | solution.py:19
  14.0 5.2 %collective-permute-start.5 = (f32[65,512]{1,0:T(8,128)S(1)}, f32[65,512]{1,0:T(8,128)S(1)}, u32[]{:S(2)}, u32[]{:S(2)}) collective-permute-start(f32[65,512]{1,0:T(8,128)S(1)} %get-tuple-element.60), channel_id=1, source_target_pairs={{0,2},{1,3},{2,0},{3,1},{4,6},{5,7},{6,4},{7,5},{8,10},{9,11},{10,... | collective-permute-start | bytes 399368 | tf_op jit(solution)/shard_map/ppermute | solution.py:19
  15.6 1.7 %collective-permute-start.3 = (f32[64,1024]{1,0:T(8,128)S(1)}, f32[64,1024]{1,0:T(8,128)S(1)}, u32[]{:S(2)}, u32[]{:S(2)}) collective-permute-start(f32[64,1024]{1,0:T(8,128)S(1)} %slice.320), channel_id=1, source_target_pairs={{0,1},{1,0},{2,3},{3,2},{4,5},{5,4},{6,7},{7,6},{8,9},{9,8},{10,11... | collective-permute-start | bytes 786440 | tf_op jit(solution)/shard_map/ppermute | solution.py:19
  19.3 1.7 %collective-permute-start.7 = (f32[64,1024]{1,0:T(8,128)S(1)}, f32[64,1024]{1,0:T(8,128)S(1)}, u32[]{:S(2)}, u32[]{:S(2)}) collective-permute-start(f32[64,1024]{1,0:T(8,128)S(1)} %slice.325), channel_id=1, source_target_pairs={{0,1},{1,0},{2,3},{3,2},{4,5},{5,4},{6,7},{7,6},{8,9},{9,8},{10,11... | collective-permute-start | bytes 786440 | tf_op jit(solution)/shard_map/ppermute | solution.py:19
  22.7 5.9 %collective-permute-start.9 = (f32[32,1024]{1,0:T(8,128)S(1)}, f32[32,1024]{1,0:T(8,128)S(1)}, u32[]{:S(2)}, u32[]{:S(2)}) collective-permute-start(f32[32,1024]{1,0:T(8,128)S(1)} %get-tuple-element.72), channel_id=1, source_target_pairs={{0,2},{1,3},{2,0},{3,1},{4,6},{5,7},{6,4},{7,5},{8,10},{9,11},{10,... | collective-permute-start | bytes 393224 | tf_op jit(solution)/shard_map/ppermute | solution.py:19
  24.1 1.4 %collective-permute-start.8 = (f32[32,1024]{1,0:T(8,128)S(1)}, f32[32,1024]{1,0:T(8,128)S(1)}, u32[]{:S(2)}, u32[]{:S(2)}) collective-permute-start(f32[32,1024]{1,0:T(8,128)S(1)} %get-tuple-element.72), channel_id=1, source_target_pairs={{0,1},{1,0},{2,3},{3,2},{4,5},{5,4},{6,7},{7,6},{8,9},{9,8},{10,11... | collective-permute-start | bytes 393224 | tf_op jit(solution)/shard_map/ppermute | solution.py:19
  28.6 1.3 %collective-permute-start.10 = (f32[32,1024]{1,0:T(8,128)S(1)}, f32[32,1024]{1,0:T(8,128)S(1)}, u32[]{:S(2)}, u32[]{:S(2)}) collective-permute-start(f32[32,1024]{1,0:T(8,128)S(1)} %collective-permute-done.9), channel_id=1, source_target_pairs={{0,1},{1,0},{2,3},{3,2},{4,5},{5,4},{6,7},{7,6},{8,9},{9,8},{10,11... | collective-permute-start | bytes 393224 | tf_op jit(solution)/shard_map/ppermute | solution.py:19
  31.3 5.7 %collective-permute-start.12 = (f32[32,1024]{1,0:T(8,128)S(1)}, f32[32,1024]{1,0:T(8,128)S(1)}, u32[]{:S(2)}, u32[]{:S(2)}) collective-permute-start(f32[32,1024]{1,0:T(8,128)S(1)} %get-tuple-element.85), channel_id=1, source_target_pairs={{0,2},{1,3},{2,0},{3,1},{4,6},{5,7},{6,4},{7,5},{8,10},{9,11},{10,... | collective-permute-start | bytes 393224 | tf_op jit(solution)/shard_map/ppermute | solution.py:19
  32.9 1.4 %collective-permute-start.11 = (f32[32,1024]{1,0:T(8,128)S(1)}, f32[32,1024]{1,0:T(8,128)S(1)}, u32[]{:S(2)}, u32[]{:S(2)}) collective-permute-start(f32[32,1024]{1,0:T(8,128)S(1)} %get-tuple-element.85), channel_id=1, source_target_pairs={{0,1},{1,0},{2,3},{3,2},{4,5},{5,4},{6,7},{7,6},{8,9},{9,8},{10,11... | collective-permute-start | bytes 393224 | tf_op jit(solution)/shard_map/ppermute | solution.py:19
  37.0 1.3 %collective-permute-start.13 = (f32[32,1024]{1,0:T(8,128)S(1)}, f32[32,1024]{1,0:T(8,128)S(1)}, u32[]{:S(2)}, u32[]{:S(2)}) collective-permute-start(f32[32,1024]{1,0:T(8,128)S(1)} %collective-permute-done.12), channel_id=1, source_target_pairs={{0,1},{1,0},{2,3},{3,2},{4,5},{5,4},{6,7},{7,6},{8,9},{9,8},{10,11... | collective-permute-start | bytes 393224 | tf_op jit(solution)/shard_map/ppermute | solution.py:19
  39.7 5.6 %collective-permute-start.15 = (f32[32,1024]{1,0:T(8,128)S(1)}, f32[32,1024]{1,0:T(8,128)S(1)}, u32[]{:S(2)}, u32[]{:S(2)}) collective-permute-start(f32[32,1024]{1,0:T(8,128)S(1)} %get-tuple-element.95), channel_id=1, source_target_pairs={{0,2},{1,3},{2,0},{3,1},{4,6},{5,7},{6,4},{7,5},{8,10},{9,11},{10,... | collective-permute-start | bytes 393224 | tf_op jit(solution)/shard_map/ppermute | solution.py:19
  41.2 1.4 %collective-permute-start.14 = (f32[32,1024]{1,0:T(8,128)S(1)}, f32[32,1024]{1,0:T(8,128)S(1)}, u32[]{:S(2)}, u32[]{:S(2)}) collective-permute-start(f32[32,1024]{1,0:T(8,128)S(1)} %get-tuple-element.95), channel_id=1, source_target_pairs={{0,1},{1,0},{2,3},{3,2},{4,5},{5,4},{6,7},{7,6},{8,9},{9,8},{10,11... | collective-permute-start | bytes 393224 | tf_op jit(solution)/shard_map/ppermute | solution.py:19
  45.4 1.9 %collective-permute-start.16 = (f32[32,1024]{1,0:T(8,128)S(1)}, f32[32,1024]{1,0:T(8,128)S(1)}, u32[]{:S(2)}, u32[]{:S(2)}) collective-permute-start(f32[32,1024]{1,0:T(8,128)S(1)} %collective-permute-done.15), channel_id=1, source_target_pairs={{0,1},{1,0},{2,3},{3,2},{4,5},{5,4},{6,7},{7,6},{8,9},{9,8},{10,11... | collective-permute-start | bytes 393224 | tf_op jit(solution)/shard_map/ppermute | solution.py:19
  49.7 1.4 %collective-permute-start.17 = (f32[32]{0:T(128)S(1)}, f32[32]{0:T(128)S(1)}, u32[]{:S(2)}, u32[]{:S(2)}) collective-permute-start(f32[32]{0:T(128)S(1)} %get-tuple-element.112), channel_id=1, source_target_pairs={{0,1},{1,0},{2,3},{3,2},{4,5},{5,4},{6,7},{7,6},{8,9},{9,8},{10,11... | collective-permute-start | bytes 392 | tf_op jit(solution)/shard_map/ppermute | solution.py:19

commit v31 on v27

--- a/solution.py
+++ b/solution.py
@@ -242,6 +242,7 @@
             near = fence(apply_parts(parts, tile[0]))
             near = fence(near + apply_piece(pieces[1], tile[1]))
             far = jnp.zeros_like(near) if len(inner) == 1 else None
+            near = fence(collect(near) + noise * x)
             for k, stride in enumerate(inner[:-1]):
                 arrived = swap(join(*sent), n, stride)
                 if len(far_tile) < len(far_rows):
@@ -265,7 +266,7 @@
             curve = curve + jnp.sum(direction[:, before.shape[1] :] * pieces[-1], axis=1)
             if len(inner) > 1:
                 far = far + apply_piece(pieces[-1], tile[-1])
-            return collect(far), collect(near) + collect(far) + noise * x, join(*pieces), curve
+            return collect(far), near + collect(far), join(*pieces), curve
 
         residual = direction = join(*starts)
         my_solution = jnp.zeros_like(direction[:, :width])

time: 52.2 us -> 52.1 us (level)
  no operation moved by 1% of the time
where the time goes in v31:
time: 52.1 us; the launch traced here: 51.9 us
  starting transfers between devices  16.3 us (31%)
  matrix products  11.5 us (22%)
  Pallas kernels  8.69 us (17%)
  waiting for transfers between devices  8.64 us (17%)
  other arithmetic  5.5 us (11%)
  between operations  1.01 us (2%)
    ppermute x18, starting transfers between devices, swap(): return lax.ppermute(x, 'blk', [(i, i ^ stride) for i in range(n)])  16.3 us
    dot_general x14, matrix products, apply_parts(): jnp.dot(jnp.concatenate([parts, parts], axis=1), piece, preferred_element...  11.5 us
    pallas_call x10, Pallas kernels, call(): pl.pallas_call(kernel, out_shape=outs, in_specs=[whole] * len(args), out_...  8.69 us
    ppermute x18, waiting for transfers between devices, swap(): return lax.ppermute(x, 'blk', [(i, i ^ stride) for i in range(n)])  8.64 us
  transfers between devices with their start and end apart: 18, of which 13 were waited for; matrix products, arithmetic and copies ran while one was open for 18% of the time, Pallas kernels for 14%

profile of v31, /device:TPU:0, one launch (start us, length us, event | category | flops | bytes accessed | tf_op | source)
XLA Modules:
  0.0 51.9 jit_solution(10645150052179319355)
XLA Ops:
  0.6 0.8 %select_maximum_fusion.part_ref = f32[72,256]{1,0:T(8,128)S(1)} fusion(f32[1,256]{1,0:T(1,128)} %bitcast.32, f32[32,256]{1,0:T(8,128)} %param.7, f32[32,256]{1,0:T(8,128)} %param.4), kind=kLoop, calls=%fused_computation.285 | loop fusion | flops 73728 | bytes 140288 | tf_op jit(solution)/shard_map/concatenate | solution.py:187
  1.4 4.0 %collective-permute-start = (f32[72,256]{1,0:T(8,128)S(1)}, f32[72,256]{1,0:T(8,128)S(1)}, u32[]{:S(2)}, u32[]{:S(2)}) collective-permute-start(f32[72,256]{1,0:T(8,128)S(1)} %select_maximum_fusion.part_ref), channel_id=1, source_target_pairs={{0,8},{1,9},{2,10},{3,11},{4,12},{5,13},{6,14},{7,15},{8,0},{9,1},... | collective-permute-start | bytes 221192 | tf_op jit(solution)/shard_map/ppermute | solution.py:19
  6.3 1.6 %collective-permute-start.4 = (f32[65,256]{1,0:T(8,128)S(1)}, f32[65,256]{1,0:T(8,128)S(1)}, u32[]{:S(2)}, u32[]{:S(2)}) collective-permute-start(f32[65,256]{1,0:T(8,128)S(1)} %get-tuple-element.49), channel_id=1, source_target_pairs={{0,2},{1,3},{2,0},{3,1},{4,6},{5,7},{6,4},{7,5},{8,10},{9,11},{10,... | collective-permute-start | bytes 199688 | tf_op jit(solution)/shard_map/ppermute | solution.py:19
  7.9 1.6 %collective-permute-start.1 = (f32[65,256]{1,0:T(8,128)S(1)}, f32[65,256]{1,0:T(8,128)S(1)}, u32[]{:S(2)}, u32[]{:S(2)}) collective-permute-start(f32[65,256]{1,0:T(8,128)S(1)} %get-tuple-element.49), channel_id=1, source_target_pairs={{0,4},{1,5},{2,6},{3,7},{4,0},{5,1},{6,2},{7,3},{8,12},{9,13},{10,... | collective-permute-start | bytes 199688 | tf_op jit(solution)/shard_map/ppermute | solution.py:19
  10.2 1.9 %collective-permute-start.6 = (f32[65,256]{1,0:T(8,128)S(1)}, f32[65,256]{1,0:T(8,128)S(1)}, u32[]{:S(2)}, u32[]{:S(2)}) collective-permute-start(f32[65,256]{1,0:T(8,128)S(1)} %get-tuple-element.53), channel_id=1, source_target_pairs={{0,2},{1,3},{2,0},{3,1},{4,6},{5,7},{6,4},{7,5},{8,10},{9,11},{10,... | collective-permute-start | bytes 199688 | tf_op jit(solution)/shard_map/ppermute | solution.py:19
  12.6 1.2 %collective-permute-done.2 = f32[72,256]{1,0:T(8,128)S(1)} collective-permute-done((f32[72,256]{1,0:T(8,128)S(1)}, f32[72,256]{1,0:T(8,128)S(1)}, u32[]{:S(2)}, u32[]{:S(2)}) %collective-permute-start.2) | collective-permute-done | bytes 73760 | tf_op jit(solution)/shard_map/ppermute | solution.py:19
  14.0 1.5 %collective-permute-start.5 = (f32[65,512]{1,0:T(8,128)S(1)}, f32[65,512]{1,0:T(8,128)S(1)}, u32[]{:S(2)}, u32[]{:S(2)}) collective-permute-start(f32[65,512]{1,0:T(8,128)S(1)} %get-tuple-element.52), channel_id=1, source_target_pairs={{0,2},{1,3},{2,0},{3,1},{4,6},{5,7},{6,4},{7,5},{8,10},{9,11},{10,... | collective-permute-start | bytes 399368 | tf_op jit(solution)/shard_map/ppermute | solution.py:19
  15.7 1.5 %shard_map.62 = (bf16[2048,1024]{1,0:T(8,128)(2,1)S(1)}, f32[32,1024]{1,0:T(8,128)S(1)}) custom-call(f32[32,1024]{1,0:T(8,128)S(1)} %get-tuple-element.121.rows_ref, f32[32,1]{1,0:T(8,128)S(1)} %copy.6.scale_ref, bf16[256,1024]{1,0:T(8,128)(2,1)S(1)} %constant_dynamic-update-slice_fusion.right_ref, f32[32,1024]{1,0:T(8,128)S(1)} %get-tuple-element.122.refs_0_, ...), custom_call_target="tpu_custom_call" | custom-call | flops 872415232 | bytes 4194304 | tf_op jit(solution)/shard_map/pallas_call | solution.py:114
  17.3 1.5 %shard_map.63 = (bf16[2048,1024]{1,0:T(8,128)(2,1)S(1)}, f32[32,1024]{1,0:T(8,128)S(1)}) custom-call(f32[32,1024]{1,0:T(8,128)S(1)} %get-tuple-element.126.rows_ref, f32[32,1]{1,0:T(8,128)S(1)} %copy.6.scale_ref, bf16[256,1024]{1,0:T(8,128)(2,1)S(1)} %constant_dynamic-update-slice_fusion.right_ref, f32[32,1024]{1,0:T(8,128)S(1)} %get-tuple-element.125.refs_0_, ...), custom_call_target="tpu_custom_call" | custom-call | flops 872415232 | bytes 4194304 | tf_op jit(solution)/shard_map/pallas_call | solution.py:114
  19.5 1.5 %shard_map.64 = (bf16[2048,1024]{1,0:T(8,128)(2,1)S(1)}, f32[32,1024]{1,0:T(8,128)S(1)}) custom-call(f32[32,1024]{1,0:T(8,128)S(1)} %get-tuple-element.69.rows_ref.part_ref, f32[32,1]{1,0:T(8,128)S(1)} %copy.6.scale_ref, bf16[256,1024]{1,0:T(8,128)(2,1)S(1)} %constant_dynamic-update-slice_fusion.right_ref, f32[32,1024]{1,0:T(8,128)S(1)} %get-tuple-element.118.refs_0_, ...), custom_call_target="tpu_custom_call" | custom-call | flops 872415232 | bytes 4194304 | tf_op jit(solution)/shard_map/pallas_call | solution.py:114
  21.1 1.5 %shard_map.65 = (bf16[2048,1024]{1,0:T(8,128)(2,1)S(1)}, f32[32,1024]{1,0:T(8,128)S(1)}) custom-call(f32[32,1024]{1,0:T(8,128)S(1)} %get-tuple-element.80.rows_ref, f32[32,1]{1,0:T(8,128)S(1)} %copy.6.scale_ref, bf16[256,1024]{1,0:T(8,128)(2,1)S(1)} %constant_dynamic-update-slice_fusion.right_ref, f32[32,1024]{1,0:T(8,128)S(1)} %get-tuple-element.123.refs_0_, ...), custom_call_target="tpu_custom_call" | custom-call | flops 872415232 | bytes 4194304 | tf_op jit(solution)/shard_map/pallas_call | solution.py:114
  22.7 1.4 %collective-permute-start.9 = (f32[32,1024]{1,0:T(8,128)S(1)}, f32[32,1024]{1,0:T(8,128)S(1)}, u32[]{:S(2)}, u32[]{:S(2)}) collective-permute-start(f32[32,1024]{1,0:T(8,128)S(1)} %get-tuple-element.64), channel_id=1, source_target_pairs={{0,2},{1,3},{2,0},{3,1},{4,6},{5,7},{6,4},{7,5},{8,10},{9,11},{10,... | collective-permute-start | bytes 393224 | tf_op jit(solution)/shard_map/ppermute | solution.py:19
  25.5 0.8 %convolution_add_fusion.6 = f32[96,1024]{1,0:T(8,128)S(1)} fusion(f32[96,1024]{1,0:T(8,128)S(1)} %fusion.6, bf16[2048,1024]{1,0:T(8,128)(2,1)S(1)} %get-tuple-element.67, bf16[32,1024]{1,0:T(8,128)(2,1)S(1)} %get-tuple-element.159, bf16[32,1024]{1,0:T(8,128)(2,1)S(1)} %get-tuple-element.160, bf16[32,1024]{1,0:T(8,128)(2,1)S(1)} %get-tuple-element.158), kind=kOutput, calls=%fused_computation.6 | convolution fusion | flops 405110784 | bytes 5177344 | tf_op jit(solution)/shard_map/dot_general | solution.py:152
  26.5 1.1 %shard_map.67 = bf16[2048,1024]{1,0:T(8,128)(2,1)S(1)} custom-call(f32[32,1024]{1,0:T(8,128)S(1)} %get-tuple-element.69.rows_ref.part_ref, f32[32,1]{1,0:T(8,128)S(1)} %copy.6.scale_ref, bf16[256,1024]{1,0:T(8,128)(2,1)S(1)} %shard_map.66.right_ref), custom_call_target="tpu_custom_call" | custom-call | flops 872415232 | bytes 4194304 | tf_op jit(solution)/shard_map/pallas_call | solution.py:114
  27.6 1.0 %collective-permute-done.9 = f32[32,1024]{1,0:T(8,128)S(1)} collective-permute-done((f32[32,1024]{1,0:T(8,128)S(1)}, f32[32,1024]{1,0:T(8,128)S(1)}, u32[]{:S(2)}, u32[]{:S(2)}) %collective-permute-start.9) | collective-permute-done | bytes 131104 | tf_op jit(solution)/shard_map/ppermute | solution.py:19
  28.6 0.8 %fusion.21 = f32[96,1024]{1,0:T(8,128)S(1)} fusion(bf16[2048,1024]{1,0:T(8,128)(2,1)S(1)} %get-tuple-element.73, bf16[32,1024]{1,0:T(8,128)(2,1)S(1)} %get-tuple-element.156, bf16[32,1024]{1,0:T(8,128)(2,1)S(1)} %get-tuple-element.157, bf16[32,1024]{1,0:T(8,128)(2,1)S(1)} %get-tuple-element.155), kind=kOutput, calls=%fused_computation.42 | convolution fusion | flops 405012480 | bytes 4784128 | tf_op jit(solution)/shard_map/dot_general | solution.py:152
  30.4 0.8 %convolution_add_fusion.5 = f32[96,1024]{1,0:T(8,128)S(1)} fusion(f32[96,1024]{1,0:T(8,128)S(1)} %fusion.21, bf16[2048,1024]{1,0:T(8,128)(2,1)S(1)} %get-tuple-element.77, bf16[32,1024]{1,0:T(8,128)(2,1)S(1)} %get-tuple-element.152, bf16[32,1024]{1,0:T(8,128)(2,1)S(1)} %get-tuple-element.153, bf16[32,1024]{1,0:T(8,128)(2,1)S(1)} %get-tuple-element.151), kind=kOutput, calls=%fused_computation.5 | convolution fusion | flops 405110784 | bytes 5177344 | tf_op jit(solution)/shard_map/dot_general | solution.py:152
  31.3 1.5 %collective-permute-start.12 = (f32[32,1024]{1,0:T(8,128)S(1)}, f32[32,1024]{1,0:T(8,128)S(1)}, u32[]{:S(2)}, u32[]{:S(2)}) collective-permute-start(f32[32,1024]{1,0:T(8,128)S(1)} %get-tuple-element.78), channel_id=1, source_target_pairs={{0,2},{1,3},{2,0},{3,1},{4,6},{5,7},{6,4},{7,5},{8,10},{9,11},{10,... | collective-permute-start | bytes 393224 | tf_op jit(solution)/shard_map/ppermute | solution.py:19
  33.0 0.8 %fusion.44 = f32[96,1024]{1,0:T(8,128)S(1)} fusion(bf16[2048,1024]{1,0:T(8,128)(2,1)S(1)} %get-tuple-element.66, bf16[96,1024]{1,0:T(8,128)(2,1)S(1)} %pad_maximum_fusion.3), kind=kOutput, calls=%fused_computation.65 | convolution fusion | flops 403439616 | bytes 4784128 | tf_op jit(solution)/shard_map/dot_general | solution.py:152
  34.4 1.0 %convolution_add_fusion.4 = f32[96,1024]{1,0:T(8,128)S(1)} fusion(f32[96,1024]{1,0:T(8,128)S(1)} %fusion.44, bf16[2048,1024]{1,0:T(8,128)(2,1)S(1)} %get-tuple-element.67, bf16[32,1024]{1,0:T(8,128)(2,1)S(1)} %get-tuple-element.147, bf16[32,1024]{1,0:T(8,128)(2,1)S(1)} %get-tuple-element.148, bf16[32,1024]{1,0:T(8,128)(2,1)S(1)} %get-tuple-element.146), kind=kOutput, calls=%fused_computation.4 | convolution fusion | flops 405110784 | bytes 5177344 | tf_op jit(solution)/shard_map/dot_general | solution.py:152
  35.4 1.1 %shard_map.68 = bf16[2048,1024]{1,0:T(8,128)(2,1)S(1)} custom-call(f32[32,1024]{1,0:T(8,128)S(1)} %get-tuple-element.80.rows_ref, f32[32,1]{1,0:T(8,128)S(1)} %copy.6.scale_ref, bf16[256,1024]{1,0:T(8,128)(2,1)S(1)} %shard_map.66.right_ref), custom_call_target="tpu_custom_call" | custom-call | flops 872415232 | bytes 4194304 | tf_op jit(solution)/shard_map/pallas_call | solution.py:114
  37.0 0.8 %fusion.59 = f32[96,1024]{1,0:T(8,128)S(1)} fusion(bf16[2048,1024]{1,0:T(8,128)(2,1)S(1)} %get-tuple-element.73, bf16[32,1024]{1,0:T(8,128)(2,1)S(1)} %get-tuple-element.144, bf16[32,1024]{1,0:T(8,128)(2,1)S(1)} %get-tuple-element.145, bf16[32,1024]{1,0:T(8,128)(2,1)S(1)} %get-tuple-element.143), kind=kOutput, calls=%fused_computation.80 | convolution fusion | flops 405012480 | bytes 4784128 | tf_op jit(solution)/shard_map/dot_general | solution.py:152
  38.7 0.8 %convolution_add_fusion.3 = f32[96,1024]{1,0:T(8,128)S(1)} fusion(f32[96,1024]{1,0:T(8,128)S(1)} %fusion.59, bf16[2048,1024]{1,0:T(8,128)(2,1)S(1)} %get-tuple-element.77, bf16[32,1024]{1,0:T(8,128)(2,1)S(1)} %get-tuple-element.140, bf16[32,1024]{1,0:T(8,128)(2,1)S(1)} %get-tuple-element.141, bf16[32,1024]{1,0:T(8,128)(2,1)S(1)} %get-tuple-element.139), kind=kOutput, calls=%fused_computation.3 | convolution fusion | flops 405110784 | bytes 5177344 | tf_op jit(solution)/shard_map/dot_general | solution.py:152
  39.7 1.5 %collective-permute-start.15 = (f32[32,1024]{1,0:T(8,128)S(1)}, f32[32,1024]{1,0:T(8,128)S(1)}, u32[]{:S(2)}, u32[]{:S(2)}) collective-permute-start(f32[32,1024]{1,0:T(8,128)S(1)} %get-tuple-element.88), channel_id=1, source_target_pairs={{0,2},{1,3},{2,0},{3,1},{4,6},{5,7},{6,4},{7,5},{8,10},{9,11},{10,... | collective-permute-start | bytes 393224 | tf_op jit(solution)/shard_map/ppermute | solution.py:19
  41.4 0.8 %fusion.82 = f32[96,1024]{1,0:T(8,128)S(1)} fusion(bf16[2048,1024]{1,0:T(8,128)(2,1)S(1)} %get-tuple-element.66, bf16[96,1024]{1,0:T(8,128)(2,1)S(1)} %pad_maximum_fusion.4), kind=kOutput, calls=%fused_computation.103 | convolution fusion | flops 403439616 | bytes 4784128 | tf_op jit(solution)/shard_map/dot_general | solution.py:152
  42.6 0.8 %convolution_add_fusion.2 = f32[96,1024]{1,0:T(8,128)S(1)} fusion(f32[96,1024]{1,0:T(8,128)S(1)} %fusion.82, bf16[2048,1024]{1,0:T(8,128)(2,1)S(1)} %get-tuple-element.67, bf16[32,1024]{1,0:T(8,128)(2,1)S(1)} %get-tuple-element.135, bf16[32,1024]{1,0:T(8,128)(2,1)S(1)} %get-tuple-element.136, bf16[32,1024]{1,0:T(8,128)(2,1)S(1)} %get-tuple-element.134), kind=kOutput, calls=%fused_computation.2 | convolution fusion | flops 405110784 | bytes 5177344 | tf_op jit(solution)/shard_map/dot_general | solution.py:152
  43.5 1.9 %collective-permute-done.15 = f32[32,1024]{1,0:T(8,128)S(1)} collective-permute-done((f32[32,1024]{1,0:T(8,128)S(1)}, f32[32,1024]{1,0:T(8,128)S(1)}, u32[]{:S(2)}, u32[]{:S(2)}) %collective-permute-start.15) | collective-permute-done | bytes 131104 | tf_op jit(solution)/shard_map/ppermute | solution.py:19
  45.4 0.8 %fusion.97 = f32[96,1024]{1,0:T(8,128)S(1)} fusion(bf16[2048,1024]{1,0:T(8,128)(2,1)S(1)} %get-tuple-element.73, bf16[32,1024]{1,0:T(8,128)(2,1)S(1)} %get-tuple-element.132, bf16[32,1024]{1,0:T(8,128)(2,1)S(1)} %get-tuple-element.133, bf16[32,1024]{1,0:T(8,128)(2,1)S(1)} %get-tuple-element.131), kind=kOutput, calls=%fused_computation.118 | convolution fusion | flops 405012480 | bytes 4784128 | tf_op jit(solution)/shard_map/dot_general | solution.py:152
  47.3 0.8 %convolution_add_fusion.1 = f32[96,1024]{1,0:T(8,128)S(1)} fusion(f32[96,1024]{1,0:T(8,128)S(1)} %fusion.97, bf16[2048,1024]{1,0:T(8,128)(2,1)S(1)} %get-tuple-element.77, bf16[32,1024]{1,0:T(8,128)(2,1)S(1)} %get-tuple-element.128, bf16[32,1024]{1,0:T(8,128)(2,1)S(1)} %get-tuple-element.129, bf16[32,1024]{1,0:T(8,128)(2,1)S(1)} %get-tuple-element.127), kind=kOutput, calls=%fused_computation.1 | convolution fusion | flops 405110784 | bytes 5177344 | tf_op jit(solution)/shard_map/dot_general | solution.py:152
  48.1 0.8 %fusion.120 = f32[96,1024]{1,0:T(8,128)S(1)} fusion(bf16[2048,1024]{1,0:T(8,128)(2,1)S(1)} %shard_map.67, bf16[32,1024]{1,0:T(8,128)(2,1)S(1)} %get-tuple-element.114, bf16[32,1024]{1,0:T(8,128)(2,1)S(1)} %get-tuple-element.113, bf16[32,1024]{1,0:T(8,128)(2,1)S(1)} %get-tuple-element.117), kind=kOutput, calls=%fused_computation.141 | convolution fusion | flops 405012480 | bytes 4784128 | tf_op jit(solution)/shard_map/dot_general | solution.py:152
  48.9 0.8 %convolution_add_fusion = f32[96,1024]{1,0:T(8,128)S(1)} fusion(f32[96,1024]{1,0:T(8,128)S(1)} %fusion.120, bf16[2048,1024]{1,0:T(8,128)(2,1)S(1)} %shard_map.68, bf16[32,1024]{1,0:T(8,128)(2,1)S(1)} %get-tuple-element.115, bf16[32,1024]{1,0:T(8,128)(2,1)S(1)} %get-tuple-element.116, bf16[32,1024]{1,0:T(8,128)(2,1)S(1)} %get-tuple-element.112), kind=kOutput, calls=%fused_computation | convolution fusion | flops 405110784 | bytes 5177344 | tf_op jit(solution)/shard_map/dot_general | solution.py:152
  50.3 1.0 %collective-permute-done.17 = f32[32]{0:T(128)S(1)} collective-permute-done((f32[32]{0:T(128)S(1)}, f32[32]{0:T(128)S(1)}, u32[]{:S(2)}, u32[]{:S(2)}) %collective-permute-start.17) | collective-permute-done | bytes 160 | tf_op jit(solution)/shard_map/ppermute | solution.py:19
  (89 shorter events, 11.4 us)
Async XLA Ops:
  1.4 8.1 %collective-permute-start = (f32[72,256]{1,0:T(8,128)S(1)}, f32[72,256]{1,0:T(8,128)S(1)}, u32[]{:S(2)}, u32[]{:S(2)}) collective-permute-start(f32[72,256]{1,0:T(8,128)S(1)} %select_maximum_fusion.part_ref), channel_id=1, source_target_pairs={{0,8},{1,9},{2,10},{3,11},{4,12},{5,13},{6,14},{7,15},{8,0},{9,1},... | collective-permute-start | bytes 221192 | tf_op jit(solution)/shard_map/ppermute | solution.py:19
  6.3 7.7 %collective-permute-start.4 = (f32[65,256]{1,0:T(8,128)S(1)}, f32[65,256]{1,0:T(8,128)S(1)}, u32[]{:S(2)}, u32[]{:S(2)}) collective-permute-start(f32[65,256]{1,0:T(8,128)S(1)} %get-tuple-element.49), channel_id=1, source_target_pairs={{0,2},{1,3},{2,0},{3,1},{4,6},{5,7},{6,4},{7,5},{8,10},{9,11},{10,... | collective-permute-start | bytes 199688 | tf_op jit(solution)/shard_map/ppermute | solution.py:19
  7.9 4.7 %collective-permute-start.1 = (f32[65,256]{1,0:T(8,128)S(1)}, f32[65,256]{1,0:T(8,128)S(1)}, u32[]{:S(2)}, u32[]{:S(2)}) collective-permute-start(f32[65,256]{1,0:T(8,128)S(1)} %get-tuple-element.49), channel_id=1, source_target_pairs={{0,4},{1,5},{2,6},{3,7},{4,0},{5,1},{6,2},{7,3},{8,12},{9,13},{10,... | collective-permute-start | bytes 199688 | tf_op jit(solution)/shard_map/ppermute | solution.py:19
  9.5 4.4 %collective-permute-start.2 = (f32[72,256]{1,0:T(8,128)S(1)}, f32[72,256]{1,0:T(8,128)S(1)}, u32[]{:S(2)}, u32[]{:S(2)}) collective-permute-start(f32[72,256]{1,0:T(8,128)S(1)} %collective-permute-done.part_ref), channel_id=1, source_target_pairs={{0,4},{1,5},{2,6},{3,7},{4,0},{5,1},{6,2},{7,3},{8,12},{9,13},{10,... | collective-permute-start | bytes 221192 | tf_op jit(solution)/shard_map/ppermute | solution.py:19
  10.2 8.6 %collective-permute-start.6 = (f32[65,256]{1,0:T(8,128)S(1)}, f32[65,256]{1,0:T(8,128)S(1)}, u32[]{:S(2)}, u32[]{:S(2)}) collective-permute-start(f32[65,256]{1,0:T(8,128)S(1)} %get-tuple-element.53), channel_id=1, source_target_pairs={{0,2},{1,3},{2,0},{3,1},{4,6},{5,7},{6,4},{7,5},{8,10},{9,11},{10,... | collective-permute-start | bytes 199688 | tf_op jit(solution)/shard_map/ppermute | solution.py:19
  14.0 5.2 %collective-permute-start.5 = (f32[65,512]{1,0:T(8,128)S(1)}, f32[65,512]{1,0:T(8,128)S(1)}, u32[]{:S(2)}, u32[]{:S(2)}) collective-permute-start(f32[65,512]{1,0:T(8,128)S(1)} %get-tuple-element.52), channel_id=1, source_target_pairs={{0,2},{1,3},{2,0},{3,1},{4,6},{5,7},{6,4},{7,5},{8,10},{9,11},{10,... | collective-permute-start | bytes 399368 | tf_op jit(solution)/shard_map/ppermute | solution.py:19
  15.6 1.7 %collective-permute-start.3 = (f32[64,1024]{1,0:T(8,128)S(1)}, f32[64,1024]{1,0:T(8,128)S(1)}, u32[]{:S(2)}, u32[]{:S(2)}) collective-permute-start(f32[64,1024]{1,0:T(8,128)S(1)} %slice.225), channel_id=1, source_target_pairs={{0,1},{1,0},{2,3},{3,2},{4,5},{5,4},{6,7},{7,6},{8,9},{9,8},{10,11... | collective-permute-start | bytes 786440 | tf_op jit(solution)/shard_map/ppermute | solution.py:19
  19.3 1.7 %collective-permute-start.7 = (f32[64,1024]{1,0:T(8,128)S(1)}, f32[64,1024]{1,0:T(8,128)S(1)}, u32[]{:S(2)}, u32[]{:S(2)}) collective-permute-start(f32[64,1024]{1,0:T(8,128)S(1)} %slice.230), channel_id=1, source_target_pairs={{0,1},{1,0},{2,3},{3,2},{4,5},{5,4},{6,7},{7,6},{8,9},{9,8},{10,11... | collective-permute-start | bytes 786440 | tf_op jit(solution)/shard_map/ppermute | solution.py:19
  22.7 5.9 %collective-permute-start.9 = (f32[32,1024]{1,0:T(8,128)S(1)}, f32[32,1024]{1,0:T(8,128)S(1)}, u32[]{:S(2)}, u32[]{:S(2)}) collective-permute-start(f32[32,1024]{1,0:T(8,128)S(1)} %get-tuple-element.64), channel_id=1, source_target_pairs={{0,2},{1,3},{2,0},{3,1},{4,6},{5,7},{6,4},{7,5},{8,10},{9,11},{10,... | collective-permute-start | bytes 393224 | tf_op jit(solution)/shard_map/ppermute | solution.py:19
  24.1 1.4 %collective-permute-start.8 = (f32[32,1024]{1,0:T(8,128)S(1)}, f32[32,1024]{1,0:T(8,128)S(1)}, u32[]{:S(2)}, u32[]{:S(2)}) collective-permute-start(f32[32,1024]{1,0:T(8,128)S(1)} %get-tuple-element.64), channel_id=1, source_target_pairs={{0,1},{1,0},{2,3},{3,2},{4,5},{5,4},{6,7},{7,6},{8,9},{9,8},{10,11... | collective-permute-start | bytes 393224 | tf_op jit(solution)/shard_map/ppermute | solution.py:19
  28.6 1.3 %collective-permute-start.10 = (f32[32,1024]{1,0:T(8,128)S(1)}, f32[32,1024]{1,0:T(8,128)S(1)}, u32[]{:S(2)}, u32[]{:S(2)}) collective-permute-start(f32[32,1024]{1,0:T(8,128)S(1)} %collective-permute-done.9), channel_id=1, source_target_pairs={{0,1},{1,0},{2,3},{3,2},{4,5},{5,4},{6,7},{7,6},{8,9},{9,8},{10,11... | collective-permute-start | bytes 393224 | tf_op jit(solution)/shard_map/ppermute | solution.py:19
  31.3 5.6 %collective-permute-start.12 = (f32[32,1024]{1,0:T(8,128)S(1)}, f32[32,1024]{1,0:T(8,128)S(1)}, u32[]{:S(2)}, u32[]{:S(2)}) collective-permute-start(f32[32,1024]{1,0:T(8,128)S(1)} %get-tuple-element.78), channel_id=1, source_target_pairs={{0,2},{1,3},{2,0},{3,1},{4,6},{5,7},{6,4},{7,5},{8,10},{9,11},{10,... | collective-permute-start | bytes 393224 | tf_op jit(solution)/shard_map/ppermute | solution.py:19
  32.9 1.4 %collective-permute-start.11 = (f32[32,1024]{1,0:T(8,128)S(1)}, f32[32,1024]{1,0:T(8,128)S(1)}, u32[]{:S(2)}, u32[]{:S(2)}) collective-permute-start(f32[32,1024]{1,0:T(8,128)S(1)} %get-tuple-element.78), channel_id=1, source_target_pairs={{0,1},{1,0},{2,3},{3,2},{4,5},{5,4},{6,7},{7,6},{8,9},{9,8},{10,11... | collective-permute-start | bytes 393224 | tf_op jit(solution)/shard_map/ppermute | solution.py:19
  37.0 1.3 %collective-permute-start.13 = (f32[32,1024]{1,0:T(8,128)S(1)}, f32[32,1024]{1,0:T(8,128)S(1)}, u32[]{:S(2)}, u32[]{:S(2)}) collective-permute-start(f32[32,1024]{1,0:T(8,128)S(1)} %collective-permute-done.12), channel_id=1, source_target_pairs={{0,1},{1,0},{2,3},{3,2},{4,5},{5,4},{6,7},{7,6},{8,9},{9,8},{10,11... | collective-permute-start | bytes 393224 | tf_op jit(solution)/shard_map/ppermute | solution.py:19
  39.7 5.6 %collective-permute-start.15 = (f32[32,1024]{1,0:T(8,128)S(1)}, f32[32,1024]{1,0:T(8,128)S(1)}, u32[]{:S(2)}, u32[]{:S(2)}) collective-permute-start(f32[32,1024]{1,0:T(8,128)S(1)} %get-tuple-element.88), channel_id=1, source_target_pairs={{0,2},{1,3},{2,0},{3,1},{4,6},{5,7},{6,4},{7,5},{8,10},{9,11},{10,... | collective-permute-start | bytes 393224 | tf_op jit(solution)/shard_map/ppermute | solution.py:19
  41.2 1.4 %collective-permute-start.14 = (f32[32,1024]{1,0:T(8,128)S(1)}, f32[32,1024]{1,0:T(8,128)S(1)}, u32[]{:S(2)}, u32[]{:S(2)}) collective-permute-start(f32[32,1024]{1,0:T(8,128)S(1)} %get-tuple-element.88), channel_id=1, source_target_pairs={{0,1},{1,0},{2,3},{3,2},{4,5},{5,4},{6,7},{7,6},{8,9},{9,8},{10,11... | collective-permute-start | bytes 393224 | tf_op jit(solution)/shard_map/ppermute | solution.py:19
  45.3 1.3 %collective-permute-start.16 = (f32[32,1024]{1,0:T(8,128)S(1)}, f32[32,1024]{1,0:T(8,128)S(1)}, u32[]{:S(2)}, u32[]{:S(2)}) collective-permute-start(f32[32,1024]{1,0:T(8,128)S(1)} %collective-permute-done.15), channel_id=1, source_target_pairs={{0,1},{1,0},{2,3},{3,2},{4,5},{5,4},{6,7},{7,6},{8,9},{9,8},{10,11... | collective-permute-start | bytes 393224 | tf_op jit(solution)/shard_map/ppermute | solution.py:19
  50.0 1.2 %collective-permute-start.17 = (f32[32]{0:T(128)S(1)}, f32[32]{0:T(128)S(1)}, u32[]{:S(2)}, u32[]{:S(2)}) collective-permute-start(f32[32]{0:T(128)S(1)} %get-tuple-element.96), channel_id=1, source_target_pairs={{0,1},{1,0},{2,3},{3,2},{4,5},{5,4},{6,7},{7,6},{8,9},{9,8},{10,11... | collective-permute-start | bytes 392 | tf_op jit(solution)/shard_map/ppermute | solution.py:19

commit v32 on v27

--- a/solution.py
+++ b/solution.py
@@ -68,7 +68,7 @@
     applies = len(refs) > 1
     vectors_ref, sum_ref, tile_ref, out_ref = refs if applies else (None, None, *refs, None)
     total, cols = rows_ref.shape[1], right_ref.shape[1]
-    block, step = min(total, BUILD_ROWS), min(cols, 256)
+    block, step = min(total, BUILD_ROWS), min(cols, 512)
     if applies:
         probes = vectors_ref.shape[0]
         high, rest = halve(vectors_ref[...])

time: 52.2 us -> 52.8 us (1.011)
  Pallas kernels: 8.69 us -> 9.64 us
    pallas_call x10, Pallas kernels: 8.69 us -> 9.64 us  [call(): pl.pallas_call(kernel, out_shape=outs, in_specs=[whole] * len(args), out_...]
  transfers between devices with their start and end apart: 18 -> 18, of which waited for: 13 -> 12; matrix products, arithmetic and copies ran while one was open for 18% -> 18% of each run, Pallas kernels for 14% -> 15%
where the time goes in v32:
time: 52.8 us; the launch traced here: 52.6 us
  starting transfers between devices  16.1 us (30%)
  matrix products  11.5 us (22%)
  Pallas kernels  9.64 us (18%)
  waiting for transfers between devices  8.58 us (16%)
  other arithmetic  5.42 us (10%)
  between operations  0.99 us (2%)
    ppermute x18, starting transfers between devices, swap(): return lax.ppermute(x, 'blk', [(i, i ^ stride) for i in range(n)])  16.1 us
    dot_general x14, matrix products, apply_parts(): jnp.dot(jnp.concatenate([parts, parts], axis=1), piece, preferred_element...  11.5 us
    pallas_call x10, Pallas kernels, call(): pl.pallas_call(kernel, out_shape=outs, in_specs=[whole] * len(args), out_...  9.64 us
    ppermute x18, waiting for transfers between devices, swap(): return lax.ppermute(x, 'blk', [(i, i ^ stride) for i in range(n)])  8.58 us
  transfers between devices with their start and end apart: 18, of which 12 were waited for; matrix products, arithmetic and copies ran while one was open for 18% of the time, Pallas kernels for 15%

profile of v32, /device:TPU:0, one launch (start us, length us, event | category | flops | bytes accessed | tf_op | source)
XLA Modules:
  0.0 52.6 jit_solution(14651657392683199074)
XLA Ops:
  0.6 0.8 %select_maximum_fusion.part_ref = f32[72,256]{1,0:T(8,128)S(1)} fusion(f32[1,256]{1,0:T(1,128)} %bitcast.32, f32[32,256]{1,0:T(8,128)} %param.7, f32[32,256]{1,0:T(8,128)} %param.4), kind=kLoop, calls=%fused_computation.276 | loop fusion | flops 73728 | bytes 140288 | tf_op jit(solution)/shard_map/concatenate | solution.py:187
  1.4 4.0 %collective-permute-start = (f32[72,256]{1,0:T(8,128)S(1)}, f32[72,256]{1,0:T(8,128)S(1)}, u32[]{:S(2)}, u32[]{:S(2)}) collective-permute-start(f32[72,256]{1,0:T(8,128)S(1)} %select_maximum_fusion.part_ref), channel_id=1, source_target_pairs={{0,8},{1,9},{2,10},{3,11},{4,12},{5,13},{6,14},{7,15},{8,0},{9,1},... | collective-permute-start | bytes 221192 | tf_op jit(solution)/shard_map/ppermute | solution.py:19
  6.3 1.6 %collective-permute-start.4 = (f32[65,256]{1,0:T(8,128)S(1)}, f32[65,256]{1,0:T(8,128)S(1)}, u32[]{:S(2)}, u32[]{:S(2)}) collective-permute-start(f32[65,256]{1,0:T(8,128)S(1)} %get-tuple-element.49), channel_id=1, source_target_pairs={{0,2},{1,3},{2,0},{3,1},{4,6},{5,7},{6,4},{7,5},{8,10},{9,11},{10,... | collective-permute-start | bytes 199688 | tf_op jit(solution)/shard_map/ppermute | solution.py:19
  7.9 1.6 %collective-permute-start.1 = (f32[65,256]{1,0:T(8,128)S(1)}, f32[65,256]{1,0:T(8,128)S(1)}, u32[]{:S(2)}, u32[]{:S(2)}) collective-permute-start(f32[65,256]{1,0:T(8,128)S(1)} %get-tuple-element.49), channel_id=1, source_target_pairs={{0,4},{1,5},{2,6},{3,7},{4,0},{5,1},{6,2},{7,3},{8,12},{9,13},{10,... | collective-permute-start | bytes 199688 | tf_op jit(solution)/shard_map/ppermute | solution.py:19
  10.2 1.9 %collective-permute-start.6 = (f32[65,256]{1,0:T(8,128)S(1)}, f32[65,256]{1,0:T(8,128)S(1)}, u32[]{:S(2)}, u32[]{:S(2)}) collective-permute-start(f32[65,256]{1,0:T(8,128)S(1)} %get-tuple-element.53), channel_id=1, source_target_pairs={{0,2},{1,3},{2,0},{3,1},{4,6},{5,7},{6,4},{7,5},{8,10},{9,11},{10,... | collective-permute-start | bytes 199688 | tf_op jit(solution)/shard_map/ppermute | solution.py:19
  12.6 1.2 %collective-permute-done.2 = f32[72,256]{1,0:T(8,128)S(1)} collective-permute-done((f32[72,256]{1,0:T(8,128)S(1)}, f32[72,256]{1,0:T(8,128)S(1)}, u32[]{:S(2)}, u32[]{:S(2)}) %collective-permute-start.2) | collective-permute-done | bytes 73760 | tf_op jit(solution)/shard_map/ppermute | solution.py:19
  14.0 1.5 %collective-permute-start.5 = (f32[65,512]{1,0:T(8,128)S(1)}, f32[65,512]{1,0:T(8,128)S(1)}, u32[]{:S(2)}, u32[]{:S(2)}) collective-permute-start(f32[65,512]{1,0:T(8,128)S(1)} %get-tuple-element.52), channel_id=1, source_target_pairs={{0,2},{1,3},{2,0},{3,1},{4,6},{5,7},{6,4},{7,5},{8,10},{9,11},{10,... | collective-permute-start | bytes 399368 | tf_op jit(solution)/shard_map/ppermute | solution.py:19
  15.7 1.8 %shard_map.62 = (bf16[2048,1024]{1,0:T(8,128)(2,1)S(1)}, f32[32,1024]{1,0:T(8,128)S(1)}) custom-call(f32[32,1024]{1,0:T(8,128)S(1)} %get-tuple-element.121.rows_ref, f32[32,1]{1,0:T(8,128)S(1)} %copy.6.scale_ref, bf16[256,1024]{1,0:T(8,128)(2,1)S(1)} %constant_dynamic-update-slice_fusion.right_ref, f32[32,1024]{1,0:T(8,128)S(1)} %get-tuple-element.122.refs_0_, ...), custom_call_target="tpu_custom_call" | custom-call | flops 872415232 | bytes 4194304 | tf_op jit(solution)/shard_map/pallas_call | solution.py:114
  17.5 1.8 %shard_map.63 = (bf16[2048,1024]{1,0:T(8,128)(2,1)S(1)}, f32[32,1024]{1,0:T(8,128)S(1)}) custom-call(f32[32,1024]{1,0:T(8,128)S(1)} %get-tuple-element.126.rows_ref, f32[32,1]{1,0:T(8,128)S(1)} %copy.6.scale_ref, bf16[256,1024]{1,0:T(8,128)(2,1)S(1)} %constant_dynamic-update-slice_fusion.right_ref, f32[32,1024]{1,0:T(8,128)S(1)} %get-tuple-element.125.refs_0_, ...), custom_call_target="tpu_custom_call" | custom-call | flops 872415232 | bytes 4194304 | tf_op jit(solution)/shard_map/pallas_call | solution.py:114
  20.0 1.8 %shard_map.64 = (bf16[2048,1024]{1,0:T(8,128)(2,1)S(1)}, f32[32,1024]{1,0:T(8,128)S(1)}) custom-call(f32[32,1024]{1,0:T(8,128)S(1)} %get-tuple-element.69.rows_ref.part_ref, f32[32,1]{1,0:T(8,128)S(1)} %copy.6.scale_ref, bf16[256,1024]{1,0:T(8,128)(2,1)S(1)} %constant_dynamic-update-slice_fusion.right_ref, f32[32,1024]{1,0:T(8,128)S(1)} %get-tuple-element.118.refs_0_, ...), custom_call_target="tpu_custom_call" | custom-call | flops 872415232 | bytes 4194304 | tf_op jit(solution)/shard_map/pallas_call | solution.py:114
  21.8 1.8 %shard_map.65 = (bf16[2048,1024]{1,0:T(8,128)(2,1)S(1)}, f32[32,1024]{1,0:T(8,128)S(1)}) custom-call(f32[32,1024]{1,0:T(8,128)S(1)} %get-tuple-element.80.rows_ref, f32[32,1]{1,0:T(8,128)S(1)} %copy.6.scale_ref, bf16[256,1024]{1,0:T(8,128)(2,1)S(1)} %constant_dynamic-update-slice_fusion.right_ref, f32[32,1024]{1,0:T(8,128)S(1)} %get-tuple-element.123.refs_0_, ...), custom_call_target="tpu_custom_call" | custom-call | flops 872415232 | bytes 4194304 | tf_op jit(solution)/shard_map/pallas_call | solution.py:114
  23.7 0.9 %collective-permute-start.9 = (f32[32,1024]{1,0:T(8,128)S(1)}, f32[32,1024]{1,0:T(8,128)S(1)}, u32[]{:S(2)}, u32[]{:S(2)}) collective-permute-start(f32[32,1024]{1,0:T(8,128)S(1)} %get-tuple-element.64), channel_id=1, source_target_pairs={{0,2},{1,3},{2,0},{3,1},{4,6},{5,7},{6,4},{7,5},{8,10},{9,11},{10,... | collective-permute-start | bytes 393224 | tf_op jit(solution)/shard_map/ppermute | solution.py:19
  26.0 0.8 %convolution_add_fusion.6 = f32[96,1024]{1,0:T(8,128)S(1)} fusion(f32[96,1024]{1,0:T(8,128)S(1)} %fusion.6, bf16[2048,1024]{1,0:T(8,128)(2,1)S(1)} %get-tuple-element.67, bf16[32,1024]{1,0:T(8,128)(2,1)S(1)} %get-tuple-element.159, bf16[32,1024]{1,0:T(8,128)(2,1)S(1)} %get-tuple-element.160, bf16[32,1024]{1,0:T(8,128)(2,1)S(1)} %get-tuple-element.158), kind=kOutput, calls=%fused_computation.6 | convolution fusion | flops 405110784 | bytes 5177344 | tf_op jit(solution)/shard_map/dot_general | solution.py:152
  27.0 1.1 %shard_map.67 = bf16[2048,1024]{1,0:T(8,128)(2,1)S(1)} custom-call(f32[32,1024]{1,0:T(8,128)S(1)} %get-tuple-element.69.rows_ref.part_ref, f32[32,1]{1,0:T(8,128)S(1)} %copy.6.scale_ref, bf16[256,1024]{1,0:T(8,128)(2,1)S(1)} %shard_map.66.right_ref), custom_call_target="tpu_custom_call" | custom-call | flops 872415232 | bytes 4194304 | tf_op jit(solution)/shard_map/pallas_call | solution.py:114
  28.1 1.1 %collective-permute-done.9 = f32[32,1024]{1,0:T(8,128)S(1)} collective-permute-done((f32[32,1024]{1,0:T(8,128)S(1)}, f32[32,1024]{1,0:T(8,128)S(1)}, u32[]{:S(2)}, u32[]{:S(2)}) %collective-permute-start.9) | collective-permute-done | bytes 131104 | tf_op jit(solution)/shard_map/ppermute | solution.py:19
  29.2 0.8 %fusion.21 = f32[96,1024]{1,0:T(8,128)S(1)} fusion(bf16[2048,1024]{1,0:T(8,128)(2,1)S(1)} %get-tuple-element.73, bf16[32,1024]{1,0:T(8,128)(2,1)S(1)} %get-tuple-element.156, bf16[32,1024]{1,0:T(8,128)(2,1)S(1)} %get-tuple-element.157, bf16[32,1024]{1,0:T(8,128)(2,1)S(1)} %get-tuple-element.155), kind=kOutput, calls=%fused_computation.42 | convolution fusion | flops 405012480 | bytes 4784128 | tf_op jit(solution)/shard_map/dot_general | solution.py:152
  30.9 0.8 %convolution_add_fusion.5 = f32[96,1024]{1,0:T(8,128)S(1)} fusion(f32[96,1024]{1,0:T(8,128)S(1)} %fusion.21, bf16[2048,1024]{1,0:T(8,128)(2,1)S(1)} %get-tuple-element.77, bf16[32,1024]{1,0:T(8,128)(2,1)S(1)} %get-tuple-element.152, bf16[32,1024]{1,0:T(8,128)(2,1)S(1)} %get-tuple-element.153, bf16[32,1024]{1,0:T(8,128)(2,1)S(1)} %get-tuple-element.151), kind=kOutput, calls=%fused_computation.5 | convolution fusion | flops 405110784 | bytes 5177344 | tf_op jit(solution)/shard_map/dot_general | solution.py:152
  31.9 1.4 %collective-permute-start.12 = (f32[32,1024]{1,0:T(8,128)S(1)}, f32[32,1024]{1,0:T(8,128)S(1)}, u32[]{:S(2)}, u32[]{:S(2)}) collective-permute-start(f32[32,1024]{1,0:T(8,128)S(1)} %get-tuple-element.78), channel_id=1, source_target_pairs={{0,2},{1,3},{2,0},{3,1},{4,6},{5,7},{6,4},{7,5},{8,10},{9,11},{10,... | collective-permute-start | bytes 393224 | tf_op jit(solution)/shard_map/ppermute | solution.py:19
  33.5 1.0 %fusion.44 = f32[96,1024]{1,0:T(8,128)S(1)} fusion(bf16[2048,1024]{1,0:T(8,128)(2,1)S(1)} %get-tuple-element.66, bf16[96,1024]{1,0:T(8,128)(2,1)S(1)} %pad_maximum_fusion.3), kind=kOutput, calls=%fused_computation.65 | convolution fusion | flops 403439616 | bytes 4784128 | tf_op jit(solution)/shard_map/dot_general | solution.py:152
  34.9 0.8 %convolution_add_fusion.4 = f32[96,1024]{1,0:T(8,128)S(1)} fusion(f32[96,1024]{1,0:T(8,128)S(1)} %fusion.44, bf16[2048,1024]{1,0:T(8,128)(2,1)S(1)} %get-tuple-element.67, bf16[32,1024]{1,0:T(8,128)(2,1)S(1)} %get-tuple-element.147, bf16[32,1024]{1,0:T(8,128)(2,1)S(1)} %get-tuple-element.148, bf16[32,1024]{1,0:T(8,128)(2,1)S(1)} %get-tuple-element.146), kind=kOutput, calls=%fused_computation.4 | convolution fusion | flops 405110784 | bytes 5177344 | tf_op jit(solution)/shard_map/dot_general | solution.py:152
  35.7 1.1 %shard_map.68 = bf16[2048,1024]{1,0:T(8,128)(2,1)S(1)} custom-call(f32[32,1024]{1,0:T(8,128)S(1)} %get-tuple-element.80.rows_ref, f32[32,1]{1,0:T(8,128)S(1)} %copy.6.scale_ref, bf16[256,1024]{1,0:T(8,128)(2,1)S(1)} %shard_map.66.right_ref), custom_call_target="tpu_custom_call" | custom-call | flops 872415232 | bytes 4194304 | tf_op jit(solution)/shard_map/pallas_call | solution.py:114
  37.6 0.8 %fusion.59 = f32[96,1024]{1,0:T(8,128)S(1)} fusion(bf16[2048,1024]{1,0:T(8,128)(2,1)S(1)} %get-tuple-element.73, bf16[32,1024]{1,0:T(8,128)(2,1)S(1)} %get-tuple-element.144, bf16[32,1024]{1,0:T(8,128)(2,1)S(1)} %get-tuple-element.145, bf16[32,1024]{1,0:T(8,128)(2,1)S(1)} %get-tuple-element.143), kind=kOutput, calls=%fused_computation.80 | convolution fusion | flops 405012480 | bytes 4784128 | tf_op jit(solution)/shard_map/dot_general | solution.py:152
  39.3 0.8 %convolution_add_fusion.3 = f32[96,1024]{1,0:T(8,128)S(1)} fusion(f32[96,1024]{1,0:T(8,128)S(1)} %fusion.59, bf16[2048,1024]{1,0:T(8,128)(2,1)S(1)} %get-tuple-element.77, bf16[32,1024]{1,0:T(8,128)(2,1)S(1)} %get-tuple-element.140, bf16[32,1024]{1,0:T(8,128)(2,1)S(1)} %get-tuple-element.141, bf16[32,1024]{1,0:T(8,128)(2,1)S(1)} %get-tuple-element.139), kind=kOutput, calls=%fused_computation.3 | convolution fusion | flops 405110784 | bytes 5177344 | tf_op jit(solution)/shard_map/dot_general | solution.py:152
  40.3 1.4 %collective-permute-start.15 = (f32[32,1024]{1,0:T(8,128)S(1)}, f32[32,1024]{1,0:T(8,128)S(1)}, u32[]{:S(2)}, u32[]{:S(2)}) collective-permute-start(f32[32,1024]{1,0:T(8,128)S(1)} %get-tuple-element.88), channel_id=1, source_target_pairs={{0,2},{1,3},{2,0},{3,1},{4,6},{5,7},{6,4},{7,5},{8,10},{9,11},{10,... | collective-permute-start | bytes 393224 | tf_op jit(solution)/shard_map/ppermute | solution.py:19
  41.9 0.8 %fusion.82 = f32[96,1024]{1,0:T(8,128)S(1)} fusion(bf16[2048,1024]{1,0:T(8,128)(2,1)S(1)} %get-tuple-element.66, bf16[96,1024]{1,0:T(8,128)(2,1)S(1)} %pad_maximum_fusion.4), kind=kOutput, calls=%fused_computation.103 | convolution fusion | flops 403439616 | bytes 4784128 | tf_op jit(solution)/shard_map/dot_general | solution.py:152
  43.1 0.8 %convolution_add_fusion.2 = f32[96,1024]{1,0:T(8,128)S(1)} fusion(f32[96,1024]{1,0:T(8,128)S(1)} %fusion.82, bf16[2048,1024]{1,0:T(8,128)(2,1)S(1)} %get-tuple-element.67, bf16[32,1024]{1,0:T(8,128)(2,1)S(1)} %get-tuple-element.135, bf16[32,1024]{1,0:T(8,128)(2,1)S(1)} %get-tuple-element.136, bf16[32,1024]{1,0:T(8,128)(2,1)S(1)} %get-tuple-element.134), kind=kOutput, calls=%fused_computation.2 | convolution fusion | flops 405110784 | bytes 5177344 | tf_op jit(solution)/shard_map/dot_general | solution.py:152
  43.9 2.0 %collective-permute-done.15 = f32[32,1024]{1,0:T(8,128)S(1)} collective-permute-done((f32[32,1024]{1,0:T(8,128)S(1)}, f32[32,1024]{1,0:T(8,128)S(1)}, u32[]{:S(2)}, u32[]{:S(2)}) %collective-permute-start.15) | collective-permute-done | bytes 131104 | tf_op jit(solution)/shard_map/ppermute | solution.py:19
  45.9 0.8 %fusion.97 = f32[96,1024]{1,0:T(8,128)S(1)} fusion(bf16[2048,1024]{1,0:T(8,128)(2,1)S(1)} %get-tuple-element.73, bf16[32,1024]{1,0:T(8,128)(2,1)S(1)} %get-tuple-element.132, bf16[32,1024]{1,0:T(8,128)(2,1)S(1)} %get-tuple-element.133, bf16[32,1024]{1,0:T(8,128)(2,1)S(1)} %get-tuple-element.131), kind=kOutput, calls=%fused_computation.118 | convolution fusion | flops 405012480 | bytes 4784128 | tf_op jit(solution)/shard_map/dot_general | solution.py:152
  47.9 0.8 %convolution_add_fusion.1 = f32[96,1024]{1,0:T(8,128)S(1)} fusion(f32[96,1024]{1,0:T(8,128)S(1)} %fusion.97, bf16[2048,1024]{1,0:T(8,128)(2,1)S(1)} %get-tuple-element.77, bf16[32,1024]{1,0:T(8,128)(2,1)S(1)} %get-tuple-element.128, bf16[32,1024]{1,0:T(8,128)(2,1)S(1)} %get-tuple-element.129, bf16[32,1024]{1,0:T(8,128)(2,1)S(1)} %get-tuple-element.127), kind=kOutput, calls=%fused_computation.1 | convolution fusion | flops 405110784 | bytes 5177344 | tf_op jit(solution)/shard_map/dot_general | solution.py:152
  48.7 0.8 %fusion.120 = f32[96,1024]{1,0:T(8,128)S(1)} fusion(bf16[2048,1024]{1,0:T(8,128)(2,1)S(1)} %shard_map.67, bf16[32,1024]{1,0:T(8,128)(2,1)S(1)} %get-tuple-element.114, bf16[32,1024]{1,0:T(8,128)(2,1)S(1)} %get-tuple-element.113, bf16[32,1024]{1,0:T(8,128)(2,1)S(1)} %get-tuple-element.117), kind=kOutput, calls=%fused_computation.141 | convolution fusion | flops 405012480 | bytes 4784128 | tf_op jit(solution)/shard_map/dot_general | solution.py:152
  49.5 0.8 %convolution_add_fusion = f32[96,1024]{1,0:T(8,128)S(1)} fusion(f32[96,1024]{1,0:T(8,128)S(1)} %fusion.120, bf16[2048,1024]{1,0:T(8,128)(2,1)S(1)} %shard_map.68, bf16[32,1024]{1,0:T(8,128)(2,1)S(1)} %get-tuple-element.115, bf16[32,1024]{1,0:T(8,128)(2,1)S(1)} %get-tuple-element.116, bf16[32,1024]{1,0:T(8,128)(2,1)S(1)} %get-tuple-element.112), kind=kOutput, calls=%fused_computation | convolution fusion | flops 405110784 | bytes 5177344 | tf_op jit(solution)/shard_map/dot_general | solution.py:152
  50.9 0.9 %collective-permute-done.17 = f32[32]{0:T(128)S(1)} collective-permute-done((f32[32]{0:T(128)S(1)}, f32[32]{0:T(128)S(1)}, u32[]{:S(2)}, u32[]{:S(2)}) %collective-permute-start.17) | collective-permute-done | bytes 160 | tf_op jit(solution)/shard_map/ppermute | solution.py:19
  (86 shorter events, 11.5 us)
Async XLA Ops:
  1.4 8.1 %collective-permute-start = (f32[72,256]{1,0:T(8,128)S(1)}, f32[72,256]{1,0:T(8,128)S(1)}, u32[]{:S(2)}, u32[]{:S(2)}) collective-permute-start(f32[72,256]{1,0:T(8,128)S(1)} %select_maximum_fusion.part_ref), channel_id=1, source_target_pairs={{0,8},{1,9},{2,10},{3,11},{4,12},{5,13},{6,14},{7,15},{8,0},{9,1},... | collective-permute-start | bytes 221192 | tf_op jit(solution)/shard_map/ppermute | solution.py:19
  6.3 7.7 %collective-permute-start.4 = (f32[65,256]{1,0:T(8,128)S(1)}, f32[65,256]{1,0:T(8,128)S(1)}, u32[]{:S(2)}, u32[]{:S(2)}) collective-permute-start(f32[65,256]{1,0:T(8,128)S(1)} %get-tuple-element.49), channel_id=1, source_target_pairs={{0,2},{1,3},{2,0},{3,1},{4,6},{5,7},{6,4},{7,5},{8,10},{9,11},{10,... | collective-permute-start | bytes 199688 | tf_op jit(solution)/shard_map/ppermute | solution.py:19
  7.9 4.7 %collective-permute-start.1 = (f32[65,256]{1,0:T(8,128)S(1)}, f32[65,256]{1,0:T(8,128)S(1)}, u32[]{:S(2)}, u32[]{:S(2)}) collective-permute-start(f32[65,256]{1,0:T(8,128)S(1)} %get-tuple-element.49), channel_id=1, source_target_pairs={{0,4},{1,5},{2,6},{3,7},{4,0},{5,1},{6,2},{7,3},{8,12},{9,13},{10,... | collective-permute-start | bytes 199688 | tf_op jit(solution)/shard_map/ppermute | solution.py:19
  9.5 4.4 %collective-permute-start.2 = (f32[72,256]{1,0:T(8,128)S(1)}, f32[72,256]{1,0:T(8,128)S(1)}, u32[]{:S(2)}, u32[]{:S(2)}) collective-permute-start(f32[72,256]{1,0:T(8,128)S(1)} %collective-permute-done.part_ref), channel_id=1, source_target_pairs={{0,4},{1,5},{2,6},{3,7},{4,0},{5,1},{6,2},{7,3},{8,12},{9,13},{10,... | collective-permute-start | bytes 221192 | tf_op jit(solution)/shard_map/ppermute | solution.py:19
  10.2 9.1 %collective-permute-start.6 = (f32[65,256]{1,0:T(8,128)S(1)}, f32[65,256]{1,0:T(8,128)S(1)}, u32[]{:S(2)}, u32[]{:S(2)}) collective-permute-start(f32[65,256]{1,0:T(8,128)S(1)} %get-tuple-element.53), channel_id=1, source_target_pairs={{0,2},{1,3},{2,0},{3,1},{4,6},{5,7},{6,4},{7,5},{8,10},{9,11},{10,... | collective-permute-start | bytes 199688 | tf_op jit(solution)/shard_map/ppermute | solution.py:19
  14.0 5.3 %collective-permute-start.5 = (f32[65,512]{1,0:T(8,128)S(1)}, f32[65,512]{1,0:T(8,128)S(1)}, u32[]{:S(2)}, u32[]{:S(2)}) collective-permute-start(f32[65,512]{1,0:T(8,128)S(1)} %get-tuple-element.52), channel_id=1, source_target_pairs={{0,2},{1,3},{2,0},{3,1},{4,6},{5,7},{6,4},{7,5},{8,10},{9,11},{10,... | collective-permute-start | bytes 399368 | tf_op jit(solution)/shard_map/ppermute | solution.py:19
  15.6 1.9 %collective-permute-start.3 = (f32[64,1024]{1,0:T(8,128)S(1)}, f32[64,1024]{1,0:T(8,128)S(1)}, u32[]{:S(2)}, u32[]{:S(2)}) collective-permute-start(f32[64,1024]{1,0:T(8,128)S(1)} %slice.225), channel_id=1, source_target_pairs={{0,1},{1,0},{2,3},{3,2},{4,5},{5,4},{6,7},{7,6},{8,9},{9,8},{10,11... | collective-permute-start | bytes 786440 | tf_op jit(solution)/shard_map/ppermute | solution.py:19
  19.4 2.4 %collective-permute-start.7 = (f32[64,1024]{1,0:T(8,128)S(1)}, f32[64,1024]{1,0:T(8,128)S(1)}, u32[]{:S(2)}, u32[]{:S(2)}) collective-permute-start(f32[64,1024]{1,0:T(8,128)S(1)} %slice.230), channel_id=1, source_target_pairs={{0,1},{1,0},{2,3},{3,2},{4,5},{5,4},{6,7},{7,6},{8,9},{9,8},{10,11... | collective-permute-start | bytes 786440 | tf_op jit(solution)/shard_map/ppermute | solution.py:19
  23.7 5.5 %collective-permute-start.9 = (f32[32,1024]{1,0:T(8,128)S(1)}, f32[32,1024]{1,0:T(8,128)S(1)}, u32[]{:S(2)}, u32[]{:S(2)}) collective-permute-start(f32[32,1024]{1,0:T(8,128)S(1)} %get-tuple-element.64), channel_id=1, source_target_pairs={{0,2},{1,3},{2,0},{3,1},{4,6},{5,7},{6,4},{7,5},{8,10},{9,11},{10,... | collective-permute-start | bytes 393224 | tf_op jit(solution)/shard_map/ppermute | solution.py:19
  24.6 1.4 %collective-permute-start.8 = (f32[32,1024]{1,0:T(8,128)S(1)}, f32[32,1024]{1,0:T(8,128)S(1)}, u32[]{:S(2)}, u32[]{:S(2)}) collective-permute-start(f32[32,1024]{1,0:T(8,128)S(1)} %get-tuple-element.64), channel_id=1, source_target_pairs={{0,1},{1,0},{2,3},{3,2},{4,5},{5,4},{6,7},{7,6},{8,9},{9,8},{10,11... | collective-permute-start | bytes 393224 | tf_op jit(solution)/shard_map/ppermute | solution.py:19
  29.2 1.3 %collective-permute-start.10 = (f32[32,1024]{1,0:T(8,128)S(1)}, f32[32,1024]{1,0:T(8,128)S(1)}, u32[]{:S(2)}, u32[]{:S(2)}) collective-permute-start(f32[32,1024]{1,0:T(8,128)S(1)} %collective-permute-done.9), channel_id=1, source_target_pairs={{0,1},{1,0},{2,3},{3,2},{4,5},{5,4},{6,7},{7,6},{8,9},{9,8},{10,11... | collective-permute-start | bytes 393224 | tf_op jit(solution)/shard_map/ppermute | solution.py:19
  31.9 5.6 %collective-permute-start.12 = (f32[32,1024]{1,0:T(8,128)S(1)}, f32[32,1024]{1,0:T(8,128)S(1)}, u32[]{:S(2)}, u32[]{:S(2)}) collective-permute-start(f32[32,1024]{1,0:T(8,128)S(1)} %get-tuple-element.78), channel_id=1, source_target_pairs={{0,2},{1,3},{2,0},{3,1},{4,6},{5,7},{6,4},{7,5},{8,10},{9,11},{10,... | collective-permute-start | bytes 393224 | tf_op jit(solution)/shard_map/ppermute | solution.py:19
  33.4 1.4 %collective-permute-start.11 = (f32[32,1024]{1,0:T(8,128)S(1)}, f32[32,1024]{1,0:T(8,128)S(1)}, u32[]{:S(2)}, u32[]{:S(2)}) collective-permute-start(f32[32,1024]{1,0:T(8,128)S(1)} %get-tuple-element.78), channel_id=1, source_target_pairs={{0,1},{1,0},{2,3},{3,2},{4,5},{5,4},{6,7},{7,6},{8,9},{9,8},{10,11... | collective-permute-start | bytes 393224 | tf_op jit(solution)/shard_map/ppermute | solution.py:19
  37.5 1.3 %collective-permute-start.13 = (f32[32,1024]{1,0:T(8,128)S(1)}, f32[32,1024]{1,0:T(8,128)S(1)}, u32[]{:S(2)}, u32[]{:S(2)}) collective-permute-start(f32[32,1024]{1,0:T(8,128)S(1)} %collective-permute-done.12), channel_id=1, source_target_pairs={{0,1},{1,0},{2,3},{3,2},{4,5},{5,4},{6,7},{7,6},{8,9},{9,8},{10,11... | collective-permute-start | bytes 393224 | tf_op jit(solution)/shard_map/ppermute | solution.py:19
  40.3 5.6 %collective-permute-start.15 = (f32[32,1024]{1,0:T(8,128)S(1)}, f32[32,1024]{1,0:T(8,128)S(1)}, u32[]{:S(2)}, u32[]{:S(2)}) collective-permute-start(f32[32,1024]{1,0:T(8,128)S(1)} %get-tuple-element.88), channel_id=1, source_target_pairs={{0,2},{1,3},{2,0},{3,1},{4,6},{5,7},{6,4},{7,5},{8,10},{9,11},{10,... | collective-permute-start | bytes 393224 | tf_op jit(solution)/shard_map/ppermute | solution.py:19
  41.7 1.4 %collective-permute-start.14 = (f32[32,1024]{1,0:T(8,128)S(1)}, f32[32,1024]{1,0:T(8,128)S(1)}, u32[]{:S(2)}, u32[]{:S(2)}) collective-permute-start(f32[32,1024]{1,0:T(8,128)S(1)} %get-tuple-element.88), channel_id=1, source_target_pairs={{0,1},{1,0},{2,3},{3,2},{4,5},{5,4},{6,7},{7,6},{8,9},{9,8},{10,11... | collective-permute-start | bytes 393224 | tf_op jit(solution)/shard_map/ppermute | solution.py:19
  45.9 1.3 %collective-permute-start.16 = (f32[32,1024]{1,0:T(8,128)S(1)}, f32[32,1024]{1,0:T(8,128)S(1)}, u32[]{:S(2)}, u32[]{:S(2)}) collective-permute-start(f32[32,1024]{1,0:T(8,128)S(1)} %collective-permute-done.15), channel_id=1, source_target_pairs={{0,1},{1,0},{2,3},{3,2},{4,5},{5,4},{6,7},{7,6},{8,9},{9,8},{10,11... | collective-permute-start | bytes 393224 | tf_op jit(solution)/shard_map/ppermute | solution.py:19
  50.7 1.2 %collective-permute-start.17 = (f32[32]{0:T(128)S(1)}, f32[32]{0:T(128)S(1)}, u32[]{:S(2)}, u32[]{:S(2)}) collective-permute-start(f32[32]{0:T(128)S(1)} %get-tuple-element.96), channel_id=1, source_target_pairs={{0,1},{1,0},{2,3},{3,2},{4,5},{5,4},{6,7},{7,6},{8,9},{9,8},{10,11... | collective-permute-start | bytes 392 | tf_op jit(solution)/shard_map/ppermute | solution.py:19

commit v33 on v27

--- a/solution.py
+++ b/solution.py
@@ -74,28 +74,33 @@
         high, rest = halve(vectors_ref[...])
         mid, rest = halve(rest)
         thrice = jnp.concatenate([high, mid, rest.astype(jnp.bfloat16)], axis=0)
-    steps = [(top, at) for top in range(0, total, block) for at in range(0, cols, step)]
+    steps = [(top, at, block) for top in range(0, total, block) for at in range(0, cols, step)]
+    if len(steps) > 1:
+        top, at, _ = steps.pop()
+        steps += [(top, at, block // 2), (top + block // 2, at, block // 2)]
     lefts, powers, parts = {}, {}, {}
-
-    def contract(top, at):
-        if top not in lefts:
-            lefts[top] = jnp.transpose(operands(rows_ref[:, top : top + block] * scale_ref[...])[0])
-        powers[top, at] = jnp.dot(lefts[top], right_ref[:, at : at + step], preferred_element_type=jnp.float32)
-
-    def raise_power(top, at):
+    fresh = {(0, at) for at in range(0, cols, step)}
+
+    def contract(top, at, size):
+        base = top // block * block
+        if base not in lefts:
+            lefts[base] = jnp.transpose(operands(rows_ref[:, base : base + block] * scale_ref[...])[0])
+        powers[top, at] = jnp.dot(lefts[base][top - base : top - base + size], right_ref[:, at : at + step], preferred_element_type=jnp.float32)
+
+    def raise_power(top, at, block):
         high, rest = halve(jnp.exp2(powers.pop((top, at))))
         low = rest.astype(jnp.bfloat16)
         tile_ref[top : top + block, at : at + step] = high
         tile_ref[total + top : total + top + block, at : at + step] = low
         parts[top, at] = high, low
 
-    def apply(top, at):
+    def apply(top, at, block):
         down, here = slice(top, top + block), slice(at, at + step)
         vectors = jnp.concatenate([thrice[:, down]] * 2, axis=1)
         both = jnp.concatenate(parts.pop((top, at)), axis=0)
         term = jnp.dot(vectors, both, preferred_element_type=jnp.float32)
         term = term[:probes] + (term[probes : 2 * probes] + term[2 * probes :])
-        before = sum_ref if top == 0 else out_ref
+        before = sum_ref if (top, at) in fresh else out_ref
         out_ref[:, here] = before[:, here] + term
 
     contract(*steps[0])

time: 52.2 us -> 52.1 us (level)
  no operation moved by 1% of the time
where the time goes in v33:
time: 52.1 us; the launch traced here: 51.9 us
  starting transfers between devices  16.4 us (31%)
  matrix products  11.5 us (22%)
  waiting for transfers between devices  8.73 us (17%)
  Pallas kernels  8.63 us (17%)
  other arithmetic  5.41 us (10%)
  between operations  1 us (2%)
    ppermute x18, starting transfers between devices, swap(): return lax.ppermute(x, 'blk', [(i, i ^ stride) for i in range(n)])  16.4 us
    dot_general x14, matrix products, apply_parts(): jnp.dot(jnp.concatenate([parts, parts], axis=1), piece, preferred_element...  11.5 us
    ppermute x18, waiting for transfers between devices, swap(): return lax.ppermute(x, 'blk', [(i, i ^ stride) for i in range(n)])  8.73 us
    pallas_call x10, Pallas kernels, call(): pl.pallas_call(kernel, out_shape=outs, in_specs=[whole] * len(args), out_...  8.63 us
  transfers between devices with their start and end apart: 18, of which 13 were waited for; matrix products, arithmetic and copies ran while one was open for 18% of the time, Pallas kernels for 14%

profile of v33, /device:TPU:0, one launch (start us, length us, event | category | flops | bytes accessed | tf_op | source)
XLA Modules:
  0.0 51.9 jit_solution(8581401199304080531)
XLA Ops:
  0.6 0.8 %select_maximum_fusion.part_ref = f32[72,256]{1,0:T(8,128)S(1)} fusion(f32[1,256]{1,0:T(1,128)} %bitcast.32, f32[32,256]{1,0:T(8,128)} %param.7, f32[32,256]{1,0:T(8,128)} %param.4), kind=kLoop, calls=%fused_computation.276 | loop fusion | flops 73728 | bytes 140288 | tf_op jit(solution)/shard_map/concatenate | solution.py:192
  1.4 4.0 %collective-permute-start = (f32[72,256]{1,0:T(8,128)S(1)}, f32[72,256]{1,0:T(8,128)S(1)}, u32[]{:S(2)}, u32[]{:S(2)}) collective-permute-start(f32[72,256]{1,0:T(8,128)S(1)} %select_maximum_fusion.part_ref), channel_id=1, source_target_pairs={{0,8},{1,9},{2,10},{3,11},{4,12},{5,13},{6,14},{7,15},{8,0},{9,1},... | collective-permute-start | bytes 221192 | tf_op jit(solution)/shard_map/ppermute | solution.py:19
  6.3 1.6 %collective-permute-start.4 = (f32[65,256]{1,0:T(8,128)S(1)}, f32[65,256]{1,0:T(8,128)S(1)}, u32[]{:S(2)}, u32[]{:S(2)}) collective-permute-start(f32[65,256]{1,0:T(8,128)S(1)} %get-tuple-element.49), channel_id=1, source_target_pairs={{0,2},{1,3},{2,0},{3,1},{4,6},{5,7},{6,4},{7,5},{8,10},{9,11},{10,... | collective-permute-start | bytes 199688 | tf_op jit(solution)/shard_map/ppermute | solution.py:19
  7.9 1.6 %collective-permute-start.1 = (f32[65,256]{1,0:T(8,128)S(1)}, f32[65,256]{1,0:T(8,128)S(1)}, u32[]{:S(2)}, u32[]{:S(2)}) collective-permute-start(f32[65,256]{1,0:T(8,128)S(1)} %get-tuple-element.49), channel_id=1, source_target_pairs={{0,4},{1,5},{2,6},{3,7},{4,0},{5,1},{6,2},{7,3},{8,12},{9,13},{10,... | collective-permute-start | bytes 199688 | tf_op jit(solution)/shard_map/ppermute | solution.py:19
  10.2 1.9 %collective-permute-start.6 = (f32[65,256]{1,0:T(8,128)S(1)}, f32[65,256]{1,0:T(8,128)S(1)}, u32[]{:S(2)}, u32[]{:S(2)}) collective-permute-start(f32[65,256]{1,0:T(8,128)S(1)} %get-tuple-element.53), channel_id=1, source_target_pairs={{0,2},{1,3},{2,0},{3,1},{4,6},{5,7},{6,4},{7,5},{8,10},{9,11},{10,... | collective-permute-start | bytes 199688 | tf_op jit(solution)/shard_map/ppermute | solution.py:19
  12.6 1.2 %collective-permute-done.2 = f32[72,256]{1,0:T(8,128)S(1)} collective-permute-done((f32[72,256]{1,0:T(8,128)S(1)}, f32[72,256]{1,0:T(8,128)S(1)}, u32[]{:S(2)}, u32[]{:S(2)}) %collective-permute-start.2) | collective-permute-done | bytes 73760 | tf_op jit(solution)/shard_map/ppermute | solution.py:19
  14.0 1.5 %collective-permute-start.5 = (f32[65,512]{1,0:T(8,128)S(1)}, f32[65,512]{1,0:T(8,128)S(1)}, u32[]{:S(2)}, u32[]{:S(2)}) collective-permute-start(f32[65,512]{1,0:T(8,128)S(1)} %get-tuple-element.52), channel_id=1, source_target_pairs={{0,2},{1,3},{2,0},{3,1},{4,6},{5,7},{6,4},{7,5},{8,10},{9,11},{10,... | collective-permute-start | bytes 399368 | tf_op jit(solution)/shard_map/ppermute | solution.py:19
  15.7 1.5 %shard_map.62 = (bf16[2048,1024]{1,0:T(8,128)(2,1)S(1)}, f32[32,1024]{1,0:T(8,128)S(1)}) custom-call(f32[32,1024]{1,0:T(8,128)S(1)} %get-tuple-element.121.rows_ref, f32[32,1]{1,0:T(8,128)S(1)} %copy.6.scale_ref, bf16[256,1024]{1,0:T(8,128)(2,1)S(1)} %constant_dynamic-update-slice_fusion.right_ref, f32[32,1024]{1,0:T(8,128)S(1)} %get-tuple-element.122.refs_0_, ...), custom_call_target="tpu_custom_call" | custom-call | flops 872415232 | bytes 4194304 | tf_op jit(solution)/shard_map/pallas_call | solution.py:119
  17.3 1.5 %shard_map.63 = (bf16[2048,1024]{1,0:T(8,128)(2,1)S(1)}, f32[32,1024]{1,0:T(8,128)S(1)}) custom-call(f32[32,1024]{1,0:T(8,128)S(1)} %get-tuple-element.126.rows_ref, f32[32,1]{1,0:T(8,128)S(1)} %copy.6.scale_ref, bf16[256,1024]{1,0:T(8,128)(2,1)S(1)} %constant_dynamic-update-slice_fusion.right_ref, f32[32,1024]{1,0:T(8,128)S(1)} %get-tuple-element.125.refs_0_, ...), custom_call_target="tpu_custom_call" | custom-call | flops 872415232 | bytes 4194304 | tf_op jit(solution)/shard_map/pallas_call | solution.py:119
  19.5 1.5 %shard_map.64 = (bf16[2048,1024]{1,0:T(8,128)(2,1)S(1)}, f32[32,1024]{1,0:T(8,128)S(1)}) custom-call(f32[32,1024]{1,0:T(8,128)S(1)} %get-tuple-element.69.rows_ref.part_ref, f32[32,1]{1,0:T(8,128)S(1)} %copy.6.scale_ref, bf16[256,1024]{1,0:T(8,128)(2,1)S(1)} %constant_dynamic-update-slice_fusion.right_ref, f32[32,1024]{1,0:T(8,128)S(1)} %get-tuple-element.118.refs_0_, ...), custom_call_target="tpu_custom_call" | custom-call | flops 872415232 | bytes 4194304 | tf_op jit(solution)/shard_map/pallas_call | solution.py:119
  21.0 1.5 %shard_map.65 = (bf16[2048,1024]{1,0:T(8,128)(2,1)S(1)}, f32[32,1024]{1,0:T(8,128)S(1)}) custom-call(f32[32,1024]{1,0:T(8,128)S(1)} %get-tuple-element.80.rows_ref, f32[32,1]{1,0:T(8,128)S(1)} %copy.6.scale_ref, bf16[256,1024]{1,0:T(8,128)(2,1)S(1)} %constant_dynamic-update-slice_fusion.right_ref, f32[32,1024]{1,0:T(8,128)S(1)} %get-tuple-element.123.refs_0_, ...), custom_call_target="tpu_custom_call" | custom-call | flops 872415232 | bytes 4194304 | tf_op jit(solution)/shard_map/pallas_call | solution.py:119
  22.6 1.4 %collective-permute-start.9 = (f32[32,1024]{1,0:T(8,128)S(1)}, f32[32,1024]{1,0:T(8,128)S(1)}, u32[]{:S(2)}, u32[]{:S(2)}) collective-permute-start(f32[32,1024]{1,0:T(8,128)S(1)} %get-tuple-element.64), channel_id=1, source_target_pairs={{0,2},{1,3},{2,0},{3,1},{4,6},{5,7},{6,4},{7,5},{8,10},{9,11},{10,... | collective-permute-start | bytes 393224 | tf_op jit(solution)/shard_map/ppermute | solution.py:19
  25.5 0.8 %convolution_add_fusion.6 = f32[96,1024]{1,0:T(8,128)S(1)} fusion(f32[96,1024]{1,0:T(8,128)S(1)} %fusion.6, bf16[2048,1024]{1,0:T(8,128)(2,1)S(1)} %get-tuple-element.67, bf16[32,1024]{1,0:T(8,128)(2,1)S(1)} %get-tuple-element.159, bf16[32,1024]{1,0:T(8,128)(2,1)S(1)} %get-tuple-element.160, bf16[32,1024]{1,0:T(8,128)(2,1)S(1)} %get-tuple-element.158), kind=kOutput, calls=%fused_computation.6 | convolution fusion | flops 405110784 | bytes 5177344 | tf_op jit(solution)/shard_map/dot_general | solution.py:157
  26.5 1.1 %shard_map.67 = bf16[2048,1024]{1,0:T(8,128)(2,1)S(1)} custom-call(f32[32,1024]{1,0:T(8,128)S(1)} %get-tuple-element.69.rows_ref.part_ref, f32[32,1]{1,0:T(8,128)S(1)} %copy.6.scale_ref, bf16[256,1024]{1,0:T(8,128)(2,1)S(1)} %shard_map.66.right_ref), custom_call_target="tpu_custom_call" | custom-call | flops 872415232 | bytes 4194304 | tf_op jit(solution)/shard_map/pallas_call | solution.py:119
  27.5 1.0 %collective-permute-done.9 = f32[32,1024]{1,0:T(8,128)S(1)} collective-permute-done((f32[32,1024]{1,0:T(8,128)S(1)}, f32[32,1024]{1,0:T(8,128)S(1)}, u32[]{:S(2)}, u32[]{:S(2)}) %collective-permute-start.9) | collective-permute-done | bytes 131104 | tf_op jit(solution)/shard_map/ppermute | solution.py:19
  28.6 0.8 %fusion.21 = f32[96,1024]{1,0:T(8,128)S(1)} fusion(bf16[2048,1024]{1,0:T(8,128)(2,1)S(1)} %get-tuple-element.73, bf16[32,1024]{1,0:T(8,128)(2,1)S(1)} %get-tuple-element.156, bf16[32,1024]{1,0:T(8,128)(2,1)S(1)} %get-tuple-element.157, bf16[32,1024]{1,0:T(8,128)(2,1)S(1)} %get-tuple-element.155), kind=kOutput, calls=%fused_computation.42 | convolution fusion | flops 405012480 | bytes 4784128 | tf_op jit(solution)/shard_map/dot_general | solution.py:157
  30.3 0.8 %convolution_add_fusion.5 = f32[96,1024]{1,0:T(8,128)S(1)} fusion(f32[96,1024]{1,0:T(8,128)S(1)} %fusion.21, bf16[2048,1024]{1,0:T(8,128)(2,1)S(1)} %get-tuple-element.77, bf16[32,1024]{1,0:T(8,128)(2,1)S(1)} %get-tuple-element.152, bf16[32,1024]{1,0:T(8,128)(2,1)S(1)} %get-tuple-element.153, bf16[32,1024]{1,0:T(8,128)(2,1)S(1)} %get-tuple-element.151), kind=kOutput, calls=%fused_computation.5 | convolution fusion | flops 405110784 | bytes 5177344 | tf_op jit(solution)/shard_map/dot_general | solution.py:157
  31.3 1.5 %collective-permute-start.12 = (f32[32,1024]{1,0:T(8,128)S(1)}, f32[32,1024]{1,0:T(8,128)S(1)}, u32[]{:S(2)}, u32[]{:S(2)}) collective-permute-start(f32[32,1024]{1,0:T(8,128)S(1)} %get-tuple-element.78), channel_id=1, source_target_pairs={{0,2},{1,3},{2,0},{3,1},{4,6},{5,7},{6,4},{7,5},{8,10},{9,11},{10,... | collective-permute-start | bytes 393224 | tf_op jit(solution)/shard_map/ppermute | solution.py:19
  33.0 0.8 %fusion.44 = f32[96,1024]{1,0:T(8,128)S(1)} fusion(bf16[2048,1024]{1,0:T(8,128)(2,1)S(1)} %get-tuple-element.66, bf16[96,1024]{1,0:T(8,128)(2,1)S(1)} %pad_maximum_fusion.3), kind=kOutput, calls=%fused_computation.65 | convolution fusion | flops 403439616 | bytes 4784128 | tf_op jit(solution)/shard_map/dot_general | solution.py:157
  34.3 1.0 %convolution_add_fusion.4 = f32[96,1024]{1,0:T(8,128)S(1)} fusion(f32[96,1024]{1,0:T(8,128)S(1)} %fusion.44, bf16[2048,1024]{1,0:T(8,128)(2,1)S(1)} %get-tuple-element.67, bf16[32,1024]{1,0:T(8,128)(2,1)S(1)} %get-tuple-element.147, bf16[32,1024]{1,0:T(8,128)(2,1)S(1)} %get-tuple-element.148, bf16[32,1024]{1,0:T(8,128)(2,1)S(1)} %get-tuple-element.146), kind=kOutput, calls=%fused_computation.4 | convolution fusion | flops 405110784 | bytes 5177344 | tf_op jit(solution)/shard_map/dot_general | solution.py:157
  35.3 1.1 %shard_map.68 = bf16[2048,1024]{1,0:T(8,128)(2,1)S(1)} custom-call(f32[32,1024]{1,0:T(8,128)S(1)} %get-tuple-element.80.rows_ref, f32[32,1]{1,0:T(8,128)S(1)} %copy.6.scale_ref, bf16[256,1024]{1,0:T(8,128)(2,1)S(1)} %shard_map.66.right_ref), custom_call_target="tpu_custom_call" | custom-call | flops 872415232 | bytes 4194304 | tf_op jit(solution)/shard_map/pallas_call | solution.py:119
  36.9 0.8 %fusion.59 = f32[96,1024]{1,0:T(8,128)S(1)} fusion(bf16[2048,1024]{1,0:T(8,128)(2,1)S(1)} %get-tuple-element.73, bf16[32,1024]{1,0:T(8,128)(2,1)S(1)} %get-tuple-element.144, bf16[32,1024]{1,0:T(8,128)(2,1)S(1)} %get-tuple-element.145, bf16[32,1024]{1,0:T(8,128)(2,1)S(1)} %get-tuple-element.143), kind=kOutput, calls=%fused_computation.80 | convolution fusion | flops 405012480 | bytes 4784128 | tf_op jit(solution)/shard_map/dot_general | solution.py:157
  38.7 0.8 %convolution_add_fusion.3 = f32[96,1024]{1,0:T(8,128)S(1)} fusion(f32[96,1024]{1,0:T(8,128)S(1)} %fusion.59, bf16[2048,1024]{1,0:T(8,128)(2,1)S(1)} %get-tuple-element.77, bf16[32,1024]{1,0:T(8,128)(2,1)S(1)} %get-tuple-element.140, bf16[32,1024]{1,0:T(8,128)(2,1)S(1)} %get-tuple-element.141, bf16[32,1024]{1,0:T(8,128)(2,1)S(1)} %get-tuple-element.139), kind=kOutput, calls=%fused_computation.3 | convolution fusion | flops 405110784 | bytes 5177344 | tf_op jit(solution)/shard_map/dot_general | solution.py:157
  39.6 1.5 %collective-permute-start.15 = (f32[32,1024]{1,0:T(8,128)S(1)}, f32[32,1024]{1,0:T(8,128)S(1)}, u32[]{:S(2)}, u32[]{:S(2)}) collective-permute-start(f32[32,1024]{1,0:T(8,128)S(1)} %get-tuple-element.88), channel_id=1, source_target_pairs={{0,2},{1,3},{2,0},{3,1},{4,6},{5,7},{6,4},{7,5},{8,10},{9,11},{10,... | collective-permute-start | bytes 393224 | tf_op jit(solution)/shard_map/ppermute | solution.py:19
  41.3 0.8 %fusion.82 = f32[96,1024]{1,0:T(8,128)S(1)} fusion(bf16[2048,1024]{1,0:T(8,128)(2,1)S(1)} %get-tuple-element.66, bf16[96,1024]{1,0:T(8,128)(2,1)S(1)} %pad_maximum_fusion.4), kind=kOutput, calls=%fused_computation.103 | convolution fusion | flops 403439616 | bytes 4784128 | tf_op jit(solution)/shard_map/dot_general | solution.py:157
  42.6 0.8 %convolution_add_fusion.2 = f32[96,1024]{1,0:T(8,128)S(1)} fusion(f32[96,1024]{1,0:T(8,128)S(1)} %fusion.82, bf16[2048,1024]{1,0:T(8,128)(2,1)S(1)} %get-tuple-element.67, bf16[32,1024]{1,0:T(8,128)(2,1)S(1)} %get-tuple-element.135, bf16[32,1024]{1,0:T(8,128)(2,1)S(1)} %get-tuple-element.136, bf16[32,1024]{1,0:T(8,128)(2,1)S(1)} %get-tuple-element.134), kind=kOutput, calls=%fused_computation.2 | convolution fusion | flops 405110784 | bytes 5177344 | tf_op jit(solution)/shard_map/dot_general | solution.py:157
  43.4 1.9 %collective-permute-done.15 = f32[32,1024]{1,0:T(8,128)S(1)} collective-permute-done((f32[32,1024]{1,0:T(8,128)S(1)}, f32[32,1024]{1,0:T(8,128)S(1)}, u32[]{:S(2)}, u32[]{:S(2)}) %collective-permute-start.15) | collective-permute-done | bytes 131104 | tf_op jit(solution)/shard_map/ppermute | solution.py:19
  45.3 0.8 %fusion.97 = f32[96,1024]{1,0:T(8,128)S(1)} fusion(bf16[2048,1024]{1,0:T(8,128)(2,1)S(1)} %get-tuple-element.73, bf16[32,1024]{1,0:T(8,128)(2,1)S(1)} %get-tuple-element.132, bf16[32,1024]{1,0:T(8,128)(2,1)S(1)} %get-tuple-element.133, bf16[32,1024]{1,0:T(8,128)(2,1)S(1)} %get-tuple-element.131), kind=kOutput, calls=%fused_computation.118 | convolution fusion | flops 405012480 | bytes 4784128 | tf_op jit(solution)/shard_map/dot_general | solution.py:157
  47.2 0.8 %convolution_add_fusion.1 = f32[96,1024]{1,0:T(8,128)S(1)} fusion(f32[96,1024]{1,0:T(8,128)S(1)} %fusion.97, bf16[2048,1024]{1,0:T(8,128)(2,1)S(1)} %get-tuple-element.77, bf16[32,1024]{1,0:T(8,128)(2,1)S(1)} %get-tuple-element.128, bf16[32,1024]{1,0:T(8,128)(2,1)S(1)} %get-tuple-element.129, bf16[32,1024]{1,0:T(8,128)(2,1)S(1)} %get-tuple-element.127), kind=kOutput, calls=%fused_computation.1 | convolution fusion | flops 405110784 | bytes 5177344 | tf_op jit(solution)/shard_map/dot_general | solution.py:157
  48.1 0.8 %fusion.120 = f32[96,1024]{1,0:T(8,128)S(1)} fusion(bf16[2048,1024]{1,0:T(8,128)(2,1)S(1)} %shard_map.67, bf16[32,1024]{1,0:T(8,128)(2,1)S(1)} %get-tuple-element.114, bf16[32,1024]{1,0:T(8,128)(2,1)S(1)} %get-tuple-element.113, bf16[32,1024]{1,0:T(8,128)(2,1)S(1)} %get-tuple-element.117), kind=kOutput, calls=%fused_computation.141 | convolution fusion | flops 405012480 | bytes 4784128 | tf_op jit(solution)/shard_map/dot_general | solution.py:157
  48.9 0.8 %convolution_add_fusion = f32[96,1024]{1,0:T(8,128)S(1)} fusion(f32[96,1024]{1,0:T(8,128)S(1)} %fusion.120, bf16[2048,1024]{1,0:T(8,128)(2,1)S(1)} %shard_map.68, bf16[32,1024]{1,0:T(8,128)(2,1)S(1)} %get-tuple-element.115, bf16[32,1024]{1,0:T(8,128)(2,1)S(1)} %get-tuple-element.116, bf16[32,1024]{1,0:T(8,128)(2,1)S(1)} %get-tuple-element.112), kind=kOutput, calls=%fused_computation | convolution fusion | flops 405110784 | bytes 5177344 | tf_op jit(solution)/shard_map/dot_general | solution.py:157
  50.3 0.9 %collective-permute-done.17 = f32[32]{0:T(128)S(1)} collective-permute-done((f32[32]{0:T(128)S(1)}, f32[32]{0:T(128)S(1)}, u32[]{:S(2)}, u32[]{:S(2)}) %collective-permute-start.17) | collective-permute-done | bytes 160 | tf_op jit(solution)/shard_map/ppermute | solution.py:19
  (86 shorter events, 11.3 us)
Async XLA Ops:
  1.4 8.1 %collective-permute-start = (f32[72,256]{1,0:T(8,128)S(1)}, f32[72,256]{1,0:T(8,128)S(1)}, u32[]{:S(2)}, u32[]{:S(2)}) collective-permute-start(f32[72,256]{1,0:T(8,128)S(1)} %select_maximum_fusion.part_ref), channel_id=1, source_target_pairs={{0,8},{1,9},{2,10},{3,11},{4,12},{5,13},{6,14},{7,15},{8,0},{9,1},... | collective-permute-start | bytes 221192 | tf_op jit(solution)/shard_map/ppermute | solution.py:19
  6.3 7.7 %collective-permute-start.4 = (f32[65,256]{1,0:T(8,128)S(1)}, f32[65,256]{1,0:T(8,128)S(1)}, u32[]{:S(2)}, u32[]{:S(2)}) collective-permute-start(f32[65,256]{1,0:T(8,128)S(1)} %get-tuple-element.49), channel_id=1, source_target_pairs={{0,2},{1,3},{2,0},{3,1},{4,6},{5,7},{6,4},{7,5},{8,10},{9,11},{10,... | collective-permute-start | bytes 199688 | tf_op jit(solution)/shard_map/ppermute | solution.py:19
  7.9 4.7 %collective-permute-start.1 = (f32[65,256]{1,0:T(8,128)S(1)}, f32[65,256]{1,0:T(8,128)S(1)}, u32[]{:S(2)}, u32[]{:S(2)}) collective-permute-start(f32[65,256]{1,0:T(8,128)S(1)} %get-tuple-element.49), channel_id=1, source_target_pairs={{0,4},{1,5},{2,6},{3,7},{4,0},{5,1},{6,2},{7,3},{8,12},{9,13},{10,... | collective-permute-start | bytes 199688 | tf_op jit(solution)/shard_map/ppermute | solution.py:19
  9.5 4.4 %collective-permute-start.2 = (f32[72,256]{1,0:T(8,128)S(1)}, f32[72,256]{1,0:T(8,128)S(1)}, u32[]{:S(2)}, u32[]{:S(2)}) collective-permute-start(f32[72,256]{1,0:T(8,128)S(1)} %collective-permute-done.part_ref), channel_id=1, source_target_pairs={{0,4},{1,5},{2,6},{3,7},{4,0},{5,1},{6,2},{7,3},{8,12},{9,13},{10,... | collective-permute-start | bytes 221192 | tf_op jit(solution)/shard_map/ppermute | solution.py:19
  10.2 8.6 %collective-permute-start.6 = (f32[65,256]{1,0:T(8,128)S(1)}, f32[65,256]{1,0:T(8,128)S(1)}, u32[]{:S(2)}, u32[]{:S(2)}) collective-permute-start(f32[65,256]{1,0:T(8,128)S(1)} %get-tuple-element.53), channel_id=1, source_target_pairs={{0,2},{1,3},{2,0},{3,1},{4,6},{5,7},{6,4},{7,5},{8,10},{9,11},{10,... | collective-permute-start | bytes 199688 | tf_op jit(solution)/shard_map/ppermute | solution.py:19
  14.0 5.2 %collective-permute-start.5 = (f32[65,512]{1,0:T(8,128)S(1)}, f32[65,512]{1,0:T(8,128)S(1)}, u32[]{:S(2)}, u32[]{:S(2)}) collective-permute-start(f32[65,512]{1,0:T(8,128)S(1)} %get-tuple-element.52), channel_id=1, source_target_pairs={{0,2},{1,3},{2,0},{3,1},{4,6},{5,7},{6,4},{7,5},{8,10},{9,11},{10,... | collective-permute-start | bytes 399368 | tf_op jit(solution)/shard_map/ppermute | solution.py:19
  15.6 1.7 %collective-permute-start.3 = (f32[64,1024]{1,0:T(8,128)S(1)}, f32[64,1024]{1,0:T(8,128)S(1)}, u32[]{:S(2)}, u32[]{:S(2)}) collective-permute-start(f32[64,1024]{1,0:T(8,128)S(1)} %slice.225), channel_id=1, source_target_pairs={{0,1},{1,0},{2,3},{3,2},{4,5},{5,4},{6,7},{7,6},{8,9},{9,8},{10,11... | collective-permute-start | bytes 786440 | tf_op jit(solution)/shard_map/ppermute | solution.py:19
  19.3 1.7 %collective-permute-start.7 = (f32[64,1024]{1,0:T(8,128)S(1)}, f32[64,1024]{1,0:T(8,128)S(1)}, u32[]{:S(2)}, u32[]{:S(2)}) collective-permute-start(f32[64,1024]{1,0:T(8,128)S(1)} %slice.230), channel_id=1, source_target_pairs={{0,1},{1,0},{2,3},{3,2},{4,5},{5,4},{6,7},{7,6},{8,9},{9,8},{10,11... | collective-permute-start | bytes 786440 | tf_op jit(solution)/shard_map/ppermute | solution.py:19
  22.6 5.9 %collective-permute-start.9 = (f32[32,1024]{1,0:T(8,128)S(1)}, f32[32,1024]{1,0:T(8,128)S(1)}, u32[]{:S(2)}, u32[]{:S(2)}) collective-permute-start(f32[32,1024]{1,0:T(8,128)S(1)} %get-tuple-element.64), channel_id=1, source_target_pairs={{0,2},{1,3},{2,0},{3,1},{4,6},{5,7},{6,4},{7,5},{8,10},{9,11},{10,... | collective-permute-start | bytes 393224 | tf_op jit(solution)/shard_map/ppermute | solution.py:19
  24.1 1.4 %collective-permute-start.8 = (f32[32,1024]{1,0:T(8,128)S(1)}, f32[32,1024]{1,0:T(8,128)S(1)}, u32[]{:S(2)}, u32[]{:S(2)}) collective-permute-start(f32[32,1024]{1,0:T(8,128)S(1)} %get-tuple-element.64), channel_id=1, source_target_pairs={{0,1},{1,0},{2,3},{3,2},{4,5},{5,4},{6,7},{7,6},{8,9},{9,8},{10,11... | collective-permute-start | bytes 393224 | tf_op jit(solution)/shard_map/ppermute | solution.py:19
  28.5 1.3 %collective-permute-start.10 = (f32[32,1024]{1,0:T(8,128)S(1)}, f32[32,1024]{1,0:T(8,128)S(1)}, u32[]{:S(2)}, u32[]{:S(2)}) collective-permute-start(f32[32,1024]{1,0:T(8,128)S(1)} %collective-permute-done.9), channel_id=1, source_target_pairs={{0,1},{1,0},{2,3},{3,2},{4,5},{5,4},{6,7},{7,6},{8,9},{9,8},{10,11... | collective-permute-start | bytes 393224 | tf_op jit(solution)/shard_map/ppermute | solution.py:19
  31.3 5.6 %collective-permute-start.12 = (f32[32,1024]{1,0:T(8,128)S(1)}, f32[32,1024]{1,0:T(8,128)S(1)}, u32[]{:S(2)}, u32[]{:S(2)}) collective-permute-start(f32[32,1024]{1,0:T(8,128)S(1)} %get-tuple-element.78), channel_id=1, source_target_pairs={{0,2},{1,3},{2,0},{3,1},{4,6},{5,7},{6,4},{7,5},{8,10},{9,11},{10,... | collective-permute-start | bytes 393224 | tf_op jit(solution)/shard_map/ppermute | solution.py:19
  32.9 1.4 %collective-permute-start.11 = (f32[32,1024]{1,0:T(8,128)S(1)}, f32[32,1024]{1,0:T(8,128)S(1)}, u32[]{:S(2)}, u32[]{:S(2)}) collective-permute-start(f32[32,1024]{1,0:T(8,128)S(1)} %get-tuple-element.78), channel_id=1, source_target_pairs={{0,1},{1,0},{2,3},{3,2},{4,5},{5,4},{6,7},{7,6},{8,9},{9,8},{10,11... | collective-permute-start | bytes 393224 | tf_op jit(solution)/shard_map/ppermute | solution.py:19
  36.9 1.3 %collective-permute-start.13 = (f32[32,1024]{1,0:T(8,128)S(1)}, f32[32,1024]{1,0:T(8,128)S(1)}, u32[]{:S(2)}, u32[]{:S(2)}) collective-permute-start(f32[32,1024]{1,0:T(8,128)S(1)} %collective-permute-done.12), channel_id=1, source_target_pairs={{0,1},{1,0},{2,3},{3,2},{4,5},{5,4},{6,7},{7,6},{8,9},{9,8},{10,11... | collective-permute-start | bytes 393224 | tf_op jit(solution)/shard_map/ppermute | solution.py:19
  39.6 5.6 %collective-permute-start.15 = (f32[32,1024]{1,0:T(8,128)S(1)}, f32[32,1024]{1,0:T(8,128)S(1)}, u32[]{:S(2)}, u32[]{:S(2)}) collective-permute-start(f32[32,1024]{1,0:T(8,128)S(1)} %get-tuple-element.88), channel_id=1, source_target_pairs={{0,2},{1,3},{2,0},{3,1},{4,6},{5,7},{6,4},{7,5},{8,10},{9,11},{10,... | collective-permute-start | bytes 393224 | tf_op jit(solution)/shard_map/ppermute | solution.py:19
  41.1 1.4 %collective-permute-start.14 = (f32[32,1024]{1,0:T(8,128)S(1)}, f32[32,1024]{1,0:T(8,128)S(1)}, u32[]{:S(2)}, u32[]{:S(2)}) collective-permute-start(f32[32,1024]{1,0:T(8,128)S(1)} %get-tuple-element.88), channel_id=1, source_target_pairs={{0,1},{1,0},{2,3},{3,2},{4,5},{5,4},{6,7},{7,6},{8,9},{9,8},{10,11... | collective-permute-start | bytes 393224 | tf_op jit(solution)/shard_map/ppermute | solution.py:19
  45.3 1.3 %collective-permute-start.16 = (f32[32,1024]{1,0:T(8,128)S(1)}, f32[32,1024]{1,0:T(8,128)S(1)}, u32[]{:S(2)}, u32[]{:S(2)}) collective-permute-start(f32[32,1024]{1,0:T(8,128)S(1)} %collective-permute-done.15), channel_id=1, source_target_pairs={{0,1},{1,0},{2,3},{3,2},{4,5},{5,4},{6,7},{7,6},{8,9},{9,8},{10,11... | collective-permute-start | bytes 393224 | tf_op jit(solution)/shard_map/ppermute | solution.py:19
  50.0 1.2 %collective-permute-start.17 = (f32[32]{0:T(128)S(1)}, f32[32]{0:T(128)S(1)}, u32[]{:S(2)}, u32[]{:S(2)}) collective-permute-start(f32[32]{0:T(128)S(1)} %get-tuple-element.96), channel_id=1, source_target_pairs={{0,1},{1,0},{2,3},{3,2},{4,5},{5,4},{6,7},{7,6},{8,9},{9,8},{10,11... | collective-permute-start | bytes 392 | tf_op jit(solution)/shard_map/ppermute | solution.py:19

commit v34 on v33

--- a/solution.py
+++ b/solution.py
@@ -247,6 +247,7 @@
             near = fence(apply_parts(parts, tile[0]))
             near = fence(near + apply_piece(pieces[1], tile[1]))
             far = jnp.zeros_like(near) if len(inner) == 1 else None
+            near = fence(collect(near) + noise * x)
             for k, stride in enumerate(inner[:-1]):
                 arrived = swap(join(*sent), n, stride)
                 if len(far_tile) < len(far_rows):
@@ -270,7 +271,7 @@
             curve = curve + jnp.sum(direction[:, before.shape[1] :] * pieces[-1], axis=1)
             if len(inner) > 1:
                 far = far + apply_piece(pieces[-1], tile[-1])
-            return collect(far), collect(near) + collect(far) + noise * x, join(*pieces), curve
+            return collect(far), near + collect(far), join(*pieces), curve
 
         residual = direction = join(*starts)
         my_solution = jnp.zeros_like(direction[:, :width])

time: 52.1 us -> 52.1 us (level)
  no operation moved by 1% of the time
where the time goes in v34:
time: 52.1 us; the launch traced here: 51.9 us
  starting transfers between devices  16.4 us (31%)
  matrix products  11.5 us (22%)
  waiting for transfers between devices  8.63 us (17%)
  Pallas kernels  8.62 us (17%)
  other arithmetic  5.5 us (11%)
  between operations  1.01 us (2%)
    ppermute x18, starting transfers between devices, swap(): return lax.ppermute(x, 'blk', [(i, i ^ stride) for i in range(n)])  16.4 us
    dot_general x14, matrix products, apply_parts(): jnp.dot(jnp.concatenate([parts, parts], axis=1), piece, preferred_element...  11.5 us
    ppermute x18, waiting for transfers between devices, swap(): return lax.ppermute(x, 'blk', [(i, i ^ stride) for i in range(n)])  8.63 us
    pallas_call x10, Pallas kernels, call(): pl.pallas_call(kernel, out_shape=outs, in_specs=[whole] * len(args), out_...  8.62 us
  transfers between devices with their start and end apart: 18, of which 13 were waited for; matrix products, arithmetic and copies ran while one was open for 18% of the time, Pallas kernels for 14%

profile of v34, /device:TPU:0, one launch (start us, length us, event | category | flops | bytes accessed | tf_op | source)
XLA Modules:
  0.0 51.9 jit_solution(14132536333802017079)
XLA Ops:
  0.6 0.8 %select_maximum_fusion.part_ref = f32[72,256]{1,0:T(8,128)S(1)} fusion(f32[1,256]{1,0:T(1,128)} %bitcast.32, f32[32,256]{1,0:T(8,128)} %param.7, f32[32,256]{1,0:T(8,128)} %param.4), kind=kLoop, calls=%fused_computation.285 | loop fusion | flops 73728 | bytes 140288 | tf_op jit(solution)/shard_map/concatenate | solution.py:192
  1.4 4.0 %collective-permute-start = (f32[72,256]{1,0:T(8,128)S(1)}, f32[72,256]{1,0:T(8,128)S(1)}, u32[]{:S(2)}, u32[]{:S(2)}) collective-permute-start(f32[72,256]{1,0:T(8,128)S(1)} %select_maximum_fusion.part_ref), channel_id=1, source_target_pairs={{0,8},{1,9},{2,10},{3,11},{4,12},{5,13},{6,14},{7,15},{8,0},{9,1},... | collective-permute-start | bytes 221192 | tf_op jit(solution)/shard_map/ppermute | solution.py:19
  6.3 1.6 %collective-permute-start.4 = (f32[65,256]{1,0:T(8,128)S(1)}, f32[65,256]{1,0:T(8,128)S(1)}, u32[]{:S(2)}, u32[]{:S(2)}) collective-permute-start(f32[65,256]{1,0:T(8,128)S(1)} %get-tuple-element.49), channel_id=1, source_target_pairs={{0,2},{1,3},{2,0},{3,1},{4,6},{5,7},{6,4},{7,5},{8,10},{9,11},{10,... | collective-permute-start | bytes 199688 | tf_op jit(solution)/shard_map/ppermute | solution.py:19
  7.9 1.6 %collective-permute-start.1 = (f32[65,256]{1,0:T(8,128)S(1)}, f32[65,256]{1,0:T(8,128)S(1)}, u32[]{:S(2)}, u32[]{:S(2)}) collective-permute-start(f32[65,256]{1,0:T(8,128)S(1)} %get-tuple-element.49), channel_id=1, source_target_pairs={{0,4},{1,5},{2,6},{3,7},{4,0},{5,1},{6,2},{7,3},{8,12},{9,13},{10,... | collective-permute-start | bytes 199688 | tf_op jit(solution)/shard_map/ppermute | solution.py:19
  10.2 1.9 %collective-permute-start.6 = (f32[65,256]{1,0:T(8,128)S(1)}, f32[65,256]{1,0:T(8,128)S(1)}, u32[]{:S(2)}, u32[]{:S(2)}) collective-permute-start(f32[65,256]{1,0:T(8,128)S(1)} %get-tuple-element.53), channel_id=1, source_target_pairs={{0,2},{1,3},{2,0},{3,1},{4,6},{5,7},{6,4},{7,5},{8,10},{9,11},{10,... | collective-permute-start | bytes 199688 | tf_op jit(solution)/shard_map/ppermute | solution.py:19
  12.6 1.2 %collective-permute-done.2 = f32[72,256]{1,0:T(8,128)S(1)} collective-permute-done((f32[72,256]{1,0:T(8,128)S(1)}, f32[72,256]{1,0:T(8,128)S(1)}, u32[]{:S(2)}, u32[]{:S(2)}) %collective-permute-start.2) | collective-permute-done | bytes 73760 | tf_op jit(solution)/shard_map/ppermute | solution.py:19
  14.0 1.5 %collective-permute-start.5 = (f32[65,512]{1,0:T(8,128)S(1)}, f32[65,512]{1,0:T(8,128)S(1)}, u32[]{:S(2)}, u32[]{:S(2)}) collective-permute-start(f32[65,512]{1,0:T(8,128)S(1)} %get-tuple-element.52), channel_id=1, source_target_pairs={{0,2},{1,3},{2,0},{3,1},{4,6},{5,7},{6,4},{7,5},{8,10},{9,11},{10,... | collective-permute-start | bytes 399368 | tf_op jit(solution)/shard_map/ppermute | solution.py:19
  15.7 1.5 %shard_map.62 = (bf16[2048,1024]{1,0:T(8,128)(2,1)S(1)}, f32[32,1024]{1,0:T(8,128)S(1)}) custom-call(f32[32,1024]{1,0:T(8,128)S(1)} %get-tuple-element.121.rows_ref, f32[32,1]{1,0:T(8,128)S(1)} %copy.6.scale_ref, bf16[256,1024]{1,0:T(8,128)(2,1)S(1)} %constant_dynamic-update-slice_fusion.right_ref, f32[32,1024]{1,0:T(8,128)S(1)} %get-tuple-element.122.refs_0_, ...), custom_call_target="tpu_custom_call" | custom-call | flops 872415232 | bytes 4194304 | tf_op jit(solution)/shard_map/pallas_call | solution.py:119
  17.3 1.5 %shard_map.63 = (bf16[2048,1024]{1,0:T(8,128)(2,1)S(1)}, f32[32,1024]{1,0:T(8,128)S(1)}) custom-call(f32[32,1024]{1,0:T(8,128)S(1)} %get-tuple-element.126.rows_ref, f32[32,1]{1,0:T(8,128)S(1)} %copy.6.scale_ref, bf16[256,1024]{1,0:T(8,128)(2,1)S(1)} %constant_dynamic-update-slice_fusion.right_ref, f32[32,1024]{1,0:T(8,128)S(1)} %get-tuple-element.125.refs_0_, ...), custom_call_target="tpu_custom_call" | custom-call | flops 872415232 | bytes 4194304 | tf_op jit(solution)/shard_map/pallas_call | solution.py:119
  19.5 1.5 %shard_map.64 = (bf16[2048,1024]{1,0:T(8,128)(2,1)S(1)}, f32[32,1024]{1,0:T(8,128)S(1)}) custom-call(f32[32,1024]{1,0:T(8,128)S(1)} %get-tuple-element.69.rows_ref.part_ref, f32[32,1]{1,0:T(8,128)S(1)} %copy.6.scale_ref, bf16[256,1024]{1,0:T(8,128)(2,1)S(1)} %constant_dynamic-update-slice_fusion.right_ref, f32[32,1024]{1,0:T(8,128)S(1)} %get-tuple-element.118.refs_0_, ...), custom_call_target="tpu_custom_call" | custom-call | flops 872415232 | bytes 4194304 | tf_op jit(solution)/shard_map/pallas_call | solution.py:119
  21.0 1.5 %shard_map.65 = (bf16[2048,1024]{1,0:T(8,128)(2,1)S(1)}, f32[32,1024]{1,0:T(8,128)S(1)}) custom-call(f32[32,1024]{1,0:T(8,128)S(1)} %get-tuple-element.80.rows_ref, f32[32,1]{1,0:T(8,128)S(1)} %copy.6.scale_ref, bf16[256,1024]{1,0:T(8,128)(2,1)S(1)} %constant_dynamic-update-slice_fusion.right_ref, f32[32,1024]{1,0:T(8,128)S(1)} %get-tuple-element.123.refs_0_, ...), custom_call_target="tpu_custom_call" | custom-call | flops 872415232 | bytes 4194304 | tf_op jit(solution)/shard_map/pallas_call | solution.py:119
  22.6 1.4 %collective-permute-start.9 = (f32[32,1024]{1,0:T(8,128)S(1)}, f32[32,1024]{1,0:T(8,128)S(1)}, u32[]{:S(2)}, u32[]{:S(2)}) collective-permute-start(f32[32,1024]{1,0:T(8,128)S(1)} %get-tuple-element.64), channel_id=1, source_target_pairs={{0,2},{1,3},{2,0},{3,1},{4,6},{5,7},{6,4},{7,5},{8,10},{9,11},{10,... | collective-permute-start | bytes 393224 | tf_op jit(solution)/shard_map/ppermute | solution.py:19
  25.5 0.8 %convolution_add_fusion.6 = f32[96,1024]{1,0:T(8,128)S(1)} fusion(f32[96,1024]{1,0:T(8,128)S(1)} %fusion.6, bf16[2048,1024]{1,0:T(8,128)(2,1)S(1)} %get-tuple-element.67, bf16[32,1024]{1,0:T(8,128)(2,1)S(1)} %get-tuple-element.159, bf16[32,1024]{1,0:T(8,128)(2,1)S(1)} %get-tuple-element.160, bf16[32,1024]{1,0:T(8,128)(2,1)S(1)} %get-tuple-element.158), kind=kOutput, calls=%fused_computation.6 | convolution fusion | flops 405110784 | bytes 5177344 | tf_op jit(solution)/shard_map/dot_general | solution.py:157
  26.5 1.1 %shard_map.67 = bf16[2048,1024]{1,0:T(8,128)(2,1)S(1)} custom-call(f32[32,1024]{1,0:T(8,128)S(1)} %get-tuple-element.69.rows_ref.part_ref, f32[32,1]{1,0:T(8,128)S(1)} %copy.6.scale_ref, bf16[256,1024]{1,0:T(8,128)(2,1)S(1)} %shard_map.66.right_ref), custom_call_target="tpu_custom_call" | custom-call | flops 872415232 | bytes 4194304 | tf_op jit(solution)/shard_map/pallas_call | solution.py:119
  27.6 0.9 %collective-permute-done.9 = f32[32,1024]{1,0:T(8,128)S(1)} collective-permute-done((f32[32,1024]{1,0:T(8,128)S(1)}, f32[32,1024]{1,0:T(8,128)S(1)}, u32[]{:S(2)}, u32[]{:S(2)}) %collective-permute-start.9) | collective-permute-done | bytes 131104 | tf_op jit(solution)/shard_map/ppermute | solution.py:19
  28.6 0.8 %fusion.21 = f32[96,1024]{1,0:T(8,128)S(1)} fusion(bf16[2048,1024]{1,0:T(8,128)(2,1)S(1)} %get-tuple-element.73, bf16[32,1024]{1,0:T(8,128)(2,1)S(1)} %get-tuple-element.156, bf16[32,1024]{1,0:T(8,128)(2,1)S(1)} %get-tuple-element.157, bf16[32,1024]{1,0:T(8,128)(2,1)S(1)} %get-tuple-element.155), kind=kOutput, calls=%fused_computation.42 | convolution fusion | flops 405012480 | bytes 4784128 | tf_op jit(solution)/shard_map/dot_general | solution.py:157
  30.3 0.8 %convolution_add_fusion.5 = f32[96,1024]{1,0:T(8,128)S(1)} fusion(f32[96,1024]{1,0:T(8,128)S(1)} %fusion.21, bf16[2048,1024]{1,0:T(8,128)(2,1)S(1)} %get-tuple-element.77, bf16[32,1024]{1,0:T(8,128)(2,1)S(1)} %get-tuple-element.152, bf16[32,1024]{1,0:T(8,128)(2,1)S(1)} %get-tuple-element.153, bf16[32,1024]{1,0:T(8,128)(2,1)S(1)} %get-tuple-element.151), kind=kOutput, calls=%fused_computation.5 | convolution fusion | flops 405110784 | bytes 5177344 | tf_op jit(solution)/shard_map/dot_general | solution.py:157
  31.3 1.5 %collective-permute-start.12 = (f32[32,1024]{1,0:T(8,128)S(1)}, f32[32,1024]{1,0:T(8,128)S(1)}, u32[]{:S(2)}, u32[]{:S(2)}) collective-permute-start(f32[32,1024]{1,0:T(8,128)S(1)} %get-tuple-element.78), channel_id=1, source_target_pairs={{0,2},{1,3},{2,0},{3,1},{4,6},{5,7},{6,4},{7,5},{8,10},{9,11},{10,... | collective-permute-start | bytes 393224 | tf_op jit(solution)/shard_map/ppermute | solution.py:19
  33.0 0.8 %fusion.44 = f32[96,1024]{1,0:T(8,128)S(1)} fusion(bf16[2048,1024]{1,0:T(8,128)(2,1)S(1)} %get-tuple-element.66, bf16[96,1024]{1,0:T(8,128)(2,1)S(1)} %pad_maximum_fusion.3), kind=kOutput, calls=%fused_computation.65 | convolution fusion | flops 403439616 | bytes 4784128 | tf_op jit(solution)/shard_map/dot_general | solution.py:157
  34.3 1.0 %convolution_add_fusion.4 = f32[96,1024]{1,0:T(8,128)S(1)} fusion(f32[96,1024]{1,0:T(8,128)S(1)} %fusion.44, bf16[2048,1024]{1,0:T(8,128)(2,1)S(1)} %get-tuple-element.67, bf16[32,1024]{1,0:T(8,128)(2,1)S(1)} %get-tuple-element.147, bf16[32,1024]{1,0:T(8,128)(2,1)S(1)} %get-tuple-element.148, bf16[32,1024]{1,0:T(8,128)(2,1)S(1)} %get-tuple-element.146), kind=kOutput, calls=%fused_computation.4 | convolution fusion | flops 405110784 | bytes 5177344 | tf_op jit(solution)/shard_map/dot_general | solution.py:157
  35.4 1.1 %shard_map.68 = bf16[2048,1024]{1,0:T(8,128)(2,1)S(1)} custom-call(f32[32,1024]{1,0:T(8,128)S(1)} %get-tuple-element.80.rows_ref, f32[32,1]{1,0:T(8,128)S(1)} %copy.6.scale_ref, bf16[256,1024]{1,0:T(8,128)(2,1)S(1)} %shard_map.66.right_ref), custom_call_target="tpu_custom_call" | custom-call | flops 872415232 | bytes 4194304 | tf_op jit(solution)/shard_map/pallas_call | solution.py:119
  36.9 0.8 %fusion.59 = f32[96,1024]{1,0:T(8,128)S(1)} fusion(bf16[2048,1024]{1,0:T(8,128)(2,1)S(1)} %get-tuple-element.73, bf16[32,1024]{1,0:T(8,128)(2,1)S(1)} %get-tuple-element.144, bf16[32,1024]{1,0:T(8,128)(2,1)S(1)} %get-tuple-element.145, bf16[32,1024]{1,0:T(8,128)(2,1)S(1)} %get-tuple-element.143), kind=kOutput, calls=%fused_computation.80 | convolution fusion | flops 405012480 | bytes 4784128 | tf_op jit(solution)/shard_map/dot_general | solution.py:157
  38.7 0.8 %convolution_add_fusion.3 = f32[96,1024]{1,0:T(8,128)S(1)} fusion(f32[96,1024]{1,0:T(8,128)S(1)} %fusion.59, bf16[2048,1024]{1,0:T(8,128)(2,1)S(1)} %get-tuple-element.77, bf16[32,1024]{1,0:T(8,128)(2,1)S(1)} %get-tuple-element.140, bf16[32,1024]{1,0:T(8,128)(2,1)S(1)} %get-tuple-element.141, bf16[32,1024]{1,0:T(8,128)(2,1)S(1)} %get-tuple-element.139), kind=kOutput, calls=%fused_computation.3 | convolution fusion | flops 405110784 | bytes 5177344 | tf_op jit(solution)/shard_map/dot_general | solution.py:157
  39.6 1.5 %collective-permute-start.15 = (f32[32,1024]{1,0:T(8,128)S(1)}, f32[32,1024]{1,0:T(8,128)S(1)}, u32[]{:S(2)}, u32[]{:S(2)}) collective-permute-start(f32[32,1024]{1,0:T(8,128)S(1)} %get-tuple-element.88), channel_id=1, source_target_pairs={{0,2},{1,3},{2,0},{3,1},{4,6},{5,7},{6,4},{7,5},{8,10},{9,11},{10,... | collective-permute-start | bytes 393224 | tf_op jit(solution)/shard_map/ppermute | solution.py:19
  41.3 0.8 %fusion.82 = f32[96,1024]{1,0:T(8,128)S(1)} fusion(bf16[2048,1024]{1,0:T(8,128)(2,1)S(1)} %get-tuple-element.66, bf16[96,1024]{1,0:T(8,128)(2,1)S(1)} %pad_maximum_fusion.4), kind=kOutput, calls=%fused_computation.103 | convolution fusion | flops 403439616 | bytes 4784128 | tf_op jit(solution)/shard_map/dot_general | solution.py:157
  42.6 0.8 %convolution_add_fusion.2 = f32[96,1024]{1,0:T(8,128)S(1)} fusion(f32[96,1024]{1,0:T(8,128)S(1)} %fusion.82, bf16[2048,1024]{1,0:T(8,128)(2,1)S(1)} %get-tuple-element.67, bf16[32,1024]{1,0:T(8,128)(2,1)S(1)} %get-tuple-element.135, bf16[32,1024]{1,0:T(8,128)(2,1)S(1)} %get-tuple-element.136, bf16[32,1024]{1,0:T(8,128)(2,1)S(1)} %get-tuple-element.134), kind=kOutput, calls=%fused_computation.2 | convolution fusion | flops 405110784 | bytes 5177344 | tf_op jit(solution)/shard_map/dot_general | solution.py:157
  43.4 1.8 %collective-permute-done.15 = f32[32,1024]{1,0:T(8,128)S(1)} collective-permute-done((f32[32,1024]{1,0:T(8,128)S(1)}, f32[32,1024]{1,0:T(8,128)S(1)}, u32[]{:S(2)}, u32[]{:S(2)}) %collective-permute-start.15) | collective-permute-done | bytes 131104 | tf_op jit(solution)/shard_map/ppermute | solution.py:19
  45.3 0.8 %fusion.97 = f32[96,1024]{1,0:T(8,128)S(1)} fusion(bf16[2048,1024]{1,0:T(8,128)(2,1)S(1)} %get-tuple-element.73, bf16[32,1024]{1,0:T(8,128)(2,1)S(1)} %get-tuple-element.132, bf16[32,1024]{1,0:T(8,128)(2,1)S(1)} %get-tuple-element.133, bf16[32,1024]{1,0:T(8,128)(2,1)S(1)} %get-tuple-element.131), kind=kOutput, calls=%fused_computation.118 | convolution fusion | flops 405012480 | bytes 4784128 | tf_op jit(solution)/shard_map/dot_general | solution.py:157
  47.3 0.8 %convolution_add_fusion.1 = f32[96,1024]{1,0:T(8,128)S(1)} fusion(f32[96,1024]{1,0:T(8,128)S(1)} %fusion.97, bf16[2048,1024]{1,0:T(8,128)(2,1)S(1)} %get-tuple-element.77, bf16[32,1024]{1,0:T(8,128)(2,1)S(1)} %get-tuple-element.128, bf16[32,1024]{1,0:T(8,128)(2,1)S(1)} %get-tuple-element.129, bf16[32,1024]{1,0:T(8,128)(2,1)S(1)} %get-tuple-element.127), kind=kOutput, calls=%fused_computation.1 | convolution fusion | flops 405110784 | bytes 5177344 | tf_op jit(solution)/shard_map/dot_general | solution.py:157
  48.1 0.8 %fusion.120 = f32[96,1024]{1,0:T(8,128)S(1)} fusion(bf16[2048,1024]{1,0:T(8,128)(2,1)S(1)} %shard_map.67, bf16[32,1024]{1,0:T(8,128)(2,1)S(1)} %get-tuple-element.114, bf16[32,1024]{1,0:T(8,128)(2,1)S(1)} %get-tuple-element.113, bf16[32,1024]{1,0:T(8,128)(2,1)S(1)} %get-tuple-element.117), kind=kOutput, calls=%fused_computation.141 | convolution fusion | flops 405012480 | bytes 4784128 | tf_op jit(solution)/shard_map/dot_general | solution.py:157
  48.9 0.8 %convolution_add_fusion = f32[96,1024]{1,0:T(8,128)S(1)} fusion(f32[96,1024]{1,0:T(8,128)S(1)} %fusion.120, bf16[2048,1024]{1,0:T(8,128)(2,1)S(1)} %shard_map.68, bf16[32,1024]{1,0:T(8,128)(2,1)S(1)} %get-tuple-element.115, bf16[32,1024]{1,0:T(8,128)(2,1)S(1)} %get-tuple-element.116, bf16[32,1024]{1,0:T(8,128)(2,1)S(1)} %get-tuple-element.112), kind=kOutput, calls=%fused_computation | convolution fusion | flops 405110784 | bytes 5177344 | tf_op jit(solution)/shard_map/dot_general | solution.py:157
  50.2 1.0 %collective-permute-done.17 = f32[32]{0:T(128)S(1)} collective-permute-done((f32[32]{0:T(128)S(1)}, f32[32]{0:T(128)S(1)}, u32[]{:S(2)}, u32[]{:S(2)}) %collective-permute-start.17) | collective-permute-done | bytes 160 | tf_op jit(solution)/shard_map/ppermute | solution.py:19
  (89 shorter events, 11.4 us)
Async XLA Ops:
  1.4 8.1 %collective-permute-start = (f32[72,256]{1,0:T(8,128)S(1)}, f32[72,256]{1,0:T(8,128)S(1)}, u32[]{:S(2)}, u32[]{:S(2)}) collective-permute-start(f32[72,256]{1,0:T(8,128)S(1)} %select_maximum_fusion.part_ref), channel_id=1, source_target_pairs={{0,8},{1,9},{2,10},{3,11},{4,12},{5,13},{6,14},{7,15},{8,0},{9,1},... | collective-permute-start | bytes 221192 | tf_op jit(solution)/shard_map/ppermute | solution.py:19
  6.3 7.7 %collective-permute-start.4 = (f32[65,256]{1,0:T(8,128)S(1)}, f32[65,256]{1,0:T(8,128)S(1)}, u32[]{:S(2)}, u32[]{:S(2)}) collective-permute-start(f32[65,256]{1,0:T(8,128)S(1)} %get-tuple-element.49), channel_id=1, source_target_pairs={{0,2},{1,3},{2,0},{3,1},{4,6},{5,7},{6,4},{7,5},{8,10},{9,11},{10,... | collective-permute-start | bytes 199688 | tf_op jit(solution)/shard_map/ppermute | solution.py:19
  7.9 4.7 %collective-permute-start.1 = (f32[65,256]{1,0:T(8,128)S(1)}, f32[65,256]{1,0:T(8,128)S(1)}, u32[]{:S(2)}, u32[]{:S(2)}) collective-permute-start(f32[65,256]{1,0:T(8,128)S(1)} %get-tuple-element.49), channel_id=1, source_target_pairs={{0,4},{1,5},{2,6},{3,7},{4,0},{5,1},{6,2},{7,3},{8,12},{9,13},{10,... | collective-permute-start | bytes 199688 | tf_op jit(solution)/shard_map/ppermute | solution.py:19
  9.5 4.4 %collective-permute-start.2 = (f32[72,256]{1,0:T(8,128)S(1)}, f32[72,256]{1,0:T(8,128)S(1)}, u32[]{:S(2)}, u32[]{:S(2)}) collective-permute-start(f32[72,256]{1,0:T(8,128)S(1)} %collective-permute-done.part_ref), channel_id=1, source_target_pairs={{0,4},{1,5},{2,6},{3,7},{4,0},{5,1},{6,2},{7,3},{8,12},{9,13},{10,... | collective-permute-start | bytes 221192 | tf_op jit(solution)/shard_map/ppermute | solution.py:19
  10.2 8.6 %collective-permute-start.6 = (f32[65,256]{1,0:T(8,128)S(1)}, f32[65,256]{1,0:T(8,128)S(1)}, u32[]{:S(2)}, u32[]{:S(2)}) collective-permute-start(f32[65,256]{1,0:T(8,128)S(1)} %get-tuple-element.53), channel_id=1, source_target_pairs={{0,2},{1,3},{2,0},{3,1},{4,6},{5,7},{6,4},{7,5},{8,10},{9,11},{10,... | collective-permute-start | bytes 199688 | tf_op jit(solution)/shard_map/ppermute | solution.py:19
  14.0 5.2 %collective-permute-start.5 = (f32[65,512]{1,0:T(8,128)S(1)}, f32[65,512]{1,0:T(8,128)S(1)}, u32[]{:S(2)}, u32[]{:S(2)}) collective-permute-start(f32[65,512]{1,0:T(8,128)S(1)} %get-tuple-element.52), channel_id=1, source_target_pairs={{0,2},{1,3},{2,0},{3,1},{4,6},{5,7},{6,4},{7,5},{8,10},{9,11},{10,... | collective-permute-start | bytes 399368 | tf_op jit(solution)/shard_map/ppermute | solution.py:19
  15.6 1.7 %collective-permute-start.3 = (f32[64,1024]{1,0:T(8,128)S(1)}, f32[64,1024]{1,0:T(8,128)S(1)}, u32[]{:S(2)}, u32[]{:S(2)}) collective-permute-start(f32[64,1024]{1,0:T(8,128)S(1)} %slice.225), channel_id=1, source_target_pairs={{0,1},{1,0},{2,3},{3,2},{4,5},{5,4},{6,7},{7,6},{8,9},{9,8},{10,11... | collective-permute-start | bytes 786440 | tf_op jit(solution)/shard_map/ppermute | solution.py:19
  19.3 1.7 %collective-permute-start.7 = (f32[64,1024]{1,0:T(8,128)S(1)}, f32[64,1024]{1,0:T(8,128)S(1)}, u32[]{:S(2)}, u32[]{:S(2)}) collective-permute-start(f32[64,1024]{1,0:T(8,128)S(1)} %slice.230), channel_id=1, source_target_pairs={{0,1},{1,0},{2,3},{3,2},{4,5},{5,4},{6,7},{7,6},{8,9},{9,8},{10,11... | collective-permute-start | bytes 786440 | tf_op jit(solution)/shard_map/ppermute | solution.py:19
  22.6 5.9 %collective-permute-start.9 = (f32[32,1024]{1,0:T(8,128)S(1)}, f32[32,1024]{1,0:T(8,128)S(1)}, u32[]{:S(2)}, u32[]{:S(2)}) collective-permute-start(f32[32,1024]{1,0:T(8,128)S(1)} %get-tuple-element.64), channel_id=1, source_target_pairs={{0,2},{1,3},{2,0},{3,1},{4,6},{5,7},{6,4},{7,5},{8,10},{9,11},{10,... | collective-permute-start | bytes 393224 | tf_op jit(solution)/shard_map/ppermute | solution.py:19
  24.1 1.4 %collective-permute-start.8 = (f32[32,1024]{1,0:T(8,128)S(1)}, f32[32,1024]{1,0:T(8,128)S(1)}, u32[]{:S(2)}, u32[]{:S(2)}) collective-permute-start(f32[32,1024]{1,0:T(8,128)S(1)} %get-tuple-element.64), channel_id=1, source_target_pairs={{0,1},{1,0},{2,3},{3,2},{4,5},{5,4},{6,7},{7,6},{8,9},{9,8},{10,11... | collective-permute-start | bytes 393224 | tf_op jit(solution)/shard_map/ppermute | solution.py:19
  28.5 1.3 %collective-permute-start.10 = (f32[32,1024]{1,0:T(8,128)S(1)}, f32[32,1024]{1,0:T(8,128)S(1)}, u32[]{:S(2)}, u32[]{:S(2)}) collective-permute-start(f32[32,1024]{1,0:T(8,128)S(1)} %collective-permute-done.9), channel_id=1, source_target_pairs={{0,1},{1,0},{2,3},{3,2},{4,5},{5,4},{6,7},{7,6},{8,9},{9,8},{10,11... | collective-permute-start | bytes 393224 | tf_op jit(solution)/shard_map/ppermute | solution.py:19
  31.3 5.6 %collective-permute-start.12 = (f32[32,1024]{1,0:T(8,128)S(1)}, f32[32,1024]{1,0:T(8,128)S(1)}, u32[]{:S(2)}, u32[]{:S(2)}) collective-permute-start(f32[32,1024]{1,0:T(8,128)S(1)} %get-tuple-element.78), channel_id=1, source_target_pairs={{0,2},{1,3},{2,0},{3,1},{4,6},{5,7},{6,4},{7,5},{8,10},{9,11},{10,... | collective-permute-start | bytes 393224 | tf_op jit(solution)/shard_map/ppermute | solution.py:19
  32.9 1.4 %collective-permute-start.11 = (f32[32,1024]{1,0:T(8,128)S(1)}, f32[32,1024]{1,0:T(8,128)S(1)}, u32[]{:S(2)}, u32[]{:S(2)}) collective-permute-start(f32[32,1024]{1,0:T(8,128)S(1)} %get-tuple-element.78), channel_id=1, source_target_pairs={{0,1},{1,0},{2,3},{3,2},{4,5},{5,4},{6,7},{7,6},{8,9},{9,8},{10,11... | collective-permute-start | bytes 393224 | tf_op jit(solution)/shard_map/ppermute | solution.py:19
  36.9 1.3 %collective-permute-start.13 = (f32[32,1024]{1,0:T(8,128)S(1)}, f32[32,1024]{1,0:T(8,128)S(1)}, u32[]{:S(2)}, u32[]{:S(2)}) collective-permute-start(f32[32,1024]{1,0:T(8,128)S(1)} %collective-permute-done.12), channel_id=1, source_target_pairs={{0,1},{1,0},{2,3},{3,2},{4,5},{5,4},{6,7},{7,6},{8,9},{9,8},{10,11... | collective-permute-start | bytes 393224 | tf_op jit(solution)/shard_map/ppermute | solution.py:19
  39.6 5.6 %collective-permute-start.15 = (f32[32,1024]{1,0:T(8,128)S(1)}, f32[32,1024]{1,0:T(8,128)S(1)}, u32[]{:S(2)}, u32[]{:S(2)}) collective-permute-start(f32[32,1024]{1,0:T(8,128)S(1)} %get-tuple-element.88), channel_id=1, source_target_pairs={{0,2},{1,3},{2,0},{3,1},{4,6},{5,7},{6,4},{7,5},{8,10},{9,11},{10,... | collective-permute-start | bytes 393224 | tf_op jit(solution)/shard_map/ppermute | solution.py:19
  41.1 1.4 %collective-permute-start.14 = (f32[32,1024]{1,0:T(8,128)S(1)}, f32[32,1024]{1,0:T(8,128)S(1)}, u32[]{:S(2)}, u32[]{:S(2)}) collective-permute-start(f32[32,1024]{1,0:T(8,128)S(1)} %get-tuple-element.88), channel_id=1, source_target_pairs={{0,1},{1,0},{2,3},{3,2},{4,5},{5,4},{6,7},{7,6},{8,9},{9,8},{10,11... | collective-permute-start | bytes 393224 | tf_op jit(solution)/shard_map/ppermute | solution.py:19
  45.3 1.3 %collective-permute-start.16 = (f32[32,1024]{1,0:T(8,128)S(1)}, f32[32,1024]{1,0:T(8,128)S(1)}, u32[]{:S(2)}, u32[]{:S(2)}) collective-permute-start(f32[32,1024]{1,0:T(8,128)S(1)} %collective-permute-done.15), channel_id=1, source_target_pairs={{0,1},{1,0},{2,3},{3,2},{4,5},{5,4},{6,7},{7,6},{8,9},{9,8},{10,11... | collective-permute-start | bytes 393224 | tf_op jit(solution)/shard_map/ppermute | solution.py:19
  50.0 1.2 %collective-permute-start.17 = (f32[32]{0:T(128)S(1)}, f32[32]{0:T(128)S(1)}, u32[]{:S(2)}, u32[]{:S(2)}) collective-permute-start(f32[32]{0:T(128)S(1)} %get-tuple-element.96), channel_id=1, source_target_pairs={{0,1},{1,0},{2,3},{3,2},{4,5},{5,4},{6,7},{7,6},{8,9},{9,8},{10,11... | collective-permute-start | bytes 392 | tf_op jit(solution)/shard_map/ppermute | solution.py:19
